TPU v7x, 32 devices: a whole 2x2x4 slice. The times are simulated.
32 devices in a mesh: sta: 8 (over z, x), sat: 4 (over y, core).
Axes of the slice: x: 2, y: 2, z: 4, core: 2. Of those that a mesh axis runs over, the one named last changes fastest.
Arguments:
- sight: float32 [64, 3, 32, 256], P(('sta', 'sat')), may hold values from -1 to 1
- mapping: float32 [64, 32, 256], P(('sta', 'sat')), may hold values from 1 to 10
- residual: float32 [64, 32, 256], P(('sta', 'sat')), may hold values from -6 to 6
- counts: int32 [64, 32, 256], P(('sta', 'sat')), may hold values from 0 to 3, as said below
- track: int32 [64, 32], P(('sta', 'sat')), may hold values from 0 to 119, all different within a row
- knots: int32 [64, 256], P(('sta', 'sat')), may hold values from 0 to 3, as said below
- orbit: float32 [120, 3, 8, 256], P('sat'), may hold values from -6 to 6
Outputs:
- normal: float32 [960, 960], P('sat', 'sta')
- right_hand: float32 [960], P('sat')
- own_blocks: float32 [120, 8, 8], P('sat')
Inputs may be any that keep to these rules, and one draw needn't show every extreme that they name: `track`: each station's row names 32 different satellites, and every satellite is tracked by some station. `knots`: along the epochs of each station the index never falls, and every index from 0 to 3 occurs for every station. `counts`: some stations observe no satellite at all over a run of epochs.
All inputs are finite; a program needn't handle non-finite values.
Results may differ from a plain program's by a relative error of at most 0.00012.
Values sent between devices are 32-bit elements; how exact they have to be, the bound alone decides.
No kernel may reach another device: no remote copies, remote signals or barrier semaphores. Data moves between devices by JAX's collectives and lax.ppermute only.
A program may use at most 256 MiB of HBM per device.

v0:
```python
import math

import jax
import jax.numpy as jnp
from jax import lax
from jax.sharding import PartitionSpec as P

KNOTS = 4


PRIOR = 1.0
HIGH = lax.Precision.HIGHEST


def reduce_station(
    station_sight, station_map, station_res, station_count, station_track, station_knot, orbit
):
    tracked = station_sight.shape[1]
    epochs = station_sight.shape[2]
    params = orbit.shape[2]
    span = tracked * params
    tracked_orbit = jnp.take(orbit, station_track, axis=0)
    design = jnp.sum(jnp.transpose(station_sight, (1, 0, 2))[:, :, None, :] * tracked_orbit, axis=1)
    weight = station_count.astype(jnp.float32)
    epoch_total = jnp.maximum(jnp.sum(weight, 0), 1.0)
    weighted = design * weight[:, None, :]
    weighted_rows = weighted.reshape(span, epochs)
    design_rows = design.reshape(span, epochs)
    clock_term = jnp.dot(weighted_rows / epoch_total, weighted_rows.T, precision=HIGH)
    slot_of = jnp.arange(span, dtype=jnp.int32) // params
    block_mask = (slot_of[:, None] == slot_of[None, :]).astype(jnp.float32)
    station_normal = jnp.dot(weighted_rows, design_rows.T, precision=HIGH) * block_mask - clock_term
    knot_select = (station_knot[None, :] == jnp.arange(KNOTS, dtype=jnp.int32)[:, None]).astype(
        jnp.float32
    )
    weight_map = weight * station_map
    sum_map = jnp.sum(weight_map, 0)
    sum_res = jnp.sum(weight * station_res, 0)
    tropo_rows = (weighted * station_map[:, None, :]).reshape(span, epochs) - weighted_rows * (
        sum_map / epoch_total
    )
    tropo_cross = jnp.dot(tropo_rows, knot_select.T, precision=HIGH)
    tropo_diag = (
        jnp.dot(
            knot_select,
            jnp.sum(weight_map * station_map, 0) - sum_map * sum_map / epoch_total,
            precision=HIGH,
        )
        + PRIOR
    )
    right_global = jnp.sum(
        (weighted * station_res[:, None, :]).reshape(span, epochs)
        - weighted_rows * (sum_res / epoch_total),
        1,
    )
    right_local = jnp.dot(
        knot_select,
        jnp.sum(weight_map * station_res, 0) - sum_map * sum_res / epoch_total,
        precision=HIGH,
    )
    scaled_cross = tropo_cross / tropo_diag
    station_normal = station_normal - jnp.dot(scaled_cross, tropo_cross.T, precision=HIGH)
    station_right = right_global - jnp.dot(scaled_cross, right_local, precision=HIGH)
    return (station_normal, station_right)


def spread_blocks(station_normal, station_right, station_track, sats, params):
    tracked = station_track.shape[0]
    span = tracked * params
    full_width = sats * params
    select = (station_track[:, None] == jnp.arange(sats, dtype=jnp.int32)[None, :]).astype(
        jnp.float32
    )
    rows_view = station_normal.reshape(tracked, params * span)
    left = jnp.dot(select.T, rows_view, precision=HIGH).reshape(full_width, span)
    left_turned = left.T.reshape(tracked, params * full_width)
    spread = jnp.dot(select.T, left_turned, precision=HIGH).reshape(full_width, full_width)
    right_spread = jnp.dot(
        select.T, station_right.reshape(tracked, params), precision=HIGH
    ).reshape(full_width)
    return (spread.T, right_spread)


def shards(sight, mapping, residual, counts, track, knots, orbit):
    all_orbit = lax.all_gather(orbit, "sat", axis=0, tiled=True)
    sats = all_orbit.shape[0]
    params = all_orbit.shape[2]
    full_width = sats * params

    def visit(station, carry):
        normal_sum, right_sum = carry
        station_normal, station_right = reduce_station(
            sight[station],
            mapping[station],
            residual[station],
            counts[station],
            track[station],
            knots[station],
            all_orbit,
        )
        spread, right_spread = spread_blocks(
            station_normal, station_right, track[station], sats, params
        )
        return (normal_sum + spread, right_sum + right_spread)

    start = (
        jnp.zeros((full_width, full_width), jnp.float32),
        jnp.zeros((full_width,), jnp.float32),
    )
    normal_sum, right_sum = lax.fori_loop(0, sight.shape[0], visit, start)
    stations = sight.shape[0] * lax.axis_size("sta") * lax.axis_size("sat")
    factor = sats / (stations * sight.shape[2] * sight.shape[3])
    cross_factor = sats / math.sqrt(stations * sight.shape[3])
    row_block = lax.psum_scatter(normal_sum, "sat", scatter_dimension=0, tiled=True)
    owned_block = lax.psum_scatter(row_block, "sta", scatter_dimension=1, tiled=True)
    diagonal_part = jnp.transpose(
        jnp.diagonal(normal_sum.reshape(sats, params, sats, params), axis1=0, axis2=2), (2, 0, 1)
    )
    right_all, blocks_all = lax.psum((right_sum, diagonal_part), ("sta", "sat"))
    own_sats = sats // lax.axis_size("sat")
    right_own = lax.dynamic_slice_in_dim(
        right_all, lax.axis_index("sat") * own_sats * params, own_sats * params
    )
    blocks_own = lax.dynamic_slice_in_dim(blocks_all, lax.axis_index("sat") * own_sats, own_sats)
    row_global = lax.axis_index("sat") * owned_block.shape[0] + jnp.arange(
        owned_block.shape[0], dtype=jnp.int32
    )
    column_global = lax.axis_index("sta") * owned_block.shape[1] + jnp.arange(
        owned_block.shape[1], dtype=jnp.int32
    )
    same_owner = row_global[:, None] // params == column_global[None, :] // params
    cross_part = jnp.where(same_owner, 0.0, owned_block)
    return (cross_part * cross_factor, right_own * factor, blocks_own * factor)


def solution(mesh):
    placed = (
        P(("sta", "sat"), None, None, None),
        P(("sta", "sat"), None, None),
        P(("sta", "sat"), None, None),
        P(("sta", "sat"), None, None),
        P(("sta", "sat"), None),
        P(("sta", "sat"), None),
        P("sat", None, None, None),
    )
    return jax.shard_map(
        shards,
        mesh=mesh,
        in_specs=placed,
        out_specs=(P("sat", "sta"), P("sat"), P("sat", None, None)),
        check_vma=False,
    )
```

profile of v0, /device:TPU:0, one launch (start us, length us, event | category | flops | bytes accessed | tf_op | source)
XLA Modules:
  0.0 293.2 jit_solution(9909130253294771036)
XLA Ops:
  7.2 0.7 all-gather.2.cloned.1.call-update
  8.0 31.7 %all-gather.2.cloned.1.call-done = f32[120,3,8,256]{3,2,1,0:T(8,128)} async-done(((f32[30,3,8,256]{3,2,1,0:T(8,128)}), f32[120,3,8,256]{3,2,1,0:T(8,128)}) %all-gather.2.cloned.1.call-update) | async-done | bytes 2949136 | tf_op jit(solution)/shard_map/all_gather | solution.py:85
  39.7 54.2 %while.18 = (s32[]{:T(128)}, f32[960,960]{0,1:T(8,128)}, f32[960]{0:T(1024)S(1)}, s32[2,32]{1,0:T(2,128)}, f32[2,3,32,256]{3,2,1,0:T(8,128)}, /*index=5*/f32[120...) while((s32[]{:T(128)}, f32[960,960]{0,1:T(8,128)}, ...), condition=%wide.region_8.9_spmd.clone, body=%wide.region_0.8_spmd.clone.sunk | while | flops 861211008 | bytes 36746156 | solution.py:110
  39.7 0.7 fusion.77
  40.4 2.4 gather_fusion
  42.8 0.9 dynamic-slice_bitcast_fusion.6
  43.8 0.7 compare_and_fusion.2
  44.5 0.1 multiply_reduce_fusion.7
  44.7 0.8 multiply_reduce_fusion.8
  45.5 0.8 convert_reduce_fusion.2
  46.3 0.7 constant_dynamic-slice_fusion.3
  47.0 0.2 fusion.78
  47.2 0.2 fusion.79
  47.4 0.5 fusion.80
  47.9 0.4 convolution_select_fusion.2
  48.3 0.4 fusion.81
  48.8 0.7 fusion.82
  49.5 0.2 reshape.423
  49.6 0.3 copy.40
  50.0 0.5 reshape.424
  50.4 3.6 %fusion.83 = f32[120,7680]{1,0:T(8,128)} fusion(f32[32,7680]{1,0:T(8,128)S(1)} %reshape.424, s32[32]{0:T(128)S(1)} %get-tuple-element.412), kind=kOutput, calls=%fused_computation.42.clone.1 | convolution fusion | flops 353898240 | bytes 4669568 | tf_op jit(solution)/shard_map/while/body/eval_jaxpr/dot_general | solution.py:77
  54.0 5.8 %reshape.425 = f32[960,960]{1,0:T(8,128)} reshape(f32[120,7680]{1,0:T(8,128)} %fusion.83) | data formatting | bytes 7372800 | tf_op jit(solution)/shard_map/while/body/eval_jaxpr/reshape | solution.py:77
  59.8 5.3 %bitcast_add_fusion.2 = f32[960,960]{0,1:T(8,128)} fusion(f32[960,960]{1,0:T(8,128)} %reshape.425, f32[960,960]{0,1:T(8,128)} %get-tuple-element.429, pred[]{:T(512)S(6)} %compare.27), kind=kLoop, calls=%fused_computation.2.clone.1 | loop fusion | flops 1843200 | bytes 11059201 | tf_op jit(solution)/shard_map/while/body/eval_jaxpr/add | solution.py:104
  65.1 0.1 fusion.84
  65.3 0.1 convolution_bitcast_fusion.3
  65.4 0.2 fusion.85
  65.7 0.4 fusion.86
  66.1 0.1 reshape.427
  66.2 0.7 fusion.77
  66.9 2.4 gather_fusion
  69.4 0.9 dynamic-slice_bitcast_fusion.6
  70.3 0.7 compare_and_fusion.2
  71.0 0.1 multiply_reduce_fusion.7
  71.2 0.8 multiply_reduce_fusion.8
  72.0 0.8 convert_reduce_fusion.2
  72.8 0.7 constant_dynamic-slice_fusion.3
  73.5 0.2 fusion.78
  73.7 0.2 fusion.79
  73.9 0.5 fusion.80
  74.4 0.4 convolution_select_fusion.2
  74.8 0.4 fusion.81
  75.3 0.7 fusion.82
  76.0 0.2 reshape.423
  76.1 0.3 copy.40
  76.5 0.5 reshape.424
  77.0 3.6 %fusion.83 = f32[120,7680]{1,0:T(8,128)} fusion(f32[32,7680]{1,0:T(8,128)S(1)} %reshape.424, s32[32]{0:T(128)S(1)} %get-tuple-element.412), kind=kOutput, calls=%fused_computation.42.clone.1 | convolution fusion | flops 353898240 | bytes 4669568 | tf_op jit(solution)/shard_map/while/body/eval_jaxpr/dot_general | solution.py:77
  80.5 5.8 %reshape.425 = f32[960,960]{1,0:T(8,128)} reshape(f32[120,7680]{1,0:T(8,128)} %fusion.83) | data formatting | bytes 7372800 | tf_op jit(solution)/shard_map/while/body/eval_jaxpr/reshape | solution.py:77
  86.3 6.5 %bitcast_add_fusion.2 = f32[960,960]{0,1:T(8,128)} fusion(f32[960,960]{1,0:T(8,128)} %reshape.425, f32[960,960]{0,1:T(8,128)} %get-tuple-element.429, pred[]{:T(512)S(6)} %compare.27), kind=kLoop, calls=%fused_computation.2.clone.1 | loop fusion | flops 1843200 | bytes 11059201 | tf_op jit(solution)/shard_map/while/body/eval_jaxpr/add | solution.py:104
  92.8 0.1 fusion.84
  93.0 0.1 convolution_bitcast_fusion.3
  93.2 0.2 fusion.85
  93.5 0.4 fusion.86
  93.8 0.1 reshape.427
  93.9 5.2 %copy.28 = f32[960,960]{1,0:T(8,128)} copy(f32[960,960]{0,1:T(8,128)} %get-tuple-element.247) | data formatting | bytes 7372800 | tf_op jit(solution)/shard_map/while | solution.py:110
  99.2 43.0 %reduce-scatter.5.cloned.1.call-done = f32[240,960]{1,0:T(8,128)} async-done(((f32[960,960]{1,0:T(8,128)}), f32[240,960]{1,0:T(8,128)}) %reduce-scatter.5.cloned.1.call-update) | async-done | bytes 921616 | tf_op jit(solution)/shard_map/reduce_scatter | solution.py:114
  142.2 2.5 copy.35
  144.8 31.4 %reshape.409 = f32[120,8,120,8]{1,0,3,2:T(8,128)} reshape(f32[960,960]{0,1:T(8,128)} %get-tuple-element.247) | data formatting | bytes 7372800 | tf_op jit(solution)/shard_map/reshape | solution.py:117
  176.2 58.9 %copy.30 = f32[120,8,120,8]{3,1,2,0:T(8,128)} copy(f32[120,8,120,8]{1,0,3,2:T(8,128)} %reshape.409) | data formatting | bytes 7372800 | tf_op jit(solution)/shard_map/reshape | solution.py:117
  235.1 2.3 gather_fusion.1
  237.3 46.1 %all-reduce = (f32[960]{0:T(1024)S(1)}, f32[120,8,8]{2,1,0:T(8,128)S(1)}) all-reduce(f32[960]{0:T(1024)S(1)} %get-tuple-element.248, f32[120,8,8]{2,1,0:T(8,128)S(1)} %gather_fusion.1), channel_id=1, replica_groups=mesh['sta'=8,'sat'=4] {'sta','sat'}, use_global_device_ids=true, to_apply=%region_11.12 | all-reduce | flops 8640 | bytes 69120 | tf_op jit(solution)/shard_map/psum | solution.py:119
  283.5 0.7 copy.31
  284.2 0.6 dynamic-slice_multiply_fusion.1
  284.9 1.0 copy.36
  285.9 0.8 select_multiply_fusion
  (30 shorter events, 0.8 us)
Async XLA Ops:
  7.2 32.5 %all-gather.2.cloned.1.call-start = ((), (), s32[]{:S(2)}) async-start(), calls=%async_computation.2 | async-start | bytes 3686400 | tf_op jit(solution)/shard_map/all_gather | solution.py:85
  7.9 134.3 %reduce-scatter.5.cloned.1.call-start = ((), (), s32[]{:S(2)}) async-start(), calls=%async_computation.3 | async-start | bytes 4915200 | tf_op jit(solution)/shard_map/reduce_scatter | solution.py:114
  99.1 185.8 %reduce-scatter.7.cloned.1.call-start = ((), (), s32[]{:S(2)}) async-start(), calls=%async_computation.4 | async-start | bytes 1105920
Sparse Core Ops, SparseCore 0:
  9.6 30.1 all-gather.1
  99.2 42.9 reduce-scatter.4
  145.9 63.3 reduce-scatter.6
where the time goes:
time: 296 us; the launch traced here: 293 us
  local copies, waits for them, and re-layouts  124 us (42%)
  waiting for transfers between devices  75.5 us (26%)
  blocking collectives  46.1 us (16%)
  other arithmetic  19.8 us (7%)
  between operations  13.8 us (5%)
  matrix products  13.2 us (4%)
    reshape x2, local copies, waits for them, and re-layouts, shards(): normal_sum.reshape(sats, params, sats, params)  90.3 us
    psum x1, blocking collectives, shards(): right_all, blocks_all = lax.psum((right_sum, diagonal_part), ('sta', 'sat'))  46.1 us
    reduce_scatter x1, waiting for transfers between devices, shards(): lax.psum_scatter(normal_sum, 'sat', scatter_dimension=0, tiled=True)  43 us
    all_gather x1, waiting for transfers between devices, shards(): all_orbit = lax.all_gather(orbit, 'sat', axis=0, tiled=True)  31.7 us
    add x4, other arithmetic, visit(): return (normal_sum + spread, right_sum + right_spread)  11.8 us
    reshape x2, local copies, waits for them, and re-layouts, spread_blocks(): jnp.dot(select.T, left_turned, precision=HIGH)  11.7 us
    dot_general x2, matrix products, spread_blocks(): jnp.dot(select.T, left_turned, precision=HIGH)  7.11 us
  transfers between devices with their start and end apart: 3, of which 2 were waited for; matrix products, arithmetic and copies ran while one was open for 32% of the time, Pallas kernels for 0%

commit v1 on v0

v1 whole, which is shorter than its diff:
```python
import functools

import jax
import jax.numpy as jnp
from jax import lax
from jax.experimental import pallas as pl
from jax.experimental.pallas import tpu as pltpu
from jax.sharding import PartitionSpec as P

KNOTS = 4
PRIOR = 1.0
HIGH = lax.Precision.HIGH
HIGHEST = lax.Precision.HIGHEST
PLANES = 6
VMEM_LIMIT = 56 * 1024 * 1024
NT = (((1,), (1,)), ((), ()))


def vmem():
    return pl.BlockSpec(memory_space=pltpu.VMEM)


def smem():
    return pl.BlockSpec(memory_space=pltpu.SMEM)


def anywhere():
    return pl.BlockSpec(memory_space=pl.ANY)


def prepare_kernel(sight, mapping, residual, counts, knots, planes):
    stations, _, tracked, _ = sight.shape
    for s in range(stations):
        weight = counts[s].astype(jnp.float32)
        total = jnp.maximum(jnp.sum(weight, 0, keepdims=True), 1.0)
        root = jnp.sqrt(total)
        scaled = weight / root
        for c in range(3):
            planes[s, c * tracked : (c + 1) * tracked, :] = sight[s, c] * scaled
        map_mean = jnp.sum(weight * mapping[s], 0, keepdims=True) / total
        res_mean = jnp.sum(weight * residual[s], 0, keepdims=True) / total
        map_off = mapping[s] - map_mean
        res_off = residual[s] - res_mean
        weighted_off = weight * map_off
        map_square = jnp.sum(weighted_off * map_off, 0, keepdims=True)
        map_res = jnp.sum(weighted_off * res_off, 0, keepdims=True)
        knot = knots[s : s + 1, :]
        inverse = jnp.zeros_like(total)
        right = jnp.zeros_like(total)
        for k in range(KNOTS):
            select = (knot == k).astype(jnp.float32)
            diagonal = jnp.sum(select * map_square, 1, keepdims=True) + PRIOR
            root_inverse = 1.0 / jnp.sqrt(diagonal)
            local = jnp.sum(select * map_res, 1, keepdims=True)
            inverse = inverse + select * root_inverse
            right = right + select * (local * root_inverse)
        tropo = map_off * (root * inverse)
        planes[s, 3 * tracked : 4 * tracked, :] = tropo
        planes[s, 4 * tracked : 5 * tracked, :] = res_off * root - tropo * right
        planes[s, 5 * tracked : 6 * tracked, :] = jnp.where(
            weight > 0.0, total / jnp.maximum(weight, 1.0), 0.0
        )
        planes[s, 6 * tracked :, :] = jnp.broadcast_to(
            knot.astype(jnp.float32), (8, knot.shape[1])
        )


def prepare(sight, mapping, residual, counts, knots):
    stations, _, tracked, epochs = sight.shape
    return pl.pallas_call(
        prepare_kernel,
        out_shape=jax.ShapeDtypeStruct(
            (stations, PLANES * tracked + 8, epochs), jnp.float32
        ),
        in_specs=[vmem()] * 5,
        out_specs=vmem(),
        compiler_params=pltpu.CompilerParams(vmem_limit_bytes=VMEM_LIMIT),
        name="prepare",
    )(sight, mapping, residual, counts, knots)


def main_kernel(groups, per, own, nx, nz, window, *refs):
    tracks = refs[:groups]
    meta = refs[groups]
    plane_pieces = refs[groups + 1 : 2 * groups + 1]
    orbit_pieces = refs[2 * groups + 1 : 3 * groups + 1]
    outs = refs[3 * groups + 1 : 3 * groups + 1 + nx]
    (track, planes, orbit, acc, compact, tropo, product, dense, factor, dense_tropo, rights,
     blocks, sems) = refs[3 * groups + 1 + nx :]
    tracked = compact.shape[0]
    epochs = compact.shape[2]
    width = acc.shape[2]
    first = meta[0]

    copies = []
    for d in range(groups):
        copies.append(pltpu.make_async_copy(
            orbit_pieces[d], orbit.at[pl.ds(meta[1 + d], own)], sems.at[2 * d]))
        copies.append(pltpu.make_async_copy(
            plane_pieces[d], planes.at[pl.ds(d * per, per)], sems.at[2 * d + 1]))
    for copy in copies:
        copy.start()
    for d in range(groups):
        for s in range(per):
            for m in range(tracked):
                track[d * per + s, m] = tracks[d][s, m]
    acc[...] = jnp.zeros_like(acc)
    rights[...] = jnp.zeros_like(rights)
    blocks[...] = jnp.zeros_like(blocks)
    for copy in copies:
        copy.wait()

    def visit(s, carry):
        dense[...] = jnp.zeros_like(dense)
        factor[...] = jnp.zeros_like(factor)
        dense_tropo[...] = jnp.zeros_like(dense_tropo)
        for m in range(tracked):
            k = track[s, m]
            local = k - first
            inside = jnp.logical_and(local >= 0, local < own)
            place = jnp.where(inside, local, own)

            def row(plane):
                return planes[s, pl.ds(plane * tracked + m, 1), :]

            value = row(0) * orbit[k, 0] + row(1) * orbit[k, 1] + row(2) * orbit[k, 2]
            compact[m] = value
            tropo[m] = value * row(3)
            dense[place] = value
            factor[place] = value * row(5)
            rights[place] = rights[place] + value * row(4)
        knot = planes[s, pl.ds(PLANES * tracked, 1), :]
        lanes = lax.broadcasted_iota(jnp.int32, (128, epochs), 0).astype(jnp.float32)
        select = (lanes == knot).astype(jnp.float32)
        span = tracked * 8
        mixed = lax.dot_general(tropo[...].reshape(span, epochs), select, NT, precision=HIGH,
                                preferred_element_type=jnp.float32)
        product[:, :, :128] = mixed.reshape(tracked, 8, 128)
        for m in range(tracked):
            local = track[s, m] - first
            inside = jnp.logical_and(local >= 0, local < own)
            dense_tropo[jnp.where(inside, local, own)] = product[m, :, :128]
        rows = dense[...].reshape((own + 2) * 8, epochs)[:width]
        rows_factor = factor[...].reshape((own + 2) * 8, epochs)[:width]
        rows_tropo = dense_tropo[...].reshape((own + 2) * 8, 128)[:width]
        result = lax.dot_general(compact[...].reshape(span, epochs), rows, NT, precision=HIGH,
                                 preferred_element_type=jnp.float32)
        result = result + lax.dot_general(mixed, rows_tropo, NT, precision=HIGH,
                                          preferred_element_type=jnp.float32)
        blocks[...] = blocks[...] + lax.dot_general(
            rows, rows_factor, NT, precision=HIGH, preferred_element_type=jnp.float32)
        product[...] = result.reshape(tracked, 8, width)
        for m in range(tracked):
            k = track[s, m]
            acc[k] = acc[k] - product[m]
        return carry

    lax.fori_loop(0, groups * per, visit, 0)

    span = own * 8
    lane_owner = lax.broadcasted_iota(jnp.int32, (8, width), 1) // 8
    small = jnp.zeros((8, width), jnp.float32)
    for o in range(own):
        tile = acc[first + o] + blocks[o * 8 : o * 8 + 8, :]
        small = small + jnp.where(lane_owner == o, tile, 0.0)
    right_rows = rights[...].reshape((own + 2) * 8, epochs)[:width]
    right = lax.dot_general(jnp.ones((8, epochs), jnp.float32), right_rows, NT,
                            precision=HIGHEST, preferred_element_type=jnp.float32)
    for dx in range(nx):
        for dz in range(nz):
            start = meta[1 + groups + dx * nz + dz]
            outs[dx][dz * window : (dz + 1) * window] = acc[pl.ds(start, window)]
        outs[dx][nz * window] = small
        outs[dx][nz * window + 1] = right


def accumulate(tracks, meta, planes, orbits, sats, nx, nz, window, width):
    groups = len(planes)
    per, rows, epochs = planes[0].shape
    tracked = tracks[0].shape[1]
    own = orbits[0].shape[0]
    out = jax.ShapeDtypeStruct((nz * window + 2, 8, width), jnp.float32)
    return pl.pallas_call(
        functools.partial(main_kernel, groups, per, own, nx, nz, window),
        out_shape=[out] * nx,
        in_specs=[smem()] * (groups + 1) + [anywhere()] * (2 * groups),
        out_specs=[vmem()] * nx,
        scratch_shapes=[
            pltpu.SMEM((groups * per, tracked), jnp.int32),
            pltpu.VMEM((groups * per, rows, epochs), jnp.float32),
            pltpu.VMEM((sats,) + orbits[0].shape[1:], jnp.float32),
            pltpu.VMEM((sats, 8, width), jnp.float32),
            pltpu.VMEM((tracked, 8, epochs), jnp.float32),
            pltpu.VMEM((tracked, 8, epochs), jnp.float32),
            pltpu.VMEM((tracked, 8, width), jnp.float32),
            pltpu.VMEM((own + 2, 8, epochs), jnp.float32),
            pltpu.VMEM((own + 2, 8, epochs), jnp.float32),
            pltpu.VMEM((own + 2, 8, 128), jnp.float32),
            pltpu.VMEM((own + 2, 8, epochs), jnp.float32),
            pltpu.VMEM((width, width), jnp.float32),
            pltpu.SemaphoreType.DMA((2 * groups,)),
        ],
        compiler_params=pltpu.CompilerParams(vmem_limit_bytes=VMEM_LIMIT),
        name="accumulate",
    )(*tracks, meta, *planes, *orbits)


def combine_kernel(nx, nz, window, *refs):
    pieces = refs[:nx]
    outs = refs[nx:]
    small = pieces[0][nz * window :]
    for piece in pieces[1:]:
        small = small + piece[nz * window :]
    for dz in range(nz):
        part = pieces[0][dz * window : (dz + 1) * window]
        for piece in pieces[1:]:
            part = part + piece[dz * window : (dz + 1) * window]
        outs[dz][:window] = part
        outs[dz][window:] = small


def combine(pieces, nz, window):
    nx = len(pieces)
    width = pieces[0].shape[2]
    out = jax.ShapeDtypeStruct((window + 2, 8, width), jnp.float32)
    return pl.pallas_call(
        functools.partial(combine_kernel, nx, nz, window),
        out_shape=[out] * nz,
        in_specs=[vmem()] * nx,
        out_specs=[vmem()] * nz,
        compiler_params=pltpu.CompilerParams(vmem_limit_bytes=VMEM_LIMIT),
        name="combine",
    )(*pieces)


def finish_kernel(nz, window, own, factor, cross_factor, meta, *refs):
    pieces = refs[:nz]
    normal, right, blocks = refs[nz:]
    width = pieces[0].shape[2]
    total = pieces[0][...]
    for piece in pieces[1:]:
        total = total + piece[...]
    first, start = meta[0], meta[1]
    span = own * 8
    part = total[:window].reshape(window * 8, width)
    row_owner = start + lax.broadcasted_iota(jnp.int32, part.shape, 0) // 8
    lane_owner = first + lax.broadcasted_iota(jnp.int32, part.shape, 1) // 8
    part = jnp.where(row_owner == lane_owner, 0.0, part * cross_factor)
    normal[...] = part.T[:span, :]
    right[...] = total[window + 1, :1, :span] * factor
    small = total[window]
    lane = lax.broadcasted_iota(jnp.int32, (width, own), 0)
    wanted = lax.broadcasted_iota(jnp.int32, (width, own), 1) * 8
    for p in range(8):
        pick = (lane == wanted + p).astype(jnp.float32)
        blocks[p] = factor * jnp.dot(small, pick, precision=HIGHEST,
                                     preferred_element_type=jnp.float32)


def finish(meta, pieces, window, own, factor, cross_factor):
    nz = len(pieces)
    return pl.pallas_call(
        functools.partial(finish_kernel, nz, window, own, factor, cross_factor),
        out_shape=[
            jax.ShapeDtypeStruct((own * 8, window * 8), jnp.float32),
            jax.ShapeDtypeStruct((1, own * 8), jnp.float32),
            jax.ShapeDtypeStruct((8, 8, own), jnp.float32),
        ],
        in_specs=[smem()] + [vmem()] * nz,
        out_specs=[vmem()] * 3,
        compiler_params=pltpu.CompilerParams(vmem_limit_bytes=VMEM_LIMIT),
        name="finish",
    )(meta, *pieces)


def shift(value, axis, size, step):
    return lax.ppermute(value, axis, [(i, i ^ step) for i in range(size)])


def gather_pieces(value, size):
    pieces = [None] * size
    pieces[0] = value
    for d in range(2, size, 2):
        pieces[d] = shift(value, "sat", size, d)
    for d in range(0, size, 2):
        pieces[d + 1] = shift(pieces[d], "sat", size, 1)
    return pieces


def shards(sight, mapping, residual, counts, track, knots, orbit):
    group = lax.axis_size("sat")
    columns_axis = lax.axis_size("sta")
    nx = 1 << ((columns_axis.bit_length()) // 2 - (0 if columns_axis.bit_length() % 2 else 1))
    nz = columns_axis // nx
    own, _, params, epochs = orbit.shape
    stations, _, tracked, _ = sight.shape
    sats = own * group
    span = sats * params
    columns = span // columns_axis
    width = -(-(own * params) // 128) * 128
    me = lax.axis_index("sat").astype(jnp.int32)
    mine = lax.axis_index("sta").astype(jnp.int32)

    window = max(
        -(-(((columns * i) % 8) + columns) // 8) for i in range(columns_axis)
    )

    def window_start(i):
        return jnp.minimum(i * columns // 8, sats - window)

    meta = [me * own]
    for d in range(group):
        meta.append((me ^ d) * own)
    for dx in range(nx):
        for dz in range(nz):
            meta.append(window_start(mine ^ (dz * nx + dx)))
    meta = jnp.stack(meta)

    planes = prepare(sight, mapping, residual, counts, knots)
    orbit_pieces = gather_pieces(orbit, group)
    track_pieces = gather_pieces(track, group)
    plane_pieces = gather_pieces(planes, group)
    parts = accumulate(track_pieces, meta, plane_pieces, orbit_pieces, sats, nx, nz, window, width)
    arrived = [parts[0]] + [
        shift(parts[d], "sta", columns_axis, d) for d in range(1, nx)
    ]
    chunks = combine(arrived, nz, window)
    final = [chunks[0]] + [
        shift(chunks[d], "sta", columns_axis, d * nx) for d in range(1, nz)
    ]
    total_stations = stations * columns_axis * group
    factor = sats / (total_stations * tracked * epochs)
    cross_factor = sats / (total_stations * epochs) ** 0.5
    start = window_start(mine)
    normal, right, blocks = finish(
        jnp.stack([me * own, start]), final, window, own, factor, cross_factor
    )
    if window * 8 != columns:
        normal = lax.dynamic_slice_in_dim(normal, mine * columns - start * 8, columns, 1)
    return normal, right.reshape(own * params), jnp.transpose(blocks, (2, 0, 1))


def solution(mesh):
    placed = (
        P(("sta", "sat"), None, None, None),
        P(("sta", "sat"), None, None),
        P(("sta", "sat"), None, None),
        P(("sta", "sat"), None, None),
        P(("sta", "sat"), None),
        P(("sta", "sat"), None),
        P("sat", None, None, None),
    )
    return jax.shard_map(
        shards,
        mesh=mesh,
        in_specs=placed,
        out_specs=(P("sat", "sta"), P("sat"), P("sat", None, None)),
        check_vma=False,
    )
```

time: 296 us -> 85.9 us (0.29)
  local copies, waits for them, and re-layouts: 124 us -> 4.41 us
  blocking collectives: 46.1 us -> 0 us
  waiting for transfers between devices: 75.5 us -> 48.1 us
  Pallas kernels: 0 us -> 19.7 us
  other arithmetic: 19.8 us -> 0.61 us
  matrix products: 13.2 us -> 0 us
  between operations: 13.8 us -> 0.74 us
  starting transfers between devices: 0.12 us -> 12.1 us
    reshape x16 -> x0, local copies, waits for them, and re-layouts: 104 us -> none  [the longest x2 90.3 us: shards(): normal_sum.reshape(sats, params, sats, params)]
    ppermute x0 -> x13, waiting for transfers between devices: none -> 48.1 us  [shift(): return lax.ppermute(value, axis, [(i, i ^ step) for i in range(size)])]
    psum x1 -> x0, blocking collectives: 46.1 us -> none  [shards(): right_all, blocks_all = lax.psum((right_sum, diagonal_part), ('sta', 'sat'))]
    reduce_scatter x1 -> x0, waiting for transfers between devices: 43 us -> none  [shards(): lax.psum_scatter(normal_sum, 'sat', scatter_dimension=0, tiled=True)]
    all_gather x1 -> x0, waiting for transfers between devices: 31.7 us -> none  [shards(): all_orbit = lax.all_gather(orbit, 'sat', axis=0, tiled=True)]
    pallas_call x0 -> x4, Pallas kernels: none -> 19.7 us  [the longest x1 13.4 us: accumulate(): pl.pallas_call(functools.partial(main_kernel, groups, per, own, nx, nz, w...]
    dot_general x20 -> x0, matrix products: 13.2 us -> none  [the longest x2 7.11 us: spread_blocks(): jnp.dot(select.T, left_turned, precision=HIGH)]
    ppermute x0 -> x13, starting transfers between devices: none -> 12.1 us  [shift(): return lax.ppermute(value, axis, [(i, i ^ step) for i in range(size)])]
  transfers between devices with their start and end apart: 3 -> 13, of which waited for: 2 -> 7; matrix products, arithmetic and copies ran while one was open for 32% -> 1% of each run, Pallas kernels for 0% -> 2%
where the time goes in v1:
time: 85.9 us; the launch traced here: 85.7 us
  waiting for transfers between devices  48.1 us (56%)
  Pallas kernels  19.7 us (23%)
  starting transfers between devices  12.1 us (14%)
  local copies, waits for them, and re-layouts  4.41 us (5%)
    ppermute x13, waiting for transfers between devices, shift(): return lax.ppermute(value, axis, [(i, i ^ step) for i in range(size)])  48.1 us
    pallas_call x1, Pallas kernels, accumulate(): pl.pallas_call(functools.partial(main_kernel, groups, per, own, nx, nz, w...  13.4 us
    ppermute x13, starting transfers between devices, shift(): return lax.ppermute(value, axis, [(i, i ^ step) for i in range(size)])  12.1 us
    unnamed x26, local copies, waits for them, and re-layouts  3.8 us
    pallas_call x1, Pallas kernels, finish(): pl.pallas_call(functools.partial(finish_kernel, nz, window, own, factor,...  2.35 us
    pallas_call x1, Pallas kernels, combine(): pl.pallas_call(functools.partial(combine_kernel, nx, nz, window), out_sha...  2.02 us
    pallas_call x1, Pallas kernels, prepare(): pl.pallas_call(prepare_kernel, out_shape=jax.ShapeDtypeStruct((stations,...  1.93 us
  transfers between devices with their start and end apart: 13, of which 7 were waited for; matrix products, arithmetic and copies ran while one was open for 1% of the time, Pallas kernels for 2%

profile of v1, /device:TPU:0, one launch (start us, length us, event | category | flops | bytes accessed | tf_op | source)
XLA Modules:
  0.0 85.7 jit_solution(17015984433545316946)
XLA Ops:
  0.6 0.0 copy-start
  0.6 0.0 copy-start.9
  0.7 3.0 %collective-permute-start.7 = (f32[30,3,8,256]{3,2,1,0:T(8,128)}, f32[30,3,8,256]{3,2,1,0:T(8,128)S(1)}, u32[]{:S(2)}, u32[]{:S(2)}) collective-permute-start(f32[30,3,8,256]{3,2,1,0:T(8,128)} %refs_9_.1), channel_id=1, source_target_pairs={{0,2},{1,3},{2,0},{3,1},{4,6},{5,7},{6,4},{7,5},{8,10},{9,11},{10,... | collective-permute-start | bytes 2211848 | tf_op jit(solution)/shard_map/ppermute | solution.py:277
  3.7 1.9 %prepare.1.refs_5_ = f32[2,200,256]{2,1,0:T(8,128)} custom-call(f32[2,3,32,256]{3,2,1,0:T(8,128)} %sight.1, f32[2,32,256]{2,1,0:T(8,128)} %mapping.1, f32[2,32,256]{2,1,0:T(8,128)} %residual.1, s32[2,32,256]{2,1,0:T(8,128)} %counts.1, s32[2,256]{1,0:T(2,128)} %knots.1), custom_call_target="tpu_custom_call" | custom-call | tf_op jit(solution)/shard_map/prepare/pallas_call | solution.py:70
  5.6 0.1 collective-permute-start.4
  5.7 0.0 copy-done
  5.7 0.0 collective-permute-start.6
  5.7 15.5 %collective-permute-done.7.refs_11_ = f32[30,3,8,256]{3,2,1,0:T(8,128)S(1)} collective-permute-done((f32[30,3,8,256]{3,2,1,0:T(8,128)}, f32[30,3,8,256]{3,2,1,0:T(8,128)S(1)}, u32[]{:S(2)}, u32[]{:S(2)}) %collective-permute-start.7) | collective-permute-done | bytes 737312 | tf_op jit(solution)/shard_map/ppermute | solution.py:277
  21.2 0.0 copy-start.1
  21.2 0.0 collective-permute-start.8
  21.2 0.5 collective-permute-start.3
  21.7 7.4 %collective-permute-done.4.refs_7_ = f32[2,200,256]{2,1,0:T(8,128)S(1)} collective-permute-done((f32[2,200,256]{2,1,0:T(8,128)}, f32[2,200,256]{2,1,0:T(8,128)S(1)}, u32[]{:S(2)}, u32[]{:S(2)}) %collective-permute-start.4) | collective-permute-done | bytes 409632 | tf_op jit(solution)/shard_map/ppermute | solution.py:277
  29.2 0.0 copy-start.5
  29.2 0.0 collective-permute-start.5
  29.2 0.0 copy-done.9
  29.2 0.5 collective-permute-start
  29.7 1.2 %collective-permute-done.refs_1_ = s32[2,32]{1,0:T(2,128)S(1)} collective-permute-done((s32[2,32]{1,0:T(2,128)S(1)}, s32[2,32]{1,0:T(2,128)S(1)}, u32[]{:S(2)}, u32[]{:S(2)}) %collective-permute-start) | collective-permute-done | bytes 288 | tf_op jit(solution)/shard_map/ppermute | solution.py:277
  30.9 0.0 copy-start.10
  30.9 1.7 %collective-permute-start.1 = (s32[2,32]{1,0:T(2,128)S(1)}, s32[2,32]{1,0:T(2,128)S(1)}, u32[]{:S(2)}, u32[]{:S(2)}) collective-permute-start(s32[2,32]{1,0:T(2,128)S(1)} %copy-done.9), channel_id=1, source_target_pairs={{0,2},{1,3},{2,0},{3,1},{4,6},{5,7},{6,4},{7,5},{8,10},{9,11},{10,... | collective-permute-start | bytes 776 | tf_op jit(solution)/shard_map/ppermute | solution.py:277
  32.6 0.0 copy-done.10
  32.6 1.8 %collective-permute-done.1.refs_2_ = s32[2,32]{1,0:T(2,128)S(1)} collective-permute-done((s32[2,32]{1,0:T(2,128)S(1)}, s32[2,32]{1,0:T(2,128)S(1)}, u32[]{:S(2)}, u32[]{:S(2)}) %collective-permute-start.1) | collective-permute-done | bytes 288 | tf_op jit(solution)/shard_map/ppermute | solution.py:277
  34.5 0.0 copy-start.11
  34.5 0.0 collective-permute-start.2
  34.5 0.6 copy-done.11
  35.0 0.6 stack.58.refs_4_
  35.6 0.0 collective-permute-done.2.refs_3_
  35.6 0.0 copy-start.12
  35.6 0.0 collective-permute-done.3.refs_6_
  35.7 0.0 collective-permute-done.6.refs_10_
  35.7 0.0 copy-start.2
  35.7 0.0 collective-permute-done.5.refs_8_
  35.7 0.0 collective-permute-done.8.refs_12_
  35.7 0.0 copy-done.1
  35.7 0.0 copy-done.5
  35.7 0.5 copy-done.12
  36.2 0.4 copy-done.2
  36.6 0.0 copy-start.3
  36.6 0.9 %copy-done.3 = f32[30,3,8,256]{3,2,1,0:T(8,128)} copy-done((f32[30,3,8,256]{3,2,1,0:T(8,128)}, f32[30,3,8,256]{3,2,1,0:T(8,128)S(1)}, u32[]{:S(2)}) %copy-start.3) | copy-done | bytes 737304
  37.4 13.4 %accumulate.1 = (f32[62,8,256]{2,1,0:T(8,128)}, f32[62,8,256]{2,1,0:T(8,128)}) custom-call(s32[2,32]{1,0:T(2,128)} %refs_0_.1, s32[2,32]{1,0:T(2,128)} %copy-done.10, s32[2,32]{1,0:T(2,128)} %copy-done.11, s32[2,32]{1,0:T(2,128)} %copy-done.12, s32[13]{0:T(128)} %stack.58.refs_4_, f32[2,200,256]{2,1,0:T(8,128)} %prepare.1.refs_5_, ...), custom_call_target="tpu_custom_call" | custom-call | tf_op jit(solution)/shard_map/accumulate/pallas_call | solution.py:183
  50.9 1.8 %collective-permute-start.9 = (f32[62,8,256]{2,1,0:T(8,128)}, f32[62,8,256]{2,1,0:T(8,128)S(1)}, u32[]{:S(2)}, u32[]{:S(2)}) collective-permute-start(f32[62,8,256]{2,1,0:T(8,128)} %get-tuple-element.13), channel_id=1, source_target_pairs={{0,4},{4,0},{8,12},{12,8},{16,20},{20,16},{24,28},{28,24},{1,5},{5... | collective-permute-start | bytes 1523720 | tf_op jit(solution)/shard_map/ppermute | solution.py:277
  52.7 12.1 %collective-permute-done.9.refs_1_ = f32[62,8,256]{2,1,0:T(8,128)S(1)} collective-permute-done((f32[62,8,256]{2,1,0:T(8,128)}, f32[62,8,256]{2,1,0:T(8,128)S(1)}, u32[]{:S(2)}, u32[]{:S(2)}) %collective-permute-start.9) | collective-permute-done | bytes 507936 | tf_op jit(solution)/shard_map/ppermute | solution.py:277
  64.7 0.0 copy-start.4
  64.8 0.8 copy-done.4
  65.6 2.0 %combine.1 = (f32[17,8,256]{2,1,0:T(8,128)}, f32[17,8,256]{2,1,0:T(8,128)}, f32[17,8,256]{2,1,0:T(8,128)}, f32[17,8,256]{2,1,0:T(8,128)}) custom-call(f32[62,8,256]{2,1,0:T(8,128)} %get-tuple-element.12.refs_0_, f32[62,8,256]{2,1,0:T(8,128)} %copy-done.4), custom_call_target="tpu_custom_call" | custom-call | tf_op jit(solution)/shard_map/combine/pallas_call | solution.py:226
  67.6 1.8 %collective-permute-start.10 = (f32[17,8,256]{2,1,0:T(8,128)}, f32[17,8,256]{2,1,0:T(8,128)S(1)}, u32[]{:S(2)}, u32[]{:S(2)}) collective-permute-start(f32[17,8,256]{2,1,0:T(8,128)} %get-tuple-element.15), channel_id=1, source_target_pairs={{0,8},{4,12},{8,0},{12,4},{16,24},{20,28},{24,16},{28,20},{1,9},{5... | collective-permute-start | bytes 417800 | tf_op jit(solution)/shard_map/ppermute | solution.py:277
  69.4 2.6 %collective-permute-start.11 = (f32[17,8,256]{2,1,0:T(8,128)}, f32[17,8,256]{2,1,0:T(8,128)S(1)}, u32[]{:S(2)}, u32[]{:S(2)}) collective-permute-start(f32[17,8,256]{2,1,0:T(8,128)} %get-tuple-element.16), channel_id=1, source_target_pairs={{0,16},{4,20},{8,24},{12,28},{16,0},{20,4},{24,8},{28,12},{1,17},{... | collective-permute-start | bytes 417800 | tf_op jit(solution)/shard_map/ppermute | solution.py:277
  72.0 0.0 collective-permute-start.12
  72.0 0.6 pad_add_fusion.meta
  72.6 1.8 %collective-permute-done.10.refs_1_ = f32[17,8,256]{2,1,0:T(8,128)S(1)} collective-permute-done((f32[17,8,256]{2,1,0:T(8,128)}, f32[17,8,256]{2,1,0:T(8,128)S(1)}, u32[]{:S(2)}, u32[]{:S(2)}) %collective-permute-start.10) | collective-permute-done | bytes 139296 | tf_op jit(solution)/shard_map/ppermute | solution.py:277
  74.4 0.0 copy-start.6
  74.4 8.3 %collective-permute-done.11.refs_2_ = f32[17,8,256]{2,1,0:T(8,128)S(1)} collective-permute-done((f32[17,8,256]{2,1,0:T(8,128)}, f32[17,8,256]{2,1,0:T(8,128)S(1)}, u32[]{:S(2)}, u32[]{:S(2)}) %collective-permute-start.11) | collective-permute-done | bytes 139296 | tf_op jit(solution)/shard_map/ppermute | solution.py:277
  82.7 0.0 copy-start.7
  82.7 0.0 collective-permute-done.12.refs_3_
  82.7 0.0 copy-start.8
  82.7 0.0 copy-done.6
  82.7 0.6 copy-done.7
  83.3 0.1 copy-done.8
  83.4 2.4 %finish.1 = (f32[240,120]{1,0:T(8,128)}, f32[1,240]{1,0:T(1,128)}, f32[8,8,30]{2,1,0:T(8,128)}) custom-call(s32[2]{0:T(128)} %pad_add_fusion.meta, f32[17,8,256]{2,1,0:T(8,128)} %get-tuple-element.14.refs_0_, f32[17,8,256]{2,1,0:T(8,128)} %copy-done.6, f32[17,8,256]{2,1,0:T(8,128)} %copy-done.7, f32[17,8,256]{2,1,0:T(8,128)} %copy-done.8), custom_call_target="tpu_custom_call" | custom-call | tf_op jit(solution)/shard_map/finish/pallas_call | solution.py:262
Async XLA Ops:
  0.6 5.1 %copy-start = (f32[30,3,8,256]{3,2,1,0:T(8,128)S(1)}, f32[30,3,8,256]{3,2,1,0:T(8,128)}, u32[]{:S(2)}) copy-start(f32[30,3,8,256]{3,2,1,0:T(8,128)} %refs_9_.1) | copy-start | bytes 2211844
  0.6 28.5 %copy-start.9 = (s32[2,32]{1,0:T(2,128)S(1)}, s32[2,32]{1,0:T(2,128)}, u32[]{:S(2)}) copy-start(s32[2,32]{1,0:T(2,128)} %refs_0_.1) | copy-start | bytes 772
  0.7 20.6 %collective-permute-start.7 = (f32[30,3,8,256]{3,2,1,0:T(8,128)}, f32[30,3,8,256]{3,2,1,0:T(8,128)S(1)}, u32[]{:S(2)}, u32[]{:S(2)}) collective-permute-start(f32[30,3,8,256]{3,2,1,0:T(8,128)} %refs_9_.1), channel_id=1, source_target_pairs={{0,2},{1,3},{2,0},{3,1},{4,6},{5,7},{6,4},{7,5},{8,10},{9,11},{10,... | collective-permute-start | bytes 2211848 | tf_op jit(solution)/shard_map/ppermute | solution.py:277
  5.6 23.5 %collective-permute-start.4 = (f32[2,200,256]{2,1,0:T(8,128)}, f32[2,200,256]{2,1,0:T(8,128)S(1)}, u32[]{:S(2)}, u32[]{:S(2)}) collective-permute-start(f32[2,200,256]{2,1,0:T(8,128)} %prepare.1.refs_5_), channel_id=1, source_target_pairs={{0,2},{1,3},{2,0},{3,1},{4,6},{5,7},{6,4},{7,5},{8,10},{9,11},{10,... | collective-permute-start | bytes 1228808 | tf_op jit(solution)/shard_map/ppermute | solution.py:277
  5.7 30.0 %collective-permute-start.6 = (f32[30,3,8,256]{3,2,1,0:T(8,128)S(1)}, f32[30,3,8,256]{3,2,1,0:T(8,128)S(1)}, u32[]{:S(2)}, u32[]{:S(2)}) collective-permute-start(f32[30,3,8,256]{3,2,1,0:T(8,128)S(1)} %copy-done), channel_id=1, source_target_pairs={{0,1},{1,0},{2,3},{3,2},{4,5},{5,4},{6,7},{7,6},{8,9},{9,8},{10,11... | collective-permute-start | bytes 2211848 | tf_op jit(solution)/shard_map/ppermute | solution.py:277
  21.2 14.5 %copy-start.1 = (f32[30,3,8,256]{3,2,1,0:T(8,128)}, f32[30,3,8,256]{3,2,1,0:T(8,128)S(1)}, u32[]{:S(2)}) copy-start(f32[30,3,8,256]{3,2,1,0:T(8,128)S(1)} %collective-permute-done.7.refs_11_) | copy-start | bytes 2211844
  21.2 14.5 %collective-permute-start.8 = (f32[30,3,8,256]{3,2,1,0:T(8,128)S(1)}, f32[30,3,8,256]{3,2,1,0:T(8,128)S(1)}, u32[]{:S(2)}, u32[]{:S(2)}) collective-permute-start(f32[30,3,8,256]{3,2,1,0:T(8,128)S(1)} %collective-permute-done.7.refs_11_), channel_id=1, source_target_pairs={{0,1},{1,0},{2,3},{3,2},{4,5},{5,4},{6,7},{7,6},{8,9},{9,8},{10,11... | collective-permute-start | bytes 2211848 | tf_op jit(solution)/shard_map/ppermute | solution.py:277
  21.2 14.4 %collective-permute-start.3 = (f32[2,200,256]{2,1,0:T(8,128)}, f32[2,200,256]{2,1,0:T(8,128)}, u32[]{:S(2)}, u32[]{:S(2)}) collective-permute-start(f32[2,200,256]{2,1,0:T(8,128)} %prepare.1.refs_5_), channel_id=1, source_target_pairs={{0,1},{1,0},{2,3},{3,2},{4,5},{5,4},{6,7},{7,6},{8,9},{9,8},{10,11... | collective-permute-start | bytes 1228808 | tf_op jit(solution)/shard_map/ppermute | solution.py:277
  29.2 6.5 %copy-start.5 = (f32[2,200,256]{2,1,0:T(8,128)}, f32[2,200,256]{2,1,0:T(8,128)S(1)}, u32[]{:S(2)}) copy-start(f32[2,200,256]{2,1,0:T(8,128)S(1)} %collective-permute-done.4.refs_7_) | copy-start | bytes 1228804
  29.2 6.5 %collective-permute-start.5 = (f32[2,200,256]{2,1,0:T(8,128)S(1)}, f32[2,200,256]{2,1,0:T(8,128)}, u32[]{:S(2)}, u32[]{:S(2)}) collective-permute-start(f32[2,200,256]{2,1,0:T(8,128)S(1)} %collective-permute-done.4.refs_7_), channel_id=1, source_target_pairs={{0,1},{1,0},{2,3},{3,2},{4,5},{5,4},{6,7},{7,6},{8,9},{9,8},{10,11... | collective-permute-start | bytes 1228808 | tf_op jit(solution)/shard_map/ppermute | solution.py:277
  29.2 1.7 %collective-permute-start = (s32[2,32]{1,0:T(2,128)S(1)}, s32[2,32]{1,0:T(2,128)S(1)}, u32[]{:S(2)}, u32[]{:S(2)}) collective-permute-start(s32[2,32]{1,0:T(2,128)S(1)} %copy-done.9), channel_id=1, source_target_pairs={{0,1},{1,0},{2,3},{3,2},{4,5},{5,4},{6,7},{7,6},{8,9},{9,8},{10,11... | collective-permute-start | bytes 776 | tf_op jit(solution)/shard_map/ppermute | solution.py:277
  30.9 1.7 %copy-start.10 = (s32[2,32]{1,0:T(2,128)}, s32[2,32]{1,0:T(2,128)S(1)}, u32[]{:S(2)}) copy-start(s32[2,32]{1,0:T(2,128)S(1)} %collective-permute-done.refs_1_) | copy-start | bytes 772
  30.9 3.6 %collective-permute-start.1 = (s32[2,32]{1,0:T(2,128)S(1)}, s32[2,32]{1,0:T(2,128)S(1)}, u32[]{:S(2)}, u32[]{:S(2)}) collective-permute-start(s32[2,32]{1,0:T(2,128)S(1)} %copy-done.9), channel_id=1, source_target_pairs={{0,2},{1,3},{2,0},{3,1},{4,6},{5,7},{6,4},{7,5},{8,10},{9,11},{10,... | collective-permute-start | bytes 776 | tf_op jit(solution)/shard_map/ppermute | solution.py:277
  34.5 0.6 copy-start.11
  34.5 1.2 %collective-permute-start.2 = (s32[2,32]{1,0:T(2,128)S(1)}, s32[2,32]{1,0:T(2,128)S(1)}, u32[]{:S(2)}, u32[]{:S(2)}) collective-permute-start(s32[2,32]{1,0:T(2,128)S(1)} %collective-permute-done.1.refs_2_), channel_id=1, source_target_pairs={{0,1},{1,0},{2,3},{3,2},{4,5},{5,4},{6,7},{7,6},{8,9},{9,8},{10,11... | collective-permute-start | bytes 776 | tf_op jit(solution)/shard_map/ppermute | solution.py:277
  35.6 0.6 copy-start.12
  35.7 0.9 %copy-start.2 = (f32[30,3,8,256]{3,2,1,0:T(8,128)}, f32[30,3,8,256]{3,2,1,0:T(8,128)S(1)}, u32[]{:S(2)}) copy-start(f32[30,3,8,256]{3,2,1,0:T(8,128)S(1)} %collective-permute-done.6.refs_10_) | copy-start | bytes 2211844
  36.6 0.9 %copy-start.3 = (f32[30,3,8,256]{3,2,1,0:T(8,128)}, f32[30,3,8,256]{3,2,1,0:T(8,128)S(1)}, u32[]{:S(2)}) copy-start(f32[30,3,8,256]{3,2,1,0:T(8,128)S(1)} %collective-permute-done.8.refs_12_) | copy-start | bytes 2211844
  50.9 13.9 %collective-permute-start.9 = (f32[62,8,256]{2,1,0:T(8,128)}, f32[62,8,256]{2,1,0:T(8,128)S(1)}, u32[]{:S(2)}, u32[]{:S(2)}) collective-permute-start(f32[62,8,256]{2,1,0:T(8,128)} %get-tuple-element.13), channel_id=1, source_target_pairs={{0,4},{4,0},{8,12},{12,8},{16,20},{20,16},{24,28},{28,24},{1,5},{5... | collective-permute-start | bytes 1523720 | tf_op jit(solution)/shard_map/ppermute | solution.py:277
  64.7 0.8 copy-start.4
  67.6 6.8 %collective-permute-start.10 = (f32[17,8,256]{2,1,0:T(8,128)}, f32[17,8,256]{2,1,0:T(8,128)S(1)}, u32[]{:S(2)}, u32[]{:S(2)}) collective-permute-start(f32[17,8,256]{2,1,0:T(8,128)} %get-tuple-element.15), channel_id=1, source_target_pairs={{0,8},{4,12},{8,0},{12,4},{16,24},{20,28},{24,16},{28,20},{1,9},{5... | collective-permute-start | bytes 417800 | tf_op jit(solution)/shard_map/ppermute | solution.py:277
  69.4 13.3 %collective-permute-start.11 = (f32[17,8,256]{2,1,0:T(8,128)}, f32[17,8,256]{2,1,0:T(8,128)S(1)}, u32[]{:S(2)}, u32[]{:S(2)}) collective-permute-start(f32[17,8,256]{2,1,0:T(8,128)} %get-tuple-element.16), channel_id=1, source_target_pairs={{0,16},{4,20},{8,24},{12,28},{16,0},{20,4},{24,8},{28,12},{1,17},{... | collective-permute-start | bytes 417800 | tf_op jit(solution)/shard_map/ppermute | solution.py:277
  72.0 10.7 %collective-permute-start.12 = (f32[17,8,256]{2,1,0:T(8,128)}, f32[17,8,256]{2,1,0:T(8,128)S(1)}, u32[]{:S(2)}, u32[]{:S(2)}) collective-permute-start(f32[17,8,256]{2,1,0:T(8,128)} %get-tuple-element.17), channel_id=1, source_target_pairs={{0,24},{4,28},{8,16},{12,20},{16,8},{20,12},{24,0},{28,4},{1,25},{... | collective-permute-start | bytes 417800 | tf_op jit(solution)/shard_map/ppermute | solution.py:277
  74.4 8.3 %copy-start.6 = (f32[17,8,256]{2,1,0:T(8,128)}, f32[17,8,256]{2,1,0:T(8,128)S(1)}, u32[]{:S(2)}) copy-start(f32[17,8,256]{2,1,0:T(8,128)S(1)} %collective-permute-done.10.refs_1_) | copy-start | bytes 417796
  82.7 0.6 copy-start.7
  82.7 0.7 copy-start.8

commit v2 on v1

--- a/solution.py
+++ b/solution.py
@@ -12,7 +12,8 @@
 HIGH = lax.Precision.HIGH
 HIGHEST = lax.Precision.HIGHEST
 PLANES = 6
-VMEM_LIMIT = 56 * 1024 * 1024
+SMALL_LIMIT = 8 * 1024 * 1024
+LARGE_LIMIT = 24 * 1024 * 1024
 NT = (((1,), (1,)), ((), ()))
 
 
@@ -28,7 +29,7 @@
     return pl.BlockSpec(memory_space=pl.ANY)
 
 
-def prepare_kernel(sight, mapping, residual, counts, knots, planes):
+def prepare_kernel(sight, mapping, residual, counts, track, knots, planes):
     stations, _, tracked, _ = sight.shape
     for s in range(stations):
         weight = counts[s].astype(jnp.float32)
@@ -60,54 +61,70 @@
         planes[s, 5 * tracked : 6 * tracked, :] = jnp.where(
             weight > 0.0, total / jnp.maximum(weight, 1.0), 0.0
         )
-        planes[s, 6 * tracked :, :] = jnp.broadcast_to(
-            knot.astype(jnp.float32), (8, knot.shape[1])
+        planes[s, 6 * tracked :, :] = jnp.zeros((8, knot.shape[1]), jnp.float32)
+        planes[s, 6 * tracked : 6 * tracked + 1, :] = knot.astype(jnp.float32)
+        planes[s, 6 * tracked + 1 : 6 * tracked + 2, :tracked] = track[s : s + 1, :].astype(
+            jnp.float32
         )
 
 
-def prepare(sight, mapping, residual, counts, knots):
+def prepare(sight, mapping, residual, counts, track, knots):
     stations, _, tracked, epochs = sight.shape
     return pl.pallas_call(
         prepare_kernel,
         out_shape=jax.ShapeDtypeStruct(
             (stations, PLANES * tracked + 8, epochs), jnp.float32
         ),
-        in_specs=[vmem()] * 5,
+        in_specs=[vmem()] * 6,
         out_specs=vmem(),
-        compiler_params=pltpu.CompilerParams(vmem_limit_bytes=VMEM_LIMIT),
+        compiler_params=pltpu.CompilerParams(vmem_limit_bytes=SMALL_LIMIT),
         name="prepare",
-    )(sight, mapping, residual, counts, knots)
-
-
-def main_kernel(groups, per, own, nx, nz, window, *refs):
-    tracks = refs[:groups]
-    meta = refs[groups]
-    plane_pieces = refs[groups + 1 : 2 * groups + 1]
-    orbit_pieces = refs[2 * groups + 1 : 3 * groups + 1]
-    outs = refs[3 * groups + 1 : 3 * groups + 1 + nx]
-    (track, planes, orbit, acc, compact, tropo, product, dense, factor, dense_tropo, rights,
-     blocks, sems) = refs[3 * groups + 1 + nx :]
+    )(sight, mapping, residual, counts, track, knots)
+
+
+def window_start(i, columns, sats, window):
+    return jnp.minimum(lax.div(i * columns, 8), sats - window)
+
+
+def main_kernel(groups, per, own, nx, nz, window, places, *refs):
+    plane_pieces = refs[:groups]
+    orbit_pieces = refs[groups : groups + len(places)]
+    outs = refs[groups + len(places) : groups + len(places) + nx]
+    (track, rows_int, planes, orbit, acc, compact, tropo, product, dense, factor, dense_tropo,
+     rights, blocks, sems, track_sem) = refs[groups + len(places) + nx :]
     tracked = compact.shape[0]
     epochs = compact.shape[2]
     width = acc.shape[2]
-    first = meta[0]
+    sats = orbit.shape[0]
+    me = lax.axis_index("sat")
+    mine = lax.axis_index("sta")
+    first = me * own
 
     copies = []
     for d in range(groups):
         copies.append(pltpu.make_async_copy(
-            orbit_pieces[d], orbit.at[pl.ds(meta[1 + d], own)], sems.at[2 * d]))
+            plane_pieces[d], planes.at[pl.ds(d * per, per)], sems.at[d]))
+    for n, (d, part, parts) in enumerate(places):
+        size = own // parts
+        at = (me ^ d) * own
+        if parts > 1:
+            at = at + (lax.rem(lax.div(mine, nx), 2) ^ part) * size
         copies.append(pltpu.make_async_copy(
-            plane_pieces[d], planes.at[pl.ds(d * per, per)], sems.at[2 * d + 1]))
+            orbit_pieces[n], orbit.at[pl.ds(at, size)], sems.at[groups + n]))
     for copy in copies:
         copy.start()
-    for d in range(groups):
-        for s in range(per):
-            for m in range(tracked):
-                track[d * per + s, m] = tracks[d][s, m]
     acc[...] = jnp.zeros_like(acc)
     rights[...] = jnp.zeros_like(rights)
     blocks[...] = jnp.zeros_like(blocks)
-    for copy in copies:
+    for copy in copies[:groups]:
+        copy.wait()
+    for s in range(groups * per):
+        rows_int[s : s + 1, :] = planes[
+            s, PLANES * tracked + 1 : PLANES * tracked + 2, :128].astype(jnp.int32)
+    to_scalar = pltpu.make_async_copy(rows_int, track, track_sem)
+    to_scalar.start()
+    to_scalar.wait()
+    for copy in copies[groups:]:
         copy.wait()
 
     def visit(s, carry):
@@ -168,25 +185,25 @@
                             precision=HIGHEST, preferred_element_type=jnp.float32)
     for dx in range(nx):
         for dz in range(nz):
-            start = meta[1 + groups + dx * nz + dz]
+            start = window_start(mine ^ (dz * nx + dx), sats * 8 // (nx * nz), sats, window)
             outs[dx][dz * window : (dz + 1) * window] = acc[pl.ds(start, window)]
         outs[dx][nz * window] = small
         outs[dx][nz * window + 1] = right
 
 
-def accumulate(tracks, meta, planes, orbits, sats, nx, nz, window, width):
+def accumulate(planes, orbits, places, tracked, sats, nx, nz, window, width):
     groups = len(planes)
     per, rows, epochs = planes[0].shape
-    tracked = tracks[0].shape[1]
-    own = orbits[0].shape[0]
+    own = sats // groups
     out = jax.ShapeDtypeStruct((nz * window + 2, 8, width), jnp.float32)
     return pl.pallas_call(
-        functools.partial(main_kernel, groups, per, own, nx, nz, window),
+        functools.partial(main_kernel, groups, per, own, nx, nz, window, places),
         out_shape=[out] * nx,
-        in_specs=[smem()] * (groups + 1) + [anywhere()] * (2 * groups),
+        in_specs=[anywhere()] * (groups + len(orbits)),
         out_specs=[vmem()] * nx,
         scratch_shapes=[
-            pltpu.SMEM((groups * per, tracked), jnp.int32),
+            pltpu.SMEM((groups * per, 128), jnp.int32),
+            pltpu.VMEM((groups * per, 128), jnp.int32),
             pltpu.VMEM((groups * per, rows, epochs), jnp.float32),
             pltpu.VMEM((sats,) + orbits[0].shape[1:], jnp.float32),
             pltpu.VMEM((sats, 8, width), jnp.float32),
@@ -198,11 +215,12 @@
             pltpu.VMEM((own + 2, 8, 128), jnp.float32),
             pltpu.VMEM((own + 2, 8, epochs), jnp.float32),
             pltpu.VMEM((width, width), jnp.float32),
-            pltpu.SemaphoreType.DMA((2 * groups,)),
+            pltpu.SemaphoreType.DMA((groups + len(orbits),)),
+            pltpu.SemaphoreType.DMA,
         ],
-        compiler_params=pltpu.CompilerParams(vmem_limit_bytes=VMEM_LIMIT),
+        compiler_params=pltpu.CompilerParams(vmem_limit_bytes=LARGE_LIMIT),
         name="accumulate",
-    )(*tracks, meta, *planes, *orbits)
+    )(*planes, *orbits)
 
 
 def combine_kernel(nx, nz, window, *refs):
@@ -228,19 +246,20 @@
         out_shape=[out] * nz,
         in_specs=[vmem()] * nx,
         out_specs=[vmem()] * nz,
-        compiler_params=pltpu.CompilerParams(vmem_limit_bytes=VMEM_LIMIT),
+        compiler_params=pltpu.CompilerParams(vmem_limit_bytes=SMALL_LIMIT),
         name="combine",
     )(*pieces)
 
 
-def finish_kernel(nz, window, own, factor, cross_factor, meta, *refs):
+def finish_kernel(nz, window, own, columns, sats, factor, cross_factor, *refs):
     pieces = refs[:nz]
     normal, right, blocks = refs[nz:]
     width = pieces[0].shape[2]
     total = pieces[0][...]
     for piece in pieces[1:]:
         total = total + piece[...]
-    first, start = meta[0], meta[1]
+    first = lax.axis_index("sat") * own
+    start = window_start(lax.axis_index("sta"), columns, sats, window)
     span = own * 8
     part = total[:window].reshape(window * 8, width)
     row_owner = start + lax.broadcasted_iota(jnp.int32, part.shape, 0) // 8
@@ -257,20 +276,20 @@
                                      preferred_element_type=jnp.float32)
 
 
-def finish(meta, pieces, window, own, factor, cross_factor):
+def finish(pieces, window, own, columns, sats, factor, cross_factor):
     nz = len(pieces)
     return pl.pallas_call(
-        functools.partial(finish_kernel, nz, window, own, factor, cross_factor),
+        functools.partial(finish_kernel, nz, window, own, columns, sats, factor, cross_factor),
         out_shape=[
             jax.ShapeDtypeStruct((own * 8, window * 8), jnp.float32),
             jax.ShapeDtypeStruct((1, own * 8), jnp.float32),
             jax.ShapeDtypeStruct((8, 8, own), jnp.float32),
         ],
-        in_specs=[smem()] + [vmem()] * nz,
+        in_specs=[vmem()] * nz,
         out_specs=[vmem()] * 3,
-        compiler_params=pltpu.CompilerParams(vmem_limit_bytes=VMEM_LIMIT),
+        compiler_params=pltpu.CompilerParams(vmem_limit_bytes=SMALL_LIMIT),
         name="finish",
-    )(meta, *pieces)
+    )(*pieces)
 
 
 def shift(value, axis, size, step):
@@ -285,6 +304,25 @@
     for d in range(0, size, 2):
         pieces[d + 1] = shift(pieces[d], "sat", size, 1)
     return pieces
+
+
+def gather_orbit(orbit, size, columns_axis, nx):
+    own = orbit.shape[0]
+    if own % 2 or columns_axis // nx < 2:
+        return gather_pieces(orbit, size), tuple((d, 0, 1) for d in range(size))
+    half = own // 2
+    turn = lax.rem(lax.div(lax.axis_index("sta"), nx), 2)
+    mine = lax.dynamic_slice_in_dim(orbit, turn * half, half, 0)
+    pieces, places = [orbit], [(0, 0, 1)]
+    for d in range(2, size, 2):
+        near = shift(mine, "sat", size, d)
+        far = shift(near, "sta", columns_axis, nx)
+        pieces += [near, far]
+        places += [(d, 0, 2), (d, 1, 2)]
+    for piece, (d, part, parts) in list(zip(pieces, places)):
+        pieces.append(shift(piece, "sat", size, 1))
+        places.append((d + 1, part, parts))
+    return pieces, tuple(places)
 
 
 def shards(sight, mapping, residual, counts, track, knots, orbit):
@@ -298,29 +336,15 @@
     span = sats * params
     columns = span // columns_axis
     width = -(-(own * params) // 128) * 128
-    me = lax.axis_index("sat").astype(jnp.int32)
-    mine = lax.axis_index("sta").astype(jnp.int32)
 
     window = max(
         -(-(((columns * i) % 8) + columns) // 8) for i in range(columns_axis)
     )
 
-    def window_start(i):
-        return jnp.minimum(i * columns // 8, sats - window)
-
-    meta = [me * own]
-    for d in range(group):
-        meta.append((me ^ d) * own)
-    for dx in range(nx):
-        for dz in range(nz):
-            meta.append(window_start(mine ^ (dz * nx + dx)))
-    meta = jnp.stack(meta)
-
-    planes = prepare(sight, mapping, residual, counts, knots)
-    orbit_pieces = gather_pieces(orbit, group)
-    track_pieces = gather_pieces(track, group)
+    planes = prepare(sight, mapping, residual, counts, track, knots)
+    orbit_pieces, places = gather_orbit(orbit, group, columns_axis, nx)
     plane_pieces = gather_pieces(planes, group)
-    parts = accumulate(track_pieces, meta, plane_pieces, orbit_pieces, sats, nx, nz, window, width)
+    parts = accumulate(plane_pieces, orbit_pieces, places, tracked, sats, nx, nz, window, width)
     arrived = [parts[0]] + [
         shift(parts[d], "sta", columns_axis, d) for d in range(1, nx)
     ]
@@ -331,11 +355,10 @@
     total_stations = stations * columns_axis * group
     factor = sats / (total_stations * tracked * epochs)
     cross_factor = sats / (total_stations * epochs) ** 0.5
-    start = window_start(mine)
-    normal, right, blocks = finish(
-        jnp.stack([me * own, start]), final, window, own, factor, cross_factor
-    )
+    normal, right, blocks = finish(final, window, own, columns, sats, factor, cross_factor)
     if window * 8 != columns:
+        mine = lax.axis_index("sta")
+        start = window_start(mine, columns, sats, window)
         normal = lax.dynamic_slice_in_dim(normal, mine * columns - start * 8, columns, 1)
     return normal, right.reshape(own * params), jnp.transpose(blocks, (2, 0, 1))
 

time: 85.9 us -> 67.4 us (0.78)
  waiting for transfers between devices: 48.1 us -> 39.4 us
  Pallas kernels: 19.7 us -> 13.7 us
  local copies, waits for them, and re-layouts: 4.41 us -> 1.15 us
    ppermute x13 -> x12, waiting for transfers between devices: 48.1 us -> 39.4 us  [shift(): return lax.ppermute(value, axis, [(i, i ^ step) for i in range(size)])]
    unnamed x26 -> x14, local copies, waits for them, and re-layouts: 3.8 us -> 0.03 us
    pallas_call x1, Pallas kernels: 2.02 us -> 0.05 us  [combine(): pl.pallas_call(functools.partial(combine_kernel, nx, nz, window), out_sha...]
    pallas_call x1, Pallas kernels: 1.93 us -> 0.17 us  [prepare(): pl.pallas_call(prepare_kernel, out_shape=jax.ShapeDtypeStruct((stations,...]
    pallas_call x1, Pallas kernels: 13.4 us -> 12.3 us  [accumulate(): pl.pallas_call(functools.partial(main_kernel, groups, per, own, nx, nz, w...]
    dynamic_slice x0 -> x1, local copies, waits for them, and re-layouts: none -> 1.12 us  [gather_orbit(): mine = lax.dynamic_slice_in_dim(orbit, turn * half, half, 0)]
    pallas_call x1, Pallas kernels: 2.35 us -> 1.24 us  [finish(): pl.pallas_call(functools.partial(finish_kernel, nz, window, own, columns,...]
    ppermute x13 -> x12, starting transfers between devices: 12.1 us -> 12.1 us  [shift(): return lax.ppermute(value, axis, [(i, i ^ step) for i in range(size)])]
  transfers between devices with their start and end apart: 13 -> 12, of which waited for: 7 -> 8; matrix products, arithmetic and copies ran while one was open for 1% -> 0% of each run, Pallas kernels for 2% -> 0%
where the time goes in v2:
time: 67.4 us; the launch traced here: 67.2 us
  waiting for transfers between devices  39.4 us (58%)
  Pallas kernels  13.7 us (20%)
  starting transfers between devices  12.1 us (18%)
  local copies, waits for them, and re-layouts  1.15 us (2%)
  between operations  0.77 us (1%)
    ppermute x12, waiting for transfers between devices, shift(): return lax.ppermute(value, axis, [(i, i ^ step) for i in range(size)])  39.4 us
    pallas_call x1, Pallas kernels, accumulate(): pl.pallas_call(functools.partial(main_kernel, groups, per, own, nx, nz, w...  12.3 us
    ppermute x12, starting transfers between devices, shift(): return lax.ppermute(value, axis, [(i, i ^ step) for i in range(size)])  12.1 us
  transfers between devices with their start and end apart: 12, of which 8 were waited for; matrix products, arithmetic and copies ran while one was open for 0% of the time, Pallas kernels for 0%

profile of v2, /device:TPU:0, one launch (start us, length us, event | category | flops | bytes accessed | tf_op | source)
XLA Modules:
  0.0 67.2 jit_solution(4543351068679207536)
XLA Ops:
  0.6 0.0 copy-start.1
  0.7 0.0 copy-start.2
  0.7 0.0 copy-start.3
  0.7 0.0 copy-start.4
  0.7 0.0 copy-start.5
  0.7 0.0 copy-start.6
  0.7 0.0 copy-start
  0.7 1.1 %constant_dynamic-slice_fusion = f32[15,3,8,256]{3,2,1,0:T(8,128)S(1)} fusion(f32[30,3,8,256]{3,2,1,0:T(8,128)} %refs_4_.1, s32[]{:T(128)S(6)} %select_n.3), kind=kLoop, calls=%fused_computation | loop fusion | bytes 737284 | tf_op jit(solution)/shard_map/dynamic_slice | solution.py:315
  1.8 3.0 %collective-permute-start.3 = (f32[15,3,8,256]{3,2,1,0:T(8,128)S(1)}, f32[15,3,8,256]{3,2,1,0:T(8,128)S(1)}, u32[]{:S(2)}, u32[]{:S(2)}) collective-permute-start(f32[15,3,8,256]{3,2,1,0:T(8,128)S(1)} %constant_dynamic-slice_fusion), channel_id=1, source_target_pairs={{0,2},{1,3},{2,0},{3,1},{4,6},{5,7},{6,4},{7,5},{8,10},{9,11},{10,... | collective-permute-start | bytes 1105928 | tf_op jit(solution)/shard_map/ppermute | solution.py:296
  4.9 0.0 copy-done.1
  4.9 0.0 copy-done.2
  4.9 0.0 copy-done.3
  4.9 0.0 copy-done.4
  4.9 0.0 copy-done.5
  4.9 0.0 copy-done.6
  4.9 0.2 prepare.1.refs_0_
  5.1 0.1 collective-permute-start.1
  5.2 0.0 copy-done
  5.2 0.1 collective-permute-start.5
  5.3 9.0 %collective-permute-done.3.refs_5_ = f32[15,3,8,256]{3,2,1,0:T(8,128)S(1)} collective-permute-done((f32[15,3,8,256]{3,2,1,0:T(8,128)S(1)}, f32[15,3,8,256]{3,2,1,0:T(8,128)S(1)}, u32[]{:S(2)}, u32[]{:S(2)}) %collective-permute-start.3) | collective-permute-done | bytes 368672 | tf_op jit(solution)/shard_map/ppermute | solution.py:296
  14.3 2.1 %collective-permute-start.4 = (f32[15,3,8,256]{3,2,1,0:T(8,128)S(1)}, f32[15,3,8,256]{3,2,1,0:T(8,128)S(1)}, u32[]{:S(2)}, u32[]{:S(2)}) collective-permute-start(f32[15,3,8,256]{3,2,1,0:T(8,128)S(1)} %collective-permute-done.3.refs_5_), channel_id=1, source_target_pairs={{0,8},{4,12},{8,0},{12,4},{16,24},{20,28},{24,16},{28,20},{1,9},{5... | collective-permute-start | bytes 1105928 | tf_op jit(solution)/shard_map/ppermute | solution.py:296
  16.4 0.0 collective-permute-start
  16.4 5.8 %collective-permute-done.1.refs_2_ = f32[2,200,256]{2,1,0:T(8,128)S(1)} collective-permute-done((f32[2,200,256]{2,1,0:T(8,128)S(1)}, f32[2,200,256]{2,1,0:T(8,128)S(1)}, u32[]{:S(2)}, u32[]{:S(2)}) %collective-permute-start.1) | collective-permute-done | bytes 409632 | tf_op jit(solution)/shard_map/ppermute | solution.py:296
  22.2 0.0 collective-permute-start.2
  22.2 0.5 collective-permute-start.6
  22.8 0.5 collective-permute-done.4.refs_6_
  23.2 0.0 collective-permute-start.7
  23.2 0.0 collective-permute-done.refs_1_
  23.2 1.3 %collective-permute-done.6.refs_8_ = f32[15,3,8,256]{3,2,1,0:T(8,128)S(1)} collective-permute-done((f32[15,3,8,256]{3,2,1,0:T(8,128)S(1)}, f32[15,3,8,256]{3,2,1,0:T(8,128)S(1)}, u32[]{:S(2)}, u32[]{:S(2)}) %collective-permute-start.6) | collective-permute-done | bytes 368672 | tf_op jit(solution)/shard_map/ppermute | solution.py:296
  24.5 0.0 collective-permute-done.5.refs_7_
  24.5 0.0 collective-permute-done.2.refs_3_
  24.5 0.5 collective-permute-done.7.refs_9_
  25.0 12.3 %accumulate.1 = (f32[62,8,256]{2,1,0:T(8,128)S(1)}, f32[62,8,256]{2,1,0:T(8,128)S(1)}) custom-call(f32[2,200,256]{2,1,0:T(8,128)S(1)} %prepare.1.refs_0_, f32[2,200,256]{2,1,0:T(8,128)S(1)} %collective-permute-done.refs_1_, f32[2,200,256]{2,1,0:T(8,128)S(1)} %collective-permute-done.1.refs_2_, f32[2,200,256]{2,1,0:T(8,128)S(1)} %collective-permute-done.2.refs_3_, ...), custom_call_target="tpu_custom_call" | custom-call | tf_op jit(solution)/shard_map/accumulate/pallas_call | solution.py:199
  37.3 1.8 %collective-permute-start.8 = (f32[62,8,256]{2,1,0:T(8,128)S(1)}, f32[62,8,256]{2,1,0:T(8,128)S(1)}, u32[]{:S(2)}, u32[]{:S(2)}) collective-permute-start(f32[62,8,256]{2,1,0:T(8,128)S(1)} %get-tuple-element.13), channel_id=1, source_target_pairs={{0,4},{4,0},{8,12},{12,8},{16,20},{20,16},{24,28},{28,24},{1,5},{5... | collective-permute-start | bytes 1523720 | tf_op jit(solution)/shard_map/ppermute | solution.py:296
  39.1 11.9 %collective-permute-done.8.refs_1_ = f32[62,8,256]{2,1,0:T(8,128)S(1)} collective-permute-done((f32[62,8,256]{2,1,0:T(8,128)S(1)}, f32[62,8,256]{2,1,0:T(8,128)S(1)}, u32[]{:S(2)}, u32[]{:S(2)}) %collective-permute-start.8) | collective-permute-done | bytes 507936 | tf_op jit(solution)/shard_map/ppermute | solution.py:296
  51.0 0.1 combine.1
  51.0 1.9 %collective-permute-start.9 = (f32[17,8,256]{2,1,0:T(8,128)S(1)}, f32[17,8,256]{2,1,0:T(8,128)S(1)}, u32[]{:S(2)}, u32[]{:S(2)}) collective-permute-start(f32[17,8,256]{2,1,0:T(8,128)S(1)} %get-tuple-element.15), channel_id=1, source_target_pairs={{0,8},{4,12},{8,0},{12,4},{16,24},{20,28},{24,16},{28,20},{1,9},{5... | collective-permute-start | bytes 417800 | tf_op jit(solution)/shard_map/ppermute | solution.py:296
  52.9 2.6 %collective-permute-start.10 = (f32[17,8,256]{2,1,0:T(8,128)S(1)}, f32[17,8,256]{2,1,0:T(8,128)S(1)}, u32[]{:S(2)}, u32[]{:S(2)}) collective-permute-start(f32[17,8,256]{2,1,0:T(8,128)S(1)} %get-tuple-element.16), channel_id=1, source_target_pairs={{0,16},{4,20},{8,24},{12,28},{16,0},{20,4},{24,8},{28,12},{1,17},{... | collective-permute-start | bytes 417800 | tf_op jit(solution)/shard_map/ppermute | solution.py:296
  55.5 0.0 collective-permute-start.11
  55.5 2.2 %collective-permute-done.9.refs_1_ = f32[17,8,256]{2,1,0:T(8,128)S(1)} collective-permute-done((f32[17,8,256]{2,1,0:T(8,128)S(1)}, f32[17,8,256]{2,1,0:T(8,128)S(1)}, u32[]{:S(2)}, u32[]{:S(2)}) %collective-permute-start.9) | collective-permute-done | bytes 139296 | tf_op jit(solution)/shard_map/ppermute | solution.py:296
  57.7 8.2 %collective-permute-done.10.refs_2_ = f32[17,8,256]{2,1,0:T(8,128)S(1)} collective-permute-done((f32[17,8,256]{2,1,0:T(8,128)S(1)}, f32[17,8,256]{2,1,0:T(8,128)S(1)}, u32[]{:S(2)}, u32[]{:S(2)}) %collective-permute-start.10) | collective-permute-done | bytes 139296 | tf_op jit(solution)/shard_map/ppermute | solution.py:296
  65.9 0.0 collective-permute-done.11.refs_3_
  65.9 1.2 %finish.1 = (f32[240,120]{1,0:T(8,128)}, f32[1,240]{1,0:T(1,128)}, f32[8,8,30]{2,1,0:T(8,128)}) custom-call(f32[17,8,256]{2,1,0:T(8,128)S(1)} %get-tuple-element.14.refs_0_, f32[17,8,256]{2,1,0:T(8,128)S(1)} %collective-permute-done.9.refs_1_, f32[17,8,256]{2,1,0:T(8,128)S(1)} %collective-permute-done.10.refs_2_, ...), custom_call_target="tpu_custom_call" | custom-call | tf_op jit(solution)/shard_map/finish/pallas_call | solution.py:281
Async XLA Ops:
  0.6 4.2 %copy-start.1 = (f32[2,3,32,256]{3,2,1,0:T(8,128)S(1)}, f32[2,3,32,256]{3,2,1,0:T(8,128)}, u32[]{:S(2)}) copy-start(f32[2,3,32,256]{3,2,1,0:T(8,128)} %sight.1) | copy-start | bytes 589828
  0.7 4.2 %copy-start.2 = (f32[2,32,256]{2,1,0:T(8,128)S(1)}, f32[2,32,256]{2,1,0:T(8,128)}, u32[]{:S(2)}) copy-start(f32[2,32,256]{2,1,0:T(8,128)} %mapping.1) | copy-start | bytes 196612
  0.7 4.2 %copy-start.3 = (f32[2,32,256]{2,1,0:T(8,128)S(1)}, f32[2,32,256]{2,1,0:T(8,128)}, u32[]{:S(2)}) copy-start(f32[2,32,256]{2,1,0:T(8,128)} %residual.1) | copy-start | bytes 196612
  0.7 4.2 %copy-start.4 = (s32[2,32,256]{2,1,0:T(8,128)S(1)}, s32[2,32,256]{2,1,0:T(8,128)}, u32[]{:S(2)}) copy-start(s32[2,32,256]{2,1,0:T(8,128)} %counts.1) | copy-start | bytes 196612
  0.7 4.2 %copy-start.5 = (s32[2,256]{1,0:T(2,128)S(1)}, s32[2,256]{1,0:T(2,128)}, u32[]{:S(2)}) copy-start(s32[2,256]{1,0:T(2,128)} %knots.1) | copy-start | bytes 6148
  0.7 4.2 %copy-start.6 = (s32[2,32]{1,0:T(2,128)S(1)}, s32[2,32]{1,0:T(2,128)}, u32[]{:S(2)}) copy-start(s32[2,32]{1,0:T(2,128)} %track.1) | copy-start | bytes 772
  0.7 4.5 %copy-start = (f32[30,3,8,256]{3,2,1,0:T(8,128)S(1)}, f32[30,3,8,256]{3,2,1,0:T(8,128)}, u32[]{:S(2)}) copy-start(f32[30,3,8,256]{3,2,1,0:T(8,128)} %refs_4_.1) | copy-start | bytes 2211844
  1.8 12.4 %collective-permute-start.3 = (f32[15,3,8,256]{3,2,1,0:T(8,128)S(1)}, f32[15,3,8,256]{3,2,1,0:T(8,128)S(1)}, u32[]{:S(2)}, u32[]{:S(2)}) collective-permute-start(f32[15,3,8,256]{3,2,1,0:T(8,128)S(1)} %constant_dynamic-slice_fusion), channel_id=1, source_target_pairs={{0,2},{1,3},{2,0},{3,1},{4,6},{5,7},{6,4},{7,5},{8,10},{9,11},{10,... | collective-permute-start | bytes 1105928 | tf_op jit(solution)/shard_map/ppermute | solution.py:296
  5.1 17.2 %collective-permute-start.1 = (f32[2,200,256]{2,1,0:T(8,128)S(1)}, f32[2,200,256]{2,1,0:T(8,128)S(1)}, u32[]{:S(2)}, u32[]{:S(2)}) collective-permute-start(f32[2,200,256]{2,1,0:T(8,128)S(1)} %prepare.1.refs_0_), channel_id=1, source_target_pairs={{0,2},{1,3},{2,0},{3,1},{4,6},{5,7},{6,4},{7,5},{8,10},{9,11},{10,... | collective-permute-start | bytes 1228808 | tf_op jit(solution)/shard_map/ppermute | solution.py:296
  5.2 19.3 %collective-permute-start.5 = (f32[30,3,8,256]{3,2,1,0:T(8,128)S(1)}, f32[30,3,8,256]{3,2,1,0:T(8,128)S(1)}, u32[]{:S(2)}, u32[]{:S(2)}) collective-permute-start(f32[30,3,8,256]{3,2,1,0:T(8,128)S(1)} %copy-done), channel_id=1, source_target_pairs={{0,1},{1,0},{2,3},{3,2},{4,5},{5,4},{6,7},{7,6},{8,9},{9,8},{10,11... | collective-permute-start | bytes 2211848 | tf_op jit(solution)/shard_map/ppermute | solution.py:296
  14.3 8.9 %collective-permute-start.4 = (f32[15,3,8,256]{3,2,1,0:T(8,128)S(1)}, f32[15,3,8,256]{3,2,1,0:T(8,128)S(1)}, u32[]{:S(2)}, u32[]{:S(2)}) collective-permute-start(f32[15,3,8,256]{3,2,1,0:T(8,128)S(1)} %collective-permute-done.3.refs_5_), channel_id=1, source_target_pairs={{0,8},{4,12},{8,0},{12,4},{16,24},{20,28},{24,16},{28,20},{1,9},{5... | collective-permute-start | bytes 1105928 | tf_op jit(solution)/shard_map/ppermute | solution.py:296
  16.4 6.8 %collective-permute-start = (f32[2,200,256]{2,1,0:T(8,128)S(1)}, f32[2,200,256]{2,1,0:T(8,128)S(1)}, u32[]{:S(2)}, u32[]{:S(2)}) collective-permute-start(f32[2,200,256]{2,1,0:T(8,128)S(1)} %prepare.1.refs_0_), channel_id=1, source_target_pairs={{0,1},{1,0},{2,3},{3,2},{4,5},{5,4},{6,7},{7,6},{8,9},{9,8},{10,11... | collective-permute-start | bytes 1228808 | tf_op jit(solution)/shard_map/ppermute | solution.py:296
  22.2 2.3 %collective-permute-start.2 = (f32[2,200,256]{2,1,0:T(8,128)S(1)}, f32[2,200,256]{2,1,0:T(8,128)S(1)}, u32[]{:S(2)}, u32[]{:S(2)}) collective-permute-start(f32[2,200,256]{2,1,0:T(8,128)S(1)} %collective-permute-done.1.refs_2_), channel_id=1, source_target_pairs={{0,1},{1,0},{2,3},{3,2},{4,5},{5,4},{6,7},{7,6},{8,9},{9,8},{10,11... | collective-permute-start | bytes 1228808 | tf_op jit(solution)/shard_map/ppermute | solution.py:296
  22.2 2.3 %collective-permute-start.6 = (f32[15,3,8,256]{3,2,1,0:T(8,128)S(1)}, f32[15,3,8,256]{3,2,1,0:T(8,128)S(1)}, u32[]{:S(2)}, u32[]{:S(2)}) collective-permute-start(f32[15,3,8,256]{3,2,1,0:T(8,128)S(1)} %collective-permute-done.3.refs_5_), channel_id=1, source_target_pairs={{0,1},{1,0},{2,3},{3,2},{4,5},{5,4},{6,7},{7,6},{8,9},{9,8},{10,11... | collective-permute-start | bytes 1105928 | tf_op jit(solution)/shard_map/ppermute | solution.py:296
  23.2 1.8 %collective-permute-start.7 = (f32[15,3,8,256]{3,2,1,0:T(8,128)S(1)}, f32[15,3,8,256]{3,2,1,0:T(8,128)S(1)}, u32[]{:S(2)}, u32[]{:S(2)}) collective-permute-start(f32[15,3,8,256]{3,2,1,0:T(8,128)S(1)} %collective-permute-done.4.refs_6_), channel_id=1, source_target_pairs={{0,1},{1,0},{2,3},{3,2},{4,5},{5,4},{6,7},{7,6},{8,9},{9,8},{10,11... | collective-permute-start | bytes 1105928 | tf_op jit(solution)/shard_map/ppermute | solution.py:296
  37.3 13.7 %collective-permute-start.8 = (f32[62,8,256]{2,1,0:T(8,128)S(1)}, f32[62,8,256]{2,1,0:T(8,128)S(1)}, u32[]{:S(2)}, u32[]{:S(2)}) collective-permute-start(f32[62,8,256]{2,1,0:T(8,128)S(1)} %get-tuple-element.13), channel_id=1, source_target_pairs={{0,4},{4,0},{8,12},{12,8},{16,20},{20,16},{24,28},{28,24},{1,5},{5... | collective-permute-start | bytes 1523720 | tf_op jit(solution)/shard_map/ppermute | solution.py:296
  51.0 6.7 %collective-permute-start.9 = (f32[17,8,256]{2,1,0:T(8,128)S(1)}, f32[17,8,256]{2,1,0:T(8,128)S(1)}, u32[]{:S(2)}, u32[]{:S(2)}) collective-permute-start(f32[17,8,256]{2,1,0:T(8,128)S(1)} %get-tuple-element.15), channel_id=1, source_target_pairs={{0,8},{4,12},{8,0},{12,4},{16,24},{20,28},{24,16},{28,20},{1,9},{5... | collective-permute-start | bytes 417800 | tf_op jit(solution)/shard_map/ppermute | solution.py:296
  52.9 13.0 %collective-permute-start.10 = (f32[17,8,256]{2,1,0:T(8,128)S(1)}, f32[17,8,256]{2,1,0:T(8,128)S(1)}, u32[]{:S(2)}, u32[]{:S(2)}) collective-permute-start(f32[17,8,256]{2,1,0:T(8,128)S(1)} %get-tuple-element.16), channel_id=1, source_target_pairs={{0,16},{4,20},{8,24},{12,28},{16,0},{20,4},{24,8},{28,12},{1,17},{... | collective-permute-start | bytes 417800 | tf_op jit(solution)/shard_map/ppermute | solution.py:296
  55.5 10.4 %collective-permute-start.11 = (f32[17,8,256]{2,1,0:T(8,128)S(1)}, f32[17,8,256]{2,1,0:T(8,128)S(1)}, u32[]{:S(2)}, u32[]{:S(2)}) collective-permute-start(f32[17,8,256]{2,1,0:T(8,128)S(1)} %get-tuple-element.17), channel_id=1, source_target_pairs={{0,24},{4,28},{8,16},{12,20},{16,8},{20,12},{24,0},{28,4},{1,25},{... | collective-permute-start | bytes 417800 | tf_op jit(solution)/shard_map/ppermute | solution.py:296

commit v3 on v2

v3 whole, which is shorter than its diff:
```python
import functools

import jax
import jax.numpy as jnp
from jax import lax
from jax.experimental import pallas as pl
from jax.experimental.pallas import tpu as pltpu
from jax.sharding import PartitionSpec as P

KNOTS = 4
PRIOR = 1.0
HIGHEST = lax.Precision.HIGHEST
SMALL_LIMIT = 8 * 1024 * 1024
MEDIUM_LIMIT = 16 * 1024 * 1024
LARGE_LIMIT = 32 * 1024 * 1024
NT = (((1,), (1,)), ((), ()))


def vmem():
    return pl.BlockSpec(memory_space=pltpu.VMEM)


def smem():
    return pl.BlockSpec(memory_space=pltpu.SMEM)


def anywhere():
    return pl.BlockSpec(memory_space=pl.ANY)


def prepare_kernel(parts, turn_of, sight, mapping, residual, counts, track, knots, orbit, planes,
                   extra, mine, sem):
    stations, _, tracked, _ = sight.shape
    half = mine.shape[0]
    at = turn_of(lax.axis_index("sta")) * half if parts > 1 else 0
    cut = pltpu.make_async_copy(orbit.at[pl.ds(at, half)], mine, sem)
    cut.start()
    for s in range(stations):
        weight = counts[s].astype(jnp.float32)
        total = jnp.maximum(jnp.sum(weight, 0, keepdims=True), 1.0)
        root = jnp.sqrt(total)
        scaled = weight / root
        for c in range(3):
            planes[s, c * tracked : (c + 1) * tracked, :] = sight[s, c] * scaled
        map_mean = jnp.sum(weight * mapping[s], 0, keepdims=True) / total
        res_mean = jnp.sum(weight * residual[s], 0, keepdims=True) / total
        map_off = mapping[s] - map_mean
        res_off = residual[s] - res_mean
        weighted_off = weight * map_off
        map_square = jnp.sum(weighted_off * map_off, 0, keepdims=True)
        map_res = jnp.sum(weighted_off * res_off, 0, keepdims=True)
        knot = knots[s : s + 1, :]
        inverse = jnp.zeros_like(total)
        right = jnp.zeros_like(total)
        for k in range(KNOTS):
            select = (knot == k).astype(jnp.float32)
            diagonal = jnp.sum(select * map_square, 1, keepdims=True) + PRIOR
            root_inverse = 1.0 / jnp.sqrt(diagonal)
            local = jnp.sum(select * map_res, 1, keepdims=True)
            inverse = inverse + select * root_inverse
            right = right + select * (local * root_inverse)
        tropo = map_off * (root * inverse)
        planes[s, 3 * tracked : 4 * tracked, :] = tropo
        planes[s, 4 * tracked :, :] = jnp.zeros((8, knot.shape[1]), jnp.float32)
        planes[s, 4 * tracked : 4 * tracked + 1, :] = knot.astype(jnp.float32)
        planes[s, 4 * tracked + 1 : 4 * tracked + 2, :tracked] = track[s : s + 1, :].astype(
            jnp.float32
        )
        extra[s, :tracked, :] = res_off * root - tropo * right
        extra[s, tracked:, :] = jnp.where(weight > 0.0, total / jnp.maximum(weight, 1.0), 0.0)
    cut.wait()


def prepare(sight, mapping, residual, counts, track, knots, orbit, parts, turn_of):
    stations, _, tracked, epochs = sight.shape
    f32 = jnp.float32
    return pl.pallas_call(
        functools.partial(prepare_kernel, parts, turn_of),
        out_shape=[
            jax.ShapeDtypeStruct((stations, 4 * tracked + 8, epochs), f32),
            jax.ShapeDtypeStruct((stations, 2 * tracked, epochs), f32),
            jax.ShapeDtypeStruct((orbit.shape[0] // parts,) + orbit.shape[1:], f32),
        ],
        in_specs=[vmem()] * 6 + [anywhere()],
        out_specs=[vmem()] * 3,
        scratch_shapes=[pltpu.SemaphoreType.DMA],
        compiler_params=pltpu.CompilerParams(vmem_limit_bytes=SMALL_LIMIT),
        name="prepare",
    )(sight, mapping, residual, counts, track, knots, orbit)


def window_start(i, columns, sats, window):
    return jnp.minimum(lax.div(i * columns, 8), sats - window)


def split(value):
    high = value.astype(jnp.bfloat16)
    return high, (value - high.astype(jnp.float32)).astype(jnp.bfloat16)


def dot_nt(left, right, precision=None):
    return lax.dot_general(left, right, NT, precision=precision,
                           preferred_element_type=jnp.float32)


def main_kernel(groups, per, own, nx, nz, window, places, *refs):
    plane_pieces = refs[:groups]
    orbit_pieces = refs[groups : groups + len(places)]
    outs = refs[groups + len(places) : groups + len(places) + nx]
    own_out = refs[groups + len(places) + nx]
    (track, rows_int, planes, orbit, acc, stream, dense, product, tropo, spread_tropo, sems,
     track_sem) = refs[groups + len(places) + nx + 1 :]
    stations, tracked, _, width = product.shape
    epochs = planes.shape[2]
    sats = orbit.shape[0]
    span = tracked * 8
    spare = width - own * 8
    packed = spare // KNOTS
    me = lax.axis_index("sat")
    mine = lax.axis_index("sta")
    first = me * own

    copies = []
    for d in range(groups):
        copies.append(pltpu.make_async_copy(
            plane_pieces[d], planes.at[pl.ds(d * per, per)], sems.at[d]))
    for n, (d, part, parts) in enumerate(places):
        size = own // parts
        at = (me ^ d) * own
        if parts > 1:
            at = at + (lax.rem(lax.div(mine, nx), 2) ^ part) * size
        copies.append(pltpu.make_async_copy(
            orbit_pieces[n], orbit.at[pl.ds(at, size)], sems.at[groups + n]))
    for copy in copies:
        copy.start()
    acc[...] = jnp.zeros_like(acc)
    dense[...] = jnp.zeros_like(dense)
    spread_tropo[...] = jnp.zeros_like(spread_tropo)
    for copy in copies[:groups]:
        copy.wait()
    for s in range(stations):
        rows_int[s : s + 1, :] = planes[
            s, 4 * tracked + 1 : 4 * tracked + 2, :128].astype(jnp.int32)
    to_scalar = pltpu.make_async_copy(rows_int, track, track_sem)
    to_scalar.start()
    to_scalar.wait()
    for copy in copies[groups:]:
        copy.wait()

    def build(s, carry):
        for pair in range(0, tracked, 2):
            values, mixed = [], []
            for m in (pair, pair + 1):
                k = track[s, m]
                local = k - first
                inside = jnp.logical_and(local >= 0, local < own)

                def row(plane):
                    return planes[s, pl.ds(plane * tracked + m, 1), :]

                value = row(0) * orbit[k, 0] + row(1) * orbit[k, 1] + row(2) * orbit[k, 2]
                dense[s, jnp.where(inside, local, own)] = value
                values.append(value)
                mixed.append(value * row(3))
            rows = slice(pair * 8, pair * 8 + 16)
            high, low = split(jnp.concatenate(values, 0))
            stream[s, pair * 8 : pair * 8 + 16, :] = high
            stream[s, span + pair * 8 : span + pair * 8 + 16, :] = low
            high, low = split(jnp.concatenate(mixed, 0))
            stream[s, 2 * span + pair * 8 : 2 * span + pair * 8 + 16, :] = high
            stream[s, 3 * span + pair * 8 : 3 * span + pair * 8 + 16, :] = low
        return carry

    lax.fori_loop(0, stations, build, 0)

    lane = lax.broadcasted_iota(jnp.int32, (span, 128), 1) - (128 - spare)
    index = lax.broadcasted_iota(jnp.int32, (spare, epochs), 0)

    def multiply(s, carry):
        turn = lax.rem(s, packed)
        knot = planes[s, 4 * tracked : 4 * tracked + 1, :].astype(jnp.int32)
        select = (index - turn * KNOTS == knot).astype(jnp.float32)
        rows = jnp.concatenate(
            [dense[s].reshape((own + 1) * 8, epochs)[: own * 8], select], 0)
        high, low = split(rows)
        large = dot_nt(stream[s], high)
        result = large[:span] + large[span : 2 * span] + dot_nt(stream[s, :span, :], low)
        product[s] = result.reshape(tracked, 8, width)
        mixed = large[2 * span : 3 * span, width - 128 :] + large[3 * span :, width - 128 :]
        kept = jnp.logical_and(lane >= turn * KNOTS, lane < turn * KNOTS + KNOTS)
        tropo[s] = jnp.where(kept, mixed, 0.0).reshape(tracked, 8, 128)
        return carry

    lax.fori_loop(0, stations, multiply, 0)

    def scatter(s, carry):
        slab = lax.div(s, packed)
        for m in range(tracked):
            k = track[s, m]
            acc[k] = acc[k] - product[s, m]
            spread_tropo[slab, k] = spread_tropo[slab, k] + tropo[s, m]
        return carry

    lax.fori_loop(0, stations, scatter, 0)

    slabs = spread_tropo.shape[0]
    left, right = [], []
    for slab in range(slabs):
        high, low = split(spread_tropo[slab].reshape(sats * 8, 128))
        own_high, own_low = split(
            spread_tropo[slab, pl.ds(first, own + 0)].reshape(own * 8, 128))
        left += [high, high, low]
        right += [own_high, own_low, own_high]
    outer = dot_nt(jnp.concatenate(left, 1), jnp.concatenate(right, 1))
    if own * 8 < width:
        outer = jnp.concatenate(
            [outer, jnp.zeros((sats * 8, width - own * 8), jnp.float32)], 1)
    acc[...] = acc[...] - outer.reshape(sats, 8, width)

    own_out[...] = acc[pl.ds(first, own)]
    for dx in range(nx):
        for dz in range(nz):
            start = window_start(mine ^ (dz * nx + dx), sats * 8 // (nx * nz), sats, window)
            outs[dx][dz * window : (dz + 1) * window] = acc[pl.ds(start, window)]


def accumulate(planes, orbits, places, tracked, sats, nx, nz, window, width):
    groups = len(planes)
    per, rows, epochs = planes[0].shape
    own = sats // groups
    stations = groups * per
    slabs = -(-stations // ((width - own * 8) // KNOTS))
    out = jax.ShapeDtypeStruct((nz * window, 8, width), jnp.float32)
    return pl.pallas_call(
        functools.partial(main_kernel, groups, per, own, nx, nz, window, places),
        out_shape=[out] * nx + [jax.ShapeDtypeStruct((own, 8, width), jnp.float32)],
        in_specs=[anywhere()] * (groups + len(orbits)),
        out_specs=[vmem()] * (nx + 1),
        scratch_shapes=[
            pltpu.SMEM((stations, 128), jnp.int32),
            pltpu.VMEM((stations, 128), jnp.int32),
            pltpu.VMEM((stations, rows, epochs), jnp.float32),
            pltpu.VMEM((sats,) + orbits[0].shape[1:], jnp.float32),
            pltpu.VMEM((sats, 8, width), jnp.float32),
            pltpu.VMEM((stations, 4 * tracked * 8, epochs), jnp.bfloat16),
            pltpu.VMEM((stations, own + 1, 8, epochs), jnp.float32),
            pltpu.VMEM((stations, tracked, 8, width), jnp.float32),
            pltpu.VMEM((stations, tracked, 8, 128), jnp.float32),
            pltpu.VMEM((slabs, sats, 8, 128), jnp.float32),
            pltpu.SemaphoreType.DMA((groups + len(orbits),)),
            pltpu.SemaphoreType.DMA,
        ],
        compiler_params=pltpu.CompilerParams(vmem_limit_bytes=LARGE_LIMIT),
        cost_estimate=pl.CostEstimate(
            flops=8 * 10**9, bytes_accessed=8 * 10**6, transcendentals=0),
        name="accumulate",
    )(*planes, *orbits)


def blocks_kernel(groups, per, own, *refs):
    plane_pieces = refs[:groups]
    extra_pieces = refs[groups : 2 * groups]
    own_rows, orbit, small = refs[2 * groups :]
    tracked = extra_pieces[0].shape[1] // 2
    epochs = orbit.shape[3]
    width = own_rows.shape[2]
    first = lax.axis_index("sat") * own
    satellite = first + lax.broadcasted_iota(jnp.int32, (own, tracked), 0)
    pairs = [(0, 0), (0, 1), (0, 2), (1, 1), (1, 2), (2, 2)]
    sums = [jnp.zeros((own, epochs), jnp.float32) for _ in range(9)]
    for d in range(groups):
        for s in range(per):
            named = plane_pieces[d][s, 4 * tracked + 1 : 4 * tracked + 2, :tracked]
            pick = (satellite == named.astype(jnp.int32)).astype(jnp.float32)
            a = [plane_pieces[d][s, c * tracked : (c + 1) * tracked, :] for c in range(3)]
            residual = extra_pieces[d][s, :tracked, :]
            inverse = extra_pieces[d][s, tracked:, :]
            weighted = [v * inverse for v in a]
            terms = [weighted[c] * a[e] for c, e in pairs] + [v * residual for v in a]
            for n in range(9):
                sums[n] = sums[n] + jnp.dot(pick, terms[n], precision=HIGHEST,
                                            preferred_element_type=jnp.float32)
    index = {}
    for n, (c, e) in enumerate(pairs):
        index[c, e] = index[e, c] = n

    def spread(value):
        return jnp.broadcast_to(value[:, None, :], (own, 8, epochs))

    parts = [orbit[:, c].reshape(own * 8, epochs) for c in range(3)]
    wide = [spread(value).reshape(own * 8, epochs) for value in sums]
    blocks = jnp.zeros((own * 8, own * 8), jnp.float32)
    right_rows = jnp.zeros((own * 8, epochs), jnp.float32)
    for c in range(3):
        mixed = sum(wide[index[c, e]] * parts[e] for e in range(3))
        blocks = blocks + dot_nt(parts[c], mixed, HIGHEST)
        right_rows = right_rows + wide[6 + c] * parts[c]
    right = dot_nt(jnp.ones((8, epochs), jnp.float32), right_rows, HIGHEST)
    owner = lax.broadcasted_iota(jnp.int32, (8, own * 8), 1) // 8
    folded = jnp.zeros((8, own * 8), jnp.float32)
    for o in range(own):
        tile = own_rows[o, :, : own * 8] + blocks[o * 8 : o * 8 + 8, :]
        folded = folded + jnp.where(owner == o, tile, 0.0)
    small[...] = jnp.zeros_like(small)
    small[0, :, : own * 8] = folded
    small[1, :, : own * 8] = right


def own_sums(planes, extras, own_rows, orbit):
    groups = len(planes)
    per = planes[0].shape[0]
    own, _, width = own_rows.shape
    return pl.pallas_call(
        functools.partial(blocks_kernel, groups, per, own),
        out_shape=jax.ShapeDtypeStruct((2, 8, width), jnp.float32),
        in_specs=[vmem()] * (2 * groups + 2),
        out_specs=vmem(),
        compiler_params=pltpu.CompilerParams(vmem_limit_bytes=MEDIUM_LIMIT),
        cost_estimate=pl.CostEstimate(
            flops=4 * 10**9, bytes_accessed=4 * 10**6, transcendentals=0),
        name="own_sums",
    )(*planes, *extras, own_rows, orbit)


def combine_kernel(nx, nz, window, *refs):
    pieces = refs[:nx]
    smalls = refs[nx : 2 * nx]
    outs = refs[2 * nx :]
    small = smalls[0][...]
    for piece in smalls[1:]:
        small = small + piece[...]
    for dz in range(nz):
        part = pieces[0][dz * window : (dz + 1) * window]
        for piece in pieces[1:]:
            part = part + piece[dz * window : (dz + 1) * window]
        outs[dz][:window] = part
        outs[dz][window:] = small


def combine(pieces, smalls, nz, window):
    nx = len(pieces)
    width = pieces[0].shape[2]
    out = jax.ShapeDtypeStruct((window + 2, 8, width), jnp.float32)
    return pl.pallas_call(
        functools.partial(combine_kernel, nx, nz, window),
        out_shape=[out] * nz,
        in_specs=[vmem()] * (2 * nx),
        out_specs=[vmem()] * nz,
        compiler_params=pltpu.CompilerParams(vmem_limit_bytes=SMALL_LIMIT),
        name="combine",
    )(*pieces, *smalls)


def finish_kernel(nz, window, own, columns, sats, factor, cross_factor, *refs):
    pieces = refs[:nz]
    normal, right, blocks = refs[nz:]
    width = pieces[0].shape[2]
    total = pieces[0][...]
    for piece in pieces[1:]:
        total = total + piece[...]
    first = lax.axis_index("sat") * own
    start = window_start(lax.axis_index("sta"), columns, sats, window)
    span = own * 8
    part = total[:window].reshape(window * 8, width)
    row_owner = start + lax.broadcasted_iota(jnp.int32, part.shape, 0) // 8
    lane_owner = first + lax.broadcasted_iota(jnp.int32, part.shape, 1) // 8
    part = jnp.where(row_owner == lane_owner, 0.0, part * cross_factor)
    normal[...] = part.T[:span, :]
    right[...] = total[window + 1, :1, :span] * factor
    small = total[window]
    lane = lax.broadcasted_iota(jnp.int32, (width, own), 0)
    wanted = lax.broadcasted_iota(jnp.int32, (width, own), 1) * 8
    for p in range(8):
        pick = (lane == wanted + p).astype(jnp.float32)
        blocks[p] = factor * jnp.dot(small, pick, precision=HIGHEST,
                                     preferred_element_type=jnp.float32)


def finish(pieces, window, own, columns, sats, factor, cross_factor):
    nz = len(pieces)
    return pl.pallas_call(
        functools.partial(finish_kernel, nz, window, own, columns, sats, factor, cross_factor),
        out_shape=[
            jax.ShapeDtypeStruct((own * 8, window * 8), jnp.float32),
            jax.ShapeDtypeStruct((1, own * 8), jnp.float32),
            jax.ShapeDtypeStruct((8, 8, own), jnp.float32),
        ],
        in_specs=[vmem()] * nz,
        out_specs=[vmem()] * 3,
        compiler_params=pltpu.CompilerParams(vmem_limit_bytes=SMALL_LIMIT),
        name="finish",
    )(*pieces)


def shift(value, axis, size, step):
    return lax.ppermute(value, axis, [(i, i ^ step) for i in range(size)])


def gather_pieces(value, size):
    pieces = [None] * size
    pieces[0] = value
    for d in range(2, size, 2):
        pieces[d] = shift(value, "sat", size, d)
    for d in range(0, size, 2):
        pieces[d + 1] = shift(pieces[d], "sat", size, 1)
    return pieces


def gather_orbit(orbit, mine, size, columns_axis, nx):
    if mine is None:
        return gather_pieces(orbit, size), tuple((d, 0, 1) for d in range(size))
    pieces, places = [orbit], [(0, 0, 1)]
    for d in range(2, size, 2):
        near = shift(mine, "sat", size, d)
        far = shift(near, "sta", columns_axis, nx)
        pieces += [near, far]
        places += [(d, 0, 2), (d, 1, 2)]
    for piece, (d, part, parts) in list(zip(pieces, places)):
        pieces.append(shift(piece, "sat", size, 1))
        places.append((d + 1, part, parts))
    return pieces, tuple(places)


def shards(sight, mapping, residual, counts, track, knots, orbit):
    group = lax.axis_size("sat")
    columns_axis = lax.axis_size("sta")
    nx = 1 << ((columns_axis.bit_length()) // 2 - (0 if columns_axis.bit_length() % 2 else 1))
    nz = columns_axis // nx
    own, _, params, epochs = orbit.shape
    stations, _, tracked, _ = sight.shape
    sats = own * group
    span = sats * params
    columns = span // columns_axis
    width = -(-(own * params) // 128) * 128

    window = max(
        -(-(((columns * i) % 8) + columns) // 8) for i in range(columns_axis)
    )

    parts = 2 if own % 2 == 0 and nz > 1 else 1
    planes, extra, half = prepare(
        sight, mapping, residual, counts, track, knots, orbit, parts,
        lambda mine: lax.rem(lax.div(mine, nx), 2),
    )
    orbit_pieces, places = gather_orbit(
        orbit, half if parts > 1 else None, group, columns_axis, nx)
    plane_pieces = gather_pieces(planes, group)
    extra_pieces = gather_pieces(extra, group)
    *sums, own_rows = accumulate(
        plane_pieces, orbit_pieces, places, tracked, sats, nx, nz, window, width)
    small = own_sums(plane_pieces, extra_pieces, own_rows, orbit)
    arrived = [sums[0]] + [shift(sums[d], "sta", columns_axis, d) for d in range(1, nx)]
    smalls = [small] + [shift(small, "sta", columns_axis, d) for d in range(1, nx)]
    chunks = combine(arrived, smalls, nz, window)
    final = [chunks[0]] + [
        shift(chunks[d], "sta", columns_axis, d * nx) for d in range(1, nz)
    ]
    total_stations = stations * columns_axis * group
    factor = sats / (total_stations * tracked * epochs)
    cross_factor = sats / (total_stations * epochs) ** 0.5
    normal, right, blocks = finish(final, window, own, columns, sats, factor, cross_factor)
    if window * 8 != columns:
        mine = lax.axis_index("sta")
        start = window_start(mine, columns, sats, window)
        normal = lax.dynamic_slice_in_dim(normal, mine * columns - start * 8, columns, 1)
    return normal, right.reshape(own * params), jnp.transpose(blocks, (2, 0, 1))


def solution(mesh):
    placed = (
        P(("sta", "sat"), None, None, None),
        P(("sta", "sat"), None, None),
        P(("sta", "sat"), None, None),
        P(("sta", "sat"), None, None),
        P(("sta", "sat"), None),
        P(("sta", "sat"), None),
        P("sat", None, None, None),
    )
    return jax.shard_map(
        shards,
        mesh=mesh,
        in_specs=placed,
        out_specs=(P("sat", "sta"), P("sat"), P("sat", None, None)),
        check_vma=False,
    )
```

time: 67.4 us -> 72.4 us (1.074)
  local copies, waits for them, and re-layouts: 1.15 us -> 5.92 us
  waiting for transfers between devices: 39.4 us -> 36.9 us
  starting transfers between devices: 12.1 us -> 14.3 us
    unnamed x14 -> x16, local copies, waits for them, and re-layouts: 0.03 us -> 5.92 us
    pallas_call x1, Pallas kernels: 12.3 us -> 8.7 us  [accumulate(): pl.pallas_call(functools.partial(main_kernel, groups, per, own, nx, nz, w...]
    pallas_call x1 -> x2, Pallas kernels: 0.17 us -> 3.74 us  [the longest x1 3.41 us: own_sums(): pl.pallas_call(functools.partial(blocks_kernel, groups, per, own), out_sh...]
    ppermute x12 -> x16, waiting for transfers between devices: 39.4 us -> 36.9 us  [shift(): return lax.ppermute(value, axis, [(i, i ^ step) for i in range(size)])]
    ppermute x12 -> x16, starting transfers between devices: 12.1 us -> 14.3 us  [shift(): return lax.ppermute(value, axis, [(i, i ^ step) for i in range(size)])]
    dynamic_slice x1 -> x0, local copies, waits for them, and re-layouts: 1.12 us -> none  [gather_orbit(): mine = lax.dynamic_slice_in_dim(orbit, turn * half, half, 0)]
  transfers between devices with their start and end apart: 12 -> 16, of which waited for: 8 -> 8; matrix products, arithmetic and copies ran while one was open for 0% -> 0% of each run, Pallas kernels for 0% -> 17%
where the time goes in v3:
time: 72.4 us; the launch traced here: 71.5 us
  waiting for transfers between devices  36.9 us (51%)
  starting transfers between devices  14.3 us (20%)
  Pallas kernels  13.7 us (19%)
  local copies, waits for them, and re-layouts  5.92 us (8%)
    ppermute x16, waiting for transfers between devices, shift(): return lax.ppermute(value, axis, [(i, i ^ step) for i in range(size)])  36.9 us
    ppermute x16, starting transfers between devices, shift(): return lax.ppermute(value, axis, [(i, i ^ step) for i in range(size)])  14.3 us
    pallas_call x1, Pallas kernels, accumulate(): pl.pallas_call(functools.partial(main_kernel, groups, per, own, nx, nz, w...  8.7 us
    unnamed x16, local copies, waits for them, and re-layouts  5.92 us
    pallas_call x1, Pallas kernels, own_sums(): pl.pallas_call(functools.partial(blocks_kernel, groups, per, own), out_sh...  3.41 us
  transfers between devices with their start and end apart: 16, of which 8 were waited for; matrix products, arithmetic and copies ran while one was open for 0% of the time, Pallas kernels for 17%

profile of v3, /device:TPU:0, one launch (start us, length us, event | category | flops | bytes accessed | tf_op | source)
XLA Modules:
  0.0 71.5 jit_solution(1165550764622452905)
XLA Ops:
  0.6 0.0 copy-start
  0.6 1.1 %copy-done = f32[30,3,8,256]{3,2,1,0:T(8,128)S(1)} copy-done((f32[30,3,8,256]{3,2,1,0:T(8,128)S(1)}, f32[30,3,8,256]{3,2,1,0:T(8,128)}, u32[]{:S(2)}) %copy-start) | copy-done | bytes 737304
  1.7 0.0 copy-start.2
  1.8 0.9 %copy-done.2 = f32[2,3,32,256]{3,2,1,0:T(8,128)S(1)} copy-done((f32[2,3,32,256]{3,2,1,0:T(8,128)S(1)}, f32[2,3,32,256]{3,2,1,0:T(8,128)}, u32[]{:S(2)}) %copy-start.2) | copy-done | bytes 196632
  2.7 0.0 copy-start.3
  2.7 0.8 %copy-done.3 = f32[2,32,256]{2,1,0:T(8,128)S(1)} copy-done((f32[2,32,256]{2,1,0:T(8,128)S(1)}, f32[2,32,256]{2,1,0:T(8,128)}, u32[]{:S(2)}) %copy-start.3) | copy-done | bytes 65560
  3.5 0.0 copy-start.4
  3.5 0.8 %copy-done.4 = f32[2,32,256]{2,1,0:T(8,128)S(1)} copy-done((f32[2,32,256]{2,1,0:T(8,128)S(1)}, f32[2,32,256]{2,1,0:T(8,128)}, u32[]{:S(2)}) %copy-start.4) | copy-done | bytes 65560
  4.4 0.0 copy-start.5
  4.4 0.8 %copy-done.5 = s32[2,32,256]{2,1,0:T(8,128)S(1)} copy-done((s32[2,32,256]{2,1,0:T(8,128)S(1)}, s32[2,32,256]{2,1,0:T(8,128)}, u32[]{:S(2)}) %copy-start.5) | copy-done | bytes 65560
  5.2 0.0 copy-start.6
  5.2 0.7 copy-done.6
  5.9 0.0 copy-start.7
  5.9 0.7 copy-done.7
  6.6 0.0 copy-start.1
  6.6 0.3 prepare.1
  6.9 3.0 %collective-permute-start.3 = (f32[15,3,8,256]{3,2,1,0:T(8,128)S(1)}, f32[15,3,8,256]{3,2,1,0:T(8,128)S(1)}, u32[]{:S(2)}, u32[]{:S(2)}) collective-permute-start(f32[15,3,8,256]{3,2,1,0:T(8,128)S(1)} %get-tuple-element.17), channel_id=1, source_target_pairs={{0,2},{1,3},{2,0},{3,1},{4,6},{5,7},{6,4},{7,5},{8,10},{9,11},{10,... | collective-permute-start | bytes 1105928 | tf_op jit(solution)/shard_map/ppermute | solution.py:396
  9.9 8.6 %collective-permute-done.3.refs_5_ = f32[15,3,8,256]{3,2,1,0:T(8,128)S(1)} collective-permute-done((f32[15,3,8,256]{3,2,1,0:T(8,128)S(1)}, f32[15,3,8,256]{3,2,1,0:T(8,128)S(1)}, u32[]{:S(2)}, u32[]{:S(2)}) %collective-permute-start.3) | collective-permute-done | bytes 368672 | tf_op jit(solution)/shard_map/ppermute | solution.py:396
  18.5 1.8 %collective-permute-start.4 = (f32[15,3,8,256]{3,2,1,0:T(8,128)S(1)}, f32[15,3,8,256]{3,2,1,0:T(8,128)S(1)}, u32[]{:S(2)}, u32[]{:S(2)}) collective-permute-start(f32[15,3,8,256]{3,2,1,0:T(8,128)S(1)} %collective-permute-done.3.refs_5_), channel_id=1, source_target_pairs={{0,8},{4,12},{8,0},{12,4},{16,24},{20,28},{24,16},{28,20},{1,9},{5... | collective-permute-start | bytes 1105928 | tf_op jit(solution)/shard_map/ppermute | solution.py:396
  20.3 0.0 collective-permute-start.5
  20.3 1.5 %collective-permute-start.1 = (f32[2,136,256]{2,1,0:T(8,128)S(1)}, f32[2,136,256]{2,1,0:T(8,128)S(1)}, u32[]{:S(2)}, u32[]{:S(2)}) collective-permute-start(f32[2,136,256]{2,1,0:T(8,128)S(1)} %get-tuple-element.16.refs_0_), channel_id=1, source_target_pairs={{0,2},{1,3},{2,0},{3,1},{4,6},{5,7},{6,4},{7,5},{8,10},{9,11},{10,... | collective-permute-start | bytes 835592 | tf_op jit(solution)/shard_map/ppermute | solution.py:396
  21.8 0.5 collective-permute-start.10
  22.3 0.0 collective-permute-start.6
  22.4 5.9 %collective-permute-done.4.refs_6_ = f32[15,3,8,256]{3,2,1,0:T(8,128)S(1)} collective-permute-done((f32[15,3,8,256]{3,2,1,0:T(8,128)S(1)}, f32[15,3,8,256]{3,2,1,0:T(8,128)S(1)}, u32[]{:S(2)}, u32[]{:S(2)}) %collective-permute-start.4) | collective-permute-done | bytes 368672 | tf_op jit(solution)/shard_map/ppermute | solution.py:396
  28.3 0.0 collective-permute-start.7
  28.3 3.9 %collective-permute-done.10.refs_6_ = f32[2,64,256]{2,1,0:T(8,128)S(1)} collective-permute-done((f32[2,64,256]{2,1,0:T(8,128)S(1)}, f32[2,64,256]{2,1,0:T(8,128)S(1)}, u32[]{:S(2)}, u32[]{:S(2)}) %collective-permute-start.10) | collective-permute-done | bytes 131104 | tf_op jit(solution)/shard_map/ppermute | solution.py:396
  32.2 0.0 collective-permute-start
  32.2 0.0 collective-permute-done.1.refs_2_
  32.2 0.5 collective-permute-start.2
  32.7 1.0 %collective-permute-done.refs_1_ = f32[2,136,256]{2,1,0:T(8,128)S(1)} collective-permute-done((f32[2,136,256]{2,1,0:T(8,128)S(1)}, f32[2,136,256]{2,1,0:T(8,128)S(1)}, u32[]{:S(2)}, u32[]{:S(2)}) %collective-permute-start) | collective-permute-done | bytes 278560 | tf_op jit(solution)/shard_map/ppermute | solution.py:396
  33.8 0.1 collective-permute-start.9
  33.9 0.3 collective-permute-done.2.refs_3_
  34.2 0.1 collective-permute-start.11
  34.3 0.0 collective-permute-done.6.refs_8_
  34.3 0.0 collective-permute-done.5.refs_7_
  34.3 0.0 collective-permute-done.7.refs_9_
  34.3 0.0 copy-done.1
  34.3 8.7 %accumulate.1 = (f32[60,8,256]{2,1,0:T(8,128)S(1)}, f32[60,8,256]{2,1,0:T(8,128)S(1)}, f32[30,8,256]{2,1,0:T(8,128)S(1)}) custom-call(f32[2,136,256]{2,1,0:T(8,128)S(1)} %get-tuple-element.16.refs_0_, f32[2,136,256]{2,1,0:T(8,128)S(1)} %collective-permute-done.refs_1_, f32[2,136,256]{2,1,0:T(8,128)S(1)} %collective-permute-done.1.refs_2_, ...), custom_call_target="tpu_custom_call" | custom-call | flops 8000000000 | bytes 8000000 | tf_op jit(solution)/shard_map/accumulate/pallas_call | solution.py:234
  43.0 1.6 %collective-permute-start.8 = (f32[60,8,256]{2,1,0:T(8,128)S(1)}, f32[60,8,256]{2,1,0:T(8,128)S(1)}, u32[]{:S(2)}, u32[]{:S(2)}) collective-permute-start(f32[60,8,256]{2,1,0:T(8,128)S(1)} %get-tuple-element.19), channel_id=1, source_target_pairs={{0,4},{4,0},{8,12},{12,8},{16,20},{20,16},{24,28},{28,24},{1,5},{5... | collective-permute-start | bytes 1474568 | tf_op jit(solution)/shard_map/ppermute | solution.py:396
  44.6 0.0 collective-permute-done.9.refs_5_
  44.6 0.0 collective-permute-done.11.refs_7_
  44.6 3.4 %own_sums.1.refs_2_ = f32[2,8,256]{2,1,0:T(8,128)S(1)} custom-call(f32[2,136,256]{2,1,0:T(8,128)S(1)} %get-tuple-element.16.refs_0_, f32[2,136,256]{2,1,0:T(8,128)S(1)} %collective-permute-done.refs_1_, f32[2,136,256]{2,1,0:T(8,128)S(1)} %collective-permute-done.1.refs_2_, f32[2,136,256]{2,1,0:T(8,128)S(1)} %collective-permute-done.2.refs_3_, ...), custom_call_target="tpu_custom_call" | custom-call | flops 4000000000 | bytes 4000000 | tf_op jit(solution)/shard_map/own_sums/pallas_call | solution.py:313
  48.0 0.6 collective-permute-start.12
  48.6 8.3 %collective-permute-done.12.refs_3_ = f32[2,8,256]{2,1,0:T(8,128)S(1)} collective-permute-done((f32[2,8,256]{2,1,0:T(8,128)S(1)}, f32[2,8,256]{2,1,0:T(8,128)S(1)}, u32[]{:S(2)}, u32[]{:S(2)}) %collective-permute-start.12) | collective-permute-done | bytes 16416 | tf_op jit(solution)/shard_map/ppermute | solution.py:396
  56.9 0.0 collective-permute-done.8.refs_1_
  56.9 0.1 combine.1
  57.0 0.3 collective-permute-start.13
  57.3 2.8 %collective-permute-start.14 = (f32[17,8,256]{2,1,0:T(8,128)S(1)}, f32[17,8,256]{2,1,0:T(8,128)S(1)}, u32[]{:S(2)}, u32[]{:S(2)}) collective-permute-start(f32[17,8,256]{2,1,0:T(8,128)S(1)} %get-tuple-element.24), channel_id=1, source_target_pairs={{0,16},{4,20},{8,24},{12,28},{16,0},{20,4},{24,8},{28,12},{1,17},{... | collective-permute-start | bytes 417800 | tf_op jit(solution)/shard_map/ppermute | solution.py:396
  60.1 1.3 %collective-permute-start.15 = (f32[17,8,256]{2,1,0:T(8,128)S(1)}, f32[17,8,256]{2,1,0:T(8,128)S(1)}, u32[]{:S(2)}, u32[]{:S(2)}) collective-permute-start(f32[17,8,256]{2,1,0:T(8,128)S(1)} %get-tuple-element.25), channel_id=1, source_target_pairs={{0,24},{4,28},{8,16},{12,20},{16,8},{20,12},{24,0},{28,4},{1,25},{... | collective-permute-start | bytes 417800 | tf_op jit(solution)/shard_map/ppermute | solution.py:396
  61.4 3.7 %collective-permute-done.13.refs_1_ = f32[17,8,256]{2,1,0:T(8,128)S(1)} collective-permute-done((f32[17,8,256]{2,1,0:T(8,128)S(1)}, f32[17,8,256]{2,1,0:T(8,128)S(1)}, u32[]{:S(2)}, u32[]{:S(2)}) %collective-permute-start.13) | collective-permute-done | bytes 139296 | tf_op jit(solution)/shard_map/ppermute | solution.py:396
  65.2 0.0 collective-permute-done.14.refs_2_
  65.2 5.1 %collective-permute-done.15.refs_3_ = f32[17,8,256]{2,1,0:T(8,128)S(1)} collective-permute-done((f32[17,8,256]{2,1,0:T(8,128)S(1)}, f32[17,8,256]{2,1,0:T(8,128)S(1)}, u32[]{:S(2)}, u32[]{:S(2)}) %collective-permute-start.15) | collective-permute-done | bytes 139296 | tf_op jit(solution)/shard_map/ppermute | solution.py:396
  70.3 1.2 %finish.1 = (f32[240,120]{1,0:T(8,128)}, f32[1,240]{1,0:T(1,128)}, f32[8,8,30]{2,1,0:T(8,128)}) custom-call(f32[17,8,256]{2,1,0:T(8,128)S(1)} %get-tuple-element.22.refs_0_, f32[17,8,256]{2,1,0:T(8,128)S(1)} %collective-permute-done.13.refs_1_, f32[17,8,256]{2,1,0:T(8,128)S(1)} %collective-permute-done.14.refs_2_, ...), custom_call_target="tpu_custom_call" | custom-call | tf_op jit(solution)/shard_map/finish/pallas_call | solution.py:381
Async XLA Ops:
  0.6 1.1 %copy-start = (f32[30,3,8,256]{3,2,1,0:T(8,128)S(1)}, f32[30,3,8,256]{3,2,1,0:T(8,128)}, u32[]{:S(2)}) copy-start(f32[30,3,8,256]{3,2,1,0:T(8,128)} %refs_9_.1) | copy-start | bytes 2211844
  1.7 0.9 %copy-start.2 = (f32[2,3,32,256]{3,2,1,0:T(8,128)S(1)}, f32[2,3,32,256]{3,2,1,0:T(8,128)}, u32[]{:S(2)}) copy-start(f32[2,3,32,256]{3,2,1,0:T(8,128)} %sight.1) | copy-start | bytes 589828
  2.7 0.8 %copy-start.3 = (f32[2,32,256]{2,1,0:T(8,128)S(1)}, f32[2,32,256]{2,1,0:T(8,128)}, u32[]{:S(2)}) copy-start(f32[2,32,256]{2,1,0:T(8,128)} %mapping.1) | copy-start | bytes 196612
  3.5 0.8 %copy-start.4 = (f32[2,32,256]{2,1,0:T(8,128)S(1)}, f32[2,32,256]{2,1,0:T(8,128)}, u32[]{:S(2)}) copy-start(f32[2,32,256]{2,1,0:T(8,128)} %residual.1) | copy-start | bytes 196612
  4.4 0.8 %copy-start.5 = (s32[2,32,256]{2,1,0:T(8,128)S(1)}, s32[2,32,256]{2,1,0:T(8,128)}, u32[]{:S(2)}) copy-start(s32[2,32,256]{2,1,0:T(8,128)} %counts.1) | copy-start | bytes 196612
  5.2 0.7 copy-start.6
  5.9 0.7 copy-start.7
  6.6 27.8 %copy-start.1 = (f32[30,3,8,256]{3,2,1,0:T(8,128)S(1)}, f32[30,3,8,256]{3,2,1,0:T(8,128)}, u32[]{:S(2)}) copy-start(f32[30,3,8,256]{3,2,1,0:T(8,128)} %refs_9_.1) | copy-start | bytes 2211844
  6.9 11.6 %collective-permute-start.3 = (f32[15,3,8,256]{3,2,1,0:T(8,128)S(1)}, f32[15,3,8,256]{3,2,1,0:T(8,128)S(1)}, u32[]{:S(2)}, u32[]{:S(2)}) collective-permute-start(f32[15,3,8,256]{3,2,1,0:T(8,128)S(1)} %get-tuple-element.17), channel_id=1, source_target_pairs={{0,2},{1,3},{2,0},{3,1},{4,6},{5,7},{6,4},{7,5},{8,10},{9,11},{10,... | collective-permute-start | bytes 1105928 | tf_op jit(solution)/shard_map/ppermute | solution.py:396
  18.5 9.8 %collective-permute-start.4 = (f32[15,3,8,256]{3,2,1,0:T(8,128)S(1)}, f32[15,3,8,256]{3,2,1,0:T(8,128)S(1)}, u32[]{:S(2)}, u32[]{:S(2)}) collective-permute-start(f32[15,3,8,256]{3,2,1,0:T(8,128)S(1)} %collective-permute-done.3.refs_5_), channel_id=1, source_target_pairs={{0,8},{4,12},{8,0},{12,4},{16,24},{20,28},{24,16},{28,20},{1,9},{5... | collective-permute-start | bytes 1105928 | tf_op jit(solution)/shard_map/ppermute | solution.py:396
  20.3 14.0 %collective-permute-start.5 = (f32[30,3,8,256]{3,2,1,0:T(8,128)S(1)}, f32[30,3,8,256]{3,2,1,0:T(8,128)S(1)}, u32[]{:S(2)}, u32[]{:S(2)}) collective-permute-start(f32[30,3,8,256]{3,2,1,0:T(8,128)S(1)} %copy-done), channel_id=1, source_target_pairs={{0,1},{1,0},{2,3},{3,2},{4,5},{5,4},{6,7},{7,6},{8,9},{9,8},{10,11... | collective-permute-start | bytes 2211848 | tf_op jit(solution)/shard_map/ppermute | solution.py:396
  20.3 11.9 %collective-permute-start.1 = (f32[2,136,256]{2,1,0:T(8,128)S(1)}, f32[2,136,256]{2,1,0:T(8,128)S(1)}, u32[]{:S(2)}, u32[]{:S(2)}) collective-permute-start(f32[2,136,256]{2,1,0:T(8,128)S(1)} %get-tuple-element.16.refs_0_), channel_id=1, source_target_pairs={{0,2},{1,3},{2,0},{3,1},{4,6},{5,7},{6,4},{7,5},{8,10},{9,11},{10,... | collective-permute-start | bytes 835592 | tf_op jit(solution)/shard_map/ppermute | solution.py:396
  21.8 10.4 %collective-permute-start.10 = (f32[2,64,256]{2,1,0:T(8,128)S(1)}, f32[2,64,256]{2,1,0:T(8,128)S(1)}, u32[]{:S(2)}, u32[]{:S(2)}) collective-permute-start(f32[2,64,256]{2,1,0:T(8,128)S(1)} %get-tuple-element.20.refs_4_), channel_id=1, source_target_pairs={{0,2},{1,3},{2,0},{3,1},{4,6},{5,7},{6,4},{7,5},{8,10},{9,11},{10,... | collective-permute-start | bytes 393224 | tf_op jit(solution)/shard_map/ppermute | solution.py:396
  22.3 11.9 %collective-permute-start.6 = (f32[15,3,8,256]{3,2,1,0:T(8,128)S(1)}, f32[15,3,8,256]{3,2,1,0:T(8,128)S(1)}, u32[]{:S(2)}, u32[]{:S(2)}) collective-permute-start(f32[15,3,8,256]{3,2,1,0:T(8,128)S(1)} %collective-permute-done.3.refs_5_), channel_id=1, source_target_pairs={{0,1},{1,0},{2,3},{3,2},{4,5},{5,4},{6,7},{7,6},{8,9},{9,8},{10,11... | collective-permute-start | bytes 1105928 | tf_op jit(solution)/shard_map/ppermute | solution.py:396
  28.3 6.0 %collective-permute-start.7 = (f32[15,3,8,256]{3,2,1,0:T(8,128)S(1)}, f32[15,3,8,256]{3,2,1,0:T(8,128)S(1)}, u32[]{:S(2)}, u32[]{:S(2)}) collective-permute-start(f32[15,3,8,256]{3,2,1,0:T(8,128)S(1)} %collective-permute-done.4.refs_6_), channel_id=1, source_target_pairs={{0,1},{1,0},{2,3},{3,2},{4,5},{5,4},{6,7},{7,6},{8,9},{9,8},{10,11... | collective-permute-start | bytes 1105928 | tf_op jit(solution)/shard_map/ppermute | solution.py:396
  32.2 1.6 %collective-permute-start = (f32[2,136,256]{2,1,0:T(8,128)S(1)}, f32[2,136,256]{2,1,0:T(8,128)S(1)}, u32[]{:S(2)}, u32[]{:S(2)}) collective-permute-start(f32[2,136,256]{2,1,0:T(8,128)S(1)} %get-tuple-element.16.refs_0_), channel_id=1, source_target_pairs={{0,1},{1,0},{2,3},{3,2},{4,5},{5,4},{6,7},{7,6},{8,9},{9,8},{10,11... | collective-permute-start | bytes 835592 | tf_op jit(solution)/shard_map/ppermute | solution.py:396
  32.2 2.0 %collective-permute-start.2 = (f32[2,136,256]{2,1,0:T(8,128)S(1)}, f32[2,136,256]{2,1,0:T(8,128)S(1)}, u32[]{:S(2)}, u32[]{:S(2)}) collective-permute-start(f32[2,136,256]{2,1,0:T(8,128)S(1)} %collective-permute-done.1.refs_2_), channel_id=1, source_target_pairs={{0,1},{1,0},{2,3},{3,2},{4,5},{5,4},{6,7},{7,6},{8,9},{9,8},{10,11... | collective-permute-start | bytes 835592 | tf_op jit(solution)/shard_map/ppermute | solution.py:396
  33.8 10.8 %collective-permute-start.9 = (f32[2,64,256]{2,1,0:T(8,128)S(1)}, f32[2,64,256]{2,1,0:T(8,128)S(1)}, u32[]{:S(2)}, u32[]{:S(2)}) collective-permute-start(f32[2,64,256]{2,1,0:T(8,128)S(1)} %get-tuple-element.20.refs_4_), channel_id=1, source_target_pairs={{0,1},{1,0},{2,3},{3,2},{4,5},{5,4},{6,7},{7,6},{8,9},{9,8},{10,11... | collective-permute-start | bytes 393224 | tf_op jit(solution)/shard_map/ppermute | solution.py:396
  34.2 10.4 %collective-permute-start.11 = (f32[2,64,256]{2,1,0:T(8,128)S(1)}, f32[2,64,256]{2,1,0:T(8,128)S(1)}, u32[]{:S(2)}, u32[]{:S(2)}) collective-permute-start(f32[2,64,256]{2,1,0:T(8,128)S(1)} %collective-permute-done.10.refs_6_), channel_id=1, source_target_pairs={{0,1},{1,0},{2,3},{3,2},{4,5},{5,4},{6,7},{7,6},{8,9},{9,8},{10,11... | collective-permute-start | bytes 393224 | tf_op jit(solution)/shard_map/ppermute | solution.py:396
  43.0 13.9 %collective-permute-start.8 = (f32[60,8,256]{2,1,0:T(8,128)S(1)}, f32[60,8,256]{2,1,0:T(8,128)S(1)}, u32[]{:S(2)}, u32[]{:S(2)}) collective-permute-start(f32[60,8,256]{2,1,0:T(8,128)S(1)} %get-tuple-element.19), channel_id=1, source_target_pairs={{0,4},{4,0},{8,12},{12,8},{16,20},{20,16},{24,28},{28,24},{1,5},{5... | collective-permute-start | bytes 1474568 | tf_op jit(solution)/shard_map/ppermute | solution.py:396
  48.0 8.9 %collective-permute-start.12 = (f32[2,8,256]{2,1,0:T(8,128)S(1)}, f32[2,8,256]{2,1,0:T(8,128)S(1)}, u32[]{:S(2)}, u32[]{:S(2)}) collective-permute-start(f32[2,8,256]{2,1,0:T(8,128)S(1)} %own_sums.1.refs_2_), channel_id=1, source_target_pairs={{0,4},{4,0},{8,12},{12,8},{16,20},{20,16},{24,28},{28,24},{1,5},{5... | collective-permute-start | bytes 49160 | tf_op jit(solution)/shard_map/ppermute | solution.py:396
  57.0 8.2 %collective-permute-start.13 = (f32[17,8,256]{2,1,0:T(8,128)S(1)}, f32[17,8,256]{2,1,0:T(8,128)S(1)}, u32[]{:S(2)}, u32[]{:S(2)}) collective-permute-start(f32[17,8,256]{2,1,0:T(8,128)S(1)} %get-tuple-element.23), channel_id=1, source_target_pairs={{0,8},{4,12},{8,0},{12,4},{16,24},{20,28},{24,16},{28,20},{1,9},{5... | collective-permute-start | bytes 417800 | tf_op jit(solution)/shard_map/ppermute | solution.py:396
  57.3 7.9 %collective-permute-start.14 = (f32[17,8,256]{2,1,0:T(8,128)S(1)}, f32[17,8,256]{2,1,0:T(8,128)S(1)}, u32[]{:S(2)}, u32[]{:S(2)}) collective-permute-start(f32[17,8,256]{2,1,0:T(8,128)S(1)} %get-tuple-element.24), channel_id=1, source_target_pairs={{0,16},{4,20},{8,24},{12,28},{16,0},{20,4},{24,8},{28,12},{1,17},{... | collective-permute-start | bytes 417800 | tf_op jit(solution)/shard_map/ppermute | solution.py:396
  60.1 10.2 %collective-permute-start.15 = (f32[17,8,256]{2,1,0:T(8,128)S(1)}, f32[17,8,256]{2,1,0:T(8,128)S(1)}, u32[]{:S(2)}, u32[]{:S(2)}) collective-permute-start(f32[17,8,256]{2,1,0:T(8,128)S(1)} %get-tuple-element.25), channel_id=1, source_target_pairs={{0,24},{4,28},{8,16},{12,20},{16,8},{20,12},{24,0},{28,4},{1,25},{... | collective-permute-start | bytes 417800 | tf_op jit(solution)/shard_map/ppermute | solution.py:396

commit v4 on v3

--- a/solution.py
+++ b/solution.py
@@ -12,7 +12,7 @@
 HIGHEST = lax.Precision.HIGHEST
 SMALL_LIMIT = 8 * 1024 * 1024
 MEDIUM_LIMIT = 16 * 1024 * 1024
-LARGE_LIMIT = 32 * 1024 * 1024
+HUGE_LIMIT = 56 * 1024 * 1024
 NT = (((1,), (1,)), ((), ()))
 
 
@@ -20,21 +20,41 @@
     return pl.BlockSpec(memory_space=pltpu.VMEM)
 
 
-def smem():
-    return pl.BlockSpec(memory_space=pltpu.SMEM)
-
-
-def anywhere():
-    return pl.BlockSpec(memory_space=pl.ANY)
-
-
-def prepare_kernel(parts, turn_of, sight, mapping, residual, counts, track, knots, orbit, planes,
-                   extra, mine, sem):
-    stations, _, tracked, _ = sight.shape
+def hbm():
+    return pl.BlockSpec(memory_space=pltpu.HBM)
+
+
+def cut_kernel(turn_of, orbit, mine, sem):
     half = mine.shape[0]
-    at = turn_of(lax.axis_index("sta")) * half if parts > 1 else 0
+    at = turn_of(lax.axis_index("sta")) * half
     cut = pltpu.make_async_copy(orbit.at[pl.ds(at, half)], mine, sem)
     cut.start()
+    cut.wait()
+
+
+def cut_half(orbit, turn_of):
+    return pl.pallas_call(
+        functools.partial(cut_kernel, turn_of),
+        out_shape=jax.ShapeDtypeStruct((orbit.shape[0] // 2,) + orbit.shape[1:], jnp.float32),
+        in_specs=[hbm()],
+        out_specs=vmem(),
+        scratch_shapes=[pltpu.SemaphoreType.DMA],
+        compiler_params=pltpu.CompilerParams(vmem_limit_bytes=HUGE_LIMIT),
+        name="cut_half",
+    )(orbit)
+
+
+def prepare_kernel(*refs):
+    arguments = refs[:6]
+    planes, extra = refs[6:8]
+    sems = refs[14]
+    copies = [pltpu.make_async_copy(arguments[n], refs[8 + n], sems.at[n]) for n in range(6)]
+    for copy in copies:
+        copy.start()
+    for copy in copies:
+        copy.wait()
+    sight, mapping, residual, counts, track, knots = refs[8:14]
+    stations, _, tracked, _ = sight.shape
     for s in range(stations):
         weight = counts[s].astype(jnp.float32)
         total = jnp.maximum(jnp.sum(weight, 0, keepdims=True), 1.0)
@@ -68,25 +88,24 @@
         )
         extra[s, :tracked, :] = res_off * root - tropo * right
         extra[s, tracked:, :] = jnp.where(weight > 0.0, total / jnp.maximum(weight, 1.0), 0.0)
-    cut.wait()
-
-
-def prepare(sight, mapping, residual, counts, track, knots, orbit, parts, turn_of):
-    stations, _, tracked, epochs = sight.shape
+
+
+def prepare(*arguments):
+    stations, _, tracked, epochs = arguments[0].shape
     f32 = jnp.float32
     return pl.pallas_call(
-        functools.partial(prepare_kernel, parts, turn_of),
+        prepare_kernel,
         out_shape=[
             jax.ShapeDtypeStruct((stations, 4 * tracked + 8, epochs), f32),
             jax.ShapeDtypeStruct((stations, 2 * tracked, epochs), f32),
-            jax.ShapeDtypeStruct((orbit.shape[0] // parts,) + orbit.shape[1:], f32),
         ],
-        in_specs=[vmem()] * 6 + [anywhere()],
-        out_specs=[vmem()] * 3,
-        scratch_shapes=[pltpu.SemaphoreType.DMA],
-        compiler_params=pltpu.CompilerParams(vmem_limit_bytes=SMALL_LIMIT),
+        in_specs=[hbm()] * 6,
+        out_specs=[vmem()] * 2,
+        scratch_shapes=[pltpu.VMEM(a.shape, a.dtype) for a in arguments]
+        + [pltpu.SemaphoreType.DMA((6,))],
+        compiler_params=pltpu.CompilerParams(vmem_limit_bytes=HUGE_LIMIT),
         name="prepare",
-    )(sight, mapping, residual, counts, track, knots, orbit)
+    )(*arguments)
 
 
 def window_start(i, columns, sats, window):
@@ -103,15 +122,103 @@
                            preferred_element_type=jnp.float32)
 
 
+def own_rows_kernel(groups, per, own, width, *refs):
+    plane_pieces = refs[:groups]
+    orbit = refs[groups]
+    planes, track, highs, lows = refs[groups + 1 : groups + 5]
+    rows_int, dense_a, dense_b, track_sem = refs[groups + 5 :]
+    denses = (dense_a, dense_b)
+    stations = groups * per
+    tracked = (planes.shape[1] - 8) // 4
+    epochs = planes.shape[2]
+    spare = width - own * 8
+    packed = spare // KNOTS
+    first = lax.axis_index("sat") * own
+
+    for d in range(groups):
+        for p in range(per):
+            s = d * per + p
+            rows_int[s : s + 1, :] = plane_pieces[d][
+                p, 4 * tracked + 1 : 4 * tracked + 2, :128].astype(jnp.int32)
+    to_scalar = pltpu.make_async_copy(rows_int, track, track_sem)
+    to_scalar.start()
+    for d in range(groups):
+        planes[d * per : (d + 1) * per] = plane_pieces[d][...]
+    to_scalar.wait()
+    index = lax.broadcasted_iota(jnp.int32, (spare, epochs), 0)
+
+    def build(s, dense):
+        dense[...] = jnp.zeros_like(dense)
+        for m in range(tracked):
+            local = track[s, m] - first
+            inside = jnp.logical_and(local >= 0, local < own)
+            near = jnp.clip(local, 0, own - 1)
+
+            def row(plane):
+                return planes[s, pl.ds(plane * tracked + m, 1), :]
+
+            value = row(0) * orbit[near, 0] + row(1) * orbit[near, 1] + row(2) * orbit[near, 2]
+            dense[jnp.where(inside, local, own)] = value
+
+    def finish(s, dense):
+        knot = planes[s, 4 * tracked : 4 * tracked + 1, :].astype(jnp.int32)
+        select = (index - lax.rem(s, packed) * KNOTS == knot).astype(jnp.float32)
+        rows = jnp.concatenate(
+            [dense[...].reshape((own + 1) * 8, epochs)[: own * 8], select], 0)
+        highs[s], lows[s] = split(rows)
+
+    build(0, dense_a)
+
+    def visit(i, carry):
+        build(2 * i + 1, dense_b)
+        finish(2 * i, dense_a)
+        build(lax.rem(2 * i + 2, stations), dense_a)
+        finish(2 * i + 1, dense_b)
+        return carry
+
+    lax.fori_loop(0, stations // 2, visit, 0)
+
+
+def own_rows_of(planes, orbit, width):
+    groups = len(planes)
+    per, rows, epochs = planes[0].shape
+    own = orbit.shape[0]
+    stations = groups * per
+    half = jax.ShapeDtypeStruct((stations, width, epochs), jnp.bfloat16)
+    return pl.pallas_call(
+        functools.partial(own_rows_kernel, groups, per, own, width),
+        out_shape=[
+            jax.ShapeDtypeStruct((stations, rows, epochs), jnp.float32),
+            jax.ShapeDtypeStruct((stations, 128), jnp.int32),
+            half,
+            half,
+        ],
+        in_specs=[vmem()] * (groups + 1),
+        out_specs=[vmem(), pl.BlockSpec(memory_space=pltpu.SMEM), vmem(), vmem()],
+        scratch_shapes=[
+            pltpu.VMEM((stations, 128), jnp.int32),
+            *[pltpu.VMEM((own + 1, 8, epochs), jnp.float32)] * 2,
+            pltpu.SemaphoreType.DMA,
+        ],
+        compiler_params=pltpu.CompilerParams(vmem_limit_bytes=MEDIUM_LIMIT),
+        cost_estimate=pl.CostEstimate(
+            flops=8 * 10**9, bytes_accessed=8 * 10**6, transcendentals=0),
+        name="own_rows",
+    )(*planes, orbit)
+
+
 def main_kernel(groups, per, own, nx, nz, window, places, *refs):
-    plane_pieces = refs[:groups]
-    orbit_pieces = refs[groups : groups + len(places)]
-    outs = refs[groups + len(places) : groups + len(places) + nx]
-    own_out = refs[groups + len(places) + nx]
-    (track, rows_int, planes, orbit, acc, stream, dense, product, tropo, spread_tropo, sems,
-     track_sem) = refs[groups + len(places) + nx + 1 :]
-    stations, tracked, _, width = product.shape
-    epochs = planes.shape[2]
+    planes, track, highs, lows = refs[:4]
+    refs = refs[4:]
+    orbit_pieces = refs[: len(places)]
+    outs = refs[len(places) : len(places) + nx]
+    own_out = refs[len(places) + nx]
+    (orbit, acc, stream_a, stream_b, product_a, product_b, tropo_a, tropo_b,
+     spread_tropo) = refs[len(places) + nx + 1 :]
+    streams = (stream_a, stream_b)
+    products, tropos = (product_a, product_b), (tropo_a, tropo_b)
+    stations = groups * per
+    tracked, _, width = product_a.shape
     sats = orbit.shape[0]
     span = tracked * 8
     spare = width - own * 8
@@ -120,95 +227,80 @@
     mine = lax.axis_index("sta")
     first = me * own
 
-    copies = []
-    for d in range(groups):
-        copies.append(pltpu.make_async_copy(
-            plane_pieces[d], planes.at[pl.ds(d * per, per)], sems.at[d]))
     for n, (d, part, parts) in enumerate(places):
         size = own // parts
         at = (me ^ d) * own
         if parts > 1:
             at = at + (lax.rem(lax.div(mine, nx), 2) ^ part) * size
-        copies.append(pltpu.make_async_copy(
-            orbit_pieces[n], orbit.at[pl.ds(at, size)], sems.at[groups + n]))
-    for copy in copies:
-        copy.start()
+        orbit[pl.ds(at, size)] = orbit_pieces[n][...]
     acc[...] = jnp.zeros_like(acc)
-    dense[...] = jnp.zeros_like(dense)
     spread_tropo[...] = jnp.zeros_like(spread_tropo)
-    for copy in copies[:groups]:
-        copy.wait()
-    for s in range(stations):
-        rows_int[s : s + 1, :] = planes[
-            s, 4 * tracked + 1 : 4 * tracked + 2, :128].astype(jnp.int32)
-    to_scalar = pltpu.make_async_copy(rows_int, track, track_sem)
-    to_scalar.start()
-    to_scalar.wait()
-    for copy in copies[groups:]:
-        copy.wait()
-
-    def build(s, carry):
+
+    def build(s, turn):
+        stream = streams[turn]
         for pair in range(0, tracked, 2):
             values, mixed = [], []
             for m in (pair, pair + 1):
                 k = track[s, m]
-                local = k - first
-                inside = jnp.logical_and(local >= 0, local < own)
 
                 def row(plane):
                     return planes[s, pl.ds(plane * tracked + m, 1), :]
 
                 value = row(0) * orbit[k, 0] + row(1) * orbit[k, 1] + row(2) * orbit[k, 2]
-                dense[s, jnp.where(inside, local, own)] = value
                 values.append(value)
                 mixed.append(value * row(3))
-            rows = slice(pair * 8, pair * 8 + 16)
             high, low = split(jnp.concatenate(values, 0))
-            stream[s, pair * 8 : pair * 8 + 16, :] = high
-            stream[s, span + pair * 8 : span + pair * 8 + 16, :] = low
+            stream[pair * 8 : pair * 8 + 16, :] = high
+            stream[span + pair * 8 : span + pair * 8 + 16, :] = low
             high, low = split(jnp.concatenate(mixed, 0))
-            stream[s, 2 * span + pair * 8 : 2 * span + pair * 8 + 16, :] = high
-            stream[s, 3 * span + pair * 8 : 3 * span + pair * 8 + 16, :] = low
-        return carry
-
-    lax.fori_loop(0, stations, build, 0)
+            stream[2 * span + pair * 8 : 2 * span + pair * 8 + 16, :] = high
+            stream[3 * span + pair * 8 : 3 * span + pair * 8 + 16, :] = low
 
     lane = lax.broadcasted_iota(jnp.int32, (span, 128), 1) - (128 - spare)
-    index = lax.broadcasted_iota(jnp.int32, (spare, epochs), 0)
-
-    def multiply(s, carry):
-        turn = lax.rem(s, packed)
-        knot = planes[s, 4 * tracked : 4 * tracked + 1, :].astype(jnp.int32)
-        select = (index - turn * KNOTS == knot).astype(jnp.float32)
-        rows = jnp.concatenate(
-            [dense[s].reshape((own + 1) * 8, epochs)[: own * 8], select], 0)
-        high, low = split(rows)
-        large = dot_nt(stream[s], high)
-        result = large[:span] + large[span : 2 * span] + dot_nt(stream[s, :span, :], low)
-        product[s] = result.reshape(tracked, 8, width)
-        mixed = large[2 * span : 3 * span, width - 128 :] + large[3 * span :, width - 128 :]
-        kept = jnp.logical_and(lane >= turn * KNOTS, lane < turn * KNOTS + KNOTS)
-        tropo[s] = jnp.where(kept, mixed, 0.0).reshape(tracked, 8, 128)
-        return carry
-
-    lax.fori_loop(0, stations, multiply, 0)
-
-    def scatter(s, carry):
+
+    def multiply(s, turn):
+        stream = streams[turn]
+        place = lax.rem(s, packed) * KNOTS
+        high, low = highs[s], lows[s]
+        result = dot_nt(stream[:span, :], high) + dot_nt(stream[span : 2 * span, :], high)
+        result = result + dot_nt(stream[:span, :], low)
+        products[turn][...] = result.reshape(tracked, 8, width)
+        mixed = dot_nt(stream[2 * span : 3 * span, :], high)
+        mixed = (mixed + dot_nt(stream[3 * span :, :], high))[:, width - 128 :]
+        kept = jnp.logical_and(lane >= place, lane < place + KNOTS)
+        tropos[turn][...] = jnp.where(kept, mixed, 0.0).reshape(tracked, 8, 128)
+
+    def scatter(s, turn):
         slab = lax.div(s, packed)
         for m in range(tracked):
             k = track[s, m]
-            acc[k] = acc[k] - product[s, m]
-            spread_tropo[slab, k] = spread_tropo[slab, k] + tropo[s, m]
+            acc[k] = acc[k] - products[turn][m]
+            spread_tropo[slab, k] = spread_tropo[slab, k] + tropos[turn][m]
+
+    build(0, 0)
+    build(1, 1)
+    multiply(0, 0)
+
+    def visit(i, carry):
+        s = 2 * i
+        scatter(s - 2, 0)
+        build(s, 0)
+        multiply(s - 1, 1)
+        scatter(s - 1, 1)
+        build(s + 1, 1)
+        multiply(s, 0)
         return carry
 
-    lax.fori_loop(0, stations, scatter, 0)
+    lax.fori_loop(1, stations // 2, visit, 0)
+    scatter(stations - 2, 0)
+    multiply(stations - 1, 1)
+    scatter(stations - 1, 1)
 
     slabs = spread_tropo.shape[0]
     left, right = [], []
     for slab in range(slabs):
         high, low = split(spread_tropo[slab].reshape(sats * 8, 128))
-        own_high, own_low = split(
-            spread_tropo[slab, pl.ds(first, own + 0)].reshape(own * 8, 128))
+        own_high, own_low = split(spread_tropo[slab, pl.ds(first, own)].reshape(own * 8, 128))
         left += [high, high, low]
         right += [own_high, own_low, own_high]
     outer = dot_nt(jnp.concatenate(left, 1), jnp.concatenate(right, 1))
@@ -224,37 +316,33 @@
             outs[dx][dz * window : (dz + 1) * window] = acc[pl.ds(start, window)]
 
 
-def accumulate(planes, orbits, places, tracked, sats, nx, nz, window, width):
-    groups = len(planes)
-    per, rows, epochs = planes[0].shape
-    own = sats // groups
-    stations = groups * per
+def accumulate(groups, planes, track, highs, lows, orbits, places, nx, nz, window):
+    stations, rows, epochs = planes.shape
+    own = orbits[0].shape[0]
+    sats = own * groups
+    tracked = (rows - 8) // 4
+    width = highs.shape[1]
     slabs = -(-stations // ((width - own * 8) // KNOTS))
     out = jax.ShapeDtypeStruct((nz * window, 8, width), jnp.float32)
     return pl.pallas_call(
-        functools.partial(main_kernel, groups, per, own, nx, nz, window, places),
+        functools.partial(
+            main_kernel, groups, stations // groups, own, nx, nz, window, places),
         out_shape=[out] * nx + [jax.ShapeDtypeStruct((own, 8, width), jnp.float32)],
-        in_specs=[anywhere()] * (groups + len(orbits)),
+        in_specs=[vmem(), pl.BlockSpec(memory_space=pltpu.SMEM)] + [vmem()] * (2 + len(orbits)),
         out_specs=[vmem()] * (nx + 1),
         scratch_shapes=[
-            pltpu.SMEM((stations, 128), jnp.int32),
-            pltpu.VMEM((stations, 128), jnp.int32),
-            pltpu.VMEM((stations, rows, epochs), jnp.float32),
             pltpu.VMEM((sats,) + orbits[0].shape[1:], jnp.float32),
             pltpu.VMEM((sats, 8, width), jnp.float32),
-            pltpu.VMEM((stations, 4 * tracked * 8, epochs), jnp.bfloat16),
-            pltpu.VMEM((stations, own + 1, 8, epochs), jnp.float32),
-            pltpu.VMEM((stations, tracked, 8, width), jnp.float32),
-            pltpu.VMEM((stations, tracked, 8, 128), jnp.float32),
+            *[pltpu.VMEM((4 * tracked * 8, epochs), jnp.bfloat16)] * 2,
+            *[pltpu.VMEM((tracked, 8, width), jnp.float32)] * 2,
+            *[pltpu.VMEM((tracked, 8, 128), jnp.float32)] * 2,
             pltpu.VMEM((slabs, sats, 8, 128), jnp.float32),
-            pltpu.SemaphoreType.DMA((groups + len(orbits),)),
-            pltpu.SemaphoreType.DMA,
         ],
-        compiler_params=pltpu.CompilerParams(vmem_limit_bytes=LARGE_LIMIT),
+        compiler_params=pltpu.CompilerParams(vmem_limit_bytes=MEDIUM_LIMIT),
         cost_estimate=pl.CostEstimate(
             flops=8 * 10**9, bytes_accessed=8 * 10**6, transcendentals=0),
         name="accumulate",
-    )(*planes, *orbits)
+    )(planes, track, highs, lows, *orbits)
 
 
 def blocks_kernel(groups, per, own, *refs):
@@ -438,16 +526,15 @@
     )
 
     parts = 2 if own % 2 == 0 and nz > 1 else 1
-    planes, extra, half = prepare(
-        sight, mapping, residual, counts, track, knots, orbit, parts,
-        lambda mine: lax.rem(lax.div(mine, nx), 2),
-    )
-    orbit_pieces, places = gather_orbit(
-        orbit, half if parts > 1 else None, group, columns_axis, nx)
+    half = cut_half(orbit, lambda mine: lax.rem(lax.div(mine, nx), 2)) if parts > 1 else None
+    planes, extra = prepare(sight, mapping, residual, counts, track, knots)
+    orbit_pieces, places = gather_orbit(orbit, half, group, columns_axis, nx)
     plane_pieces = gather_pieces(planes, group)
+    extra, _ = lax.optimization_barrier((extra, plane_pieces[group - 2]))
     extra_pieces = gather_pieces(extra, group)
+    all_planes, all_track, highs, lows = own_rows_of(plane_pieces, orbit, width)
     *sums, own_rows = accumulate(
-        plane_pieces, orbit_pieces, places, tracked, sats, nx, nz, window, width)
+        group, all_planes, all_track, highs, lows, orbit_pieces, places, nx, nz, window)
     small = own_sums(plane_pieces, extra_pieces, own_rows, orbit)
     arrived = [sums[0]] + [shift(sums[d], "sta", columns_axis, d) for d in range(1, nx)]
     smalls = [small] + [shift(small, "sta", columns_axis, d) for d in range(1, nx)]

time: 72.4 us -> 66.4 us (0.917)
  local copies, waits for them, and re-layouts: 5.92 us -> 0.96 us
  waiting for transfers between devices: 36.9 us -> 33.6 us
  Pallas kernels: 13.7 us -> 16.2 us
    unnamed x16 -> x6, local copies, waits for them, and re-layouts: 5.92 us -> 0.96 us
    ppermute x16, waiting for transfers between devices: 36.9 us -> 33.6 us  [shift(): return lax.ppermute(value, axis, [(i, i ^ step) for i in range(size)])]
    pallas_call x2 -> x4, Pallas kernels: 9.03 us -> 11.5 us  [the longest x1 4.92 us: accumulate(): pl.pallas_call(functools.partial(main_kernel, groups, stations // groups,...]
  transfers between devices with their start and end apart: 16 -> 16, of which waited for: 8 -> 6; matrix products, arithmetic and copies ran while one was open for 0% -> 0% of each run, Pallas kernels for 17% -> 20%
where the time goes in v4:
time: 66.4 us; the launch traced here: 66.2 us
  waiting for transfers between devices  33.6 us (51%)
  Pallas kernels  16.2 us (24%)
  starting transfers between devices  14.7 us (22%)
  local copies, waits for them, and re-layouts  0.96 us (1%)
  between operations  0.73 us (1%)
    ppermute x16, waiting for transfers between devices, shift(): return lax.ppermute(value, axis, [(i, i ^ step) for i in range(size)])  33.6 us
    ppermute x16, starting transfers between devices, shift(): return lax.ppermute(value, axis, [(i, i ^ step) for i in range(size)])  14.7 us
    pallas_call x1, Pallas kernels, accumulate(): pl.pallas_call(functools.partial(main_kernel, groups, stations // groups,...  4.92 us
    pallas_call x1, Pallas kernels, own_sums(): pl.pallas_call(functools.partial(blocks_kernel, groups, per, own), out_sh...  3.42 us
    pallas_call x1, Pallas kernels, own_rows_of(): pl.pallas_call(functools.partial(own_rows_kernel, groups, per, own, width...  2.76 us
    pallas_call x1, Pallas kernels, prepare(): pl.pallas_call(prepare_kernel, out_shape=[jax.ShapeDtypeStruct((stations,...  1.96 us
    pallas_call x1, Pallas kernels, cut_half(): pl.pallas_call(functools.partial(cut_kernel, turn_of), out_shape=jax.Shap...  1.81 us
  transfers between devices with their start and end apart: 16, of which 6 were waited for; matrix products, arithmetic and copies ran while one was open for 0% of the time, Pallas kernels for 20%

profile of v4, /device:TPU:0, one launch (start us, length us, event | category | flops | bytes accessed | tf_op | source)
XLA Modules:
  0.0 66.2 jit_solution(4778247753727615795)
XLA Ops:
  0.6 0.0 copy-start
  0.6 1.8 %cut_half.1 = f32[15,3,8,256]{3,2,1,0:T(8,128)} custom-call(f32[30,3,8,256]{3,2,1,0:T(8,128)} %refs_9_.1), custom_call_target="tpu_custom_call" | custom-call | tf_op jit(solution)/shard_map/cut_half/pallas_call | solution.py:36
  2.5 3.0 %collective-permute-start.3 = (f32[15,3,8,256]{3,2,1,0:T(8,128)}, f32[15,3,8,256]{3,2,1,0:T(8,128)S(1)}, u32[]{:S(2)}, u32[]{:S(2)}) collective-permute-start(f32[15,3,8,256]{3,2,1,0:T(8,128)} %cut_half.1), channel_id=1, source_target_pairs={{0,2},{1,3},{2,0},{3,1},{4,6},{5,7},{6,4},{7,5},{8,10},{9,11},{10,... | collective-permute-start | bytes 1105928 | tf_op jit(solution)/shard_map/ppermute | solution.py:484
  5.5 2.0 %prepare.1 = (f32[2,136,256]{2,1,0:T(8,128)}, f32[2,64,256]{2,1,0:T(8,128)}) custom-call(f32[2,3,32,256]{3,2,1,0:T(8,128)} %refs_0_.1, f32[2,32,256]{2,1,0:T(8,128)} %refs_1_.1, f32[2,32,256]{2,1,0:T(8,128)} %refs_2_.1, s32[2,32,256]{2,1,0:T(8,128)} %refs_3_.1, s32[2,32]{1,0:T(2,128)} %refs_4_.3, s32[2,256]{1,0:T(2,128)} %refs_5_.1), custom_call_target="tpu_custom_call" | custom-call | tf_op jit(solution)/shard_map/prepare/pallas_call | solution.py:96
  7.5 0.1 collective-permute-start.1
  7.5 7.6 %collective-permute-done.3.refs_5_ = f32[15,3,8,256]{3,2,1,0:T(8,128)S(1)} collective-permute-done((f32[15,3,8,256]{3,2,1,0:T(8,128)}, f32[15,3,8,256]{3,2,1,0:T(8,128)S(1)}, u32[]{:S(2)}, u32[]{:S(2)}) %collective-permute-start.3) | collective-permute-done | bytes 368672 | tf_op jit(solution)/shard_map/ppermute | solution.py:484
  15.1 2.1 %collective-permute-start.4 = (f32[15,3,8,256]{3,2,1,0:T(8,128)S(1)}, f32[15,3,8,256]{3,2,1,0:T(8,128)S(1)}, u32[]{:S(2)}, u32[]{:S(2)}) collective-permute-start(f32[15,3,8,256]{3,2,1,0:T(8,128)S(1)} %collective-permute-done.3.refs_5_), channel_id=1, source_target_pairs={{0,8},{4,12},{8,0},{12,4},{16,24},{20,28},{24,16},{28,20},{1,9},{5... | collective-permute-start | bytes 1105928 | tf_op jit(solution)/shard_map/ppermute | solution.py:484
  17.2 0.0 collective-permute-start
  17.2 3.0 %collective-permute-done.1.refs_2_ = f32[2,136,256]{2,1,0:T(8,128)S(1)} collective-permute-done((f32[2,136,256]{2,1,0:T(8,128)}, f32[2,136,256]{2,1,0:T(8,128)S(1)}, u32[]{:S(2)}, u32[]{:S(2)}) %collective-permute-start.1) | collective-permute-done | bytes 278560 | tf_op jit(solution)/shard_map/ppermute | solution.py:484
  20.3 0.0 collective-permute-start.2
  20.3 1.7 %collective-permute-start.10 = (f32[2,64,256]{2,1,0:T(8,128)}, f32[2,64,256]{2,1,0:T(8,128)S(1)}, u32[]{:S(2)}, u32[]{:S(2)}) collective-permute-start(f32[2,64,256]{2,1,0:T(8,128)} %get-tuple-element.28.refs_4_), channel_id=1, source_target_pairs={{0,2},{1,3},{2,0},{3,1},{4,6},{5,7},{6,4},{7,5},{8,10},{9,11},{10,... | collective-permute-start | bytes 393224 | tf_op jit(solution)/shard_map/ppermute | solution.py:484
  22.0 0.0 copy-done
  22.0 0.2 collective-permute-start.5
  22.2 0.0 collective-permute-done.refs_1_
  22.2 0.3 collective-permute-start.9
  22.5 3.9 %collective-permute-done.10.refs_6_ = f32[2,64,256]{2,1,0:T(8,128)S(1)} collective-permute-done((f32[2,64,256]{2,1,0:T(8,128)}, f32[2,64,256]{2,1,0:T(8,128)S(1)}, u32[]{:S(2)}, u32[]{:S(2)}) %collective-permute-start.10) | collective-permute-done | bytes 131104 | tf_op jit(solution)/shard_map/ppermute | solution.py:484
  26.4 0.0 collective-permute-start.6
  26.4 0.0 collective-permute-done.2.refs_3_
  26.4 0.5 collective-permute-start.11
  26.9 0.0 collective-permute-done.4.refs_6_
  26.9 0.1 collective-permute-start.7
  27.0 0.0 copy-start.1
  27.0 1.0 %copy-done.1 = f32[2,136,256]{2,1,0:T(8,128)S(1)} copy-done((f32[2,136,256]{2,1,0:T(8,128)S(1)}, f32[2,136,256]{2,1,0:T(8,128)}, u32[]{:S(2)}) %copy-start.1) | copy-done | bytes 278552
  27.9 2.8 %own_rows.1 = (f32[8,136,256]{2,1,0:T(8,128)S(1)}, s32[8,128]{1,0:T(8,128)S(1)}, bf16[8,256,256]{2,1,0:T(8,128)(2,1)S(1)}, bf16[8,256,256]{2,1,0:T(8,128)(2,1)S(1)}) custom-call(f32[2,136,256]{2,1,0:T(8,128)S(1)} %copy-done.1, f32[2,136,256]{2,1,0:T(8,128)S(1)} %collective-permute-done.refs_1_, f32[2,136,256]{2,1,0:T(8,128)S(1)} %collective-permute-done.1.refs_2_, ...), custom_call_target="tpu_custom_call" | custom-call | flops 8000000000 | bytes 8000000 | tf_op jit(solution)/shard_map/own_rows/pallas_call | solution.py:188
  30.7 0.0 collective-permute-done.6.refs_8_
  30.7 0.0 collective-permute-done.5.refs_7_
  30.7 0.0 collective-permute-done.7.refs_9_
  30.7 0.0 copy-start.2
  30.7 4.9 %accumulate.1 = (f32[60,8,256]{2,1,0:T(8,128)S(1)}, f32[60,8,256]{2,1,0:T(8,128)S(1)}, f32[30,8,256]{2,1,0:T(8,128)S(1)}) custom-call(f32[8,136,256]{2,1,0:T(8,128)S(1)} %get-tuple-element.21.refs_0_, s32[8,128]{1,0:T(8,128)S(1)} %get-tuple-element.22.refs_1_, bf16[8,256,256]{2,1,0:T(8,128)(2,1)S(1)} %get-tuple-element.23.refs_2_, ...), custom_call_target="tpu_custom_call" | custom-call | flops 8000000000 | bytes 8000000 | tf_op jit(solution)/shard_map/accumulate/pallas_call | solution.py:327
  35.7 1.7 %collective-permute-start.8 = (f32[60,8,256]{2,1,0:T(8,128)S(1)}, f32[60,8,256]{2,1,0:T(8,128)S(1)}, u32[]{:S(2)}, u32[]{:S(2)}) collective-permute-start(f32[60,8,256]{2,1,0:T(8,128)S(1)} %get-tuple-element.26), channel_id=1, source_target_pairs={{0,4},{4,0},{8,12},{12,8},{16,20},{20,16},{24,28},{28,24},{1,5},{5... | collective-permute-start | bytes 1474568 | tf_op jit(solution)/shard_map/ppermute | solution.py:484
  37.4 0.0 collective-permute-done.9.refs_5_
  37.4 0.0 collective-permute-done.11.refs_7_
  37.4 0.0 copy-done.2
  37.4 3.4 %own_sums.1.refs_2_ = f32[2,8,256]{2,1,0:T(8,128)S(1)} custom-call(f32[2,136,256]{2,1,0:T(8,128)S(1)} %copy-done.1, f32[2,136,256]{2,1,0:T(8,128)S(1)} %collective-permute-done.refs_1_, f32[2,136,256]{2,1,0:T(8,128)S(1)} %collective-permute-done.1.refs_2_, f32[2,136,256]{2,1,0:T(8,128)S(1)} %collective-permute-done.2.refs_3_, f32[2,64,256]{2,1,0:T(8,128)S(1)} %copy-done.2, ...), custom_call_target="tpu_custom_call" | custom-call | flops 4000000000 | bytes 4000000 | tf_op jit(solution)/shard_map/own_sums/pallas_call | solution.py:401
  40.9 0.4 collective-permute-start.12
  41.3 8.4 %collective-permute-done.12.refs_3_ = f32[2,8,256]{2,1,0:T(8,128)S(1)} collective-permute-done((f32[2,8,256]{2,1,0:T(8,128)S(1)}, f32[2,8,256]{2,1,0:T(8,128)S(1)}, u32[]{:S(2)}, u32[]{:S(2)}) %collective-permute-start.12) | collective-permute-done | bytes 16416 | tf_op jit(solution)/shard_map/ppermute | solution.py:484
  49.7 0.0 collective-permute-done.8.refs_1_
  49.7 0.1 combine.1
  49.7 1.8 %collective-permute-start.13 = (f32[17,8,256]{2,1,0:T(8,128)S(1)}, f32[17,8,256]{2,1,0:T(8,128)S(1)}, u32[]{:S(2)}, u32[]{:S(2)}) collective-permute-start(f32[17,8,256]{2,1,0:T(8,128)S(1)} %get-tuple-element.31), channel_id=1, source_target_pairs={{0,8},{4,12},{8,0},{12,4},{16,24},{20,28},{24,16},{28,20},{1,9},{5... | collective-permute-start | bytes 417800 | tf_op jit(solution)/shard_map/ppermute | solution.py:484
  51.6 2.6 %collective-permute-start.14 = (f32[17,8,256]{2,1,0:T(8,128)S(1)}, f32[17,8,256]{2,1,0:T(8,128)S(1)}, u32[]{:S(2)}, u32[]{:S(2)}) collective-permute-start(f32[17,8,256]{2,1,0:T(8,128)S(1)} %get-tuple-element.32), channel_id=1, source_target_pairs={{0,16},{4,20},{8,24},{12,28},{16,0},{20,4},{24,8},{28,12},{1,17},{... | collective-permute-start | bytes 417800 | tf_op jit(solution)/shard_map/ppermute | solution.py:484
  54.2 0.0 collective-permute-start.15
  54.2 2.5 %collective-permute-done.13.refs_1_ = f32[17,8,256]{2,1,0:T(8,128)S(1)} collective-permute-done((f32[17,8,256]{2,1,0:T(8,128)S(1)}, f32[17,8,256]{2,1,0:T(8,128)S(1)}, u32[]{:S(2)}, u32[]{:S(2)}) %collective-permute-start.13) | collective-permute-done | bytes 139296 | tf_op jit(solution)/shard_map/ppermute | solution.py:484
  56.7 8.2 %collective-permute-done.14.refs_2_ = f32[17,8,256]{2,1,0:T(8,128)S(1)} collective-permute-done((f32[17,8,256]{2,1,0:T(8,128)S(1)}, f32[17,8,256]{2,1,0:T(8,128)S(1)}, u32[]{:S(2)}, u32[]{:S(2)}) %collective-permute-start.14) | collective-permute-done | bytes 139296 | tf_op jit(solution)/shard_map/ppermute | solution.py:484
  64.9 0.0 collective-permute-done.15.refs_3_
  64.9 1.3 %finish.1 = (f32[240,120]{1,0:T(8,128)}, f32[1,240]{1,0:T(1,128)}, f32[8,8,30]{2,1,0:T(8,128)}) custom-call(f32[17,8,256]{2,1,0:T(8,128)S(1)} %get-tuple-element.30.refs_0_, f32[17,8,256]{2,1,0:T(8,128)S(1)} %collective-permute-done.13.refs_1_, f32[17,8,256]{2,1,0:T(8,128)S(1)} %collective-permute-done.14.refs_2_, ...), custom_call_target="tpu_custom_call" | custom-call | tf_op jit(solution)/shard_map/finish/pallas_call | solution.py:469
Async XLA Ops:
  0.6 21.4 %copy-start = (f32[30,3,8,256]{3,2,1,0:T(8,128)S(1)}, f32[30,3,8,256]{3,2,1,0:T(8,128)}, u32[]{:S(2)}) copy-start(f32[30,3,8,256]{3,2,1,0:T(8,128)} %refs_9_.1) | copy-start | bytes 2211844
  2.5 12.7 %collective-permute-start.3 = (f32[15,3,8,256]{3,2,1,0:T(8,128)}, f32[15,3,8,256]{3,2,1,0:T(8,128)S(1)}, u32[]{:S(2)}, u32[]{:S(2)}) collective-permute-start(f32[15,3,8,256]{3,2,1,0:T(8,128)} %cut_half.1), channel_id=1, source_target_pairs={{0,2},{1,3},{2,0},{3,1},{4,6},{5,7},{6,4},{7,5},{8,10},{9,11},{10,... | collective-permute-start | bytes 1105928 | tf_op jit(solution)/shard_map/ppermute | solution.py:484
  7.5 12.8 %collective-permute-start.1 = (f32[2,136,256]{2,1,0:T(8,128)}, f32[2,136,256]{2,1,0:T(8,128)S(1)}, u32[]{:S(2)}, u32[]{:S(2)}) collective-permute-start(f32[2,136,256]{2,1,0:T(8,128)} %get-tuple-element.20.refs_0_), channel_id=1, source_target_pairs={{0,2},{1,3},{2,0},{3,1},{4,6},{5,7},{6,4},{7,5},{8,10},{9,11},{10,... | collective-permute-start | bytes 835592 | tf_op jit(solution)/shard_map/ppermute | solution.py:484
  15.1 11.8 %collective-permute-start.4 = (f32[15,3,8,256]{3,2,1,0:T(8,128)S(1)}, f32[15,3,8,256]{3,2,1,0:T(8,128)S(1)}, u32[]{:S(2)}, u32[]{:S(2)}) collective-permute-start(f32[15,3,8,256]{3,2,1,0:T(8,128)S(1)} %collective-permute-done.3.refs_5_), channel_id=1, source_target_pairs={{0,8},{4,12},{8,0},{12,4},{16,24},{20,28},{24,16},{28,20},{1,9},{5... | collective-permute-start | bytes 1105928 | tf_op jit(solution)/shard_map/ppermute | solution.py:484
  17.2 5.0 %collective-permute-start = (f32[2,136,256]{2,1,0:T(8,128)}, f32[2,136,256]{2,1,0:T(8,128)S(1)}, u32[]{:S(2)}, u32[]{:S(2)}) collective-permute-start(f32[2,136,256]{2,1,0:T(8,128)} %get-tuple-element.20.refs_0_), channel_id=1, source_target_pairs={{0,1},{1,0},{2,3},{3,2},{4,5},{5,4},{6,7},{7,6},{8,9},{9,8},{10,11... | collective-permute-start | bytes 835592 | tf_op jit(solution)/shard_map/ppermute | solution.py:484
  20.3 6.1 %collective-permute-start.2 = (f32[2,136,256]{2,1,0:T(8,128)S(1)}, f32[2,136,256]{2,1,0:T(8,128)S(1)}, u32[]{:S(2)}, u32[]{:S(2)}) collective-permute-start(f32[2,136,256]{2,1,0:T(8,128)S(1)} %collective-permute-done.1.refs_2_), channel_id=1, source_target_pairs={{0,1},{1,0},{2,3},{3,2},{4,5},{5,4},{6,7},{7,6},{8,9},{9,8},{10,11... | collective-permute-start | bytes 835592 | tf_op jit(solution)/shard_map/ppermute | solution.py:484
  20.3 6.1 %collective-permute-start.10 = (f32[2,64,256]{2,1,0:T(8,128)}, f32[2,64,256]{2,1,0:T(8,128)S(1)}, u32[]{:S(2)}, u32[]{:S(2)}) collective-permute-start(f32[2,64,256]{2,1,0:T(8,128)} %get-tuple-element.28.refs_4_), channel_id=1, source_target_pairs={{0,2},{1,3},{2,0},{3,1},{4,6},{5,7},{6,4},{7,5},{8,10},{9,11},{10,... | collective-permute-start | bytes 393224 | tf_op jit(solution)/shard_map/ppermute | solution.py:484
  22.0 8.7 %collective-permute-start.5 = (f32[30,3,8,256]{3,2,1,0:T(8,128)S(1)}, f32[30,3,8,256]{3,2,1,0:T(8,128)S(1)}, u32[]{:S(2)}, u32[]{:S(2)}) collective-permute-start(f32[30,3,8,256]{3,2,1,0:T(8,128)S(1)} %copy-done), channel_id=1, source_target_pairs={{0,1},{1,0},{2,3},{3,2},{4,5},{5,4},{6,7},{7,6},{8,9},{9,8},{10,11... | collective-permute-start | bytes 2211848 | tf_op jit(solution)/shard_map/ppermute | solution.py:484
  22.2 15.2 %collective-permute-start.9 = (f32[2,64,256]{2,1,0:T(8,128)}, f32[2,64,256]{2,1,0:T(8,128)S(1)}, u32[]{:S(2)}, u32[]{:S(2)}) collective-permute-start(f32[2,64,256]{2,1,0:T(8,128)} %get-tuple-element.28.refs_4_), channel_id=1, source_target_pairs={{0,1},{1,0},{2,3},{3,2},{4,5},{5,4},{6,7},{7,6},{8,9},{9,8},{10,11... | collective-permute-start | bytes 393224 | tf_op jit(solution)/shard_map/ppermute | solution.py:484
  26.4 4.3 %collective-permute-start.6 = (f32[15,3,8,256]{3,2,1,0:T(8,128)S(1)}, f32[15,3,8,256]{3,2,1,0:T(8,128)S(1)}, u32[]{:S(2)}, u32[]{:S(2)}) collective-permute-start(f32[15,3,8,256]{3,2,1,0:T(8,128)S(1)} %collective-permute-done.3.refs_5_), channel_id=1, source_target_pairs={{0,1},{1,0},{2,3},{3,2},{4,5},{5,4},{6,7},{7,6},{8,9},{9,8},{10,11... | collective-permute-start | bytes 1105928 | tf_op jit(solution)/shard_map/ppermute | solution.py:484
  26.4 11.0 %collective-permute-start.11 = (f32[2,64,256]{2,1,0:T(8,128)S(1)}, f32[2,64,256]{2,1,0:T(8,128)S(1)}, u32[]{:S(2)}, u32[]{:S(2)}) collective-permute-start(f32[2,64,256]{2,1,0:T(8,128)S(1)} %collective-permute-done.10.refs_6_), channel_id=1, source_target_pairs={{0,1},{1,0},{2,3},{3,2},{4,5},{5,4},{6,7},{7,6},{8,9},{9,8},{10,11... | collective-permute-start | bytes 393224 | tf_op jit(solution)/shard_map/ppermute | solution.py:484
  26.9 3.8 %collective-permute-start.7 = (f32[15,3,8,256]{3,2,1,0:T(8,128)S(1)}, f32[15,3,8,256]{3,2,1,0:T(8,128)S(1)}, u32[]{:S(2)}, u32[]{:S(2)}) collective-permute-start(f32[15,3,8,256]{3,2,1,0:T(8,128)S(1)} %collective-permute-done.4.refs_6_), channel_id=1, source_target_pairs={{0,1},{1,0},{2,3},{3,2},{4,5},{5,4},{6,7},{7,6},{8,9},{9,8},{10,11... | collective-permute-start | bytes 1105928 | tf_op jit(solution)/shard_map/ppermute | solution.py:484
  27.0 1.0 %copy-start.1 = (f32[2,136,256]{2,1,0:T(8,128)S(1)}, f32[2,136,256]{2,1,0:T(8,128)}, u32[]{:S(2)}) copy-start(f32[2,136,256]{2,1,0:T(8,128)} %get-tuple-element.20.refs_0_) | copy-start | bytes 835588
  30.7 6.7 %copy-start.2 = (f32[2,64,256]{2,1,0:T(8,128)S(1)}, f32[2,64,256]{2,1,0:T(8,128)}, u32[]{:S(2)}) copy-start(f32[2,64,256]{2,1,0:T(8,128)} %get-tuple-element.28.refs_4_) | copy-start | bytes 393220
  35.7 14.0 %collective-permute-start.8 = (f32[60,8,256]{2,1,0:T(8,128)S(1)}, f32[60,8,256]{2,1,0:T(8,128)S(1)}, u32[]{:S(2)}, u32[]{:S(2)}) collective-permute-start(f32[60,8,256]{2,1,0:T(8,128)S(1)} %get-tuple-element.26), channel_id=1, source_target_pairs={{0,4},{4,0},{8,12},{12,8},{16,20},{20,16},{24,28},{28,24},{1,5},{5... | collective-permute-start | bytes 1474568 | tf_op jit(solution)/shard_map/ppermute | solution.py:484
  40.9 8.8 %collective-permute-start.12 = (f32[2,8,256]{2,1,0:T(8,128)S(1)}, f32[2,8,256]{2,1,0:T(8,128)S(1)}, u32[]{:S(2)}, u32[]{:S(2)}) collective-permute-start(f32[2,8,256]{2,1,0:T(8,128)S(1)} %own_sums.1.refs_2_), channel_id=1, source_target_pairs={{0,4},{4,0},{8,12},{12,8},{16,20},{20,16},{24,28},{28,24},{1,5},{5... | collective-permute-start | bytes 49160 | tf_op jit(solution)/shard_map/ppermute | solution.py:484
  49.7 7.0 %collective-permute-start.13 = (f32[17,8,256]{2,1,0:T(8,128)S(1)}, f32[17,8,256]{2,1,0:T(8,128)S(1)}, u32[]{:S(2)}, u32[]{:S(2)}) collective-permute-start(f32[17,8,256]{2,1,0:T(8,128)S(1)} %get-tuple-element.31), channel_id=1, source_target_pairs={{0,8},{4,12},{8,0},{12,4},{16,24},{20,28},{24,16},{28,20},{1,9},{5... | collective-permute-start | bytes 417800 | tf_op jit(solution)/shard_map/ppermute | solution.py:484
  51.6 13.4 %collective-permute-start.14 = (f32[17,8,256]{2,1,0:T(8,128)S(1)}, f32[17,8,256]{2,1,0:T(8,128)S(1)}, u32[]{:S(2)}, u32[]{:S(2)}) collective-permute-start(f32[17,8,256]{2,1,0:T(8,128)S(1)} %get-tuple-element.32), channel_id=1, source_target_pairs={{0,16},{4,20},{8,24},{12,28},{16,0},{20,4},{24,8},{28,12},{1,17},{... | collective-permute-start | bytes 417800 | tf_op jit(solution)/shard_map/ppermute | solution.py:484
  54.2 10.8 %collective-permute-start.15 = (f32[17,8,256]{2,1,0:T(8,128)S(1)}, f32[17,8,256]{2,1,0:T(8,128)S(1)}, u32[]{:S(2)}, u32[]{:S(2)}) collective-permute-start(f32[17,8,256]{2,1,0:T(8,128)S(1)} %get-tuple-element.33), channel_id=1, source_target_pairs={{0,24},{4,28},{8,16},{12,20},{16,8},{20,12},{24,0},{28,4},{1,25},{... | collective-permute-start | bytes 417800 | tf_op jit(solution)/shard_map/ppermute | solution.py:484

commit v5 on v4

--- a/solution.py
+++ b/solution.py
@@ -22,26 +22,6 @@
 
 def hbm():
     return pl.BlockSpec(memory_space=pltpu.HBM)
-
-
-def cut_kernel(turn_of, orbit, mine, sem):
-    half = mine.shape[0]
-    at = turn_of(lax.axis_index("sta")) * half
-    cut = pltpu.make_async_copy(orbit.at[pl.ds(at, half)], mine, sem)
-    cut.start()
-    cut.wait()
-
-
-def cut_half(orbit, turn_of):
-    return pl.pallas_call(
-        functools.partial(cut_kernel, turn_of),
-        out_shape=jax.ShapeDtypeStruct((orbit.shape[0] // 2,) + orbit.shape[1:], jnp.float32),
-        in_specs=[hbm()],
-        out_specs=vmem(),
-        scratch_shapes=[pltpu.SemaphoreType.DMA],
-        compiler_params=pltpu.CompilerParams(vmem_limit_bytes=HUGE_LIMIT),
-        name="cut_half",
-    )(orbit)
 
 
 def prepare_kernel(*refs):
@@ -207,14 +187,37 @@
     )(*planes, orbit)
 
 
-def main_kernel(groups, per, own, nx, nz, window, places, *refs):
-    planes, track, highs, lows = refs[:4]
-    refs = refs[4:]
-    orbit_pieces = refs[: len(places)]
-    outs = refs[len(places) : len(places) + nx]
-    own_out = refs[len(places) + nx]
-    (orbit, acc, stream_a, stream_b, product_a, product_b, tropo_a, tropo_b,
-     spread_tropo) = refs[len(places) + nx + 1 :]
+def place_kernel(own, nx, places, *refs):
+    orbit_pieces, orbit = refs[:-1], refs[-1]
+    me = lax.axis_index("sat")
+    mine = lax.axis_index("sta")
+    for n, (d, far, start, size) in enumerate(places):
+        at = (me ^ d) * own
+        if far >= 0:
+            at = at + (turn_of(mine, nx) ^ far) * (own // 2) + start
+        orbit[pl.ds(at, size)] = orbit_pieces[n][...]
+
+
+def place(orbits, places, sats, nx):
+    own = orbits[0].shape[0]
+    return pl.pallas_call(
+        functools.partial(place_kernel, own, nx, places),
+        out_shape=jax.ShapeDtypeStruct((sats,) + orbits[0].shape[1:], jnp.float32),
+        in_specs=[vmem()] * len(orbits),
+        out_specs=vmem(),
+        compiler_params=pltpu.CompilerParams(vmem_limit_bytes=SMALL_LIMIT),
+        cost_estimate=pl.CostEstimate(
+            flops=int(0.1 * 10**9), bytes_accessed=int(0.1 * 10**6), transcendentals=0),
+        name="place",
+    )(*orbits)
+
+
+def main_kernel(groups, per, own, nx, nz, window, *refs):
+    planes, track, highs, lows, orbit = refs[:5]
+    outs = refs[5 : 5 + nx]
+    own_out = refs[5 + nx]
+    (acc, stream_a, stream_b, product_a, product_b, tropo_a, tropo_b,
+     spread_tropo) = refs[6 + nx :]
     streams = (stream_a, stream_b)
     products, tropos = (product_a, product_b), (tropo_a, tropo_b)
     stations = groups * per
@@ -227,12 +230,6 @@
     mine = lax.axis_index("sta")
     first = me * own
 
-    for n, (d, part, parts) in enumerate(places):
-        size = own // parts
-        at = (me ^ d) * own
-        if parts > 1:
-            at = at + (lax.rem(lax.div(mine, nx), 2) ^ part) * size
-        orbit[pl.ds(at, size)] = orbit_pieces[n][...]
     acc[...] = jnp.zeros_like(acc)
     spread_tropo[...] = jnp.zeros_like(spread_tropo)
 
@@ -316,22 +313,21 @@
             outs[dx][dz * window : (dz + 1) * window] = acc[pl.ds(start, window)]
 
 
-def accumulate(groups, planes, track, highs, lows, orbits, places, nx, nz, window):
+def accumulate(groups, planes, track, highs, lows, orbit, nx, nz, window):
     stations, rows, epochs = planes.shape
-    own = orbits[0].shape[0]
-    sats = own * groups
+    sats = orbit.shape[0]
+    own = sats // groups
     tracked = (rows - 8) // 4
     width = highs.shape[1]
     slabs = -(-stations // ((width - own * 8) // KNOTS))
     out = jax.ShapeDtypeStruct((nz * window, 8, width), jnp.float32)
     return pl.pallas_call(
         functools.partial(
-            main_kernel, groups, stations // groups, own, nx, nz, window, places),
+            main_kernel, groups, stations // groups, own, nx, nz, window),
         out_shape=[out] * nx + [jax.ShapeDtypeStruct((own, 8, width), jnp.float32)],
-        in_specs=[vmem(), pl.BlockSpec(memory_space=pltpu.SMEM)] + [vmem()] * (2 + len(orbits)),
+        in_specs=[vmem(), pl.BlockSpec(memory_space=pltpu.SMEM)] + [vmem()] * 3,
         out_specs=[vmem()] * (nx + 1),
         scratch_shapes=[
-            pltpu.VMEM((sats,) + orbits[0].shape[1:], jnp.float32),
             pltpu.VMEM((sats, 8, width), jnp.float32),
             *[pltpu.VMEM((4 * tracked * 8, epochs), jnp.bfloat16)] * 2,
             *[pltpu.VMEM((tracked, 8, width), jnp.float32)] * 2,
@@ -342,7 +338,7 @@
         cost_estimate=pl.CostEstimate(
             flops=8 * 10**9, bytes_accessed=8 * 10**6, transcendentals=0),
         name="accumulate",
-    )(planes, track, highs, lows, *orbits)
+    )(planes, track, highs, lows, orbit)
 
 
 def blocks_kernel(groups, per, own, *refs):
@@ -494,18 +490,40 @@
     return pieces
 
 
-def gather_orbit(orbit, mine, size, columns_axis, nx):
-    if mine is None:
-        return gather_pieces(orbit, size), tuple((d, 0, 1) for d in range(size))
-    pieces, places = [orbit], [(0, 0, 1)]
+def turn_of(mine, nx):
+    return lax.rem(lax.div(mine, nx) + lax.rem(mine, nx), 2)
+
+
+def cut_parts(orbit, columns_axis, nx):
+    own = orbit.shape[0]
+    if own % 2 or nx % 2 or (columns_axis // nx) % 2:
+        return []
+    half = own // 2
+    lead = half - half // 2
+    at = turn_of(lax.axis_index("sta"), nx) * half
+    return [lax.dynamic_slice_in_dim(orbit, at, lead, 0),
+            lax.dynamic_slice_in_dim(orbit, at + lead, half - lead, 0)]
+
+
+def gather_orbit(orbit, parts, size, columns_axis, nx):
+    own = orbit.shape[0]
+    if not parts:
+        return gather_pieces(orbit, size), tuple((d, -1, 0, own) for d in range(size))
+    half = own // 2
+    lead = half - half // 2
+    first, second = parts
+    pieces, places = [orbit], [(0, -1, 0, own)]
     for d in range(2, size, 2):
-        near = shift(mine, "sat", size, d)
-        far = shift(near, "sta", columns_axis, nx)
-        pieces += [near, far]
-        places += [(d, 0, 2), (d, 1, 2)]
-    for piece, (d, part, parts) in list(zip(pieces, places)):
+        near_first = shift(first, "sat", size, d)
+        near_second = shift(second, "sat", size, d)
+        far_first = shift(near_first, "sta", columns_axis, nx)
+        far_second = shift(near_second, "sta", columns_axis, 1)
+        pieces += [near_first, near_second, far_first, far_second]
+        places += [(d, 0, 0, lead), (d, 0, lead, half - lead),
+                   (d, 1, 0, lead), (d, 1, lead, half - lead)]
+    for piece, (d, *rest) in list(zip(pieces, places)):
         pieces.append(shift(piece, "sat", size, 1))
-        places.append((d + 1, part, parts))
+        places.append((d + 1, *rest))
     return pieces, tuple(places)
 
 
@@ -525,17 +543,25 @@
         -(-(((columns * i) % 8) + columns) // 8) for i in range(columns_axis)
     )
 
-    parts = 2 if own % 2 == 0 and nz > 1 else 1
-    half = cut_half(orbit, lambda mine: lax.rem(lax.div(mine, nx), 2)) if parts > 1 else None
+    parts = cut_parts(orbit, columns_axis, nx)
+    orbit_pieces, places = gather_orbit(orbit, parts, group, columns_axis, nx)
+    if parts:
+        knots, orbit_pieces[1] = lax.optimization_barrier((knots, orbit_pieces[1]))
     planes, extra = prepare(sight, mapping, residual, counts, track, knots)
-    orbit_pieces, places = gather_orbit(orbit, half, group, columns_axis, nx)
     plane_pieces = gather_pieces(planes, group)
-    extra, _ = lax.optimization_barrier((extra, plane_pieces[group - 2]))
-    extra_pieces = gather_pieces(extra, group)
     all_planes, all_track, highs, lows = own_rows_of(plane_pieces, orbit, width)
     *sums, own_rows = accumulate(
-        group, all_planes, all_track, highs, lows, orbit_pieces, places, nx, nz, window)
-    small = own_sums(plane_pieces, extra_pieces, own_rows, orbit)
+        group, all_planes, all_track, highs, lows, place(orbit_pieces, places, sats, nx),
+        nx, nz, window)
+    extra, _ = lax.optimization_barrier((extra, all_track))
+    extra_pieces = {0: extra}
+    for d in range(2, group, 2):
+        extra_pieces[d] = shift(extra, "sat", group, d)
+    for d in range(0, group, 2):
+        held, _ = lax.optimization_barrier((extra_pieces[d], own_rows))
+        extra_pieces[d + 1] = shift(held, "sat", group, 1)
+    small = own_sums(
+        plane_pieces, [extra_pieces[d] for d in range(group)], own_rows, orbit)
     arrived = [sums[0]] + [shift(sums[d], "sta", columns_axis, d) for d in range(1, nx)]
     smalls = [small] + [shift(small, "sta", columns_axis, d) for d in range(1, nx)]
     chunks = combine(arrived, smalls, nz, window)

time: 66.4 us -> 65.8 us (level)
  waiting for transfers between devices: 33.6 us -> 29.4 us
  local copies, waits for them, and re-layouts: 0.96 us -> 3.78 us
  starting transfers between devices: 14.7 us -> 17.2 us
  Pallas kernels: 16.2 us -> 14.4 us
    ppermute x16 -> x20, waiting for transfers between devices: 33.6 us -> 29.4 us  [shift(): return lax.ppermute(value, axis, [(i, i ^ step) for i in range(size)])]
    ppermute x16 -> x20, starting transfers between devices: 14.7 us -> 17.2 us  [shift(): return lax.ppermute(value, axis, [(i, i ^ step) for i in range(size)])]
    dynamic_slice x0 -> x2, local copies, waits for them, and re-layouts: none -> 1.94 us  [the longest x1 1 us: cut_parts(): lax.dynamic_slice_in_dim(orbit, at + lead, half - lead, 0)]
    pallas_call x1, Pallas kernels: 1.81 us -> 0.2 us  [place(): pl.pallas_call(functools.partial(place_kernel, own, nx, places), out_shap...]
    unnamed x6 -> x8, local copies, waits for them, and re-layouts: 0.96 us -> 1.84 us
  transfers between devices with their start and end apart: 16 -> 20, of which waited for: 6 -> 9; matrix products, arithmetic and copies ran while one was open for 0% -> 3% of each run, Pallas kernels for 20% -> 16%
where the time goes in v5:
time: 65.8 us; the launch traced here: 65.6 us
  waiting for transfers between devices  29.4 us (45%)
  starting transfers between devices  17.2 us (26%)
  Pallas kernels  14.4 us (22%)
  local copies, waits for them, and re-layouts  3.78 us (6%)
  between operations  0.75 us (1%)
    ppermute x20, waiting for transfers between devices, shift(): return lax.ppermute(value, axis, [(i, i ^ step) for i in range(size)])  29.4 us
    ppermute x20, starting transfers between devices, shift(): return lax.ppermute(value, axis, [(i, i ^ step) for i in range(size)])  17.2 us
    pallas_call x1, Pallas kernels, accumulate(): pl.pallas_call(functools.partial(main_kernel, groups, stations // groups,...  4.76 us
    pallas_call x1, Pallas kernels, own_sums(): pl.pallas_call(functools.partial(blocks_kernel, groups, per, own), out_sh...  3.43 us
    pallas_call x1, Pallas kernels, own_rows_of(): pl.pallas_call(functools.partial(own_rows_kernel, groups, per, own, width...  2.73 us
    pallas_call x1, Pallas kernels, prepare(): pl.pallas_call(prepare_kernel, out_shape=[jax.ShapeDtypeStruct((stations,...  1.98 us
    unnamed x8, local copies, waits for them, and re-layouts  1.84 us
  transfers between devices with their start and end apart: 20, of which 9 were waited for; matrix products, arithmetic and copies ran while one was open for 3% of the time, Pallas kernels for 16%

profile of v5, /device:TPU:0, one launch (start us, length us, event | category | flops | bytes accessed | tf_op | source)
XLA Modules:
  0.0 65.6 jit_solution(11744740216429097457)
XLA Ops:
  0.6 0.5 collective-permute-start.7
  1.1 0.9 %constant_dynamic-slice_fusion.1 = f32[8,3,8,256]{3,2,1,0:T(8,128)S(1)} fusion(f32[30,3,8,256]{3,2,1,0:T(8,128)} %refs_9_.1, s32[]{:T(128)S(6)} %select_n.6), kind=kLoop, calls=%fused_computation.1 | loop fusion | bytes 393220 | tf_op jit(solution)/shard_map/dynamic_slice | solution.py:504
  2.1 2.6 %collective-permute-start = (f32[8,3,8,256]{3,2,1,0:T(8,128)S(1)}, f32[8,3,8,256]{3,2,1,0:T(8,128)S(1)}, u32[]{:S(2)}, u32[]{:S(2)}) collective-permute-start(f32[8,3,8,256]{3,2,1,0:T(8,128)S(1)} %constant_dynamic-slice_fusion.1), channel_id=1, source_target_pairs={{0,2},{1,3},{2,0},{3,1},{4,6},{5,7},{6,4},{7,5},{8,10},{9,11},{10,... | collective-permute-start | bytes 589832 | tf_op jit(solution)/shard_map/ppermute | solution.py:480
  4.7 0.0 copy-start.1
  4.7 1.0 %constant_dynamic-slice_fusion = f32[7,3,8,256]{3,2,1,0:T(8,128)S(1)} fusion(f32[30,3,8,256]{3,2,1,0:T(8,128)} %refs_9_.1, s32[]{:T(128)S(6)} %select_n.7), kind=kLoop, calls=%fused_computation | loop fusion | bytes 344068 | tf_op jit(solution)/shard_map/dynamic_slice | solution.py:505
  5.7 0.1 collective-permute-start.4
  5.8 4.7 %collective-permute-done.refs_1_ = f32[8,3,8,256]{3,2,1,0:T(8,128)S(1)} collective-permute-done((f32[8,3,8,256]{3,2,1,0:T(8,128)S(1)}, f32[8,3,8,256]{3,2,1,0:T(8,128)S(1)}, u32[]{:S(2)}, u32[]{:S(2)}) %collective-permute-start) | collective-permute-done | bytes 196640 | tf_op jit(solution)/shard_map/ppermute | solution.py:480
  10.5 2.0 %prepare.1 = (f32[2,136,256]{2,1,0:T(8,128)}, f32[2,64,256]{2,1,0:T(8,128)}) custom-call(f32[2,3,32,256]{3,2,1,0:T(8,128)} %refs_0_.2, f32[2,32,256]{2,1,0:T(8,128)} %refs_1_.1, f32[2,32,256]{2,1,0:T(8,128)} %refs_2_.1, s32[2,32,256]{2,1,0:T(8,128)} %refs_3_.1, s32[2,32]{1,0:T(2,128)} %refs_4_.2, s32[2,256]{1,0:T(2,128)} %refs_5_), custom_call_target="tpu_custom_call" | custom-call | tf_op jit(solution)/shard_map/prepare/pallas_call | solution.py:76
  12.5 2.0 %collective-permute-start.2 = (f32[2,136,256]{2,1,0:T(8,128)}, f32[2,136,256]{2,1,0:T(8,128)S(1)}, u32[]{:S(2)}, u32[]{:S(2)}) collective-permute-start(f32[2,136,256]{2,1,0:T(8,128)} %get-tuple-element.25.refs_0_), channel_id=1, source_target_pairs={{0,2},{1,3},{2,0},{3,1},{4,6},{5,7},{6,4},{7,5},{8,10},{9,11},{10,... | collective-permute-start | bytes 835592 | tf_op jit(solution)/shard_map/ppermute | solution.py:480
  14.5 0.0 collective-permute-done.4.refs_2_
  14.5 0.0 collective-permute-start.9
  14.5 1.5 %collective-permute-start.6 = (f32[7,3,8,256]{3,2,1,0:T(8,128)S(1)}, f32[7,3,8,256]{3,2,1,0:T(8,128)S(1)}, u32[]{:S(2)}, u32[]{:S(2)}) collective-permute-start(f32[7,3,8,256]{3,2,1,0:T(8,128)S(1)} %collective-permute-done.4.refs_2_), channel_id=1, source_target_pairs={{0,4},{4,0},{8,12},{12,8},{16,20},{20,16},{24,28},{28,24},{1,5},{5... | collective-permute-start | bytes 516104 | tf_op jit(solution)/shard_map/ppermute | solution.py:480
  16.0 1.6 %collective-permute-start.5 = (f32[8,3,8,256]{3,2,1,0:T(8,128)S(1)}, f32[8,3,8,256]{3,2,1,0:T(8,128)S(1)}, u32[]{:S(2)}, u32[]{:S(2)}) collective-permute-start(f32[8,3,8,256]{3,2,1,0:T(8,128)S(1)} %collective-permute-done.refs_1_), channel_id=1, source_target_pairs={{0,8},{4,12},{8,0},{12,4},{16,24},{20,28},{24,16},{28,20},{1,9},{5... | collective-permute-start | bytes 589832 | tf_op jit(solution)/shard_map/ppermute | solution.py:480
  17.5 0.0 collective-permute-done.9.refs_7_
  17.5 0.0 collective-permute-start.8
  17.6 3.7 %collective-permute-done.6.refs_4_ = f32[7,3,8,256]{3,2,1,0:T(8,128)S(1)} collective-permute-done((f32[7,3,8,256]{3,2,1,0:T(8,128)S(1)}, f32[7,3,8,256]{3,2,1,0:T(8,128)S(1)}, u32[]{:S(2)}, u32[]{:S(2)}) %collective-permute-start.6) | collective-permute-done | bytes 172064 | tf_op jit(solution)/shard_map/ppermute | solution.py:480
  21.3 0.0 collective-permute-start.1
  21.3 0.0 collective-permute-done.2.refs_2_
  21.3 0.5 collective-permute-start.3
  21.8 1.2 %collective-permute-done.5.refs_3_ = f32[8,3,8,256]{3,2,1,0:T(8,128)S(1)} collective-permute-done((f32[8,3,8,256]{3,2,1,0:T(8,128)S(1)}, f32[8,3,8,256]{3,2,1,0:T(8,128)S(1)}, u32[]{:S(2)}, u32[]{:S(2)}) %collective-permute-start.5) | collective-permute-done | bytes 196640 | tf_op jit(solution)/shard_map/ppermute | solution.py:480
  23.0 0.0 collective-permute-start.10
  23.0 0.0 collective-permute-done.8.refs_6_
  23.0 0.5 collective-permute-start.11
  23.5 1.2 %collective-permute-done.11.refs_9_ = f32[7,3,8,256]{3,2,1,0:T(8,128)S(1)} collective-permute-done((f32[7,3,8,256]{3,2,1,0:T(8,128)S(1)}, f32[7,3,8,256]{3,2,1,0:T(8,128)S(1)}, u32[]{:S(2)}, u32[]{:S(2)}) %collective-permute-start.11) | collective-permute-done | bytes 172064 | tf_op jit(solution)/shard_map/ppermute | solution.py:480
  24.7 0.0 collective-permute-done.10.refs_8_
  24.7 0.0 collective-permute-done.7.refs_5_
  24.7 0.0 copy-start
  24.7 1.1 %copy-done = f32[30,3,8,256]{3,2,1,0:T(8,128)S(1)} copy-done((f32[30,3,8,256]{3,2,1,0:T(8,128)S(1)}, f32[30,3,8,256]{3,2,1,0:T(8,128)}, u32[]{:S(2)}) %copy-start) | copy-done | bytes 737304
  25.8 0.0 copy-start.2
  25.8 0.2 place.1.refs_4_
  26.0 0.0 copy-start.3
  26.0 0.0 collective-permute-done.1.refs_1_
  26.0 0.0 collective-permute-done.3.refs_3_
  26.0 0.0 copy-done.1
  26.1 0.7 %copy-done.2 = f32[2,136,256]{2,1,0:T(8,128)S(1)} copy-done((f32[2,136,256]{2,1,0:T(8,128)S(1)}, f32[2,136,256]{2,1,0:T(8,128)}, u32[]{:S(2)}) %copy-start.2) | copy-done | bytes 278552
  26.8 2.7 %own_rows.1 = (f32[8,136,256]{2,1,0:T(8,128)S(1)}, s32[8,128]{1,0:T(8,128)S(1)}, bf16[8,256,256]{2,1,0:T(8,128)(2,1)S(1)}, bf16[8,256,256]{2,1,0:T(8,128)(2,1)S(1)}) custom-call(f32[2,136,256]{2,1,0:T(8,128)S(1)} %copy-done.2, f32[2,136,256]{2,1,0:T(8,128)S(1)} %collective-permute-done.1.refs_1_, f32[2,136,256]{2,1,0:T(8,128)S(1)} %collective-permute-done.2.refs_2_, ...), custom_call_target="tpu_custom_call" | custom-call | flops 8000000000 | bytes 8000000 | tf_op jit(solution)/shard_map/own_rows/pallas_call | solution.py:168
  29.5 0.0 copy-done.3
  29.5 1.2 %collective-permute-start.14 = (f32[2,64,256]{2,1,0:T(8,128)S(1)}, f32[2,64,256]{2,1,0:T(8,128)S(1)}, u32[]{:S(2)}, u32[]{:S(2)}) collective-permute-start(f32[2,64,256]{2,1,0:T(8,128)S(1)} %copy-done.3), channel_id=1, source_target_pairs={{0,2},{1,3},{2,0},{3,1},{4,6},{5,7},{6,4},{7,5},{8,10},{9,11},{10,... | collective-permute-start | bytes 393224 | tf_op jit(solution)/shard_map/ppermute | solution.py:480
  30.8 4.8 %accumulate.1 = (f32[60,8,256]{2,1,0:T(8,128)S(1)}, f32[60,8,256]{2,1,0:T(8,128)S(1)}, f32[30,8,256]{2,1,0:T(8,128)S(1)}) custom-call(f32[8,136,256]{2,1,0:T(8,128)S(1)} %get-tuple-element.26.refs_0_, s32[8,128]{1,0:T(8,128)S(1)} %get-tuple-element.27.refs_1_, bf16[8,256,256]{2,1,0:T(8,128)(2,1)S(1)} %get-tuple-element.28.refs_2_, ...), custom_call_target="tpu_custom_call" | custom-call | flops 8000000000 | bytes 8000000 | tf_op jit(solution)/shard_map/accumulate/pallas_call | solution.py:324
  35.5 0.1 collective-permute-start.13
  35.6 0.0 collective-permute-done.14.refs_6_
  35.6 0.5 collective-permute-start.15
  36.1 0.6 collective-permute-start.12
  36.7 0.3 collective-permute-done.13.refs_5_
  37.0 0.2 collective-permute-done.15.refs_7_
  37.1 3.4 %own_sums.1.refs_2_ = f32[2,8,256]{2,1,0:T(8,128)S(1)} custom-call(f32[2,136,256]{2,1,0:T(8,128)S(1)} %copy-done.2, f32[2,136,256]{2,1,0:T(8,128)S(1)} %collective-permute-done.1.refs_1_, f32[2,136,256]{2,1,0:T(8,128)S(1)} %collective-permute-done.2.refs_2_, f32[2,136,256]{2,1,0:T(8,128)S(1)} %collective-permute-done.3.refs_3_, f32[2,64,256]{2,1,0:T(8,128)S(1)} %copy-done.3, ...), custom_call_target="tpu_custom_call" | custom-call | flops 4000000000 | bytes 4000000 | tf_op jit(solution)/shard_map/own_sums/pallas_call | solution.py:397
  40.6 1.1 %collective-permute-start.16 = (f32[2,8,256]{2,1,0:T(8,128)S(1)}, f32[2,8,256]{2,1,0:T(8,128)S(1)}, u32[]{:S(2)}, u32[]{:S(2)}) collective-permute-start(f32[2,8,256]{2,1,0:T(8,128)S(1)} %own_sums.1.refs_2_), channel_id=1, source_target_pairs={{0,4},{4,0},{8,12},{12,8},{16,20},{20,16},{24,28},{28,24},{1,5},{5... | collective-permute-start | bytes 49160 | tf_op jit(solution)/shard_map/ppermute | solution.py:480
  41.7 8.0 %collective-permute-done.16.refs_3_ = f32[2,8,256]{2,1,0:T(8,128)S(1)} collective-permute-done((f32[2,8,256]{2,1,0:T(8,128)S(1)}, f32[2,8,256]{2,1,0:T(8,128)S(1)}, u32[]{:S(2)}, u32[]{:S(2)}) %collective-permute-start.16) | collective-permute-done | bytes 16416 | tf_op jit(solution)/shard_map/ppermute | solution.py:480
  49.7 0.0 collective-permute-done.12.refs_1_
  49.7 0.1 combine.1
  49.7 1.6 %collective-permute-start.17 = (f32[17,8,256]{2,1,0:T(8,128)S(1)}, f32[17,8,256]{2,1,0:T(8,128)S(1)}, u32[]{:S(2)}, u32[]{:S(2)}) collective-permute-start(f32[17,8,256]{2,1,0:T(8,128)S(1)} %get-tuple-element.39), channel_id=1, source_target_pairs={{0,8},{4,12},{8,0},{12,4},{16,24},{20,28},{24,16},{28,20},{1,9},{5... | collective-permute-start | bytes 417800 | tf_op jit(solution)/shard_map/ppermute | solution.py:480
  51.4 2.6 %collective-permute-start.18 = (f32[17,8,256]{2,1,0:T(8,128)S(1)}, f32[17,8,256]{2,1,0:T(8,128)S(1)}, u32[]{:S(2)}, u32[]{:S(2)}) collective-permute-start(f32[17,8,256]{2,1,0:T(8,128)S(1)} %get-tuple-element.40), channel_id=1, source_target_pairs={{0,16},{4,20},{8,24},{12,28},{16,0},{20,4},{24,8},{28,12},{1,17},{... | collective-permute-start | bytes 417800 | tf_op jit(solution)/shard_map/ppermute | solution.py:480
  54.0 0.2 collective-permute-start.19
  54.2 2.3 %collective-permute-done.17.refs_1_ = f32[17,8,256]{2,1,0:T(8,128)S(1)} collective-permute-done((f32[17,8,256]{2,1,0:T(8,128)S(1)}, f32[17,8,256]{2,1,0:T(8,128)S(1)}, u32[]{:S(2)}, u32[]{:S(2)}) %collective-permute-start.17) | collective-permute-done | bytes 139296 | tf_op jit(solution)/shard_map/ppermute | solution.py:480
  56.5 7.9 %collective-permute-done.18.refs_2_ = f32[17,8,256]{2,1,0:T(8,128)S(1)} collective-permute-done((f32[17,8,256]{2,1,0:T(8,128)S(1)}, f32[17,8,256]{2,1,0:T(8,128)S(1)}, u32[]{:S(2)}, u32[]{:S(2)}) %collective-permute-start.18) | collective-permute-done | bytes 139296 | tf_op jit(solution)/shard_map/ppermute | solution.py:480
  64.3 0.0 collective-permute-done.19.refs_3_
  64.3 1.2 %finish.1 = (f32[240,120]{1,0:T(8,128)}, f32[1,240]{1,0:T(1,128)}, f32[8,8,30]{2,1,0:T(8,128)}) custom-call(f32[17,8,256]{2,1,0:T(8,128)S(1)} %get-tuple-element.38.refs_0_, f32[17,8,256]{2,1,0:T(8,128)S(1)} %collective-permute-done.17.refs_1_, f32[17,8,256]{2,1,0:T(8,128)S(1)} %collective-permute-done.18.refs_2_, ...), custom_call_target="tpu_custom_call" | custom-call | tf_op jit(solution)/shard_map/finish/pallas_call | solution.py:465
Async XLA Ops:
  0.6 24.1 %collective-permute-start.7 = (f32[30,3,8,256]{3,2,1,0:T(8,128)}, f32[30,3,8,256]{3,2,1,0:T(8,128)S(1)}, u32[]{:S(2)}, u32[]{:S(2)}) collective-permute-start(f32[30,3,8,256]{3,2,1,0:T(8,128)} %refs_9_.1), channel_id=1, source_target_pairs={{0,1},{1,0},{2,3},{3,2},{4,5},{5,4},{6,7},{7,6},{8,9},{9,8},{10,11... | collective-permute-start | bytes 2211848 | tf_op jit(solution)/shard_map/ppermute | solution.py:480
  2.1 8.4 %collective-permute-start = (f32[8,3,8,256]{3,2,1,0:T(8,128)S(1)}, f32[8,3,8,256]{3,2,1,0:T(8,128)S(1)}, u32[]{:S(2)}, u32[]{:S(2)}) collective-permute-start(f32[8,3,8,256]{3,2,1,0:T(8,128)S(1)} %constant_dynamic-slice_fusion.1), channel_id=1, source_target_pairs={{0,2},{1,3},{2,0},{3,1},{4,6},{5,7},{6,4},{7,5},{8,10},{9,11},{10,... | collective-permute-start | bytes 589832 | tf_op jit(solution)/shard_map/ppermute | solution.py:480
  4.7 21.3 %copy-start.1 = (f32[30,3,8,256]{3,2,1,0:T(8,128)S(1)}, f32[30,3,8,256]{3,2,1,0:T(8,128)}, u32[]{:S(2)}) copy-start(f32[30,3,8,256]{3,2,1,0:T(8,128)} %refs_9_.1) | copy-start | bytes 2211844
  5.7 8.8 %collective-permute-start.4 = (f32[7,3,8,256]{3,2,1,0:T(8,128)S(1)}, f32[7,3,8,256]{3,2,1,0:T(8,128)S(1)}, u32[]{:S(2)}, u32[]{:S(2)}) collective-permute-start(f32[7,3,8,256]{3,2,1,0:T(8,128)S(1)} %constant_dynamic-slice_fusion), channel_id=1, source_target_pairs={{0,2},{1,3},{2,0},{3,1},{4,6},{5,7},{6,4},{7,5},{8,10},{9,11},{10,... | collective-permute-start | bytes 516104 | tf_op jit(solution)/shard_map/ppermute | solution.py:480
  12.5 8.8 %collective-permute-start.2 = (f32[2,136,256]{2,1,0:T(8,128)}, f32[2,136,256]{2,1,0:T(8,128)S(1)}, u32[]{:S(2)}, u32[]{:S(2)}) collective-permute-start(f32[2,136,256]{2,1,0:T(8,128)} %get-tuple-element.25.refs_0_), channel_id=1, source_target_pairs={{0,2},{1,3},{2,0},{3,1},{4,6},{5,7},{6,4},{7,5},{8,10},{9,11},{10,... | collective-permute-start | bytes 835592 | tf_op jit(solution)/shard_map/ppermute | solution.py:480
  14.5 3.1 %collective-permute-start.9 = (f32[7,3,8,256]{3,2,1,0:T(8,128)S(1)}, f32[7,3,8,256]{3,2,1,0:T(8,128)S(1)}, u32[]{:S(2)}, u32[]{:S(2)}) collective-permute-start(f32[7,3,8,256]{3,2,1,0:T(8,128)S(1)} %collective-permute-done.4.refs_2_), channel_id=1, source_target_pairs={{0,1},{1,0},{2,3},{3,2},{4,5},{5,4},{6,7},{7,6},{8,9},{9,8},{10,11... | collective-permute-start | bytes 516104 | tf_op jit(solution)/shard_map/ppermute | solution.py:480
  14.5 6.8 %collective-permute-start.6 = (f32[7,3,8,256]{3,2,1,0:T(8,128)S(1)}, f32[7,3,8,256]{3,2,1,0:T(8,128)S(1)}, u32[]{:S(2)}, u32[]{:S(2)}) collective-permute-start(f32[7,3,8,256]{3,2,1,0:T(8,128)S(1)} %collective-permute-done.4.refs_2_), channel_id=1, source_target_pairs={{0,4},{4,0},{8,12},{12,8},{16,20},{20,16},{24,28},{28,24},{1,5},{5... | collective-permute-start | bytes 516104 | tf_op jit(solution)/shard_map/ppermute | solution.py:480
  16.0 7.0 %collective-permute-start.5 = (f32[8,3,8,256]{3,2,1,0:T(8,128)S(1)}, f32[8,3,8,256]{3,2,1,0:T(8,128)S(1)}, u32[]{:S(2)}, u32[]{:S(2)}) collective-permute-start(f32[8,3,8,256]{3,2,1,0:T(8,128)S(1)} %collective-permute-done.refs_1_), channel_id=1, source_target_pairs={{0,8},{4,12},{8,0},{12,4},{16,24},{20,28},{24,16},{28,20},{1,9},{5... | collective-permute-start | bytes 589832 | tf_op jit(solution)/shard_map/ppermute | solution.py:480
  17.5 5.5 %collective-permute-start.8 = (f32[8,3,8,256]{3,2,1,0:T(8,128)S(1)}, f32[8,3,8,256]{3,2,1,0:T(8,128)S(1)}, u32[]{:S(2)}, u32[]{:S(2)}) collective-permute-start(f32[8,3,8,256]{3,2,1,0:T(8,128)S(1)} %collective-permute-done.refs_1_), channel_id=1, source_target_pairs={{0,1},{1,0},{2,3},{3,2},{4,5},{5,4},{6,7},{7,6},{8,9},{9,8},{10,11... | collective-permute-start | bytes 589832 | tf_op jit(solution)/shard_map/ppermute | solution.py:480
  21.3 4.8 %collective-permute-start.1 = (f32[2,136,256]{2,1,0:T(8,128)}, f32[2,136,256]{2,1,0:T(8,128)S(1)}, u32[]{:S(2)}, u32[]{:S(2)}) collective-permute-start(f32[2,136,256]{2,1,0:T(8,128)} %get-tuple-element.25.refs_0_), channel_id=1, source_target_pairs={{0,1},{1,0},{2,3},{3,2},{4,5},{5,4},{6,7},{7,6},{8,9},{9,8},{10,11... | collective-permute-start | bytes 835592 | tf_op jit(solution)/shard_map/ppermute | solution.py:480
  21.3 4.8 %collective-permute-start.3 = (f32[2,136,256]{2,1,0:T(8,128)S(1)}, f32[2,136,256]{2,1,0:T(8,128)S(1)}, u32[]{:S(2)}, u32[]{:S(2)}) collective-permute-start(f32[2,136,256]{2,1,0:T(8,128)S(1)} %collective-permute-done.2.refs_2_), channel_id=1, source_target_pairs={{0,1},{1,0},{2,3},{3,2},{4,5},{5,4},{6,7},{7,6},{8,9},{9,8},{10,11... | collective-permute-start | bytes 835592 | tf_op jit(solution)/shard_map/ppermute | solution.py:480
  23.0 1.7 %collective-permute-start.10 = (f32[8,3,8,256]{3,2,1,0:T(8,128)S(1)}, f32[8,3,8,256]{3,2,1,0:T(8,128)S(1)}, u32[]{:S(2)}, u32[]{:S(2)}) collective-permute-start(f32[8,3,8,256]{3,2,1,0:T(8,128)S(1)} %collective-permute-done.5.refs_3_), channel_id=1, source_target_pairs={{0,1},{1,0},{2,3},{3,2},{4,5},{5,4},{6,7},{7,6},{8,9},{9,8},{10,11... | collective-permute-start | bytes 589832 | tf_op jit(solution)/shard_map/ppermute | solution.py:480
  23.0 1.7 %collective-permute-start.11 = (f32[7,3,8,256]{3,2,1,0:T(8,128)S(1)}, f32[7,3,8,256]{3,2,1,0:T(8,128)S(1)}, u32[]{:S(2)}, u32[]{:S(2)}) collective-permute-start(f32[7,3,8,256]{3,2,1,0:T(8,128)S(1)} %collective-permute-done.6.refs_4_), channel_id=1, source_target_pairs={{0,1},{1,0},{2,3},{3,2},{4,5},{5,4},{6,7},{7,6},{8,9},{9,8},{10,11... | collective-permute-start | bytes 516104 | tf_op jit(solution)/shard_map/ppermute | solution.py:480
  24.7 1.1 %copy-start = (f32[30,3,8,256]{3,2,1,0:T(8,128)S(1)}, f32[30,3,8,256]{3,2,1,0:T(8,128)}, u32[]{:S(2)}) copy-start(f32[30,3,8,256]{3,2,1,0:T(8,128)} %refs_9_.1) | copy-start | bytes 2211844
  25.8 1.0 %copy-start.2 = (f32[2,136,256]{2,1,0:T(8,128)S(1)}, f32[2,136,256]{2,1,0:T(8,128)}, u32[]{:S(2)}) copy-start(f32[2,136,256]{2,1,0:T(8,128)} %get-tuple-element.25.refs_0_) | copy-start | bytes 835588
  26.0 3.5 %copy-start.3 = (f32[2,64,256]{2,1,0:T(8,128)S(1)}, f32[2,64,256]{2,1,0:T(8,128)}, u32[]{:S(2)}) copy-start(f32[2,64,256]{2,1,0:T(8,128)} %get-tuple-element.36.refs_4_) | copy-start | bytes 393220
  29.5 6.1 %collective-permute-start.14 = (f32[2,64,256]{2,1,0:T(8,128)S(1)}, f32[2,64,256]{2,1,0:T(8,128)S(1)}, u32[]{:S(2)}, u32[]{:S(2)}) collective-permute-start(f32[2,64,256]{2,1,0:T(8,128)S(1)} %copy-done.3), channel_id=1, source_target_pairs={{0,2},{1,3},{2,0},{3,1},{4,6},{5,7},{6,4},{7,5},{8,10},{9,11},{10,... | collective-permute-start | bytes 393224 | tf_op jit(solution)/shard_map/ppermute | solution.py:480
  35.5 1.4 %collective-permute-start.13 = (f32[2,64,256]{2,1,0:T(8,128)S(1)}, f32[2,64,256]{2,1,0:T(8,128)S(1)}, u32[]{:S(2)}, u32[]{:S(2)}) collective-permute-start(f32[2,64,256]{2,1,0:T(8,128)S(1)} %copy-done.3), channel_id=1, source_target_pairs={{0,1},{1,0},{2,3},{3,2},{4,5},{5,4},{6,7},{7,6},{8,9},{9,8},{10,11... | collective-permute-start | bytes 393224 | tf_op jit(solution)/shard_map/ppermute | solution.py:480
  35.6 1.5 %collective-permute-start.15 = (f32[2,64,256]{2,1,0:T(8,128)S(1)}, f32[2,64,256]{2,1,0:T(8,128)S(1)}, u32[]{:S(2)}, u32[]{:S(2)}) collective-permute-start(f32[2,64,256]{2,1,0:T(8,128)S(1)} %collective-permute-done.14.refs_6_), channel_id=1, source_target_pairs={{0,1},{1,0},{2,3},{3,2},{4,5},{5,4},{6,7},{7,6},{8,9},{9,8},{10,11... | collective-permute-start | bytes 393224 | tf_op jit(solution)/shard_map/ppermute | solution.py:480
  36.1 13.6 %collective-permute-start.12 = (f32[60,8,256]{2,1,0:T(8,128)S(1)}, f32[60,8,256]{2,1,0:T(8,128)S(1)}, u32[]{:S(2)}, u32[]{:S(2)}) collective-permute-start(f32[60,8,256]{2,1,0:T(8,128)S(1)} %get-tuple-element.32), channel_id=1, source_target_pairs={{0,4},{4,0},{8,12},{12,8},{16,20},{20,16},{24,28},{28,24},{1,5},{5... | collective-permute-start | bytes 1474568 | tf_op jit(solution)/shard_map/ppermute | solution.py:480
  40.6 9.1 %collective-permute-start.16 = (f32[2,8,256]{2,1,0:T(8,128)S(1)}, f32[2,8,256]{2,1,0:T(8,128)S(1)}, u32[]{:S(2)}, u32[]{:S(2)}) collective-permute-start(f32[2,8,256]{2,1,0:T(8,128)S(1)} %own_sums.1.refs_2_), channel_id=1, source_target_pairs={{0,4},{4,0},{8,12},{12,8},{16,20},{20,16},{24,28},{28,24},{1,5},{5... | collective-permute-start | bytes 49160 | tf_op jit(solution)/shard_map/ppermute | solution.py:480
  49.7 6.7 %collective-permute-start.17 = (f32[17,8,256]{2,1,0:T(8,128)S(1)}, f32[17,8,256]{2,1,0:T(8,128)S(1)}, u32[]{:S(2)}, u32[]{:S(2)}) collective-permute-start(f32[17,8,256]{2,1,0:T(8,128)S(1)} %get-tuple-element.39), channel_id=1, source_target_pairs={{0,8},{4,12},{8,0},{12,4},{16,24},{20,28},{24,16},{28,20},{1,9},{5... | collective-permute-start | bytes 417800 | tf_op jit(solution)/shard_map/ppermute | solution.py:480
  51.4 12.9 %collective-permute-start.18 = (f32[17,8,256]{2,1,0:T(8,128)S(1)}, f32[17,8,256]{2,1,0:T(8,128)S(1)}, u32[]{:S(2)}, u32[]{:S(2)}) collective-permute-start(f32[17,8,256]{2,1,0:T(8,128)S(1)} %get-tuple-element.40), channel_id=1, source_target_pairs={{0,16},{4,20},{8,24},{12,28},{16,0},{20,4},{24,8},{28,12},{1,17},{... | collective-permute-start | bytes 417800 | tf_op jit(solution)/shard_map/ppermute | solution.py:480
  54.0 10.4 %collective-permute-start.19 = (f32[17,8,256]{2,1,0:T(8,128)S(1)}, f32[17,8,256]{2,1,0:T(8,128)S(1)}, u32[]{:S(2)}, u32[]{:S(2)}) collective-permute-start(f32[17,8,256]{2,1,0:T(8,128)S(1)} %get-tuple-element.41), channel_id=1, source_target_pairs={{0,24},{4,28},{8,16},{12,20},{16,8},{20,12},{24,0},{28,4},{1,25},{... | collective-permute-start | bytes 417800 | tf_op jit(solution)/shard_map/ppermute | solution.py:480

commit v6 on v5

--- a/solution.py
+++ b/solution.py
@@ -9,9 +9,10 @@
 
 KNOTS = 4
 PRIOR = 1.0
+PACKED = 128 // KNOTS
 HIGHEST = lax.Precision.HIGHEST
 SMALL_LIMIT = 8 * 1024 * 1024
-MEDIUM_LIMIT = 16 * 1024 * 1024
+MEDIUM_LIMIT = 40 * 1024 * 1024
 HUGE_LIMIT = 56 * 1024 * 1024
 NT = (((1,), (1,)), ((), ()))
 
@@ -214,10 +215,10 @@
 
 def main_kernel(groups, per, own, nx, nz, window, *refs):
     planes, track, highs, lows, orbit = refs[:5]
-    outs = refs[5 : 5 + nx]
-    own_out = refs[5 + nx]
+    outs = refs[5 : 5 + nz]
+    own_out = refs[5 + nz]
     (acc, stream_a, stream_b, product_a, product_b, tropo_a, tropo_b,
-     spread_tropo) = refs[6 + nx :]
+     spread_tropo) = refs[6 + nz :]
     streams = (stream_a, stream_b)
     products, tropos = (product_a, product_b), (tropo_a, tropo_b)
     stations = groups * per
@@ -265,10 +266,13 @@
         mixed = dot_nt(stream[2 * span : 3 * span, :], high)
         mixed = (mixed + dot_nt(stream[3 * span :, :], high))[:, width - 128 :]
         kept = jnp.logical_and(lane >= place, lane < place + KNOTS)
-        tropos[turn][...] = jnp.where(kept, mixed, 0.0).reshape(tracked, 8, 128)
+        kept = jnp.where(kept, mixed, 0.0)
+        home = lax.rem(s, PACKED) * KNOTS
+        kept = pltpu.roll(kept, lax.rem(home + spare - place, 128), 1)
+        tropos[turn][...] = kept.reshape(tracked, 8, 128)
 
     def scatter(s, turn):
-        slab = lax.div(s, packed)
+        slab = lax.div(s, PACKED)
         for m in range(tracked):
             k = track[s, m]
             acc[k] = acc[k] - products[turn][m]
@@ -293,24 +297,25 @@
     multiply(stations - 1, 1)
     scatter(stations - 1, 1)
 
-    slabs = spread_tropo.shape[0]
-    left, right = [], []
-    for slab in range(slabs):
+    outer = jnp.zeros((sats * 8, own * 8), jnp.float32)
+    for slab in range(spread_tropo.shape[0]):
         high, low = split(spread_tropo[slab].reshape(sats * 8, 128))
         own_high, own_low = split(spread_tropo[slab, pl.ds(first, own)].reshape(own * 8, 128))
-        left += [high, high, low]
-        right += [own_high, own_low, own_high]
-    outer = dot_nt(jnp.concatenate(left, 1), jnp.concatenate(right, 1))
+        left = jnp.concatenate([high, high, low], 1)
+        right = jnp.concatenate([own_high, own_low, own_high], 1)
+        outer = outer + dot_nt(left, right)
     if own * 8 < width:
         outer = jnp.concatenate(
             [outer, jnp.zeros((sats * 8, width - own * 8), jnp.float32)], 1)
     acc[...] = acc[...] - outer.reshape(sats, 8, width)
 
-    own_out[...] = acc[pl.ds(first, own)]
-    for dx in range(nx):
-        for dz in range(nz):
-            start = window_start(mine ^ (dz * nx + dx), sats * 8 // (nx * nz), sats, window)
-            outs[dx][dz * window : (dz + 1) * window] = acc[pl.ds(start, window)]
+    columns = sats * 8 // (nx * nz)
+    owner = first + lax.broadcasted_iota(jnp.int32, (own, 8, width), 0)
+    here = lax.rem(lax.div(owner * 8, columns), nx) == lax.rem(mine, nx)
+    own_out[...] = jnp.where(here, acc[pl.ds(first, own)], 0.0)
+    for dz in range(nz):
+        start = window_start(mine ^ (dz * nx), columns, sats, window)
+        outs[dz][...] = acc[pl.ds(start, window)]
 
 
 def accumulate(groups, planes, track, highs, lows, orbit, nx, nz, window):
@@ -319,14 +324,14 @@
     own = sats // groups
     tracked = (rows - 8) // 4
     width = highs.shape[1]
-    slabs = -(-stations // ((width - own * 8) // KNOTS))
-    out = jax.ShapeDtypeStruct((nz * window, 8, width), jnp.float32)
+    slabs = -(-stations // PACKED)
+    out = jax.ShapeDtypeStruct((window, 8, width), jnp.float32)
     return pl.pallas_call(
         functools.partial(
             main_kernel, groups, stations // groups, own, nx, nz, window),
-        out_shape=[out] * nx + [jax.ShapeDtypeStruct((own, 8, width), jnp.float32)],
+        out_shape=[out] * nz + [jax.ShapeDtypeStruct((own, 8, width), jnp.float32)],
         in_specs=[vmem(), pl.BlockSpec(memory_space=pltpu.SMEM)] + [vmem()] * 3,
-        out_specs=[vmem()] * (nx + 1),
+        out_specs=[vmem()] * (nz + 1),
         scratch_shapes=[
             pltpu.VMEM((sats, 8, width), jnp.float32),
             *[pltpu.VMEM((4 * tracked * 8, epochs), jnp.bfloat16)] * 2,
@@ -406,52 +411,43 @@
     )(*planes, *extras, own_rows, orbit)
 
 
-def combine_kernel(nx, nz, window, *refs):
-    pieces = refs[:nx]
-    smalls = refs[nx : 2 * nx]
-    outs = refs[2 * nx :]
-    small = smalls[0][...]
-    for piece in smalls[1:]:
-        small = small + piece[...]
-    for dz in range(nz):
-        part = pieces[0][dz * window : (dz + 1) * window]
-        for piece in pieces[1:]:
-            part = part + piece[dz * window : (dz + 1) * window]
-        outs[dz][:window] = part
-        outs[dz][window:] = small
-
-
-def combine(pieces, smalls, nz, window):
-    nx = len(pieces)
-    width = pieces[0].shape[2]
-    out = jax.ShapeDtypeStruct((window + 2, 8, width), jnp.float32)
+def add_kernel(*refs):
+    total = refs[0][...]
+    for ref in refs[1:-1]:
+        total = total + ref[...]
+    refs[-1][...] = total
+
+
+def add_smalls(pieces):
     return pl.pallas_call(
-        functools.partial(combine_kernel, nx, nz, window),
-        out_shape=[out] * nz,
-        in_specs=[vmem()] * (2 * nx),
-        out_specs=[vmem()] * nz,
+        add_kernel,
+        out_shape=jax.ShapeDtypeStruct(pieces[0].shape, jnp.float32),
+        in_specs=[vmem()] * len(pieces),
+        out_specs=vmem(),
         compiler_params=pltpu.CompilerParams(vmem_limit_bytes=SMALL_LIMIT),
-        name="combine",
-    )(*pieces, *smalls)
+        name="add_smalls",
+    )(*pieces)
 
 
 def finish_kernel(nz, window, own, columns, sats, factor, cross_factor, *refs):
-    pieces = refs[:nz]
-    normal, right, blocks = refs[nz:]
+    pieces, smalls = refs[:nz], refs[nz : 2 * nz]
+    normal, right, blocks = refs[2 * nz :]
     width = pieces[0].shape[2]
     total = pieces[0][...]
-    for piece in pieces[1:]:
+    small_total = smalls[0][...]
+    for piece, small in zip(pieces[1:], smalls[1:]):
         total = total + piece[...]
+        small_total = small_total + small[...]
     first = lax.axis_index("sat") * own
     start = window_start(lax.axis_index("sta"), columns, sats, window)
     span = own * 8
-    part = total[:window].reshape(window * 8, width)
+    part = total.reshape(window * 8, width)
     row_owner = start + lax.broadcasted_iota(jnp.int32, part.shape, 0) // 8
     lane_owner = first + lax.broadcasted_iota(jnp.int32, part.shape, 1) // 8
     part = jnp.where(row_owner == lane_owner, 0.0, part * cross_factor)
     normal[...] = part.T[:span, :]
-    right[...] = total[window + 1, :1, :span] * factor
-    small = total[window]
+    right[...] = small_total[1, :1, :span] * factor
+    small = small_total[0]
     lane = lax.broadcasted_iota(jnp.int32, (width, own), 0)
     wanted = lax.broadcasted_iota(jnp.int32, (width, own), 1) * 8
     for p in range(8):
@@ -460,7 +456,7 @@
                                      preferred_element_type=jnp.float32)
 
 
-def finish(pieces, window, own, columns, sats, factor, cross_factor):
+def finish(pieces, smalls, window, own, columns, sats, factor, cross_factor):
     nz = len(pieces)
     return pl.pallas_call(
         functools.partial(finish_kernel, nz, window, own, columns, sats, factor, cross_factor),
@@ -469,11 +465,11 @@
             jax.ShapeDtypeStruct((1, own * 8), jnp.float32),
             jax.ShapeDtypeStruct((8, 8, own), jnp.float32),
         ],
-        in_specs=[vmem()] * nz,
+        in_specs=[vmem()] * (2 * nz),
         out_specs=[vmem()] * 3,
         compiler_params=pltpu.CompilerParams(vmem_limit_bytes=SMALL_LIMIT),
         name="finish",
-    )(*pieces)
+    )(*pieces, *smalls)
 
 
 def shift(value, axis, size, step):
@@ -490,19 +486,51 @@
     return pieces
 
 
+def gather_planes(value, size, columns_axis, nx):
+    even = {(0, 0): value}
+    for d in range(2, size, 2):
+        even[0, d] = shift(value, "sat", size, d)
+    for dx in range(1, nx):
+        for d in range(0, size, 2):
+            even[dx, d] = shift(even[0, d], "sta", columns_axis, dx)
+    pieces = []
+    for dx in range(nx):
+        for d in range(0, size, 2):
+            pieces += [even[dx, d], shift(even[dx, d], "sat", size, 1)]
+    return pieces
+
+
 def turn_of(mine, nx):
     return lax.rem(lax.div(mine, nx) + lax.rem(mine, nx), 2)
+
+
+def cut_kernel(nx, orbit, first, second, copy):
+    half = orbit.shape[0] // 2
+    lead = first.shape[0]
+    at = turn_of(lax.axis_index("sta"), nx) * half
+    first[...] = orbit[pl.ds(at, lead)]
+    second[...] = orbit[pl.ds(at + lead, half - lead)]
+    copy[...] = orbit[...]
 
 
 def cut_parts(orbit, columns_axis, nx):
     own = orbit.shape[0]
     if own % 2 or nx % 2 or (columns_axis // nx) % 2:
-        return []
+        return [], orbit
     half = own // 2
     lead = half - half // 2
-    at = turn_of(lax.axis_index("sta"), nx) * half
-    return [lax.dynamic_slice_in_dim(orbit, at, lead, 0),
-            lax.dynamic_slice_in_dim(orbit, at + lead, half - lead, 0)]
+    *parts, orbit = pl.pallas_call(
+        functools.partial(cut_kernel, nx),
+        out_shape=[
+            jax.ShapeDtypeStruct((n,) + orbit.shape[1:], jnp.float32)
+            for n in (lead, half - lead, own)
+        ],
+        in_specs=[vmem()],
+        out_specs=[vmem()] * 3,
+        compiler_params=pltpu.CompilerParams(vmem_limit_bytes=SMALL_LIMIT),
+        name="cut_parts",
+    )(orbit)
+    return parts, orbit
 
 
 def gather_orbit(orbit, parts, size, columns_axis, nx):
@@ -543,12 +571,10 @@
         -(-(((columns * i) % 8) + columns) // 8) for i in range(columns_axis)
     )
 
-    parts = cut_parts(orbit, columns_axis, nx)
+    parts, orbit = cut_parts(orbit, columns_axis, nx)
+    planes, extra = prepare(sight, mapping, residual, counts, track, knots)
+    plane_pieces = gather_planes(planes, group, columns_axis, nx)
     orbit_pieces, places = gather_orbit(orbit, parts, group, columns_axis, nx)
-    if parts:
-        knots, orbit_pieces[1] = lax.optimization_barrier((knots, orbit_pieces[1]))
-    planes, extra = prepare(sight, mapping, residual, counts, track, knots)
-    plane_pieces = gather_pieces(planes, group)
     all_planes, all_track, highs, lows = own_rows_of(plane_pieces, orbit, width)
     *sums, own_rows = accumulate(
         group, all_planes, all_track, highs, lows, place(orbit_pieces, places, sats, nx),
@@ -561,17 +587,19 @@
         held, _ = lax.optimization_barrier((extra_pieces[d], own_rows))
         extra_pieces[d + 1] = shift(held, "sat", group, 1)
     small = own_sums(
-        plane_pieces, [extra_pieces[d] for d in range(group)], own_rows, orbit)
-    arrived = [sums[0]] + [shift(sums[d], "sta", columns_axis, d) for d in range(1, nx)]
+        plane_pieces[:group], [extra_pieces[d] for d in range(group)], own_rows, orbit)
     smalls = [small] + [shift(small, "sta", columns_axis, d) for d in range(1, nx)]
-    chunks = combine(arrived, smalls, nz, window)
-    final = [chunks[0]] + [
-        shift(chunks[d], "sta", columns_axis, d * nx) for d in range(1, nz)
+    final = [sums[0]] + [
+        shift(sums[d], "sta", columns_axis, d * nx) for d in range(1, nz)
+    ]
+    small = add_smalls(smalls)
+    finals = [small] + [
+        shift(small, "sta", columns_axis, d * nx) for d in range(1, nz)
     ]
     total_stations = stations * columns_axis * group
     factor = sats / (total_stations * tracked * epochs)
     cross_factor = sats / (total_stations * epochs) ** 0.5
-    normal, right, blocks = finish(final, window, own, columns, sats, factor, cross_factor)
+    normal, right, blocks = finish(final, finals, window, own, columns, sats, factor, cross_factor)
     if window * 8 != columns:
         mine = lax.axis_index("sta")
         start = window_start(mine, columns, sats, window)

time: 65.8 us -> 73.4 us (1.12)
  starting transfers between devices: 17.2 us -> 23.4 us
  Pallas kernels: 14.4 us -> 19.2 us
  local copies, waits for them, and re-layouts: 3.78 us -> 1.12 us
    ppermute x20 -> x26, starting transfers between devices: 17.2 us -> 23.4 us  [shift(): return lax.ppermute(value, axis, [(i, i ^ step) for i in range(size)])]
    pallas_call x1, Pallas kernels: 4.76 us -> 7.98 us  [accumulate(): pl.pallas_call(functools.partial(main_kernel, groups, stations // groups,...]
    dynamic_slice x2 -> x0, local copies, waits for them, and re-layouts: 1.94 us -> none  [the longest x1 1 us: cut_parts(): lax.dynamic_slice_in_dim(orbit, at + lead, half - lead, 0)]
    pallas_call x1, Pallas kernels: 2.73 us -> 4.24 us  [own_rows_of(): pl.pallas_call(functools.partial(own_rows_kernel, groups, per, own, width...]
    unnamed x8 -> x6, local copies, waits for them, and re-layouts: 1.84 us -> 1.12 us
    ppermute x20 -> x26, waiting for transfers between devices: 29.4 us -> 28.8 us  [shift(): return lax.ppermute(value, axis, [(i, i ^ step) for i in range(size)])]
  transfers between devices with their start and end apart: 20 -> 26, of which waited for: 9 -> 10; matrix products, arithmetic and copies ran while one was open for 3% -> 0% of each run, Pallas kernels for 16% -> 16%
where the time goes in v6:
time: 73.4 us; the launch traced here: 73.2 us
  waiting for transfers between devices  28.8 us (39%)
  starting transfers between devices  23.4 us (32%)
  Pallas kernels  19.2 us (26%)
  local copies, waits for them, and re-layouts  1.12 us (2%)
  between operations  0.74 us (1%)
    ppermute x26, waiting for transfers between devices, shift(): return lax.ppermute(value, axis, [(i, i ^ step) for i in range(size)])  28.8 us
    ppermute x26, starting transfers between devices, shift(): return lax.ppermute(value, axis, [(i, i ^ step) for i in range(size)])  23.4 us
    pallas_call x1, Pallas kernels, accumulate(): pl.pallas_call(functools.partial(main_kernel, groups, stations // groups,...  7.98 us
    pallas_call x1, Pallas kernels, own_rows_of(): pl.pallas_call(functools.partial(own_rows_kernel, groups, per, own, width...  4.24 us
    pallas_call x1, Pallas kernels, own_sums(): pl.pallas_call(functools.partial(blocks_kernel, groups, per, own), out_sh...  3.49 us
    pallas_call x1, Pallas kernels, prepare(): pl.pallas_call(prepare_kernel, out_shape=[jax.ShapeDtypeStruct((stations,...  1.95 us
  transfers between devices with their start and end apart: 26, of which 10 were waited for; matrix products, arithmetic and copies ran while one was open for 0% of the time, Pallas kernels for 16%

profile of v6, /device:TPU:0, one launch (start us, length us, event | category | flops | bytes accessed | tf_op | source)
XLA Modules:
  0.0 73.2 jit_solution(10273626561667224385)
XLA Ops:
  0.6 2.0 %prepare.1 = (f32[2,136,256]{2,1,0:T(8,128)}, f32[2,64,256]{2,1,0:T(8,128)}) custom-call(f32[2,3,32,256]{3,2,1,0:T(8,128)} %refs_0_.1, f32[2,32,256]{2,1,0:T(8,128)} %refs_1_.1, f32[2,32,256]{2,1,0:T(8,128)} %refs_2_.1, s32[2,32,256]{2,1,0:T(8,128)} %refs_3_.1, s32[2,32]{1,0:T(2,128)} %refs_4_.1, s32[2,256]{1,0:T(2,128)} %refs_5_.1), custom_call_target="tpu_custom_call" | custom-call | tf_op jit(solution)/shard_map/prepare/pallas_call | solution.py:77
  2.6 3.0 %collective-permute-start.3 = (f32[2,136,256]{2,1,0:T(8,128)}, f32[2,136,256]{2,1,0:T(8,128)S(1)}, u32[]{:S(2)}, u32[]{:S(2)}) collective-permute-start(f32[2,136,256]{2,1,0:T(8,128)} %get-tuple-element.23.refs_0_), channel_id=1, source_target_pairs={{0,4},{4,0},{8,12},{12,8},{16,20},{20,16},{24,28},{28,24},{1,5},{5... | collective-permute-start | bytes 835592 | tf_op jit(solution)/shard_map/ppermute | solution.py:476
  5.6 0.0 copy-start
  5.6 1.1 %copy-done = f32[30,3,8,256]{3,2,1,0:T(8,128)S(1)} copy-done((f32[30,3,8,256]{3,2,1,0:T(8,128)S(1)}, f32[30,3,8,256]{3,2,1,0:T(8,128)}, u32[]{:S(2)}) %copy-start) | copy-done | bytes 737304
  6.7 0.1 cut_parts.1
  6.8 1.6 %collective-permute-start.7 = (f32[8,3,8,256]{3,2,1,0:T(8,128)S(1)}, f32[8,3,8,256]{3,2,1,0:T(8,128)S(1)}, u32[]{:S(2)}, u32[]{:S(2)}) collective-permute-start(f32[8,3,8,256]{3,2,1,0:T(8,128)S(1)} %get-tuple-element.29), channel_id=1, source_target_pairs={{0,2},{1,3},{2,0},{3,1},{4,6},{5,7},{6,4},{7,5},{8,10},{9,11},{10,... | collective-permute-start | bytes 589832 | tf_op jit(solution)/shard_map/ppermute | solution.py:476
  8.4 0.5 collective-permute-start.1
  8.9 1.5 %collective-permute-start.8 = (f32[7,3,8,256]{3,2,1,0:T(8,128)S(1)}, f32[7,3,8,256]{3,2,1,0:T(8,128)S(1)}, u32[]{:S(2)}, u32[]{:S(2)}) collective-permute-start(f32[7,3,8,256]{3,2,1,0:T(8,128)S(1)} %get-tuple-element.30), channel_id=1, source_target_pairs={{0,2},{1,3},{2,0},{3,1},{4,6},{5,7},{6,4},{7,5},{8,10},{9,11},{10,... | collective-permute-start | bytes 516104 | tf_op jit(solution)/shard_map/ppermute | solution.py:476
  10.4 0.0 collective-permute-start.11
  10.4 4.3 %collective-permute-done.7.refs_1_ = f32[8,3,8,256]{3,2,1,0:T(8,128)S(1)} collective-permute-done((f32[8,3,8,256]{3,2,1,0:T(8,128)S(1)}, f32[8,3,8,256]{3,2,1,0:T(8,128)S(1)}, u32[]{:S(2)}, u32[]{:S(2)}) %collective-permute-start.7) | collective-permute-done | bytes 196640 | tf_op jit(solution)/shard_map/ppermute | solution.py:476
  14.7 1.6 %collective-permute-start.9 = (f32[8,3,8,256]{3,2,1,0:T(8,128)S(1)}, f32[8,3,8,256]{3,2,1,0:T(8,128)S(1)}, u32[]{:S(2)}, u32[]{:S(2)}) collective-permute-start(f32[8,3,8,256]{3,2,1,0:T(8,128)S(1)} %collective-permute-done.7.refs_1_), channel_id=1, source_target_pairs={{0,8},{4,12},{8,0},{12,4},{16,24},{20,28},{24,16},{28,20},{1,9},{5... | collective-permute-start | bytes 589832 | tf_op jit(solution)/shard_map/ppermute | solution.py:476
  16.3 6.6 %collective-permute-done.8.refs_2_ = f32[7,3,8,256]{3,2,1,0:T(8,128)S(1)} collective-permute-done((f32[7,3,8,256]{3,2,1,0:T(8,128)S(1)}, f32[7,3,8,256]{3,2,1,0:T(8,128)S(1)}, u32[]{:S(2)}, u32[]{:S(2)}) %collective-permute-start.8) | collective-permute-done | bytes 172064 | tf_op jit(solution)/shard_map/ppermute | solution.py:476
  22.9 0.0 collective-permute-start.13
  22.9 0.0 collective-permute-done.3.refs_4_
  22.9 0.3 collective-permute-start.10
  23.2 0.0 collective-permute-done.1.refs_2_
  23.2 1.7 %collective-permute-start.5 = (f32[2,136,256]{2,1,0:T(8,128)S(1)}, f32[2,136,256]{2,1,0:T(8,128)S(1)}, u32[]{:S(2)}, u32[]{:S(2)}) collective-permute-start(f32[2,136,256]{2,1,0:T(8,128)S(1)} %collective-permute-done.1.refs_2_), channel_id=1, source_target_pairs={{0,4},{4,0},{8,12},{12,8},{16,20},{20,16},{24,28},{28,24},{1,5},{5... | collective-permute-start | bytes 835592 | tf_op jit(solution)/shard_map/ppermute | solution.py:476
  24.9 0.0 collective-permute-done.13.refs_7_
  24.9 0.0 collective-permute-start.12
  24.9 0.0 collective-permute-done.9.refs_3_
  24.9 0.5 collective-permute-start.14
  25.4 4.6 %collective-permute-done.10.refs_4_ = f32[7,3,8,256]{3,2,1,0:T(8,128)S(1)} collective-permute-done((f32[7,3,8,256]{3,2,1,0:T(8,128)S(1)}, f32[7,3,8,256]{3,2,1,0:T(8,128)S(1)}, u32[]{:S(2)}, u32[]{:S(2)}) %collective-permute-start.10) | collective-permute-done | bytes 172064 | tf_op jit(solution)/shard_map/ppermute | solution.py:476
  30.1 0.0 collective-permute-start.15
  30.1 0.0 collective-permute-done.12.refs_6_
  30.1 0.5 collective-permute-start
  30.6 1.1 %collective-permute-done.15.refs_9_ = f32[7,3,8,256]{3,2,1,0:T(8,128)S(1)} collective-permute-done((f32[7,3,8,256]{3,2,1,0:T(8,128)S(1)}, f32[7,3,8,256]{3,2,1,0:T(8,128)S(1)}, u32[]{:S(2)}, u32[]{:S(2)}) %collective-permute-start.15) | collective-permute-done | bytes 172064 | tf_op jit(solution)/shard_map/ppermute | solution.py:476
  31.6 0.1 collective-permute-start.2
  31.8 3.9 %collective-permute-done.5.refs_6_ = f32[2,136,256]{2,1,0:T(8,128)S(1)} collective-permute-done((f32[2,136,256]{2,1,0:T(8,128)S(1)}, f32[2,136,256]{2,1,0:T(8,128)S(1)}, u32[]{:S(2)}, u32[]{:S(2)}) %collective-permute-start.5) | collective-permute-done | bytes 278560 | tf_op jit(solution)/shard_map/ppermute | solution.py:476
  35.6 0.0 collective-permute-start.4
  35.6 0.0 collective-permute-done.14.refs_8_
  35.6 0.5 collective-permute-start.6
  36.2 0.0 collective-permute-done.11.refs_5_
  36.2 0.2 place.1.refs_4_
  36.4 0.0 copy-start.2
  36.4 0.0 collective-permute-done.refs_1_
  36.4 0.8 %collective-permute-done.4.refs_5_ = f32[2,136,256]{2,1,0:T(8,128)S(1)} collective-permute-done((f32[2,136,256]{2,1,0:T(8,128)S(1)}, f32[2,136,256]{2,1,0:T(8,128)S(1)}, u32[]{:S(2)}, u32[]{:S(2)}) %collective-permute-start.4) | collective-permute-done | bytes 278560 | tf_op jit(solution)/shard_map/ppermute | solution.py:476
  37.2 0.0 collective-permute-done.2.refs_3_
  37.2 0.4 collective-permute-done.6.refs_7_
  37.6 0.0 copy-done.1
  37.6 4.2 %own_rows.1 = (f32[16,136,256]{2,1,0:T(8,128)S(1)}, s32[16,128]{1,0:T(8,128)S(1)}, bf16[16,256,256]{2,1,0:T(8,128)(2,1)S(1)}, bf16[16,256,256]{2,1,0:T(8,128)(2,1)S(1)}) custom-call(f32[2,136,256]{2,1,0:T(8,128)S(1)} %copy-done.1, f32[2,136,256]{2,1,0:T(8,128)S(1)} %collective-permute-done.refs_1_, f32[2,136,256]{2,1,0:T(8,128)S(1)} %collective-permute-done.1.refs_2_, ...), custom_call_target="tpu_custom_call" | custom-call | flops 8000000000 | bytes 8000000 | tf_op jit(solution)/shard_map/own_rows/pallas_call | solution.py:169
  41.8 0.0 copy-done.2
  41.9 1.6 %collective-permute-start.20 = (f32[2,64,256]{2,1,0:T(8,128)S(1)}, f32[2,64,256]{2,1,0:T(8,128)S(1)}, u32[]{:S(2)}, u32[]{:S(2)}) collective-permute-start(f32[2,64,256]{2,1,0:T(8,128)S(1)} %copy-done.2), channel_id=1, source_target_pairs={{0,2},{1,3},{2,0},{3,1},{4,6},{5,7},{6,4},{7,5},{8,10},{9,11},{10,... | collective-permute-start | bytes 393224 | tf_op jit(solution)/shard_map/ppermute | solution.py:476
  43.4 8.0 %accumulate.1 = (f32[15,8,256]{2,1,0:T(8,128)S(1)}, f32[15,8,256]{2,1,0:T(8,128)S(1)}, f32[15,8,256]{2,1,0:T(8,128)S(1)}, f32[15,8,256]{2,1,0:T(8,128)S(1)}, f32[30,8,256]{2,1,0:T(8,128)S(1)}) custom-call(f32[16,136,256]{2,1,0:T(8,128)S(1)} %get-tuple-element.25.refs_0_, s32[16,128]{1,0:T(8,128)S(1)} %get-tuple-element.26.refs_1_, ...), custom_call_target="tpu_custom_call" | custom-call | flops 8000000000 | bytes 8000000 | tf_op jit(solution)/shard_map/accumulate/pallas_call | solution.py:329
  51.4 0.1 collective-permute-start.19
  51.5 0.0 collective-permute-done.20.refs_6_
  51.5 0.5 collective-permute-start.21
  52.0 1.6 %collective-permute-start.16 = (f32[15,8,256]{2,1,0:T(8,128)S(1)}, f32[15,8,256]{2,1,0:T(8,128)S(1)}, u32[]{:S(2)}, u32[]{:S(2)}) collective-permute-start(f32[15,8,256]{2,1,0:T(8,128)S(1)} %get-tuple-element.32), channel_id=1, source_target_pairs={{0,8},{4,12},{8,0},{12,4},{16,24},{20,28},{24,16},{28,20},{1,9},{5... | collective-permute-start | bytes 368648 | tf_op jit(solution)/shard_map/ppermute | solution.py:476
  53.6 2.6 %collective-permute-start.17 = (f32[15,8,256]{2,1,0:T(8,128)S(1)}, f32[15,8,256]{2,1,0:T(8,128)S(1)}, u32[]{:S(2)}, u32[]{:S(2)}) collective-permute-start(f32[15,8,256]{2,1,0:T(8,128)S(1)} %get-tuple-element.33), channel_id=1, source_target_pairs={{0,16},{4,20},{8,24},{12,28},{16,0},{20,4},{24,8},{28,12},{1,17},{... | collective-permute-start | bytes 368648 | tf_op jit(solution)/shard_map/ppermute | solution.py:476
  56.2 0.2 collective-permute-start.18
  56.4 0.0 collective-permute-done.19.refs_5_
  56.4 0.0 collective-permute-done.21.refs_7_
  56.4 3.5 %own_sums.1.refs_0_ = f32[2,8,256]{2,1,0:T(8,128)S(1)} custom-call(f32[2,136,256]{2,1,0:T(8,128)S(1)} %copy-done.1, f32[2,136,256]{2,1,0:T(8,128)S(1)} %collective-permute-done.refs_1_, f32[2,136,256]{2,1,0:T(8,128)S(1)} %collective-permute-done.1.refs_2_, f32[2,136,256]{2,1,0:T(8,128)S(1)} %collective-permute-done.2.refs_3_, f32[2,64,256]{2,1,0:T(8,128)S(1)} %copy-done.2, ...), custom_call_target="tpu_custom_call" | custom-call | flops 4000000000 | bytes 4000000 | tf_op jit(solution)/shard_map/own_sums/pallas_call | solution.py:402
  59.9 0.6 collective-permute-start.22
  60.5 3.2 %collective-permute-done.22.refs_1_ = f32[2,8,256]{2,1,0:T(8,128)S(1)} collective-permute-done((f32[2,8,256]{2,1,0:T(8,128)S(1)}, f32[2,8,256]{2,1,0:T(8,128)S(1)}, u32[]{:S(2)}, u32[]{:S(2)}) %collective-permute-start.22) | collective-permute-done | bytes 16416 | tf_op jit(solution)/shard_map/ppermute | solution.py:476
  63.7 3.6 %collective-permute-start.25 = (f32[2,8,256]{2,1,0:T(8,128)S(1)}, f32[2,8,256]{2,1,0:T(8,128)S(1)}, u32[]{:S(2)}, u32[]{:S(2)}) collective-permute-start(f32[2,8,256]{2,1,0:T(8,128)S(1)} %add_smalls.1.refs_4_), channel_id=1, source_target_pairs={{0,24},{4,28},{8,16},{12,20},{16,8},{20,12},{24,0},{28,4},{1,25},{... | collective-permute-start | bytes 49160 | tf_op jit(solution)/shard_map/ppermute | solution.py:476
  67.3 0.0 collective-permute-start.24
  67.3 0.0 collective-permute-done.16.refs_1_
  67.3 0.8 %collective-permute-start.23 = (f32[2,8,256]{2,1,0:T(8,128)S(1)}, f32[2,8,256]{2,1,0:T(8,128)S(1)}, u32[]{:S(2)}, u32[]{:S(2)}) collective-permute-start(f32[2,8,256]{2,1,0:T(8,128)S(1)} %add_smalls.1.refs_4_), channel_id=1, source_target_pairs={{0,8},{4,12},{8,0},{12,4},{16,24},{20,28},{24,16},{28,20},{1,9},{5... | collective-permute-start | bytes 49160 | tf_op jit(solution)/shard_map/ppermute | solution.py:476
  68.1 0.0 collective-permute-done.17.refs_2_
  68.1 0.0 collective-permute-done.18.refs_3_
  68.1 1.2 %collective-permute-done.25.refs_7_ = f32[2,8,256]{2,1,0:T(8,128)S(1)} collective-permute-done((f32[2,8,256]{2,1,0:T(8,128)S(1)}, f32[2,8,256]{2,1,0:T(8,128)S(1)}, u32[]{:S(2)}, u32[]{:S(2)}) %collective-permute-start.25) | collective-permute-done | bytes 16416 | tf_op jit(solution)/shard_map/ppermute | solution.py:476
  69.3 2.7 %collective-permute-done.24.refs_6_ = f32[2,8,256]{2,1,0:T(8,128)S(1)} collective-permute-done((f32[2,8,256]{2,1,0:T(8,128)S(1)}, f32[2,8,256]{2,1,0:T(8,128)S(1)}, u32[]{:S(2)}, u32[]{:S(2)}) %collective-permute-start.24) | collective-permute-done | bytes 16416 | tf_op jit(solution)/shard_map/ppermute | solution.py:476
  72.0 0.0 collective-permute-done.23.refs_5_
  72.0 1.2 %finish.1 = (f32[240,120]{1,0:T(8,128)}, f32[1,240]{1,0:T(1,128)}, f32[8,8,30]{2,1,0:T(8,128)}) custom-call(f32[15,8,256]{2,1,0:T(8,128)S(1)} %get-tuple-element.31.refs_0_, f32[15,8,256]{2,1,0:T(8,128)S(1)} %collective-permute-done.16.refs_1_, f32[15,8,256]{2,1,0:T(8,128)S(1)} %collective-permute-done.17.refs_2_, ...), custom_call_target="tpu_custom_call" | custom-call | tf_op jit(solution)/shard_map/finish/pallas_call | solution.py:461
  (2 shorter events, 0.0 us)
Async XLA Ops:
  2.6 20.3 %collective-permute-start.3 = (f32[2,136,256]{2,1,0:T(8,128)}, f32[2,136,256]{2,1,0:T(8,128)S(1)}, u32[]{:S(2)}, u32[]{:S(2)}) collective-permute-start(f32[2,136,256]{2,1,0:T(8,128)} %get-tuple-element.23.refs_0_), channel_id=1, source_target_pairs={{0,4},{4,0},{8,12},{12,8},{16,20},{20,16},{24,28},{28,24},{1,5},{5... | collective-permute-start | bytes 835592 | tf_op jit(solution)/shard_map/ppermute | solution.py:476
  5.6 1.1 %copy-start = (f32[30,3,8,256]{3,2,1,0:T(8,128)S(1)}, f32[30,3,8,256]{3,2,1,0:T(8,128)}, u32[]{:S(2)}) copy-start(f32[30,3,8,256]{3,2,1,0:T(8,128)} %orbit.1) | copy-start | bytes 2211844
  6.8 7.9 %collective-permute-start.7 = (f32[8,3,8,256]{3,2,1,0:T(8,128)S(1)}, f32[8,3,8,256]{3,2,1,0:T(8,128)S(1)}, u32[]{:S(2)}, u32[]{:S(2)}) collective-permute-start(f32[8,3,8,256]{3,2,1,0:T(8,128)S(1)} %get-tuple-element.29), channel_id=1, source_target_pairs={{0,2},{1,3},{2,0},{3,1},{4,6},{5,7},{6,4},{7,5},{8,10},{9,11},{10,... | collective-permute-start | bytes 589832 | tf_op jit(solution)/shard_map/ppermute | solution.py:476
  8.4 14.8 %collective-permute-start.1 = (f32[2,136,256]{2,1,0:T(8,128)}, f32[2,136,256]{2,1,0:T(8,128)S(1)}, u32[]{:S(2)}, u32[]{:S(2)}) collective-permute-start(f32[2,136,256]{2,1,0:T(8,128)} %get-tuple-element.23.refs_0_), channel_id=1, source_target_pairs={{0,2},{1,3},{2,0},{3,1},{4,6},{5,7},{6,4},{7,5},{8,10},{9,11},{10,... | collective-permute-start | bytes 835592 | tf_op jit(solution)/shard_map/ppermute | solution.py:476
  8.9 14.0 %collective-permute-start.8 = (f32[7,3,8,256]{3,2,1,0:T(8,128)S(1)}, f32[7,3,8,256]{3,2,1,0:T(8,128)S(1)}, u32[]{:S(2)}, u32[]{:S(2)}) collective-permute-start(f32[7,3,8,256]{3,2,1,0:T(8,128)S(1)} %get-tuple-element.30), channel_id=1, source_target_pairs={{0,2},{1,3},{2,0},{3,1},{4,6},{5,7},{6,4},{7,5},{8,10},{9,11},{10,... | collective-permute-start | bytes 516104 | tf_op jit(solution)/shard_map/ppermute | solution.py:476
  10.4 27.2 %copy-start.1 = (f32[2,136,256]{2,1,0:T(8,128)S(1)}, f32[2,136,256]{2,1,0:T(8,128)}, u32[]{:S(2)}) copy-start(f32[2,136,256]{2,1,0:T(8,128)} %get-tuple-element.23.refs_0_) | copy-start | bytes 835588
  10.4 25.7 %collective-permute-start.11 = (f32[30,3,8,256]{3,2,1,0:T(8,128)S(1)}, f32[30,3,8,256]{3,2,1,0:T(8,128)S(1)}, u32[]{:S(2)}, u32[]{:S(2)}) collective-permute-start(f32[30,3,8,256]{3,2,1,0:T(8,128)S(1)} %get-tuple-element.24.refs_8_.refs_0_.refs_9_), channel_id=1, source_target_pairs={{0,1},{1,0},{2,3},{3,2},{4,5},{5,4},{6,7},{7,6},{8,9},{9,8},{10,11... | collective-permute-start | bytes 2211848 | tf_op jit(solution)/shard_map/ppermute | solution.py:476
  14.7 10.2 %collective-permute-start.9 = (f32[8,3,8,256]{3,2,1,0:T(8,128)S(1)}, f32[8,3,8,256]{3,2,1,0:T(8,128)S(1)}, u32[]{:S(2)}, u32[]{:S(2)}) collective-permute-start(f32[8,3,8,256]{3,2,1,0:T(8,128)S(1)} %collective-permute-done.7.refs_1_), channel_id=1, source_target_pairs={{0,8},{4,12},{8,0},{12,4},{16,24},{20,28},{24,16},{28,20},{1,9},{5... | collective-permute-start | bytes 589832 | tf_op jit(solution)/shard_map/ppermute | solution.py:476
  22.9 2.0 %collective-permute-start.13 = (f32[7,3,8,256]{3,2,1,0:T(8,128)S(1)}, f32[7,3,8,256]{3,2,1,0:T(8,128)S(1)}, u32[]{:S(2)}, u32[]{:S(2)}) collective-permute-start(f32[7,3,8,256]{3,2,1,0:T(8,128)S(1)} %collective-permute-done.8.refs_2_), channel_id=1, source_target_pairs={{0,1},{1,0},{2,3},{3,2},{4,5},{5,4},{6,7},{7,6},{8,9},{9,8},{10,11... | collective-permute-start | bytes 516104 | tf_op jit(solution)/shard_map/ppermute | solution.py:476
  22.9 7.2 %collective-permute-start.10 = (f32[7,3,8,256]{3,2,1,0:T(8,128)S(1)}, f32[7,3,8,256]{3,2,1,0:T(8,128)S(1)}, u32[]{:S(2)}, u32[]{:S(2)}) collective-permute-start(f32[7,3,8,256]{3,2,1,0:T(8,128)S(1)} %collective-permute-done.8.refs_2_), channel_id=1, source_target_pairs={{0,4},{4,0},{8,12},{12,8},{16,20},{20,16},{24,28},{28,24},{1,5},{5... | collective-permute-start | bytes 516104 | tf_op jit(solution)/shard_map/ppermute | solution.py:476
  23.2 12.4 %collective-permute-start.5 = (f32[2,136,256]{2,1,0:T(8,128)S(1)}, f32[2,136,256]{2,1,0:T(8,128)S(1)}, u32[]{:S(2)}, u32[]{:S(2)}) collective-permute-start(f32[2,136,256]{2,1,0:T(8,128)S(1)} %collective-permute-done.1.refs_2_), channel_id=1, source_target_pairs={{0,4},{4,0},{8,12},{12,8},{16,20},{20,16},{24,28},{28,24},{1,5},{5... | collective-permute-start | bytes 835592 | tf_op jit(solution)/shard_map/ppermute | solution.py:476
  24.9 5.1 %collective-permute-start.12 = (f32[8,3,8,256]{3,2,1,0:T(8,128)S(1)}, f32[8,3,8,256]{3,2,1,0:T(8,128)S(1)}, u32[]{:S(2)}, u32[]{:S(2)}) collective-permute-start(f32[8,3,8,256]{3,2,1,0:T(8,128)S(1)} %collective-permute-done.7.refs_1_), channel_id=1, source_target_pairs={{0,1},{1,0},{2,3},{3,2},{4,5},{5,4},{6,7},{7,6},{8,9},{9,8},{10,11... | collective-permute-start | bytes 589832 | tf_op jit(solution)/shard_map/ppermute | solution.py:476
  24.9 10.7 %collective-permute-start.14 = (f32[8,3,8,256]{3,2,1,0:T(8,128)S(1)}, f32[8,3,8,256]{3,2,1,0:T(8,128)S(1)}, u32[]{:S(2)}, u32[]{:S(2)}) collective-permute-start(f32[8,3,8,256]{3,2,1,0:T(8,128)S(1)} %collective-permute-done.9.refs_3_), channel_id=1, source_target_pairs={{0,1},{1,0},{2,3},{3,2},{4,5},{5,4},{6,7},{7,6},{8,9},{9,8},{10,11... | collective-permute-start | bytes 589832 | tf_op jit(solution)/shard_map/ppermute | solution.py:476
  30.1 1.6 %collective-permute-start.15 = (f32[7,3,8,256]{3,2,1,0:T(8,128)S(1)}, f32[7,3,8,256]{3,2,1,0:T(8,128)S(1)}, u32[]{:S(2)}, u32[]{:S(2)}) collective-permute-start(f32[7,3,8,256]{3,2,1,0:T(8,128)S(1)} %collective-permute-done.10.refs_4_), channel_id=1, source_target_pairs={{0,1},{1,0},{2,3},{3,2},{4,5},{5,4},{6,7},{7,6},{8,9},{9,8},{10,11... | collective-permute-start | bytes 516104 | tf_op jit(solution)/shard_map/ppermute | solution.py:476
  30.1 6.3 %collective-permute-start = (f32[2,136,256]{2,1,0:T(8,128)}, f32[2,136,256]{2,1,0:T(8,128)S(1)}, u32[]{:S(2)}, u32[]{:S(2)}) collective-permute-start(f32[2,136,256]{2,1,0:T(8,128)} %get-tuple-element.23.refs_0_), channel_id=1, source_target_pairs={{0,1},{1,0},{2,3},{3,2},{4,5},{5,4},{6,7},{7,6},{8,9},{9,8},{10,11... | collective-permute-start | bytes 835592 | tf_op jit(solution)/shard_map/ppermute | solution.py:476
  31.6 5.6 %collective-permute-start.2 = (f32[2,136,256]{2,1,0:T(8,128)S(1)}, f32[2,136,256]{2,1,0:T(8,128)S(1)}, u32[]{:S(2)}, u32[]{:S(2)}) collective-permute-start(f32[2,136,256]{2,1,0:T(8,128)S(1)} %collective-permute-done.1.refs_2_), channel_id=1, source_target_pairs={{0,1},{1,0},{2,3},{3,2},{4,5},{5,4},{6,7},{7,6},{8,9},{9,8},{10,11... | collective-permute-start | bytes 835592 | tf_op jit(solution)/shard_map/ppermute | solution.py:476
  35.6 1.6 %collective-permute-start.4 = (f32[2,136,256]{2,1,0:T(8,128)S(1)}, f32[2,136,256]{2,1,0:T(8,128)S(1)}, u32[]{:S(2)}, u32[]{:S(2)}) collective-permute-start(f32[2,136,256]{2,1,0:T(8,128)S(1)} %collective-permute-done.3.refs_4_), channel_id=1, source_target_pairs={{0,1},{1,0},{2,3},{3,2},{4,5},{5,4},{6,7},{7,6},{8,9},{9,8},{10,11... | collective-permute-start | bytes 835592 | tf_op jit(solution)/shard_map/ppermute | solution.py:476
  35.6 2.0 %collective-permute-start.6 = (f32[2,136,256]{2,1,0:T(8,128)S(1)}, f32[2,136,256]{2,1,0:T(8,128)S(1)}, u32[]{:S(2)}, u32[]{:S(2)}) collective-permute-start(f32[2,136,256]{2,1,0:T(8,128)S(1)} %collective-permute-done.5.refs_6_), channel_id=1, source_target_pairs={{0,1},{1,0},{2,3},{3,2},{4,5},{5,4},{6,7},{7,6},{8,9},{9,8},{10,11... | collective-permute-start | bytes 835592 | tf_op jit(solution)/shard_map/ppermute | solution.py:476
  36.4 5.5 %copy-start.2 = (f32[2,64,256]{2,1,0:T(8,128)S(1)}, f32[2,64,256]{2,1,0:T(8,128)}, u32[]{:S(2)}) copy-start(f32[2,64,256]{2,1,0:T(8,128)} %get-tuple-element.38.refs_4_) | copy-start | bytes 393220
  41.9 9.6 %collective-permute-start.20 = (f32[2,64,256]{2,1,0:T(8,128)S(1)}, f32[2,64,256]{2,1,0:T(8,128)S(1)}, u32[]{:S(2)}, u32[]{:S(2)}) collective-permute-start(f32[2,64,256]{2,1,0:T(8,128)S(1)} %copy-done.2), channel_id=1, source_target_pairs={{0,2},{1,3},{2,0},{3,1},{4,6},{5,7},{6,4},{7,5},{8,10},{9,11},{10,... | collective-permute-start | bytes 393224 | tf_op jit(solution)/shard_map/ppermute | solution.py:476
  51.4 5.0 %collective-permute-start.19 = (f32[2,64,256]{2,1,0:T(8,128)S(1)}, f32[2,64,256]{2,1,0:T(8,128)S(1)}, u32[]{:S(2)}, u32[]{:S(2)}) collective-permute-start(f32[2,64,256]{2,1,0:T(8,128)S(1)} %copy-done.2), channel_id=1, source_target_pairs={{0,1},{1,0},{2,3},{3,2},{4,5},{5,4},{6,7},{7,6},{8,9},{9,8},{10,11... | collective-permute-start | bytes 393224 | tf_op jit(solution)/shard_map/ppermute | solution.py:476
  51.5 4.9 %collective-permute-start.21 = (f32[2,64,256]{2,1,0:T(8,128)S(1)}, f32[2,64,256]{2,1,0:T(8,128)S(1)}, u32[]{:S(2)}, u32[]{:S(2)}) collective-permute-start(f32[2,64,256]{2,1,0:T(8,128)S(1)} %collective-permute-done.20.refs_6_), channel_id=1, source_target_pairs={{0,1},{1,0},{2,3},{3,2},{4,5},{5,4},{6,7},{7,6},{8,9},{9,8},{10,11... | collective-permute-start | bytes 393224 | tf_op jit(solution)/shard_map/ppermute | solution.py:476
  52.0 15.3 %collective-permute-start.16 = (f32[15,8,256]{2,1,0:T(8,128)S(1)}, f32[15,8,256]{2,1,0:T(8,128)S(1)}, u32[]{:S(2)}, u32[]{:S(2)}) collective-permute-start(f32[15,8,256]{2,1,0:T(8,128)S(1)} %get-tuple-element.32), channel_id=1, source_target_pairs={{0,8},{4,12},{8,0},{12,4},{16,24},{20,28},{24,16},{28,20},{1,9},{5... | collective-permute-start | bytes 368648 | tf_op jit(solution)/shard_map/ppermute | solution.py:476
  53.6 14.5 %collective-permute-start.17 = (f32[15,8,256]{2,1,0:T(8,128)S(1)}, f32[15,8,256]{2,1,0:T(8,128)S(1)}, u32[]{:S(2)}, u32[]{:S(2)}) collective-permute-start(f32[15,8,256]{2,1,0:T(8,128)S(1)} %get-tuple-element.33), channel_id=1, source_target_pairs={{0,16},{4,20},{8,24},{12,28},{16,0},{20,4},{24,8},{28,12},{1,17},{... | collective-permute-start | bytes 368648 | tf_op jit(solution)/shard_map/ppermute | solution.py:476
  56.2 11.9 %collective-permute-start.18 = (f32[15,8,256]{2,1,0:T(8,128)S(1)}, f32[15,8,256]{2,1,0:T(8,128)S(1)}, u32[]{:S(2)}, u32[]{:S(2)}) collective-permute-start(f32[15,8,256]{2,1,0:T(8,128)S(1)} %get-tuple-element.34), channel_id=1, source_target_pairs={{0,24},{4,28},{8,16},{12,20},{16,8},{20,12},{24,0},{28,4},{1,25},{... | collective-permute-start | bytes 368648 | tf_op jit(solution)/shard_map/ppermute | solution.py:476
  59.9 3.8 %collective-permute-start.22 = (f32[2,8,256]{2,1,0:T(8,128)S(1)}, f32[2,8,256]{2,1,0:T(8,128)S(1)}, u32[]{:S(2)}, u32[]{:S(2)}) collective-permute-start(f32[2,8,256]{2,1,0:T(8,128)S(1)} %own_sums.1.refs_0_), channel_id=1, source_target_pairs={{0,4},{4,0},{8,12},{12,8},{16,20},{20,16},{24,28},{28,24},{1,5},{5... | collective-permute-start | bytes 49160 | tf_op jit(solution)/shard_map/ppermute | solution.py:476
  63.7 5.6 %collective-permute-start.25 = (f32[2,8,256]{2,1,0:T(8,128)S(1)}, f32[2,8,256]{2,1,0:T(8,128)S(1)}, u32[]{:S(2)}, u32[]{:S(2)}) collective-permute-start(f32[2,8,256]{2,1,0:T(8,128)S(1)} %add_smalls.1.refs_4_), channel_id=1, source_target_pairs={{0,24},{4,28},{8,16},{12,20},{16,8},{20,12},{24,0},{28,4},{1,25},{... | collective-permute-start | bytes 49160 | tf_op jit(solution)/shard_map/ppermute | solution.py:476
  67.3 4.6 %collective-permute-start.24 = (f32[2,8,256]{2,1,0:T(8,128)S(1)}, f32[2,8,256]{2,1,0:T(8,128)S(1)}, u32[]{:S(2)}, u32[]{:S(2)}) collective-permute-start(f32[2,8,256]{2,1,0:T(8,128)S(1)} %add_smalls.1.refs_4_), channel_id=1, source_target_pairs={{0,16},{4,20},{8,24},{12,28},{16,0},{20,4},{24,8},{28,12},{1,17},{... | collective-permute-start | bytes 49160 | tf_op jit(solution)/shard_map/ppermute | solution.py:476
  67.3 4.6 %collective-permute-start.23 = (f32[2,8,256]{2,1,0:T(8,128)S(1)}, f32[2,8,256]{2,1,0:T(8,128)S(1)}, u32[]{:S(2)}, u32[]{:S(2)}) collective-permute-start(f32[2,8,256]{2,1,0:T(8,128)S(1)} %add_smalls.1.refs_4_), channel_id=1, source_target_pairs={{0,8},{4,12},{8,0},{12,4},{16,24},{20,28},{24,16},{28,20},{1,9},{5... | collective-permute-start | bytes 49160 | tf_op jit(solution)/shard_map/ppermute | solution.py:476

commit v7 on v6

--- a/solution.py
+++ b/solution.py
@@ -10,6 +10,7 @@
 KNOTS = 4
 PRIOR = 1.0
 PACKED = 128 // KNOTS
+HIGH = lax.Precision.HIGH
 HIGHEST = lax.Precision.HIGHEST
 SMALL_LIMIT = 8 * 1024 * 1024
 MEDIUM_LIMIT = 40 * 1024 * 1024
@@ -356,19 +357,24 @@
     first = lax.axis_index("sat") * own
     satellite = first + lax.broadcasted_iota(jnp.int32, (own, tracked), 0)
     pairs = [(0, 0), (0, 1), (0, 2), (1, 1), (1, 2), (2, 2)]
-    sums = [jnp.zeros((own, epochs), jnp.float32) for _ in range(9)]
+    picks, stacks = [], [[] for _ in range(9)]
     for d in range(groups):
         for s in range(per):
             named = plane_pieces[d][s, 4 * tracked + 1 : 4 * tracked + 2, :tracked]
-            pick = (satellite == named.astype(jnp.int32)).astype(jnp.float32)
+            picks.append((satellite == named.astype(jnp.int32)).astype(jnp.float32))
             a = [plane_pieces[d][s, c * tracked : (c + 1) * tracked, :] for c in range(3)]
             residual = extra_pieces[d][s, :tracked, :]
             inverse = extra_pieces[d][s, tracked:, :]
             weighted = [v * inverse for v in a]
             terms = [weighted[c] * a[e] for c, e in pairs] + [v * residual for v in a]
-            for n in range(9):
-                sums[n] = sums[n] + jnp.dot(pick, terms[n], precision=HIGHEST,
-                                            preferred_element_type=jnp.float32)
+            for stack, term in zip(stacks, terms):
+                stack.append(term)
+    pick = jnp.concatenate(picks, 1).astype(jnp.bfloat16)
+    sums = []
+    for stack in stacks:
+        high, low = split(jnp.concatenate(stack, 0))
+        sums.append(jnp.dot(pick, high, preferred_element_type=jnp.float32)
+                    + jnp.dot(pick, low, preferred_element_type=jnp.float32))
     index = {}
     for n, (c, e) in enumerate(pairs):
         index[c, e] = index[e, c] = n
@@ -382,9 +388,9 @@
     right_rows = jnp.zeros((own * 8, epochs), jnp.float32)
     for c in range(3):
         mixed = sum(wide[index[c, e]] * parts[e] for e in range(3))
-        blocks = blocks + dot_nt(parts[c], mixed, HIGHEST)
+        blocks = blocks + dot_nt(parts[c], mixed, HIGH)
         right_rows = right_rows + wide[6 + c] * parts[c]
-    right = dot_nt(jnp.ones((8, epochs), jnp.float32), right_rows, HIGHEST)
+    right = dot_nt(jnp.ones((8, epochs), jnp.float32), right_rows, HIGH)
     owner = lax.broadcasted_iota(jnp.int32, (8, own * 8), 1) // 8
     folded = jnp.zeros((8, own * 8), jnp.float32)
     for o in range(own):
@@ -518,7 +524,7 @@
     if own % 2 or nx % 2 or (columns_axis // nx) % 2:
         return [], orbit
     half = own // 2
-    lead = half - half // 2
+    lead = half * 2 // 3
     *parts, orbit = pl.pallas_call(
         functools.partial(cut_kernel, nx),
         out_shape=[
@@ -538,7 +544,7 @@
     if not parts:
         return gather_pieces(orbit, size), tuple((d, -1, 0, own) for d in range(size))
     half = own // 2
-    lead = half - half // 2
+    lead = half * 2 // 3
     first, second = parts
     pieces, places = [orbit], [(0, -1, 0, own)]
     for d in range(2, size, 2):
@@ -574,20 +580,17 @@
     parts, orbit = cut_parts(orbit, columns_axis, nx)
     planes, extra = prepare(sight, mapping, residual, counts, track, knots)
     plane_pieces = gather_planes(planes, group, columns_axis, nx)
+    if parts:
+        *parts, plane_pieces[2] = lax.optimization_barrier((*parts, plane_pieces[2]))
     orbit_pieces, places = gather_orbit(orbit, parts, group, columns_axis, nx)
+    if parts:
+        extra, orbit_pieces[2] = lax.optimization_barrier((extra, orbit_pieces[2]))
+    extra_pieces = gather_pieces(extra, group)
     all_planes, all_track, highs, lows = own_rows_of(plane_pieces, orbit, width)
     *sums, own_rows = accumulate(
         group, all_planes, all_track, highs, lows, place(orbit_pieces, places, sats, nx),
         nx, nz, window)
-    extra, _ = lax.optimization_barrier((extra, all_track))
-    extra_pieces = {0: extra}
-    for d in range(2, group, 2):
-        extra_pieces[d] = shift(extra, "sat", group, d)
-    for d in range(0, group, 2):
-        held, _ = lax.optimization_barrier((extra_pieces[d], own_rows))
-        extra_pieces[d + 1] = shift(held, "sat", group, 1)
-    small = own_sums(
-        plane_pieces[:group], [extra_pieces[d] for d in range(group)], own_rows, orbit)
+    small = own_sums(plane_pieces[:group], extra_pieces, own_rows, orbit)
     smalls = [small] + [shift(small, "sta", columns_axis, d) for d in range(1, nx)]
     final = [sums[0]] + [
         shift(sums[d], "sta", columns_axis, d * nx) for d in range(1, nz)

time: 73.4 us -> 67.7 us (0.922)
  waiting for transfers between devices: 28.8 us -> 21.7 us
  starting transfers between devices: 23.4 us -> 26.3 us
  Pallas kernels: 19.2 us -> 16.7 us
  local copies, waits for them, and re-layouts: 1.12 us -> 2.08 us
    ppermute x26, waiting for transfers between devices: 28.8 us -> 21.7 us  [shift(): return lax.ppermute(value, axis, [(i, i ^ step) for i in range(size)])]
    ppermute x26, starting transfers between devices: 23.4 us -> 26.3 us  [shift(): return lax.ppermute(value, axis, [(i, i ^ step) for i in range(size)])]
    pallas_call x1, Pallas kernels: 3.49 us -> 1.37 us  [own_sums(): pl.pallas_call(functools.partial(blocks_kernel, groups, per, own), out_sh...]
    unnamed x6 -> x8, local copies, waits for them, and re-layouts: 1.12 us -> 2.08 us
  transfers between devices with their start and end apart: 26 -> 26, of which waited for: 10 -> 7; matrix products, arithmetic and copies ran while one was open for 0% -> 0% of each run, Pallas kernels for 16% -> 20%
where the time goes in v7:
time: 67.7 us; the launch traced here: 67.5 us
  starting transfers between devices  26.3 us (39%)
  waiting for transfers between devices  21.7 us (32%)
  Pallas kernels  16.7 us (25%)
  local copies, waits for them, and re-layouts  2.08 us (3%)
  between operations  0.74 us (1%)
    ppermute x26, starting transfers between devices, shift(): return lax.ppermute(value, axis, [(i, i ^ step) for i in range(size)])  26.3 us
    ppermute x26, waiting for transfers between devices, shift(): return lax.ppermute(value, axis, [(i, i ^ step) for i in range(size)])  21.7 us
    pallas_call x1, Pallas kernels, accumulate(): pl.pallas_call(functools.partial(main_kernel, groups, stations // groups,...  7.72 us
    pallas_call x1, Pallas kernels, own_rows_of(): pl.pallas_call(functools.partial(own_rows_kernel, groups, per, own, width...  4.14 us
    unnamed x8, local copies, waits for them, and re-layouts  2.08 us
    pallas_call x1, Pallas kernels, prepare(): pl.pallas_call(prepare_kernel, out_shape=[jax.ShapeDtypeStruct((stations,...  1.97 us
    pallas_call x1, Pallas kernels, own_sums(): pl.pallas_call(functools.partial(blocks_kernel, groups, per, own), out_sh...  1.37 us
  transfers between devices with their start and end apart: 26, of which 7 were waited for; matrix products, arithmetic and copies ran while one was open for 0% of the time, Pallas kernels for 20%

profile of v7, /device:TPU:0, one launch (start us, length us, event | category | flops | bytes accessed | tf_op | source)
XLA Modules:
  0.0 67.5 jit_solution(6188063475264566004)
XLA Ops:
  0.6 2.0 %prepare.1 = (f32[2,136,256]{2,1,0:T(8,128)}, f32[2,64,256]{2,1,0:T(8,128)}) custom-call(f32[2,3,32,256]{3,2,1,0:T(8,128)} %refs_0_.1, f32[2,32,256]{2,1,0:T(8,128)} %refs_1_.1, f32[2,32,256]{2,1,0:T(8,128)} %refs_2_.1, s32[2,32,256]{2,1,0:T(8,128)} %refs_3_.1, s32[2,32]{1,0:T(2,128)} %refs_4_.1, s32[2,256]{1,0:T(2,128)} %refs_5_.1), custom_call_target="tpu_custom_call" | custom-call | tf_op jit(solution)/shard_map/prepare/pallas_call | solution.py:78
  2.6 3.0 %collective-permute-start.1 = (f32[2,136,256]{2,1,0:T(8,128)}, f32[2,136,256]{2,1,0:T(8,128)S(1)}, u32[]{:S(2)}, u32[]{:S(2)}) collective-permute-start(f32[2,136,256]{2,1,0:T(8,128)} %get-tuple-element.25.refs_0_), channel_id=1, source_target_pairs={{0,2},{1,3},{2,0},{3,1},{4,6},{5,7},{6,4},{7,5},{8,10},{9,11},{10,... | collective-permute-start | bytes 835592 | tf_op jit(solution)/shard_map/ppermute | solution.py:482
  5.6 1.5 %collective-permute-start.3 = (f32[2,136,256]{2,1,0:T(8,128)}, f32[2,136,256]{2,1,0:T(8,128)S(1)}, u32[]{:S(2)}, u32[]{:S(2)}) collective-permute-start(f32[2,136,256]{2,1,0:T(8,128)} %get-tuple-element.25.refs_0_), channel_id=1, source_target_pairs={{0,4},{4,0},{8,12},{12,8},{16,20},{20,16},{24,28},{28,24},{1,5},{5... | collective-permute-start | bytes 835592 | tf_op jit(solution)/shard_map/ppermute | solution.py:482
  7.1 0.0 collective-permute-start
  7.1 5.4 %collective-permute-done.1.refs_2_ = f32[2,136,256]{2,1,0:T(8,128)S(1)} collective-permute-done((f32[2,136,256]{2,1,0:T(8,128)}, f32[2,136,256]{2,1,0:T(8,128)S(1)}, u32[]{:S(2)}, u32[]{:S(2)}) %collective-permute-start.1) | collective-permute-done | bytes 278560 | tf_op jit(solution)/shard_map/ppermute | solution.py:482
  12.5 1.7 %collective-permute-start.5 = (f32[2,136,256]{2,1,0:T(8,128)S(1)}, f32[2,136,256]{2,1,0:T(8,128)S(1)}, u32[]{:S(2)}, u32[]{:S(2)}) collective-permute-start(f32[2,136,256]{2,1,0:T(8,128)S(1)} %collective-permute-done.1.refs_2_), channel_id=1, source_target_pairs={{0,4},{4,0},{8,12},{12,8},{16,20},{20,16},{24,28},{28,24},{1,5},{5... | collective-permute-start | bytes 835592 | tf_op jit(solution)/shard_map/ppermute | solution.py:482
  14.2 1.1 %copy-done = f32[30,3,8,256]{3,2,1,0:T(8,128)S(1)} copy-done((f32[30,3,8,256]{3,2,1,0:T(8,128)S(1)}, f32[30,3,8,256]{3,2,1,0:T(8,128)}, u32[]{:S(2)}) %copy-start) | copy-done | bytes 737304
  15.3 0.1 cut_parts.1
  15.4 1.6 %collective-permute-start.7 = (f32[10,3,8,256]{3,2,1,0:T(8,128)S(1)}, f32[10,3,8,256]{3,2,1,0:T(8,128)S(1)}, u32[]{:S(2)}, u32[]{:S(2)}) collective-permute-start(f32[10,3,8,256]{3,2,1,0:T(8,128)S(1)} %get-tuple-element.34), channel_id=1, source_target_pairs={{0,2},{1,3},{2,0},{3,1},{4,6},{5,7},{6,4},{7,5},{8,10},{9,11},{10,... | collective-permute-start | bytes 737288 | tf_op jit(solution)/shard_map/ppermute | solution.py:482
  17.0 0.5 collective-permute-start.8
  17.5 0.0 collective-permute-done.3.refs_4_
  17.5 0.0 collective-permute-start.2
  17.5 0.0 collective-permute-done.refs_1_
  17.5 0.5 collective-permute-start.4
  18.0 2.3 %collective-permute-done.5.refs_6_ = f32[2,136,256]{2,1,0:T(8,128)S(1)} collective-permute-done((f32[2,136,256]{2,1,0:T(8,128)S(1)}, f32[2,136,256]{2,1,0:T(8,128)S(1)}, u32[]{:S(2)}, u32[]{:S(2)}) %collective-permute-start.5) | collective-permute-done | bytes 278560 | tf_op jit(solution)/shard_map/ppermute | solution.py:482
  20.4 0.0 collective-permute-start.6
  20.4 4.3 %collective-permute-done.8.refs_2_ = f32[5,3,8,256]{3,2,1,0:T(8,128)S(1)} collective-permute-done((f32[5,3,8,256]{3,2,1,0:T(8,128)S(1)}, f32[5,3,8,256]{3,2,1,0:T(8,128)S(1)}, u32[]{:S(2)}, u32[]{:S(2)}) %collective-permute-start.8) | collective-permute-done | bytes 122912 | tf_op jit(solution)/shard_map/ppermute | solution.py:482
  24.7 0.6 collective-permute-start.10
  25.3 0.0 collective-permute-done.7.refs_1_
  25.3 1.5 %collective-permute-start.9 = (f32[10,3,8,256]{3,2,1,0:T(8,128)S(1)}, f32[10,3,8,256]{3,2,1,0:T(8,128)S(1)}, u32[]{:S(2)}, u32[]{:S(2)}) collective-permute-start(f32[10,3,8,256]{3,2,1,0:T(8,128)S(1)} %collective-permute-done.7.refs_1_), channel_id=1, source_target_pairs={{0,8},{4,12},{8,0},{12,4},{16,24},{20,28},{24,16},{28,20},{1,9},{5... | collective-permute-start | bytes 737288 | tf_op jit(solution)/shard_map/ppermute | solution.py:482
  26.8 2.8 %collective-permute-done.10.refs_4_ = f32[5,3,8,256]{3,2,1,0:T(8,128)S(1)} collective-permute-done((f32[5,3,8,256]{3,2,1,0:T(8,128)S(1)}, f32[5,3,8,256]{3,2,1,0:T(8,128)S(1)}, u32[]{:S(2)}, u32[]{:S(2)}) %collective-permute-start.10) | collective-permute-done | bytes 122912 | tf_op jit(solution)/shard_map/ppermute | solution.py:482
  29.5 0.0 collective-permute-start.13
  29.5 1.3 %collective-permute-done.13.refs_7_ = f32[5,3,8,256]{3,2,1,0:T(8,128)S(1)} collective-permute-done((f32[5,3,8,256]{3,2,1,0:T(8,128)S(1)}, f32[5,3,8,256]{3,2,1,0:T(8,128)S(1)}, u32[]{:S(2)}, u32[]{:S(2)}) %collective-permute-start.13) | collective-permute-done | bytes 122912 | tf_op jit(solution)/shard_map/ppermute | solution.py:482
  30.9 0.1 collective-permute-start.11
  31.0 0.0 collective-permute-done.2.refs_3_
  31.0 1.5 %collective-permute-start.20 = (f32[2,64,256]{2,1,0:T(8,128)}, f32[2,64,256]{2,1,0:T(8,128)S(1)}, u32[]{:S(2)}, u32[]{:S(2)}) collective-permute-start(f32[2,64,256]{2,1,0:T(8,128)} %get-tuple-element.42.refs_4_), channel_id=1, source_target_pairs={{0,2},{1,3},{2,0},{3,1},{4,6},{5,7},{6,4},{7,5},{8,10},{9,11},{10,... | collective-permute-start | bytes 393224 | tf_op jit(solution)/shard_map/ppermute | solution.py:482
  32.6 0.0 collective-permute-done.4.refs_5_
  32.6 0.1 collective-permute-start.12
  32.6 0.0 collective-permute-done.9.refs_3_
  32.6 0.4 collective-permute-start.15
  33.1 0.0 collective-permute-done.6.refs_7_
  33.1 0.1 collective-permute-start.14
  33.2 1.0 %copy-done.1 = f32[2,136,256]{2,1,0:T(8,128)S(1)} copy-done((f32[2,136,256]{2,1,0:T(8,128)S(1)}, f32[2,136,256]{2,1,0:T(8,128)}, u32[]{:S(2)}) %copy-start.1) | copy-done | bytes 278552
  34.1 4.1 %own_rows.1 = (f32[16,136,256]{2,1,0:T(8,128)S(1)}, s32[16,128]{1,0:T(8,128)S(1)}, bf16[16,256,256]{2,1,0:T(8,128)(2,1)S(1)}, bf16[16,256,256]{2,1,0:T(8,128)(2,1)S(1)}) custom-call(f32[2,136,256]{2,1,0:T(8,128)S(1)} %copy-done.1, f32[2,136,256]{2,1,0:T(8,128)S(1)} %collective-permute-done.refs_1_, f32[2,136,256]{2,1,0:T(8,128)S(1)} %collective-permute-done.1.refs_2_, ...), custom_call_target="tpu_custom_call" | custom-call | flops 8000000000 | bytes 8000000 | tf_op jit(solution)/shard_map/own_rows/pallas_call | solution.py:170
  38.3 0.0 collective-permute-done.20.refs_6_
  38.3 0.0 copy-done.3
  38.3 0.5 collective-permute-start.19
  38.8 0.0 collective-permute-done.15.refs_9_
  38.8 0.1 collective-permute-start.21
  38.9 0.0 collective-permute-done.11.refs_5_
  38.9 0.0 collective-permute-done.12.refs_6_
  38.9 0.0 collective-permute-done.14.refs_8_
  38.9 0.2 place.1.refs_4_
  39.1 0.0 copy-start.2
  39.1 7.7 %accumulate.1 = (f32[15,8,256]{2,1,0:T(8,128)S(1)}, f32[15,8,256]{2,1,0:T(8,128)S(1)}, f32[15,8,256]{2,1,0:T(8,128)S(1)}, f32[15,8,256]{2,1,0:T(8,128)S(1)}, f32[30,8,256]{2,1,0:T(8,128)S(1)}) custom-call(f32[16,136,256]{2,1,0:T(8,128)S(1)} %get-tuple-element.30.refs_0_, s32[16,128]{1,0:T(8,128)S(1)} %get-tuple-element.31.refs_1_, ...), custom_call_target="tpu_custom_call" | custom-call | flops 8000000000 | bytes 8000000 | tf_op jit(solution)/shard_map/accumulate/pallas_call | solution.py:330
  46.8 1.6 %collective-permute-start.16 = (f32[15,8,256]{2,1,0:T(8,128)S(1)}, f32[15,8,256]{2,1,0:T(8,128)S(1)}, u32[]{:S(2)}, u32[]{:S(2)}) collective-permute-start(f32[15,8,256]{2,1,0:T(8,128)S(1)} %get-tuple-element.39), channel_id=1, source_target_pairs={{0,8},{4,12},{8,0},{12,4},{16,24},{20,28},{24,16},{28,20},{1,9},{5... | collective-permute-start | bytes 368648 | tf_op jit(solution)/shard_map/ppermute | solution.py:482
  48.5 2.6 %collective-permute-start.17 = (f32[15,8,256]{2,1,0:T(8,128)S(1)}, f32[15,8,256]{2,1,0:T(8,128)S(1)}, u32[]{:S(2)}, u32[]{:S(2)}) collective-permute-start(f32[15,8,256]{2,1,0:T(8,128)S(1)} %get-tuple-element.40), channel_id=1, source_target_pairs={{0,16},{4,20},{8,24},{12,28},{16,0},{20,4},{24,8},{28,12},{1,17},{... | collective-permute-start | bytes 368648 | tf_op jit(solution)/shard_map/ppermute | solution.py:482
  51.1 0.2 collective-permute-start.18
  51.3 0.0 collective-permute-done.19.refs_5_
  51.3 0.0 collective-permute-done.21.refs_7_
  51.3 0.0 copy-done.2
  51.3 1.4 %own_sums.1.refs_0_ = f32[2,8,256]{2,1,0:T(8,128)S(1)} custom-call(f32[2,136,256]{2,1,0:T(8,128)S(1)} %copy-done.2, f32[2,136,256]{2,1,0:T(8,128)S(1)} %collective-permute-done.refs_1_, f32[2,136,256]{2,1,0:T(8,128)S(1)} %collective-permute-done.1.refs_2_, f32[2,136,256]{2,1,0:T(8,128)S(1)} %collective-permute-done.2.refs_3_, f32[2,64,256]{2,1,0:T(8,128)S(1)} %copy-done.3, ...), custom_call_target="tpu_custom_call" | custom-call | flops 4000000000 | bytes 4000000 | tf_op jit(solution)/shard_map/own_sums/pallas_call | solution.py:408
  52.7 0.6 collective-permute-start.22
  53.3 3.2 %collective-permute-done.22.refs_1_ = f32[2,8,256]{2,1,0:T(8,128)S(1)} collective-permute-done((f32[2,8,256]{2,1,0:T(8,128)S(1)}, f32[2,8,256]{2,1,0:T(8,128)S(1)}, u32[]{:S(2)}, u32[]{:S(2)}) %collective-permute-start.22) | collective-permute-done | bytes 16416 | tf_op jit(solution)/shard_map/ppermute | solution.py:482
  56.5 0.6 collective-permute-start.23
  57.1 3.5 %collective-permute-start.24 = (f32[2,8,256]{2,1,0:T(8,128)S(1)}, f32[2,8,256]{2,1,0:T(8,128)S(1)}, u32[]{:S(2)}, u32[]{:S(2)}) collective-permute-start(f32[2,8,256]{2,1,0:T(8,128)S(1)} %add_smalls.1.refs_4_), channel_id=1, source_target_pairs={{0,16},{4,20},{8,24},{12,28},{16,0},{20,4},{24,8},{28,12},{1,17},{... | collective-permute-start | bytes 49160 | tf_op jit(solution)/shard_map/ppermute | solution.py:482
  60.7 0.0 collective-permute-done.23.refs_5_
  60.7 3.2 %collective-permute-start.25 = (f32[2,8,256]{2,1,0:T(8,128)S(1)}, f32[2,8,256]{2,1,0:T(8,128)S(1)}, u32[]{:S(2)}, u32[]{:S(2)}) collective-permute-start(f32[2,8,256]{2,1,0:T(8,128)S(1)} %add_smalls.1.refs_4_), channel_id=1, source_target_pairs={{0,24},{4,28},{8,16},{12,20},{16,8},{20,12},{24,0},{28,4},{1,25},{... | collective-permute-start | bytes 49160 | tf_op jit(solution)/shard_map/ppermute | solution.py:482
  63.9 0.0 collective-permute-done.24.refs_6_
  63.9 2.4 %collective-permute-done.25.refs_7_ = f32[2,8,256]{2,1,0:T(8,128)S(1)} collective-permute-done((f32[2,8,256]{2,1,0:T(8,128)S(1)}, f32[2,8,256]{2,1,0:T(8,128)S(1)}, u32[]{:S(2)}, u32[]{:S(2)}) %collective-permute-start.25) | collective-permute-done | bytes 16416 | tf_op jit(solution)/shard_map/ppermute | solution.py:482
  66.2 0.0 collective-permute-done.16.refs_1_
  66.2 0.0 collective-permute-done.17.refs_2_
  66.2 0.0 collective-permute-done.18.refs_3_
  66.2 1.3 %finish.1 = (f32[240,120]{1,0:T(8,128)}, f32[1,240]{1,0:T(1,128)}, f32[8,8,30]{2,1,0:T(8,128)}) custom-call(f32[15,8,256]{2,1,0:T(8,128)S(1)} %get-tuple-element.38.refs_0_, f32[15,8,256]{2,1,0:T(8,128)S(1)} %collective-permute-done.16.refs_1_, f32[15,8,256]{2,1,0:T(8,128)S(1)} %collective-permute-done.17.refs_2_, ...), custom_call_target="tpu_custom_call" | custom-call | tf_op jit(solution)/shard_map/finish/pallas_call | solution.py:467
  (4 shorter events, 0.0 us)
Async XLA Ops:
  2.6 9.9 %collective-permute-start.1 = (f32[2,136,256]{2,1,0:T(8,128)}, f32[2,136,256]{2,1,0:T(8,128)S(1)}, u32[]{:S(2)}, u32[]{:S(2)}) collective-permute-start(f32[2,136,256]{2,1,0:T(8,128)} %get-tuple-element.25.refs_0_), channel_id=1, source_target_pairs={{0,2},{1,3},{2,0},{3,1},{4,6},{5,7},{6,4},{7,5},{8,10},{9,11},{10,... | collective-permute-start | bytes 835592 | tf_op jit(solution)/shard_map/ppermute | solution.py:482
  5.6 11.9 %collective-permute-start.3 = (f32[2,136,256]{2,1,0:T(8,128)}, f32[2,136,256]{2,1,0:T(8,128)S(1)}, u32[]{:S(2)}, u32[]{:S(2)}) collective-permute-start(f32[2,136,256]{2,1,0:T(8,128)} %get-tuple-element.25.refs_0_), channel_id=1, source_target_pairs={{0,4},{4,0},{8,12},{12,8},{16,20},{20,16},{24,28},{28,24},{1,5},{5... | collective-permute-start | bytes 835592 | tf_op jit(solution)/shard_map/ppermute | solution.py:482
  7.1 10.4 %collective-permute-start = (f32[2,136,256]{2,1,0:T(8,128)}, f32[2,136,256]{2,1,0:T(8,128)S(1)}, u32[]{:S(2)}, u32[]{:S(2)}) collective-permute-start(f32[2,136,256]{2,1,0:T(8,128)} %get-tuple-element.25.refs_0_), channel_id=1, source_target_pairs={{0,1},{1,0},{2,3},{3,2},{4,5},{5,4},{6,7},{7,6},{8,9},{9,8},{10,11... | collective-permute-start | bytes 835592 | tf_op jit(solution)/shard_map/ppermute | solution.py:482
  12.5 7.8 %collective-permute-start.5 = (f32[2,136,256]{2,1,0:T(8,128)S(1)}, f32[2,136,256]{2,1,0:T(8,128)S(1)}, u32[]{:S(2)}, u32[]{:S(2)}) collective-permute-start(f32[2,136,256]{2,1,0:T(8,128)S(1)} %collective-permute-done.1.refs_2_), channel_id=1, source_target_pairs={{0,4},{4,0},{8,12},{12,8},{16,20},{20,16},{24,28},{28,24},{1,5},{5... | collective-permute-start | bytes 835592 | tf_op jit(solution)/shard_map/ppermute | solution.py:482
  14.2 1.1 %copy-start = (f32[30,3,8,256]{3,2,1,0:T(8,128)S(1)}, f32[30,3,8,256]{3,2,1,0:T(8,128)}, u32[]{:S(2)}) copy-start(f32[30,3,8,256]{3,2,1,0:T(8,128)} %orbit.1) | copy-start | bytes 2211844
  15.4 9.9 %collective-permute-start.7 = (f32[10,3,8,256]{3,2,1,0:T(8,128)S(1)}, f32[10,3,8,256]{3,2,1,0:T(8,128)S(1)}, u32[]{:S(2)}, u32[]{:S(2)}) collective-permute-start(f32[10,3,8,256]{3,2,1,0:T(8,128)S(1)} %get-tuple-element.34), channel_id=1, source_target_pairs={{0,2},{1,3},{2,0},{3,1},{4,6},{5,7},{6,4},{7,5},{8,10},{9,11},{10,... | collective-permute-start | bytes 737288 | tf_op jit(solution)/shard_map/ppermute | solution.py:482
  17.0 7.7 %collective-permute-start.8 = (f32[5,3,8,256]{3,2,1,0:T(8,128)S(1)}, f32[5,3,8,256]{3,2,1,0:T(8,128)S(1)}, u32[]{:S(2)}, u32[]{:S(2)}) collective-permute-start(f32[5,3,8,256]{3,2,1,0:T(8,128)S(1)} %get-tuple-element.36), channel_id=1, source_target_pairs={{0,2},{1,3},{2,0},{3,1},{4,6},{5,7},{6,4},{7,5},{8,10},{9,11},{10,... | collective-permute-start | bytes 368648 | tf_op jit(solution)/shard_map/ppermute | solution.py:482
  17.5 13.5 %collective-permute-start.2 = (f32[2,136,256]{2,1,0:T(8,128)S(1)}, f32[2,136,256]{2,1,0:T(8,128)S(1)}, u32[]{:S(2)}, u32[]{:S(2)}) collective-permute-start(f32[2,136,256]{2,1,0:T(8,128)S(1)} %collective-permute-done.1.refs_2_), channel_id=1, source_target_pairs={{0,1},{1,0},{2,3},{3,2},{4,5},{5,4},{6,7},{7,6},{8,9},{9,8},{10,11... | collective-permute-start | bytes 835592 | tf_op jit(solution)/shard_map/ppermute | solution.py:482
  17.5 15.0 %collective-permute-start.4 = (f32[2,136,256]{2,1,0:T(8,128)S(1)}, f32[2,136,256]{2,1,0:T(8,128)S(1)}, u32[]{:S(2)}, u32[]{:S(2)}) collective-permute-start(f32[2,136,256]{2,1,0:T(8,128)S(1)} %collective-permute-done.3.refs_4_), channel_id=1, source_target_pairs={{0,1},{1,0},{2,3},{3,2},{4,5},{5,4},{6,7},{7,6},{8,9},{9,8},{10,11... | collective-permute-start | bytes 835592 | tf_op jit(solution)/shard_map/ppermute | solution.py:482
  20.4 12.7 %collective-permute-start.6 = (f32[2,136,256]{2,1,0:T(8,128)S(1)}, f32[2,136,256]{2,1,0:T(8,128)S(1)}, u32[]{:S(2)}, u32[]{:S(2)}) collective-permute-start(f32[2,136,256]{2,1,0:T(8,128)S(1)} %collective-permute-done.5.refs_6_), channel_id=1, source_target_pairs={{0,1},{1,0},{2,3},{3,2},{4,5},{5,4},{6,7},{7,6},{8,9},{9,8},{10,11... | collective-permute-start | bytes 835592 | tf_op jit(solution)/shard_map/ppermute | solution.py:482
  24.7 4.9 %collective-permute-start.10 = (f32[5,3,8,256]{3,2,1,0:T(8,128)S(1)}, f32[5,3,8,256]{3,2,1,0:T(8,128)S(1)}, u32[]{:S(2)}, u32[]{:S(2)}) collective-permute-start(f32[5,3,8,256]{3,2,1,0:T(8,128)S(1)} %collective-permute-done.8.refs_2_), channel_id=1, source_target_pairs={{0,4},{4,0},{8,12},{12,8},{16,20},{20,16},{24,28},{28,24},{1,5},{5... | collective-permute-start | bytes 368648 | tf_op jit(solution)/shard_map/ppermute | solution.py:482
  25.3 7.3 %collective-permute-start.9 = (f32[10,3,8,256]{3,2,1,0:T(8,128)S(1)}, f32[10,3,8,256]{3,2,1,0:T(8,128)S(1)}, u32[]{:S(2)}, u32[]{:S(2)}) collective-permute-start(f32[10,3,8,256]{3,2,1,0:T(8,128)S(1)} %collective-permute-done.7.refs_1_), channel_id=1, source_target_pairs={{0,8},{4,12},{8,0},{12,4},{16,24},{20,28},{24,16},{28,20},{1,9},{5... | collective-permute-start | bytes 737288 | tf_op jit(solution)/shard_map/ppermute | solution.py:482
  29.5 1.3 %collective-permute-start.13 = (f32[5,3,8,256]{3,2,1,0:T(8,128)S(1)}, f32[5,3,8,256]{3,2,1,0:T(8,128)S(1)}, u32[]{:S(2)}, u32[]{:S(2)}) collective-permute-start(f32[5,3,8,256]{3,2,1,0:T(8,128)S(1)} %collective-permute-done.8.refs_2_), channel_id=1, source_target_pairs={{0,1},{1,0},{2,3},{3,2},{4,5},{5,4},{6,7},{7,6},{8,9},{9,8},{10,11... | collective-permute-start | bytes 368648 | tf_op jit(solution)/shard_map/ppermute | solution.py:482
  30.9 8.0 %collective-permute-start.11 = (f32[30,3,8,256]{3,2,1,0:T(8,128)S(1)}, f32[30,3,8,256]{3,2,1,0:T(8,128)S(1)}, u32[]{:S(2)}, u32[]{:S(2)}) collective-permute-start(f32[30,3,8,256]{3,2,1,0:T(8,128)S(1)} %get-tuple-element.29.refs_8_.refs_0_.refs_9_), channel_id=1, source_target_pairs={{0,1},{1,0},{2,3},{3,2},{4,5},{5,4},{6,7},{7,6},{8,9},{9,8},{10,11... | collective-permute-start | bytes 2211848 | tf_op jit(solution)/shard_map/ppermute | solution.py:482
  31.0 7.2 %collective-permute-start.20 = (f32[2,64,256]{2,1,0:T(8,128)}, f32[2,64,256]{2,1,0:T(8,128)S(1)}, u32[]{:S(2)}, u32[]{:S(2)}) collective-permute-start(f32[2,64,256]{2,1,0:T(8,128)} %get-tuple-element.42.refs_4_), channel_id=1, source_target_pairs={{0,2},{1,3},{2,0},{3,1},{4,6},{5,7},{6,4},{7,5},{8,10},{9,11},{10,... | collective-permute-start | bytes 393224 | tf_op jit(solution)/shard_map/ppermute | solution.py:482
  32.6 6.3 %collective-permute-start.12 = (f32[10,3,8,256]{3,2,1,0:T(8,128)S(1)}, f32[10,3,8,256]{3,2,1,0:T(8,128)S(1)}, u32[]{:S(2)}, u32[]{:S(2)}) collective-permute-start(f32[10,3,8,256]{3,2,1,0:T(8,128)S(1)} %collective-permute-done.7.refs_1_), channel_id=1, source_target_pairs={{0,1},{1,0},{2,3},{3,2},{4,5},{5,4},{6,7},{7,6},{8,9},{9,8},{10,11... | collective-permute-start | bytes 737288 | tf_op jit(solution)/shard_map/ppermute | solution.py:482
  32.6 6.2 %collective-permute-start.15 = (f32[5,3,8,256]{3,2,1,0:T(8,128)S(1)}, f32[5,3,8,256]{3,2,1,0:T(8,128)S(1)}, u32[]{:S(2)}, u32[]{:S(2)}) collective-permute-start(f32[5,3,8,256]{3,2,1,0:T(8,128)S(1)} %collective-permute-done.10.refs_4_), channel_id=1, source_target_pairs={{0,1},{1,0},{2,3},{3,2},{4,5},{5,4},{6,7},{7,6},{8,9},{9,8},{10,11... | collective-permute-start | bytes 368648 | tf_op jit(solution)/shard_map/ppermute | solution.py:482
  33.1 5.8 %collective-permute-start.14 = (f32[10,3,8,256]{3,2,1,0:T(8,128)S(1)}, f32[10,3,8,256]{3,2,1,0:T(8,128)S(1)}, u32[]{:S(2)}, u32[]{:S(2)}) collective-permute-start(f32[10,3,8,256]{3,2,1,0:T(8,128)S(1)} %collective-permute-done.9.refs_3_), channel_id=1, source_target_pairs={{0,1},{1,0},{2,3},{3,2},{4,5},{5,4},{6,7},{7,6},{8,9},{9,8},{10,11... | collective-permute-start | bytes 737288 | tf_op jit(solution)/shard_map/ppermute | solution.py:482
  33.2 1.0 %copy-start.1 = (f32[2,136,256]{2,1,0:T(8,128)S(1)}, f32[2,136,256]{2,1,0:T(8,128)}, u32[]{:S(2)}) copy-start(f32[2,136,256]{2,1,0:T(8,128)} %get-tuple-element.25.refs_0_) | copy-start | bytes 835588
  34.1 4.2 %copy-start.3 = (f32[2,64,256]{2,1,0:T(8,128)S(1)}, f32[2,64,256]{2,1,0:T(8,128)}, u32[]{:S(2)}) copy-start(f32[2,64,256]{2,1,0:T(8,128)} %get-tuple-element.42.refs_4_) | copy-start | bytes 393220
  38.3 13.0 %collective-permute-start.19 = (f32[2,64,256]{2,1,0:T(8,128)S(1)}, f32[2,64,256]{2,1,0:T(8,128)S(1)}, u32[]{:S(2)}, u32[]{:S(2)}) collective-permute-start(f32[2,64,256]{2,1,0:T(8,128)S(1)} %copy-done.3), channel_id=1, source_target_pairs={{0,1},{1,0},{2,3},{3,2},{4,5},{5,4},{6,7},{7,6},{8,9},{9,8},{10,11... | collective-permute-start | bytes 393224 | tf_op jit(solution)/shard_map/ppermute | solution.py:482
  38.8 12.5 %collective-permute-start.21 = (f32[2,64,256]{2,1,0:T(8,128)S(1)}, f32[2,64,256]{2,1,0:T(8,128)S(1)}, u32[]{:S(2)}, u32[]{:S(2)}) collective-permute-start(f32[2,64,256]{2,1,0:T(8,128)S(1)} %collective-permute-done.20.refs_6_), channel_id=1, source_target_pairs={{0,1},{1,0},{2,3},{3,2},{4,5},{5,4},{6,7},{7,6},{8,9},{9,8},{10,11... | collective-permute-start | bytes 393224 | tf_op jit(solution)/shard_map/ppermute | solution.py:482
  39.1 12.2 %copy-start.2 = (f32[2,136,256]{2,1,0:T(8,128)S(1)}, f32[2,136,256]{2,1,0:T(8,128)}, u32[]{:S(2)}) copy-start(f32[2,136,256]{2,1,0:T(8,128)} %get-tuple-element.25.refs_0_) | copy-start | bytes 835588
  46.8 19.4 %collective-permute-start.16 = (f32[15,8,256]{2,1,0:T(8,128)S(1)}, f32[15,8,256]{2,1,0:T(8,128)S(1)}, u32[]{:S(2)}, u32[]{:S(2)}) collective-permute-start(f32[15,8,256]{2,1,0:T(8,128)S(1)} %get-tuple-element.39), channel_id=1, source_target_pairs={{0,8},{4,12},{8,0},{12,4},{16,24},{20,28},{24,16},{28,20},{1,9},{5... | collective-permute-start | bytes 368648 | tf_op jit(solution)/shard_map/ppermute | solution.py:482
  48.5 17.8 %collective-permute-start.17 = (f32[15,8,256]{2,1,0:T(8,128)S(1)}, f32[15,8,256]{2,1,0:T(8,128)S(1)}, u32[]{:S(2)}, u32[]{:S(2)}) collective-permute-start(f32[15,8,256]{2,1,0:T(8,128)S(1)} %get-tuple-element.40), channel_id=1, source_target_pairs={{0,16},{4,20},{8,24},{12,28},{16,0},{20,4},{24,8},{28,12},{1,17},{... | collective-permute-start | bytes 368648 | tf_op jit(solution)/shard_map/ppermute | solution.py:482
  51.1 15.1 %collective-permute-start.18 = (f32[15,8,256]{2,1,0:T(8,128)S(1)}, f32[15,8,256]{2,1,0:T(8,128)S(1)}, u32[]{:S(2)}, u32[]{:S(2)}) collective-permute-start(f32[15,8,256]{2,1,0:T(8,128)S(1)} %get-tuple-element.41), channel_id=1, source_target_pairs={{0,24},{4,28},{8,16},{12,20},{16,8},{20,12},{24,0},{28,4},{1,25},{... | collective-permute-start | bytes 368648 | tf_op jit(solution)/shard_map/ppermute | solution.py:482
  52.7 3.8 %collective-permute-start.22 = (f32[2,8,256]{2,1,0:T(8,128)S(1)}, f32[2,8,256]{2,1,0:T(8,128)S(1)}, u32[]{:S(2)}, u32[]{:S(2)}) collective-permute-start(f32[2,8,256]{2,1,0:T(8,128)S(1)} %own_sums.1.refs_0_), channel_id=1, source_target_pairs={{0,4},{4,0},{8,12},{12,8},{16,20},{20,16},{24,28},{28,24},{1,5},{5... | collective-permute-start | bytes 49160 | tf_op jit(solution)/shard_map/ppermute | solution.py:482
  56.5 4.2 %collective-permute-start.23 = (f32[2,8,256]{2,1,0:T(8,128)S(1)}, f32[2,8,256]{2,1,0:T(8,128)S(1)}, u32[]{:S(2)}, u32[]{:S(2)}) collective-permute-start(f32[2,8,256]{2,1,0:T(8,128)S(1)} %add_smalls.1.refs_4_), channel_id=1, source_target_pairs={{0,8},{4,12},{8,0},{12,4},{16,24},{20,28},{24,16},{28,20},{1,9},{5... | collective-permute-start | bytes 49160 | tf_op jit(solution)/shard_map/ppermute | solution.py:482
  57.1 6.7 %collective-permute-start.24 = (f32[2,8,256]{2,1,0:T(8,128)S(1)}, f32[2,8,256]{2,1,0:T(8,128)S(1)}, u32[]{:S(2)}, u32[]{:S(2)}) collective-permute-start(f32[2,8,256]{2,1,0:T(8,128)S(1)} %add_smalls.1.refs_4_), channel_id=1, source_target_pairs={{0,16},{4,20},{8,24},{12,28},{16,0},{20,4},{24,8},{28,12},{1,17},{... | collective-permute-start | bytes 49160 | tf_op jit(solution)/shard_map/ppermute | solution.py:482
  60.7 5.5 %collective-permute-start.25 = (f32[2,8,256]{2,1,0:T(8,128)S(1)}, f32[2,8,256]{2,1,0:T(8,128)S(1)}, u32[]{:S(2)}, u32[]{:S(2)}) collective-permute-start(f32[2,8,256]{2,1,0:T(8,128)S(1)} %add_smalls.1.refs_4_), channel_id=1, source_target_pairs={{0,24},{4,28},{8,16},{12,20},{16,8},{20,12},{24,0},{28,4},{1,25},{... | collective-permute-start | bytes 49160 | tf_op jit(solution)/shard_map/ppermute | solution.py:482

commit v8 on v7

--- a/solution.py
+++ b/solution.py
@@ -184,7 +184,7 @@
         ],
         compiler_params=pltpu.CompilerParams(vmem_limit_bytes=MEDIUM_LIMIT),
         cost_estimate=pl.CostEstimate(
-            flops=8 * 10**9, bytes_accessed=8 * 10**6, transcendentals=0),
+            flops=20 * 10**8, bytes_accessed=20 * 10**5, transcendentals=0),
         name="own_rows",
     )(*planes, orbit)
 
@@ -215,9 +215,8 @@
 
 
 def main_kernel(groups, per, own, nx, nz, window, *refs):
-    planes, track, highs, lows, orbit = refs[:5]
-    outs = refs[5 : 5 + nz]
-    own_out = refs[5 + nz]
+    planes, track, highs, lows, orbit, small = refs[:6]
+    outs = refs[6 : 6 + nz]
     (acc, stream_a, stream_b, product_a, product_b, tropo_a, tropo_b,
      spread_tropo) = refs[6 + nz :]
     streams = (stream_a, stream_b)
@@ -311,28 +310,33 @@
     acc[...] = acc[...] - outer.reshape(sats, 8, width)
 
     columns = sats * 8 // (nx * nz)
-    owner = first + lax.broadcasted_iota(jnp.int32, (own, 8, width), 0)
-    here = lax.rem(lax.div(owner * 8, columns), nx) == lax.rem(mine, nx)
-    own_out[...] = jnp.where(here, acc[pl.ds(first, own)], 0.0)
+    owner = lax.broadcasted_iota(jnp.int32, (8, width), 1) // 8
+    here = lax.rem(lax.div((first + owner) * 8, columns), nx) == lax.rem(mine, nx)
+    folded = jnp.zeros((8, width), jnp.float32)
+    for o in range(own):
+        folded = folded + jnp.where(owner == o, acc[first + o], 0.0)
+    folded = small[0] + jnp.where(here, folded, 0.0)
     for dz in range(nz):
         start = window_start(mine ^ (dz * nx), columns, sats, window)
-        outs[dz][...] = acc[pl.ds(start, window)]
-
-
-def accumulate(groups, planes, track, highs, lows, orbit, nx, nz, window):
+        outs[dz][:window] = acc[pl.ds(start, window)]
+        outs[dz][window] = folded
+        outs[dz][window + 1] = small[1]
+
+
+def accumulate(groups, planes, track, highs, lows, orbit, small, nx, nz, window):
     stations, rows, epochs = planes.shape
     sats = orbit.shape[0]
     own = sats // groups
     tracked = (rows - 8) // 4
     width = highs.shape[1]
     slabs = -(-stations // PACKED)
-    out = jax.ShapeDtypeStruct((window, 8, width), jnp.float32)
+    out = jax.ShapeDtypeStruct((window + 2, 8, width), jnp.float32)
     return pl.pallas_call(
         functools.partial(
             main_kernel, groups, stations // groups, own, nx, nz, window),
-        out_shape=[out] * nz + [jax.ShapeDtypeStruct((own, 8, width), jnp.float32)],
-        in_specs=[vmem(), pl.BlockSpec(memory_space=pltpu.SMEM)] + [vmem()] * 3,
-        out_specs=[vmem()] * (nz + 1),
+        out_shape=[out] * nz,
+        in_specs=[vmem(), pl.BlockSpec(memory_space=pltpu.SMEM)] + [vmem()] * 4,
+        out_specs=[vmem()] * nz,
         scratch_shapes=[
             pltpu.VMEM((sats, 8, width), jnp.float32),
             *[pltpu.VMEM((4 * tracked * 8, epochs), jnp.bfloat16)] * 2,
@@ -344,16 +348,17 @@
         cost_estimate=pl.CostEstimate(
             flops=8 * 10**9, bytes_accessed=8 * 10**6, transcendentals=0),
         name="accumulate",
-    )(planes, track, highs, lows, orbit)
-
-
-def blocks_kernel(groups, per, own, *refs):
+    )(planes, track, highs, lows, orbit, small)
+
+
+def blocks_kernel(groups, per, *refs):
     plane_pieces = refs[:groups]
     extra_pieces = refs[groups : 2 * groups]
-    own_rows, orbit, small = refs[2 * groups :]
+    orbit, small = refs[2 * groups :]
     tracked = extra_pieces[0].shape[1] // 2
     epochs = orbit.shape[3]
-    width = own_rows.shape[2]
+    width = small.shape[2]
+    own = orbit.shape[0]
     first = lax.axis_index("sat") * own
     satellite = first + lax.broadcasted_iota(jnp.int32, (own, tracked), 0)
     pairs = [(0, 0), (0, 1), (0, 2), (1, 1), (1, 2), (2, 2)]
@@ -394,40 +399,39 @@
     owner = lax.broadcasted_iota(jnp.int32, (8, own * 8), 1) // 8
     folded = jnp.zeros((8, own * 8), jnp.float32)
     for o in range(own):
-        tile = own_rows[o, :, : own * 8] + blocks[o * 8 : o * 8 + 8, :]
-        folded = folded + jnp.where(owner == o, tile, 0.0)
+        folded = folded + jnp.where(owner == o, blocks[o * 8 : o * 8 + 8, :], 0.0)
     small[...] = jnp.zeros_like(small)
     small[0, :, : own * 8] = folded
     small[1, :, : own * 8] = right
 
 
-def own_sums(planes, extras, own_rows, orbit):
+def own_sums(planes, extras, orbit, width):
     groups = len(planes)
     per = planes[0].shape[0]
-    own, _, width = own_rows.shape
-    return pl.pallas_call(
-        functools.partial(blocks_kernel, groups, per, own),
+    return pl.pallas_call(
+        functools.partial(blocks_kernel, groups, per),
         out_shape=jax.ShapeDtypeStruct((2, 8, width), jnp.float32),
-        in_specs=[vmem()] * (2 * groups + 2),
+        in_specs=[vmem()] * (2 * groups + 1),
         out_specs=vmem(),
         compiler_params=pltpu.CompilerParams(vmem_limit_bytes=MEDIUM_LIMIT),
         cost_estimate=pl.CostEstimate(
-            flops=4 * 10**9, bytes_accessed=4 * 10**6, transcendentals=0),
+            flops=1 * 10**8, bytes_accessed=1 * 10**5, transcendentals=0),
         name="own_sums",
-    )(*planes, *extras, own_rows, orbit)
-
-
-def add_kernel(*refs):
-    total = refs[0][...]
+    )(*planes, *extras, orbit)
+
+
+def add_kernel(window, *refs):
+    total = refs[0][window:]
     for ref in refs[1:-1]:
-        total = total + ref[...]
+        total = total + ref[window:]
     refs[-1][...] = total
 
 
-def add_smalls(pieces):
-    return pl.pallas_call(
-        add_kernel,
-        out_shape=jax.ShapeDtypeStruct(pieces[0].shape, jnp.float32),
+def add_smalls(pieces, window):
+    width = pieces[0].shape[2]
+    return pl.pallas_call(
+        functools.partial(add_kernel, window),
+        out_shape=jax.ShapeDtypeStruct((2, 8, width), jnp.float32),
         in_specs=[vmem()] * len(pieces),
         out_specs=vmem(),
         compiler_params=pltpu.CompilerParams(vmem_limit_bytes=SMALL_LIMIT),
@@ -435,61 +439,66 @@
     )(*pieces)
 
 
-def finish_kernel(nz, window, own, columns, sats, factor, cross_factor, *refs):
-    pieces, smalls = refs[:nz], refs[nz : 2 * nz]
-    normal, right, blocks = refs[2 * nz :]
+def finish_kernel(window, own, columns, sats, cross_factor, *refs):
+    pieces, normal = refs[:-1], refs[-1]
     width = pieces[0].shape[2]
-    total = pieces[0][...]
-    small_total = smalls[0][...]
-    for piece, small in zip(pieces[1:], smalls[1:]):
-        total = total + piece[...]
-        small_total = small_total + small[...]
+    total = pieces[0][:window]
+    for piece in pieces[1:]:
+        total = total + piece[:window]
     first = lax.axis_index("sat") * own
     start = window_start(lax.axis_index("sta"), columns, sats, window)
-    span = own * 8
     part = total.reshape(window * 8, width)
     row_owner = start + lax.broadcasted_iota(jnp.int32, part.shape, 0) // 8
     lane_owner = first + lax.broadcasted_iota(jnp.int32, part.shape, 1) // 8
     part = jnp.where(row_owner == lane_owner, 0.0, part * cross_factor)
-    normal[...] = part.T[:span, :]
-    right[...] = small_total[1, :1, :span] * factor
-    small = small_total[0]
+    normal[...] = part.T[: own * 8, :]
+
+
+def finish(pieces, window, own, columns, sats, cross_factor):
+    return pl.pallas_call(
+        functools.partial(finish_kernel, window, own, columns, sats, cross_factor),
+        out_shape=jax.ShapeDtypeStruct((own * 8, window * 8), jnp.float32),
+        in_specs=[vmem()] * len(pieces),
+        out_specs=vmem(),
+        compiler_params=pltpu.CompilerParams(vmem_limit_bytes=SMALL_LIMIT),
+        cost_estimate=pl.CostEstimate(
+            flops=2 * 10**9, bytes_accessed=2 * 10**6, transcendentals=0),
+        name="finish",
+    )(*pieces)
+
+
+def finish_own_kernel(own, factor, *refs):
+    smalls = refs[:-2]
+    right, blocks = refs[-2:]
+    total = smalls[0][...]
+    for small in smalls[1:]:
+        total = total + small[...]
+    width = total.shape[2]
+    right[...] = total[1, :1, : own * 8] * factor
     lane = lax.broadcasted_iota(jnp.int32, (width, own), 0)
     wanted = lax.broadcasted_iota(jnp.int32, (width, own), 1) * 8
     for p in range(8):
         pick = (lane == wanted + p).astype(jnp.float32)
-        blocks[p] = factor * jnp.dot(small, pick, precision=HIGHEST,
+        blocks[p] = factor * jnp.dot(total[0], pick, precision=HIGHEST,
                                      preferred_element_type=jnp.float32)
 
 
-def finish(pieces, smalls, window, own, columns, sats, factor, cross_factor):
-    nz = len(pieces)
-    return pl.pallas_call(
-        functools.partial(finish_kernel, nz, window, own, columns, sats, factor, cross_factor),
+def finish_own(smalls, own, factor):
+    return pl.pallas_call(
+        functools.partial(finish_own_kernel, own, factor),
         out_shape=[
-            jax.ShapeDtypeStruct((own * 8, window * 8), jnp.float32),
             jax.ShapeDtypeStruct((1, own * 8), jnp.float32),
             jax.ShapeDtypeStruct((8, 8, own), jnp.float32),
         ],
-        in_specs=[vmem()] * (2 * nz),
-        out_specs=[vmem()] * 3,
+        in_specs=[vmem()] * len(smalls),
+        out_specs=[vmem()] * 2,
         compiler_params=pltpu.CompilerParams(vmem_limit_bytes=SMALL_LIMIT),
-        name="finish",
-    )(*pieces, *smalls)
+        name="finish_own",
+    )(*smalls)
 
 
 def shift(value, axis, size, step):
     return lax.ppermute(value, axis, [(i, i ^ step) for i in range(size)])
-
-
-def gather_pieces(value, size):
-    pieces = [None] * size
-    pieces[0] = value
-    for d in range(2, size, 2):
-        pieces[d] = shift(value, "sat", size, d)
-    for d in range(0, size, 2):
-        pieces[d + 1] = shift(pieces[d], "sat", size, 1)
-    return pieces
 
 
 def gather_planes(value, size, columns_axis, nx):
@@ -539,22 +548,31 @@
     return parts, orbit
 
 
-def gather_orbit(orbit, parts, size, columns_axis, nx):
+def fetch_orbit(orbit, parts, size, columns_axis, nx):
     own = orbit.shape[0]
     if not parts:
-        return gather_pieces(orbit, size), tuple((d, -1, 0, own) for d in range(size))
-    half = own // 2
-    lead = half * 2 // 3
-    first, second = parts
-    pieces, places = [orbit], [(0, -1, 0, own)]
+        near = [orbit] + [shift(orbit, "sat", size, d) for d in range(2, size, 2)]
+        return near, [], []
+    near, far = [orbit], []
     for d in range(2, size, 2):
-        near_first = shift(first, "sat", size, d)
-        near_second = shift(second, "sat", size, d)
-        far_first = shift(near_first, "sta", columns_axis, nx)
-        far_second = shift(near_second, "sta", columns_axis, 1)
-        pieces += [near_first, near_second, far_first, far_second]
-        places += [(d, 0, 0, lead), (d, 0, lead, half - lead),
-                   (d, 1, 0, lead), (d, 1, lead, half - lead)]
+        straight = [shift(part, "sat", size, d) for part in parts]
+        near += straight
+        far += [shift(straight[0], "sta", columns_axis, nx),
+                shift(straight[1], "sta", columns_axis, 1)]
+    return near, far, [part.shape[0] for part in parts]
+
+
+def pair_orbit(near, far, sizes, size):
+    if not far:
+        own = near[0].shape[0]
+        pieces = list(near)
+        places = [(d, -1, 0, own) for d in range(0, size, 2)]
+    else:
+        pieces, places = [near[0]], [(0, -1, 0, near[0].shape[0])]
+        for n, d in enumerate(range(2, size, 2)):
+            pieces += [near[1 + 2 * n], near[2 + 2 * n], far[2 * n], far[2 * n + 1]]
+            places += [(d, half, start, count) for half in (0, 1)
+                       for start, count in ((0, sizes[0]), (sizes[0], sizes[1]))]
     for piece, (d, *rest) in list(zip(pieces, places)):
         pieces.append(shift(piece, "sat", size, 1))
         places.append((d + 1, *rest))
@@ -579,30 +597,36 @@
 
     parts, orbit = cut_parts(orbit, columns_axis, nx)
     planes, extra = prepare(sight, mapping, residual, counts, track, knots)
+    if parts:
+        planes, *parts = lax.optimization_barrier((planes, *parts))
     plane_pieces = gather_planes(planes, group, columns_axis, nx)
     if parts:
         *parts, plane_pieces[2] = lax.optimization_barrier((*parts, plane_pieces[2]))
-    orbit_pieces, places = gather_orbit(orbit, parts, group, columns_axis, nx)
-    if parts:
-        extra, orbit_pieces[2] = lax.optimization_barrier((extra, orbit_pieces[2]))
-    extra_pieces = gather_pieces(extra, group)
-    all_planes, all_track, highs, lows = own_rows_of(plane_pieces, orbit, width)
-    *sums, own_rows = accumulate(
-        group, all_planes, all_track, highs, lows, place(orbit_pieces, places, sats, nx),
-        nx, nz, window)
-    small = own_sums(plane_pieces[:group], extra_pieces, own_rows, orbit)
-    smalls = [small] + [shift(small, "sta", columns_axis, d) for d in range(1, nx)]
+    near, far, sizes = fetch_orbit(orbit, parts, group, columns_axis, nx)
+    extra, *near = lax.optimization_barrier((extra, *near))
+    plane_pieces[1], *near = lax.optimization_barrier((plane_pieces[1], *near))
+    own_planes, own_track, highs, lows = own_rows_of(plane_pieces, orbit, width)
+    extra_even = [extra] + [shift(extra, "sat", group, d) for d in range(2, group, 2)]
+    own_track, *held = lax.optimization_barrier((own_track, *extra_even, *far))
+    extra_even, far = held[: group // 2], held[group // 2 :]
+    orbit_pieces, places = pair_orbit(near, far, sizes, group)
+    extra_pieces = []
+    for piece in extra_even:
+        extra_pieces += [piece, shift(piece, "sat", group, 1)]
+    small = own_sums(plane_pieces[:group], extra_pieces, orbit, width)
+    sums = accumulate(
+        group, own_planes, own_track, highs, lows, place(orbit_pieces, places, sats, nx),
+        small, nx, nz, window)
     final = [sums[0]] + [
         shift(sums[d], "sta", columns_axis, d * nx) for d in range(1, nz)
     ]
-    small = add_smalls(smalls)
-    finals = [small] + [
-        shift(small, "sta", columns_axis, d * nx) for d in range(1, nz)
-    ]
+    small = add_smalls(final, window)
+    smalls = [small] + [shift(small, "sta", columns_axis, d) for d in range(1, nx)]
     total_stations = stations * columns_axis * group
     factor = sats / (total_stations * tracked * epochs)
     cross_factor = sats / (total_stations * epochs) ** 0.5
-    normal, right, blocks = finish(final, finals, window, own, columns, sats, factor, cross_factor)
+    normal = finish(final, window, own, columns, sats, cross_factor)
+    right, blocks = finish_own(smalls, own, factor)
     if window * 8 != columns:
         mine = lax.axis_index("sta")
         start = window_start(mine, columns, sats, window)

time: 67.7 us -> 66.3 us (0.979)
  starting transfers between devices: 26.3 us -> 20.5 us
  waiting for transfers between devices: 21.7 us -> 25 us
  Pallas kernels: 16.7 us -> 17.7 us
    ppermute x26 -> x23, starting transfers between devices: 26.3 us -> 20.5 us  [shift(): return lax.ppermute(value, axis, [(i, i ^ step) for i in range(size)])]
    ppermute x26 -> x23, waiting for transfers between devices: 21.7 us -> 25 us  [shift(): return lax.ppermute(value, axis, [(i, i ^ step) for i in range(size)])]
    pallas_call x3 -> x4, Pallas kernels: 2.62 us -> 3.26 us  [the longest x1 1.27 us: own_sums(): pl.pallas_call(functools.partial(blocks_kernel, groups, per), out_shape=j...]
    unnamed x8 -> x6, local copies, waits for them, and re-layouts: 2.08 us -> 2.07 us
  transfers between devices with their start and end apart: 26 -> 23, of which waited for: 7 -> 6; matrix products, arithmetic and copies ran while one was open for 0% -> 0% of each run, Pallas kernels for 20% -> 9%
where the time goes in v8:
time: 66.3 us; the launch traced here: 66.1 us
  waiting for transfers between devices  25 us (38%)
  starting transfers between devices  20.5 us (31%)
  Pallas kernels  17.7 us (27%)
  local copies, waits for them, and re-layouts  2.07 us (3%)
  between operations  0.8 us (1%)
    ppermute x23, waiting for transfers between devices, shift(): return lax.ppermute(value, axis, [(i, i ^ step) for i in range(size)])  25 us
    ppermute x23, starting transfers between devices, shift(): return lax.ppermute(value, axis, [(i, i ^ step) for i in range(size)])  20.5 us
    pallas_call x1, Pallas kernels, accumulate(): pl.pallas_call(functools.partial(main_kernel, groups, stations // groups,...  8.02 us
    pallas_call x1, Pallas kernels, own_rows_of(): pl.pallas_call(functools.partial(own_rows_kernel, groups, per, own, width...  4.22 us
    unnamed x6, local copies, waits for them, and re-layouts  2.07 us
    pallas_call x1, Pallas kernels, prepare(): pl.pallas_call(prepare_kernel, out_shape=[jax.ShapeDtypeStruct((stations,...  1.98 us
  transfers between devices with their start and end apart: 23, of which 6 were waited for; matrix products, arithmetic and copies ran while one was open for 0% of the time, Pallas kernels for 9%

profile of v8, /device:TPU:0, one launch (start us, length us, event | category | flops | bytes accessed | tf_op | source)
XLA Modules:
  0.0 66.1 jit_solution(10190210672607310610)
XLA Ops:
  0.6 0.0 copy-start
  0.6 1.1 %copy-done = f32[30,3,8,256]{3,2,1,0:T(8,128)S(1)} copy-done((f32[30,3,8,256]{3,2,1,0:T(8,128)S(1)}, f32[30,3,8,256]{3,2,1,0:T(8,128)}, u32[]{:S(2)}) %copy-start) | copy-done | bytes 737304
  1.7 0.1 cut_parts.1
  1.8 2.0 %prepare.1 = (f32[2,136,256]{2,1,0:T(8,128)}, f32[2,64,256]{2,1,0:T(8,128)}) custom-call(f32[2,3,32,256]{3,2,1,0:T(8,128)} %refs_0_.1, f32[2,32,256]{2,1,0:T(8,128)} %refs_1_.1, f32[2,32,256]{2,1,0:T(8,128)} %refs_2_.1, s32[2,32,256]{2,1,0:T(8,128)} %refs_3_.1, s32[2,32]{1,0:T(2,128)} %refs_4_.1, s32[2,256]{1,0:T(2,128)} %refs_5_.1), custom_call_target="tpu_custom_call" | custom-call | tf_op jit(solution)/shard_map/prepare/pallas_call | solution.py:78
  3.8 3.0 %collective-permute-start.1 = (f32[2,136,256]{2,1,0:T(8,128)}, f32[2,136,256]{2,1,0:T(8,128)S(1)}, u32[]{:S(2)}, u32[]{:S(2)}) collective-permute-start(f32[2,136,256]{2,1,0:T(8,128)} %get-tuple-element.40.refs_0_), channel_id=1, source_target_pairs={{0,2},{1,3},{2,0},{3,1},{4,6},{5,7},{6,4},{7,5},{8,10},{9,11},{10,... | collective-permute-start | bytes 835592 | tf_op jit(solution)/shard_map/ppermute | solution.py:501
  6.8 0.0 collective-permute-start
  6.8 1.5 %collective-permute-start.5 = (f32[2,136,256]{2,1,0:T(8,128)}, f32[2,136,256]{2,1,0:T(8,128)S(1)}, u32[]{:S(2)}, u32[]{:S(2)}) collective-permute-start(f32[2,136,256]{2,1,0:T(8,128)} %get-tuple-element.40.refs_0_), channel_id=1, source_target_pairs={{0,4},{4,0},{8,12},{12,8},{16,20},{20,16},{24,28},{28,24},{1,5},{5... | collective-permute-start | bytes 835592 | tf_op jit(solution)/shard_map/ppermute | solution.py:501
  8.3 5.4 %collective-permute-done.1.refs_2_ = f32[2,136,256]{2,1,0:T(8,128)S(1)} collective-permute-done((f32[2,136,256]{2,1,0:T(8,128)}, f32[2,136,256]{2,1,0:T(8,128)S(1)}, u32[]{:S(2)}, u32[]{:S(2)}) %collective-permute-start.1) | collective-permute-done | bytes 278560 | tf_op jit(solution)/shard_map/ppermute | solution.py:501
  13.7 1.7 %collective-permute-start.7 = (f32[2,136,256]{2,1,0:T(8,128)S(1)}, f32[2,136,256]{2,1,0:T(8,128)S(1)}, u32[]{:S(2)}, u32[]{:S(2)}) collective-permute-start(f32[2,136,256]{2,1,0:T(8,128)S(1)} %collective-permute-done.1.refs_2_), channel_id=1, source_target_pairs={{0,4},{4,0},{8,12},{12,8},{16,20},{20,16},{24,28},{28,24},{1,5},{5... | collective-permute-start | bytes 835592 | tf_op jit(solution)/shard_map/ppermute | solution.py:501
  15.4 1.5 %collective-permute-start.2 = (f32[10,3,8,256]{3,2,1,0:T(8,128)S(1)}, f32[10,3,8,256]{3,2,1,0:T(8,128)S(1)}, u32[]{:S(2)}, u32[]{:S(2)}) collective-permute-start(f32[10,3,8,256]{3,2,1,0:T(8,128)S(1)} %get-tuple-element.45), channel_id=1, source_target_pairs={{0,2},{1,3},{2,0},{3,1},{4,6},{5,7},{6,4},{7,5},{8,10},{9,11},{10,... | collective-permute-start | bytes 737288 | tf_op jit(solution)/shard_map/ppermute | solution.py:501
  16.9 0.5 collective-permute-start.3
  17.4 7.1 %collective-permute-done.3.refs_2_ = f32[5,3,8,256]{3,2,1,0:T(8,128)S(1)} collective-permute-done((f32[5,3,8,256]{3,2,1,0:T(8,128)S(1)}, f32[5,3,8,256]{3,2,1,0:T(8,128)S(1)}, u32[]{:S(2)}, u32[]{:S(2)}) %collective-permute-start.3) | collective-permute-done | bytes 122912 | tf_op jit(solution)/shard_map/ppermute | solution.py:501
  24.6 0.0 collective-permute-done.2.refs_1_
  24.6 0.0 collective-permute-done.refs_1_
  24.6 0.0 collective-permute-start.12
  24.6 0.0 collective-permute-done.5.refs_4_
  24.6 0.5 collective-permute-start.6
  25.1 0.1 collective-permute-start.4
  25.2 0.0 collective-permute-done.7.refs_6_
  25.2 0.4 collective-permute-start.8
  25.6 1.6 %collective-permute-start.10 = (f32[10,3,8,256]{3,2,1,0:T(8,128)S(1)}, f32[10,3,8,256]{3,2,1,0:T(8,128)S(1)}, u32[]{:S(2)}, u32[]{:S(2)}) collective-permute-start(f32[10,3,8,256]{3,2,1,0:T(8,128)S(1)} %collective-permute-done.2.refs_1_), channel_id=1, source_target_pairs={{0,8},{4,12},{8,0},{12,4},{16,24},{20,28},{24,16},{28,20},{1,9},{5... | collective-permute-start | bytes 737288 | tf_op jit(solution)/shard_map/ppermute | solution.py:501
  27.2 0.0 collective-permute-done.6.refs_5_
  27.2 0.6 collective-permute-start.11
  27.9 0.0 collective-permute-done.4.refs_3_
  27.9 1.4 %collective-permute-start.9 = (f32[2,64,256]{2,1,0:T(8,128)}, f32[2,64,256]{2,1,0:T(8,128)S(1)}, u32[]{:S(2)}, u32[]{:S(2)}) collective-permute-start(f32[2,64,256]{2,1,0:T(8,128)} %get-tuple-element.63.refs_4_), channel_id=1, source_target_pairs={{0,2},{1,3},{2,0},{3,1},{4,6},{5,7},{6,4},{7,5},{8,10},{9,11},{10,... | collective-permute-start | bytes 393224 | tf_op jit(solution)/shard_map/ppermute | solution.py:501
  29.3 0.0 collective-permute-done.8.refs_7_
  29.3 0.0 copy-start.1
  29.3 1.0 %copy-done.1 = f32[2,136,256]{2,1,0:T(8,128)S(1)} copy-done((f32[2,136,256]{2,1,0:T(8,128)S(1)}, f32[2,136,256]{2,1,0:T(8,128)}, u32[]{:S(2)}) %copy-start.1) | copy-done | bytes 278552
  30.2 0.0 copy-start.2
  30.2 4.2 %own_rows.1 = (f32[16,136,256]{2,1,0:T(8,128)S(1)}, s32[16,128]{1,0:T(8,128)S(1)}, bf16[16,256,256]{2,1,0:T(8,128)(2,1)S(1)}, bf16[16,256,256]{2,1,0:T(8,128)(2,1)S(1)}) custom-call(f32[2,136,256]{2,1,0:T(8,128)S(1)} %copy-done.1, f32[2,136,256]{2,1,0:T(8,128)S(1)} %collective-permute-done.refs_1_, f32[2,136,256]{2,1,0:T(8,128)S(1)} %collective-permute-done.1.refs_2_, ...), custom_call_target="tpu_custom_call" | custom-call | flops 2000000000 | bytes 2000000 | tf_op jit(solution)/shard_map/own_rows/pallas_call | solution.py:170
  34.5 0.0 collective-permute-done.11.refs_4_
  34.5 0.0 collective-permute-done.9.refs_6_
  34.5 0.0 collective-permute-done.10.refs_3_
  34.5 0.0 copy-done.2
  34.5 0.1 collective-permute-start.17
  34.6 0.5 collective-permute-start.18
  35.1 0.1 collective-permute-start.13
  35.2 0.4 collective-permute-start.15
  35.6 0.3 collective-permute-done.17.refs_5_
  35.9 0.1 collective-permute-start.14
  36.1 0.0 collective-permute-done.18.refs_7_
  36.1 0.3 collective-permute-start.16
  36.4 1.3 %own_sums.1.refs_5_ = f32[2,8,256]{2,1,0:T(8,128)S(1)} custom-call(f32[2,136,256]{2,1,0:T(8,128)S(1)} %copy-done.1, f32[2,136,256]{2,1,0:T(8,128)S(1)} %collective-permute-done.refs_1_, f32[2,136,256]{2,1,0:T(8,128)S(1)} %collective-permute-done.1.refs_2_, f32[2,136,256]{2,1,0:T(8,128)S(1)} %collective-permute-done.4.refs_3_, f32[2,64,256]{2,1,0:T(8,128)S(1)} %copy-done.2, ...), custom_call_target="tpu_custom_call" | custom-call | flops 100000000 | bytes 100000 | tf_op jit(solution)/shard_map/own_sums/pallas_call | solution.py:411
  37.7 0.0 collective-permute-done.14.refs_7_
  37.7 0.0 collective-permute-done.13.refs_6_
  37.7 0.0 collective-permute-done.16.refs_9_
  37.7 0.0 collective-permute-done.15.refs_8_
  37.8 0.0 collective-permute-done.12.refs_5_
  37.8 0.2 place.1.refs_4_
  38.0 8.0 %accumulate.1 = (f32[17,8,256]{2,1,0:T(8,128)S(1)}, f32[17,8,256]{2,1,0:T(8,128)S(1)}, f32[17,8,256]{2,1,0:T(8,128)S(1)}, f32[17,8,256]{2,1,0:T(8,128)S(1)}) custom-call(f32[16,136,256]{2,1,0:T(8,128)S(1)} %get-tuple-element.52.refs_0_, s32[16,128]{1,0:T(8,128)S(1)} %get-tuple-element.55.refs_1_, bf16[16,256,256]{2,1,0:T(8,128)(2,1)S(1)} %get-tuple-element.56.refs_2_, ...), custom_call_target="tpu_custom_call" | custom-call | flops 8000000000 | bytes 8000000 | tf_op jit(solution)/shard_map/accumulate/pallas_call | solution.py:334
  46.0 1.6 %collective-permute-start.19 = (f32[17,8,256]{2,1,0:T(8,128)S(1)}, f32[17,8,256]{2,1,0:T(8,128)S(1)}, u32[]{:S(2)}, u32[]{:S(2)}) collective-permute-start(f32[17,8,256]{2,1,0:T(8,128)S(1)} %get-tuple-element.66), channel_id=1, source_target_pairs={{0,8},{4,12},{8,0},{12,4},{16,24},{20,28},{24,16},{28,20},{1,9},{5... | collective-permute-start | bytes 417800 | tf_op jit(solution)/shard_map/ppermute | solution.py:501
  47.6 2.6 %collective-permute-start.20 = (f32[17,8,256]{2,1,0:T(8,128)S(1)}, f32[17,8,256]{2,1,0:T(8,128)S(1)}, u32[]{:S(2)}, u32[]{:S(2)}) collective-permute-start(f32[17,8,256]{2,1,0:T(8,128)S(1)} %get-tuple-element.67), channel_id=1, source_target_pairs={{0,16},{4,20},{8,24},{12,28},{16,0},{20,4},{24,8},{28,12},{1,17},{... | collective-permute-start | bytes 417800 | tf_op jit(solution)/shard_map/ppermute | solution.py:501
  50.2 0.2 collective-permute-start.21
  50.5 3.6 %collective-permute-done.19.refs_1_ = f32[17,8,256]{2,1,0:T(8,128)S(1)} collective-permute-done((f32[17,8,256]{2,1,0:T(8,128)S(1)}, f32[17,8,256]{2,1,0:T(8,128)S(1)}, u32[]{:S(2)}, u32[]{:S(2)}) %collective-permute-start.19) | collective-permute-done | bytes 139296 | tf_op jit(solution)/shard_map/ppermute | solution.py:501
  54.1 7.0 %collective-permute-done.20.refs_2_ = f32[17,8,256]{2,1,0:T(8,128)S(1)} collective-permute-done((f32[17,8,256]{2,1,0:T(8,128)S(1)}, f32[17,8,256]{2,1,0:T(8,128)S(1)}, u32[]{:S(2)}, u32[]{:S(2)}) %collective-permute-start.20) | collective-permute-done | bytes 139296 | tf_op jit(solution)/shard_map/ppermute | solution.py:501
  61.1 0.0 collective-permute-done.21.refs_3_
  61.1 1.6 %collective-permute-start.22 = (f32[2,8,256]{2,1,0:T(8,128)S(1)}, f32[2,8,256]{2,1,0:T(8,128)S(1)}, u32[]{:S(2)}, u32[]{:S(2)}) collective-permute-start(f32[2,8,256]{2,1,0:T(8,128)S(1)} %add_smalls.1.refs_0_), channel_id=1, source_target_pairs={{0,4},{4,0},{8,12},{12,8},{16,20},{20,16},{24,28},{28,24},{1,5},{5... | collective-permute-start | bytes 49160 | tf_op jit(solution)/shard_map/ppermute | solution.py:501
  62.7 0.8 %finish.1 = f32[240,120]{1,0:T(8,128)} custom-call(f32[17,8,256]{2,1,0:T(8,128)S(1)} %get-tuple-element.65.refs_0_, f32[17,8,256]{2,1,0:T(8,128)S(1)} %collective-permute-done.19.refs_1_, f32[17,8,256]{2,1,0:T(8,128)S(1)} %collective-permute-done.20.refs_2_, f32[17,8,256]{2,1,0:T(8,128)S(1)} %collective-permute-done.21.refs_3_), custom_call_target="tpu_custom_call" | custom-call | flops 2000000000 | bytes 2000000 | tf_op jit(solution)/shard_map/finish/pallas_call | solution.py:458
  63.4 1.5 %collective-permute-done.22.refs_1_ = f32[2,8,256]{2,1,0:T(8,128)S(1)} collective-permute-done((f32[2,8,256]{2,1,0:T(8,128)S(1)}, f32[2,8,256]{2,1,0:T(8,128)S(1)}, u32[]{:S(2)}, u32[]{:S(2)}) %collective-permute-start.22) | collective-permute-done | bytes 16416 | tf_op jit(solution)/shard_map/ppermute | solution.py:501
  64.9 1.2 %finish_own.1 = (f32[1,240]{1,0:T(1,128)}, f32[8,8,30]{2,1,0:T(8,128)}) custom-call(f32[2,8,256]{2,1,0:T(8,128)S(1)} %add_smalls.1.refs_0_, f32[2,8,256]{2,1,0:T(8,128)S(1)} %collective-permute-done.22.refs_1_), custom_call_target="tpu_custom_call" | custom-call | tf_op jit(solution)/shard_map/finish_own/pallas_call | solution.py:487
  (1 shorter events, 0.0 us)
Async XLA Ops:
  0.6 1.1 %copy-start = (f32[30,3,8,256]{3,2,1,0:T(8,128)S(1)}, f32[30,3,8,256]{3,2,1,0:T(8,128)}, u32[]{:S(2)}) copy-start(f32[30,3,8,256]{3,2,1,0:T(8,128)} %orbit.1) | copy-start | bytes 2211844
  3.8 9.9 %collective-permute-start.1 = (f32[2,136,256]{2,1,0:T(8,128)}, f32[2,136,256]{2,1,0:T(8,128)S(1)}, u32[]{:S(2)}, u32[]{:S(2)}) collective-permute-start(f32[2,136,256]{2,1,0:T(8,128)} %get-tuple-element.40.refs_0_), channel_id=1, source_target_pairs={{0,2},{1,3},{2,0},{3,1},{4,6},{5,7},{6,4},{7,5},{8,10},{9,11},{10,... | collective-permute-start | bytes 835592 | tf_op jit(solution)/shard_map/ppermute | solution.py:501
  6.8 17.8 %collective-permute-start = (f32[2,136,256]{2,1,0:T(8,128)}, f32[2,136,256]{2,1,0:T(8,128)S(1)}, u32[]{:S(2)}, u32[]{:S(2)}) collective-permute-start(f32[2,136,256]{2,1,0:T(8,128)} %get-tuple-element.40.refs_0_), channel_id=1, source_target_pairs={{0,1},{1,0},{2,3},{3,2},{4,5},{5,4},{6,7},{7,6},{8,9},{9,8},{10,11... | collective-permute-start | bytes 835592 | tf_op jit(solution)/shard_map/ppermute | solution.py:501
  6.8 17.8 %collective-permute-start.5 = (f32[2,136,256]{2,1,0:T(8,128)}, f32[2,136,256]{2,1,0:T(8,128)S(1)}, u32[]{:S(2)}, u32[]{:S(2)}) collective-permute-start(f32[2,136,256]{2,1,0:T(8,128)} %get-tuple-element.40.refs_0_), channel_id=1, source_target_pairs={{0,4},{4,0},{8,12},{12,8},{16,20},{20,16},{24,28},{28,24},{1,5},{5... | collective-permute-start | bytes 835592 | tf_op jit(solution)/shard_map/ppermute | solution.py:501
  13.7 11.5 %collective-permute-start.7 = (f32[2,136,256]{2,1,0:T(8,128)S(1)}, f32[2,136,256]{2,1,0:T(8,128)S(1)}, u32[]{:S(2)}, u32[]{:S(2)}) collective-permute-start(f32[2,136,256]{2,1,0:T(8,128)S(1)} %collective-permute-done.1.refs_2_), channel_id=1, source_target_pairs={{0,4},{4,0},{8,12},{12,8},{16,20},{20,16},{24,28},{28,24},{1,5},{5... | collective-permute-start | bytes 835592 | tf_op jit(solution)/shard_map/ppermute | solution.py:501
  15.4 9.2 %collective-permute-start.2 = (f32[10,3,8,256]{3,2,1,0:T(8,128)S(1)}, f32[10,3,8,256]{3,2,1,0:T(8,128)S(1)}, u32[]{:S(2)}, u32[]{:S(2)}) collective-permute-start(f32[10,3,8,256]{3,2,1,0:T(8,128)S(1)} %get-tuple-element.45), channel_id=1, source_target_pairs={{0,2},{1,3},{2,0},{3,1},{4,6},{5,7},{6,4},{7,5},{8,10},{9,11},{10,... | collective-permute-start | bytes 737288 | tf_op jit(solution)/shard_map/ppermute | solution.py:501
  16.9 7.7 %collective-permute-start.3 = (f32[5,3,8,256]{3,2,1,0:T(8,128)S(1)}, f32[5,3,8,256]{3,2,1,0:T(8,128)S(1)}, u32[]{:S(2)}, u32[]{:S(2)}) collective-permute-start(f32[5,3,8,256]{3,2,1,0:T(8,128)S(1)} %get-tuple-element.46), channel_id=1, source_target_pairs={{0,2},{1,3},{2,0},{3,1},{4,6},{5,7},{6,4},{7,5},{8,10},{9,11},{10,... | collective-permute-start | bytes 368648 | tf_op jit(solution)/shard_map/ppermute | solution.py:501
  24.6 13.2 %collective-permute-start.12 = (f32[30,3,8,256]{3,2,1,0:T(8,128)S(1)}, f32[30,3,8,256]{3,2,1,0:T(8,128)S(1)}, u32[]{:S(2)}, u32[]{:S(2)}) collective-permute-start(f32[30,3,8,256]{3,2,1,0:T(8,128)S(1)} %get-tuple-element.58.refs_8_.refs_0_), channel_id=1, source_target_pairs={{0,1},{1,0},{2,3},{3,2},{4,5},{5,4},{6,7},{7,6},{8,9},{9,8},{10,11... | collective-permute-start | bytes 2211848 | tf_op jit(solution)/shard_map/ppermute | solution.py:501
  24.6 2.6 %collective-permute-start.6 = (f32[2,136,256]{2,1,0:T(8,128)S(1)}, f32[2,136,256]{2,1,0:T(8,128)S(1)}, u32[]{:S(2)}, u32[]{:S(2)}) collective-permute-start(f32[2,136,256]{2,1,0:T(8,128)S(1)} %collective-permute-done.5.refs_4_), channel_id=1, source_target_pairs={{0,1},{1,0},{2,3},{3,2},{4,5},{5,4},{6,7},{7,6},{8,9},{9,8},{10,11... | collective-permute-start | bytes 835592 | tf_op jit(solution)/shard_map/ppermute | solution.py:501
  25.1 2.7 %collective-permute-start.4 = (f32[2,136,256]{2,1,0:T(8,128)S(1)}, f32[2,136,256]{2,1,0:T(8,128)S(1)}, u32[]{:S(2)}, u32[]{:S(2)}) collective-permute-start(f32[2,136,256]{2,1,0:T(8,128)S(1)} %collective-permute-done.1.refs_2_), channel_id=1, source_target_pairs={{0,1},{1,0},{2,3},{3,2},{4,5},{5,4},{6,7},{7,6},{8,9},{9,8},{10,11... | collective-permute-start | bytes 835592 | tf_op jit(solution)/shard_map/ppermute | solution.py:501
  25.2 4.1 %collective-permute-start.8 = (f32[2,136,256]{2,1,0:T(8,128)S(1)}, f32[2,136,256]{2,1,0:T(8,128)S(1)}, u32[]{:S(2)}, u32[]{:S(2)}) collective-permute-start(f32[2,136,256]{2,1,0:T(8,128)S(1)} %collective-permute-done.7.refs_6_), channel_id=1, source_target_pairs={{0,1},{1,0},{2,3},{3,2},{4,5},{5,4},{6,7},{7,6},{8,9},{9,8},{10,11... | collective-permute-start | bytes 835592 | tf_op jit(solution)/shard_map/ppermute | solution.py:501
  25.6 8.9 %collective-permute-start.10 = (f32[10,3,8,256]{3,2,1,0:T(8,128)S(1)}, f32[10,3,8,256]{3,2,1,0:T(8,128)S(1)}, u32[]{:S(2)}, u32[]{:S(2)}) collective-permute-start(f32[10,3,8,256]{3,2,1,0:T(8,128)S(1)} %collective-permute-done.2.refs_1_), channel_id=1, source_target_pairs={{0,8},{4,12},{8,0},{12,4},{16,24},{20,28},{24,16},{28,20},{1,9},{5... | collective-permute-start | bytes 737288 | tf_op jit(solution)/shard_map/ppermute | solution.py:501
  27.2 7.2 %collective-permute-start.11 = (f32[5,3,8,256]{3,2,1,0:T(8,128)S(1)}, f32[5,3,8,256]{3,2,1,0:T(8,128)S(1)}, u32[]{:S(2)}, u32[]{:S(2)}) collective-permute-start(f32[5,3,8,256]{3,2,1,0:T(8,128)S(1)} %collective-permute-done.3.refs_2_), channel_id=1, source_target_pairs={{0,4},{4,0},{8,12},{12,8},{16,20},{20,16},{24,28},{28,24},{1,5},{5... | collective-permute-start | bytes 368648 | tf_op jit(solution)/shard_map/ppermute | solution.py:501
  27.9 6.6 %collective-permute-start.9 = (f32[2,64,256]{2,1,0:T(8,128)}, f32[2,64,256]{2,1,0:T(8,128)S(1)}, u32[]{:S(2)}, u32[]{:S(2)}) collective-permute-start(f32[2,64,256]{2,1,0:T(8,128)} %get-tuple-element.63.refs_4_), channel_id=1, source_target_pairs={{0,2},{1,3},{2,0},{3,1},{4,6},{5,7},{6,4},{7,5},{8,10},{9,11},{10,... | collective-permute-start | bytes 393224 | tf_op jit(solution)/shard_map/ppermute | solution.py:501
  29.3 1.0 %copy-start.1 = (f32[2,136,256]{2,1,0:T(8,128)S(1)}, f32[2,136,256]{2,1,0:T(8,128)}, u32[]{:S(2)}) copy-start(f32[2,136,256]{2,1,0:T(8,128)} %get-tuple-element.40.refs_0_) | copy-start | bytes 835588
  30.2 4.3 %copy-start.2 = (f32[2,64,256]{2,1,0:T(8,128)S(1)}, f32[2,64,256]{2,1,0:T(8,128)}, u32[]{:S(2)}) copy-start(f32[2,64,256]{2,1,0:T(8,128)} %get-tuple-element.63.refs_4_) | copy-start | bytes 393220
  34.5 1.4 %collective-permute-start.17 = (f32[2,64,256]{2,1,0:T(8,128)S(1)}, f32[2,64,256]{2,1,0:T(8,128)S(1)}, u32[]{:S(2)}, u32[]{:S(2)}) collective-permute-start(f32[2,64,256]{2,1,0:T(8,128)S(1)} %copy-done.2), channel_id=1, source_target_pairs={{0,1},{1,0},{2,3},{3,2},{4,5},{5,4},{6,7},{7,6},{8,9},{9,8},{10,11... | collective-permute-start | bytes 393224 | tf_op jit(solution)/shard_map/ppermute | solution.py:501
  34.6 1.5 %collective-permute-start.18 = (f32[2,64,256]{2,1,0:T(8,128)S(1)}, f32[2,64,256]{2,1,0:T(8,128)S(1)}, u32[]{:S(2)}, u32[]{:S(2)}) collective-permute-start(f32[2,64,256]{2,1,0:T(8,128)S(1)} %collective-permute-done.9.refs_6_), channel_id=1, source_target_pairs={{0,1},{1,0},{2,3},{3,2},{4,5},{5,4},{6,7},{7,6},{8,9},{9,8},{10,11... | collective-permute-start | bytes 393224 | tf_op jit(solution)/shard_map/ppermute | solution.py:501
  35.1 2.6 %collective-permute-start.13 = (f32[10,3,8,256]{3,2,1,0:T(8,128)S(1)}, f32[10,3,8,256]{3,2,1,0:T(8,128)S(1)}, u32[]{:S(2)}, u32[]{:S(2)}) collective-permute-start(f32[10,3,8,256]{3,2,1,0:T(8,128)S(1)} %collective-permute-done.2.refs_1_), channel_id=1, source_target_pairs={{0,1},{1,0},{2,3},{3,2},{4,5},{5,4},{6,7},{7,6},{8,9},{9,8},{10,11... | collective-permute-start | bytes 737288 | tf_op jit(solution)/shard_map/ppermute | solution.py:501
  35.2 2.6 %collective-permute-start.15 = (f32[10,3,8,256]{3,2,1,0:T(8,128)S(1)}, f32[10,3,8,256]{3,2,1,0:T(8,128)S(1)}, u32[]{:S(2)}, u32[]{:S(2)}) collective-permute-start(f32[10,3,8,256]{3,2,1,0:T(8,128)S(1)} %collective-permute-done.10.refs_3_), channel_id=1, source_target_pairs={{0,1},{1,0},{2,3},{3,2},{4,5},{5,4},{6,7},{7,6},{8,9},{9,8},{10,11... | collective-permute-start | bytes 737288 | tf_op jit(solution)/shard_map/ppermute | solution.py:501
  35.9 1.8 %collective-permute-start.14 = (f32[5,3,8,256]{3,2,1,0:T(8,128)S(1)}, f32[5,3,8,256]{3,2,1,0:T(8,128)S(1)}, u32[]{:S(2)}, u32[]{:S(2)}) collective-permute-start(f32[5,3,8,256]{3,2,1,0:T(8,128)S(1)} %collective-permute-done.3.refs_2_), channel_id=1, source_target_pairs={{0,1},{1,0},{2,3},{3,2},{4,5},{5,4},{6,7},{7,6},{8,9},{9,8},{10,11... | collective-permute-start | bytes 368648 | tf_op jit(solution)/shard_map/ppermute | solution.py:501
  36.1 1.6 %collective-permute-start.16 = (f32[5,3,8,256]{3,2,1,0:T(8,128)S(1)}, f32[5,3,8,256]{3,2,1,0:T(8,128)S(1)}, u32[]{:S(2)}, u32[]{:S(2)}) collective-permute-start(f32[5,3,8,256]{3,2,1,0:T(8,128)S(1)} %collective-permute-done.11.refs_4_), channel_id=1, source_target_pairs={{0,1},{1,0},{2,3},{3,2},{4,5},{5,4},{6,7},{7,6},{8,9},{9,8},{10,11... | collective-permute-start | bytes 368648 | tf_op jit(solution)/shard_map/ppermute | solution.py:501
  46.0 8.1 %collective-permute-start.19 = (f32[17,8,256]{2,1,0:T(8,128)S(1)}, f32[17,8,256]{2,1,0:T(8,128)S(1)}, u32[]{:S(2)}, u32[]{:S(2)}) collective-permute-start(f32[17,8,256]{2,1,0:T(8,128)S(1)} %get-tuple-element.66), channel_id=1, source_target_pairs={{0,8},{4,12},{8,0},{12,4},{16,24},{20,28},{24,16},{28,20},{1,9},{5... | collective-permute-start | bytes 417800 | tf_op jit(solution)/shard_map/ppermute | solution.py:501
  47.6 13.4 %collective-permute-start.20 = (f32[17,8,256]{2,1,0:T(8,128)S(1)}, f32[17,8,256]{2,1,0:T(8,128)S(1)}, u32[]{:S(2)}, u32[]{:S(2)}) collective-permute-start(f32[17,8,256]{2,1,0:T(8,128)S(1)} %get-tuple-element.67), channel_id=1, source_target_pairs={{0,16},{4,20},{8,24},{12,28},{16,0},{20,4},{24,8},{28,12},{1,17},{... | collective-permute-start | bytes 417800 | tf_op jit(solution)/shard_map/ppermute | solution.py:501
  50.2 10.9 %collective-permute-start.21 = (f32[17,8,256]{2,1,0:T(8,128)S(1)}, f32[17,8,256]{2,1,0:T(8,128)S(1)}, u32[]{:S(2)}, u32[]{:S(2)}) collective-permute-start(f32[17,8,256]{2,1,0:T(8,128)S(1)} %get-tuple-element.68), channel_id=1, source_target_pairs={{0,24},{4,28},{8,16},{12,20},{16,8},{20,12},{24,0},{28,4},{1,25},{... | collective-permute-start | bytes 417800 | tf_op jit(solution)/shard_map/ppermute | solution.py:501
  61.1 3.8 %collective-permute-start.22 = (f32[2,8,256]{2,1,0:T(8,128)S(1)}, f32[2,8,256]{2,1,0:T(8,128)S(1)}, u32[]{:S(2)}, u32[]{:S(2)}) collective-permute-start(f32[2,8,256]{2,1,0:T(8,128)S(1)} %add_smalls.1.refs_0_), channel_id=1, source_target_pairs={{0,4},{4,0},{8,12},{12,8},{16,20},{20,16},{24,28},{28,24},{1,5},{5... | collective-permute-start | bytes 49160 | tf_op jit(solution)/shard_map/ppermute | solution.py:501

commit v9 on v8

--- a/solution.py
+++ b/solution.py
@@ -11,7 +11,6 @@
 PRIOR = 1.0
 PACKED = 128 // KNOTS
 HIGH = lax.Precision.HIGH
-HIGHEST = lax.Precision.HIGHEST
 SMALL_LIMIT = 8 * 1024 * 1024
 MEDIUM_LIMIT = 40 * 1024 * 1024
 HUGE_LIMIT = 56 * 1024 * 1024
@@ -26,16 +25,26 @@
     return pl.BlockSpec(memory_space=pltpu.HBM)
 
 
-def prepare_kernel(*refs):
-    arguments = refs[:6]
-    planes, extra = refs[6:8]
-    sems = refs[14]
-    copies = [pltpu.make_async_copy(arguments[n], refs[8 + n], sems.at[n]) for n in range(6)]
+def turn_of(mine, nx):
+    return lax.rem(lax.div(mine, nx) + lax.rem(mine, nx), 2)
+
+
+def prepare_kernel(parts, nx, *refs):
+    arguments, orbit = refs[:6], refs[6]
+    planes, extra, message = refs[7:10]
+    copied, sems, cut_sem = refs[10:16], refs[16], refs[17]
+    copies = [pltpu.make_async_copy(arguments[n], copied[n], sems.at[n]) for n in range(6)]
     for copy in copies:
         copy.start()
+    size = orbit.shape[0] // parts
+    at = turn_of(lax.axis_index("sta"), nx) * size if parts > 1 else 0
+    head = planes.shape[0] * planes.shape[1]
+    cut = pltpu.make_async_copy(orbit.at[pl.ds(at, size)], message.at[pl.ds(head, size * 24)]
+                                .reshape(size, 3, 8, orbit.shape[3]), cut_sem)
+    cut.start()
     for copy in copies:
         copy.wait()
-    sight, mapping, residual, counts, track, knots = refs[8:14]
+    sight, mapping, residual, counts, track, knots = copied
     stations, _, tracked, _ = sight.shape
     for s in range(stations):
         weight = counts[s].astype(jnp.float32)
@@ -72,22 +81,50 @@
         extra[s, tracked:, :] = jnp.where(weight > 0.0, total / jnp.maximum(weight, 1.0), 0.0)
 
 
-def prepare(*arguments):
+    message[:head] = planes[...].reshape(head, planes.shape[2])
+    cut.wait()
+
+
+def prepare(arguments, orbit, parts, nx):
     stations, _, tracked, epochs = arguments[0].shape
+    rows = 4 * tracked + 8
+    size = orbit.shape[0] // parts
     f32 = jnp.float32
     return pl.pallas_call(
-        prepare_kernel,
+        functools.partial(prepare_kernel, parts, nx),
         out_shape=[
-            jax.ShapeDtypeStruct((stations, 4 * tracked + 8, epochs), f32),
+            jax.ShapeDtypeStruct((stations, rows, epochs), f32),
             jax.ShapeDtypeStruct((stations, 2 * tracked, epochs), f32),
+            jax.ShapeDtypeStruct((stations * rows + size * 24, epochs), f32),
         ],
-        in_specs=[hbm()] * 6,
-        out_specs=[vmem()] * 2,
+        in_specs=[hbm()] * 7,
+        out_specs=[vmem()] * 3,
         scratch_shapes=[pltpu.VMEM(a.shape, a.dtype) for a in arguments]
-        + [pltpu.SemaphoreType.DMA((6,))],
+        + [pltpu.SemaphoreType.DMA((6,)), pltpu.SemaphoreType.DMA],
         compiler_params=pltpu.CompilerParams(vmem_limit_bytes=HUGE_LIMIT),
         name="prepare",
-    )(*arguments)
+    )(*arguments, orbit)
+
+
+def open_kernel(message, planes, partials):
+    head = planes.shape[0] * planes.shape[1]
+    planes[...] = message[:head].reshape(planes.shape)
+    partials[...] = message[head:]
+
+
+def open_message(message, shape):
+    rows, epochs = message.shape
+    return pl.pallas_call(
+        open_kernel,
+        out_shape=[
+            jax.ShapeDtypeStruct(shape, jnp.float32),
+            jax.ShapeDtypeStruct((rows - shape[0] * shape[1], epochs), jnp.float32),
+        ],
+        in_specs=[vmem()],
+        out_specs=[vmem()] * 2,
+        compiler_params=pltpu.CompilerParams(vmem_limit_bytes=SMALL_LIMIT),
+        name="open_message",
+    )(message)
 
 
 def window_start(i, columns, sats, window):
@@ -104,14 +141,15 @@
                            preferred_element_type=jnp.float32)
 
 
-def own_rows_kernel(groups, per, own, width, *refs):
+def own_rows_kernel(groups, per, own, width, base, *refs):
     plane_pieces = refs[:groups]
     orbit = refs[groups]
     planes, track, highs, lows = refs[groups + 1 : groups + 5]
     rows_int, dense_a, dense_b, track_sem = refs[groups + 5 :]
     denses = (dense_a, dense_b)
     stations = groups * per
-    tracked = (planes.shape[1] - 8) // 4
+    rows = planes.shape[1]
+    tracked = (rows - 8) // 4
     epochs = planes.shape[2]
     spare = width - own * 8
     packed = spare // KNOTS
@@ -120,12 +158,14 @@
     for d in range(groups):
         for p in range(per):
             s = d * per + p
-            rows_int[s : s + 1, :] = plane_pieces[d][
-                p, 4 * tracked + 1 : 4 * tracked + 2, :128].astype(jnp.int32)
+            if len(plane_pieces[d].shape) == 3:
+                planes[s] = plane_pieces[d][p]
+            else:
+                planes[s] = plane_pieces[d][p * rows : (p + 1) * rows, :]
+            rows_int[s : s + 1, :] = planes[
+                s, 4 * tracked + 1 : 4 * tracked + 2, :128].astype(jnp.int32)
     to_scalar = pltpu.make_async_copy(rows_int, track, track_sem)
     to_scalar.start()
-    for d in range(groups):
-        planes[d * per : (d + 1) * per] = plane_pieces[d][...]
     to_scalar.wait()
     index = lax.broadcasted_iota(jnp.int32, (spare, epochs), 0)
 
@@ -144,7 +184,7 @@
 
     def finish(s, dense):
         knot = planes[s, 4 * tracked : 4 * tracked + 1, :].astype(jnp.int32)
-        select = (index - lax.rem(s, packed) * KNOTS == knot).astype(jnp.float32)
+        select = (index - lax.rem(base + s, packed) * KNOTS == knot).astype(jnp.float32)
         rows = jnp.concatenate(
             [dense[...].reshape((own + 1) * 8, epochs)[: own * 8], select], 0)
         highs[s], lows[s] = split(rows)
@@ -161,14 +201,14 @@
     lax.fori_loop(0, stations // 2, visit, 0)
 
 
-def own_rows_of(planes, orbit, width):
+def own_rows_of(planes, shape, orbit, width, base):
     groups = len(planes)
-    per, rows, epochs = planes[0].shape
+    per, rows, epochs = shape
     own = orbit.shape[0]
     stations = groups * per
     half = jax.ShapeDtypeStruct((stations, width, epochs), jnp.bfloat16)
     return pl.pallas_call(
-        functools.partial(own_rows_kernel, groups, per, own, width),
+        functools.partial(own_rows_kernel, groups, per, own, width, base),
         out_shape=[
             jax.ShapeDtypeStruct((stations, rows, epochs), jnp.float32),
             jax.ShapeDtypeStruct((stations, 128), jnp.int32),
@@ -190,38 +230,38 @@
 
 
 def place_kernel(own, nx, places, *refs):
-    orbit_pieces, orbit = refs[:-1], refs[-1]
+    pieces, orbit = refs[:-1], refs[-1]
     me = lax.axis_index("sat")
     mine = lax.axis_index("sta")
-    for n, (d, far, start, size) in enumerate(places):
+    for piece, (d, far, head, size) in zip(pieces, places):
         at = (me ^ d) * own
-        if far >= 0:
-            at = at + (turn_of(mine, nx) ^ far) * (own // 2) + start
-        orbit[pl.ds(at, size)] = orbit_pieces[n][...]
-
-
-def place(orbits, places, sats, nx):
-    own = orbits[0].shape[0]
+        if size < own:
+            at = at + (turn_of(mine, nx) ^ far) * size
+        value = piece[...] if len(piece.shape) == 4 else piece[head:]
+        orbit[pl.ds(at, size)] = value.reshape((size,) + orbit.shape[1:])
+
+
+def place(pieces, places, sats, own, nx):
     return pl.pallas_call(
         functools.partial(place_kernel, own, nx, places),
-        out_shape=jax.ShapeDtypeStruct((sats,) + orbits[0].shape[1:], jnp.float32),
-        in_specs=[vmem()] * len(orbits),
+        out_shape=jax.ShapeDtypeStruct((sats,) + pieces[0].shape[1:], jnp.float32),
+        in_specs=[vmem()] * len(pieces),
         out_specs=vmem(),
         compiler_params=pltpu.CompilerParams(vmem_limit_bytes=SMALL_LIMIT),
-        cost_estimate=pl.CostEstimate(
-            flops=int(0.1 * 10**9), bytes_accessed=int(0.1 * 10**6), transcendentals=0),
         name="place",
-    )(*orbits)
-
-
-def main_kernel(groups, per, own, nx, nz, window, *refs):
-    planes, track, highs, lows, orbit, small = refs[:6]
-    outs = refs[6 : 6 + nz]
+    )(*pieces)
+
+
+def main_kernel(own, nx, nz, window, *refs):
+    sets = [refs[4 * n : 4 * n + 4] for n in range(nx)]
+    orbit, small = refs[4 * nx : 4 * nx + 2]
+    refs = refs[4 * nx + 2 :]
+    outs = refs[:nz]
     (acc, stream_a, stream_b, product_a, product_b, tropo_a, tropo_b,
-     spread_tropo) = refs[6 + nz :]
+     spread_tropo) = refs[nz:]
     streams = (stream_a, stream_b)
     products, tropos = (product_a, product_b), (tropo_a, tropo_b)
-    stations = groups * per
+    stations = sets[0][0].shape[0]
     tracked, _, width = product_a.shape
     sats = orbit.shape[0]
     span = tracked * 8
@@ -234,68 +274,72 @@
     acc[...] = jnp.zeros_like(acc)
     spread_tropo[...] = jnp.zeros_like(spread_tropo)
 
-    def build(s, turn):
-        stream = streams[turn]
-        for pair in range(0, tracked, 2):
-            values, mixed = [], []
-            for m in (pair, pair + 1):
+    lane = lax.broadcasted_iota(jnp.int32, (span, 128), 1) - (128 - spare)
+
+    def run(base, planes, track, highs, lows):
+        def build(s, turn):
+            stream = streams[turn]
+            for pair in range(0, tracked, 2):
+                values, mixed = [], []
+                for m in (pair, pair + 1):
+                    k = track[s, m]
+
+                    def row(plane):
+                        return planes[s, pl.ds(plane * tracked + m, 1), :]
+
+                    value = row(0) * orbit[k, 0] + row(1) * orbit[k, 1] + row(2) * orbit[k, 2]
+                    values.append(value)
+                    mixed.append(value * row(3))
+                high, low = split(jnp.concatenate(values, 0))
+                stream[pair * 8 : pair * 8 + 16, :] = high
+                stream[span + pair * 8 : span + pair * 8 + 16, :] = low
+                high, low = split(jnp.concatenate(mixed, 0))
+                stream[2 * span + pair * 8 : 2 * span + pair * 8 + 16, :] = high
+                stream[3 * span + pair * 8 : 3 * span + pair * 8 + 16, :] = low
+
+        def multiply(s, turn):
+            stream = streams[turn]
+            place = lax.rem(base + s, packed) * KNOTS
+            high, low = highs[s], lows[s]
+            result = dot_nt(stream[:span, :], high) + dot_nt(stream[span : 2 * span, :], high)
+            result = result + dot_nt(stream[:span, :], low)
+            products[turn][...] = result.reshape(tracked, 8, width)
+            mixed = dot_nt(stream[2 * span : 3 * span, :], high)
+            mixed = (mixed + dot_nt(stream[3 * span :, :], high))[:, width - 128 :]
+            kept = jnp.logical_and(lane >= place, lane < place + KNOTS)
+            kept = jnp.where(kept, mixed, 0.0)
+            home = lax.rem(base + s, PACKED) * KNOTS
+            kept = pltpu.roll(kept, lax.rem(home + spare - place, 128), 1)
+            tropos[turn][...] = kept.reshape(tracked, 8, 128)
+
+        def scatter(s, turn):
+            slab = lax.div(base + s, PACKED)
+            for m in range(tracked):
                 k = track[s, m]
-
-                def row(plane):
-                    return planes[s, pl.ds(plane * tracked + m, 1), :]
-
-                value = row(0) * orbit[k, 0] + row(1) * orbit[k, 1] + row(2) * orbit[k, 2]
-                values.append(value)
-                mixed.append(value * row(3))
-            high, low = split(jnp.concatenate(values, 0))
-            stream[pair * 8 : pair * 8 + 16, :] = high
-            stream[span + pair * 8 : span + pair * 8 + 16, :] = low
-            high, low = split(jnp.concatenate(mixed, 0))
-            stream[2 * span + pair * 8 : 2 * span + pair * 8 + 16, :] = high
-            stream[3 * span + pair * 8 : 3 * span + pair * 8 + 16, :] = low
-
-    lane = lax.broadcasted_iota(jnp.int32, (span, 128), 1) - (128 - spare)
-
-    def multiply(s, turn):
-        stream = streams[turn]
-        place = lax.rem(s, packed) * KNOTS
-        high, low = highs[s], lows[s]
-        result = dot_nt(stream[:span, :], high) + dot_nt(stream[span : 2 * span, :], high)
-        result = result + dot_nt(stream[:span, :], low)
-        products[turn][...] = result.reshape(tracked, 8, width)
-        mixed = dot_nt(stream[2 * span : 3 * span, :], high)
-        mixed = (mixed + dot_nt(stream[3 * span :, :], high))[:, width - 128 :]
-        kept = jnp.logical_and(lane >= place, lane < place + KNOTS)
-        kept = jnp.where(kept, mixed, 0.0)
-        home = lax.rem(s, PACKED) * KNOTS
-        kept = pltpu.roll(kept, lax.rem(home + spare - place, 128), 1)
-        tropos[turn][...] = kept.reshape(tracked, 8, 128)
-
-    def scatter(s, turn):
-        slab = lax.div(s, PACKED)
-        for m in range(tracked):
-            k = track[s, m]
-            acc[k] = acc[k] - products[turn][m]
-            spread_tropo[slab, k] = spread_tropo[slab, k] + tropos[turn][m]
-
-    build(0, 0)
-    build(1, 1)
-    multiply(0, 0)
-
-    def visit(i, carry):
-        s = 2 * i
-        scatter(s - 2, 0)
-        build(s, 0)
-        multiply(s - 1, 1)
-        scatter(s - 1, 1)
-        build(s + 1, 1)
-        multiply(s, 0)
-        return carry
-
-    lax.fori_loop(1, stations // 2, visit, 0)
-    scatter(stations - 2, 0)
-    multiply(stations - 1, 1)
-    scatter(stations - 1, 1)
+                acc[k] = acc[k] - products[turn][m]
+                spread_tropo[slab, k] = spread_tropo[slab, k] + tropos[turn][m]
+
+        build(0, 0)
+        build(1, 1)
+        multiply(0, 0)
+
+        def visit(i, carry):
+            s = 2 * i
+            scatter(s - 2, 0)
+            build(s, 0)
+            multiply(s - 1, 1)
+            scatter(s - 1, 1)
+            build(s + 1, 1)
+            multiply(s, 0)
+            return carry
+
+        lax.fori_loop(1, stations // 2, visit, 0)
+        scatter(stations - 2, 0)
+        multiply(stations - 1, 1)
+        scatter(stations - 1, 1)
+
+    for n in range(nx):
+        run(n * stations, *sets[n])
 
     outer = jnp.zeros((sats * 8, own * 8), jnp.float32)
     for slab in range(spread_tropo.shape[0]):
@@ -323,19 +367,19 @@
         outs[dz][window + 1] = small[1]
 
 
-def accumulate(groups, planes, track, highs, lows, orbit, small, nx, nz, window):
-    stations, rows, epochs = planes.shape
+def accumulate(sets, orbit, small, own, nz, window):
+    nx = len(sets)
+    stations, rows, epochs = sets[0][0].shape
     sats = orbit.shape[0]
-    own = sats // groups
     tracked = (rows - 8) // 4
-    width = highs.shape[1]
-    slabs = -(-stations // PACKED)
+    width = sets[0][2].shape[1]
+    slabs = -(-nx * stations // PACKED)
     out = jax.ShapeDtypeStruct((window + 2, 8, width), jnp.float32)
     return pl.pallas_call(
-        functools.partial(
-            main_kernel, groups, stations // groups, own, nx, nz, window),
+        functools.partial(main_kernel, own, nx, nz, window),
         out_shape=[out] * nz,
-        in_specs=[vmem(), pl.BlockSpec(memory_space=pltpu.SMEM)] + [vmem()] * 4,
+        in_specs=[vmem(), pl.BlockSpec(memory_space=pltpu.SMEM), vmem(), vmem()] * nx
+        + [vmem()] * 2,
         out_specs=[vmem()] * nz,
         scratch_shapes=[
             pltpu.VMEM((sats, 8, width), jnp.float32),
@@ -348,7 +392,7 @@
         cost_estimate=pl.CostEstimate(
             flops=8 * 10**9, bytes_accessed=8 * 10**6, transcendentals=0),
         name="accumulate",
-    )(planes, track, highs, lows, orbit, small)
+    )(*[part for group in sets for part in group], orbit, small)
 
 
 def blocks_kernel(groups, per, *refs):
@@ -356,6 +400,7 @@
     extra_pieces = refs[groups : 2 * groups]
     orbit, small = refs[2 * groups :]
     tracked = extra_pieces[0].shape[1] // 2
+    rows = 4 * tracked + 8
     epochs = orbit.shape[3]
     width = small.shape[2]
     own = orbit.shape[0]
@@ -365,9 +410,13 @@
     picks, stacks = [], [[] for _ in range(9)]
     for d in range(groups):
         for s in range(per):
-            named = plane_pieces[d][s, 4 * tracked + 1 : 4 * tracked + 2, :tracked]
+            if len(plane_pieces[d].shape) == 3:
+                station = plane_pieces[d][s]
+            else:
+                station = plane_pieces[d][s * rows : (s + 1) * rows, :]
+            named = station[4 * tracked + 1 : 4 * tracked + 2, :tracked]
             picks.append((satellite == named.astype(jnp.int32)).astype(jnp.float32))
-            a = [plane_pieces[d][s, c * tracked : (c + 1) * tracked, :] for c in range(3)]
+            a = [station[c * tracked : (c + 1) * tracked, :] for c in range(3)]
             residual = extra_pieces[d][s, :tracked, :]
             inverse = extra_pieces[d][s, tracked:, :]
             weighted = [v * inverse for v in a]
@@ -407,7 +456,7 @@
 
 def own_sums(planes, extras, orbit, width):
     groups = len(planes)
-    per = planes[0].shape[0]
+    per = extras[0].shape[0]
     return pl.pallas_call(
         functools.partial(blocks_kernel, groups, per),
         out_shape=jax.ShapeDtypeStruct((2, 8, width), jnp.float32),
@@ -475,12 +524,16 @@
         total = total + small[...]
     width = total.shape[2]
     right[...] = total[1, :1, : own * 8] * factor
-    lane = lax.broadcasted_iota(jnp.int32, (width, own), 0)
-    wanted = lax.broadcasted_iota(jnp.int32, (width, own), 1) * 8
+    room = -(-own // 32) * 32
+    lane = lax.broadcasted_iota(jnp.int32, (width, 8 * room), 0)
+    slot = lax.broadcasted_iota(jnp.int32, (width, 8 * room), 1)
+    pick = (lane == slot % room * 8 + slot // room).astype(jnp.bfloat16)
+    high, low = split(total[0])
+    lower = (total[0] - high.astype(jnp.float32) - low.astype(jnp.float32)).astype(jnp.bfloat16)
+    spread = sum(jnp.dot(part, pick, preferred_element_type=jnp.float32)
+                 for part in (high, low, lower))
     for p in range(8):
-        pick = (lane == wanted + p).astype(jnp.float32)
-        blocks[p] = factor * jnp.dot(total[0], pick, precision=HIGHEST,
-                                     preferred_element_type=jnp.float32)
+        blocks[p] = factor * spread[:, p * room : p * room + own]
 
 
 def finish_own(smalls, own, factor):
@@ -499,84 +552,6 @@
 
 def shift(value, axis, size, step):
     return lax.ppermute(value, axis, [(i, i ^ step) for i in range(size)])
-
-
-def gather_planes(value, size, columns_axis, nx):
-    even = {(0, 0): value}
-    for d in range(2, size, 2):
-        even[0, d] = shift(value, "sat", size, d)
-    for dx in range(1, nx):
-        for d in range(0, size, 2):
-            even[dx, d] = shift(even[0, d], "sta", columns_axis, dx)
-    pieces = []
-    for dx in range(nx):
-        for d in range(0, size, 2):
-            pieces += [even[dx, d], shift(even[dx, d], "sat", size, 1)]
-    return pieces
-
-
-def turn_of(mine, nx):
-    return lax.rem(lax.div(mine, nx) + lax.rem(mine, nx), 2)
-
-
-def cut_kernel(nx, orbit, first, second, copy):
-    half = orbit.shape[0] // 2
-    lead = first.shape[0]
-    at = turn_of(lax.axis_index("sta"), nx) * half
-    first[...] = orbit[pl.ds(at, lead)]
-    second[...] = orbit[pl.ds(at + lead, half - lead)]
-    copy[...] = orbit[...]
-
-
-def cut_parts(orbit, columns_axis, nx):
-    own = orbit.shape[0]
-    if own % 2 or nx % 2 or (columns_axis // nx) % 2:
-        return [], orbit
-    half = own // 2
-    lead = half * 2 // 3
-    *parts, orbit = pl.pallas_call(
-        functools.partial(cut_kernel, nx),
-        out_shape=[
-            jax.ShapeDtypeStruct((n,) + orbit.shape[1:], jnp.float32)
-            for n in (lead, half - lead, own)
-        ],
-        in_specs=[vmem()],
-        out_specs=[vmem()] * 3,
-        compiler_params=pltpu.CompilerParams(vmem_limit_bytes=SMALL_LIMIT),
-        name="cut_parts",
-    )(orbit)
-    return parts, orbit
-
-
-def fetch_orbit(orbit, parts, size, columns_axis, nx):
-    own = orbit.shape[0]
-    if not parts:
-        near = [orbit] + [shift(orbit, "sat", size, d) for d in range(2, size, 2)]
-        return near, [], []
-    near, far = [orbit], []
-    for d in range(2, size, 2):
-        straight = [shift(part, "sat", size, d) for part in parts]
-        near += straight
-        far += [shift(straight[0], "sta", columns_axis, nx),
-                shift(straight[1], "sta", columns_axis, 1)]
-    return near, far, [part.shape[0] for part in parts]
-
-
-def pair_orbit(near, far, sizes, size):
-    if not far:
-        own = near[0].shape[0]
-        pieces = list(near)
-        places = [(d, -1, 0, own) for d in range(0, size, 2)]
-    else:
-        pieces, places = [near[0]], [(0, -1, 0, near[0].shape[0])]
-        for n, d in enumerate(range(2, size, 2)):
-            pieces += [near[1 + 2 * n], near[2 + 2 * n], far[2 * n], far[2 * n + 1]]
-            places += [(d, half, start, count) for half in (0, 1)
-                       for start, count in ((0, sizes[0]), (sizes[0], sizes[1]))]
-    for piece, (d, *rest) in list(zip(pieces, places)):
-        pieces.append(shift(piece, "sat", size, 1))
-        places.append((d + 1, *rest))
-    return pieces, tuple(places)
 
 
 def shards(sight, mapping, residual, counts, track, knots, orbit):
@@ -595,28 +570,59 @@
         -(-(((columns * i) % 8) + columns) // 8) for i in range(columns_axis)
     )
 
-    parts, orbit = cut_parts(orbit, columns_axis, nx)
-    planes, extra = prepare(sight, mapping, residual, counts, track, knots)
-    if parts:
-        planes, *parts = lax.optimization_barrier((planes, *parts))
-    plane_pieces = gather_planes(planes, group, columns_axis, nx)
-    if parts:
-        *parts, plane_pieces[2] = lax.optimization_barrier((*parts, plane_pieces[2]))
-    near, far, sizes = fetch_orbit(orbit, parts, group, columns_axis, nx)
-    extra, *near = lax.optimization_barrier((extra, *near))
-    plane_pieces[1], *near = lax.optimization_barrier((plane_pieces[1], *near))
-    own_planes, own_track, highs, lows = own_rows_of(plane_pieces, orbit, width)
-    extra_even = [extra] + [shift(extra, "sat", group, d) for d in range(2, group, 2)]
-    own_track, *held = lax.optimization_barrier((own_track, *extra_even, *far))
-    extra_even, far = held[: group // 2], held[group // 2 :]
-    orbit_pieces, places = pair_orbit(near, far, sizes, group)
-    extra_pieces = []
-    for piece in extra_even:
-        extra_pieces += [piece, shift(piece, "sat", group, 1)]
-    small = own_sums(plane_pieces[:group], extra_pieces, orbit, width)
-    sums = accumulate(
-        group, own_planes, own_track, highs, lows, place(orbit_pieces, places, sats, nx),
-        small, nx, nz, window)
+    parts = 2 if own % 2 == 0 and nz % 2 == 0 else 1
+    planes, extra, message = prepare(
+        (sight, mapping, residual, counts, track, knots), orbit, parts, nx)
+    head = planes.shape[0] * planes.shape[1]
+
+    def core(value):
+        return shift(value, "sat", group, 1)
+
+    early = [planes, orbit, extra]
+    early += [core(value) for value in early]
+    beside = {dx: shift(planes, "sta", columns_axis, dx) for dx in range(1, nx)}
+    crossed = {dx: core(value) for dx, value in beside.items()}
+    messages = {d: shift(message, "sat", group, d) for d in range(2, group, 2)}
+    (early, beside, crossed, messages) = lax.optimization_barrier(
+        (early, beside, crossed, messages))
+    _, orbit, extra, other_planes, other_orbit, other_extra = early
+
+    pieces = [[(0, planes), (1, other_planes)]]
+    pieces += [[(0, beside[dx]), (1, crossed[dx])] for dx in range(1, nx)]
+    partials = [(0, 0, orbit), (1, 0, other_orbit)]
+    extras = {0: extra, 1: other_extra}
+    far = {}
+    for d, arrived in messages.items():
+        value, part = open_message(arrived, planes.shape)
+        across = core(arrived)
+        partials += [(d, 0, arrived), (d + 1, 0, across)]
+        if parts > 1:
+            far[d] = shift(part, "sta", columns_axis, nx)
+        for dx in range(1, nx):
+            passed = shift(value, "sta", columns_axis, dx)
+            pieces[dx] += [(d, passed), (d + 1, core(passed))]
+        held, _ = lax.optimization_barrier((extra, value))
+        extras[d], across = lax.optimization_barrier((shift(held, "sat", group, d), across))
+        pieces[0] += [(d, arrived), (d + 1, across)]
+    sets = [own_rows_of([value for _, value in pieces[0]], planes.shape, orbit, width, 0)]
+    for d in range(2, group, 2):
+        held, _ = lax.optimization_barrier((extras[d], sets[0][1]))
+        extras[d + 1] = core(held)
+    small = own_sums([value for _, value in pieces[0]],
+                     [extras[d] for d, _ in pieces[0]], orbit, width)
+    far, small = lax.optimization_barrier((far, small))
+    for d, value in far.items():
+        partials += [(d, 1, value), (d + 1, 1, core(value))]
+    for dx in range(1, nx):
+        sets.append(own_rows_of(
+            [value for _, value in pieces[dx]], planes.shape, orbit, width,
+            dx * group * stations))
+    places = tuple((d, turn, head, own if value.ndim == 4 else own // parts)
+                   for d, turn, value in partials)
+    places = tuple((d, turn, head if value.shape[0] == message.shape[0] else 0, size)
+                   for (d, turn, head, size), (_, _, value) in zip(places, partials))
+    every = place([value for _, _, value in partials], places, sats, own, nx)
+    sums = accumulate(sets, every, small, own, nz, window)
     final = [sums[0]] + [
         shift(sums[d], "sta", columns_axis, d * nx) for d in range(1, nz)
     ]

time: 66.3 us -> 66.1 us (level)
  starting transfers between devices: 20.5 us -> 15.5 us
  waiting for transfers between devices: 25 us -> 29.8 us
  Pallas kernels: 17.7 us -> 18.9 us
  local copies, waits for them, and re-layouts: 2.07 us -> 0.96 us
    ppermute x23 -> x17, starting transfers between devices: 20.5 us -> 15.5 us  [shift(): return lax.ppermute(value, axis, [(i, i ^ step) for i in range(size)])]
    ppermute x23 -> x17, waiting for transfers between devices: 25 us -> 29.8 us  [shift(): return lax.ppermute(value, axis, [(i, i ^ step) for i in range(size)])]
    pallas_call x1 -> x2, Pallas kernels: 4.22 us -> 5.67 us  [own_rows_of(): pl.pallas_call(functools.partial(own_rows_kernel, groups, per, own, width...]
    unnamed x6, local copies, waits for them, and re-layouts: 2.07 us -> 0.96 us
  transfers between devices with their start and end apart: 23 -> 17, of which waited for: 6 -> 10; matrix products, arithmetic and copies ran while one was open for 0% -> 0% of each run, Pallas kernels for 9% -> 15%
where the time goes in v9:
time: 66.1 us; the launch traced here: 65.9 us
  waiting for transfers between devices  29.8 us (45%)
  Pallas kernels  18.9 us (29%)
  starting transfers between devices  15.5 us (23%)
  local copies, waits for them, and re-layouts  0.96 us (1%)
  between operations  0.73 us (1%)
    ppermute x17, waiting for transfers between devices, shift(): return lax.ppermute(value, axis, [(i, i ^ step) for i in range(size)])  29.8 us
    ppermute x17, starting transfers between devices, shift(): return lax.ppermute(value, axis, [(i, i ^ step) for i in range(size)])  15.5 us
    pallas_call x1, Pallas kernels, accumulate(): pl.pallas_call(functools.partial(main_kernel, own, nx, nz, window), out_s...  7.78 us
    pallas_call x2, Pallas kernels, own_rows_of(): pl.pallas_call(functools.partial(own_rows_kernel, groups, per, own, width...  5.67 us
    pallas_call x1, Pallas kernels, prepare(): pl.pallas_call(functools.partial(prepare_kernel, parts, nx), out_shape=[j...  2.29 us
  transfers between devices with their start and end apart: 17, of which 10 were waited for; matrix products, arithmetic and copies ran while one was open for 0% of the time, Pallas kernels for 15%

profile of v9, /device:TPU:0, one launch (start us, length us, event | category | flops | bytes accessed | tf_op | source)
XLA Modules:
  0.0 65.9 jit_solution(15034011064022768890)
XLA Ops:
  0.6 0.0 copy-start
  0.6 0.5 collective-permute-start.1
  1.2 2.3 %prepare.1 = (f32[2,136,256]{2,1,0:T(8,128)}, f32[2,64,256]{2,1,0:T(8,128)}, f32[632,256]{1,0:T(8,128)}) custom-call(f32[2,3,32,256]{3,2,1,0:T(8,128)} %refs_0_.1, f32[2,32,256]{2,1,0:T(8,128)} %refs_1_.1, f32[2,32,256]{2,1,0:T(8,128)} %refs_2_.1, s32[2,32,256]{2,1,0:T(8,128)} %refs_3_.1, s32[2,32]{1,0:T(2,128)} %refs_4_.1, s32[2,256]{1,0:T(2,128)} %refs_5_.1, ...), custom_call_target="tpu_custom_call" | custom-call | tf_op jit(solution)/shard_map/prepare/pallas_call | solution.py:93
  3.5 2.6 %collective-permute-start.5 = (f32[632,256]{1,0:T(8,128)}, f32[632,256]{1,0:T(8,128)S(1)}, u32[]{:S(2)}, u32[]{:S(2)}) collective-permute-start(f32[632,256]{1,0:T(8,128)} %get-tuple-element.38), channel_id=1, source_target_pairs={{0,2},{1,3},{2,0},{3,1},{4,6},{5,7},{6,4},{7,5},{8,10},{9,11},{10,... | collective-permute-start | bytes 1941512 | tf_op jit(solution)/shard_map/ppermute | solution.py:554
  6.1 1.5 %collective-permute-start.3 = (f32[2,136,256]{2,1,0:T(8,128)}, f32[2,136,256]{2,1,0:T(8,128)S(1)}, u32[]{:S(2)}, u32[]{:S(2)}) collective-permute-start(f32[2,136,256]{2,1,0:T(8,128)} %get-tuple-element.36.refs_0_), channel_id=1, source_target_pairs={{0,4},{4,0},{8,12},{12,8},{16,20},{20,16},{24,28},{28,24},{1,5},{5... | collective-permute-start | bytes 835592 | tf_op jit(solution)/shard_map/ppermute | solution.py:554
  7.6 0.0 collective-permute-start
  7.6 7.4 %collective-permute-done.3.refs_0_ = f32[2,136,256]{2,1,0:T(8,128)S(1)} collective-permute-done((f32[2,136,256]{2,1,0:T(8,128)}, f32[2,136,256]{2,1,0:T(8,128)S(1)}, u32[]{:S(2)}, u32[]{:S(2)}) %collective-permute-start.3) | collective-permute-done | bytes 278560 | tf_op jit(solution)/shard_map/ppermute | solution.py:554
  15.0 0.0 collective-permute-start.4
  15.0 0.5 collective-permute-start.2
  15.6 1.3 %collective-permute-done.2.refs_5_ = f32[2,64,256]{2,1,0:T(8,128)S(1)} collective-permute-done((f32[2,64,256]{2,1,0:T(8,128)}, f32[2,64,256]{2,1,0:T(8,128)S(1)}, u32[]{:S(2)}, u32[]{:S(2)}) %collective-permute-start.2) | collective-permute-done | bytes 131104 | tf_op jit(solution)/shard_map/ppermute | solution.py:554
  16.8 0.0 collective-permute-done.refs_1_
  16.8 0.0 collective-permute-done.4.refs_1_
  16.8 4.6 %collective-permute-done.5.message.refs_2_ = f32[632,256]{1,0:T(8,128)S(1)} collective-permute-done((f32[632,256]{1,0:T(8,128)}, f32[632,256]{1,0:T(8,128)S(1)}, u32[]{:S(2)}, u32[]{:S(2)}) %collective-permute-start.5) | collective-permute-done | bytes 647200 | tf_op jit(solution)/shard_map/ppermute | solution.py:554
  21.5 0.0 collective-permute-done.1.refs_1_
  21.5 0.0 collective-permute-start.7
  21.5 1.8 %collective-permute-start.6 = (f32[2,64,256]{2,1,0:T(8,128)}, f32[2,64,256]{2,1,0:T(8,128)S(1)}, u32[]{:S(2)}, u32[]{:S(2)}) collective-permute-start(f32[2,64,256]{2,1,0:T(8,128)} %get-tuple-element.43.refs_4_), channel_id=1, source_target_pairs={{0,2},{1,3},{2,0},{3,1},{4,6},{5,7},{6,4},{7,5},{8,10},{9,11},{10,... | collective-permute-start | bytes 393224 | tf_op jit(solution)/shard_map/ppermute | solution.py:554
  23.3 1.5 %collective-permute-start.8 = (f32[2,136,256]{2,1,0:T(8,128)S(1)}, f32[2,136,256]{2,1,0:T(8,128)S(1)}, u32[]{:S(2)}, u32[]{:S(2)}) collective-permute-start(f32[2,136,256]{2,1,0:T(8,128)S(1)} %get-tuple-element.42), channel_id=1, source_target_pairs={{0,4},{4,0},{8,12},{12,8},{16,20},{20,16},{24,28},{28,24},{1,5},{5... | collective-permute-start | bytes 835592 | tf_op jit(solution)/shard_map/ppermute | solution.py:554
  24.8 1.6 %collective-permute-start.10 = (f32[360,256]{1,0:T(8,128)S(1)}, f32[360,256]{1,0:T(8,128)S(1)}, u32[]{:S(2)}, u32[]{:S(2)}) collective-permute-start(f32[360,256]{1,0:T(8,128)S(1)} %get-tuple-element.57), channel_id=1, source_target_pairs={{0,8},{4,12},{8,0},{12,4},{16,24},{20,28},{24,16},{28,20},{1,9},{5... | collective-permute-start | bytes 1105928 | tf_op jit(solution)/shard_map/ppermute | solution.py:554
  26.4 1.3 %collective-permute-done.6.refs_6_ = f32[2,64,256]{2,1,0:T(8,128)S(1)} collective-permute-done((f32[2,64,256]{2,1,0:T(8,128)}, f32[2,64,256]{2,1,0:T(8,128)S(1)}, u32[]{:S(2)}, u32[]{:S(2)}) %collective-permute-start.6) | collective-permute-done | bytes 131104 | tf_op jit(solution)/shard_map/ppermute | solution.py:554
  27.7 0.0 collective-permute-done.7.refs_3_
  27.7 0.0 copy-done
  27.7 0.0 copy-start.1
  27.7 1.0 %copy-done.1 = f32[2,136,256]{2,1,0:T(8,128)S(1)} copy-done((f32[2,136,256]{2,1,0:T(8,128)S(1)}, f32[2,136,256]{2,1,0:T(8,128)}, u32[]{:S(2)}) %copy-start.1) | copy-done | bytes 278552
  28.7 0.0 copy-start.2
  28.7 2.8 %own_rows.2 = (f32[8,136,256]{2,1,0:T(8,128)S(1)}, s32[8,128]{1,0:T(8,128)S(1)}, bf16[8,256,256]{2,1,0:T(8,128)(2,1)S(1)}, bf16[8,256,256]{2,1,0:T(8,128)(2,1)S(1)}) custom-call(f32[2,136,256]{2,1,0:T(8,128)S(1)} %copy-done.1, f32[2,136,256]{2,1,0:T(8,128)S(1)} %collective-permute-done.refs_1_, f32[632,256]{1,0:T(8,128)S(1)} %collective-permute-done.5.message.refs_2_, ...), custom_call_target="tpu_custom_call" | custom-call | flops 2000000000 | bytes 2000000 | tf_op jit(solution)/shard_map/own_rows/pallas_call | solution.py:210
  31.5 0.1 collective-permute-start.11
  31.6 0.5 collective-permute-done.8.refs_2_
  32.1 0.0 collective-permute-start.9
  32.1 0.8 %collective-permute-done.11.refs_7_ = f32[2,64,256]{2,1,0:T(8,128)S(1)} collective-permute-done((f32[2,64,256]{2,1,0:T(8,128)S(1)}, f32[2,64,256]{2,1,0:T(8,128)S(1)}, u32[]{:S(2)}, u32[]{:S(2)}) %collective-permute-start.11) | collective-permute-done | bytes 131104 | tf_op jit(solution)/shard_map/ppermute | solution.py:554
  32.9 0.0 copy-done.2
  32.9 1.3 %own_sums.1.refs_9_ = f32[2,8,256]{2,1,0:T(8,128)S(1)} custom-call(f32[2,136,256]{2,1,0:T(8,128)S(1)} %copy-done.1, f32[2,136,256]{2,1,0:T(8,128)S(1)} %collective-permute-done.refs_1_, f32[632,256]{1,0:T(8,128)S(1)} %collective-permute-done.5.message.refs_2_, f32[632,256]{1,0:T(8,128)S(1)} %collective-permute-done.7.refs_3_, f32[2,64,256]{2,1,0:T(8,128)S(1)} %copy-done.2, ...), custom_call_target="tpu_custom_call" | custom-call | flops 100000000 | bytes 100000 | tf_op jit(solution)/shard_map/own_sums/pallas_call | solution.py:460
  34.2 1.0 %collective-permute-done.10.refs_4_ = f32[360,256]{1,0:T(8,128)S(1)} collective-permute-done((f32[360,256]{1,0:T(8,128)S(1)}, f32[360,256]{1,0:T(8,128)S(1)}, u32[]{:S(2)}, u32[]{:S(2)}) %collective-permute-start.10) | collective-permute-done | bytes 368672 | tf_op jit(solution)/shard_map/ppermute | solution.py:554
  35.3 0.0 collective-permute-start.12
  35.3 0.0 collective-permute-done.9.refs_3_
  35.3 2.9 %own_rows.3 = (f32[8,136,256]{2,1,0:T(8,128)S(1)}, s32[8,128]{1,0:T(8,128)S(1)}, bf16[8,256,256]{2,1,0:T(8,128)(2,1)S(1)}, bf16[8,256,256]{2,1,0:T(8,128)(2,1)S(1)}) custom-call(f32[2,136,256]{2,1,0:T(8,128)S(1)} %collective-permute-done.3.refs_0_, f32[2,136,256]{2,1,0:T(8,128)S(1)} %collective-permute-done.4.refs_1_, ...), custom_call_target="tpu_custom_call" | custom-call | flops 2000000000 | bytes 2000000 | tf_op jit(solution)/shard_map/own_rows/pallas_call | solution.py:210
  38.1 0.0 collective-permute-done.12.refs_5_
  38.1 0.2 place.1.refs_8_
  38.4 7.8 %accumulate.1 = (f32[17,8,256]{2,1,0:T(8,128)S(1)}, f32[17,8,256]{2,1,0:T(8,128)S(1)}, f32[17,8,256]{2,1,0:T(8,128)S(1)}, f32[17,8,256]{2,1,0:T(8,128)S(1)}) custom-call(f32[8,136,256]{2,1,0:T(8,128)S(1)} %get-tuple-element.46.refs_0_, s32[8,128]{1,0:T(8,128)S(1)} %get-tuple-element.47.refs_1_, bf16[8,256,256]{2,1,0:T(8,128)(2,1)S(1)} %get-tuple-element.48.refs_2_, ...), custom_call_target="tpu_custom_call" | custom-call | flops 8000000000 | bytes 8000000 | tf_op jit(solution)/shard_map/accumulate/pallas_call | solution.py:378
  46.1 1.7 %collective-permute-start.13 = (f32[17,8,256]{2,1,0:T(8,128)S(1)}, f32[17,8,256]{2,1,0:T(8,128)S(1)}, u32[]{:S(2)}, u32[]{:S(2)}) collective-permute-start(f32[17,8,256]{2,1,0:T(8,128)S(1)} %get-tuple-element.64), channel_id=1, source_target_pairs={{0,8},{4,12},{8,0},{12,4},{16,24},{20,28},{24,16},{28,20},{1,9},{5... | collective-permute-start | bytes 417800 | tf_op jit(solution)/shard_map/ppermute | solution.py:554
  47.8 2.6 %collective-permute-start.14 = (f32[17,8,256]{2,1,0:T(8,128)S(1)}, f32[17,8,256]{2,1,0:T(8,128)S(1)}, u32[]{:S(2)}, u32[]{:S(2)}) collective-permute-start(f32[17,8,256]{2,1,0:T(8,128)S(1)} %get-tuple-element.65), channel_id=1, source_target_pairs={{0,16},{4,20},{8,24},{12,28},{16,0},{20,4},{24,8},{28,12},{1,17},{... | collective-permute-start | bytes 417800 | tf_op jit(solution)/shard_map/ppermute | solution.py:554
  50.4 0.2 collective-permute-start.15
  50.6 4.3 %collective-permute-done.13.refs_1_ = f32[17,8,256]{2,1,0:T(8,128)S(1)} collective-permute-done((f32[17,8,256]{2,1,0:T(8,128)S(1)}, f32[17,8,256]{2,1,0:T(8,128)S(1)}, u32[]{:S(2)}, u32[]{:S(2)}) %collective-permute-start.13) | collective-permute-done | bytes 139296 | tf_op jit(solution)/shard_map/ppermute | solution.py:554
  54.9 6.4 %collective-permute-done.14.refs_2_ = f32[17,8,256]{2,1,0:T(8,128)S(1)} collective-permute-done((f32[17,8,256]{2,1,0:T(8,128)S(1)}, f32[17,8,256]{2,1,0:T(8,128)S(1)}, u32[]{:S(2)}, u32[]{:S(2)}) %collective-permute-start.14) | collective-permute-done | bytes 139296 | tf_op jit(solution)/shard_map/ppermute | solution.py:554
  61.2 0.0 collective-permute-done.15.refs_3_
  61.3 1.0 %collective-permute-start.16 = (f32[2,8,256]{2,1,0:T(8,128)S(1)}, f32[2,8,256]{2,1,0:T(8,128)S(1)}, u32[]{:S(2)}, u32[]{:S(2)}) collective-permute-start(f32[2,8,256]{2,1,0:T(8,128)S(1)} %add_smalls.1.refs_0_), channel_id=1, source_target_pairs={{0,4},{4,0},{8,12},{12,8},{16,20},{20,16},{24,28},{28,24},{1,5},{5... | collective-permute-start | bytes 49160 | tf_op jit(solution)/shard_map/ppermute | solution.py:554
  62.2 0.8 %finish.1 = f32[240,120]{1,0:T(8,128)} custom-call(f32[17,8,256]{2,1,0:T(8,128)S(1)} %get-tuple-element.63.refs_0_, f32[17,8,256]{2,1,0:T(8,128)S(1)} %collective-permute-done.13.refs_1_, f32[17,8,256]{2,1,0:T(8,128)S(1)} %collective-permute-done.14.refs_2_, f32[17,8,256]{2,1,0:T(8,128)S(1)} %collective-permute-done.15.refs_3_), custom_call_target="tpu_custom_call" | custom-call | flops 2000000000 | bytes 2000000 | tf_op jit(solution)/shard_map/finish/pallas_call | solution.py:507
  63.0 2.1 %collective-permute-done.16.refs_1_ = f32[2,8,256]{2,1,0:T(8,128)S(1)} collective-permute-done((f32[2,8,256]{2,1,0:T(8,128)S(1)}, f32[2,8,256]{2,1,0:T(8,128)S(1)}, u32[]{:S(2)}, u32[]{:S(2)}) %collective-permute-start.16) | collective-permute-done | bytes 16416 | tf_op jit(solution)/shard_map/ppermute | solution.py:554
  65.1 0.9 %finish_own.1 = (f32[1,240]{1,0:T(1,128)}, f32[8,8,30]{2,1,0:T(8,128)}) custom-call(f32[2,8,256]{2,1,0:T(8,128)S(1)} %add_smalls.1.refs_0_, f32[2,8,256]{2,1,0:T(8,128)S(1)} %collective-permute-done.16.refs_1_), custom_call_target="tpu_custom_call" | custom-call | tf_op jit(solution)/shard_map/finish_own/pallas_call | solution.py:540
  (2 shorter events, 0.0 us)
Async XLA Ops:
  0.6 27.1 %copy-start = (f32[30,3,8,256]{3,2,1,0:T(8,128)S(1)}, f32[30,3,8,256]{3,2,1,0:T(8,128)}, u32[]{:S(2)}) copy-start(f32[30,3,8,256]{3,2,1,0:T(8,128)} %refs_0_.2) | copy-start | bytes 2211844
  0.6 20.8 %collective-permute-start.1 = (f32[30,3,8,256]{3,2,1,0:T(8,128)}, f32[30,3,8,256]{3,2,1,0:T(8,128)S(1)}, u32[]{:S(2)}, u32[]{:S(2)}) collective-permute-start(f32[30,3,8,256]{3,2,1,0:T(8,128)} %refs_0_.2), channel_id=1, source_target_pairs={{0,1},{1,0},{2,3},{3,2},{4,5},{5,4},{6,7},{7,6},{8,9},{9,8},{10,11... | collective-permute-start | bytes 2211848 | tf_op jit(solution)/shard_map/ppermute | solution.py:554
  3.5 18.0 %collective-permute-start.5 = (f32[632,256]{1,0:T(8,128)}, f32[632,256]{1,0:T(8,128)S(1)}, u32[]{:S(2)}, u32[]{:S(2)}) collective-permute-start(f32[632,256]{1,0:T(8,128)} %get-tuple-element.38), channel_id=1, source_target_pairs={{0,2},{1,3},{2,0},{3,1},{4,6},{5,7},{6,4},{7,5},{8,10},{9,11},{10,... | collective-permute-start | bytes 1941512 | tf_op jit(solution)/shard_map/ppermute | solution.py:554
  6.1 8.9 %collective-permute-start.3 = (f32[2,136,256]{2,1,0:T(8,128)}, f32[2,136,256]{2,1,0:T(8,128)S(1)}, u32[]{:S(2)}, u32[]{:S(2)}) collective-permute-start(f32[2,136,256]{2,1,0:T(8,128)} %get-tuple-element.36.refs_0_), channel_id=1, source_target_pairs={{0,4},{4,0},{8,12},{12,8},{16,20},{20,16},{24,28},{28,24},{1,5},{5... | collective-permute-start | bytes 835592 | tf_op jit(solution)/shard_map/ppermute | solution.py:554
  7.6 9.2 %collective-permute-start = (f32[2,136,256]{2,1,0:T(8,128)}, f32[2,136,256]{2,1,0:T(8,128)S(1)}, u32[]{:S(2)}, u32[]{:S(2)}) collective-permute-start(f32[2,136,256]{2,1,0:T(8,128)} %get-tuple-element.36.refs_0_), channel_id=1, source_target_pairs={{0,1},{1,0},{2,3},{3,2},{4,5},{5,4},{6,7},{7,6},{8,9},{9,8},{10,11... | collective-permute-start | bytes 835592 | tf_op jit(solution)/shard_map/ppermute | solution.py:554
  15.0 1.8 %collective-permute-start.4 = (f32[2,136,256]{2,1,0:T(8,128)S(1)}, f32[2,136,256]{2,1,0:T(8,128)S(1)}, u32[]{:S(2)}, u32[]{:S(2)}) collective-permute-start(f32[2,136,256]{2,1,0:T(8,128)S(1)} %collective-permute-done.3.refs_0_), channel_id=1, source_target_pairs={{0,1},{1,0},{2,3},{3,2},{4,5},{5,4},{6,7},{7,6},{8,9},{9,8},{10,11... | collective-permute-start | bytes 835592 | tf_op jit(solution)/shard_map/ppermute | solution.py:554
  15.0 1.8 %collective-permute-start.2 = (f32[2,64,256]{2,1,0:T(8,128)}, f32[2,64,256]{2,1,0:T(8,128)S(1)}, u32[]{:S(2)}, u32[]{:S(2)}) collective-permute-start(f32[2,64,256]{2,1,0:T(8,128)} %get-tuple-element.43.refs_4_), channel_id=1, source_target_pairs={{0,1},{1,0},{2,3},{3,2},{4,5},{5,4},{6,7},{7,6},{8,9},{9,8},{10,11... | collective-permute-start | bytes 393224 | tf_op jit(solution)/shard_map/ppermute | solution.py:554
  21.5 6.2 %collective-permute-start.7 = (f32[632,256]{1,0:T(8,128)S(1)}, f32[632,256]{1,0:T(8,128)S(1)}, u32[]{:S(2)}, u32[]{:S(2)}) collective-permute-start(f32[632,256]{1,0:T(8,128)S(1)} %collective-permute-done.5.message.refs_2_), channel_id=1, source_target_pairs={{0,1},{1,0},{2,3},{3,2},{4,5},{5,4},{6,7},{7,6},{8,9},{9,8},{10,11... | collective-permute-start | bytes 1941512 | tf_op jit(solution)/shard_map/ppermute | solution.py:554
  21.5 6.2 %collective-permute-start.6 = (f32[2,64,256]{2,1,0:T(8,128)}, f32[2,64,256]{2,1,0:T(8,128)S(1)}, u32[]{:S(2)}, u32[]{:S(2)}) collective-permute-start(f32[2,64,256]{2,1,0:T(8,128)} %get-tuple-element.43.refs_4_), channel_id=1, source_target_pairs={{0,2},{1,3},{2,0},{3,1},{4,6},{5,7},{6,4},{7,5},{8,10},{9,11},{10,... | collective-permute-start | bytes 393224 | tf_op jit(solution)/shard_map/ppermute | solution.py:554
  23.3 8.8 %collective-permute-start.8 = (f32[2,136,256]{2,1,0:T(8,128)S(1)}, f32[2,136,256]{2,1,0:T(8,128)S(1)}, u32[]{:S(2)}, u32[]{:S(2)}) collective-permute-start(f32[2,136,256]{2,1,0:T(8,128)S(1)} %get-tuple-element.42), channel_id=1, source_target_pairs={{0,4},{4,0},{8,12},{12,8},{16,20},{20,16},{24,28},{28,24},{1,5},{5... | collective-permute-start | bytes 835592 | tf_op jit(solution)/shard_map/ppermute | solution.py:554
  24.8 10.4 %collective-permute-start.10 = (f32[360,256]{1,0:T(8,128)S(1)}, f32[360,256]{1,0:T(8,128)S(1)}, u32[]{:S(2)}, u32[]{:S(2)}) collective-permute-start(f32[360,256]{1,0:T(8,128)S(1)} %get-tuple-element.57), channel_id=1, source_target_pairs={{0,8},{4,12},{8,0},{12,4},{16,24},{20,28},{24,16},{28,20},{1,9},{5... | collective-permute-start | bytes 1105928 | tf_op jit(solution)/shard_map/ppermute | solution.py:554
  27.7 1.0 %copy-start.1 = (f32[2,136,256]{2,1,0:T(8,128)S(1)}, f32[2,136,256]{2,1,0:T(8,128)}, u32[]{:S(2)}) copy-start(f32[2,136,256]{2,1,0:T(8,128)} %get-tuple-element.36.refs_0_) | copy-start | bytes 835588
  28.7 4.2 %copy-start.2 = (f32[2,64,256]{2,1,0:T(8,128)S(1)}, f32[2,64,256]{2,1,0:T(8,128)}, u32[]{:S(2)}) copy-start(f32[2,64,256]{2,1,0:T(8,128)} %get-tuple-element.43.refs_4_) | copy-start | bytes 393220
  31.5 1.4 %collective-permute-start.11 = (f32[2,64,256]{2,1,0:T(8,128)S(1)}, f32[2,64,256]{2,1,0:T(8,128)S(1)}, u32[]{:S(2)}, u32[]{:S(2)}) collective-permute-start(f32[2,64,256]{2,1,0:T(8,128)S(1)} %collective-permute-done.6.refs_6_), channel_id=1, source_target_pairs={{0,1},{1,0},{2,3},{3,2},{4,5},{5,4},{6,7},{7,6},{8,9},{9,8},{10,11... | collective-permute-start | bytes 393224 | tf_op jit(solution)/shard_map/ppermute | solution.py:554
  32.1 3.1 %collective-permute-start.9 = (f32[2,136,256]{2,1,0:T(8,128)S(1)}, f32[2,136,256]{2,1,0:T(8,128)S(1)}, u32[]{:S(2)}, u32[]{:S(2)}) collective-permute-start(f32[2,136,256]{2,1,0:T(8,128)S(1)} %collective-permute-done.8.refs_2_), channel_id=1, source_target_pairs={{0,1},{1,0},{2,3},{3,2},{4,5},{5,4},{6,7},{7,6},{8,9},{9,8},{10,11... | collective-permute-start | bytes 835592 | tf_op jit(solution)/shard_map/ppermute | solution.py:554
  35.3 2.9 %collective-permute-start.12 = (f32[360,256]{1,0:T(8,128)S(1)}, f32[360,256]{1,0:T(8,128)S(1)}, u32[]{:S(2)}, u32[]{:S(2)}) collective-permute-start(f32[360,256]{1,0:T(8,128)S(1)} %collective-permute-done.10.refs_4_), channel_id=1, source_target_pairs={{0,1},{1,0},{2,3},{3,2},{4,5},{5,4},{6,7},{7,6},{8,9},{9,8},{10,11... | collective-permute-start | bytes 1105928 | tf_op jit(solution)/shard_map/ppermute | solution.py:554
  46.1 8.7 %collective-permute-start.13 = (f32[17,8,256]{2,1,0:T(8,128)S(1)}, f32[17,8,256]{2,1,0:T(8,128)S(1)}, u32[]{:S(2)}, u32[]{:S(2)}) collective-permute-start(f32[17,8,256]{2,1,0:T(8,128)S(1)} %get-tuple-element.64), channel_id=1, source_target_pairs={{0,8},{4,12},{8,0},{12,4},{16,24},{20,28},{24,16},{28,20},{1,9},{5... | collective-permute-start | bytes 417800 | tf_op jit(solution)/shard_map/ppermute | solution.py:554
  47.8 13.4 %collective-permute-start.14 = (f32[17,8,256]{2,1,0:T(8,128)S(1)}, f32[17,8,256]{2,1,0:T(8,128)S(1)}, u32[]{:S(2)}, u32[]{:S(2)}) collective-permute-start(f32[17,8,256]{2,1,0:T(8,128)S(1)} %get-tuple-element.65), channel_id=1, source_target_pairs={{0,16},{4,20},{8,24},{12,28},{16,0},{20,4},{24,8},{28,12},{1,17},{... | collective-permute-start | bytes 417800 | tf_op jit(solution)/shard_map/ppermute | solution.py:554
  50.4 10.9 %collective-permute-start.15 = (f32[17,8,256]{2,1,0:T(8,128)S(1)}, f32[17,8,256]{2,1,0:T(8,128)S(1)}, u32[]{:S(2)}, u32[]{:S(2)}) collective-permute-start(f32[17,8,256]{2,1,0:T(8,128)S(1)} %get-tuple-element.66), channel_id=1, source_target_pairs={{0,24},{4,28},{8,16},{12,20},{16,8},{20,12},{24,0},{28,4},{1,25},{... | collective-permute-start | bytes 417800 | tf_op jit(solution)/shard_map/ppermute | solution.py:554
  61.3 3.8 %collective-permute-start.16 = (f32[2,8,256]{2,1,0:T(8,128)S(1)}, f32[2,8,256]{2,1,0:T(8,128)S(1)}, u32[]{:S(2)}, u32[]{:S(2)}) collective-permute-start(f32[2,8,256]{2,1,0:T(8,128)S(1)} %add_smalls.1.refs_0_), channel_id=1, source_target_pairs={{0,4},{4,0},{8,12},{12,8},{16,20},{20,16},{24,28},{28,24},{1,5},{5... | collective-permute-start | bytes 49160 | tf_op jit(solution)/shard_map/ppermute | solution.py:554

commit v10 on v9

--- a/solution.py
+++ b/solution.py
@@ -38,9 +38,7 @@
         copy.start()
     size = orbit.shape[0] // parts
     at = turn_of(lax.axis_index("sta"), nx) * size if parts > 1 else 0
-    head = planes.shape[0] * planes.shape[1]
-    cut = pltpu.make_async_copy(orbit.at[pl.ds(at, size)], message.at[pl.ds(head, size * 24)]
-                                .reshape(size, 3, 8, orbit.shape[3]), cut_sem)
+    cut = pltpu.make_async_copy(orbit.at[pl.ds(at, size)], message, cut_sem)
     cut.start()
     for copy in copies:
         copy.wait()
@@ -81,7 +79,6 @@
         extra[s, tracked:, :] = jnp.where(weight > 0.0, total / jnp.maximum(weight, 1.0), 0.0)
 
 
-    message[:head] = planes[...].reshape(head, planes.shape[2])
     cut.wait()
 
 
@@ -95,7 +92,7 @@
         out_shape=[
             jax.ShapeDtypeStruct((stations, rows, epochs), f32),
             jax.ShapeDtypeStruct((stations, 2 * tracked, epochs), f32),
-            jax.ShapeDtypeStruct((stations * rows + size * 24, epochs), f32),
+            jax.ShapeDtypeStruct((size,) + orbit.shape[1:], f32),
         ],
         in_specs=[hbm()] * 7,
         out_specs=[vmem()] * 3,
@@ -106,19 +103,20 @@
     )(*arguments, orbit)
 
 
-def open_kernel(message, planes, partials):
-    head = planes.shape[0] * planes.shape[1]
-    planes[...] = message[:head].reshape(planes.shape)
-    partials[...] = message[head:]
-
-
-def open_message(message, shape):
-    rows, epochs = message.shape
+def open_kernel(message, first, second):
+    size = first.shape[0]
+    first[...] = message[:size]
+    second[...] = message[size:]
+
+
+def open_message(message):
+    size = message.shape[0]
+    lead = size * 2 // 3
     return pl.pallas_call(
         open_kernel,
         out_shape=[
-            jax.ShapeDtypeStruct(shape, jnp.float32),
-            jax.ShapeDtypeStruct((rows - shape[0] * shape[1], epochs), jnp.float32),
+            jax.ShapeDtypeStruct((n,) + message.shape[1:], jnp.float32)
+            for n in (lead, size - lead)
         ],
         in_specs=[vmem()],
         out_specs=[vmem()] * 2,
@@ -148,8 +146,7 @@
     rows_int, dense_a, dense_b, track_sem = refs[groups + 5 :]
     denses = (dense_a, dense_b)
     stations = groups * per
-    rows = planes.shape[1]
-    tracked = (rows - 8) // 4
+    tracked = (planes.shape[1] - 8) // 4
     epochs = planes.shape[2]
     spare = width - own * 8
     packed = spare // KNOTS
@@ -158,10 +155,7 @@
     for d in range(groups):
         for p in range(per):
             s = d * per + p
-            if len(plane_pieces[d].shape) == 3:
-                planes[s] = plane_pieces[d][p]
-            else:
-                planes[s] = plane_pieces[d][p * rows : (p + 1) * rows, :]
+            planes[s] = plane_pieces[d][p]
             rows_int[s : s + 1, :] = planes[
                 s, 4 * tracked + 1 : 4 * tracked + 2, :128].astype(jnp.int32)
     to_scalar = pltpu.make_async_copy(rows_int, track, track_sem)
@@ -233,12 +227,11 @@
     pieces, orbit = refs[:-1], refs[-1]
     me = lax.axis_index("sat")
     mine = lax.axis_index("sta")
-    for piece, (d, far, head, size) in zip(pieces, places):
+    for piece, (d, far, start) in zip(pieces, places):
         at = (me ^ d) * own
-        if size < own:
-            at = at + (turn_of(mine, nx) ^ far) * size
-        value = piece[...] if len(piece.shape) == 4 else piece[head:]
-        orbit[pl.ds(at, size)] = value.reshape((size,) + orbit.shape[1:])
+        if piece.shape[0] < own:
+            at = at + (turn_of(mine, nx) ^ far) * (own // 2) + start
+        orbit[pl.ds(at, piece.shape[0])] = piece[...]
 
 
 def place(pieces, places, sats, own, nx):
@@ -400,7 +393,6 @@
     extra_pieces = refs[groups : 2 * groups]
     orbit, small = refs[2 * groups :]
     tracked = extra_pieces[0].shape[1] // 2
-    rows = 4 * tracked + 8
     epochs = orbit.shape[3]
     width = small.shape[2]
     own = orbit.shape[0]
@@ -410,10 +402,7 @@
     picks, stacks = [], [[] for _ in range(9)]
     for d in range(groups):
         for s in range(per):
-            if len(plane_pieces[d].shape) == 3:
-                station = plane_pieces[d][s]
-            else:
-                station = plane_pieces[d][s * rows : (s + 1) * rows, :]
+            station = plane_pieces[d][s]
             named = station[4 * tracked + 1 : 4 * tracked + 2, :tracked]
             picks.append((satellite == named.astype(jnp.int32)).astype(jnp.float32))
             a = [station[c * tracked : (c + 1) * tracked, :] for c in range(3)]
@@ -570,10 +559,9 @@
         -(-(((columns * i) % 8) + columns) // 8) for i in range(columns_axis)
     )
 
-    parts = 2 if own % 2 == 0 and nz % 2 == 0 else 1
+    parts = 2 if own % 2 == 0 and nz % 2 == 0 and nx % 2 == 0 else 1
     planes, extra, message = prepare(
         (sight, mapping, residual, counts, track, knots), orbit, parts, nx)
-    head = planes.shape[0] * planes.shape[1]
 
     def core(value):
         return shift(value, "sat", group, 1)
@@ -582,46 +570,48 @@
     early += [core(value) for value in early]
     beside = {dx: shift(planes, "sta", columns_axis, dx) for dx in range(1, nx)}
     crossed = {dx: core(value) for dx, value in beside.items()}
-    messages = {d: shift(message, "sat", group, d) for d in range(2, group, 2)}
-    (early, beside, crossed, messages) = lax.optimization_barrier(
-        (early, beside, crossed, messages))
-    _, orbit, extra, other_planes, other_orbit, other_extra = early
+    arrived = {d: shift(planes, "sat", group, d) for d in range(2, group, 2)}
+    (early, beside, arrived, message) = lax.optimization_barrier(
+        (early, beside, arrived, message))
+    planes, orbit, extra, other_planes, other_orbit, other_extra = early
 
     pieces = [[(0, planes), (1, other_planes)]]
     pieces += [[(0, beside[dx]), (1, crossed[dx])] for dx in range(1, nx)]
-    partials = [(0, 0, orbit), (1, 0, other_orbit)]
+    partials = [(0, 0, 0, orbit), (1, 0, 0, other_orbit)]
     extras = {0: extra, 1: other_extra}
-    far = {}
-    for d, arrived in messages.items():
-        value, part = open_message(arrived, planes.shape)
-        across = core(arrived)
-        partials += [(d, 0, arrived), (d + 1, 0, across)]
+    messages, passed = {}, {}
+    for d, value in arrived.items():
+        messages[d] = shift(message, "sat", group, d)
+        pieces[0] += [(d, value), (d + 1, core(value))]
+        for dx in range(1, nx):
+            passed[dx, d] = shift(value, "sta", columns_axis, dx)
+    sets = [own_rows_of([value for _, value in pieces[0]], planes.shape, orbit, width, 0)]
+    sets[0], messages, passed = lax.optimization_barrier((tuple(sets[0]), messages, passed))
+    for (dx, d), value in passed.items():
+        pieces[dx] += [(d, value), (d + 1, core(value))]
+    far = []
+    for d, value in messages.items():
+        held, value = lax.optimization_barrier((extra, value))
+        extras[d] = shift(held, "sat", group, d)
+        extras[d + 1] = core(extras[d])
+        partials += [(d, 0, 0, value), (d + 1, 0, 0, core(value))]
         if parts > 1:
-            far[d] = shift(part, "sta", columns_axis, nx)
-        for dx in range(1, nx):
-            passed = shift(value, "sta", columns_axis, dx)
-            pieces[dx] += [(d, passed), (d + 1, core(passed))]
-        held, _ = lax.optimization_barrier((extra, value))
-        extras[d], across = lax.optimization_barrier((shift(held, "sat", group, d), across))
-        pieces[0] += [(d, arrived), (d + 1, across)]
-    sets = [own_rows_of([value for _, value in pieces[0]], planes.shape, orbit, width, 0)]
-    for d in range(2, group, 2):
-        held, _ = lax.optimization_barrier((extras[d], sets[0][1]))
-        extras[d + 1] = core(held)
-    small = own_sums([value for _, value in pieces[0]],
-                     [extras[d] for d, _ in pieces[0]], orbit, width)
-    far, small = lax.optimization_barrier((far, small))
-    for d, value in far.items():
-        partials += [(d, 1, value), (d + 1, 1, core(value))]
+            first, second = open_message(value)
+            far += [(d, 0, shift(first, "sta", columns_axis, nx)),
+                    (d, first.shape[0], shift(second, "sta", columns_axis, 1))]
     for dx in range(1, nx):
         sets.append(own_rows_of(
             [value for _, value in pieces[dx]], planes.shape, orbit, width,
             dx * group * stations))
-    places = tuple((d, turn, head, own if value.ndim == 4 else own // parts)
-                   for d, turn, value in partials)
-    places = tuple((d, turn, head if value.shape[0] == message.shape[0] else 0, size)
-                   for (d, turn, head, size), (_, _, value) in zip(places, partials))
-    every = place([value for _, _, value in partials], places, sats, own, nx)
+    held = [value for _, _, value in far]
+    track1, held = lax.optimization_barrier((sets[-1][1], held))
+    sets[-1] = (sets[-1][0], track1, *sets[-1][2:])
+    for (d, start, _), value in zip(far, held):
+        partials += [(d, 1, start, value), (d + 1, 1, start, core(value))]
+    small = own_sums([value for _, value in pieces[0]],
+                     [extras[d] for d, _ in pieces[0]], orbit, width)
+    places = tuple((d, turn, start) for d, turn, start, _ in partials)
+    every = place([part[3] for part in partials], places, sats, own, nx)
     sums = accumulate(sets, every, small, own, nz, window)
     final = [sums[0]] + [
         shift(sums[d], "sta", columns_axis, d * nx) for d in range(1, nz)

time: 66.1 us -> 65.7 us (level)
  waiting for transfers between devices: 29.8 us -> 27.2 us
  starting transfers between devices: 15.5 us -> 17.6 us
    ppermute x17 -> x21, waiting for transfers between devices: 29.8 us -> 27.2 us  [shift(): return lax.ppermute(value, axis, [(i, i ^ step) for i in range(size)])]
    ppermute x17 -> x21, starting transfers between devices: 15.5 us -> 17.6 us  [shift(): return lax.ppermute(value, axis, [(i, i ^ step) for i in range(size)])]
  transfers between devices with their start and end apart: 17 -> 21, of which waited for: 10 -> 11; matrix products, arithmetic and copies ran while one was open for 0% -> 0% of each run, Pallas kernels for 15% -> 15%
where the time goes in v10:
time: 65.7 us; the launch traced here: 65.5 us
  waiting for transfers between devices  27.2 us (41%)
  Pallas kernels  19 us (29%)
  starting transfers between devices  17.6 us (27%)
  local copies, waits for them, and re-layouts  0.96 us (1%)
  between operations  0.76 us (1%)
    ppermute x21, waiting for transfers between devices, shift(): return lax.ppermute(value, axis, [(i, i ^ step) for i in range(size)])  27.2 us
    ppermute x21, starting transfers between devices, shift(): return lax.ppermute(value, axis, [(i, i ^ step) for i in range(size)])  17.6 us
    pallas_call x1, Pallas kernels, accumulate(): pl.pallas_call(functools.partial(main_kernel, own, nx, nz, window), out_s...  7.94 us
    pallas_call x2, Pallas kernels, own_rows_of(): pl.pallas_call(functools.partial(own_rows_kernel, groups, per, own, width...  5.66 us
    pallas_call x1, Pallas kernels, prepare(): pl.pallas_call(functools.partial(prepare_kernel, parts, nx), out_shape=[j...  2.18 us
  transfers between devices with their start and end apart: 21, of which 11 were waited for; matrix products, arithmetic and copies ran while one was open for 0% of the time, Pallas kernels for 15%

profile of v10, /device:TPU:0, one launch (start us, length us, event | category | flops | bytes accessed | tf_op | source)
XLA Modules:
  0.0 65.5 jit_solution(365521046162424871)
XLA Ops:
  0.6 0.0 copy-start
  0.6 0.5 collective-permute-start.1
  1.2 2.2 %prepare.1 = (f32[2,136,256]{2,1,0:T(8,128)}, f32[2,64,256]{2,1,0:T(8,128)}, f32[15,3,8,256]{3,2,1,0:T(8,128)}) custom-call(f32[2,3,32,256]{3,2,1,0:T(8,128)} %refs_0_.1, f32[2,32,256]{2,1,0:T(8,128)} %refs_1_.1, f32[2,32,256]{2,1,0:T(8,128)} %refs_2_.1, s32[2,32,256]{2,1,0:T(8,128)} %refs_3_.1, s32[2,32]{1,0:T(2,128)} %refs_4_.1, s32[2,256]{1,0:T(2,128)} %refs_5_.1, ...), custom_call_target="tpu_custom_call" | custom-call | tf_op jit(solution)/shard_map/prepare/pallas_call | solution.py:90
  3.3 2.6 %collective-permute-start.4 = (f32[2,136,256]{2,1,0:T(8,128)}, f32[2,136,256]{2,1,0:T(8,128)S(1)}, u32[]{:S(2)}, u32[]{:S(2)}) collective-permute-start(f32[2,136,256]{2,1,0:T(8,128)} %get-tuple-element.45.refs_0_), channel_id=1, source_target_pairs={{0,2},{1,3},{2,0},{3,1},{4,6},{5,7},{6,4},{7,5},{8,10},{9,11},{10,... | collective-permute-start | bytes 835592 | tf_op jit(solution)/shard_map/ppermute | solution.py:543
  6.0 1.5 %collective-permute-start.3 = (f32[2,136,256]{2,1,0:T(8,128)}, f32[2,136,256]{2,1,0:T(8,128)S(1)}, u32[]{:S(2)}, u32[]{:S(2)}) collective-permute-start(f32[2,136,256]{2,1,0:T(8,128)} %get-tuple-element.45.refs_0_), channel_id=1, source_target_pairs={{0,4},{4,0},{8,12},{12,8},{16,20},{20,16},{24,28},{28,24},{1,5},{5... | collective-permute-start | bytes 835592 | tf_op jit(solution)/shard_map/ppermute | solution.py:543
  7.5 0.0 collective-permute-start
  7.5 0.5 collective-permute-start.2
  8.0 1.4 %collective-permute-done.2.refs_5_ = f32[2,64,256]{2,1,0:T(8,128)S(1)} collective-permute-done((f32[2,64,256]{2,1,0:T(8,128)}, f32[2,64,256]{2,1,0:T(8,128)S(1)}, u32[]{:S(2)}, u32[]{:S(2)}) %collective-permute-start.2) | collective-permute-done | bytes 131104 | tf_op jit(solution)/shard_map/ppermute | solution.py:543
  9.4 4.0 %collective-permute-done.4.refs_2_ = f32[2,136,256]{2,1,0:T(8,128)S(1)} collective-permute-done((f32[2,136,256]{2,1,0:T(8,128)}, f32[2,136,256]{2,1,0:T(8,128)S(1)}, u32[]{:S(2)}, u32[]{:S(2)}) %collective-permute-start.4) | collective-permute-done | bytes 278560 | tf_op jit(solution)/shard_map/ppermute | solution.py:543
  13.5 1.5 %collective-permute-done.3.refs_0_ = f32[2,136,256]{2,1,0:T(8,128)S(1)} collective-permute-done((f32[2,136,256]{2,1,0:T(8,128)}, f32[2,136,256]{2,1,0:T(8,128)S(1)}, u32[]{:S(2)}, u32[]{:S(2)}) %collective-permute-start.3) | collective-permute-done | bytes 278560 | tf_op jit(solution)/shard_map/ppermute | solution.py:543
  14.9 0.0 collective-permute-done.refs_1_
  14.9 0.0 collective-permute-done.1.refs_1_
  14.9 0.0 collective-permute-start.5
  14.9 0.5 collective-permute-start.6
  15.4 1.6 %collective-permute-start.7 = (f32[2,136,256]{2,1,0:T(8,128)S(1)}, f32[2,136,256]{2,1,0:T(8,128)S(1)}, u32[]{:S(2)}, u32[]{:S(2)}) collective-permute-start(f32[2,136,256]{2,1,0:T(8,128)S(1)} %collective-permute-done.4.refs_2_), channel_id=1, source_target_pairs={{0,4},{4,0},{8,12},{12,8},{16,20},{20,16},{24,28},{28,24},{1,5},{5... | collective-permute-start | bytes 835592 | tf_op jit(solution)/shard_map/ppermute | solution.py:543
  17.0 0.0 collective-permute-start.8
  17.0 0.0 collective-permute-done.5.refs_3_
  17.0 0.0 copy-done
  17.0 0.0 copy-start.1
  17.0 0.9 %copy-done.1 = f32[2,136,256]{2,1,0:T(8,128)S(1)} copy-done((f32[2,136,256]{2,1,0:T(8,128)S(1)}, f32[2,136,256]{2,1,0:T(8,128)}, u32[]{:S(2)}) %copy-start.1) | copy-done | bytes 278552
  18.0 0.0 copy-start.3
  18.0 2.8 %own_rows.2 = (f32[8,136,256]{2,1,0:T(8,128)S(1)}, s32[8,128]{1,0:T(8,128)S(1)}, bf16[8,256,256]{2,1,0:T(8,128)(2,1)S(1)}, bf16[8,256,256]{2,1,0:T(8,128)(2,1)S(1)}) custom-call(f32[2,136,256]{2,1,0:T(8,128)S(1)} %copy-done.1, f32[2,136,256]{2,1,0:T(8,128)S(1)} %collective-permute-done.refs_1_, f32[2,136,256]{2,1,0:T(8,128)S(1)} %collective-permute-done.4.refs_2_, ...), custom_call_target="tpu_custom_call" | custom-call | flops 2000000000 | bytes 2000000 | tf_op jit(solution)/shard_map/own_rows/pallas_call | solution.py:204
  20.8 3.3 %collective-permute-done.7.refs_2_ = f32[2,136,256]{2,1,0:T(8,128)S(1)} collective-permute-done((f32[2,136,256]{2,1,0:T(8,128)S(1)}, f32[2,136,256]{2,1,0:T(8,128)S(1)}, u32[]{:S(2)}, u32[]{:S(2)}) %collective-permute-start.7) | collective-permute-done | bytes 278560 | tf_op jit(solution)/shard_map/ppermute | solution.py:543
  24.1 2.0 %collective-permute-done.6.message.refs_2_ = f32[15,3,8,256]{3,2,1,0:T(8,128)S(1)} collective-permute-done((f32[15,3,8,256]{3,2,1,0:T(8,128)}, f32[15,3,8,256]{3,2,1,0:T(8,128)S(1)}, u32[]{:S(2)}, u32[]{:S(2)}) %collective-permute-start.6) | collective-permute-done | bytes 368672 | tf_op jit(solution)/shard_map/ppermute | solution.py:543
  26.2 0.0 collective-permute-start.9
  26.2 1.6 %collective-permute-start.10 = (f32[10,3,8,256]{3,2,1,0:T(8,128)S(1)}, f32[10,3,8,256]{3,2,1,0:T(8,128)S(1)}, u32[]{:S(2)}, u32[]{:S(2)}) collective-permute-start(f32[10,3,8,256]{3,2,1,0:T(8,128)S(1)} %get-tuple-element.65), channel_id=1, source_target_pairs={{0,8},{4,12},{8,0},{12,4},{16,24},{20,28},{24,16},{28,20},{1,9},{5... | collective-permute-start | bytes 737288 | tf_op jit(solution)/shard_map/ppermute | solution.py:543
  27.8 0.2 collective-permute-start.12
  28.1 0.0 copy-done.3
  28.1 0.5 collective-permute-start.15
  28.6 0.0 collective-permute-done.8.refs_1_
  28.6 0.0 copy-start.2
  28.6 1.5 %collective-permute-start.11 = (f32[5,3,8,256]{3,2,1,0:T(8,128)S(1)}, f32[5,3,8,256]{3,2,1,0:T(8,128)S(1)}, u32[]{:S(2)}, u32[]{:S(2)}) collective-permute-start(f32[5,3,8,256]{3,2,1,0:T(8,128)S(1)} %get-tuple-element.66), channel_id=1, source_target_pairs={{0,4},{4,0},{8,12},{12,8},{16,20},{20,16},{24,28},{28,24},{1,5},{5... | collective-permute-start | bytes 368648 | tf_op jit(solution)/shard_map/ppermute | solution.py:543
  30.1 0.0 collective-permute-done.9.refs_3_
  30.1 2.8 %own_rows.3 = (f32[8,136,256]{2,1,0:T(8,128)S(1)}, s32[8,128]{1,0:T(8,128)S(1)}, bf16[8,256,256]{2,1,0:T(8,128)(2,1)S(1)}, bf16[8,256,256]{2,1,0:T(8,128)(2,1)S(1)}) custom-call(f32[2,136,256]{2,1,0:T(8,128)S(1)} %collective-permute-done.3.refs_0_, f32[2,136,256]{2,1,0:T(8,128)S(1)} %collective-permute-done.8.refs_1_, ...), custom_call_target="tpu_custom_call" | custom-call | flops 2000000000 | bytes 2000000 | tf_op jit(solution)/shard_map/own_rows/pallas_call | solution.py:204
  32.9 0.9 %collective-permute-done.11.refs_6_ = f32[5,3,8,256]{3,2,1,0:T(8,128)S(1)} collective-permute-done((f32[5,3,8,256]{3,2,1,0:T(8,128)S(1)}, f32[5,3,8,256]{3,2,1,0:T(8,128)S(1)}, u32[]{:S(2)}, u32[]{:S(2)}) %collective-permute-start.11) | collective-permute-done | bytes 122912 | tf_op jit(solution)/shard_map/ppermute | solution.py:543
  33.8 0.8 %collective-permute-done.10.refs_4_ = f32[10,3,8,256]{3,2,1,0:T(8,128)S(1)} collective-permute-done((f32[10,3,8,256]{3,2,1,0:T(8,128)S(1)}, f32[10,3,8,256]{3,2,1,0:T(8,128)S(1)}, u32[]{:S(2)}, u32[]{:S(2)}) %collective-permute-start.10) | collective-permute-done | bytes 245792 | tf_op jit(solution)/shard_map/ppermute | solution.py:543
  34.6 0.0 collective-permute-start.13
  34.6 0.0 collective-permute-done.15.refs_6_
  34.6 0.5 collective-permute-start.16
  35.1 0.0 collective-permute-start.14
  35.1 1.2 %collective-permute-done.16.refs_7_ = f32[2,64,256]{2,1,0:T(8,128)S(1)} collective-permute-done((f32[2,64,256]{2,1,0:T(8,128)S(1)}, f32[2,64,256]{2,1,0:T(8,128)S(1)}, u32[]{:S(2)}, u32[]{:S(2)}) %collective-permute-start.16) | collective-permute-done | bytes 131104 | tf_op jit(solution)/shard_map/ppermute | solution.py:543
  36.3 0.0 copy-done.2
  36.3 1.3 %own_sums.1.refs_9_ = f32[2,8,256]{2,1,0:T(8,128)S(1)} custom-call(f32[2,136,256]{2,1,0:T(8,128)S(1)} %copy-done.2, f32[2,136,256]{2,1,0:T(8,128)S(1)} %collective-permute-done.refs_1_, f32[2,136,256]{2,1,0:T(8,128)S(1)} %collective-permute-done.4.refs_2_, f32[2,136,256]{2,1,0:T(8,128)S(1)} %collective-permute-done.5.refs_3_, f32[2,64,256]{2,1,0:T(8,128)S(1)} %copy-done.3, ...), custom_call_target="tpu_custom_call" | custom-call | flops 100000000 | bytes 100000 | tf_op jit(solution)/shard_map/own_sums/pallas_call | solution.py:449
  37.6 0.0 collective-permute-done.12.refs_3_
  37.6 0.0 collective-permute-done.14.refs_7_
  37.7 0.0 collective-permute-done.13.refs_5_
  37.7 0.2 place.1.refs_8_
  37.9 7.9 %accumulate.1 = (f32[17,8,256]{2,1,0:T(8,128)S(1)}, f32[17,8,256]{2,1,0:T(8,128)S(1)}, f32[17,8,256]{2,1,0:T(8,128)S(1)}, f32[17,8,256]{2,1,0:T(8,128)S(1)}) custom-call(f32[8,136,256]{2,1,0:T(8,128)S(1)} %get-tuple-element.54.refs_0_, s32[8,128]{1,0:T(8,128)S(1)} %get-tuple-element.55.refs_1_, bf16[8,256,256]{2,1,0:T(8,128)(2,1)S(1)} %get-tuple-element.56.refs_2_, ...), custom_call_target="tpu_custom_call" | custom-call | flops 8000000000 | bytes 8000000 | tf_op jit(solution)/shard_map/accumulate/pallas_call | solution.py:371
  45.8 1.6 %collective-permute-start.17 = (f32[17,8,256]{2,1,0:T(8,128)S(1)}, f32[17,8,256]{2,1,0:T(8,128)S(1)}, u32[]{:S(2)}, u32[]{:S(2)}) collective-permute-start(f32[17,8,256]{2,1,0:T(8,128)S(1)} %get-tuple-element.76), channel_id=1, source_target_pairs={{0,8},{4,12},{8,0},{12,4},{16,24},{20,28},{24,16},{28,20},{1,9},{5... | collective-permute-start | bytes 417800 | tf_op jit(solution)/shard_map/ppermute | solution.py:543
  47.4 2.6 %collective-permute-start.18 = (f32[17,8,256]{2,1,0:T(8,128)S(1)}, f32[17,8,256]{2,1,0:T(8,128)S(1)}, u32[]{:S(2)}, u32[]{:S(2)}) collective-permute-start(f32[17,8,256]{2,1,0:T(8,128)S(1)} %get-tuple-element.77), channel_id=1, source_target_pairs={{0,16},{4,20},{8,24},{12,28},{16,0},{20,4},{24,8},{28,12},{1,17},{... | collective-permute-start | bytes 417800 | tf_op jit(solution)/shard_map/ppermute | solution.py:543
  50.0 0.2 collective-permute-start.19
  50.3 3.6 %collective-permute-done.17.refs_1_ = f32[17,8,256]{2,1,0:T(8,128)S(1)} collective-permute-done((f32[17,8,256]{2,1,0:T(8,128)S(1)}, f32[17,8,256]{2,1,0:T(8,128)S(1)}, u32[]{:S(2)}, u32[]{:S(2)}) %collective-permute-start.17) | collective-permute-done | bytes 139296 | tf_op jit(solution)/shard_map/ppermute | solution.py:543
  53.8 7.0 %collective-permute-done.18.refs_2_ = f32[17,8,256]{2,1,0:T(8,128)S(1)} collective-permute-done((f32[17,8,256]{2,1,0:T(8,128)S(1)}, f32[17,8,256]{2,1,0:T(8,128)S(1)}, u32[]{:S(2)}, u32[]{:S(2)}) %collective-permute-start.18) | collective-permute-done | bytes 139296 | tf_op jit(solution)/shard_map/ppermute | solution.py:543
  60.9 0.0 collective-permute-done.19.refs_3_
  60.9 1.6 %collective-permute-start.20 = (f32[2,8,256]{2,1,0:T(8,128)S(1)}, f32[2,8,256]{2,1,0:T(8,128)S(1)}, u32[]{:S(2)}, u32[]{:S(2)}) collective-permute-start(f32[2,8,256]{2,1,0:T(8,128)S(1)} %add_smalls.1.refs_0_), channel_id=1, source_target_pairs={{0,4},{4,0},{8,12},{12,8},{16,20},{20,16},{24,28},{28,24},{1,5},{5... | collective-permute-start | bytes 49160 | tf_op jit(solution)/shard_map/ppermute | solution.py:543
  62.4 0.8 %finish.1 = f32[240,120]{1,0:T(8,128)} custom-call(f32[17,8,256]{2,1,0:T(8,128)S(1)} %get-tuple-element.75.refs_0_, f32[17,8,256]{2,1,0:T(8,128)S(1)} %collective-permute-done.17.refs_1_, f32[17,8,256]{2,1,0:T(8,128)S(1)} %collective-permute-done.18.refs_2_, f32[17,8,256]{2,1,0:T(8,128)S(1)} %collective-permute-done.19.refs_3_), custom_call_target="tpu_custom_call" | custom-call | flops 2000000000 | bytes 2000000 | tf_op jit(solution)/shard_map/finish/pallas_call | solution.py:496
  63.2 1.5 %collective-permute-done.20.refs_1_ = f32[2,8,256]{2,1,0:T(8,128)S(1)} collective-permute-done((f32[2,8,256]{2,1,0:T(8,128)S(1)}, f32[2,8,256]{2,1,0:T(8,128)S(1)}, u32[]{:S(2)}, u32[]{:S(2)}) %collective-permute-start.20) | collective-permute-done | bytes 16416 | tf_op jit(solution)/shard_map/ppermute | solution.py:543
  64.7 0.9 %finish_own.1 = (f32[1,240]{1,0:T(1,128)}, f32[8,8,30]{2,1,0:T(8,128)}) custom-call(f32[2,8,256]{2,1,0:T(8,128)S(1)} %add_smalls.1.refs_0_, f32[2,8,256]{2,1,0:T(8,128)S(1)} %collective-permute-done.20.refs_1_), custom_call_target="tpu_custom_call" | custom-call | tf_op jit(solution)/shard_map/finish_own/pallas_call | solution.py:529
  (2 shorter events, 0.0 us)
Async XLA Ops:
  0.6 16.4 %copy-start = (f32[30,3,8,256]{3,2,1,0:T(8,128)S(1)}, f32[30,3,8,256]{3,2,1,0:T(8,128)}, u32[]{:S(2)}) copy-start(f32[30,3,8,256]{3,2,1,0:T(8,128)} %refs_8_) | copy-start | bytes 2211844
  0.6 14.3 %collective-permute-start.1 = (f32[30,3,8,256]{3,2,1,0:T(8,128)}, f32[30,3,8,256]{3,2,1,0:T(8,128)S(1)}, u32[]{:S(2)}, u32[]{:S(2)}) collective-permute-start(f32[30,3,8,256]{3,2,1,0:T(8,128)} %refs_8_), channel_id=1, source_target_pairs={{0,1},{1,0},{2,3},{3,2},{4,5},{5,4},{6,7},{7,6},{8,9},{9,8},{10,11... | collective-permute-start | bytes 2211848 | tf_op jit(solution)/shard_map/ppermute | solution.py:543
  3.3 10.1 %collective-permute-start.4 = (f32[2,136,256]{2,1,0:T(8,128)}, f32[2,136,256]{2,1,0:T(8,128)S(1)}, u32[]{:S(2)}, u32[]{:S(2)}) collective-permute-start(f32[2,136,256]{2,1,0:T(8,128)} %get-tuple-element.45.refs_0_), channel_id=1, source_target_pairs={{0,2},{1,3},{2,0},{3,1},{4,6},{5,7},{6,4},{7,5},{8,10},{9,11},{10,... | collective-permute-start | bytes 835592 | tf_op jit(solution)/shard_map/ppermute | solution.py:543
  6.0 8.9 %collective-permute-start.3 = (f32[2,136,256]{2,1,0:T(8,128)}, f32[2,136,256]{2,1,0:T(8,128)S(1)}, u32[]{:S(2)}, u32[]{:S(2)}) collective-permute-start(f32[2,136,256]{2,1,0:T(8,128)} %get-tuple-element.45.refs_0_), channel_id=1, source_target_pairs={{0,4},{4,0},{8,12},{12,8},{16,20},{20,16},{24,28},{28,24},{1,5},{5... | collective-permute-start | bytes 835592 | tf_op jit(solution)/shard_map/ppermute | solution.py:543
  7.5 7.5 %collective-permute-start = (f32[2,136,256]{2,1,0:T(8,128)}, f32[2,136,256]{2,1,0:T(8,128)S(1)}, u32[]{:S(2)}, u32[]{:S(2)}) collective-permute-start(f32[2,136,256]{2,1,0:T(8,128)} %get-tuple-element.45.refs_0_), channel_id=1, source_target_pairs={{0,1},{1,0},{2,3},{3,2},{4,5},{5,4},{6,7},{7,6},{8,9},{9,8},{10,11... | collective-permute-start | bytes 835592 | tf_op jit(solution)/shard_map/ppermute | solution.py:543
  7.5 2.0 %collective-permute-start.2 = (f32[2,64,256]{2,1,0:T(8,128)}, f32[2,64,256]{2,1,0:T(8,128)S(1)}, u32[]{:S(2)}, u32[]{:S(2)}) collective-permute-start(f32[2,64,256]{2,1,0:T(8,128)} %get-tuple-element.74.refs_4_), channel_id=1, source_target_pairs={{0,1},{1,0},{2,3},{3,2},{4,5},{5,4},{6,7},{7,6},{8,9},{9,8},{10,11... | collective-permute-start | bytes 393224 | tf_op jit(solution)/shard_map/ppermute | solution.py:543
  14.9 2.1 %collective-permute-start.5 = (f32[2,136,256]{2,1,0:T(8,128)S(1)}, f32[2,136,256]{2,1,0:T(8,128)S(1)}, u32[]{:S(2)}, u32[]{:S(2)}) collective-permute-start(f32[2,136,256]{2,1,0:T(8,128)S(1)} %collective-permute-done.4.refs_2_), channel_id=1, source_target_pairs={{0,1},{1,0},{2,3},{3,2},{4,5},{5,4},{6,7},{7,6},{8,9},{9,8},{10,11... | collective-permute-start | bytes 835592 | tf_op jit(solution)/shard_map/ppermute | solution.py:543
  14.9 11.2 %collective-permute-start.6 = (f32[15,3,8,256]{3,2,1,0:T(8,128)}, f32[15,3,8,256]{3,2,1,0:T(8,128)S(1)}, u32[]{:S(2)}, u32[]{:S(2)}) collective-permute-start(f32[15,3,8,256]{3,2,1,0:T(8,128)} %get-tuple-element.53), channel_id=1, source_target_pairs={{0,2},{1,3},{2,0},{3,1},{4,6},{5,7},{6,4},{7,5},{8,10},{9,11},{10,... | collective-permute-start | bytes 1105928 | tf_op jit(solution)/shard_map/ppermute | solution.py:543
  15.4 8.7 %collective-permute-start.7 = (f32[2,136,256]{2,1,0:T(8,128)S(1)}, f32[2,136,256]{2,1,0:T(8,128)S(1)}, u32[]{:S(2)}, u32[]{:S(2)}) collective-permute-start(f32[2,136,256]{2,1,0:T(8,128)S(1)} %collective-permute-done.4.refs_2_), channel_id=1, source_target_pairs={{0,4},{4,0},{8,12},{12,8},{16,20},{20,16},{24,28},{28,24},{1,5},{5... | collective-permute-start | bytes 835592 | tf_op jit(solution)/shard_map/ppermute | solution.py:543
  17.0 11.6 %collective-permute-start.8 = (f32[2,136,256]{2,1,0:T(8,128)S(1)}, f32[2,136,256]{2,1,0:T(8,128)S(1)}, u32[]{:S(2)}, u32[]{:S(2)}) collective-permute-start(f32[2,136,256]{2,1,0:T(8,128)S(1)} %collective-permute-done.3.refs_0_), channel_id=1, source_target_pairs={{0,1},{1,0},{2,3},{3,2},{4,5},{5,4},{6,7},{7,6},{8,9},{9,8},{10,11... | collective-permute-start | bytes 835592 | tf_op jit(solution)/shard_map/ppermute | solution.py:543
  17.0 1.0 %copy-start.1 = (f32[2,136,256]{2,1,0:T(8,128)S(1)}, f32[2,136,256]{2,1,0:T(8,128)}, u32[]{:S(2)}) copy-start(f32[2,136,256]{2,1,0:T(8,128)} %get-tuple-element.45.refs_0_) | copy-start | bytes 835588
  18.0 10.1 %copy-start.3 = (f32[2,64,256]{2,1,0:T(8,128)S(1)}, f32[2,64,256]{2,1,0:T(8,128)}, u32[]{:S(2)}) copy-start(f32[2,64,256]{2,1,0:T(8,128)} %get-tuple-element.74.refs_4_) | copy-start | bytes 393220
  26.2 3.9 %collective-permute-start.9 = (f32[2,136,256]{2,1,0:T(8,128)S(1)}, f32[2,136,256]{2,1,0:T(8,128)S(1)}, u32[]{:S(2)}, u32[]{:S(2)}) collective-permute-start(f32[2,136,256]{2,1,0:T(8,128)S(1)} %collective-permute-done.7.refs_2_), channel_id=1, source_target_pairs={{0,1},{1,0},{2,3},{3,2},{4,5},{5,4},{6,7},{7,6},{8,9},{9,8},{10,11... | collective-permute-start | bytes 835592 | tf_op jit(solution)/shard_map/ppermute | solution.py:543
  26.2 8.4 %collective-permute-start.10 = (f32[10,3,8,256]{3,2,1,0:T(8,128)S(1)}, f32[10,3,8,256]{3,2,1,0:T(8,128)S(1)}, u32[]{:S(2)}, u32[]{:S(2)}) collective-permute-start(f32[10,3,8,256]{3,2,1,0:T(8,128)S(1)} %get-tuple-element.65), channel_id=1, source_target_pairs={{0,8},{4,12},{8,0},{12,4},{16,24},{20,28},{24,16},{28,20},{1,9},{5... | collective-permute-start | bytes 737288 | tf_op jit(solution)/shard_map/ppermute | solution.py:543
  27.8 9.8 %collective-permute-start.12 = (f32[15,3,8,256]{3,2,1,0:T(8,128)S(1)}, f32[15,3,8,256]{3,2,1,0:T(8,128)S(1)}, u32[]{:S(2)}, u32[]{:S(2)}) collective-permute-start(f32[15,3,8,256]{3,2,1,0:T(8,128)S(1)} %collective-permute-done.6.message.refs_2_), channel_id=1, source_target_pairs={{0,1},{1,0},{2,3},{3,2},{4,5},{5,4},{6,7},{7,6},{8,9},{9,8},{10,11... | collective-permute-start | bytes 1105928 | tf_op jit(solution)/shard_map/ppermute | solution.py:543
  28.1 6.6 %collective-permute-start.15 = (f32[2,64,256]{2,1,0:T(8,128)S(1)}, f32[2,64,256]{2,1,0:T(8,128)S(1)}, u32[]{:S(2)}, u32[]{:S(2)}) collective-permute-start(f32[2,64,256]{2,1,0:T(8,128)S(1)} %copy-done.3), channel_id=1, source_target_pairs={{0,2},{1,3},{2,0},{3,1},{4,6},{5,7},{6,4},{7,5},{8,10},{9,11},{10,... | collective-permute-start | bytes 393224 | tf_op jit(solution)/shard_map/ppermute | solution.py:543
  28.6 7.8 %copy-start.2 = (f32[2,136,256]{2,1,0:T(8,128)S(1)}, f32[2,136,256]{2,1,0:T(8,128)}, u32[]{:S(2)}) copy-start(f32[2,136,256]{2,1,0:T(8,128)} %get-tuple-element.45.refs_0_) | copy-start | bytes 835588
  28.6 5.2 %collective-permute-start.11 = (f32[5,3,8,256]{3,2,1,0:T(8,128)S(1)}, f32[5,3,8,256]{3,2,1,0:T(8,128)S(1)}, u32[]{:S(2)}, u32[]{:S(2)}) collective-permute-start(f32[5,3,8,256]{3,2,1,0:T(8,128)S(1)} %get-tuple-element.66), channel_id=1, source_target_pairs={{0,4},{4,0},{8,12},{12,8},{16,20},{20,16},{24,28},{28,24},{1,5},{5... | collective-permute-start | bytes 368648 | tf_op jit(solution)/shard_map/ppermute | solution.py:543
  34.6 3.0 %collective-permute-start.13 = (f32[10,3,8,256]{3,2,1,0:T(8,128)S(1)}, f32[10,3,8,256]{3,2,1,0:T(8,128)S(1)}, u32[]{:S(2)}, u32[]{:S(2)}) collective-permute-start(f32[10,3,8,256]{3,2,1,0:T(8,128)S(1)} %collective-permute-done.10.refs_4_), channel_id=1, source_target_pairs={{0,1},{1,0},{2,3},{3,2},{4,5},{5,4},{6,7},{7,6},{8,9},{9,8},{10,11... | collective-permute-start | bytes 737288 | tf_op jit(solution)/shard_map/ppermute | solution.py:543
  34.6 1.7 %collective-permute-start.16 = (f32[2,64,256]{2,1,0:T(8,128)S(1)}, f32[2,64,256]{2,1,0:T(8,128)S(1)}, u32[]{:S(2)}, u32[]{:S(2)}) collective-permute-start(f32[2,64,256]{2,1,0:T(8,128)S(1)} %collective-permute-done.15.refs_6_), channel_id=1, source_target_pairs={{0,1},{1,0},{2,3},{3,2},{4,5},{5,4},{6,7},{7,6},{8,9},{9,8},{10,11... | collective-permute-start | bytes 393224 | tf_op jit(solution)/shard_map/ppermute | solution.py:543
  35.1 2.5 %collective-permute-start.14 = (f32[5,3,8,256]{3,2,1,0:T(8,128)S(1)}, f32[5,3,8,256]{3,2,1,0:T(8,128)S(1)}, u32[]{:S(2)}, u32[]{:S(2)}) collective-permute-start(f32[5,3,8,256]{3,2,1,0:T(8,128)S(1)} %collective-permute-done.11.refs_6_), channel_id=1, source_target_pairs={{0,1},{1,0},{2,3},{3,2},{4,5},{5,4},{6,7},{7,6},{8,9},{9,8},{10,11... | collective-permute-start | bytes 368648 | tf_op jit(solution)/shard_map/ppermute | solution.py:543
  45.8 8.0 %collective-permute-start.17 = (f32[17,8,256]{2,1,0:T(8,128)S(1)}, f32[17,8,256]{2,1,0:T(8,128)S(1)}, u32[]{:S(2)}, u32[]{:S(2)}) collective-permute-start(f32[17,8,256]{2,1,0:T(8,128)S(1)} %get-tuple-element.76), channel_id=1, source_target_pairs={{0,8},{4,12},{8,0},{12,4},{16,24},{20,28},{24,16},{28,20},{1,9},{5... | collective-permute-start | bytes 417800 | tf_op jit(solution)/shard_map/ppermute | solution.py:543
  47.4 13.4 %collective-permute-start.18 = (f32[17,8,256]{2,1,0:T(8,128)S(1)}, f32[17,8,256]{2,1,0:T(8,128)S(1)}, u32[]{:S(2)}, u32[]{:S(2)}) collective-permute-start(f32[17,8,256]{2,1,0:T(8,128)S(1)} %get-tuple-element.77), channel_id=1, source_target_pairs={{0,16},{4,20},{8,24},{12,28},{16,0},{20,4},{24,8},{28,12},{1,17},{... | collective-permute-start | bytes 417800 | tf_op jit(solution)/shard_map/ppermute | solution.py:543
  50.0 10.8 %collective-permute-start.19 = (f32[17,8,256]{2,1,0:T(8,128)S(1)}, f32[17,8,256]{2,1,0:T(8,128)S(1)}, u32[]{:S(2)}, u32[]{:S(2)}) collective-permute-start(f32[17,8,256]{2,1,0:T(8,128)S(1)} %get-tuple-element.78), channel_id=1, source_target_pairs={{0,24},{4,28},{8,16},{12,20},{16,8},{20,12},{24,0},{28,4},{1,25},{... | collective-permute-start | bytes 417800 | tf_op jit(solution)/shard_map/ppermute | solution.py:543
  60.9 3.8 %collective-permute-start.20 = (f32[2,8,256]{2,1,0:T(8,128)S(1)}, f32[2,8,256]{2,1,0:T(8,128)S(1)}, u32[]{:S(2)}, u32[]{:S(2)}) collective-permute-start(f32[2,8,256]{2,1,0:T(8,128)S(1)} %add_smalls.1.refs_0_), channel_id=1, source_target_pairs={{0,4},{4,0},{8,12},{12,8},{16,20},{20,16},{24,28},{28,24},{1,5},{5... | collective-permute-start | bytes 49160 | tf_op jit(solution)/shard_map/ppermute | solution.py:543

commit v11 on v10

--- a/solution.py
+++ b/solution.py
@@ -29,17 +29,13 @@
     return lax.rem(lax.div(mine, nx) + lax.rem(mine, nx), 2)
 
 
-def prepare_kernel(parts, nx, *refs):
-    arguments, orbit = refs[:6], refs[6]
-    planes, extra, message = refs[7:10]
-    copied, sems, cut_sem = refs[10:16], refs[16], refs[17]
+def prepare_kernel(*refs):
+    arguments = refs[:6]
+    planes, extra = refs[6:8]
+    copied, sems = refs[8:14], refs[14]
     copies = [pltpu.make_async_copy(arguments[n], copied[n], sems.at[n]) for n in range(6)]
     for copy in copies:
         copy.start()
-    size = orbit.shape[0] // parts
-    at = turn_of(lax.axis_index("sta"), nx) * size if parts > 1 else 0
-    cut = pltpu.make_async_copy(orbit.at[pl.ds(at, size)], message, cut_sem)
-    cut.start()
     for copy in copies:
         copy.wait()
     sight, mapping, residual, counts, track, knots = copied
@@ -79,50 +75,48 @@
         extra[s, tracked:, :] = jnp.where(weight > 0.0, total / jnp.maximum(weight, 1.0), 0.0)
 
 
-    cut.wait()
-
-
-def prepare(arguments, orbit, parts, nx):
+def prepare(*arguments):
     stations, _, tracked, epochs = arguments[0].shape
-    rows = 4 * tracked + 8
-    size = orbit.shape[0] // parts
     f32 = jnp.float32
     return pl.pallas_call(
-        functools.partial(prepare_kernel, parts, nx),
+        prepare_kernel,
         out_shape=[
-            jax.ShapeDtypeStruct((stations, rows, epochs), f32),
+            jax.ShapeDtypeStruct((stations, 4 * tracked + 8, epochs), f32),
             jax.ShapeDtypeStruct((stations, 2 * tracked, epochs), f32),
-            jax.ShapeDtypeStruct((size,) + orbit.shape[1:], f32),
         ],
-        in_specs=[hbm()] * 7,
-        out_specs=[vmem()] * 3,
+        in_specs=[hbm()] * 6,
+        out_specs=[vmem()] * 2,
         scratch_shapes=[pltpu.VMEM(a.shape, a.dtype) for a in arguments]
-        + [pltpu.SemaphoreType.DMA((6,)), pltpu.SemaphoreType.DMA],
+        + [pltpu.SemaphoreType.DMA((6,))],
         compiler_params=pltpu.CompilerParams(vmem_limit_bytes=HUGE_LIMIT),
         name="prepare",
-    )(*arguments, orbit)
-
-
-def open_kernel(message, first, second):
-    size = first.shape[0]
-    first[...] = message[:size]
-    second[...] = message[size:]
-
-
-def open_message(message):
-    size = message.shape[0]
-    lead = size * 2 // 3
-    return pl.pallas_call(
-        open_kernel,
+    )(*arguments)
+
+
+def cut_kernel(nx, orbit, first, second, copy):
+    half = orbit.shape[0] // 2
+    lead = first.shape[0]
+    at = turn_of(lax.axis_index("sta"), nx) * half
+    first[...] = orbit[pl.ds(at, lead)]
+    second[...] = orbit[pl.ds(at + lead, half - lead)]
+    copy[...] = orbit[...]
+
+
+def cut_parts(orbit, nx):
+    own = orbit.shape[0]
+    lead = own // 2 - own // 4
+    *parts, copy = pl.pallas_call(
+        functools.partial(cut_kernel, nx),
         out_shape=[
-            jax.ShapeDtypeStruct((n,) + message.shape[1:], jnp.float32)
-            for n in (lead, size - lead)
+            jax.ShapeDtypeStruct((n,) + orbit.shape[1:], jnp.float32)
+            for n in (lead, own // 2 - lead, own)
         ],
         in_specs=[vmem()],
-        out_specs=[vmem()] * 2,
+        out_specs=[vmem()] * 3,
         compiler_params=pltpu.CompilerParams(vmem_limit_bytes=SMALL_LIMIT),
-        name="open_message",
-    )(message)
+        name="cut_parts",
+    )(orbit)
+    return parts, copy
 
 
 def window_start(i, columns, sats, window):
@@ -245,13 +239,14 @@
     )(*pieces)
 
 
-def main_kernel(own, nx, nz, window, *refs):
-    sets = [refs[4 * n : 4 * n + 4] for n in range(nx)]
-    orbit, small = refs[4 * nx : 4 * nx + 2]
-    refs = refs[4 * nx + 2 :]
-    outs = refs[:nz]
+def main_kernel(count, own, nx, nz, window, *refs):
+    sets = [refs[4 * n : 4 * n + 4] for n in range(count)]
+    orbit = refs[4 * count]
+    refs = refs[4 * count + 1 :]
+    outs = refs[: 2 * nx]
+    own_out = refs[2 * nx]
     (acc, stream_a, stream_b, product_a, product_b, tropo_a, tropo_b,
-     spread_tropo) = refs[nz:]
+     spread_tropo) = refs[2 * nx + 1 :]
     streams = (stream_a, stream_b)
     products, tropos = (product_a, product_b), (tropo_a, tropo_b)
     stations = sets[0][0].shape[0]
@@ -331,7 +326,7 @@
         multiply(stations - 1, 1)
         scatter(stations - 1, 1)
 
-    for n in range(nx):
+    for n in range(count):
         run(n * stations, *sets[n])
 
     outer = jnp.zeros((sats * 8, own * 8), jnp.float32)
@@ -347,33 +342,29 @@
     acc[...] = acc[...] - outer.reshape(sats, 8, width)
 
     columns = sats * 8 // (nx * nz)
-    owner = lax.broadcasted_iota(jnp.int32, (8, width), 1) // 8
-    here = lax.rem(lax.div((first + owner) * 8, columns), nx) == lax.rem(mine, nx)
-    folded = jnp.zeros((8, width), jnp.float32)
-    for o in range(own):
-        folded = folded + jnp.where(owner == o, acc[first + o], 0.0)
-    folded = small[0] + jnp.where(here, folded, 0.0)
-    for dz in range(nz):
-        start = window_start(mine ^ (dz * nx), columns, sats, window)
-        outs[dz][:window] = acc[pl.ds(start, window)]
-        outs[dz][window] = folded
-        outs[dz][window + 1] = small[1]
-
-
-def accumulate(sets, orbit, small, own, nz, window):
-    nx = len(sets)
+    own_out[...] = acc[pl.ds(first, own)]
+    half = nz // 2
+    for dx in range(nx):
+        for dz in range(nz):
+            start = window_start(mine ^ (dz * nx + dx), columns, sats, window)
+            at = (dz % half) * window
+            outs[2 * dx + (dz < half)][at : at + window] = acc[pl.ds(start, window)]
+
+
+def accumulate(sets, orbit, own, nx, nz, window):
+    count = len(sets)
     stations, rows, epochs = sets[0][0].shape
     sats = orbit.shape[0]
     tracked = (rows - 8) // 4
     width = sets[0][2].shape[1]
-    slabs = -(-nx * stations // PACKED)
-    out = jax.ShapeDtypeStruct((window + 2, 8, width), jnp.float32)
+    slabs = -(-count * stations // PACKED)
+    out = jax.ShapeDtypeStruct((nz // 2 * window, 8, width), jnp.float32)
     return pl.pallas_call(
-        functools.partial(main_kernel, own, nx, nz, window),
-        out_shape=[out] * nz,
-        in_specs=[vmem(), pl.BlockSpec(memory_space=pltpu.SMEM), vmem(), vmem()] * nx
-        + [vmem()] * 2,
-        out_specs=[vmem()] * nz,
+        functools.partial(main_kernel, count, own, nx, nz, window),
+        out_shape=[out] * (2 * nx) + [jax.ShapeDtypeStruct((own, 8, width), jnp.float32)],
+        in_specs=[vmem(), pl.BlockSpec(memory_space=pltpu.SMEM), vmem(), vmem()] * count
+        + [vmem()],
+        out_specs=[vmem()] * (2 * nx + 1),
         scratch_shapes=[
             pltpu.VMEM((sats, 8, width), jnp.float32),
             *[pltpu.VMEM((4 * tracked * 8, epochs), jnp.bfloat16)] * 2,
@@ -385,13 +376,13 @@
         cost_estimate=pl.CostEstimate(
             flops=8 * 10**9, bytes_accessed=8 * 10**6, transcendentals=0),
         name="accumulate",
-    )(*[part for group in sets for part in group], orbit, small)
+    )(*[part for group in sets for part in group], orbit)
 
 
 def blocks_kernel(groups, per, *refs):
     plane_pieces = refs[:groups]
     extra_pieces = refs[groups : 2 * groups]
-    orbit, small = refs[2 * groups :]
+    own_rows, orbit, small = refs[2 * groups :]
     tracked = extra_pieces[0].shape[1] // 2
     epochs = orbit.shape[3]
     width = small.shape[2]
@@ -437,106 +428,97 @@
     owner = lax.broadcasted_iota(jnp.int32, (8, own * 8), 1) // 8
     folded = jnp.zeros((8, own * 8), jnp.float32)
     for o in range(own):
-        folded = folded + jnp.where(owner == o, blocks[o * 8 : o * 8 + 8, :], 0.0)
+        tile = own_rows[o, :, : own * 8] + blocks[o * 8 : o * 8 + 8, :]
+        folded = folded + jnp.where(owner == o, tile, 0.0)
     small[...] = jnp.zeros_like(small)
     small[0, :, : own * 8] = folded
     small[1, :, : own * 8] = right
 
 
-def own_sums(planes, extras, orbit, width):
+def own_sums(planes, extras, own_rows, orbit):
     groups = len(planes)
     per = extras[0].shape[0]
+    width = own_rows.shape[2]
     return pl.pallas_call(
         functools.partial(blocks_kernel, groups, per),
         out_shape=jax.ShapeDtypeStruct((2, 8, width), jnp.float32),
-        in_specs=[vmem()] * (2 * groups + 1),
+        in_specs=[vmem()] * (2 * groups + 2),
         out_specs=vmem(),
         compiler_params=pltpu.CompilerParams(vmem_limit_bytes=MEDIUM_LIMIT),
         cost_estimate=pl.CostEstimate(
             flops=1 * 10**8, bytes_accessed=1 * 10**5, transcendentals=0),
         name="own_sums",
-    )(*planes, *extras, orbit)
-
-
-def add_kernel(window, *refs):
-    total = refs[0][window:]
-    for ref in refs[1:-1]:
-        total = total + ref[window:]
-    refs[-1][...] = total
-
-
-def add_smalls(pieces, window):
+    )(*planes, *extras, own_rows, orbit)
+
+
+def combine_kernel(pieces_count, smalls_count, window, *refs):
+    pieces, smalls = refs[:pieces_count], refs[pieces_count : pieces_count + smalls_count]
+    outs = refs[pieces_count + smalls_count :]
+    small = smalls[0][...]
+    for ref in smalls[1:]:
+        small = small + ref[...]
+    for n, out in enumerate(outs):
+        part = pieces[0][n * window : (n + 1) * window]
+        for piece in pieces[1:]:
+            part = part + piece[n * window : (n + 1) * window]
+        out[:window] = part
+        out[window:] = small
+
+
+def combine(pieces, smalls, window):
+    count = pieces[0].shape[0] // window
     width = pieces[0].shape[2]
     return pl.pallas_call(
-        functools.partial(add_kernel, window),
-        out_shape=jax.ShapeDtypeStruct((2, 8, width), jnp.float32),
-        in_specs=[vmem()] * len(pieces),
-        out_specs=vmem(),
+        functools.partial(combine_kernel, len(pieces), len(smalls), window),
+        out_shape=[jax.ShapeDtypeStruct((window + 2, 8, width), jnp.float32)] * count,
+        in_specs=[vmem()] * (len(pieces) + len(smalls)),
+        out_specs=[vmem()] * count,
         compiler_params=pltpu.CompilerParams(vmem_limit_bytes=SMALL_LIMIT),
-        name="add_smalls",
-    )(*pieces)
-
-
-def finish_kernel(window, own, columns, sats, cross_factor, *refs):
-    pieces, normal = refs[:-1], refs[-1]
+        name="combine",
+    )(*pieces, *smalls)
+
+
+def finish_kernel(window, own, columns, sats, factor, cross_factor, *refs):
+    pieces = refs[:-3]
+    normal, right, blocks = refs[-3:]
     width = pieces[0].shape[2]
-    total = pieces[0][:window]
+    total = pieces[0][...]
     for piece in pieces[1:]:
-        total = total + piece[:window]
+        total = total + piece[...]
     first = lax.axis_index("sat") * own
     start = window_start(lax.axis_index("sta"), columns, sats, window)
-    part = total.reshape(window * 8, width)
+    part = total[:window].reshape(window * 8, width)
     row_owner = start + lax.broadcasted_iota(jnp.int32, part.shape, 0) // 8
     lane_owner = first + lax.broadcasted_iota(jnp.int32, part.shape, 1) // 8
     part = jnp.where(row_owner == lane_owner, 0.0, part * cross_factor)
     normal[...] = part.T[: own * 8, :]
-
-
-def finish(pieces, window, own, columns, sats, cross_factor):
-    return pl.pallas_call(
-        functools.partial(finish_kernel, window, own, columns, sats, cross_factor),
-        out_shape=jax.ShapeDtypeStruct((own * 8, window * 8), jnp.float32),
-        in_specs=[vmem()] * len(pieces),
-        out_specs=vmem(),
-        compiler_params=pltpu.CompilerParams(vmem_limit_bytes=SMALL_LIMIT),
-        cost_estimate=pl.CostEstimate(
-            flops=2 * 10**9, bytes_accessed=2 * 10**6, transcendentals=0),
-        name="finish",
-    )(*pieces)
-
-
-def finish_own_kernel(own, factor, *refs):
-    smalls = refs[:-2]
-    right, blocks = refs[-2:]
-    total = smalls[0][...]
-    for small in smalls[1:]:
-        total = total + small[...]
-    width = total.shape[2]
-    right[...] = total[1, :1, : own * 8] * factor
+    right[...] = total[window + 1, :1, : own * 8] * factor
+    small = total[window]
     room = -(-own // 32) * 32
     lane = lax.broadcasted_iota(jnp.int32, (width, 8 * room), 0)
     slot = lax.broadcasted_iota(jnp.int32, (width, 8 * room), 1)
     pick = (lane == slot % room * 8 + slot // room).astype(jnp.bfloat16)
-    high, low = split(total[0])
-    lower = (total[0] - high.astype(jnp.float32) - low.astype(jnp.float32)).astype(jnp.bfloat16)
+    high, low = split(small)
+    lower = (small - high.astype(jnp.float32) - low.astype(jnp.float32)).astype(jnp.bfloat16)
     spread = sum(jnp.dot(part, pick, preferred_element_type=jnp.float32)
                  for part in (high, low, lower))
     for p in range(8):
         blocks[p] = factor * spread[:, p * room : p * room + own]
 
 
-def finish_own(smalls, own, factor):
+def finish(pieces, window, own, columns, sats, factor, cross_factor):
     return pl.pallas_call(
-        functools.partial(finish_own_kernel, own, factor),
+        functools.partial(finish_kernel, window, own, columns, sats, factor, cross_factor),
         out_shape=[
+            jax.ShapeDtypeStruct((own * 8, window * 8), jnp.float32),
             jax.ShapeDtypeStruct((1, own * 8), jnp.float32),
             jax.ShapeDtypeStruct((8, 8, own), jnp.float32),
         ],
-        in_specs=[vmem()] * len(smalls),
-        out_specs=[vmem()] * 2,
+        in_specs=[vmem()] * len(pieces),
+        out_specs=[vmem()] * 3,
         compiler_params=pltpu.CompilerParams(vmem_limit_bytes=SMALL_LIMIT),
-        name="finish_own",
-    )(*smalls)
+        name="finish",
+    )(*pieces)
 
 
 def shift(value, axis, size, step):
@@ -559,70 +541,62 @@
         -(-(((columns * i) % 8) + columns) // 8) for i in range(columns_axis)
     )
 
-    parts = 2 if own % 2 == 0 and nz % 2 == 0 and nx % 2 == 0 else 1
-    planes, extra, message = prepare(
-        (sight, mapping, residual, counts, track, knots), orbit, parts, nx)
 
     def core(value):
         return shift(value, "sat", group, 1)
 
-    early = [planes, orbit, extra]
-    early += [core(value) for value in early]
-    beside = {dx: shift(planes, "sta", columns_axis, dx) for dx in range(1, nx)}
-    crossed = {dx: core(value) for dx, value in beside.items()}
-    arrived = {d: shift(planes, "sat", group, d) for d in range(2, group, 2)}
-    (early, beside, arrived, message) = lax.optimization_barrier(
-        (early, beside, arrived, message))
-    planes, orbit, extra, other_planes, other_orbit, other_extra = early
-
-    pieces = [[(0, planes), (1, other_planes)]]
-    pieces += [[(0, beside[dx]), (1, crossed[dx])] for dx in range(1, nx)]
+    def across(value, step):
+        return shift(value, "sta", columns_axis, step)
+
+    parts = [orbit]
+    if own % 2 == 0 and nz % 2 == 0 and nx % 2 == 0:
+        parts, orbit = cut_parts(orbit, nx)
+    near = {d: [shift(part, "sat", group, d) for part in parts] for d in range(2, group, 2)}
+    planes, extra = prepare(sight, mapping, residual, counts, track, knots)
+    own_planes = planes
+    other_planes, other_orbit, other_extra = core(planes), core(orbit), core(extra)
+    planes, near = lax.optimization_barrier((planes, near))
+    arrived = {d: shift(planes, "sat", group, d) for d in near}
+    far = {}
+    if len(parts) == 2:
+        far = {d: [across(near[d][0], nx), across(near[d][1], 1)] for d in near}
+    sets = [own_rows_of([own_planes, other_planes], planes.shape, orbit, width, 0)]
+    sets[0], arrived = lax.optimization_barrier((tuple(sets[0]), arrived))
     partials = [(0, 0, 0, orbit), (1, 0, 0, other_orbit)]
+    for d in near:
+        for turn, values in ((0, near[d]), (1, far.get(d, []))):
+            for start, value in zip((0, parts[0].shape[0]), values):
+                partials += [(d, turn, start, value), (d + 1, turn, start, core(value))]
+    pieces = {0: own_planes, 1: other_planes}
     extras = {0: extra, 1: other_extra}
-    messages, passed = {}, {}
     for d, value in arrived.items():
-        messages[d] = shift(message, "sat", group, d)
-        pieces[0] += [(d, value), (d + 1, core(value))]
-        for dx in range(1, nx):
-            passed[dx, d] = shift(value, "sta", columns_axis, dx)
-    sets = [own_rows_of([value for _, value in pieces[0]], planes.shape, orbit, width, 0)]
-    sets[0], messages, passed = lax.optimization_barrier((tuple(sets[0]), messages, passed))
-    for (dx, d), value in passed.items():
-        pieces[dx] += [(d, value), (d + 1, core(value))]
-    far = []
-    for d, value in messages.items():
-        held, value = lax.optimization_barrier((extra, value))
+        pieces[d], pieces[d + 1] = value, core(value)
+        sets.append(own_rows_of([pieces[d], pieces[d + 1]], planes.shape, orbit, width,
+                                d * stations))
+        held, _ = lax.optimization_barrier((extra, value))
         extras[d] = shift(held, "sat", group, d)
+        sets[-1], extras[d] = lax.optimization_barrier((tuple(sets[-1]), extras[d]))
         extras[d + 1] = core(extras[d])
-        partials += [(d, 0, 0, value), (d + 1, 0, 0, core(value))]
-        if parts > 1:
-            first, second = open_message(value)
-            far += [(d, 0, shift(first, "sta", columns_axis, nx)),
-                    (d, first.shape[0], shift(second, "sta", columns_axis, 1))]
-    for dx in range(1, nx):
-        sets.append(own_rows_of(
-            [value for _, value in pieces[dx]], planes.shape, orbit, width,
-            dx * group * stations))
-    held = [value for _, _, value in far]
-    track1, held = lax.optimization_barrier((sets[-1][1], held))
-    sets[-1] = (sets[-1][0], track1, *sets[-1][2:])
-    for (d, start, _), value in zip(far, held):
-        partials += [(d, 1, start, value), (d + 1, 1, start, core(value))]
-    small = own_sums([value for _, value in pieces[0]],
-                     [extras[d] for d, _ in pieces[0]], orbit, width)
     places = tuple((d, turn, start) for d, turn, start, _ in partials)
     every = place([part[3] for part in partials], places, sats, own, nx)
-    sums = accumulate(sets, every, small, own, nz, window)
-    final = [sums[0]] + [
-        shift(sums[d], "sta", columns_axis, d * nx) for d in range(1, nz)
-    ]
-    small = add_smalls(final, window)
-    smalls = [small] + [shift(small, "sta", columns_axis, d) for d in range(1, nx)]
+    *sums, own_rows = accumulate(sets, every, own, nx, nz, window)
+
+    far_sums = [sums[0]] + [across(sums[2 * dx], dx) for dx in range(1, nx)]
+    small = own_sums([pieces[d] for d in range(group)], [extras[d] for d in range(group)],
+                     own_rows, orbit)
+    smalls = [small] + [across(small, dx) for dx in range(1, nx)]
+    near_out, far_sums, smalls = lax.optimization_barrier((sums[1::2], far_sums, smalls))
+    near_sums = [near_out[0]] + [across(near_out[dx], dx) for dx in range(1, nx)]
+    far_chunks = combine(far_sums, smalls, window)
+    near_chunks = combine(near_sums, smalls, window)
+    half = nz // 2
+    final = [across(chunk, (half + n) * nx) for n, chunk in enumerate(far_chunks)]
+    final += [near_chunks[0]]
+    final += [across(near_chunks[n], n * nx) for n in range(1, half)]
     total_stations = stations * columns_axis * group
     factor = sats / (total_stations * tracked * epochs)
     cross_factor = sats / (total_stations * epochs) ** 0.5
-    normal = finish(final, window, own, columns, sats, cross_factor)
-    right, blocks = finish_own(smalls, own, factor)
+    normal, right, blocks = finish(final, window, own, columns, sats, factor, cross_factor)
     if window * 8 != columns:
         mine = lax.axis_index("sta")
         start = window_start(mine, columns, sats, window)

time: 65.7 us -> 57.4 us (0.87)
  Pallas kernels: 19 us -> 12.1 us
  waiting for transfers between devices: 27.2 us -> 23 us
  starting transfers between devices: 17.6 us -> 19.3 us
  local copies, waits for them, and re-layouts: 0.96 us -> 2.07 us
    pallas_call x5, Pallas kernels: 11 us -> 5.54 us  [the longest x1 3.43 us: accumulate(): pl.pallas_call(functools.partial(main_kernel, count, own, nx, nz, window)...]
    ppermute x21, waiting for transfers between devices: 27.2 us -> 23 us  [shift(): return lax.ppermute(value, axis, [(i, i ^ step) for i in range(size)])]
    ppermute x21, starting transfers between devices: 17.6 us -> 19.3 us  [shift(): return lax.ppermute(value, axis, [(i, i ^ step) for i in range(size)])]
    pallas_call x2, Pallas kernels: 5.66 us -> 4.1 us  [own_rows_of(): pl.pallas_call(functools.partial(own_rows_kernel, groups, per, own, width...]
    unnamed x8, local copies, waits for them, and re-layouts: 0.96 us -> 2.07 us
  transfers between devices with their start and end apart: 21 -> 21, of which waited for: 11 -> 11; matrix products, arithmetic and copies ran while one was open for 0% -> 0% of each run, Pallas kernels for 15% -> 13%
where the time goes in v11:
time: 57.4 us; the launch traced here: 57.3 us
  waiting for transfers between devices  23 us (40%)
  starting transfers between devices  19.3 us (34%)
  Pallas kernels  12.1 us (21%)
  local copies, waits for them, and re-layouts  2.07 us (4%)
  between operations  0.73 us (1%)
    ppermute x21, waiting for transfers between devices, shift(): return lax.ppermute(value, axis, [(i, i ^ step) for i in range(size)])  23 us
    ppermute x21, starting transfers between devices, shift(): return lax.ppermute(value, axis, [(i, i ^ step) for i in range(size)])  19.3 us
    pallas_call x2, Pallas kernels, own_rows_of(): pl.pallas_call(functools.partial(own_rows_kernel, groups, per, own, width...  4.1 us
    pallas_call x1, Pallas kernels, accumulate(): pl.pallas_call(functools.partial(main_kernel, count, own, nx, nz, window)...  3.43 us
    unnamed x8, local copies, waits for them, and re-layouts  2.07 us
    pallas_call x1, Pallas kernels, prepare(): pl.pallas_call(prepare_kernel, out_shape=[jax.ShapeDtypeStruct((stations,...  1.97 us
    pallas_call x1, Pallas kernels, own_sums(): pl.pallas_call(functools.partial(blocks_kernel, groups, per), out_shape=j...  1.31 us
  transfers between devices with their start and end apart: 21, of which 11 were waited for; matrix products, arithmetic and copies ran while one was open for 0% of the time, Pallas kernels for 13%

profile of v11, /device:TPU:0, one launch (start us, length us, event | category | flops | bytes accessed | tf_op | source)
XLA Modules:
  0.0 57.3 jit_solution(18432122566036551183)
XLA Ops:
  0.6 0.0 copy-start
  0.6 1.1 %copy-done = f32[30,3,8,256]{3,2,1,0:T(8,128)S(1)} copy-done((f32[30,3,8,256]{3,2,1,0:T(8,128)S(1)}, f32[30,3,8,256]{3,2,1,0:T(8,128)}, u32[]{:S(2)}) %copy-start) | copy-done | bytes 737304
  1.7 0.1 cut_parts.1
  1.8 3.0 %collective-permute-start.1 = (f32[8,3,8,256]{3,2,1,0:T(8,128)S(1)}, f32[8,3,8,256]{3,2,1,0:T(8,128)S(1)}, u32[]{:S(2)}, u32[]{:S(2)}) collective-permute-start(f32[8,3,8,256]{3,2,1,0:T(8,128)S(1)} %get-tuple-element.54), channel_id=1, source_target_pairs={{0,2},{1,3},{2,0},{3,1},{4,6},{5,7},{6,4},{7,5},{8,10},{9,11},{10,... | collective-permute-start | bytes 589832 | tf_op jit(solution)/shard_map/ppermute | solution.py:525
  4.9 2.0 %prepare.1 = (f32[2,136,256]{2,1,0:T(8,128)}, f32[2,64,256]{2,1,0:T(8,128)}) custom-call(f32[2,3,32,256]{3,2,1,0:T(8,128)} %refs_0_.1, f32[2,32,256]{2,1,0:T(8,128)} %refs_1_.1, f32[2,32,256]{2,1,0:T(8,128)} %refs_2_.1, s32[2,32,256]{2,1,0:T(8,128)} %refs_3_.1, s32[2,32]{1,0:T(2,128)} %refs_4_.1, s32[2,256]{1,0:T(2,128)} %refs_5_.1), custom_call_target="tpu_custom_call" | custom-call | tf_op jit(solution)/shard_map/prepare/pallas_call | solution.py:81
  6.8 0.1 collective-permute-start
  6.9 0.5 collective-permute-start.6
  7.4 0.0 collective-permute-start.2
  7.4 6.3 %collective-permute-done.2.refs_4_ = f32[7,3,8,256]{3,2,1,0:T(8,128)S(1)} collective-permute-done((f32[7,3,8,256]{3,2,1,0:T(8,128)S(1)}, f32[7,3,8,256]{3,2,1,0:T(8,128)S(1)}, u32[]{:S(2)}, u32[]{:S(2)}) %collective-permute-start.2) | collective-permute-done | bytes 172064 | tf_op jit(solution)/shard_map/ppermute | solution.py:525
  13.8 0.0 collective-permute-done.1.refs_2_
  13.8 1.4 %collective-permute-start.3 = (f32[2,136,256]{2,1,0:T(8,128)}, f32[2,136,256]{2,1,0:T(8,128)S(1)}, u32[]{:S(2)}, u32[]{:S(2)}) collective-permute-start(f32[2,136,256]{2,1,0:T(8,128)} %get-tuple-element.56.refs_0_), channel_id=1, source_target_pairs={{0,2},{1,3},{2,0},{3,1},{4,6},{5,7},{6,4},{7,5},{8,10},{9,11},{10,... | collective-permute-start | bytes 835592 | tf_op jit(solution)/shard_map/ppermute | solution.py:525
  15.2 1.5 %collective-permute-start.11 = (f32[7,3,8,256]{3,2,1,0:T(8,128)S(1)}, f32[7,3,8,256]{3,2,1,0:T(8,128)S(1)}, u32[]{:S(2)}, u32[]{:S(2)}) collective-permute-start(f32[7,3,8,256]{3,2,1,0:T(8,128)S(1)} %collective-permute-done.2.refs_4_), channel_id=1, source_target_pairs={{0,4},{4,0},{8,12},{12,8},{16,20},{20,16},{24,28},{28,24},{1,5},{5... | collective-permute-start | bytes 516104 | tf_op jit(solution)/shard_map/ppermute | solution.py:525
  16.7 0.0 collective-permute-start.8
  16.7 0.0 collective-permute-done.refs_1_
  16.7 1.6 %collective-permute-start.9 = (f32[8,3,8,256]{3,2,1,0:T(8,128)S(1)}, f32[8,3,8,256]{3,2,1,0:T(8,128)S(1)}, u32[]{:S(2)}, u32[]{:S(2)}) collective-permute-start(f32[8,3,8,256]{3,2,1,0:T(8,128)S(1)} %collective-permute-done.1.refs_2_), channel_id=1, source_target_pairs={{0,8},{4,12},{8,0},{12,4},{16,24},{20,28},{24,16},{28,20},{1,9},{5... | collective-permute-start | bytes 589832 | tf_op jit(solution)/shard_map/ppermute | solution.py:525
  18.3 0.0 copy-start.1
  18.3 1.0 %copy-done.1 = f32[2,136,256]{2,1,0:T(8,128)S(1)} copy-done((f32[2,136,256]{2,1,0:T(8,128)S(1)}, f32[2,136,256]{2,1,0:T(8,128)}, u32[]{:S(2)}) %copy-start.1) | copy-done | bytes 278552
  19.2 0.0 copy-start.3
  19.2 2.1 %own_rows.2 = (f32[4,136,256]{2,1,0:T(8,128)S(1)}, s32[4,128]{1,0:T(4,128)S(1)}, bf16[4,256,256]{2,1,0:T(8,128)(2,1)S(1)}, bf16[4,256,256]{2,1,0:T(8,128)(2,1)S(1)}) custom-call(f32[2,136,256]{2,1,0:T(8,128)S(1)} %copy-done.1, f32[2,136,256]{2,1,0:T(8,128)S(1)} %collective-permute-done.refs_1_, f32[30,3,8,256]{3,2,1,0:T(8,128)S(1)} %get-tuple-element.49.refs_2_.refs_0_.refs_9_), custom_call_target="tpu_custom_call" | custom-call | flops 2000000000 | bytes 2000000 | tf_op jit(solution)/shard_map/own_rows/pallas_call | solution.py:198
  21.3 0.5 collective-permute-done.3.refs_0_.refs_2_
  21.8 0.0 collective-permute-start.4
  21.8 0.0 collective-permute-done.11.refs_8_
  21.8 0.5 collective-permute-start.7
  22.3 1.7 %collective-permute-done.9.refs_6_ = f32[8,3,8,256]{3,2,1,0:T(8,128)S(1)} collective-permute-done((f32[8,3,8,256]{3,2,1,0:T(8,128)S(1)}, f32[8,3,8,256]{3,2,1,0:T(8,128)S(1)}, u32[]{:S(2)}, u32[]{:S(2)}) %collective-permute-start.9) | collective-permute-done | bytes 196640 | tf_op jit(solution)/shard_map/ppermute | solution.py:525
  24.0 0.0 collective-permute-start.10
  24.0 0.0 collective-permute-done.8.refs_5_
  24.0 0.5 collective-permute-start.12
  24.5 0.0 collective-permute-done.7.refs_3_
  24.5 0.0 copy-done.3
  24.5 0.6 %collective-permute-start.5 = (f32[2,64,256]{2,1,0:T(8,128)S(1)}, f32[2,64,256]{2,1,0:T(8,128)S(1)}, u32[]{:S(2)}, u32[]{:S(2)}) collective-permute-start(f32[2,64,256]{2,1,0:T(8,128)S(1)} %copy-done.3), channel_id=1, source_target_pairs={{0,2},{1,3},{2,0},{3,1},{4,6},{5,7},{6,4},{7,5},{8,10},{9,11},{10,... | collective-permute-start | bytes 393224 | tf_op jit(solution)/shard_map/ppermute | solution.py:525
  25.1 0.6 collective-permute-done.12.refs_9_
  25.7 0.0 collective-permute-done.10.refs_7_
  25.7 0.0 collective-permute-done.6.refs_1_
  25.7 0.2 place.1.refs_8_
  25.9 0.0 collective-permute-done.4.refs_1_.refs_3_
  25.9 2.0 %own_rows.3 = (f32[4,136,256]{2,1,0:T(8,128)S(1)}, s32[4,128]{1,0:T(4,128)S(1)}, bf16[4,256,256]{2,1,0:T(8,128)(2,1)S(1)}, bf16[4,256,256]{2,1,0:T(8,128)(2,1)S(1)}) custom-call(f32[2,136,256]{2,1,0:T(8,128)S(1)} %collective-permute-done.3.refs_0_.refs_2_, f32[2,136,256]{2,1,0:T(8,128)S(1)} %collective-permute-done.4.refs_1_.refs_3_, ...), custom_call_target="tpu_custom_call" | custom-call | flops 2000000000 | bytes 2000000 | tf_op jit(solution)/shard_map/own_rows/pallas_call | solution.py:198
  28.0 2.0 %collective-permute-done.5.refs_6_ = f32[2,64,256]{2,1,0:T(8,128)S(1)} collective-permute-done((f32[2,64,256]{2,1,0:T(8,128)S(1)}, f32[2,64,256]{2,1,0:T(8,128)S(1)}, u32[]{:S(2)}, u32[]{:S(2)}) %collective-permute-start.5) | collective-permute-done | bytes 131104 | tf_op jit(solution)/shard_map/ppermute | solution.py:525
  30.0 0.0 copy-start.2
  30.0 3.4 %accumulate.1 = (f32[30,8,256]{2,1,0:T(8,128)S(1)}, f32[30,8,256]{2,1,0:T(8,128)S(1)}, f32[30,8,256]{2,1,0:T(8,128)S(1)}, f32[30,8,256]{2,1,0:T(8,128)S(1)}, f32[30,8,256]{2,1,0:T(8,128)S(1)}) custom-call(f32[4,136,256]{2,1,0:T(8,128)S(1)} %get-tuple-element.57.refs_0_, s32[4,128]{1,0:T(4,128)S(1)} %get-tuple-element.58.refs_1_, ...), custom_call_target="tpu_custom_call" | custom-call | flops 8000000000 | bytes 8000000 | tf_op jit(solution)/shard_map/accumulate/pallas_call | solution.py:362
  33.4 0.7 %collective-permute-start.13 = (f32[30,8,256]{2,1,0:T(8,128)S(1)}, f32[30,8,256]{2,1,0:T(8,128)S(1)}, u32[]{:S(2)}, u32[]{:S(2)}) collective-permute-start(f32[30,8,256]{2,1,0:T(8,128)S(1)} %get-tuple-element.77), channel_id=1, source_target_pairs={{0,4},{4,0},{8,12},{12,8},{16,20},{20,16},{24,28},{28,24},{1,5},{5... | collective-permute-start | bytes 737288 | tf_op jit(solution)/shard_map/ppermute | solution.py:525
  34.2 0.0 collective-permute-start.14
  34.2 0.5 collective-permute-start.15
  34.7 0.8 %collective-permute-done.14.refs_5_ = f32[2,64,256]{2,1,0:T(8,128)S(1)} collective-permute-done((f32[2,64,256]{2,1,0:T(8,128)S(1)}, f32[2,64,256]{2,1,0:T(8,128)S(1)}, u32[]{:S(2)}, u32[]{:S(2)}) %collective-permute-start.14) | collective-permute-done | bytes 131104 | tf_op jit(solution)/shard_map/ppermute | solution.py:525
  35.5 0.2 collective-permute-done.15.refs_7_
  35.7 0.0 copy-done.2
  35.7 1.3 %own_sums.1.refs_2_ = f32[2,8,256]{2,1,0:T(8,128)S(1)} custom-call(f32[2,136,256]{2,1,0:T(8,128)S(1)} %copy-done.2, f32[2,136,256]{2,1,0:T(8,128)S(1)} %collective-permute-done.refs_1_, f32[2,136,256]{2,1,0:T(8,128)S(1)} %collective-permute-done.3.refs_0_.refs_2_, f32[2,136,256]{2,1,0:T(8,128)S(1)} %collective-permute-done.4.refs_1_.refs_3_, ...), custom_call_target="tpu_custom_call" | custom-call | flops 100000000 | bytes 100000 | tf_op jit(solution)/shard_map/own_sums/pallas_call | solution.py:442
  37.0 1.4 %collective-permute-start.16 = (f32[2,8,256]{2,1,0:T(8,128)S(1)}, f32[2,8,256]{2,1,0:T(8,128)S(1)}, u32[]{:S(2)}, u32[]{:S(2)}) collective-permute-start(f32[2,8,256]{2,1,0:T(8,128)S(1)} %own_sums.1.refs_2_), channel_id=1, source_target_pairs={{0,4},{4,0},{8,12},{12,8},{16,20},{20,16},{24,28},{28,24},{1,5},{5... | collective-permute-start | bytes 49160 | tf_op jit(solution)/shard_map/ppermute | solution.py:525
  38.5 2.5 %collective-permute-done.16.refs_3_ = f32[2,8,256]{2,1,0:T(8,128)S(1)} collective-permute-done((f32[2,8,256]{2,1,0:T(8,128)S(1)}, f32[2,8,256]{2,1,0:T(8,128)S(1)}, u32[]{:S(2)}, u32[]{:S(2)}) %collective-permute-start.16) | collective-permute-done | bytes 16416 | tf_op jit(solution)/shard_map/ppermute | solution.py:525
  40.9 0.0 collective-permute-done.13.refs_1_
  40.9 1.2 %collective-permute-start.19 = (f32[30,8,256]{2,1,0:T(8,128)S(1)}, f32[30,8,256]{2,1,0:T(8,128)S(1)}, u32[]{:S(2)}, u32[]{:S(2)}) collective-permute-start(f32[30,8,256]{2,1,0:T(8,128)S(1)} %get-tuple-element.87), channel_id=1, source_target_pairs={{0,4},{4,0},{8,12},{12,8},{16,20},{20,16},{24,28},{28,24},{1,5},{5... | collective-permute-start | bytes 737288 | tf_op jit(solution)/shard_map/ppermute | solution.py:525
  42.2 2.7 %collective-permute-start.17 = (f32[17,8,256]{2,1,0:T(8,128)S(1)}, f32[17,8,256]{2,1,0:T(8,128)S(1)}, u32[]{:S(2)}, u32[]{:S(2)}) collective-permute-start(f32[17,8,256]{2,1,0:T(8,128)S(1)} %get-tuple-element.84), channel_id=1, source_target_pairs={{0,16},{4,20},{8,24},{12,28},{16,0},{20,4},{24,8},{28,12},{1,17},{... | collective-permute-start | bytes 417800 | tf_op jit(solution)/shard_map/ppermute | solution.py:525
  44.9 1.3 %collective-permute-start.18 = (f32[17,8,256]{2,1,0:T(8,128)S(1)}, f32[17,8,256]{2,1,0:T(8,128)S(1)}, u32[]{:S(2)}, u32[]{:S(2)}) collective-permute-start(f32[17,8,256]{2,1,0:T(8,128)S(1)} %get-tuple-element.85), channel_id=1, source_target_pairs={{0,24},{4,28},{8,16},{12,20},{16,8},{20,12},{24,0},{28,4},{1,25},{... | collective-permute-start | bytes 417800 | tf_op jit(solution)/shard_map/ppermute | solution.py:525
  46.2 2.2 %collective-permute-done.19.refs_1_ = f32[30,8,256]{2,1,0:T(8,128)S(1)} collective-permute-done((f32[30,8,256]{2,1,0:T(8,128)S(1)}, f32[30,8,256]{2,1,0:T(8,128)S(1)}, u32[]{:S(2)}, u32[]{:S(2)}) %collective-permute-start.19) | collective-permute-done | bytes 245792 | tf_op jit(solution)/shard_map/ppermute | solution.py:525
  48.4 1.6 %collective-permute-start.20 = (f32[17,8,256]{2,1,0:T(8,128)S(1)}, f32[17,8,256]{2,1,0:T(8,128)S(1)}, u32[]{:S(2)}, u32[]{:S(2)}) collective-permute-start(f32[17,8,256]{2,1,0:T(8,128)S(1)} %get-tuple-element.89), channel_id=1, source_target_pairs={{0,8},{4,12},{8,0},{12,4},{16,24},{20,28},{24,16},{28,20},{1,9},{5... | collective-permute-start | bytes 417800 | tf_op jit(solution)/shard_map/ppermute | solution.py:525
  50.1 4.9 %collective-permute-done.17.refs_0_ = f32[17,8,256]{2,1,0:T(8,128)S(1)} collective-permute-done((f32[17,8,256]{2,1,0:T(8,128)S(1)}, f32[17,8,256]{2,1,0:T(8,128)S(1)}, u32[]{:S(2)}, u32[]{:S(2)}) %collective-permute-start.17) | collective-permute-done | bytes 139296 | tf_op jit(solution)/shard_map/ppermute | solution.py:525
  54.9 0.0 collective-permute-done.18.refs_1_
  54.9 1.3 %collective-permute-done.20.refs_3_ = f32[17,8,256]{2,1,0:T(8,128)S(1)} collective-permute-done((f32[17,8,256]{2,1,0:T(8,128)S(1)}, f32[17,8,256]{2,1,0:T(8,128)S(1)}, u32[]{:S(2)}, u32[]{:S(2)}) %collective-permute-start.20) | collective-permute-done | bytes 139296 | tf_op jit(solution)/shard_map/ppermute | solution.py:525
  56.3 1.0 %finish.1 = (f32[240,120]{1,0:T(8,128)}, f32[1,240]{1,0:T(1,128)}, f32[8,8,30]{2,1,0:T(8,128)}) custom-call(f32[17,8,256]{2,1,0:T(8,128)S(1)} %collective-permute-done.17.refs_0_, f32[17,8,256]{2,1,0:T(8,128)S(1)} %collective-permute-done.18.refs_1_, f32[17,8,256]{2,1,0:T(8,128)S(1)} %get-tuple-element.88.refs_2_, ...), custom_call_target="tpu_custom_call" | custom-call | tf_op jit(solution)/shard_map/finish/pallas_call | solution.py:510
  (2 shorter events, 0.1 us)
Async XLA Ops:
  0.6 1.1 %copy-start = (f32[30,3,8,256]{3,2,1,0:T(8,128)S(1)}, f32[30,3,8,256]{3,2,1,0:T(8,128)}, u32[]{:S(2)}) copy-start(f32[30,3,8,256]{3,2,1,0:T(8,128)} %orbit.1) | copy-start | bytes 2211844
  1.8 11.9 %collective-permute-start.1 = (f32[8,3,8,256]{3,2,1,0:T(8,128)S(1)}, f32[8,3,8,256]{3,2,1,0:T(8,128)S(1)}, u32[]{:S(2)}, u32[]{:S(2)}) collective-permute-start(f32[8,3,8,256]{3,2,1,0:T(8,128)S(1)} %get-tuple-element.54), channel_id=1, source_target_pairs={{0,2},{1,3},{2,0},{3,1},{4,6},{5,7},{6,4},{7,5},{8,10},{9,11},{10,... | collective-permute-start | bytes 589832 | tf_op jit(solution)/shard_map/ppermute | solution.py:525
  6.8 9.9 %collective-permute-start = (f32[2,136,256]{2,1,0:T(8,128)}, f32[2,136,256]{2,1,0:T(8,128)S(1)}, u32[]{:S(2)}, u32[]{:S(2)}) collective-permute-start(f32[2,136,256]{2,1,0:T(8,128)} %get-tuple-element.56.refs_0_), channel_id=1, source_target_pairs={{0,1},{1,0},{2,3},{3,2},{4,5},{5,4},{6,7},{7,6},{8,9},{9,8},{10,11... | collective-permute-start | bytes 835592 | tf_op jit(solution)/shard_map/ppermute | solution.py:525
  6.9 18.8 %collective-permute-start.6 = (f32[30,3,8,256]{3,2,1,0:T(8,128)S(1)}, f32[30,3,8,256]{3,2,1,0:T(8,128)S(1)}, u32[]{:S(2)}, u32[]{:S(2)}) collective-permute-start(f32[30,3,8,256]{3,2,1,0:T(8,128)S(1)} %get-tuple-element.49.refs_2_.refs_0_.refs_9_), channel_id=1, source_target_pairs={{0,1},{1,0},{2,3},{3,2},{4,5},{5,4},{6,7},{7,6},{8,9},{9,8},{10,11... | collective-permute-start | bytes 2211848 | tf_op jit(solution)/shard_map/ppermute | solution.py:525
  7.4 6.4 %collective-permute-start.2 = (f32[7,3,8,256]{3,2,1,0:T(8,128)S(1)}, f32[7,3,8,256]{3,2,1,0:T(8,128)S(1)}, u32[]{:S(2)}, u32[]{:S(2)}) collective-permute-start(f32[7,3,8,256]{3,2,1,0:T(8,128)S(1)} %get-tuple-element.55), channel_id=1, source_target_pairs={{0,2},{1,3},{2,0},{3,1},{4,6},{5,7},{6,4},{7,5},{8,10},{9,11},{10,... | collective-permute-start | bytes 516104 | tf_op jit(solution)/shard_map/ppermute | solution.py:525
  13.8 8.0 %collective-permute-start.3 = (f32[2,136,256]{2,1,0:T(8,128)}, f32[2,136,256]{2,1,0:T(8,128)S(1)}, u32[]{:S(2)}, u32[]{:S(2)}) collective-permute-start(f32[2,136,256]{2,1,0:T(8,128)} %get-tuple-element.56.refs_0_), channel_id=1, source_target_pairs={{0,2},{1,3},{2,0},{3,1},{4,6},{5,7},{6,4},{7,5},{8,10},{9,11},{10,... | collective-permute-start | bytes 835592 | tf_op jit(solution)/shard_map/ppermute | solution.py:525
  15.2 6.6 %collective-permute-start.11 = (f32[7,3,8,256]{3,2,1,0:T(8,128)S(1)}, f32[7,3,8,256]{3,2,1,0:T(8,128)S(1)}, u32[]{:S(2)}, u32[]{:S(2)}) collective-permute-start(f32[7,3,8,256]{3,2,1,0:T(8,128)S(1)} %collective-permute-done.2.refs_4_), channel_id=1, source_target_pairs={{0,4},{4,0},{8,12},{12,8},{16,20},{20,16},{24,28},{28,24},{1,5},{5... | collective-permute-start | bytes 516104 | tf_op jit(solution)/shard_map/ppermute | solution.py:525
  16.7 7.3 %collective-permute-start.8 = (f32[7,3,8,256]{3,2,1,0:T(8,128)S(1)}, f32[7,3,8,256]{3,2,1,0:T(8,128)S(1)}, u32[]{:S(2)}, u32[]{:S(2)}) collective-permute-start(f32[7,3,8,256]{3,2,1,0:T(8,128)S(1)} %collective-permute-done.2.refs_4_), channel_id=1, source_target_pairs={{0,1},{1,0},{2,3},{3,2},{4,5},{5,4},{6,7},{7,6},{8,9},{9,8},{10,11... | collective-permute-start | bytes 516104 | tf_op jit(solution)/shard_map/ppermute | solution.py:525
  16.7 7.3 %collective-permute-start.9 = (f32[8,3,8,256]{3,2,1,0:T(8,128)S(1)}, f32[8,3,8,256]{3,2,1,0:T(8,128)S(1)}, u32[]{:S(2)}, u32[]{:S(2)}) collective-permute-start(f32[8,3,8,256]{3,2,1,0:T(8,128)S(1)} %collective-permute-done.1.refs_2_), channel_id=1, source_target_pairs={{0,8},{4,12},{8,0},{12,4},{16,24},{20,28},{24,16},{28,20},{1,9},{5... | collective-permute-start | bytes 589832 | tf_op jit(solution)/shard_map/ppermute | solution.py:525
  18.3 1.0 %copy-start.1 = (f32[2,136,256]{2,1,0:T(8,128)S(1)}, f32[2,136,256]{2,1,0:T(8,128)}, u32[]{:S(2)}) copy-start(f32[2,136,256]{2,1,0:T(8,128)} %get-tuple-element.56.refs_0_) | copy-start | bytes 835588
  19.2 5.3 %copy-start.3 = (f32[2,64,256]{2,1,0:T(8,128)S(1)}, f32[2,64,256]{2,1,0:T(8,128)}, u32[]{:S(2)}) copy-start(f32[2,64,256]{2,1,0:T(8,128)} %get-tuple-element.67.refs_4_) | copy-start | bytes 393220
  21.8 4.1 %collective-permute-start.4 = (f32[2,136,256]{2,1,0:T(8,128)S(1)}, f32[2,136,256]{2,1,0:T(8,128)S(1)}, u32[]{:S(2)}, u32[]{:S(2)}) collective-permute-start(f32[2,136,256]{2,1,0:T(8,128)S(1)} %collective-permute-done.3.refs_0_.refs_2_), channel_id=1, source_target_pairs={{0,1},{1,0},{2,3},{3,2},{4,5},{5,4},{6,7},{7,6},{8,9},{9,8},{10,11... | collective-permute-start | bytes 835592 | tf_op jit(solution)/shard_map/ppermute | solution.py:525
  21.8 2.7 %collective-permute-start.7 = (f32[8,3,8,256]{3,2,1,0:T(8,128)S(1)}, f32[8,3,8,256]{3,2,1,0:T(8,128)S(1)}, u32[]{:S(2)}, u32[]{:S(2)}) collective-permute-start(f32[8,3,8,256]{3,2,1,0:T(8,128)S(1)} %collective-permute-done.1.refs_2_), channel_id=1, source_target_pairs={{0,1},{1,0},{2,3},{3,2},{4,5},{5,4},{6,7},{7,6},{8,9},{9,8},{10,11... | collective-permute-start | bytes 589832 | tf_op jit(solution)/shard_map/ppermute | solution.py:525
  24.0 1.7 %collective-permute-start.10 = (f32[8,3,8,256]{3,2,1,0:T(8,128)S(1)}, f32[8,3,8,256]{3,2,1,0:T(8,128)S(1)}, u32[]{:S(2)}, u32[]{:S(2)}) collective-permute-start(f32[8,3,8,256]{3,2,1,0:T(8,128)S(1)} %collective-permute-done.9.refs_6_), channel_id=1, source_target_pairs={{0,1},{1,0},{2,3},{3,2},{4,5},{5,4},{6,7},{7,6},{8,9},{9,8},{10,11... | collective-permute-start | bytes 589832 | tf_op jit(solution)/shard_map/ppermute | solution.py:525
  24.0 1.7 %collective-permute-start.12 = (f32[7,3,8,256]{3,2,1,0:T(8,128)S(1)}, f32[7,3,8,256]{3,2,1,0:T(8,128)S(1)}, u32[]{:S(2)}, u32[]{:S(2)}) collective-permute-start(f32[7,3,8,256]{3,2,1,0:T(8,128)S(1)} %collective-permute-done.11.refs_8_), channel_id=1, source_target_pairs={{0,1},{1,0},{2,3},{3,2},{4,5},{5,4},{6,7},{7,6},{8,9},{9,8},{10,11... | collective-permute-start | bytes 516104 | tf_op jit(solution)/shard_map/ppermute | solution.py:525
  24.5 5.5 %collective-permute-start.5 = (f32[2,64,256]{2,1,0:T(8,128)S(1)}, f32[2,64,256]{2,1,0:T(8,128)S(1)}, u32[]{:S(2)}, u32[]{:S(2)}) collective-permute-start(f32[2,64,256]{2,1,0:T(8,128)S(1)} %copy-done.3), channel_id=1, source_target_pairs={{0,2},{1,3},{2,0},{3,1},{4,6},{5,7},{6,4},{7,5},{8,10},{9,11},{10,... | collective-permute-start | bytes 393224 | tf_op jit(solution)/shard_map/ppermute | solution.py:525
  30.0 5.7 %copy-start.2 = (f32[2,136,256]{2,1,0:T(8,128)S(1)}, f32[2,136,256]{2,1,0:T(8,128)}, u32[]{:S(2)}) copy-start(f32[2,136,256]{2,1,0:T(8,128)} %get-tuple-element.56.refs_0_) | copy-start | bytes 835588
  33.4 7.5 %collective-permute-start.13 = (f32[30,8,256]{2,1,0:T(8,128)S(1)}, f32[30,8,256]{2,1,0:T(8,128)S(1)}, u32[]{:S(2)}, u32[]{:S(2)}) collective-permute-start(f32[30,8,256]{2,1,0:T(8,128)S(1)} %get-tuple-element.77), channel_id=1, source_target_pairs={{0,4},{4,0},{8,12},{12,8},{16,20},{20,16},{24,28},{28,24},{1,5},{5... | collective-permute-start | bytes 737288 | tf_op jit(solution)/shard_map/ppermute | solution.py:525
  34.2 1.3 %collective-permute-start.14 = (f32[2,64,256]{2,1,0:T(8,128)S(1)}, f32[2,64,256]{2,1,0:T(8,128)S(1)}, u32[]{:S(2)}, u32[]{:S(2)}) collective-permute-start(f32[2,64,256]{2,1,0:T(8,128)S(1)} %copy-done.3), channel_id=1, source_target_pairs={{0,1},{1,0},{2,3},{3,2},{4,5},{5,4},{6,7},{7,6},{8,9},{9,8},{10,11... | collective-permute-start | bytes 393224 | tf_op jit(solution)/shard_map/ppermute | solution.py:525
  34.2 1.5 %collective-permute-start.15 = (f32[2,64,256]{2,1,0:T(8,128)S(1)}, f32[2,64,256]{2,1,0:T(8,128)S(1)}, u32[]{:S(2)}, u32[]{:S(2)}) collective-permute-start(f32[2,64,256]{2,1,0:T(8,128)S(1)} %collective-permute-done.5.refs_6_), channel_id=1, source_target_pairs={{0,1},{1,0},{2,3},{3,2},{4,5},{5,4},{6,7},{7,6},{8,9},{9,8},{10,11... | collective-permute-start | bytes 393224 | tf_op jit(solution)/shard_map/ppermute | solution.py:525
  37.0 3.9 %collective-permute-start.16 = (f32[2,8,256]{2,1,0:T(8,128)S(1)}, f32[2,8,256]{2,1,0:T(8,128)S(1)}, u32[]{:S(2)}, u32[]{:S(2)}) collective-permute-start(f32[2,8,256]{2,1,0:T(8,128)S(1)} %own_sums.1.refs_2_), channel_id=1, source_target_pairs={{0,4},{4,0},{8,12},{12,8},{16,20},{20,16},{24,28},{28,24},{1,5},{5... | collective-permute-start | bytes 49160 | tf_op jit(solution)/shard_map/ppermute | solution.py:525
  40.9 7.4 %collective-permute-start.19 = (f32[30,8,256]{2,1,0:T(8,128)S(1)}, f32[30,8,256]{2,1,0:T(8,128)S(1)}, u32[]{:S(2)}, u32[]{:S(2)}) collective-permute-start(f32[30,8,256]{2,1,0:T(8,128)S(1)} %get-tuple-element.87), channel_id=1, source_target_pairs={{0,4},{4,0},{8,12},{12,8},{16,20},{20,16},{24,28},{28,24},{1,5},{5... | collective-permute-start | bytes 737288 | tf_op jit(solution)/shard_map/ppermute | solution.py:525
  42.2 12.7 %collective-permute-start.17 = (f32[17,8,256]{2,1,0:T(8,128)S(1)}, f32[17,8,256]{2,1,0:T(8,128)S(1)}, u32[]{:S(2)}, u32[]{:S(2)}) collective-permute-start(f32[17,8,256]{2,1,0:T(8,128)S(1)} %get-tuple-element.84), channel_id=1, source_target_pairs={{0,16},{4,20},{8,24},{12,28},{16,0},{20,4},{24,8},{28,12},{1,17},{... | collective-permute-start | bytes 417800 | tf_op jit(solution)/shard_map/ppermute | solution.py:525
  44.9 10.0 %collective-permute-start.18 = (f32[17,8,256]{2,1,0:T(8,128)S(1)}, f32[17,8,256]{2,1,0:T(8,128)S(1)}, u32[]{:S(2)}, u32[]{:S(2)}) collective-permute-start(f32[17,8,256]{2,1,0:T(8,128)S(1)} %get-tuple-element.85), channel_id=1, source_target_pairs={{0,24},{4,28},{8,16},{12,20},{16,8},{20,12},{24,0},{28,4},{1,25},{... | collective-permute-start | bytes 417800 | tf_op jit(solution)/shard_map/ppermute | solution.py:525
  48.4 7.9 %collective-permute-start.20 = (f32[17,8,256]{2,1,0:T(8,128)S(1)}, f32[17,8,256]{2,1,0:T(8,128)S(1)}, u32[]{:S(2)}, u32[]{:S(2)}) collective-permute-start(f32[17,8,256]{2,1,0:T(8,128)S(1)} %get-tuple-element.89), channel_id=1, source_target_pairs={{0,8},{4,12},{8,0},{12,4},{16,24},{20,28},{24,16},{28,20},{1,9},{5... | collective-permute-start | bytes 417800 | tf_op jit(solution)/shard_map/ppermute | solution.py:525

commit v12 on v11

--- a/solution.py
+++ b/solution.py
@@ -239,34 +239,50 @@
     )(*pieces)
 
 
-def main_kernel(count, own, nx, nz, window, *refs):
-    sets = [refs[4 * n : 4 * n + 4] for n in range(count)]
-    orbit = refs[4 * count]
-    refs = refs[4 * count + 1 :]
-    outs = refs[: 2 * nx]
-    own_out = refs[2 * nx]
-    (acc, stream_a, stream_b, product_a, product_b, tropo_a, tropo_b,
-     spread_tropo) = refs[2 * nx + 1 :]
-    streams = (stream_a, stream_b)
+def main_kernel(raw, own, nx, nz, window, *refs):
+    ready = refs[:4]
+    raw_pieces = refs[4 : 4 + raw]
+    orbit = refs[4 + raw]
+    outs = refs[5 + raw : 5 + raw + 2 * nx]
+    own_out = refs[5 + raw + 2 * nx]
+    (acc, stream_a, stream_b, product_a, product_b, tropo_a, tropo_b, spread_tropo,
+     dense_a, dense_b, raw_planes, rows_int, raw_track, track_sem) = refs[
+         6 + raw + 2 * nx :]
+    streams, denses = (stream_a, stream_b), (dense_a, dense_b)
     products, tropos = (product_a, product_b), (tropo_a, tropo_b)
-    stations = sets[0][0].shape[0]
     tracked, _, width = product_a.shape
+    per = raw_pieces[0].shape[0]
+    epochs = orbit.shape[3]
     sats = orbit.shape[0]
     span = tracked * 8
     spare = width - own * 8
     packed = spare // KNOTS
-    me = lax.axis_index("sat")
+    first = lax.axis_index("sat") * own
     mine = lax.axis_index("sta")
-    first = me * own
-
+
+    for n, piece in enumerate(raw_pieces):
+        for p in range(per):
+            s = n * per + p
+            rows_int[s : s + 1, :] = piece[
+                p, 4 * tracked + 1 : 4 * tracked + 2, :128].astype(jnp.int32)
+    to_scalar = pltpu.make_async_copy(rows_int, raw_track, track_sem)
+    to_scalar.start()
+    for n, piece in enumerate(raw_pieces):
+        raw_planes[n * per : (n + 1) * per] = piece[...]
     acc[...] = jnp.zeros_like(acc)
     spread_tropo[...] = jnp.zeros_like(spread_tropo)
 
     lane = lax.broadcasted_iota(jnp.int32, (span, 128), 1) - (128 - spare)
 
-    def run(base, planes, track, highs, lows):
+    index = lax.broadcasted_iota(jnp.int32, (spare, epochs), 0)
+
+    def run(base, planes, track, halves):
+        stations = planes.shape[0]
+
         def build(s, turn):
-            stream = streams[turn]
+            stream, dense = streams[turn], denses[turn]
+            if halves is None:
+                dense[...] = jnp.zeros_like(dense)
             for pair in range(0, tracked, 2):
                 values, mixed = [], []
                 for m in (pair, pair + 1):
@@ -276,6 +292,10 @@
                         return planes[s, pl.ds(plane * tracked + m, 1), :]
 
                     value = row(0) * orbit[k, 0] + row(1) * orbit[k, 1] + row(2) * orbit[k, 2]
+                    if halves is None:
+                        local = k - first
+                        inside = jnp.logical_and(local >= 0, local < own)
+                        dense[jnp.where(inside, local, own)] = value
                     values.append(value)
                     mixed.append(value * row(3))
                 high, low = split(jnp.concatenate(values, 0))
@@ -288,7 +308,13 @@
         def multiply(s, turn):
             stream = streams[turn]
             place = lax.rem(base + s, packed) * KNOTS
-            high, low = highs[s], lows[s]
+            if halves is None:
+                knot = planes[s, 4 * tracked : 4 * tracked + 1, :].astype(jnp.int32)
+                select = (index - place == knot).astype(jnp.float32)
+                high, low = split(jnp.concatenate(
+                    [denses[turn][...].reshape((own + 1) * 8, epochs)[: own * 8], select], 0))
+            else:
+                high, low = halves[0][s], halves[1][s]
             result = dot_nt(stream[:span, :], high) + dot_nt(stream[span : 2 * span, :], high)
             result = result + dot_nt(stream[:span, :], low)
             products[turn][...] = result.reshape(tracked, 8, width)
@@ -326,8 +352,9 @@
         multiply(stations - 1, 1)
         scatter(stations - 1, 1)
 
-    for n in range(count):
-        run(n * stations, *sets[n])
+    run(0, ready[0], ready[1], ready[2:])
+    to_scalar.wait()
+    run(ready[0].shape[0], raw_planes, raw_track, None)
 
     outer = jnp.zeros((sats * 8, own * 8), jnp.float32)
     for slab in range(spread_tropo.shape[0]):
@@ -351,32 +378,37 @@
             outs[2 * dx + (dz < half)][at : at + window] = acc[pl.ds(start, window)]
 
 
-def accumulate(sets, orbit, own, nx, nz, window):
-    count = len(sets)
-    stations, rows, epochs = sets[0][0].shape
+def accumulate(ready, raw, orbit, own, nx, nz, window):
+    stations, rows, epochs = ready[0].shape
+    more = len(raw) * raw[0].shape[0]
     sats = orbit.shape[0]
     tracked = (rows - 8) // 4
-    width = sets[0][2].shape[1]
-    slabs = -(-count * stations // PACKED)
-    out = jax.ShapeDtypeStruct((nz // 2 * window, 8, width), jnp.float32)
+    width = ready[2].shape[1]
+    slabs = -(-(stations + more) // PACKED)
+    outs = [jax.ShapeDtypeStruct((nz // 2 * window, 8, width), jnp.float32)] * (2 * nx)
     return pl.pallas_call(
-        functools.partial(main_kernel, count, own, nx, nz, window),
-        out_shape=[out] * (2 * nx) + [jax.ShapeDtypeStruct((own, 8, width), jnp.float32)],
-        in_specs=[vmem(), pl.BlockSpec(memory_space=pltpu.SMEM), vmem(), vmem()] * count
-        + [vmem()],
-        out_specs=[vmem()] * (2 * nx + 1),
+        functools.partial(main_kernel, len(raw), own, nx, nz, window),
+        out_shape=outs + [jax.ShapeDtypeStruct((own, 8, width), jnp.float32)],
+        in_specs=[vmem(), pl.BlockSpec(memory_space=pltpu.SMEM), vmem(), vmem()]
+        + [vmem()] * (len(raw) + 1),
+        out_specs=[vmem()] * (len(outs) + 1),
         scratch_shapes=[
             pltpu.VMEM((sats, 8, width), jnp.float32),
             *[pltpu.VMEM((4 * tracked * 8, epochs), jnp.bfloat16)] * 2,
             *[pltpu.VMEM((tracked, 8, width), jnp.float32)] * 2,
             *[pltpu.VMEM((tracked, 8, 128), jnp.float32)] * 2,
             pltpu.VMEM((slabs, sats, 8, 128), jnp.float32),
+            *[pltpu.VMEM((own + 1, 8, epochs), jnp.float32)] * 2,
+            pltpu.VMEM((more, rows, epochs), jnp.float32),
+            pltpu.VMEM((more, 128), jnp.int32),
+            pltpu.SMEM((more, 128), jnp.int32),
+            pltpu.SemaphoreType.DMA,
         ],
         compiler_params=pltpu.CompilerParams(vmem_limit_bytes=MEDIUM_LIMIT),
         cost_estimate=pl.CostEstimate(
             flops=8 * 10**9, bytes_accessed=8 * 10**6, transcendentals=0),
         name="accumulate",
-    )(*[part for group in sets for part in group], orbit)
+    )(*ready, *raw, orbit)
 
 
 def blocks_kernel(groups, per, *refs):
@@ -451,49 +483,47 @@
     )(*planes, *extras, own_rows, orbit)
 
 
-def combine_kernel(pieces_count, smalls_count, window, *refs):
-    pieces, smalls = refs[:pieces_count], refs[pieces_count : pieces_count + smalls_count]
-    outs = refs[pieces_count + smalls_count :]
-    small = smalls[0][...]
-    for ref in smalls[1:]:
-        small = small + ref[...]
+def combine_kernel(pieces_count, *refs):
+    pieces, outs = refs[:pieces_count], refs[pieces_count:]
+    window = outs[0].shape[0]
     for n, out in enumerate(outs):
         part = pieces[0][n * window : (n + 1) * window]
         for piece in pieces[1:]:
             part = part + piece[n * window : (n + 1) * window]
-        out[:window] = part
-        out[window:] = small
-
-
-def combine(pieces, smalls, window):
+        out[...] = part
+
+
+def combine(pieces, window):
     count = pieces[0].shape[0] // window
-    width = pieces[0].shape[2]
     return pl.pallas_call(
-        functools.partial(combine_kernel, len(pieces), len(smalls), window),
-        out_shape=[jax.ShapeDtypeStruct((window + 2, 8, width), jnp.float32)] * count,
-        in_specs=[vmem()] * (len(pieces) + len(smalls)),
+        functools.partial(combine_kernel, len(pieces)),
+        out_shape=[jax.ShapeDtypeStruct((window,) + pieces[0].shape[1:], jnp.float32)] * count,
+        in_specs=[vmem()] * len(pieces),
         out_specs=[vmem()] * count,
         compiler_params=pltpu.CompilerParams(vmem_limit_bytes=SMALL_LIMIT),
         name="combine",
-    )(*pieces, *smalls)
+    )(*pieces)
 
 
 def finish_kernel(window, own, columns, sats, factor, cross_factor, *refs):
-    pieces = refs[:-3]
+    count = (len(refs) - 3) // 2
+    pieces, smalls = refs[:count], refs[count : 2 * count]
     normal, right, blocks = refs[-3:]
     width = pieces[0].shape[2]
     total = pieces[0][...]
-    for piece in pieces[1:]:
+    small_total = smalls[0][...]
+    for piece, small in zip(pieces[1:], smalls[1:]):
         total = total + piece[...]
+        small_total = small_total + small[...]
     first = lax.axis_index("sat") * own
     start = window_start(lax.axis_index("sta"), columns, sats, window)
-    part = total[:window].reshape(window * 8, width)
+    part = total.reshape(window * 8, width)
     row_owner = start + lax.broadcasted_iota(jnp.int32, part.shape, 0) // 8
     lane_owner = first + lax.broadcasted_iota(jnp.int32, part.shape, 1) // 8
     part = jnp.where(row_owner == lane_owner, 0.0, part * cross_factor)
     normal[...] = part.T[: own * 8, :]
-    right[...] = total[window + 1, :1, : own * 8] * factor
-    small = total[window]
+    right[...] = small_total[1, :1, : own * 8] * factor
+    small = small_total[0]
     room = -(-own // 32) * 32
     lane = lax.broadcasted_iota(jnp.int32, (width, 8 * room), 0)
     slot = lax.broadcasted_iota(jnp.int32, (width, 8 * room), 1)
@@ -506,7 +536,7 @@
         blocks[p] = factor * spread[:, p * room : p * room + own]
 
 
-def finish(pieces, window, own, columns, sats, factor, cross_factor):
+def finish(pieces, smalls, window, own, columns, sats, factor, cross_factor):
     return pl.pallas_call(
         functools.partial(finish_kernel, window, own, columns, sats, factor, cross_factor),
         out_shape=[
@@ -514,11 +544,11 @@
             jax.ShapeDtypeStruct((1, own * 8), jnp.float32),
             jax.ShapeDtypeStruct((8, 8, own), jnp.float32),
         ],
-        in_specs=[vmem()] * len(pieces),
+        in_specs=[vmem()] * (2 * len(pieces)),
         out_specs=[vmem()] * 3,
         compiler_params=pltpu.CompilerParams(vmem_limit_bytes=SMALL_LIMIT),
         name="finish",
-    )(*pieces)
+    )(*pieces, *smalls)
 
 
 def shift(value, axis, size, step):
@@ -555,48 +585,55 @@
     planes, extra = prepare(sight, mapping, residual, counts, track, knots)
     own_planes = planes
     other_planes, other_orbit, other_extra = core(planes), core(orbit), core(extra)
-    planes, near = lax.optimization_barrier((planes, near))
+    firsts = {d: values[0] for d, values in near.items()}
+    planes, firsts = lax.optimization_barrier((planes, firsts))
+    near = {d: [firsts[d]] + values[1:] for d, values in near.items()}
     arrived = {d: shift(planes, "sat", group, d) for d in near}
     far = {}
     if len(parts) == 2:
         far = {d: [across(near[d][0], nx), across(near[d][1], 1)] for d in near}
-    sets = [own_rows_of([own_planes, other_planes], planes.shape, orbit, width, 0)]
-    sets[0], arrived = lax.optimization_barrier((tuple(sets[0]), arrived))
+    ready = own_rows_of([own_planes, other_planes], planes.shape, orbit, width, 0)
+    ready, arrived, held_near, far = lax.optimization_barrier(
+        (tuple(ready), arrived, near, far))
     partials = [(0, 0, 0, orbit), (1, 0, 0, other_orbit)]
     for d in near:
-        for turn, values in ((0, near[d]), (1, far.get(d, []))):
+        for turn, values in ((0, held_near[d]), (1, far.get(d, []))):
             for start, value in zip((0, parts[0].shape[0]), values):
                 partials += [(d, turn, start, value), (d + 1, turn, start, core(value))]
     pieces = {0: own_planes, 1: other_planes}
     extras = {0: extra, 1: other_extra}
     for d, value in arrived.items():
         pieces[d], pieces[d + 1] = value, core(value)
-        sets.append(own_rows_of([pieces[d], pieces[d + 1]], planes.shape, orbit, width,
-                                d * stations))
         held, _ = lax.optimization_barrier((extra, value))
         extras[d] = shift(held, "sat", group, d)
-        sets[-1], extras[d] = lax.optimization_barrier((tuple(sets[-1]), extras[d]))
-        extras[d + 1] = core(extras[d])
     places = tuple((d, turn, start) for d, turn, start, _ in partials)
     every = place([part[3] for part in partials], places, sats, own, nx)
-    *sums, own_rows = accumulate(sets, every, own, nx, nz, window)
-
+    every, extras = lax.optimization_barrier((every, extras))
+    for d in near:
+        extras[d + 1] = core(extras[d])
+    *sums, own_rows = accumulate(
+        ready, [pieces[d] for d in range(2, group)], every, own, nx, nz, window)
+
+    half = nz // 2
     far_sums = [sums[0]] + [across(sums[2 * dx], dx) for dx in range(1, nx)]
     small = own_sums([pieces[d] for d in range(group)], [extras[d] for d in range(group)],
                      own_rows, orbit)
+    far_sums, small = lax.optimization_barrier((far_sums, small))
+    near_out, far_sums = lax.optimization_barrier((sums[1::2], far_sums))
+    chunks = list(combine(far_sums, window))
     smalls = [small] + [across(small, dx) for dx in range(1, nx)]
-    near_out, far_sums, smalls = lax.optimization_barrier((sums[1::2], far_sums, smalls))
-    near_sums = [near_out[0]] + [across(near_out[dx], dx) for dx in range(1, nx)]
-    far_chunks = combine(far_sums, smalls, window)
-    near_chunks = combine(near_sums, smalls, window)
-    half = nz // 2
-    final = [across(chunk, (half + n) * nx) for n, chunk in enumerate(far_chunks)]
-    final += [near_chunks[0]]
+    small = combine(smalls, 2)[0]
+    chunks[-1], small = lax.optimization_barrier((chunks[-1], small))
+    near_chunks = combine(
+        [near_out[0]] + [across(near_out[dx], dx) for dx in range(1, nx)], window)
+    final = [near_chunks[0]]
     final += [across(near_chunks[n], n * nx) for n in range(1, half)]
+    final += [across(chunk, (half + n) * nx) for n, chunk in enumerate(chunks)]
+    finals = [small] + [across(small, dz * nx) for dz in range(1, nz)]
     total_stations = stations * columns_axis * group
     factor = sats / (total_stations * tracked * epochs)
     cross_factor = sats / (total_stations * epochs) ** 0.5
-    normal, right, blocks = finish(final, window, own, columns, sats, factor, cross_factor)
+    normal, right, blocks = finish(final, finals, window, own, columns, sats, factor, cross_factor)
     if window * 8 != columns:
         mine = lax.axis_index("sta")
         start = window_start(mine, columns, sats, window)

time: 57.4 us -> 62.1 us (1.082)
  starting transfers between devices: 19.3 us -> 26 us
  waiting for transfers between devices: 23 us -> 21.9 us
  Pallas kernels: 12.1 us -> 11.1 us
    ppermute x21 -> x24, starting transfers between devices: 19.3 us -> 26 us  [shift(): return lax.ppermute(value, axis, [(i, i ^ step) for i in range(size)])]
    pallas_call x2 -> x1, Pallas kernels: 4.1 us -> 2.07 us  [own_rows_of(): pl.pallas_call(functools.partial(own_rows_kernel, groups, per, own, width...]
    ppermute x21 -> x24, waiting for transfers between devices: 23 us -> 21.9 us  [shift(): return lax.ppermute(value, axis, [(i, i ^ step) for i in range(size)])]
    pallas_call x3 -> x4, Pallas kernels: 3.5 us -> 4.55 us  [the longest x1 4.49 us: accumulate(): pl.pallas_call(functools.partial(main_kernel, len(raw), own, nx, nz, wind...]
  transfers between devices with their start and end apart: 21 -> 24, of which waited for: 11 -> 11; matrix products, arithmetic and copies ran while one was open for 0% -> 0% of each run, Pallas kernels for 13% -> 9%
where the time goes in v12:
time: 62.1 us; the launch traced here: 61.9 us
  starting transfers between devices  26 us (42%)
  waiting for transfers between devices  21.9 us (35%)
  Pallas kernels  11.1 us (18%)
  local copies, waits for them, and re-layouts  2.07 us (3%)
  between operations  0.75 us (1%)
    ppermute x24, starting transfers between devices, shift(): return lax.ppermute(value, axis, [(i, i ^ step) for i in range(size)])  26 us
    ppermute x24, waiting for transfers between devices, shift(): return lax.ppermute(value, axis, [(i, i ^ step) for i in range(size)])  21.9 us
    pallas_call x1, Pallas kernels, accumulate(): pl.pallas_call(functools.partial(main_kernel, len(raw), own, nx, nz, wind...  4.49 us
    unnamed x8, local copies, waits for them, and re-layouts  2.07 us
    pallas_call x1, Pallas kernels, own_rows_of(): pl.pallas_call(functools.partial(own_rows_kernel, groups, per, own, width...  2.07 us
    pallas_call x1, Pallas kernels, prepare(): pl.pallas_call(prepare_kernel, out_shape=[jax.ShapeDtypeStruct((stations,...  1.97 us
    pallas_call x1, Pallas kernels, own_sums(): pl.pallas_call(functools.partial(blocks_kernel, groups, per), out_shape=j...  1.32 us
  transfers between devices with their start and end apart: 24, of which 11 were waited for; matrix products, arithmetic and copies ran while one was open for 0% of the time, Pallas kernels for 9%

profile of v12, /device:TPU:0, one launch (start us, length us, event | category | flops | bytes accessed | tf_op | source)
XLA Modules:
  0.0 61.9 jit_solution(12998006945206151801)
XLA Ops:
  0.6 0.0 copy-start
  0.6 1.1 %copy-done = f32[30,3,8,256]{3,2,1,0:T(8,128)S(1)} copy-done((f32[30,3,8,256]{3,2,1,0:T(8,128)S(1)}, f32[30,3,8,256]{3,2,1,0:T(8,128)}, u32[]{:S(2)}) %copy-start) | copy-done | bytes 737304
  1.7 0.1 cut_parts.1
  1.8 3.0 %collective-permute-start.1 = (f32[8,3,8,256]{3,2,1,0:T(8,128)S(1)}, f32[8,3,8,256]{3,2,1,0:T(8,128)S(1)}, u32[]{:S(2)}, u32[]{:S(2)}) collective-permute-start(f32[8,3,8,256]{3,2,1,0:T(8,128)S(1)} %get-tuple-element.55), channel_id=1, source_target_pairs={{0,2},{1,3},{2,0},{3,1},{4,6},{5,7},{6,4},{7,5},{8,10},{9,11},{10,... | collective-permute-start | bytes 589832 | tf_op jit(solution)/shard_map/ppermute | solution.py:555
  4.9 2.0 %prepare.1 = (f32[2,136,256]{2,1,0:T(8,128)}, f32[2,64,256]{2,1,0:T(8,128)}) custom-call(f32[2,3,32,256]{3,2,1,0:T(8,128)} %refs_0_.1, f32[2,32,256]{2,1,0:T(8,128)} %refs_1_.1, f32[2,32,256]{2,1,0:T(8,128)} %refs_2_.1, s32[2,32,256]{2,1,0:T(8,128)} %refs_3_.1, s32[2,32]{1,0:T(2,128)} %refs_4_.1, s32[2,256]{1,0:T(2,128)} %refs_5_.1), custom_call_target="tpu_custom_call" | custom-call | tf_op jit(solution)/shard_map/prepare/pallas_call | solution.py:81
  6.8 0.1 collective-permute-start
  6.9 0.5 collective-permute-start.7
  7.4 0.0 collective-permute-start.3
  7.4 2.7 %collective-permute-done.1.refs_2_ = f32[8,3,8,256]{3,2,1,0:T(8,128)S(1)} collective-permute-done((f32[8,3,8,256]{3,2,1,0:T(8,128)S(1)}, f32[8,3,8,256]{3,2,1,0:T(8,128)S(1)}, u32[]{:S(2)}, u32[]{:S(2)}) %collective-permute-start.1) | collective-permute-done | bytes 196640 | tf_op jit(solution)/shard_map/ppermute | solution.py:555
  10.1 2.5 %collective-permute-start.2 = (f32[2,136,256]{2,1,0:T(8,128)}, f32[2,136,256]{2,1,0:T(8,128)S(1)}, u32[]{:S(2)}, u32[]{:S(2)}) collective-permute-start(f32[2,136,256]{2,1,0:T(8,128)} %get-tuple-element.56.refs_0_), channel_id=1, source_target_pairs={{0,2},{1,3},{2,0},{3,1},{4,6},{5,7},{6,4},{7,5},{8,10},{9,11},{10,... | collective-permute-start | bytes 835592 | tf_op jit(solution)/shard_map/ppermute | solution.py:555
  12.6 1.4 %collective-permute-start.4 = (f32[8,3,8,256]{3,2,1,0:T(8,128)S(1)}, f32[8,3,8,256]{3,2,1,0:T(8,128)S(1)}, u32[]{:S(2)}, u32[]{:S(2)}) collective-permute-start(f32[8,3,8,256]{3,2,1,0:T(8,128)S(1)} %collective-permute-done.1.refs_2_), channel_id=1, source_target_pairs={{0,8},{4,12},{8,0},{12,4},{16,24},{20,28},{24,16},{28,20},{1,9},{5... | collective-permute-start | bytes 589832 | tf_op jit(solution)/shard_map/ppermute | solution.py:555
  13.9 0.7 %collective-permute-done.3.refs_4_ = f32[7,3,8,256]{3,2,1,0:T(8,128)S(1)} collective-permute-done((f32[7,3,8,256]{3,2,1,0:T(8,128)S(1)}, f32[7,3,8,256]{3,2,1,0:T(8,128)S(1)}, u32[]{:S(2)}, u32[]{:S(2)}) %collective-permute-start.3) | collective-permute-done | bytes 172064 | tf_op jit(solution)/shard_map/ppermute | solution.py:555
  14.6 1.5 %collective-permute-start.5 = (f32[7,3,8,256]{3,2,1,0:T(8,128)S(1)}, f32[7,3,8,256]{3,2,1,0:T(8,128)S(1)}, u32[]{:S(2)}, u32[]{:S(2)}) collective-permute-start(f32[7,3,8,256]{3,2,1,0:T(8,128)S(1)} %collective-permute-done.3.refs_4_), channel_id=1, source_target_pairs={{0,4},{4,0},{8,12},{12,8},{16,20},{20,16},{24,28},{28,24},{1,5},{5... | collective-permute-start | bytes 516104 | tf_op jit(solution)/shard_map/ppermute | solution.py:555
  16.1 0.0 collective-permute-done.refs_1_
  16.1 0.0 copy-start.1
  16.1 1.0 %copy-done.1 = f32[2,136,256]{2,1,0:T(8,128)S(1)} copy-done((f32[2,136,256]{2,1,0:T(8,128)S(1)}, f32[2,136,256]{2,1,0:T(8,128)}, u32[]{:S(2)}) %copy-start.1) | copy-done | bytes 278552
  17.1 0.0 copy-start.3
  17.1 2.1 %own_rows.1 = (f32[4,136,256]{2,1,0:T(8,128)S(1)}, s32[4,128]{1,0:T(4,128)S(1)}, bf16[4,256,256]{2,1,0:T(8,128)(2,1)S(1)}, bf16[4,256,256]{2,1,0:T(8,128)(2,1)S(1)}) custom-call(f32[2,136,256]{2,1,0:T(8,128)S(1)} %copy-done.1, f32[2,136,256]{2,1,0:T(8,128)S(1)} %collective-permute-done.refs_1_, f32[30,3,8,256]{3,2,1,0:T(8,128)S(1)} %get-tuple-element.50.refs_2_.refs_0_.refs_9_), custom_call_target="tpu_custom_call" | custom-call | flops 2000000000 | bytes 2000000 | tf_op jit(solution)/shard_map/own_rows/pallas_call | solution.py:198
  19.2 0.9 %collective-permute-done.5.refs_8_ = f32[7,3,8,256]{3,2,1,0:T(8,128)S(1)} collective-permute-done((f32[7,3,8,256]{3,2,1,0:T(8,128)S(1)}, f32[7,3,8,256]{3,2,1,0:T(8,128)S(1)}, u32[]{:S(2)}, u32[]{:S(2)}) %collective-permute-start.5) | collective-permute-done | bytes 172064 | tf_op jit(solution)/shard_map/ppermute | solution.py:555
  20.0 0.0 collective-permute-done.4.refs_6_
  20.0 0.0 collective-permute-done.2.refs_4_.refs_2_
  20.1 0.0 collective-permute-start.11
  20.1 0.5 collective-permute-start.10
  20.6 0.1 collective-permute-start.9
  20.6 0.4 collective-permute-start.6
  21.1 0.4 collective-permute-done.11.refs_9_
  21.5 0.1 collective-permute-start.8
  21.6 0.4 collective-permute-done.9.refs_5_
  22.0 0.0 copy-done.3
  22.0 0.3 collective-permute-start.12
  22.3 0.0 collective-permute-done.10.refs_7_
  22.3 1.6 %collective-permute-start.13 = (f32[2,64,256]{2,1,0:T(8,128)S(1)}, f32[2,64,256]{2,1,0:T(8,128)S(1)}, u32[]{:S(2)}, u32[]{:S(2)}) collective-permute-start(f32[2,64,256]{2,1,0:T(8,128)S(1)} %copy-done.3), channel_id=1, source_target_pairs={{0,2},{1,3},{2,0},{3,1},{4,6},{5,7},{6,4},{7,5},{8,10},{9,11},{10,... | collective-permute-start | bytes 393224 | tf_op jit(solution)/shard_map/ppermute | solution.py:555
  23.9 0.0 collective-permute-done.8.refs_3_
  23.9 0.0 collective-permute-done.7.refs_1_
  23.9 0.2 place.1.refs_6_
  24.1 0.0 copy-start.2
  24.1 0.0 collective-permute-done.12.refs_5_
  24.1 3.8 %collective-permute-done.13.refs_6_ = f32[2,64,256]{2,1,0:T(8,128)S(1)} collective-permute-done((f32[2,64,256]{2,1,0:T(8,128)S(1)}, f32[2,64,256]{2,1,0:T(8,128)S(1)}, u32[]{:S(2)}, u32[]{:S(2)}) %collective-permute-start.13) | collective-permute-done | bytes 131104 | tf_op jit(solution)/shard_map/ppermute | solution.py:555
  27.9 0.0 collective-permute-done.6.refs_5_.refs_3_
  27.9 4.5 %accumulate.1 = (f32[30,8,256]{2,1,0:T(8,128)S(1)}, f32[30,8,256]{2,1,0:T(8,128)S(1)}, f32[30,8,256]{2,1,0:T(8,128)S(1)}, f32[30,8,256]{2,1,0:T(8,128)S(1)}, f32[30,8,256]{2,1,0:T(8,128)S(1)}) custom-call(f32[4,136,256]{2,1,0:T(8,128)S(1)} %get-tuple-element.59.refs_0_, s32[4,128]{1,0:T(4,128)S(1)} %get-tuple-element.60.refs_1_, ...), custom_call_target="tpu_custom_call" | custom-call | flops 8000000000 | bytes 8000000 | tf_op jit(solution)/shard_map/accumulate/pallas_call | solution.py:389
  32.4 1.5 %collective-permute-start.14 = (f32[30,8,256]{2,1,0:T(8,128)S(1)}, f32[30,8,256]{2,1,0:T(8,128)S(1)}, u32[]{:S(2)}, u32[]{:S(2)}) collective-permute-start(f32[30,8,256]{2,1,0:T(8,128)S(1)} %get-tuple-element.74), channel_id=1, source_target_pairs={{0,4},{4,0},{8,12},{12,8},{16,20},{20,16},{24,28},{28,24},{1,5},{5... | collective-permute-start | bytes 737288 | tf_op jit(solution)/shard_map/ppermute | solution.py:555
  34.0 0.0 collective-permute-start.15
  34.0 1.3 %collective-permute-done.15.refs_7_ = f32[2,64,256]{2,1,0:T(8,128)S(1)} collective-permute-done((f32[2,64,256]{2,1,0:T(8,128)S(1)}, f32[2,64,256]{2,1,0:T(8,128)S(1)}, u32[]{:S(2)}, u32[]{:S(2)}) %collective-permute-start.15) | collective-permute-done | bytes 131104 | tf_op jit(solution)/shard_map/ppermute | solution.py:555
  35.3 0.0 copy-done.2
  35.3 1.3 %own_sums.1.refs_0_ = f32[2,8,256]{2,1,0:T(8,128)S(1)} custom-call(f32[2,136,256]{2,1,0:T(8,128)S(1)} %copy-done.2, f32[2,136,256]{2,1,0:T(8,128)S(1)} %collective-permute-done.refs_1_, f32[2,136,256]{2,1,0:T(8,128)S(1)} %collective-permute-done.2.refs_4_.refs_2_, f32[2,136,256]{2,1,0:T(8,128)S(1)} %collective-permute-done.6.refs_5_.refs_3_, ...), custom_call_target="tpu_custom_call" | custom-call | flops 100000000 | bytes 100000 | tf_op jit(solution)/shard_map/own_sums/pallas_call | solution.py:474
  36.6 3.1 %collective-permute-done.14.refs_1_ = f32[30,8,256]{2,1,0:T(8,128)S(1)} collective-permute-done((f32[30,8,256]{2,1,0:T(8,128)S(1)}, f32[30,8,256]{2,1,0:T(8,128)S(1)}, u32[]{:S(2)}, u32[]{:S(2)}) %collective-permute-start.14) | collective-permute-done | bytes 245792 | tf_op jit(solution)/shard_map/ppermute | solution.py:555
  39.8 1.5 %collective-permute-start.16 = (f32[30,8,256]{2,1,0:T(8,128)S(1)}, f32[30,8,256]{2,1,0:T(8,128)S(1)}, u32[]{:S(2)}, u32[]{:S(2)}) collective-permute-start(f32[30,8,256]{2,1,0:T(8,128)S(1)} %get-tuple-element.82), channel_id=1, source_target_pairs={{0,4},{4,0},{8,12},{12,8},{16,20},{20,16},{24,28},{28,24},{1,5},{5... | collective-permute-start | bytes 737288 | tf_op jit(solution)/shard_map/ppermute | solution.py:555
  41.3 0.5 collective-permute-start.19
  41.8 2.6 %collective-permute-start.18 = (f32[15,8,256]{2,1,0:T(8,128)S(1)}, f32[15,8,256]{2,1,0:T(8,128)S(1)}, u32[]{:S(2)}, u32[]{:S(2)}) collective-permute-start(f32[15,8,256]{2,1,0:T(8,128)S(1)} %get-tuple-element.87), channel_id=1, source_target_pairs={{0,16},{4,20},{8,24},{12,28},{16,0},{20,4},{24,8},{28,12},{1,17},{... | collective-permute-start | bytes 368648 | tf_op jit(solution)/shard_map/ppermute | solution.py:555
  44.5 2.0 %collective-permute-done.19.refs_1_ = f32[2,8,256]{2,1,0:T(8,128)S(1)} collective-permute-done((f32[2,8,256]{2,1,0:T(8,128)S(1)}, f32[2,8,256]{2,1,0:T(8,128)S(1)}, u32[]{:S(2)}, u32[]{:S(2)}) %collective-permute-start.19) | collective-permute-done | bytes 16416 | tf_op jit(solution)/shard_map/ppermute | solution.py:555
  46.5 3.6 %collective-permute-start.20 = (f32[15,8,256]{2,1,0:T(8,128)S(1)}, f32[15,8,256]{2,1,0:T(8,128)S(1)}, u32[]{:S(2)}, u32[]{:S(2)}) collective-permute-start(f32[15,8,256]{2,1,0:T(8,128)S(1)} %get-tuple-element.90), channel_id=1, source_target_pairs={{0,24},{4,28},{8,16},{12,20},{16,8},{20,12},{24,0},{28,4},{1,25},{... | collective-permute-start | bytes 368648 | tf_op jit(solution)/shard_map/ppermute | solution.py:555
  50.1 0.0 collective-permute-done.16.refs_1_
  50.1 0.1 collective-permute-start.17
  50.2 2.0 %collective-permute-start.21 = (f32[2,8,256]{2,1,0:T(8,128)S(1)}, f32[2,8,256]{2,1,0:T(8,128)S(1)}, u32[]{:S(2)}, u32[]{:S(2)}) collective-permute-start(f32[2,8,256]{2,1,0:T(8,128)S(1)} %combine.5.refs_4_), channel_id=1, source_target_pairs={{0,8},{4,12},{8,0},{12,4},{16,24},{20,28},{24,16},{28,20},{1,9},{5... | collective-permute-start | bytes 49160 | tf_op jit(solution)/shard_map/ppermute | solution.py:555
  52.2 0.0 collective-permute-start.22
  52.2 3.1 %collective-permute-done.21.refs_5_ = f32[2,8,256]{2,1,0:T(8,128)S(1)} collective-permute-done((f32[2,8,256]{2,1,0:T(8,128)S(1)}, f32[2,8,256]{2,1,0:T(8,128)S(1)}, u32[]{:S(2)}, u32[]{:S(2)}) %collective-permute-start.21) | collective-permute-done | bytes 16416 | tf_op jit(solution)/shard_map/ppermute | solution.py:555
  55.4 2.2 %collective-permute-start.23 = (f32[2,8,256]{2,1,0:T(8,128)S(1)}, f32[2,8,256]{2,1,0:T(8,128)S(1)}, u32[]{:S(2)}, u32[]{:S(2)}) collective-permute-start(f32[2,8,256]{2,1,0:T(8,128)S(1)} %combine.5.refs_4_), channel_id=1, source_target_pairs={{0,24},{4,28},{8,16},{12,20},{16,8},{20,12},{24,0},{28,4},{1,25},{... | collective-permute-start | bytes 49160 | tf_op jit(solution)/shard_map/ppermute | solution.py:555
  57.5 0.0 collective-permute-done.22.refs_6_
  57.5 3.4 %collective-permute-done.23.refs_7_ = f32[2,8,256]{2,1,0:T(8,128)S(1)} collective-permute-done((f32[2,8,256]{2,1,0:T(8,128)S(1)}, f32[2,8,256]{2,1,0:T(8,128)S(1)}, u32[]{:S(2)}, u32[]{:S(2)}) %collective-permute-start.23) | collective-permute-done | bytes 16416 | tf_op jit(solution)/shard_map/ppermute | solution.py:555
  60.9 0.0 collective-permute-done.18.refs_2_
  60.9 0.0 collective-permute-done.20.refs_3_
  60.9 0.0 collective-permute-done.17.refs_1_
  60.9 1.0 %finish.1 = (f32[240,120]{1,0:T(8,128)}, f32[1,240]{1,0:T(1,128)}, f32[8,8,30]{2,1,0:T(8,128)}) custom-call(f32[15,8,256]{2,1,0:T(8,128)S(1)} %get-tuple-element.83.refs_0_, f32[15,8,256]{2,1,0:T(8,128)S(1)} %collective-permute-done.17.refs_1_, f32[15,8,256]{2,1,0:T(8,128)S(1)} %collective-permute-done.18.refs_2_, ...), custom_call_target="tpu_custom_call" | custom-call | tf_op jit(solution)/shard_map/finish/pallas_call | solution.py:540
  (3 shorter events, 0.1 us)
Async XLA Ops:
  0.6 1.1 %copy-start = (f32[30,3,8,256]{3,2,1,0:T(8,128)S(1)}, f32[30,3,8,256]{3,2,1,0:T(8,128)}, u32[]{:S(2)}) copy-start(f32[30,3,8,256]{3,2,1,0:T(8,128)} %orbit.1) | copy-start | bytes 2211844
  1.8 8.3 %collective-permute-start.1 = (f32[8,3,8,256]{3,2,1,0:T(8,128)S(1)}, f32[8,3,8,256]{3,2,1,0:T(8,128)S(1)}, u32[]{:S(2)}, u32[]{:S(2)}) collective-permute-start(f32[8,3,8,256]{3,2,1,0:T(8,128)S(1)} %get-tuple-element.55), channel_id=1, source_target_pairs={{0,2},{1,3},{2,0},{3,1},{4,6},{5,7},{6,4},{7,5},{8,10},{9,11},{10,... | collective-permute-start | bytes 589832 | tf_op jit(solution)/shard_map/ppermute | solution.py:555
  6.8 9.3 %collective-permute-start = (f32[2,136,256]{2,1,0:T(8,128)}, f32[2,136,256]{2,1,0:T(8,128)S(1)}, u32[]{:S(2)}, u32[]{:S(2)}) collective-permute-start(f32[2,136,256]{2,1,0:T(8,128)} %get-tuple-element.56.refs_0_), channel_id=1, source_target_pairs={{0,1},{1,0},{2,3},{3,2},{4,5},{5,4},{6,7},{7,6},{8,9},{9,8},{10,11... | collective-permute-start | bytes 835592 | tf_op jit(solution)/shard_map/ppermute | solution.py:555
  6.9 17.0 %collective-permute-start.7 = (f32[30,3,8,256]{3,2,1,0:T(8,128)S(1)}, f32[30,3,8,256]{3,2,1,0:T(8,128)S(1)}, u32[]{:S(2)}, u32[]{:S(2)}) collective-permute-start(f32[30,3,8,256]{3,2,1,0:T(8,128)S(1)} %get-tuple-element.50.refs_2_.refs_0_.refs_9_), channel_id=1, source_target_pairs={{0,1},{1,0},{2,3},{3,2},{4,5},{5,4},{6,7},{7,6},{8,9},{9,8},{10,11... | collective-permute-start | bytes 2211848 | tf_op jit(solution)/shard_map/ppermute | solution.py:555
  7.4 7.2 %collective-permute-start.3 = (f32[7,3,8,256]{3,2,1,0:T(8,128)S(1)}, f32[7,3,8,256]{3,2,1,0:T(8,128)S(1)}, u32[]{:S(2)}, u32[]{:S(2)}) collective-permute-start(f32[7,3,8,256]{3,2,1,0:T(8,128)S(1)} %get-tuple-element.58), channel_id=1, source_target_pairs={{0,2},{1,3},{2,0},{3,1},{4,6},{5,7},{6,4},{7,5},{8,10},{9,11},{10,... | collective-permute-start | bytes 516104 | tf_op jit(solution)/shard_map/ppermute | solution.py:555
  10.1 10.0 %collective-permute-start.2 = (f32[2,136,256]{2,1,0:T(8,128)}, f32[2,136,256]{2,1,0:T(8,128)S(1)}, u32[]{:S(2)}, u32[]{:S(2)}) collective-permute-start(f32[2,136,256]{2,1,0:T(8,128)} %get-tuple-element.56.refs_0_), channel_id=1, source_target_pairs={{0,2},{1,3},{2,0},{3,1},{4,6},{5,7},{6,4},{7,5},{8,10},{9,11},{10,... | collective-permute-start | bytes 835592 | tf_op jit(solution)/shard_map/ppermute | solution.py:555
  12.6 7.5 %collective-permute-start.4 = (f32[8,3,8,256]{3,2,1,0:T(8,128)S(1)}, f32[8,3,8,256]{3,2,1,0:T(8,128)S(1)}, u32[]{:S(2)}, u32[]{:S(2)}) collective-permute-start(f32[8,3,8,256]{3,2,1,0:T(8,128)S(1)} %collective-permute-done.1.refs_2_), channel_id=1, source_target_pairs={{0,8},{4,12},{8,0},{12,4},{16,24},{20,28},{24,16},{28,20},{1,9},{5... | collective-permute-start | bytes 589832 | tf_op jit(solution)/shard_map/ppermute | solution.py:555
  14.6 5.4 %collective-permute-start.5 = (f32[7,3,8,256]{3,2,1,0:T(8,128)S(1)}, f32[7,3,8,256]{3,2,1,0:T(8,128)S(1)}, u32[]{:S(2)}, u32[]{:S(2)}) collective-permute-start(f32[7,3,8,256]{3,2,1,0:T(8,128)S(1)} %collective-permute-done.3.refs_4_), channel_id=1, source_target_pairs={{0,4},{4,0},{8,12},{12,8},{16,20},{20,16},{24,28},{28,24},{1,5},{5... | collective-permute-start | bytes 516104 | tf_op jit(solution)/shard_map/ppermute | solution.py:555
  16.1 1.0 %copy-start.1 = (f32[2,136,256]{2,1,0:T(8,128)S(1)}, f32[2,136,256]{2,1,0:T(8,128)}, u32[]{:S(2)}) copy-start(f32[2,136,256]{2,1,0:T(8,128)} %get-tuple-element.56.refs_0_) | copy-start | bytes 835588
  17.1 4.9 %copy-start.3 = (f32[2,64,256]{2,1,0:T(8,128)S(1)}, f32[2,64,256]{2,1,0:T(8,128)}, u32[]{:S(2)}) copy-start(f32[2,64,256]{2,1,0:T(8,128)} %get-tuple-element.75.refs_4_) | copy-start | bytes 393220
  20.1 1.4 %collective-permute-start.11 = (f32[7,3,8,256]{3,2,1,0:T(8,128)S(1)}, f32[7,3,8,256]{3,2,1,0:T(8,128)S(1)}, u32[]{:S(2)}, u32[]{:S(2)}) collective-permute-start(f32[7,3,8,256]{3,2,1,0:T(8,128)S(1)} %collective-permute-done.5.refs_8_), channel_id=1, source_target_pairs={{0,1},{1,0},{2,3},{3,2},{4,5},{5,4},{6,7},{7,6},{8,9},{9,8},{10,11... | collective-permute-start | bytes 516104 | tf_op jit(solution)/shard_map/ppermute | solution.py:555
  20.1 2.2 %collective-permute-start.10 = (f32[8,3,8,256]{3,2,1,0:T(8,128)S(1)}, f32[8,3,8,256]{3,2,1,0:T(8,128)S(1)}, u32[]{:S(2)}, u32[]{:S(2)}) collective-permute-start(f32[8,3,8,256]{3,2,1,0:T(8,128)S(1)} %collective-permute-done.4.refs_6_), channel_id=1, source_target_pairs={{0,1},{1,0},{2,3},{3,2},{4,5},{5,4},{6,7},{7,6},{8,9},{9,8},{10,11... | collective-permute-start | bytes 589832 | tf_op jit(solution)/shard_map/ppermute | solution.py:555
  20.6 1.4 %collective-permute-start.9 = (f32[7,3,8,256]{3,2,1,0:T(8,128)S(1)}, f32[7,3,8,256]{3,2,1,0:T(8,128)S(1)}, u32[]{:S(2)}, u32[]{:S(2)}) collective-permute-start(f32[7,3,8,256]{3,2,1,0:T(8,128)S(1)} %collective-permute-done.3.refs_4_), channel_id=1, source_target_pairs={{0,1},{1,0},{2,3},{3,2},{4,5},{5,4},{6,7},{7,6},{8,9},{9,8},{10,11... | collective-permute-start | bytes 516104 | tf_op jit(solution)/shard_map/ppermute | solution.py:555
  20.6 7.3 %collective-permute-start.6 = (f32[2,136,256]{2,1,0:T(8,128)S(1)}, f32[2,136,256]{2,1,0:T(8,128)S(1)}, u32[]{:S(2)}, u32[]{:S(2)}) collective-permute-start(f32[2,136,256]{2,1,0:T(8,128)S(1)} %collective-permute-done.2.refs_4_.refs_2_), channel_id=1, source_target_pairs={{0,1},{1,0},{2,3},{3,2},{4,5},{5,4},{6,7},{7,6},{8,9},{9,8},{10,11... | collective-permute-start | bytes 835592 | tf_op jit(solution)/shard_map/ppermute | solution.py:555
  21.5 2.4 %collective-permute-start.8 = (f32[8,3,8,256]{3,2,1,0:T(8,128)S(1)}, f32[8,3,8,256]{3,2,1,0:T(8,128)S(1)}, u32[]{:S(2)}, u32[]{:S(2)}) collective-permute-start(f32[8,3,8,256]{3,2,1,0:T(8,128)S(1)} %collective-permute-done.1.refs_2_), channel_id=1, source_target_pairs={{0,1},{1,0},{2,3},{3,2},{4,5},{5,4},{6,7},{7,6},{8,9},{9,8},{10,11... | collective-permute-start | bytes 589832 | tf_op jit(solution)/shard_map/ppermute | solution.py:555
  22.0 2.1 %collective-permute-start.12 = (f32[2,64,256]{2,1,0:T(8,128)S(1)}, f32[2,64,256]{2,1,0:T(8,128)S(1)}, u32[]{:S(2)}, u32[]{:S(2)}) collective-permute-start(f32[2,64,256]{2,1,0:T(8,128)S(1)} %copy-done.3), channel_id=1, source_target_pairs={{0,1},{1,0},{2,3},{3,2},{4,5},{5,4},{6,7},{7,6},{8,9},{9,8},{10,11... | collective-permute-start | bytes 393224 | tf_op jit(solution)/shard_map/ppermute | solution.py:555
  22.3 5.6 %collective-permute-start.13 = (f32[2,64,256]{2,1,0:T(8,128)S(1)}, f32[2,64,256]{2,1,0:T(8,128)S(1)}, u32[]{:S(2)}, u32[]{:S(2)}) collective-permute-start(f32[2,64,256]{2,1,0:T(8,128)S(1)} %copy-done.3), channel_id=1, source_target_pairs={{0,2},{1,3},{2,0},{3,1},{4,6},{5,7},{6,4},{7,5},{8,10},{9,11},{10,... | collective-permute-start | bytes 393224 | tf_op jit(solution)/shard_map/ppermute | solution.py:555
  24.1 11.2 %copy-start.2 = (f32[2,136,256]{2,1,0:T(8,128)S(1)}, f32[2,136,256]{2,1,0:T(8,128)}, u32[]{:S(2)}) copy-start(f32[2,136,256]{2,1,0:T(8,128)} %get-tuple-element.56.refs_0_) | copy-start | bytes 835588
  32.4 7.4 %collective-permute-start.14 = (f32[30,8,256]{2,1,0:T(8,128)S(1)}, f32[30,8,256]{2,1,0:T(8,128)S(1)}, u32[]{:S(2)}, u32[]{:S(2)}) collective-permute-start(f32[30,8,256]{2,1,0:T(8,128)S(1)} %get-tuple-element.74), channel_id=1, source_target_pairs={{0,4},{4,0},{8,12},{12,8},{16,20},{20,16},{24,28},{28,24},{1,5},{5... | collective-permute-start | bytes 737288 | tf_op jit(solution)/shard_map/ppermute | solution.py:555
  34.0 1.3 %collective-permute-start.15 = (f32[2,64,256]{2,1,0:T(8,128)S(1)}, f32[2,64,256]{2,1,0:T(8,128)S(1)}, u32[]{:S(2)}, u32[]{:S(2)}) collective-permute-start(f32[2,64,256]{2,1,0:T(8,128)S(1)} %collective-permute-done.13.refs_6_), channel_id=1, source_target_pairs={{0,1},{1,0},{2,3},{3,2},{4,5},{5,4},{6,7},{7,6},{8,9},{9,8},{10,11... | collective-permute-start | bytes 393224 | tf_op jit(solution)/shard_map/ppermute | solution.py:555
  39.8 10.3 %collective-permute-start.16 = (f32[30,8,256]{2,1,0:T(8,128)S(1)}, f32[30,8,256]{2,1,0:T(8,128)S(1)}, u32[]{:S(2)}, u32[]{:S(2)}) collective-permute-start(f32[30,8,256]{2,1,0:T(8,128)S(1)} %get-tuple-element.82), channel_id=1, source_target_pairs={{0,4},{4,0},{8,12},{12,8},{16,20},{20,16},{24,28},{28,24},{1,5},{5... | collective-permute-start | bytes 737288 | tf_op jit(solution)/shard_map/ppermute | solution.py:555
  41.3 5.2 %collective-permute-start.19 = (f32[2,8,256]{2,1,0:T(8,128)S(1)}, f32[2,8,256]{2,1,0:T(8,128)S(1)}, u32[]{:S(2)}, u32[]{:S(2)}) collective-permute-start(f32[2,8,256]{2,1,0:T(8,128)S(1)} %own_sums.1.refs_0_), channel_id=1, source_target_pairs={{0,4},{4,0},{8,12},{12,8},{16,20},{20,16},{24,28},{28,24},{1,5},{5... | collective-permute-start | bytes 49160 | tf_op jit(solution)/shard_map/ppermute | solution.py:555
  41.8 19.1 %collective-permute-start.18 = (f32[15,8,256]{2,1,0:T(8,128)S(1)}, f32[15,8,256]{2,1,0:T(8,128)S(1)}, u32[]{:S(2)}, u32[]{:S(2)}) collective-permute-start(f32[15,8,256]{2,1,0:T(8,128)S(1)} %get-tuple-element.87), channel_id=1, source_target_pairs={{0,16},{4,20},{8,24},{12,28},{16,0},{20,4},{24,8},{28,12},{1,17},{... | collective-permute-start | bytes 368648 | tf_op jit(solution)/shard_map/ppermute | solution.py:555
  46.5 14.4 %collective-permute-start.20 = (f32[15,8,256]{2,1,0:T(8,128)S(1)}, f32[15,8,256]{2,1,0:T(8,128)S(1)}, u32[]{:S(2)}, u32[]{:S(2)}) collective-permute-start(f32[15,8,256]{2,1,0:T(8,128)S(1)} %get-tuple-element.90), channel_id=1, source_target_pairs={{0,24},{4,28},{8,16},{12,20},{16,8},{20,12},{24,0},{28,4},{1,25},{... | collective-permute-start | bytes 368648 | tf_op jit(solution)/shard_map/ppermute | solution.py:555
  50.1 10.8 %collective-permute-start.17 = (f32[15,8,256]{2,1,0:T(8,128)S(1)}, f32[15,8,256]{2,1,0:T(8,128)S(1)}, u32[]{:S(2)}, u32[]{:S(2)}) collective-permute-start(f32[15,8,256]{2,1,0:T(8,128)S(1)} %get-tuple-element.84), channel_id=1, source_target_pairs={{0,8},{4,12},{8,0},{12,4},{16,24},{20,28},{24,16},{28,20},{1,9},{5... | collective-permute-start | bytes 368648 | tf_op jit(solution)/shard_map/ppermute | solution.py:555
  50.2 5.2 %collective-permute-start.21 = (f32[2,8,256]{2,1,0:T(8,128)S(1)}, f32[2,8,256]{2,1,0:T(8,128)S(1)}, u32[]{:S(2)}, u32[]{:S(2)}) collective-permute-start(f32[2,8,256]{2,1,0:T(8,128)S(1)} %combine.5.refs_4_), channel_id=1, source_target_pairs={{0,8},{4,12},{8,0},{12,4},{16,24},{20,28},{24,16},{28,20},{1,9},{5... | collective-permute-start | bytes 49160 | tf_op jit(solution)/shard_map/ppermute | solution.py:555
  52.2 5.3 %collective-permute-start.22 = (f32[2,8,256]{2,1,0:T(8,128)S(1)}, f32[2,8,256]{2,1,0:T(8,128)S(1)}, u32[]{:S(2)}, u32[]{:S(2)}) collective-permute-start(f32[2,8,256]{2,1,0:T(8,128)S(1)} %combine.5.refs_4_), channel_id=1, source_target_pairs={{0,16},{4,20},{8,24},{12,28},{16,0},{20,4},{24,8},{28,12},{1,17},{... | collective-permute-start | bytes 49160 | tf_op jit(solution)/shard_map/ppermute | solution.py:555
  55.4 5.5 %collective-permute-start.23 = (f32[2,8,256]{2,1,0:T(8,128)S(1)}, f32[2,8,256]{2,1,0:T(8,128)S(1)}, u32[]{:S(2)}, u32[]{:S(2)}) collective-permute-start(f32[2,8,256]{2,1,0:T(8,128)S(1)} %combine.5.refs_4_), channel_id=1, source_target_pairs={{0,24},{4,28},{8,16},{12,20},{16,8},{20,12},{24,0},{28,4},{1,25},{... | collective-permute-start | bytes 49160 | tf_op jit(solution)/shard_map/ppermute | solution.py:555

commit v13 on v12

--- a/solution.py
+++ b/solution.py
@@ -31,8 +31,8 @@
 
 def prepare_kernel(*refs):
     arguments = refs[:6]
-    planes, extra = refs[6:8]
-    copied, sems = refs[8:14], refs[14]
+    planes = refs[6]
+    copied, sems = refs[7:13], refs[13]
     copies = [pltpu.make_async_copy(arguments[n], copied[n], sems.at[n]) for n in range(6)]
     for copy in copies:
         copy.start()
@@ -66,26 +66,24 @@
             right = right + select * (local * root_inverse)
         tropo = map_off * (root * inverse)
         planes[s, 3 * tracked : 4 * tracked, :] = tropo
-        planes[s, 4 * tracked :, :] = jnp.zeros((8, knot.shape[1]), jnp.float32)
+        planes[s, 4 * tracked : 4 * tracked + 8, :] = jnp.zeros((8, knot.shape[1]), jnp.float32)
         planes[s, 4 * tracked : 4 * tracked + 1, :] = knot.astype(jnp.float32)
         planes[s, 4 * tracked + 1 : 4 * tracked + 2, :tracked] = track[s : s + 1, :].astype(
             jnp.float32
         )
-        extra[s, :tracked, :] = res_off * root - tropo * right
-        extra[s, tracked:, :] = jnp.where(weight > 0.0, total / jnp.maximum(weight, 1.0), 0.0)
+        planes[s, 4 * tracked + 8 : 5 * tracked + 8, :] = res_off * root - tropo * right
+        planes[s, 5 * tracked + 8 :, :] = jnp.where(
+            weight > 0.0, total / jnp.maximum(weight, 1.0), 0.0
+        )
 
 
 def prepare(*arguments):
     stations, _, tracked, epochs = arguments[0].shape
-    f32 = jnp.float32
     return pl.pallas_call(
         prepare_kernel,
-        out_shape=[
-            jax.ShapeDtypeStruct((stations, 4 * tracked + 8, epochs), f32),
-            jax.ShapeDtypeStruct((stations, 2 * tracked, epochs), f32),
-        ],
+        out_shape=jax.ShapeDtypeStruct((stations, 6 * tracked + 8, epochs), jnp.float32),
         in_specs=[hbm()] * 6,
-        out_specs=[vmem()] * 2,
+        out_specs=vmem(),
         scratch_shapes=[pltpu.VMEM(a.shape, a.dtype) for a in arguments]
         + [pltpu.SemaphoreType.DMA((6,))],
         compiler_params=pltpu.CompilerParams(vmem_limit_bytes=HUGE_LIMIT),
@@ -149,7 +147,7 @@
     for d in range(groups):
         for p in range(per):
             s = d * per + p
-            planes[s] = plane_pieces[d][p]
+            planes[s] = plane_pieces[d][p, : planes.shape[1], :]
             rows_int[s : s + 1, :] = planes[
                 s, 4 * tracked + 1 : 4 * tracked + 2, :128].astype(jnp.int32)
     to_scalar = pltpu.make_async_copy(rows_int, track, track_sem)
@@ -189,9 +187,9 @@
     lax.fori_loop(0, stations // 2, visit, 0)
 
 
-def own_rows_of(planes, shape, orbit, width, base):
+def own_rows_of(planes, rows, orbit, width, base):
     groups = len(planes)
-    per, rows, epochs = shape
+    per, _, epochs = planes[0].shape
     own = orbit.shape[0]
     stations = groups * per
     half = jax.ShapeDtypeStruct((stations, width, epochs), jnp.bfloat16)
@@ -268,7 +266,7 @@
     to_scalar = pltpu.make_async_copy(rows_int, raw_track, track_sem)
     to_scalar.start()
     for n, piece in enumerate(raw_pieces):
-        raw_planes[n * per : (n + 1) * per] = piece[...]
+        raw_planes[n * per : (n + 1) * per] = piece[:, : raw_planes.shape[1], :]
     acc[...] = jnp.zeros_like(acc)
     spread_tropo[...] = jnp.zeros_like(spread_tropo)
 
@@ -413,9 +411,8 @@
 
 def blocks_kernel(groups, per, *refs):
     plane_pieces = refs[:groups]
-    extra_pieces = refs[groups : 2 * groups]
-    own_rows, orbit, small = refs[2 * groups :]
-    tracked = extra_pieces[0].shape[1] // 2
+    own_rows, orbit, small = refs[groups:]
+    tracked = (plane_pieces[0].shape[1] - 8) // 6
     epochs = orbit.shape[3]
     width = small.shape[2]
     own = orbit.shape[0]
@@ -429,8 +426,8 @@
             named = station[4 * tracked + 1 : 4 * tracked + 2, :tracked]
             picks.append((satellite == named.astype(jnp.int32)).astype(jnp.float32))
             a = [station[c * tracked : (c + 1) * tracked, :] for c in range(3)]
-            residual = extra_pieces[d][s, :tracked, :]
-            inverse = extra_pieces[d][s, tracked:, :]
+            residual = station[4 * tracked + 8 : 5 * tracked + 8, :]
+            inverse = station[5 * tracked + 8 :, :]
             weighted = [v * inverse for v in a]
             terms = [weighted[c] * a[e] for c, e in pairs] + [v * residual for v in a]
             for stack, term in zip(stacks, terms):
@@ -467,63 +464,65 @@
     small[1, :, : own * 8] = right
 
 
-def own_sums(planes, extras, own_rows, orbit):
+def own_sums(planes, own_rows, orbit):
     groups = len(planes)
-    per = extras[0].shape[0]
+    per = planes[0].shape[0]
     width = own_rows.shape[2]
     return pl.pallas_call(
         functools.partial(blocks_kernel, groups, per),
         out_shape=jax.ShapeDtypeStruct((2, 8, width), jnp.float32),
-        in_specs=[vmem()] * (2 * groups + 2),
+        in_specs=[vmem()] * (groups + 2),
         out_specs=vmem(),
         compiler_params=pltpu.CompilerParams(vmem_limit_bytes=MEDIUM_LIMIT),
         cost_estimate=pl.CostEstimate(
             flops=1 * 10**8, bytes_accessed=1 * 10**5, transcendentals=0),
         name="own_sums",
-    )(*planes, *extras, own_rows, orbit)
-
-
-def combine_kernel(pieces_count, *refs):
-    pieces, outs = refs[:pieces_count], refs[pieces_count:]
-    window = outs[0].shape[0]
+    )(*planes, own_rows, orbit)
+
+
+def combine_kernel(pieces_count, smalls_count, window, *refs):
+    pieces, smalls = refs[:pieces_count], refs[pieces_count : pieces_count + smalls_count]
+    outs = refs[pieces_count + smalls_count :]
+    small = smalls[0][...]
+    for ref in smalls[1:]:
+        small = small + ref[...]
     for n, out in enumerate(outs):
         part = pieces[0][n * window : (n + 1) * window]
         for piece in pieces[1:]:
             part = part + piece[n * window : (n + 1) * window]
-        out[...] = part
-
-
-def combine(pieces, window):
+        out[:window] = part
+        out[window:] = small
+
+
+def combine(pieces, smalls, window):
     count = pieces[0].shape[0] // window
+    width = pieces[0].shape[2]
     return pl.pallas_call(
-        functools.partial(combine_kernel, len(pieces)),
-        out_shape=[jax.ShapeDtypeStruct((window,) + pieces[0].shape[1:], jnp.float32)] * count,
-        in_specs=[vmem()] * len(pieces),
+        functools.partial(combine_kernel, len(pieces), len(smalls), window),
+        out_shape=[jax.ShapeDtypeStruct((window + 2, 8, width), jnp.float32)] * count,
+        in_specs=[vmem()] * (len(pieces) + len(smalls)),
         out_specs=[vmem()] * count,
         compiler_params=pltpu.CompilerParams(vmem_limit_bytes=SMALL_LIMIT),
         name="combine",
-    )(*pieces)
+    )(*pieces, *smalls)
 
 
 def finish_kernel(window, own, columns, sats, factor, cross_factor, *refs):
-    count = (len(refs) - 3) // 2
-    pieces, smalls = refs[:count], refs[count : 2 * count]
+    pieces = refs[:-3]
     normal, right, blocks = refs[-3:]
     width = pieces[0].shape[2]
     total = pieces[0][...]
-    small_total = smalls[0][...]
-    for piece, small in zip(pieces[1:], smalls[1:]):
+    for piece in pieces[1:]:
         total = total + piece[...]
-        small_total = small_total + small[...]
     first = lax.axis_index("sat") * own
     start = window_start(lax.axis_index("sta"), columns, sats, window)
-    part = total.reshape(window * 8, width)
+    part = total[:window].reshape(window * 8, width)
     row_owner = start + lax.broadcasted_iota(jnp.int32, part.shape, 0) // 8
     lane_owner = first + lax.broadcasted_iota(jnp.int32, part.shape, 1) // 8
     part = jnp.where(row_owner == lane_owner, 0.0, part * cross_factor)
     normal[...] = part.T[: own * 8, :]
-    right[...] = small_total[1, :1, : own * 8] * factor
-    small = small_total[0]
+    right[...] = total[window + 1, :1, : own * 8] * factor
+    small = total[window]
     room = -(-own // 32) * 32
     lane = lax.broadcasted_iota(jnp.int32, (width, 8 * room), 0)
     slot = lax.broadcasted_iota(jnp.int32, (width, 8 * room), 1)
@@ -536,7 +535,7 @@
         blocks[p] = factor * spread[:, p * room : p * room + own]
 
 
-def finish(pieces, smalls, window, own, columns, sats, factor, cross_factor):
+def finish(pieces, window, own, columns, sats, factor, cross_factor):
     return pl.pallas_call(
         functools.partial(finish_kernel, window, own, columns, sats, factor, cross_factor),
         out_shape=[
@@ -544,11 +543,11 @@
             jax.ShapeDtypeStruct((1, own * 8), jnp.float32),
             jax.ShapeDtypeStruct((8, 8, own), jnp.float32),
         ],
-        in_specs=[vmem()] * (2 * len(pieces)),
+        in_specs=[vmem()] * len(pieces),
         out_specs=[vmem()] * 3,
         compiler_params=pltpu.CompilerParams(vmem_limit_bytes=SMALL_LIMIT),
         name="finish",
-    )(*pieces, *smalls)
+    )(*pieces)
 
 
 def shift(value, axis, size, step):
@@ -582,17 +581,15 @@
     if own % 2 == 0 and nz % 2 == 0 and nx % 2 == 0:
         parts, orbit = cut_parts(orbit, nx)
     near = {d: [shift(part, "sat", group, d) for part in parts] for d in range(2, group, 2)}
-    planes, extra = prepare(sight, mapping, residual, counts, track, knots)
+    planes = prepare(sight, mapping, residual, counts, track, knots)
     own_planes = planes
-    other_planes, other_orbit, other_extra = core(planes), core(orbit), core(extra)
-    firsts = {d: values[0] for d, values in near.items()}
-    planes, firsts = lax.optimization_barrier((planes, firsts))
-    near = {d: [firsts[d]] + values[1:] for d, values in near.items()}
+    other_planes, other_orbit = core(planes), core(orbit)
+    planes, near = lax.optimization_barrier((planes, near))
     arrived = {d: shift(planes, "sat", group, d) for d in near}
     far = {}
     if len(parts) == 2:
         far = {d: [across(near[d][0], nx), across(near[d][1], 1)] for d in near}
-    ready = own_rows_of([own_planes, other_planes], planes.shape, orbit, width, 0)
+    ready = own_rows_of([own_planes, other_planes], 4 * tracked + 8, orbit, width, 0)
     ready, arrived, held_near, far = lax.optimization_barrier(
         (tuple(ready), arrived, near, far))
     partials = [(0, 0, 0, orbit), (1, 0, 0, other_orbit)]
@@ -601,39 +598,29 @@
             for start, value in zip((0, parts[0].shape[0]), values):
                 partials += [(d, turn, start, value), (d + 1, turn, start, core(value))]
     pieces = {0: own_planes, 1: other_planes}
-    extras = {0: extra, 1: other_extra}
     for d, value in arrived.items():
         pieces[d], pieces[d + 1] = value, core(value)
-        held, _ = lax.optimization_barrier((extra, value))
-        extras[d] = shift(held, "sat", group, d)
     places = tuple((d, turn, start) for d, turn, start, _ in partials)
     every = place([part[3] for part in partials], places, sats, own, nx)
-    every, extras = lax.optimization_barrier((every, extras))
-    for d in near:
-        extras[d + 1] = core(extras[d])
     *sums, own_rows = accumulate(
         ready, [pieces[d] for d in range(2, group)], every, own, nx, nz, window)
 
     half = nz // 2
     far_sums = [sums[0]] + [across(sums[2 * dx], dx) for dx in range(1, nx)]
-    small = own_sums([pieces[d] for d in range(group)], [extras[d] for d in range(group)],
-                     own_rows, orbit)
-    far_sums, small = lax.optimization_barrier((far_sums, small))
-    near_out, far_sums = lax.optimization_barrier((sums[1::2], far_sums))
-    chunks = list(combine(far_sums, window))
+    small = own_sums([pieces[d] for d in range(group)], own_rows, orbit)
     smalls = [small] + [across(small, dx) for dx in range(1, nx)]
-    small = combine(smalls, 2)[0]
-    chunks[-1], small = lax.optimization_barrier((chunks[-1], small))
+    far_sums, smalls = lax.optimization_barrier((far_sums, smalls))
+    chunks = list(combine(far_sums, smalls, window))
+    near_out, chunks = lax.optimization_barrier((sums[1::2], chunks))
     near_chunks = combine(
-        [near_out[0]] + [across(near_out[dx], dx) for dx in range(1, nx)], window)
+        [near_out[0]] + [across(near_out[dx], dx) for dx in range(1, nx)], smalls, window)
     final = [near_chunks[0]]
     final += [across(near_chunks[n], n * nx) for n in range(1, half)]
     final += [across(chunk, (half + n) * nx) for n, chunk in enumerate(chunks)]
-    finals = [small] + [across(small, dz * nx) for dz in range(1, nz)]
     total_stations = stations * columns_axis * group
     factor = sats / (total_stations * tracked * epochs)
     cross_factor = sats / (total_stations * epochs) ** 0.5
-    normal, right, blocks = finish(final, finals, window, own, columns, sats, factor, cross_factor)
+    normal, right, blocks = finish(final, window, own, columns, sats, factor, cross_factor)
     if window * 8 != columns:
         mine = lax.axis_index("sta")
         start = window_start(mine, columns, sats, window)

time: 62.1 us -> 57.4 us (0.924)
  starting transfers between devices: 26 us -> 18.5 us
  waiting for transfers between devices: 21.9 us -> 24.8 us
    ppermute x24 -> x18, starting transfers between devices: 26 us -> 18.5 us  [shift(): return lax.ppermute(value, axis, [(i, i ^ step) for i in range(size)])]
    ppermute x24 -> x18, waiting for transfers between devices: 21.9 us -> 24.8 us  [shift(): return lax.ppermute(value, axis, [(i, i ^ step) for i in range(size)])]
    unnamed x8 -> x6, local copies, waits for them, and re-layouts: 2.07 us -> 2.12 us
    pallas_call x4 -> x3, Pallas kernels: 2.03 us -> 2.03 us  [the longest x1 1.97 us: prepare(): pl.pallas_call(prepare_kernel, out_shape=jax.ShapeDtypeStruct((stations,...]
  transfers between devices with their start and end apart: 24 -> 18, of which waited for: 11 -> 9; matrix products, arithmetic and copies ran while one was open for 0% -> 0% of each run, Pallas kernels for 9% -> 10%
where the time goes in v13:
time: 57.4 us; the launch traced here: 57.2 us
  waiting for transfers between devices  24.8 us (43%)
  starting transfers between devices  18.5 us (32%)
  Pallas kernels  11.1 us (19%)
  local copies, waits for them, and re-layouts  2.12 us (4%)
  between operations  0.73 us (1%)
    ppermute x18, waiting for transfers between devices, shift(): return lax.ppermute(value, axis, [(i, i ^ step) for i in range(size)])  24.8 us
    ppermute x18, starting transfers between devices, shift(): return lax.ppermute(value, axis, [(i, i ^ step) for i in range(size)])  18.5 us
    pallas_call x1, Pallas kernels, accumulate(): pl.pallas_call(functools.partial(main_kernel, len(raw), own, nx, nz, wind...  4.47 us
    unnamed x6, local copies, waits for them, and re-layouts  2.12 us
    pallas_call x1, Pallas kernels, own_rows_of(): pl.pallas_call(functools.partial(own_rows_kernel, groups, per, own, width...  2.07 us
    pallas_call x1, Pallas kernels, prepare(): pl.pallas_call(prepare_kernel, out_shape=jax.ShapeDtypeStruct((stations,...  1.97 us
    pallas_call x1, Pallas kernels, own_sums(): pl.pallas_call(functools.partial(blocks_kernel, groups, per), out_shape=j...  1.3 us
  transfers between devices with their start and end apart: 18, of which 9 were waited for; matrix products, arithmetic and copies ran while one was open for 0% of the time, Pallas kernels for 10%

profile of v13, /device:TPU:0, one launch (start us, length us, event | category | flops | bytes accessed | tf_op | source)
XLA Modules:
  0.0 57.2 jit_solution(5293151900066263611)
XLA Ops:
  0.6 0.0 copy-start.2
  0.6 1.1 %copy-done.2 = f32[30,3,8,256]{3,2,1,0:T(8,128)S(1)} copy-done((f32[30,3,8,256]{3,2,1,0:T(8,128)S(1)}, f32[30,3,8,256]{3,2,1,0:T(8,128)}, u32[]{:S(2)}) %copy-start.2) | copy-done | bytes 737304
  1.7 0.1 cut_parts.1
  1.8 3.0 %collective-permute-start.1 = (f32[8,3,8,256]{3,2,1,0:T(8,128)S(1)}, f32[8,3,8,256]{3,2,1,0:T(8,128)S(1)}, u32[]{:S(2)}, u32[]{:S(2)}) collective-permute-start(f32[8,3,8,256]{3,2,1,0:T(8,128)S(1)} %get-tuple-element.47), channel_id=1, source_target_pairs={{0,2},{1,3},{2,0},{3,1},{4,6},{5,7},{6,4},{7,5},{8,10},{9,11},{10,... | collective-permute-start | bytes 589832 | tf_op jit(solution)/shard_map/ppermute | solution.py:554
  4.9 2.0 %prepare.1.refs_0_ = f32[2,200,256]{2,1,0:T(8,128)} custom-call(f32[2,3,32,256]{3,2,1,0:T(8,128)} %refs_0_.1, f32[2,32,256]{2,1,0:T(8,128)} %refs_1_.1, f32[2,32,256]{2,1,0:T(8,128)} %refs_2_.1, s32[2,32,256]{2,1,0:T(8,128)} %refs_3_.1, s32[2,32]{1,0:T(2,128)} %refs_4_.1, s32[2,256]{1,0:T(2,128)} %refs_5_.1), custom_call_target="tpu_custom_call" | custom-call | tf_op jit(solution)/shard_map/prepare/pallas_call | solution.py:82
  6.8 0.1 collective-permute-start
  6.9 0.1 collective-permute-start.2
  7.0 0.4 collective-permute-start.7
  7.4 6.3 %collective-permute-done.2.refs_4_ = f32[7,3,8,256]{3,2,1,0:T(8,128)S(1)} collective-permute-done((f32[7,3,8,256]{3,2,1,0:T(8,128)S(1)}, f32[7,3,8,256]{3,2,1,0:T(8,128)S(1)}, u32[]{:S(2)}, u32[]{:S(2)}) %collective-permute-start.2) | collective-permute-done | bytes 172064 | tf_op jit(solution)/shard_map/ppermute | solution.py:554
  13.7 0.0 collective-permute-done.1.refs_2_
  13.7 1.5 %collective-permute-start.3 = (f32[2,200,256]{2,1,0:T(8,128)}, f32[2,200,256]{2,1,0:T(8,128)S(1)}, u32[]{:S(2)}, u32[]{:S(2)}) collective-permute-start(f32[2,200,256]{2,1,0:T(8,128)} %prepare.1.refs_0_), channel_id=1, source_target_pairs={{0,2},{1,3},{2,0},{3,1},{4,6},{5,7},{6,4},{7,5},{8,10},{9,11},{10,... | collective-permute-start | bytes 1228808 | tf_op jit(solution)/shard_map/ppermute | solution.py:554
  15.2 1.6 %collective-permute-start.4 = (f32[8,3,8,256]{3,2,1,0:T(8,128)S(1)}, f32[8,3,8,256]{3,2,1,0:T(8,128)S(1)}, u32[]{:S(2)}, u32[]{:S(2)}) collective-permute-start(f32[8,3,8,256]{3,2,1,0:T(8,128)S(1)} %collective-permute-done.1.refs_2_), channel_id=1, source_target_pairs={{0,8},{4,12},{8,0},{12,4},{16,24},{20,28},{24,16},{28,20},{1,9},{5... | collective-permute-start | bytes 589832 | tf_op jit(solution)/shard_map/ppermute | solution.py:554
  16.8 1.5 %collective-permute-start.5 = (f32[7,3,8,256]{3,2,1,0:T(8,128)S(1)}, f32[7,3,8,256]{3,2,1,0:T(8,128)S(1)}, u32[]{:S(2)}, u32[]{:S(2)}) collective-permute-start(f32[7,3,8,256]{3,2,1,0:T(8,128)S(1)} %collective-permute-done.2.refs_4_), channel_id=1, source_target_pairs={{0,4},{4,0},{8,12},{12,8},{16,20},{20,16},{24,28},{28,24},{1,5},{5... | collective-permute-start | bytes 516104 | tf_op jit(solution)/shard_map/ppermute | solution.py:554
  18.3 0.0 collective-permute-done.refs_1_
  18.3 0.0 copy-start
  18.3 1.0 %copy-done = f32[2,200,256]{2,1,0:T(8,128)S(1)} copy-done((f32[2,200,256]{2,1,0:T(8,128)S(1)}, f32[2,200,256]{2,1,0:T(8,128)}, u32[]{:S(2)}) %copy-start) | copy-done | bytes 409624
  19.3 2.1 %own_rows.1 = (f32[4,136,256]{2,1,0:T(8,128)S(1)}, s32[4,128]{1,0:T(4,128)S(1)}, bf16[4,256,256]{2,1,0:T(8,128)(2,1)S(1)}, bf16[4,256,256]{2,1,0:T(8,128)(2,1)S(1)}) custom-call(f32[2,200,256]{2,1,0:T(8,128)S(1)} %copy-done, f32[2,200,256]{2,1,0:T(8,128)S(1)} %collective-permute-done.refs_1_, f32[30,3,8,256]{3,2,1,0:T(8,128)S(1)} %get-tuple-element.42.refs_2_.refs_0_.refs_5_), custom_call_target="tpu_custom_call" | custom-call | flops 2000000000 | bytes 2000000 | tf_op jit(solution)/shard_map/own_rows/pallas_call | solution.py:196
  21.3 0.8 %collective-permute-done.5.refs_8_ = f32[7,3,8,256]{3,2,1,0:T(8,128)S(1)} collective-permute-done((f32[7,3,8,256]{3,2,1,0:T(8,128)S(1)}, f32[7,3,8,256]{3,2,1,0:T(8,128)S(1)}, u32[]{:S(2)}, u32[]{:S(2)}) %collective-permute-start.5) | collective-permute-done | bytes 172064 | tf_op jit(solution)/shard_map/ppermute | solution.py:554
  22.2 0.0 collective-permute-done.4.refs_6_
  22.2 2.8 %collective-permute-done.3.refs_4_.refs_2_ = f32[2,200,256]{2,1,0:T(8,128)S(1)} collective-permute-done((f32[2,200,256]{2,1,0:T(8,128)}, f32[2,200,256]{2,1,0:T(8,128)S(1)}, u32[]{:S(2)}, u32[]{:S(2)}) %collective-permute-start.3) | collective-permute-done | bytes 409632 | tf_op jit(solution)/shard_map/ppermute | solution.py:554
  25.0 0.0 collective-permute-start.6
  25.0 0.5 collective-permute-start.10
  25.5 0.0 collective-permute-start.8
  25.5 0.5 collective-permute-start.11
  26.0 0.0 collective-permute-done.7.refs_1_
  26.0 0.0 collective-permute-start.9
  26.0 1.5 %collective-permute-done.11.refs_9_ = f32[7,3,8,256]{3,2,1,0:T(8,128)S(1)} collective-permute-done((f32[7,3,8,256]{3,2,1,0:T(8,128)S(1)}, f32[7,3,8,256]{3,2,1,0:T(8,128)S(1)}, u32[]{:S(2)}, u32[]{:S(2)}) %collective-permute-start.11) | collective-permute-done | bytes 172064 | tf_op jit(solution)/shard_map/ppermute | solution.py:554
  27.5 0.2 collective-permute-done.9.refs_5_
  27.8 0.0 collective-permute-done.10.refs_7_
  27.8 0.0 collective-permute-done.8.refs_3_
  27.8 0.2 place.1.refs_6_
  28.0 0.0 copy-start.1
  28.0 0.0 collective-permute-done.6.refs_5_.refs_3_
  28.0 4.5 %accumulate.1 = (f32[30,8,256]{2,1,0:T(8,128)S(1)}, f32[30,8,256]{2,1,0:T(8,128)S(1)}, f32[30,8,256]{2,1,0:T(8,128)S(1)}, f32[30,8,256]{2,1,0:T(8,128)S(1)}, f32[30,8,256]{2,1,0:T(8,128)S(1)}) custom-call(f32[4,136,256]{2,1,0:T(8,128)S(1)} %get-tuple-element.52.refs_0_, s32[4,128]{1,0:T(4,128)S(1)} %get-tuple-element.53.refs_1_, ...), custom_call_target="tpu_custom_call" | custom-call | flops 8000000000 | bytes 8000000 | tf_op jit(solution)/shard_map/accumulate/pallas_call | solution.py:387
  32.5 1.6 %collective-permute-start.12 = (f32[30,8,256]{2,1,0:T(8,128)S(1)}, f32[30,8,256]{2,1,0:T(8,128)S(1)}, u32[]{:S(2)}, u32[]{:S(2)}) collective-permute-start(f32[30,8,256]{2,1,0:T(8,128)S(1)} %get-tuple-element.64), channel_id=1, source_target_pairs={{0,4},{4,0},{8,12},{12,8},{16,20},{20,16},{24,28},{28,24},{1,5},{5... | collective-permute-start | bytes 737288 | tf_op jit(solution)/shard_map/ppermute | solution.py:554
  34.0 0.0 copy-done.1
  34.0 1.3 %own_sums.1.refs_2_ = f32[2,8,256]{2,1,0:T(8,128)S(1)} custom-call(f32[2,200,256]{2,1,0:T(8,128)S(1)} %copy-done.1, f32[2,200,256]{2,1,0:T(8,128)S(1)} %collective-permute-done.refs_1_, f32[2,200,256]{2,1,0:T(8,128)S(1)} %collective-permute-done.3.refs_4_.refs_2_, f32[2,200,256]{2,1,0:T(8,128)S(1)} %collective-permute-done.6.refs_5_.refs_3_, ...), custom_call_target="tpu_custom_call" | custom-call | flops 100000000 | bytes 100000 | tf_op jit(solution)/shard_map/own_sums/pallas_call | solution.py:471
  35.3 0.6 %collective-permute-start.13 = (f32[2,8,256]{2,1,0:T(8,128)S(1)}, f32[2,8,256]{2,1,0:T(8,128)S(1)}, u32[]{:S(2)}, u32[]{:S(2)}) collective-permute-start(f32[2,8,256]{2,1,0:T(8,128)S(1)} %own_sums.1.refs_2_), channel_id=1, source_target_pairs={{0,4},{4,0},{8,12},{12,8},{16,20},{20,16},{24,28},{28,24},{1,5},{5... | collective-permute-start | bytes 49160 | tf_op jit(solution)/shard_map/ppermute | solution.py:554
  35.9 4.9 %collective-permute-done.13.refs_3_ = f32[2,8,256]{2,1,0:T(8,128)S(1)} collective-permute-done((f32[2,8,256]{2,1,0:T(8,128)S(1)}, f32[2,8,256]{2,1,0:T(8,128)S(1)}, u32[]{:S(2)}, u32[]{:S(2)}) %collective-permute-start.13) | collective-permute-done | bytes 16416 | tf_op jit(solution)/shard_map/ppermute | solution.py:554
  40.9 0.0 collective-permute-done.12.refs_1_
  40.9 1.6 %collective-permute-start.14 = (f32[30,8,256]{2,1,0:T(8,128)S(1)}, f32[30,8,256]{2,1,0:T(8,128)S(1)}, u32[]{:S(2)}, u32[]{:S(2)}) collective-permute-start(f32[30,8,256]{2,1,0:T(8,128)S(1)} %get-tuple-element.73), channel_id=1, source_target_pairs={{0,4},{4,0},{8,12},{12,8},{16,20},{20,16},{24,28},{28,24},{1,5},{5... | collective-permute-start | bytes 737288 | tf_op jit(solution)/shard_map/ppermute | solution.py:554
  42.5 2.6 %collective-permute-start.16 = (f32[17,8,256]{2,1,0:T(8,128)S(1)}, f32[17,8,256]{2,1,0:T(8,128)S(1)}, u32[]{:S(2)}, u32[]{:S(2)}) collective-permute-start(f32[17,8,256]{2,1,0:T(8,128)S(1)} %get-tuple-element.76), channel_id=1, source_target_pairs={{0,16},{4,20},{8,24},{12,28},{16,0},{20,4},{24,8},{28,12},{1,17},{... | collective-permute-start | bytes 417800 | tf_op jit(solution)/shard_map/ppermute | solution.py:554
  45.1 1.3 %collective-permute-start.17 = (f32[17,8,256]{2,1,0:T(8,128)S(1)}, f32[17,8,256]{2,1,0:T(8,128)S(1)}, u32[]{:S(2)}, u32[]{:S(2)}) collective-permute-start(f32[17,8,256]{2,1,0:T(8,128)S(1)} %get-tuple-element.77), channel_id=1, source_target_pairs={{0,24},{4,28},{8,16},{12,20},{16,8},{20,12},{24,0},{28,4},{1,25},{... | collective-permute-start | bytes 417800 | tf_op jit(solution)/shard_map/ppermute | solution.py:554
  46.4 1.8 %collective-permute-done.14.refs_1_ = f32[30,8,256]{2,1,0:T(8,128)S(1)} collective-permute-done((f32[30,8,256]{2,1,0:T(8,128)S(1)}, f32[30,8,256]{2,1,0:T(8,128)S(1)}, u32[]{:S(2)}, u32[]{:S(2)}) %collective-permute-start.14) | collective-permute-done | bytes 245792 | tf_op jit(solution)/shard_map/ppermute | solution.py:554
  48.2 1.7 %collective-permute-start.15 = (f32[17,8,256]{2,1,0:T(8,128)S(1)}, f32[17,8,256]{2,1,0:T(8,128)S(1)}, u32[]{:S(2)}, u32[]{:S(2)}) collective-permute-start(f32[17,8,256]{2,1,0:T(8,128)S(1)} %get-tuple-element.75), channel_id=1, source_target_pairs={{0,8},{4,12},{8,0},{12,4},{16,24},{20,28},{24,16},{28,20},{1,9},{5... | collective-permute-start | bytes 417800 | tf_op jit(solution)/shard_map/ppermute | solution.py:554
  49.8 5.3 %collective-permute-done.16.refs_2_ = f32[17,8,256]{2,1,0:T(8,128)S(1)} collective-permute-done((f32[17,8,256]{2,1,0:T(8,128)S(1)}, f32[17,8,256]{2,1,0:T(8,128)S(1)}, u32[]{:S(2)}, u32[]{:S(2)}) %collective-permute-start.16) | collective-permute-done | bytes 139296 | tf_op jit(solution)/shard_map/ppermute | solution.py:554
  55.1 0.0 collective-permute-done.17.refs_3_
  55.1 1.1 %collective-permute-done.15.refs_1_ = f32[17,8,256]{2,1,0:T(8,128)S(1)} collective-permute-done((f32[17,8,256]{2,1,0:T(8,128)S(1)}, f32[17,8,256]{2,1,0:T(8,128)S(1)}, u32[]{:S(2)}, u32[]{:S(2)}) %collective-permute-start.15) | collective-permute-done | bytes 139296 | tf_op jit(solution)/shard_map/ppermute | solution.py:554
  56.2 1.0 %finish.1 = (f32[240,120]{1,0:T(8,128)}, f32[1,240]{1,0:T(1,128)}, f32[8,8,30]{2,1,0:T(8,128)}) custom-call(f32[17,8,256]{2,1,0:T(8,128)S(1)} %get-tuple-element.74.refs_0_, f32[17,8,256]{2,1,0:T(8,128)S(1)} %collective-permute-done.15.refs_1_, f32[17,8,256]{2,1,0:T(8,128)S(1)} %collective-permute-done.16.refs_2_, ...), custom_call_target="tpu_custom_call" | custom-call | tf_op jit(solution)/shard_map/finish/pallas_call | solution.py:539
  (2 shorter events, 0.1 us)
Async XLA Ops:
  0.6 1.1 %copy-start.2 = (f32[30,3,8,256]{3,2,1,0:T(8,128)S(1)}, f32[30,3,8,256]{3,2,1,0:T(8,128)}, u32[]{:S(2)}) copy-start(f32[30,3,8,256]{3,2,1,0:T(8,128)} %orbit.1) | copy-start | bytes 2211844
  1.8 11.9 %collective-permute-start.1 = (f32[8,3,8,256]{3,2,1,0:T(8,128)S(1)}, f32[8,3,8,256]{3,2,1,0:T(8,128)S(1)}, u32[]{:S(2)}, u32[]{:S(2)}) collective-permute-start(f32[8,3,8,256]{3,2,1,0:T(8,128)S(1)} %get-tuple-element.47), channel_id=1, source_target_pairs={{0,2},{1,3},{2,0},{3,1},{4,6},{5,7},{6,4},{7,5},{8,10},{9,11},{10,... | collective-permute-start | bytes 589832 | tf_op jit(solution)/shard_map/ppermute | solution.py:554
  6.8 11.4 %collective-permute-start = (f32[2,200,256]{2,1,0:T(8,128)}, f32[2,200,256]{2,1,0:T(8,128)S(1)}, u32[]{:S(2)}, u32[]{:S(2)}) collective-permute-start(f32[2,200,256]{2,1,0:T(8,128)} %prepare.1.refs_0_), channel_id=1, source_target_pairs={{0,1},{1,0},{2,3},{3,2},{4,5},{5,4},{6,7},{7,6},{8,9},{9,8},{10,11... | collective-permute-start | bytes 1228808 | tf_op jit(solution)/shard_map/ppermute | solution.py:554
  6.9 6.8 %collective-permute-start.2 = (f32[7,3,8,256]{3,2,1,0:T(8,128)S(1)}, f32[7,3,8,256]{3,2,1,0:T(8,128)S(1)}, u32[]{:S(2)}, u32[]{:S(2)}) collective-permute-start(f32[7,3,8,256]{3,2,1,0:T(8,128)S(1)} %get-tuple-element.48), channel_id=1, source_target_pairs={{0,2},{1,3},{2,0},{3,1},{4,6},{5,7},{6,4},{7,5},{8,10},{9,11},{10,... | collective-permute-start | bytes 516104 | tf_op jit(solution)/shard_map/ppermute | solution.py:554
  7.0 19.0 %collective-permute-start.7 = (f32[30,3,8,256]{3,2,1,0:T(8,128)S(1)}, f32[30,3,8,256]{3,2,1,0:T(8,128)S(1)}, u32[]{:S(2)}, u32[]{:S(2)}) collective-permute-start(f32[30,3,8,256]{3,2,1,0:T(8,128)S(1)} %get-tuple-element.42.refs_2_.refs_0_.refs_5_), channel_id=1, source_target_pairs={{0,1},{1,0},{2,3},{3,2},{4,5},{5,4},{6,7},{7,6},{8,9},{9,8},{10,11... | collective-permute-start | bytes 2211848 | tf_op jit(solution)/shard_map/ppermute | solution.py:554
  13.7 11.2 %collective-permute-start.3 = (f32[2,200,256]{2,1,0:T(8,128)}, f32[2,200,256]{2,1,0:T(8,128)S(1)}, u32[]{:S(2)}, u32[]{:S(2)}) collective-permute-start(f32[2,200,256]{2,1,0:T(8,128)} %prepare.1.refs_0_), channel_id=1, source_target_pairs={{0,2},{1,3},{2,0},{3,1},{4,6},{5,7},{6,4},{7,5},{8,10},{9,11},{10,... | collective-permute-start | bytes 1228808 | tf_op jit(solution)/shard_map/ppermute | solution.py:554
  15.2 7.0 %collective-permute-start.4 = (f32[8,3,8,256]{3,2,1,0:T(8,128)S(1)}, f32[8,3,8,256]{3,2,1,0:T(8,128)S(1)}, u32[]{:S(2)}, u32[]{:S(2)}) collective-permute-start(f32[8,3,8,256]{3,2,1,0:T(8,128)S(1)} %collective-permute-done.1.refs_2_), channel_id=1, source_target_pairs={{0,8},{4,12},{8,0},{12,4},{16,24},{20,28},{24,16},{28,20},{1,9},{5... | collective-permute-start | bytes 589832 | tf_op jit(solution)/shard_map/ppermute | solution.py:554
  16.8 5.4 %collective-permute-start.5 = (f32[7,3,8,256]{3,2,1,0:T(8,128)S(1)}, f32[7,3,8,256]{3,2,1,0:T(8,128)S(1)}, u32[]{:S(2)}, u32[]{:S(2)}) collective-permute-start(f32[7,3,8,256]{3,2,1,0:T(8,128)S(1)} %collective-permute-done.2.refs_4_), channel_id=1, source_target_pairs={{0,4},{4,0},{8,12},{12,8},{16,20},{20,16},{24,28},{28,24},{1,5},{5... | collective-permute-start | bytes 516104 | tf_op jit(solution)/shard_map/ppermute | solution.py:554
  18.3 1.0 %copy-start = (f32[2,200,256]{2,1,0:T(8,128)S(1)}, f32[2,200,256]{2,1,0:T(8,128)}, u32[]{:S(2)}) copy-start(f32[2,200,256]{2,1,0:T(8,128)} %prepare.1.refs_0_) | copy-start | bytes 1228804
  25.0 3.0 %collective-permute-start.6 = (f32[2,200,256]{2,1,0:T(8,128)S(1)}, f32[2,200,256]{2,1,0:T(8,128)S(1)}, u32[]{:S(2)}, u32[]{:S(2)}) collective-permute-start(f32[2,200,256]{2,1,0:T(8,128)S(1)} %collective-permute-done.3.refs_4_.refs_2_), channel_id=1, source_target_pairs={{0,1},{1,0},{2,3},{3,2},{4,5},{5,4},{6,7},{7,6},{8,9},{9,8},{10,11... | collective-permute-start | bytes 1228808 | tf_op jit(solution)/shard_map/ppermute | solution.py:554
  25.0 2.8 %collective-permute-start.10 = (f32[8,3,8,256]{3,2,1,0:T(8,128)S(1)}, f32[8,3,8,256]{3,2,1,0:T(8,128)S(1)}, u32[]{:S(2)}, u32[]{:S(2)}) collective-permute-start(f32[8,3,8,256]{3,2,1,0:T(8,128)S(1)} %collective-permute-done.4.refs_6_), channel_id=1, source_target_pairs={{0,1},{1,0},{2,3},{3,2},{4,5},{5,4},{6,7},{7,6},{8,9},{9,8},{10,11... | collective-permute-start | bytes 589832 | tf_op jit(solution)/shard_map/ppermute | solution.py:554
  25.5 2.3 %collective-permute-start.8 = (f32[8,3,8,256]{3,2,1,0:T(8,128)S(1)}, f32[8,3,8,256]{3,2,1,0:T(8,128)S(1)}, u32[]{:S(2)}, u32[]{:S(2)}) collective-permute-start(f32[8,3,8,256]{3,2,1,0:T(8,128)S(1)} %collective-permute-done.1.refs_2_), channel_id=1, source_target_pairs={{0,1},{1,0},{2,3},{3,2},{4,5},{5,4},{6,7},{7,6},{8,9},{9,8},{10,11... | collective-permute-start | bytes 589832 | tf_op jit(solution)/shard_map/ppermute | solution.py:554
  25.5 2.0 %collective-permute-start.11 = (f32[7,3,8,256]{3,2,1,0:T(8,128)S(1)}, f32[7,3,8,256]{3,2,1,0:T(8,128)S(1)}, u32[]{:S(2)}, u32[]{:S(2)}) collective-permute-start(f32[7,3,8,256]{3,2,1,0:T(8,128)S(1)} %collective-permute-done.5.refs_8_), channel_id=1, source_target_pairs={{0,1},{1,0},{2,3},{3,2},{4,5},{5,4},{6,7},{7,6},{8,9},{9,8},{10,11... | collective-permute-start | bytes 516104 | tf_op jit(solution)/shard_map/ppermute | solution.py:554
  26.0 1.8 %collective-permute-start.9 = (f32[7,3,8,256]{3,2,1,0:T(8,128)S(1)}, f32[7,3,8,256]{3,2,1,0:T(8,128)S(1)}, u32[]{:S(2)}, u32[]{:S(2)}) collective-permute-start(f32[7,3,8,256]{3,2,1,0:T(8,128)S(1)} %collective-permute-done.2.refs_4_), channel_id=1, source_target_pairs={{0,1},{1,0},{2,3},{3,2},{4,5},{5,4},{6,7},{7,6},{8,9},{9,8},{10,11... | collective-permute-start | bytes 516104 | tf_op jit(solution)/shard_map/ppermute | solution.py:554
  28.0 6.1 %copy-start.1 = (f32[2,200,256]{2,1,0:T(8,128)S(1)}, f32[2,200,256]{2,1,0:T(8,128)}, u32[]{:S(2)}) copy-start(f32[2,200,256]{2,1,0:T(8,128)} %prepare.1.refs_0_) | copy-start | bytes 1228804
  32.5 8.4 %collective-permute-start.12 = (f32[30,8,256]{2,1,0:T(8,128)S(1)}, f32[30,8,256]{2,1,0:T(8,128)S(1)}, u32[]{:S(2)}, u32[]{:S(2)}) collective-permute-start(f32[30,8,256]{2,1,0:T(8,128)S(1)} %get-tuple-element.64), channel_id=1, source_target_pairs={{0,4},{4,0},{8,12},{12,8},{16,20},{20,16},{24,28},{28,24},{1,5},{5... | collective-permute-start | bytes 737288 | tf_op jit(solution)/shard_map/ppermute | solution.py:554
  35.3 5.5 %collective-permute-start.13 = (f32[2,8,256]{2,1,0:T(8,128)S(1)}, f32[2,8,256]{2,1,0:T(8,128)S(1)}, u32[]{:S(2)}, u32[]{:S(2)}) collective-permute-start(f32[2,8,256]{2,1,0:T(8,128)S(1)} %own_sums.1.refs_2_), channel_id=1, source_target_pairs={{0,4},{4,0},{8,12},{12,8},{16,20},{20,16},{24,28},{28,24},{1,5},{5... | collective-permute-start | bytes 49160 | tf_op jit(solution)/shard_map/ppermute | solution.py:554
  40.9 7.2 %collective-permute-start.14 = (f32[30,8,256]{2,1,0:T(8,128)S(1)}, f32[30,8,256]{2,1,0:T(8,128)S(1)}, u32[]{:S(2)}, u32[]{:S(2)}) collective-permute-start(f32[30,8,256]{2,1,0:T(8,128)S(1)} %get-tuple-element.73), channel_id=1, source_target_pairs={{0,4},{4,0},{8,12},{12,8},{16,20},{20,16},{24,28},{28,24},{1,5},{5... | collective-permute-start | bytes 737288 | tf_op jit(solution)/shard_map/ppermute | solution.py:554
  42.5 12.7 %collective-permute-start.16 = (f32[17,8,256]{2,1,0:T(8,128)S(1)}, f32[17,8,256]{2,1,0:T(8,128)S(1)}, u32[]{:S(2)}, u32[]{:S(2)}) collective-permute-start(f32[17,8,256]{2,1,0:T(8,128)S(1)} %get-tuple-element.76), channel_id=1, source_target_pairs={{0,16},{4,20},{8,24},{12,28},{16,0},{20,4},{24,8},{28,12},{1,17},{... | collective-permute-start | bytes 417800 | tf_op jit(solution)/shard_map/ppermute | solution.py:554
  45.1 10.1 %collective-permute-start.17 = (f32[17,8,256]{2,1,0:T(8,128)S(1)}, f32[17,8,256]{2,1,0:T(8,128)S(1)}, u32[]{:S(2)}, u32[]{:S(2)}) collective-permute-start(f32[17,8,256]{2,1,0:T(8,128)S(1)} %get-tuple-element.77), channel_id=1, source_target_pairs={{0,24},{4,28},{8,16},{12,20},{16,8},{20,12},{24,0},{28,4},{1,25},{... | collective-permute-start | bytes 417800 | tf_op jit(solution)/shard_map/ppermute | solution.py:554
  48.2 8.0 %collective-permute-start.15 = (f32[17,8,256]{2,1,0:T(8,128)S(1)}, f32[17,8,256]{2,1,0:T(8,128)S(1)}, u32[]{:S(2)}, u32[]{:S(2)}) collective-permute-start(f32[17,8,256]{2,1,0:T(8,128)S(1)} %get-tuple-element.75), channel_id=1, source_target_pairs={{0,8},{4,12},{8,0},{12,4},{16,24},{20,28},{24,16},{28,20},{1,9},{5... | collective-permute-start | bytes 417800 | tf_op jit(solution)/shard_map/ppermute | solution.py:554

commit v14 on v13

--- a/solution.py
+++ b/solution.py
@@ -242,10 +242,11 @@
     raw_pieces = refs[4 : 4 + raw]
     orbit = refs[4 + raw]
     outs = refs[5 + raw : 5 + raw + 2 * nx]
-    own_out = refs[5 + raw + 2 * nx]
+    turned = refs[5 + raw + 2 * nx : 5 + raw + 2 * nx + nz]
+    own_out = refs[5 + raw + 2 * nx + nz]
     (acc, stream_a, stream_b, product_a, product_b, tropo_a, tropo_b, spread_tropo,
      dense_a, dense_b, raw_planes, rows_int, raw_track, track_sem) = refs[
-         6 + raw + 2 * nx :]
+         6 + raw + 2 * nx + nz :]
     streams, denses = (stream_a, stream_b), (dense_a, dense_b)
     products, tropos = (product_a, product_b), (tropo_a, tropo_b)
     tracked, _, width = product_a.shape
@@ -372,8 +373,11 @@
     for dx in range(nx):
         for dz in range(nz):
             start = window_start(mine ^ (dz * nx + dx), columns, sats, window)
-            at = (dz % half) * window
-            outs[2 * dx + (dz < half)][at : at + window] = acc[pl.ds(start, window)]
+            size = outs[0].shape[0] // half
+            last = window - size
+            at = (dz % half) * size
+            outs[2 * dx + (dz < half)][at : at + size] = acc[pl.ds(start, size)]
+            turned[dz][dx * last : (dx + 1) * last] = acc[pl.ds(start + size, last)]
 
 
 def accumulate(ready, raw, orbit, own, nx, nz, window):
@@ -383,7 +387,9 @@
     tracked = (rows - 8) // 4
     width = ready[2].shape[1]
     slabs = -(-(stations + more) // PACKED)
-    outs = [jax.ShapeDtypeStruct((nz // 2 * window, 8, width), jnp.float32)] * (2 * nx)
+    last = window // 5
+    outs = [jax.ShapeDtypeStruct((nz // 2 * (window - last), 8, width), jnp.float32)] * (2 * nx)
+    outs += [jax.ShapeDtypeStruct((nx * last, 8, width), jnp.float32)] * nz
     return pl.pallas_call(
         functools.partial(main_kernel, len(raw), own, nx, nz, window),
         out_shape=outs + [jax.ShapeDtypeStruct((own, 8, width), jnp.float32)],
@@ -507,22 +513,48 @@
     )(*pieces, *smalls)
 
 
-def finish_kernel(window, own, columns, sats, factor, cross_factor, *refs):
-    pieces = refs[:-3]
+def sum_over_z_kernel(count, *refs):
+    pieces, outs = refs[:count], refs[count:]
+    total = pieces[0][...]
+    for piece in pieces[1:]:
+        total = total + piece[...]
+    size = outs[0].shape[0]
+    for dx, out in enumerate(outs):
+        out[...] = total[dx * size : (dx + 1) * size]
+
+
+def sum_over_z(pieces, nx):
+    rows, _, width = pieces[0].shape
+    return pl.pallas_call(
+        functools.partial(sum_over_z_kernel, len(pieces)),
+        out_shape=[jax.ShapeDtypeStruct((rows // nx, 8, width), jnp.float32)] * nx,
+        in_specs=[vmem()] * len(pieces),
+        out_specs=[vmem()] * nx,
+        compiler_params=pltpu.CompilerParams(vmem_limit_bytes=SMALL_LIMIT),
+        name="sum_over_z",
+    )(*pieces)
+
+
+def finish_kernel(nz, window, own, columns, sats, factor, cross_factor, *refs):
+    pieces, lasts = refs[:nz], refs[nz:-3]
     normal, right, blocks = refs[-3:]
     width = pieces[0].shape[2]
     total = pieces[0][...]
     for piece in pieces[1:]:
         total = total + piece[...]
+    last = lasts[0][...]
+    for piece in lasts[1:]:
+        last = last + piece[...]
+    size = total.shape[0] - 2
     first = lax.axis_index("sat") * own
     start = window_start(lax.axis_index("sta"), columns, sats, window)
-    part = total[:window].reshape(window * 8, width)
+    part = jnp.concatenate([total[:size], last], 0).reshape(window * 8, width)
     row_owner = start + lax.broadcasted_iota(jnp.int32, part.shape, 0) // 8
     lane_owner = first + lax.broadcasted_iota(jnp.int32, part.shape, 1) // 8
     part = jnp.where(row_owner == lane_owner, 0.0, part * cross_factor)
     normal[...] = part.T[: own * 8, :]
-    right[...] = total[window + 1, :1, : own * 8] * factor
-    small = total[window]
+    right[...] = total[size + 1, :1, : own * 8] * factor
+    small = total[size]
     room = -(-own // 32) * 32
     lane = lax.broadcasted_iota(jnp.int32, (width, 8 * room), 0)
     slot = lax.broadcasted_iota(jnp.int32, (width, 8 * room), 1)
@@ -535,19 +567,20 @@
         blocks[p] = factor * spread[:, p * room : p * room + own]
 
 
-def finish(pieces, window, own, columns, sats, factor, cross_factor):
-    return pl.pallas_call(
-        functools.partial(finish_kernel, window, own, columns, sats, factor, cross_factor),
+def finish(pieces, lasts, window, own, columns, sats, factor, cross_factor):
+    return pl.pallas_call(
+        functools.partial(
+            finish_kernel, len(pieces), window, own, columns, sats, factor, cross_factor),
         out_shape=[
             jax.ShapeDtypeStruct((own * 8, window * 8), jnp.float32),
             jax.ShapeDtypeStruct((1, own * 8), jnp.float32),
             jax.ShapeDtypeStruct((8, 8, own), jnp.float32),
         ],
-        in_specs=[vmem()] * len(pieces),
+        in_specs=[vmem()] * (len(pieces) + len(lasts)),
         out_specs=[vmem()] * 3,
         compiler_params=pltpu.CompilerParams(vmem_limit_bytes=SMALL_LIMIT),
         name="finish",
-    )(*pieces)
+    )(*pieces, *lasts)
 
 
 def shift(value, axis, size, step):
@@ -598,29 +631,35 @@
             for start, value in zip((0, parts[0].shape[0]), values):
                 partials += [(d, turn, start, value), (d + 1, turn, start, core(value))]
     pieces = {0: own_planes, 1: other_planes}
+    places = tuple(part[:3] for part in partials)
+    every = place([part[3] for part in partials], places, sats, own, nx)
     for d, value in arrived.items():
         pieces[d], pieces[d + 1] = value, core(value)
-    places = tuple((d, turn, start) for d, turn, start, _ in partials)
-    every = place([part[3] for part in partials], places, sats, own, nx)
     *sums, own_rows = accumulate(
         ready, [pieces[d] for d in range(2, group)], every, own, nx, nz, window)
 
     half = nz // 2
+    turned = sums[2 * nx :]
+    sums = sums[: 2 * nx]
+    size = sums[0].shape[0] // half
+    turned = [turned[0]] + [across(turned[dz], dz * nx) for dz in range(1, nz)]
+    lasts = sum_over_z(turned, nx)
+    lasts = [lasts[0]] + [across(lasts[dx], dx) for dx in range(1, nx)]
     far_sums = [sums[0]] + [across(sums[2 * dx], dx) for dx in range(1, nx)]
     small = own_sums([pieces[d] for d in range(group)], own_rows, orbit)
     smalls = [small] + [across(small, dx) for dx in range(1, nx)]
     far_sums, smalls = lax.optimization_barrier((far_sums, smalls))
-    chunks = list(combine(far_sums, smalls, window))
-    near_out, chunks = lax.optimization_barrier((sums[1::2], chunks))
+    chunks = list(combine(far_sums, smalls, size))
+    near_out, _, _ = lax.optimization_barrier((sums[1::2], chunks, turned))
     near_chunks = combine(
-        [near_out[0]] + [across(near_out[dx], dx) for dx in range(1, nx)], smalls, window)
+        [near_out[0]] + [across(near_out[dx], dx) for dx in range(1, nx)], smalls, size)
     final = [near_chunks[0]]
     final += [across(near_chunks[n], n * nx) for n in range(1, half)]
     final += [across(chunk, (half + n) * nx) for n, chunk in enumerate(chunks)]
     total_stations = stations * columns_axis * group
     factor = sats / (total_stations * tracked * epochs)
     cross_factor = sats / (total_stations * epochs) ** 0.5
-    normal, right, blocks = finish(final, window, own, columns, sats, factor, cross_factor)
+    normal, right, blocks = finish(final, lasts, window, own, columns, sats, factor, cross_factor)
     if window * 8 != columns:
         mine = lax.axis_index("sta")
         start = window_start(mine, columns, sats, window)

time: 57.4 us -> 56.2 us (0.979)
  waiting for transfers between devices: 24.8 us -> 21.7 us
  starting transfers between devices: 18.5 us -> 20.3 us
    ppermute x18 -> x22, waiting for transfers between devices: 24.8 us -> 21.7 us  [shift(): return lax.ppermute(value, axis, [(i, i ^ step) for i in range(size)])]
    ppermute x18 -> x22, starting transfers between devices: 18.5 us -> 20.3 us  [shift(): return lax.ppermute(value, axis, [(i, i ^ step) for i in range(size)])]
  transfers between devices with their start and end apart: 18 -> 22, of which waited for: 9 -> 11; matrix products, arithmetic and copies ran while one was open for 0% -> 0% of each run, Pallas kernels for 10% -> 10%
where the time goes in v14:
time: 56.2 us; the launch traced here: 56 us
  waiting for transfers between devices  21.7 us (39%)
  starting transfers between devices  20.3 us (36%)
  Pallas kernels  11.1 us (20%)
  local copies, waits for them, and re-layouts  2.12 us (4%)
  between operations  0.75 us (1%)
    ppermute x22, waiting for transfers between devices, shift(): return lax.ppermute(value, axis, [(i, i ^ step) for i in range(size)])  21.7 us
    ppermute x22, starting transfers between devices, shift(): return lax.ppermute(value, axis, [(i, i ^ step) for i in range(size)])  20.3 us
    pallas_call x1, Pallas kernels, accumulate(): pl.pallas_call(functools.partial(main_kernel, len(raw), own, nx, nz, wind...  4.46 us
    unnamed x6, local copies, waits for them, and re-layouts  2.12 us
    pallas_call x1, Pallas kernels, own_rows_of(): pl.pallas_call(functools.partial(own_rows_kernel, groups, per, own, width...  2.07 us
    pallas_call x1, Pallas kernels, prepare(): pl.pallas_call(prepare_kernel, out_shape=jax.ShapeDtypeStruct((stations,...  1.98 us
    pallas_call x1, Pallas kernels, own_sums(): pl.pallas_call(functools.partial(blocks_kernel, groups, per), out_shape=j...  1.31 us
  transfers between devices with their start and end apart: 22, of which 11 were waited for; matrix products, arithmetic and copies ran while one was open for 0% of the time, Pallas kernels for 10%

profile of v14, /device:TPU:0, one launch (start us, length us, event | category | flops | bytes accessed | tf_op | source)
XLA Modules:
  0.0 56.0 jit_solution(4730303717350881235)
XLA Ops:
  0.6 0.0 copy-start.2
  0.6 1.1 %copy-done.2 = f32[30,3,8,256]{3,2,1,0:T(8,128)S(1)} copy-done((f32[30,3,8,256]{3,2,1,0:T(8,128)S(1)}, f32[30,3,8,256]{3,2,1,0:T(8,128)}, u32[]{:S(2)}) %copy-start.2) | copy-done | bytes 737304
  1.7 0.1 cut_parts.1
  1.8 3.0 %collective-permute-start.1 = (f32[8,3,8,256]{3,2,1,0:T(8,128)S(1)}, f32[8,3,8,256]{3,2,1,0:T(8,128)S(1)}, u32[]{:S(2)}, u32[]{:S(2)}) collective-permute-start(f32[8,3,8,256]{3,2,1,0:T(8,128)S(1)} %get-tuple-element.51), channel_id=1, source_target_pairs={{0,2},{1,3},{2,0},{3,1},{4,6},{5,7},{6,4},{7,5},{8,10},{9,11},{10,... | collective-permute-start | bytes 589832 | tf_op jit(solution)/shard_map/ppermute | solution.py:587
  4.9 2.0 %prepare.1.refs_0_ = f32[2,200,256]{2,1,0:T(8,128)} custom-call(f32[2,3,32,256]{3,2,1,0:T(8,128)} %refs_0_.1, f32[2,32,256]{2,1,0:T(8,128)} %refs_1_.1, f32[2,32,256]{2,1,0:T(8,128)} %refs_2_.1, s32[2,32,256]{2,1,0:T(8,128)} %refs_3_.1, s32[2,32]{1,0:T(2,128)} %refs_4_.1, s32[2,256]{1,0:T(2,128)} %refs_5_.1), custom_call_target="tpu_custom_call" | custom-call | tf_op jit(solution)/shard_map/prepare/pallas_call | solution.py:82
  6.8 0.1 collective-permute-start
  6.9 0.1 collective-permute-start.2
  7.0 0.4 collective-permute-start.7
  7.4 6.3 %collective-permute-done.2.refs_4_ = f32[7,3,8,256]{3,2,1,0:T(8,128)S(1)} collective-permute-done((f32[7,3,8,256]{3,2,1,0:T(8,128)S(1)}, f32[7,3,8,256]{3,2,1,0:T(8,128)S(1)}, u32[]{:S(2)}, u32[]{:S(2)}) %collective-permute-start.2) | collective-permute-done | bytes 172064 | tf_op jit(solution)/shard_map/ppermute | solution.py:587
  13.7 0.0 collective-permute-done.1.refs_2_
  13.7 1.5 %collective-permute-start.3 = (f32[2,200,256]{2,1,0:T(8,128)}, f32[2,200,256]{2,1,0:T(8,128)S(1)}, u32[]{:S(2)}, u32[]{:S(2)}) collective-permute-start(f32[2,200,256]{2,1,0:T(8,128)} %prepare.1.refs_0_), channel_id=1, source_target_pairs={{0,2},{1,3},{2,0},{3,1},{4,6},{5,7},{6,4},{7,5},{8,10},{9,11},{10,... | collective-permute-start | bytes 1228808 | tf_op jit(solution)/shard_map/ppermute | solution.py:587
  15.2 1.6 %collective-permute-start.4 = (f32[8,3,8,256]{3,2,1,0:T(8,128)S(1)}, f32[8,3,8,256]{3,2,1,0:T(8,128)S(1)}, u32[]{:S(2)}, u32[]{:S(2)}) collective-permute-start(f32[8,3,8,256]{3,2,1,0:T(8,128)S(1)} %collective-permute-done.1.refs_2_), channel_id=1, source_target_pairs={{0,8},{4,12},{8,0},{12,4},{16,24},{20,28},{24,16},{28,20},{1,9},{5... | collective-permute-start | bytes 589832 | tf_op jit(solution)/shard_map/ppermute | solution.py:587
  16.8 1.5 %collective-permute-start.5 = (f32[7,3,8,256]{3,2,1,0:T(8,128)S(1)}, f32[7,3,8,256]{3,2,1,0:T(8,128)S(1)}, u32[]{:S(2)}, u32[]{:S(2)}) collective-permute-start(f32[7,3,8,256]{3,2,1,0:T(8,128)S(1)} %collective-permute-done.2.refs_4_), channel_id=1, source_target_pairs={{0,4},{4,0},{8,12},{12,8},{16,20},{20,16},{24,28},{28,24},{1,5},{5... | collective-permute-start | bytes 516104 | tf_op jit(solution)/shard_map/ppermute | solution.py:587
  18.3 0.0 collective-permute-done.refs_1_
  18.3 0.0 copy-start
  18.3 1.0 %copy-done = f32[2,200,256]{2,1,0:T(8,128)S(1)} copy-done((f32[2,200,256]{2,1,0:T(8,128)S(1)}, f32[2,200,256]{2,1,0:T(8,128)}, u32[]{:S(2)}) %copy-start) | copy-done | bytes 409624
  19.3 2.1 %own_rows.1 = (f32[4,136,256]{2,1,0:T(8,128)S(1)}, s32[4,128]{1,0:T(4,128)S(1)}, bf16[4,256,256]{2,1,0:T(8,128)(2,1)S(1)}, bf16[4,256,256]{2,1,0:T(8,128)(2,1)S(1)}) custom-call(f32[2,200,256]{2,1,0:T(8,128)S(1)} %copy-done, f32[2,200,256]{2,1,0:T(8,128)S(1)} %collective-permute-done.refs_1_, f32[30,3,8,256]{3,2,1,0:T(8,128)S(1)} %get-tuple-element.46.refs_2_.refs_0_.refs_5_), custom_call_target="tpu_custom_call" | custom-call | flops 2000000000 | bytes 2000000 | tf_op jit(solution)/shard_map/own_rows/pallas_call | solution.py:196
  21.3 0.8 %collective-permute-done.5.refs_8_ = f32[7,3,8,256]{3,2,1,0:T(8,128)S(1)} collective-permute-done((f32[7,3,8,256]{3,2,1,0:T(8,128)S(1)}, f32[7,3,8,256]{3,2,1,0:T(8,128)S(1)}, u32[]{:S(2)}, u32[]{:S(2)}) %collective-permute-start.5) | collective-permute-done | bytes 172064 | tf_op jit(solution)/shard_map/ppermute | solution.py:587
  22.2 0.0 collective-permute-done.4.refs_6_
  22.2 2.8 %collective-permute-done.3.refs_4_.refs_2_ = f32[2,200,256]{2,1,0:T(8,128)S(1)} collective-permute-done((f32[2,200,256]{2,1,0:T(8,128)}, f32[2,200,256]{2,1,0:T(8,128)S(1)}, u32[]{:S(2)}, u32[]{:S(2)}) %collective-permute-start.3) | collective-permute-done | bytes 409632 | tf_op jit(solution)/shard_map/ppermute | solution.py:587
  25.0 0.0 collective-permute-start.6
  25.0 0.5 collective-permute-start.10
  25.5 0.0 collective-permute-start.8
  25.5 0.5 collective-permute-start.11
  26.0 0.0 collective-permute-done.7.refs_1_
  26.0 0.0 collective-permute-start.9
  26.0 1.5 %collective-permute-done.11.refs_9_ = f32[7,3,8,256]{3,2,1,0:T(8,128)S(1)} collective-permute-done((f32[7,3,8,256]{3,2,1,0:T(8,128)S(1)}, f32[7,3,8,256]{3,2,1,0:T(8,128)S(1)}, u32[]{:S(2)}, u32[]{:S(2)}) %collective-permute-start.11) | collective-permute-done | bytes 172064 | tf_op jit(solution)/shard_map/ppermute | solution.py:587
  27.5 0.2 collective-permute-done.9.refs_5_
  27.8 0.0 collective-permute-done.10.refs_7_
  27.8 0.0 collective-permute-done.8.refs_3_
  27.8 0.2 place.1.refs_6_
  28.0 0.0 copy-start.1
  28.0 0.0 collective-permute-done.6.refs_5_.refs_3_
  28.0 4.5 %accumulate.1 = (f32[24,8,256]{2,1,0:T(8,128)S(1)}, f32[24,8,256]{2,1,0:T(8,128)S(1)}, f32[24,8,256]{2,1,0:T(8,128)S(1)}, f32[24,8,256]{2,1,0:T(8,128)S(1)}, f32...) custom-call(f32[4,136,256]{2,1,0:T(8,128)S(1)} %get-tuple-element.56, ...), custom_call_target="tpu_custom_call" | custom-call | flops 8000000000 | bytes 8000000 | tf_op jit(solution)/shard_map/accumulate/pallas_call | solution.py:393
  32.5 1.6 %collective-permute-start.12 = (f32[24,8,256]{2,1,0:T(8,128)S(1)}, f32[24,8,256]{2,1,0:T(8,128)S(1)}, u32[]{:S(2)}, u32[]{:S(2)}) collective-permute-start(f32[24,8,256]{2,1,0:T(8,128)S(1)} %get-tuple-element.68), channel_id=1, source_target_pairs={{0,4},{4,0},{8,12},{12,8},{16,20},{20,16},{24,28},{28,24},{1,5},{5... | collective-permute-start | bytes 589832 | tf_op jit(solution)/shard_map/ppermute | solution.py:587
  34.0 1.6 %collective-permute-start.14 = (f32[6,8,256]{2,1,0:T(8,128)S(1)}, f32[6,8,256]{2,1,0:T(8,128)S(1)}, u32[]{:S(2)}, u32[]{:S(2)}) collective-permute-start(f32[6,8,256]{2,1,0:T(8,128)S(1)} %get-tuple-element.77), channel_id=1, source_target_pairs={{0,8},{4,12},{8,0},{12,4},{16,24},{20,28},{24,16},{28,20},{1,9},{5... | collective-permute-start | bytes 147464 | tf_op jit(solution)/shard_map/ppermute | solution.py:587
  35.6 2.6 %collective-permute-start.15 = (f32[6,8,256]{2,1,0:T(8,128)S(1)}, f32[6,8,256]{2,1,0:T(8,128)S(1)}, u32[]{:S(2)}, u32[]{:S(2)}) collective-permute-start(f32[6,8,256]{2,1,0:T(8,128)S(1)} %get-tuple-element.78), channel_id=1, source_target_pairs={{0,16},{4,20},{8,24},{12,28},{16,0},{20,4},{24,8},{28,12},{1,17},{... | collective-permute-start | bytes 147464 | tf_op jit(solution)/shard_map/ppermute | solution.py:587
  38.2 0.2 collective-permute-start.16
  38.4 0.0 copy-done.1
  38.4 1.3 %own_sums.1.refs_2_ = f32[2,8,256]{2,1,0:T(8,128)S(1)} custom-call(f32[2,200,256]{2,1,0:T(8,128)S(1)} %copy-done.1, f32[2,200,256]{2,1,0:T(8,128)S(1)} %collective-permute-done.refs_1_, f32[2,200,256]{2,1,0:T(8,128)S(1)} %collective-permute-done.3.refs_4_.refs_2_, f32[2,200,256]{2,1,0:T(8,128)S(1)} %collective-permute-done.6.refs_5_.refs_3_, ...), custom_call_target="tpu_custom_call" | custom-call | flops 100000000 | bytes 100000 | tf_op jit(solution)/shard_map/own_sums/pallas_call | solution.py:477
  39.8 0.6 %collective-permute-start.13 = (f32[2,8,256]{2,1,0:T(8,128)S(1)}, f32[2,8,256]{2,1,0:T(8,128)S(1)}, u32[]{:S(2)}, u32[]{:S(2)}) collective-permute-start(f32[2,8,256]{2,1,0:T(8,128)S(1)} %own_sums.1.refs_2_), channel_id=1, source_target_pairs={{0,4},{4,0},{8,12},{12,8},{16,20},{20,16},{24,28},{28,24},{1,5},{5... | collective-permute-start | bytes 49160 | tf_op jit(solution)/shard_map/ppermute | solution.py:587
  40.3 3.2 %collective-permute-done.13.refs_3_ = f32[2,8,256]{2,1,0:T(8,128)S(1)} collective-permute-done((f32[2,8,256]{2,1,0:T(8,128)S(1)}, f32[2,8,256]{2,1,0:T(8,128)S(1)}, u32[]{:S(2)}, u32[]{:S(2)}) %collective-permute-start.13) | collective-permute-done | bytes 16416 | tf_op jit(solution)/shard_map/ppermute | solution.py:587
  43.6 0.0 collective-permute-done.12.refs_1_
  43.6 0.0 collective-permute-done.14.refs_1_
  43.6 0.0 collective-permute-done.15.refs_2_
  43.6 0.5 collective-permute-done.16.refs_3_
  44.1 0.5 collective-permute-start.17
  44.6 1.3 %collective-permute-start.19 = (f32[14,8,256]{2,1,0:T(8,128)S(1)}, f32[14,8,256]{2,1,0:T(8,128)S(1)}, u32[]{:S(2)}, u32[]{:S(2)}) collective-permute-start(f32[14,8,256]{2,1,0:T(8,128)S(1)} %get-tuple-element.74), channel_id=1, source_target_pairs={{0,16},{4,20},{8,24},{12,28},{16,0},{20,4},{24,8},{28,12},{1,17},{... | collective-permute-start | bytes 344072 | tf_op jit(solution)/shard_map/ppermute | solution.py:587
  45.9 1.9 %collective-permute-start.20 = (f32[14,8,256]{2,1,0:T(8,128)S(1)}, f32[14,8,256]{2,1,0:T(8,128)S(1)}, u32[]{:S(2)}, u32[]{:S(2)}) collective-permute-start(f32[14,8,256]{2,1,0:T(8,128)S(1)} %get-tuple-element.75), channel_id=1, source_target_pairs={{0,24},{4,28},{8,16},{12,20},{16,8},{20,12},{24,0},{28,4},{1,25},{... | collective-permute-start | bytes 344072 | tf_op jit(solution)/shard_map/ppermute | solution.py:587
  47.8 2.0 %collective-permute-done.17.refs_1_ = f32[24,8,256]{2,1,0:T(8,128)S(1)} collective-permute-done((f32[24,8,256]{2,1,0:T(8,128)S(1)}, f32[24,8,256]{2,1,0:T(8,128)S(1)}, u32[]{:S(2)}, u32[]{:S(2)}) %collective-permute-start.17) | collective-permute-done | bytes 196640 | tf_op jit(solution)/shard_map/ppermute | solution.py:587
  49.8 0.3 collective-permute-start.18
  50.1 0.6 %collective-permute-start.21 = (f32[3,8,256]{2,1,0:T(8,128)S(1)}, f32[3,8,256]{2,1,0:T(8,128)S(1)}, u32[]{:S(2)}, u32[]{:S(2)}) collective-permute-start(f32[3,8,256]{2,1,0:T(8,128)S(1)} %get-tuple-element.85), channel_id=1, source_target_pairs={{0,4},{4,0},{8,12},{12,8},{16,20},{20,16},{24,28},{28,24},{1,5},{5... | collective-permute-start | bytes 73736 | tf_op jit(solution)/shard_map/ppermute | solution.py:587
  50.7 3.3 %collective-permute-done.21.refs_5_ = f32[3,8,256]{2,1,0:T(8,128)S(1)} collective-permute-done((f32[3,8,256]{2,1,0:T(8,128)S(1)}, f32[3,8,256]{2,1,0:T(8,128)S(1)}, u32[]{:S(2)}, u32[]{:S(2)}) %collective-permute-start.21) | collective-permute-done | bytes 24608 | tf_op jit(solution)/shard_map/ppermute | solution.py:587
  54.0 0.1 collective-permute-done.19.refs_2_
  54.1 0.0 collective-permute-done.20.refs_3_
  54.1 0.9 %collective-permute-done.18.refs_1_ = f32[14,8,256]{2,1,0:T(8,128)S(1)} collective-permute-done((f32[14,8,256]{2,1,0:T(8,128)S(1)}, f32[14,8,256]{2,1,0:T(8,128)S(1)}, u32[]{:S(2)}, u32[]{:S(2)}) %collective-permute-start.18) | collective-permute-done | bytes 114720 | tf_op jit(solution)/shard_map/ppermute | solution.py:587
  55.0 1.0 %finish.1 = (f32[240,120]{1,0:T(8,128)}, f32[1,240]{1,0:T(1,128)}, f32[8,8,30]{2,1,0:T(8,128)}) custom-call(f32[14,8,256]{2,1,0:T(8,128)S(1)} %get-tuple-element.82.refs_0_, f32[14,8,256]{2,1,0:T(8,128)S(1)} %collective-permute-done.18.refs_1_, f32[14,8,256]{2,1,0:T(8,128)S(1)} %collective-permute-done.19.refs_2_, ...), custom_call_target="tpu_custom_call" | custom-call | tf_op jit(solution)/shard_map/finish/pallas_call | solution.py:571
  (3 shorter events, 0.1 us)
Async XLA Ops:
  0.6 1.1 %copy-start.2 = (f32[30,3,8,256]{3,2,1,0:T(8,128)S(1)}, f32[30,3,8,256]{3,2,1,0:T(8,128)}, u32[]{:S(2)}) copy-start(f32[30,3,8,256]{3,2,1,0:T(8,128)} %orbit.1) | copy-start | bytes 2211844
  1.8 11.9 %collective-permute-start.1 = (f32[8,3,8,256]{3,2,1,0:T(8,128)S(1)}, f32[8,3,8,256]{3,2,1,0:T(8,128)S(1)}, u32[]{:S(2)}, u32[]{:S(2)}) collective-permute-start(f32[8,3,8,256]{3,2,1,0:T(8,128)S(1)} %get-tuple-element.51), channel_id=1, source_target_pairs={{0,2},{1,3},{2,0},{3,1},{4,6},{5,7},{6,4},{7,5},{8,10},{9,11},{10,... | collective-permute-start | bytes 589832 | tf_op jit(solution)/shard_map/ppermute | solution.py:587
  6.8 11.4 %collective-permute-start = (f32[2,200,256]{2,1,0:T(8,128)}, f32[2,200,256]{2,1,0:T(8,128)S(1)}, u32[]{:S(2)}, u32[]{:S(2)}) collective-permute-start(f32[2,200,256]{2,1,0:T(8,128)} %prepare.1.refs_0_), channel_id=1, source_target_pairs={{0,1},{1,0},{2,3},{3,2},{4,5},{5,4},{6,7},{7,6},{8,9},{9,8},{10,11... | collective-permute-start | bytes 1228808 | tf_op jit(solution)/shard_map/ppermute | solution.py:587
  6.9 6.8 %collective-permute-start.2 = (f32[7,3,8,256]{3,2,1,0:T(8,128)S(1)}, f32[7,3,8,256]{3,2,1,0:T(8,128)S(1)}, u32[]{:S(2)}, u32[]{:S(2)}) collective-permute-start(f32[7,3,8,256]{3,2,1,0:T(8,128)S(1)} %get-tuple-element.52), channel_id=1, source_target_pairs={{0,2},{1,3},{2,0},{3,1},{4,6},{5,7},{6,4},{7,5},{8,10},{9,11},{10,... | collective-permute-start | bytes 516104 | tf_op jit(solution)/shard_map/ppermute | solution.py:587
  7.0 19.0 %collective-permute-start.7 = (f32[30,3,8,256]{3,2,1,0:T(8,128)S(1)}, f32[30,3,8,256]{3,2,1,0:T(8,128)S(1)}, u32[]{:S(2)}, u32[]{:S(2)}) collective-permute-start(f32[30,3,8,256]{3,2,1,0:T(8,128)S(1)} %get-tuple-element.46.refs_2_.refs_0_.refs_5_), channel_id=1, source_target_pairs={{0,1},{1,0},{2,3},{3,2},{4,5},{5,4},{6,7},{7,6},{8,9},{9,8},{10,11... | collective-permute-start | bytes 2211848 | tf_op jit(solution)/shard_map/ppermute | solution.py:587
  13.7 11.2 %collective-permute-start.3 = (f32[2,200,256]{2,1,0:T(8,128)}, f32[2,200,256]{2,1,0:T(8,128)S(1)}, u32[]{:S(2)}, u32[]{:S(2)}) collective-permute-start(f32[2,200,256]{2,1,0:T(8,128)} %prepare.1.refs_0_), channel_id=1, source_target_pairs={{0,2},{1,3},{2,0},{3,1},{4,6},{5,7},{6,4},{7,5},{8,10},{9,11},{10,... | collective-permute-start | bytes 1228808 | tf_op jit(solution)/shard_map/ppermute | solution.py:587
  15.2 7.0 %collective-permute-start.4 = (f32[8,3,8,256]{3,2,1,0:T(8,128)S(1)}, f32[8,3,8,256]{3,2,1,0:T(8,128)S(1)}, u32[]{:S(2)}, u32[]{:S(2)}) collective-permute-start(f32[8,3,8,256]{3,2,1,0:T(8,128)S(1)} %collective-permute-done.1.refs_2_), channel_id=1, source_target_pairs={{0,8},{4,12},{8,0},{12,4},{16,24},{20,28},{24,16},{28,20},{1,9},{5... | collective-permute-start | bytes 589832 | tf_op jit(solution)/shard_map/ppermute | solution.py:587
  16.8 5.4 %collective-permute-start.5 = (f32[7,3,8,256]{3,2,1,0:T(8,128)S(1)}, f32[7,3,8,256]{3,2,1,0:T(8,128)S(1)}, u32[]{:S(2)}, u32[]{:S(2)}) collective-permute-start(f32[7,3,8,256]{3,2,1,0:T(8,128)S(1)} %collective-permute-done.2.refs_4_), channel_id=1, source_target_pairs={{0,4},{4,0},{8,12},{12,8},{16,20},{20,16},{24,28},{28,24},{1,5},{5... | collective-permute-start | bytes 516104 | tf_op jit(solution)/shard_map/ppermute | solution.py:587
  18.3 1.0 %copy-start = (f32[2,200,256]{2,1,0:T(8,128)S(1)}, f32[2,200,256]{2,1,0:T(8,128)}, u32[]{:S(2)}) copy-start(f32[2,200,256]{2,1,0:T(8,128)} %prepare.1.refs_0_) | copy-start | bytes 1228804
  25.0 3.0 %collective-permute-start.6 = (f32[2,200,256]{2,1,0:T(8,128)S(1)}, f32[2,200,256]{2,1,0:T(8,128)S(1)}, u32[]{:S(2)}, u32[]{:S(2)}) collective-permute-start(f32[2,200,256]{2,1,0:T(8,128)S(1)} %collective-permute-done.3.refs_4_.refs_2_), channel_id=1, source_target_pairs={{0,1},{1,0},{2,3},{3,2},{4,5},{5,4},{6,7},{7,6},{8,9},{9,8},{10,11... | collective-permute-start | bytes 1228808 | tf_op jit(solution)/shard_map/ppermute | solution.py:587
  25.0 2.8 %collective-permute-start.10 = (f32[8,3,8,256]{3,2,1,0:T(8,128)S(1)}, f32[8,3,8,256]{3,2,1,0:T(8,128)S(1)}, u32[]{:S(2)}, u32[]{:S(2)}) collective-permute-start(f32[8,3,8,256]{3,2,1,0:T(8,128)S(1)} %collective-permute-done.4.refs_6_), channel_id=1, source_target_pairs={{0,1},{1,0},{2,3},{3,2},{4,5},{5,4},{6,7},{7,6},{8,9},{9,8},{10,11... | collective-permute-start | bytes 589832 | tf_op jit(solution)/shard_map/ppermute | solution.py:587
  25.5 2.3 %collective-permute-start.8 = (f32[8,3,8,256]{3,2,1,0:T(8,128)S(1)}, f32[8,3,8,256]{3,2,1,0:T(8,128)S(1)}, u32[]{:S(2)}, u32[]{:S(2)}) collective-permute-start(f32[8,3,8,256]{3,2,1,0:T(8,128)S(1)} %collective-permute-done.1.refs_2_), channel_id=1, source_target_pairs={{0,1},{1,0},{2,3},{3,2},{4,5},{5,4},{6,7},{7,6},{8,9},{9,8},{10,11... | collective-permute-start | bytes 589832 | tf_op jit(solution)/shard_map/ppermute | solution.py:587
  25.5 2.0 %collective-permute-start.11 = (f32[7,3,8,256]{3,2,1,0:T(8,128)S(1)}, f32[7,3,8,256]{3,2,1,0:T(8,128)S(1)}, u32[]{:S(2)}, u32[]{:S(2)}) collective-permute-start(f32[7,3,8,256]{3,2,1,0:T(8,128)S(1)} %collective-permute-done.5.refs_8_), channel_id=1, source_target_pairs={{0,1},{1,0},{2,3},{3,2},{4,5},{5,4},{6,7},{7,6},{8,9},{9,8},{10,11... | collective-permute-start | bytes 516104 | tf_op jit(solution)/shard_map/ppermute | solution.py:587
  26.0 1.8 %collective-permute-start.9 = (f32[7,3,8,256]{3,2,1,0:T(8,128)S(1)}, f32[7,3,8,256]{3,2,1,0:T(8,128)S(1)}, u32[]{:S(2)}, u32[]{:S(2)}) collective-permute-start(f32[7,3,8,256]{3,2,1,0:T(8,128)S(1)} %collective-permute-done.2.refs_4_), channel_id=1, source_target_pairs={{0,1},{1,0},{2,3},{3,2},{4,5},{5,4},{6,7},{7,6},{8,9},{9,8},{10,11... | collective-permute-start | bytes 516104 | tf_op jit(solution)/shard_map/ppermute | solution.py:587
  28.0 10.5 %copy-start.1 = (f32[2,200,256]{2,1,0:T(8,128)S(1)}, f32[2,200,256]{2,1,0:T(8,128)}, u32[]{:S(2)}) copy-start(f32[2,200,256]{2,1,0:T(8,128)} %prepare.1.refs_0_) | copy-start | bytes 1228804
  32.5 11.1 %collective-permute-start.12 = (f32[24,8,256]{2,1,0:T(8,128)S(1)}, f32[24,8,256]{2,1,0:T(8,128)S(1)}, u32[]{:S(2)}, u32[]{:S(2)}) collective-permute-start(f32[24,8,256]{2,1,0:T(8,128)S(1)} %get-tuple-element.68), channel_id=1, source_target_pairs={{0,4},{4,0},{8,12},{12,8},{16,20},{20,16},{24,28},{28,24},{1,5},{5... | collective-permute-start | bytes 589832 | tf_op jit(solution)/shard_map/ppermute | solution.py:587
  34.0 9.5 %collective-permute-start.14 = (f32[6,8,256]{2,1,0:T(8,128)S(1)}, f32[6,8,256]{2,1,0:T(8,128)S(1)}, u32[]{:S(2)}, u32[]{:S(2)}) collective-permute-start(f32[6,8,256]{2,1,0:T(8,128)S(1)} %get-tuple-element.77), channel_id=1, source_target_pairs={{0,8},{4,12},{8,0},{12,4},{16,24},{20,28},{24,16},{28,20},{1,9},{5... | collective-permute-start | bytes 147464 | tf_op jit(solution)/shard_map/ppermute | solution.py:587
  35.6 8.0 %collective-permute-start.15 = (f32[6,8,256]{2,1,0:T(8,128)S(1)}, f32[6,8,256]{2,1,0:T(8,128)S(1)}, u32[]{:S(2)}, u32[]{:S(2)}) collective-permute-start(f32[6,8,256]{2,1,0:T(8,128)S(1)} %get-tuple-element.78), channel_id=1, source_target_pairs={{0,16},{4,20},{8,24},{12,28},{16,0},{20,4},{24,8},{28,12},{1,17},{... | collective-permute-start | bytes 147464 | tf_op jit(solution)/shard_map/ppermute | solution.py:587
  38.2 5.9 %collective-permute-start.16 = (f32[6,8,256]{2,1,0:T(8,128)S(1)}, f32[6,8,256]{2,1,0:T(8,128)S(1)}, u32[]{:S(2)}, u32[]{:S(2)}) collective-permute-start(f32[6,8,256]{2,1,0:T(8,128)S(1)} %get-tuple-element.79), channel_id=1, source_target_pairs={{0,24},{4,28},{8,16},{12,20},{16,8},{20,12},{24,0},{28,4},{1,25},{... | collective-permute-start | bytes 147464 | tf_op jit(solution)/shard_map/ppermute | solution.py:587
  39.8 3.8 %collective-permute-start.13 = (f32[2,8,256]{2,1,0:T(8,128)S(1)}, f32[2,8,256]{2,1,0:T(8,128)S(1)}, u32[]{:S(2)}, u32[]{:S(2)}) collective-permute-start(f32[2,8,256]{2,1,0:T(8,128)S(1)} %own_sums.1.refs_2_), channel_id=1, source_target_pairs={{0,4},{4,0},{8,12},{12,8},{16,20},{20,16},{24,28},{28,24},{1,5},{5... | collective-permute-start | bytes 49160 | tf_op jit(solution)/shard_map/ppermute | solution.py:587
  44.1 5.7 %collective-permute-start.17 = (f32[24,8,256]{2,1,0:T(8,128)S(1)}, f32[24,8,256]{2,1,0:T(8,128)S(1)}, u32[]{:S(2)}, u32[]{:S(2)}) collective-permute-start(f32[24,8,256]{2,1,0:T(8,128)S(1)} %get-tuple-element.81), channel_id=1, source_target_pairs={{0,4},{4,0},{8,12},{12,8},{16,20},{20,16},{24,28},{28,24},{1,5},{5... | collective-permute-start | bytes 589832 | tf_op jit(solution)/shard_map/ppermute | solution.py:587
  44.6 9.5 %collective-permute-start.19 = (f32[14,8,256]{2,1,0:T(8,128)S(1)}, f32[14,8,256]{2,1,0:T(8,128)S(1)}, u32[]{:S(2)}, u32[]{:S(2)}) collective-permute-start(f32[14,8,256]{2,1,0:T(8,128)S(1)} %get-tuple-element.74), channel_id=1, source_target_pairs={{0,16},{4,20},{8,24},{12,28},{16,0},{20,4},{24,8},{28,12},{1,17},{... | collective-permute-start | bytes 344072 | tf_op jit(solution)/shard_map/ppermute | solution.py:587
  45.9 8.2 %collective-permute-start.20 = (f32[14,8,256]{2,1,0:T(8,128)S(1)}, f32[14,8,256]{2,1,0:T(8,128)S(1)}, u32[]{:S(2)}, u32[]{:S(2)}) collective-permute-start(f32[14,8,256]{2,1,0:T(8,128)S(1)} %get-tuple-element.75), channel_id=1, source_target_pairs={{0,24},{4,28},{8,16},{12,20},{16,8},{20,12},{24,0},{28,4},{1,25},{... | collective-permute-start | bytes 344072 | tf_op jit(solution)/shard_map/ppermute | solution.py:587
  49.8 5.2 %collective-permute-start.18 = (f32[14,8,256]{2,1,0:T(8,128)S(1)}, f32[14,8,256]{2,1,0:T(8,128)S(1)}, u32[]{:S(2)}, u32[]{:S(2)}) collective-permute-start(f32[14,8,256]{2,1,0:T(8,128)S(1)} %get-tuple-element.83), channel_id=1, source_target_pairs={{0,8},{4,12},{8,0},{12,4},{16,24},{20,28},{24,16},{28,20},{1,9},{5... | collective-permute-start | bytes 344072 | tf_op jit(solution)/shard_map/ppermute | solution.py:587
  50.1 3.9 %collective-permute-start.21 = (f32[3,8,256]{2,1,0:T(8,128)S(1)}, f32[3,8,256]{2,1,0:T(8,128)S(1)}, u32[]{:S(2)}, u32[]{:S(2)}) collective-permute-start(f32[3,8,256]{2,1,0:T(8,128)S(1)} %get-tuple-element.85), channel_id=1, source_target_pairs={{0,4},{4,0},{8,12},{12,8},{16,20},{20,16},{24,28},{28,24},{1,5},{5... | collective-permute-start | bytes 73736 | tf_op jit(solution)/shard_map/ppermute | solution.py:587

commit v15 on v14

--- a/solution.py
+++ b/solution.py
@@ -31,8 +31,8 @@
 
 def prepare_kernel(*refs):
     arguments = refs[:6]
-    planes = refs[6]
-    copied, sems = refs[7:13], refs[13]
+    planes, extra = refs[6:8]
+    copied, sems = refs[8:14], refs[14]
     copies = [pltpu.make_async_copy(arguments[n], copied[n], sems.at[n]) for n in range(6)]
     for copy in copies:
         copy.start()
@@ -71,8 +71,8 @@
         planes[s, 4 * tracked + 1 : 4 * tracked + 2, :tracked] = track[s : s + 1, :].astype(
             jnp.float32
         )
-        planes[s, 4 * tracked + 8 : 5 * tracked + 8, :] = res_off * root - tropo * right
-        planes[s, 5 * tracked + 8 :, :] = jnp.where(
+        extra[s, :tracked, :] = res_off * root - tropo * right
+        extra[s, tracked:, :] = jnp.where(
             weight > 0.0, total / jnp.maximum(weight, 1.0), 0.0
         )
 
@@ -81,9 +81,12 @@
     stations, _, tracked, epochs = arguments[0].shape
     return pl.pallas_call(
         prepare_kernel,
-        out_shape=jax.ShapeDtypeStruct((stations, 6 * tracked + 8, epochs), jnp.float32),
+        out_shape=[
+            jax.ShapeDtypeStruct((stations, rows, epochs), jnp.float32)
+            for rows in (4 * tracked + 8, 2 * tracked)
+        ],
         in_specs=[hbm()] * 6,
-        out_specs=vmem(),
+        out_specs=[vmem()] * 2,
         scratch_shapes=[pltpu.VMEM(a.shape, a.dtype) for a in arguments]
         + [pltpu.SemaphoreType.DMA((6,))],
         compiler_params=pltpu.CompilerParams(vmem_limit_bytes=HUGE_LIMIT),
@@ -368,7 +371,12 @@
     acc[...] = acc[...] - outer.reshape(sats, 8, width)
 
     columns = sats * 8 // (nx * nz)
-    own_out[...] = acc[pl.ds(first, own)]
+    owner = lax.broadcasted_iota(jnp.int32, (8, width), 1) // 8
+    folded = jnp.zeros((8, width), jnp.float32)
+    for o in range(own):
+        folded = folded + jnp.where(owner == o, acc[first + o], 0.0)
+    own_out[0] = folded
+    own_out[1] = jnp.zeros_like(folded)
     half = nz // 2
     for dx in range(nx):
         for dz in range(nz):
@@ -392,7 +400,7 @@
     outs += [jax.ShapeDtypeStruct((nx * last, 8, width), jnp.float32)] * nz
     return pl.pallas_call(
         functools.partial(main_kernel, len(raw), own, nx, nz, window),
-        out_shape=outs + [jax.ShapeDtypeStruct((own, 8, width), jnp.float32)],
+        out_shape=outs + [jax.ShapeDtypeStruct((2, 8, width), jnp.float32)],
         in_specs=[vmem(), pl.BlockSpec(memory_space=pltpu.SMEM), vmem(), vmem()]
         + [vmem()] * (len(raw) + 1),
         out_specs=[vmem()] * (len(outs) + 1),
@@ -416,37 +424,40 @@
 
 
 def blocks_kernel(groups, per, *refs):
-    plane_pieces = refs[:groups]
-    own_rows, orbit, small = refs[groups:]
-    tracked = (plane_pieces[0].shape[1] - 8) // 6
-    epochs = orbit.shape[3]
-    width = small.shape[2]
-    own = orbit.shape[0]
-    first = lax.axis_index("sat") * own
-    satellite = first + lax.broadcasted_iota(jnp.int32, (own, tracked), 0)
+    plane_pieces, extra_pieces = refs[:2], refs[2:4]
+    orbit = refs[4]
+    smalls = refs[5:]
+    tracked = extra_pieces[0].shape[1] // 2
+    own = orbit.shape[0] // groups
     pairs = [(0, 0), (0, 1), (0, 2), (1, 1), (1, 2), (2, 2)]
-    picks, stacks = [], [[] for _ in range(9)]
-    for d in range(groups):
+    index = {}
+    for n, (c, e) in enumerate(pairs):
+        index[c, e] = index[e, c] = n
+    tracks, stacks = [], [[] for _ in range(9)]
+    for planes, extra in zip(plane_pieces, extra_pieces):
         for s in range(per):
-            station = plane_pieces[d][s]
-            named = station[4 * tracked + 1 : 4 * tracked + 2, :tracked]
-            picks.append((satellite == named.astype(jnp.int32)).astype(jnp.float32))
-            a = [station[c * tracked : (c + 1) * tracked, :] for c in range(3)]
-            residual = station[4 * tracked + 8 : 5 * tracked + 8, :]
-            inverse = station[5 * tracked + 8 :, :]
+            tracks.append(planes[s, 4 * tracked + 1 : 4 * tracked + 2, :tracked])
+            a = [planes[s, c * tracked : (c + 1) * tracked, :] for c in range(3)]
+            residual, inverse = extra[s, :tracked, :], extra[s, tracked:, :]
             weighted = [v * inverse for v in a]
             terms = [weighted[c] * a[e] for c, e in pairs] + [v * residual for v in a]
             for stack, term in zip(stacks, terms):
                 stack.append(term)
-    pick = jnp.concatenate(picks, 1).astype(jnp.bfloat16)
+    named = jnp.concatenate(tracks, 1).astype(jnp.int32)
+    stacks = [split(jnp.concatenate(stack, 0)) for stack in stacks]
+    for n, small in enumerate(smalls):
+        first = (lax.axis_index("sat") ^ (2 * n)) * own
+        sum_blocks(own, first, named, stacks, index, orbit[pl.ds(first, own)], small)
+
+
+def sum_blocks(own, first, named, stacks, index, orbit, small):
+    epochs = orbit.shape[3]
+    satellite = first + lax.broadcasted_iota(jnp.int32, (own, named.shape[1]), 0)
+    pick = (satellite == named).astype(jnp.float32).astype(jnp.bfloat16)
     sums = []
-    for stack in stacks:
-        high, low = split(jnp.concatenate(stack, 0))
+    for high, low in stacks:
         sums.append(jnp.dot(pick, high, preferred_element_type=jnp.float32)
                     + jnp.dot(pick, low, preferred_element_type=jnp.float32))
-    index = {}
-    for n, (c, e) in enumerate(pairs):
-        index[c, e] = index[e, c] = n
 
     def spread(value):
         return jnp.broadcast_to(value[:, None, :], (own, 8, epochs))
@@ -463,27 +474,25 @@
     owner = lax.broadcasted_iota(jnp.int32, (8, own * 8), 1) // 8
     folded = jnp.zeros((8, own * 8), jnp.float32)
     for o in range(own):
-        tile = own_rows[o, :, : own * 8] + blocks[o * 8 : o * 8 + 8, :]
-        folded = folded + jnp.where(owner == o, tile, 0.0)
+        folded = folded + jnp.where(owner == o, blocks[o * 8 : o * 8 + 8, :], 0.0)
     small[...] = jnp.zeros_like(small)
     small[0, :, : own * 8] = folded
     small[1, :, : own * 8] = right
 
 
-def own_sums(planes, own_rows, orbit):
-    groups = len(planes)
+def own_sums(planes, extras, orbit, groups, width):
     per = planes[0].shape[0]
-    width = own_rows.shape[2]
+    count = groups // 2
     return pl.pallas_call(
         functools.partial(blocks_kernel, groups, per),
-        out_shape=jax.ShapeDtypeStruct((2, 8, width), jnp.float32),
-        in_specs=[vmem()] * (groups + 2),
-        out_specs=vmem(),
+        out_shape=[jax.ShapeDtypeStruct((2, 8, width), jnp.float32)] * count,
+        in_specs=[vmem()] * 5,
+        out_specs=[vmem()] * count,
         compiler_params=pltpu.CompilerParams(vmem_limit_bytes=MEDIUM_LIMIT),
         cost_estimate=pl.CostEstimate(
             flops=1 * 10**8, bytes_accessed=1 * 10**5, transcendentals=0),
         name="own_sums",
-    )(*planes, own_rows, orbit)
+    )(*planes, *extras, orbit)
 
 
 def combine_kernel(pieces_count, smalls_count, window, *refs):
@@ -614,17 +623,17 @@
     if own % 2 == 0 and nz % 2 == 0 and nx % 2 == 0:
         parts, orbit = cut_parts(orbit, nx)
     near = {d: [shift(part, "sat", group, d) for part in parts] for d in range(2, group, 2)}
-    planes = prepare(sight, mapping, residual, counts, track, knots)
+    planes, extra = prepare(sight, mapping, residual, counts, track, knots)
     own_planes = planes
-    other_planes, other_orbit = core(planes), core(orbit)
+    other_planes, other_orbit, other_extra = core(planes), core(orbit), core(extra)
     planes, near = lax.optimization_barrier((planes, near))
     arrived = {d: shift(planes, "sat", group, d) for d in near}
     far = {}
     if len(parts) == 2:
         far = {d: [across(near[d][0], nx), across(near[d][1], 1)] for d in near}
     ready = own_rows_of([own_planes, other_planes], 4 * tracked + 8, orbit, width, 0)
-    ready, arrived, held_near, far = lax.optimization_barrier(
-        (tuple(ready), arrived, near, far))
+    ready, arrived, held_near, far, other_extra = lax.optimization_barrier(
+        (tuple(ready), arrived, near, far, other_extra))
     partials = [(0, 0, 0, orbit), (1, 0, 0, other_orbit)]
     for d in near:
         for turn, values in ((0, held_near[d]), (1, far.get(d, []))):
@@ -635,7 +644,11 @@
     every = place([part[3] for part in partials], places, sats, own, nx)
     for d, value in arrived.items():
         pieces[d], pieces[d + 1] = value, core(value)
-    *sums, own_rows = accumulate(
+    smalls = own_sums([own_planes, other_planes], [extra, other_extra], every, group, width)
+    every, smalls = lax.optimization_barrier((every, smalls))
+    smalls = [smalls[0]] + [shift(value, "sat", group, 2 * n + 2)
+                            for n, value in enumerate(smalls[1:])]
+    *sums, folded = accumulate(
         ready, [pieces[d] for d in range(2, group)], every, own, nx, nz, window)
 
     half = nz // 2
@@ -646,7 +659,7 @@
     lasts = sum_over_z(turned, nx)
     lasts = [lasts[0]] + [across(lasts[dx], dx) for dx in range(1, nx)]
     far_sums = [sums[0]] + [across(sums[2 * dx], dx) for dx in range(1, nx)]
-    small = own_sums([pieces[d] for d in range(group)], own_rows, orbit)
+    small, = sum_over_z(smalls + [folded], 1)
     smalls = [small] + [across(small, dx) for dx in range(1, nx)]
     far_sums, smalls = lax.optimization_barrier((far_sums, smalls))
     chunks = list(combine(far_sums, smalls, size))

time: 56.2 us -> 58.9 us (1.048)
  waiting for transfers between devices: 21.7 us -> 23.8 us
  Pallas kernels: 11.1 us -> 11.9 us
    ppermute x22 -> x24, waiting for transfers between devices: 21.7 us -> 23.8 us  [shift(): return lax.ppermute(value, axis, [(i, i ^ step) for i in range(size)])]
    pallas_call x2, Pallas kernels: 3.29 us -> 3.98 us  [the longest x1 2.03 us: own_sums(): pl.pallas_call(functools.partial(blocks_kernel, groups, per), out_shape=[...]
    ppermute x22 -> x24, starting transfers between devices: 20.3 us -> 20.2 us  [shift(): return lax.ppermute(value, axis, [(i, i ^ step) for i in range(size)])]
  transfers between devices with their start and end apart: 22 -> 24, of which waited for: 11 -> 9; matrix products, arithmetic and copies ran while one was open for 0% -> 0% of each run, Pallas kernels for 10% -> 11%
where the time goes in v15:
time: 58.9 us; the launch traced here: 58.7 us
  waiting for transfers between devices  23.8 us (40%)
  starting transfers between devices  20.2 us (34%)
  Pallas kernels  11.9 us (20%)
  local copies, waits for them, and re-layouts  2.07 us (4%)
  between operations  0.77 us (1%)
    ppermute x24, waiting for transfers between devices, shift(): return lax.ppermute(value, axis, [(i, i ^ step) for i in range(size)])  23.8 us
    ppermute x24, starting transfers between devices, shift(): return lax.ppermute(value, axis, [(i, i ^ step) for i in range(size)])  20.2 us
    pallas_call x1, Pallas kernels, accumulate(): pl.pallas_call(functools.partial(main_kernel, len(raw), own, nx, nz, wind...  4.49 us
    unnamed x6, local copies, waits for them, and re-layouts  2.07 us
    pallas_call x1, Pallas kernels, own_rows_of(): pl.pallas_call(functools.partial(own_rows_kernel, groups, per, own, width...  2.07 us
    pallas_call x1, Pallas kernels, own_sums(): pl.pallas_call(functools.partial(blocks_kernel, groups, per), out_shape=[...  2.03 us
    pallas_call x1, Pallas kernels, prepare(): pl.pallas_call(prepare_kernel, out_shape=[jax.ShapeDtypeStruct((stations,...  1.96 us
  transfers between devices with their start and end apart: 24, of which 9 were waited for; matrix products, arithmetic and copies ran while one was open for 0% of the time, Pallas kernels for 11%

profile of v15, /device:TPU:0, one launch (start us, length us, event | category | flops | bytes accessed | tf_op | source)
XLA Modules:
  0.0 58.7 jit_solution(6766923394425674576)
XLA Ops:
  0.6 0.0 copy-start
  0.6 1.1 %copy-done = f32[30,3,8,256]{3,2,1,0:T(8,128)S(1)} copy-done((f32[30,3,8,256]{3,2,1,0:T(8,128)S(1)}, f32[30,3,8,256]{3,2,1,0:T(8,128)}, u32[]{:S(2)}) %copy-start) | copy-done | bytes 737304
  1.7 0.1 cut_parts.1
  1.8 3.0 %collective-permute-start.1 = (f32[8,3,8,256]{3,2,1,0:T(8,128)S(1)}, f32[8,3,8,256]{3,2,1,0:T(8,128)S(1)}, u32[]{:S(2)}, u32[]{:S(2)}) collective-permute-start(f32[8,3,8,256]{3,2,1,0:T(8,128)S(1)} %get-tuple-element.60), channel_id=1, source_target_pairs={{0,2},{1,3},{2,0},{3,1},{4,6},{5,7},{6,4},{7,5},{8,10},{9,11},{10,... | collective-permute-start | bytes 589832 | tf_op jit(solution)/shard_map/ppermute | solution.py:596
  4.9 2.0 %prepare.1 = (f32[2,136,256]{2,1,0:T(8,128)}, f32[2,64,256]{2,1,0:T(8,128)}) custom-call(f32[2,3,32,256]{3,2,1,0:T(8,128)} %refs_0_.1, f32[2,32,256]{2,1,0:T(8,128)} %refs_1_.1, f32[2,32,256]{2,1,0:T(8,128)} %refs_2_.1, s32[2,32,256]{2,1,0:T(8,128)} %refs_3_.1, s32[2,32]{1,0:T(2,128)} %refs_4_.1, s32[2,256]{1,0:T(2,128)} %refs_5_.1), custom_call_target="tpu_custom_call" | custom-call | tf_op jit(solution)/shard_map/prepare/pallas_call | solution.py:82
  6.8 0.1 collective-permute-start
  6.9 0.1 collective-permute-start.2
  7.0 0.4 collective-permute-start.8
  7.4 6.3 %collective-permute-done.2.refs_4_ = f32[7,3,8,256]{3,2,1,0:T(8,128)S(1)} collective-permute-done((f32[7,3,8,256]{3,2,1,0:T(8,128)S(1)}, f32[7,3,8,256]{3,2,1,0:T(8,128)S(1)}, u32[]{:S(2)}, u32[]{:S(2)}) %collective-permute-start.2) | collective-permute-done | bytes 172064 | tf_op jit(solution)/shard_map/ppermute | solution.py:596
  13.7 0.0 collective-permute-done.1.refs_2_
  13.7 1.5 %collective-permute-start.3 = (f32[2,136,256]{2,1,0:T(8,128)}, f32[2,136,256]{2,1,0:T(8,128)S(1)}, u32[]{:S(2)}, u32[]{:S(2)}) collective-permute-start(f32[2,136,256]{2,1,0:T(8,128)} %get-tuple-element.62.refs_0_), channel_id=1, source_target_pairs={{0,2},{1,3},{2,0},{3,1},{4,6},{5,7},{6,4},{7,5},{8,10},{9,11},{10,... | collective-permute-start | bytes 835592 | tf_op jit(solution)/shard_map/ppermute | solution.py:596
  15.2 1.6 %collective-permute-start.4 = (f32[8,3,8,256]{3,2,1,0:T(8,128)S(1)}, f32[8,3,8,256]{3,2,1,0:T(8,128)S(1)}, u32[]{:S(2)}, u32[]{:S(2)}) collective-permute-start(f32[8,3,8,256]{3,2,1,0:T(8,128)S(1)} %collective-permute-done.1.refs_2_), channel_id=1, source_target_pairs={{0,8},{4,12},{8,0},{12,4},{16,24},{20,28},{24,16},{28,20},{1,9},{5... | collective-permute-start | bytes 589832 | tf_op jit(solution)/shard_map/ppermute | solution.py:596
  16.8 0.0 collective-permute-start.6
  16.8 0.0 collective-permute-done.refs_1_
  16.8 1.5 %collective-permute-start.5 = (f32[7,3,8,256]{3,2,1,0:T(8,128)S(1)}, f32[7,3,8,256]{3,2,1,0:T(8,128)S(1)}, u32[]{:S(2)}, u32[]{:S(2)}) collective-permute-start(f32[7,3,8,256]{3,2,1,0:T(8,128)S(1)} %collective-permute-done.2.refs_4_), channel_id=1, source_target_pairs={{0,4},{4,0},{8,12},{12,8},{16,20},{20,16},{24,28},{28,24},{1,5},{5... | collective-permute-start | bytes 516104 | tf_op jit(solution)/shard_map/ppermute | solution.py:596
  18.3 0.0 copy-start.1
  18.3 1.0 %copy-done.1 = f32[2,136,256]{2,1,0:T(8,128)S(1)} copy-done((f32[2,136,256]{2,1,0:T(8,128)S(1)}, f32[2,136,256]{2,1,0:T(8,128)}, u32[]{:S(2)}) %copy-start.1) | copy-done | bytes 278552
  19.2 2.1 %own_rows.1 = (f32[4,136,256]{2,1,0:T(8,128)S(1)}, s32[4,128]{1,0:T(4,128)S(1)}, bf16[4,256,256]{2,1,0:T(8,128)(2,1)S(1)}, bf16[4,256,256]{2,1,0:T(8,128)(2,1)S(1)}) custom-call(f32[2,136,256]{2,1,0:T(8,128)S(1)} %copy-done.1, f32[2,136,256]{2,1,0:T(8,128)S(1)} %collective-permute-done.refs_1_, f32[30,3,8,256]{3,2,1,0:T(8,128)S(1)} %get-tuple-element.55.refs_2_.refs_0_), custom_call_target="tpu_custom_call" | custom-call | flops 2000000000 | bytes 2000000 | tf_op jit(solution)/shard_map/own_rows/pallas_call | solution.py:199
  21.3 0.0 collective-permute-done.6.refs_3_
  21.3 2.3 %collective-permute-done.5.refs_8_ = f32[7,3,8,256]{3,2,1,0:T(8,128)S(1)} collective-permute-done((f32[7,3,8,256]{3,2,1,0:T(8,128)S(1)}, f32[7,3,8,256]{3,2,1,0:T(8,128)S(1)}, u32[]{:S(2)}, u32[]{:S(2)}) %collective-permute-start.5) | collective-permute-done | bytes 172064 | tf_op jit(solution)/shard_map/ppermute | solution.py:596
  23.6 0.0 collective-permute-done.4.refs_6_
  23.6 0.0 collective-permute-done.3.refs_4_
  23.6 0.0 copy-start.2
  23.6 0.1 collective-permute-start.10
  23.6 0.5 collective-permute-start.7
  24.1 0.1 collective-permute-start.9
  24.2 0.4 collective-permute-start.11
  24.7 0.4 collective-permute-done.10.refs_5_
  25.0 0.1 collective-permute-start.12
  25.2 1.3 %collective-permute-done.12.refs_9_ = f32[7,3,8,256]{3,2,1,0:T(8,128)S(1)} collective-permute-done((f32[7,3,8,256]{3,2,1,0:T(8,128)S(1)}, f32[7,3,8,256]{3,2,1,0:T(8,128)S(1)}, u32[]{:S(2)}, u32[]{:S(2)}) %collective-permute-start.12) | collective-permute-done | bytes 172064 | tf_op jit(solution)/shard_map/ppermute | solution.py:596
  26.5 0.0 collective-permute-done.9.refs_3_
  26.5 0.0 collective-permute-done.11.refs_7_
  26.5 0.0 collective-permute-done.8.refs_1_
  26.5 0.2 place.1.refs_4_.refs_6_
  26.7 0.0 copy-done.2
  26.7 2.0 %own_sums.1 = (f32[2,8,256]{2,1,0:T(8,128)S(1)}, f32[2,8,256]{2,1,0:T(8,128)S(1)}) custom-call(f32[2,136,256]{2,1,0:T(8,128)S(1)} %copy-done.1, f32[2,136,256]{2,1,0:T(8,128)S(1)} %collective-permute-done.refs_1_, f32[2,64,256]{2,1,0:T(8,128)S(1)} %copy-done.2, f32[2,64,256]{2,1,0:T(8,128)S(1)} %collective-permute-done.6.refs_3_, ...), custom_call_target="tpu_custom_call" | custom-call | flops 100000000 | bytes 100000 | tf_op jit(solution)/shard_map/own_sums/pallas_call | solution.py:486
  28.7 0.0 collective-permute-done.7.refs_5_
  28.7 4.5 %accumulate.1 = (f32[24,8,256]{2,1,0:T(8,128)S(1)}, f32[24,8,256]{2,1,0:T(8,128)S(1)}, f32[24,8,256]{2,1,0:T(8,128)S(1)}, f32[24,8,256]{2,1,0:T(8,128)S(1)}, f32...) custom-call(f32[4,136,256]{2,1,0:T(8,128)S(1)} %get-tuple-element.66, ...), custom_call_target="tpu_custom_call" | custom-call | flops 8000000000 | bytes 8000000 | tf_op jit(solution)/shard_map/accumulate/pallas_call | solution.py:401
  33.2 1.5 %collective-permute-start.13 = (f32[24,8,256]{2,1,0:T(8,128)S(1)}, f32[24,8,256]{2,1,0:T(8,128)S(1)}, u32[]{:S(2)}, u32[]{:S(2)}) collective-permute-start(f32[24,8,256]{2,1,0:T(8,128)S(1)} %get-tuple-element.82), channel_id=1, source_target_pairs={{0,4},{4,0},{8,12},{12,8},{16,20},{20,16},{24,28},{28,24},{1,5},{5... | collective-permute-start | bytes 589832 | tf_op jit(solution)/shard_map/ppermute | solution.py:596
  34.8 0.5 collective-permute-start.16
  35.2 2.6 %collective-permute-start.17 = (f32[6,8,256]{2,1,0:T(8,128)S(1)}, f32[6,8,256]{2,1,0:T(8,128)S(1)}, u32[]{:S(2)}, u32[]{:S(2)}) collective-permute-start(f32[6,8,256]{2,1,0:T(8,128)S(1)} %get-tuple-element.94), channel_id=1, source_target_pairs={{0,16},{4,20},{8,24},{12,28},{16,0},{20,4},{24,8},{28,12},{1,17},{... | collective-permute-start | bytes 147464 | tf_op jit(solution)/shard_map/ppermute | solution.py:596
  37.8 1.3 %collective-permute-start.18 = (f32[6,8,256]{2,1,0:T(8,128)S(1)}, f32[6,8,256]{2,1,0:T(8,128)S(1)}, u32[]{:S(2)}, u32[]{:S(2)}) collective-permute-start(f32[6,8,256]{2,1,0:T(8,128)S(1)} %get-tuple-element.95), channel_id=1, source_target_pairs={{0,24},{4,28},{8,16},{12,20},{16,8},{20,12},{24,0},{28,4},{1,25},{... | collective-permute-start | bytes 147464 | tf_op jit(solution)/shard_map/ppermute | solution.py:596
  39.1 0.6 collective-permute-start.14
  39.7 3.2 %collective-permute-done.14.refs_1_ = f32[2,8,256]{2,1,0:T(8,128)S(1)} collective-permute-done((f32[2,8,256]{2,1,0:T(8,128)S(1)}, f32[2,8,256]{2,1,0:T(8,128)S(1)}, u32[]{:S(2)}, u32[]{:S(2)}) %collective-permute-start.14) | collective-permute-done | bytes 16416 | tf_op jit(solution)/shard_map/ppermute | solution.py:596
  42.9 0.5 collective-permute-start.15
  43.4 3.3 %collective-permute-done.15.refs_3_ = f32[2,8,256]{2,1,0:T(8,128)S(1)} collective-permute-done((f32[2,8,256]{2,1,0:T(8,128)S(1)}, f32[2,8,256]{2,1,0:T(8,128)S(1)}, u32[]{:S(2)}, u32[]{:S(2)}) %collective-permute-start.15) | collective-permute-done | bytes 16416 | tf_op jit(solution)/shard_map/ppermute | solution.py:596
  46.8 0.0 collective-permute-done.13.refs_1_
  46.8 0.0 collective-permute-done.16.refs_1_
  46.8 0.0 collective-permute-done.17.refs_2_
  46.8 0.0 collective-permute-done.18.refs_3_
  46.8 0.6 collective-permute-start.19
  47.4 1.8 %collective-permute-start.21 = (f32[14,8,256]{2,1,0:T(8,128)S(1)}, f32[14,8,256]{2,1,0:T(8,128)S(1)}, u32[]{:S(2)}, u32[]{:S(2)}) collective-permute-start(f32[14,8,256]{2,1,0:T(8,128)S(1)} %get-tuple-element.90), channel_id=1, source_target_pairs={{0,16},{4,20},{8,24},{12,28},{16,0},{20,4},{24,8},{28,12},{1,17},{... | collective-permute-start | bytes 344072 | tf_op jit(solution)/shard_map/ppermute | solution.py:596
  49.2 0.8 %collective-permute-start.22 = (f32[14,8,256]{2,1,0:T(8,128)S(1)}, f32[14,8,256]{2,1,0:T(8,128)S(1)}, u32[]{:S(2)}, u32[]{:S(2)}) collective-permute-start(f32[14,8,256]{2,1,0:T(8,128)S(1)} %get-tuple-element.91), channel_id=1, source_target_pairs={{0,24},{4,28},{8,16},{12,20},{16,8},{20,12},{24,0},{28,4},{1,25},{... | collective-permute-start | bytes 344072 | tf_op jit(solution)/shard_map/ppermute | solution.py:596
  50.0 2.9 %collective-permute-done.19.refs_1_ = f32[24,8,256]{2,1,0:T(8,128)S(1)} collective-permute-done((f32[24,8,256]{2,1,0:T(8,128)S(1)}, f32[24,8,256]{2,1,0:T(8,128)S(1)}, u32[]{:S(2)}, u32[]{:S(2)}) %collective-permute-start.19) | collective-permute-done | bytes 196640 | tf_op jit(solution)/shard_map/ppermute | solution.py:596
  52.9 0.1 collective-permute-start.20
  53.0 0.6 collective-permute-start.23
  53.5 3.3 %collective-permute-done.23.refs_5_ = f32[3,8,256]{2,1,0:T(8,128)S(1)} collective-permute-done((f32[3,8,256]{2,1,0:T(8,128)S(1)}, f32[3,8,256]{2,1,0:T(8,128)S(1)}, u32[]{:S(2)}, u32[]{:S(2)}) %collective-permute-start.23) | collective-permute-done | bytes 24608 | tf_op jit(solution)/shard_map/ppermute | solution.py:596
  56.9 0.0 collective-permute-done.21.refs_2_
  56.9 0.0 collective-permute-done.22.refs_3_
  56.9 0.9 %collective-permute-done.20.refs_1_ = f32[14,8,256]{2,1,0:T(8,128)S(1)} collective-permute-done((f32[14,8,256]{2,1,0:T(8,128)S(1)}, f32[14,8,256]{2,1,0:T(8,128)S(1)}, u32[]{:S(2)}, u32[]{:S(2)}) %collective-permute-start.20) | collective-permute-done | bytes 114720 | tf_op jit(solution)/shard_map/ppermute | solution.py:596
  57.7 1.0 %finish.1 = (f32[240,120]{1,0:T(8,128)}, f32[1,240]{1,0:T(1,128)}, f32[8,8,30]{2,1,0:T(8,128)}) custom-call(f32[14,8,256]{2,1,0:T(8,128)S(1)} %get-tuple-element.98.refs_0_, f32[14,8,256]{2,1,0:T(8,128)S(1)} %collective-permute-done.20.refs_1_, f32[14,8,256]{2,1,0:T(8,128)S(1)} %collective-permute-done.21.refs_2_, ...), custom_call_target="tpu_custom_call" | custom-call | tf_op jit(solution)/shard_map/finish/pallas_call | solution.py:580
  (4 shorter events, 0.1 us)
Async XLA Ops:
  0.6 1.1 %copy-start = (f32[30,3,8,256]{3,2,1,0:T(8,128)S(1)}, f32[30,3,8,256]{3,2,1,0:T(8,128)}, u32[]{:S(2)}) copy-start(f32[30,3,8,256]{3,2,1,0:T(8,128)} %orbit.1) | copy-start | bytes 2211844
  1.8 11.9 %collective-permute-start.1 = (f32[8,3,8,256]{3,2,1,0:T(8,128)S(1)}, f32[8,3,8,256]{3,2,1,0:T(8,128)S(1)}, u32[]{:S(2)}, u32[]{:S(2)}) collective-permute-start(f32[8,3,8,256]{3,2,1,0:T(8,128)S(1)} %get-tuple-element.60), channel_id=1, source_target_pairs={{0,2},{1,3},{2,0},{3,1},{4,6},{5,7},{6,4},{7,5},{8,10},{9,11},{10,... | collective-permute-start | bytes 589832 | tf_op jit(solution)/shard_map/ppermute | solution.py:596
  6.8 10.0 %collective-permute-start = (f32[2,136,256]{2,1,0:T(8,128)}, f32[2,136,256]{2,1,0:T(8,128)S(1)}, u32[]{:S(2)}, u32[]{:S(2)}) collective-permute-start(f32[2,136,256]{2,1,0:T(8,128)} %get-tuple-element.62.refs_0_), channel_id=1, source_target_pairs={{0,1},{1,0},{2,3},{3,2},{4,5},{5,4},{6,7},{7,6},{8,9},{9,8},{10,11... | collective-permute-start | bytes 835592 | tf_op jit(solution)/shard_map/ppermute | solution.py:596
  6.9 6.8 %collective-permute-start.2 = (f32[7,3,8,256]{3,2,1,0:T(8,128)S(1)}, f32[7,3,8,256]{3,2,1,0:T(8,128)S(1)}, u32[]{:S(2)}, u32[]{:S(2)}) collective-permute-start(f32[7,3,8,256]{3,2,1,0:T(8,128)S(1)} %get-tuple-element.61), channel_id=1, source_target_pairs={{0,2},{1,3},{2,0},{3,1},{4,6},{5,7},{6,4},{7,5},{8,10},{9,11},{10,... | collective-permute-start | bytes 516104 | tf_op jit(solution)/shard_map/ppermute | solution.py:596
  7.0 19.5 %collective-permute-start.8 = (f32[30,3,8,256]{3,2,1,0:T(8,128)S(1)}, f32[30,3,8,256]{3,2,1,0:T(8,128)S(1)}, u32[]{:S(2)}, u32[]{:S(2)}) collective-permute-start(f32[30,3,8,256]{3,2,1,0:T(8,128)S(1)} %get-tuple-element.55.refs_2_.refs_0_), channel_id=1, source_target_pairs={{0,1},{1,0},{2,3},{3,2},{4,5},{5,4},{6,7},{7,6},{8,9},{9,8},{10,11... | collective-permute-start | bytes 2211848 | tf_op jit(solution)/shard_map/ppermute | solution.py:596
  13.7 9.9 %collective-permute-start.3 = (f32[2,136,256]{2,1,0:T(8,128)}, f32[2,136,256]{2,1,0:T(8,128)S(1)}, u32[]{:S(2)}, u32[]{:S(2)}) collective-permute-start(f32[2,136,256]{2,1,0:T(8,128)} %get-tuple-element.62.refs_0_), channel_id=1, source_target_pairs={{0,2},{1,3},{2,0},{3,1},{4,6},{5,7},{6,4},{7,5},{8,10},{9,11},{10,... | collective-permute-start | bytes 835592 | tf_op jit(solution)/shard_map/ppermute | solution.py:596
  15.2 8.4 %collective-permute-start.4 = (f32[8,3,8,256]{3,2,1,0:T(8,128)S(1)}, f32[8,3,8,256]{3,2,1,0:T(8,128)S(1)}, u32[]{:S(2)}, u32[]{:S(2)}) collective-permute-start(f32[8,3,8,256]{3,2,1,0:T(8,128)S(1)} %collective-permute-done.1.refs_2_), channel_id=1, source_target_pairs={{0,8},{4,12},{8,0},{12,4},{16,24},{20,28},{24,16},{28,20},{1,9},{5... | collective-permute-start | bytes 589832 | tf_op jit(solution)/shard_map/ppermute | solution.py:596
  16.8 4.5 %collective-permute-start.6 = (f32[2,64,256]{2,1,0:T(8,128)}, f32[2,64,256]{2,1,0:T(8,128)S(1)}, u32[]{:S(2)}, u32[]{:S(2)}) collective-permute-start(f32[2,64,256]{2,1,0:T(8,128)} %get-tuple-element.65.refs_2_), channel_id=1, source_target_pairs={{0,1},{1,0},{2,3},{3,2},{4,5},{5,4},{6,7},{7,6},{8,9},{9,8},{10,11... | collective-permute-start | bytes 393224 | tf_op jit(solution)/shard_map/ppermute | solution.py:596
  16.8 6.8 %collective-permute-start.5 = (f32[7,3,8,256]{3,2,1,0:T(8,128)S(1)}, f32[7,3,8,256]{3,2,1,0:T(8,128)S(1)}, u32[]{:S(2)}, u32[]{:S(2)}) collective-permute-start(f32[7,3,8,256]{3,2,1,0:T(8,128)S(1)} %collective-permute-done.2.refs_4_), channel_id=1, source_target_pairs={{0,4},{4,0},{8,12},{12,8},{16,20},{20,16},{24,28},{28,24},{1,5},{5... | collective-permute-start | bytes 516104 | tf_op jit(solution)/shard_map/ppermute | solution.py:596
  18.3 1.0 %copy-start.1 = (f32[2,136,256]{2,1,0:T(8,128)S(1)}, f32[2,136,256]{2,1,0:T(8,128)}, u32[]{:S(2)}) copy-start(f32[2,136,256]{2,1,0:T(8,128)} %get-tuple-element.62.refs_0_) | copy-start | bytes 835588
  23.6 3.1 %copy-start.2 = (f32[2,64,256]{2,1,0:T(8,128)S(1)}, f32[2,64,256]{2,1,0:T(8,128)}, u32[]{:S(2)}) copy-start(f32[2,64,256]{2,1,0:T(8,128)} %get-tuple-element.65.refs_2_) | copy-start | bytes 393220
  23.6 1.5 %collective-permute-start.10 = (f32[7,3,8,256]{3,2,1,0:T(8,128)S(1)}, f32[7,3,8,256]{3,2,1,0:T(8,128)S(1)}, u32[]{:S(2)}, u32[]{:S(2)}) collective-permute-start(f32[7,3,8,256]{3,2,1,0:T(8,128)S(1)} %collective-permute-done.2.refs_4_), channel_id=1, source_target_pairs={{0,1},{1,0},{2,3},{3,2},{4,5},{5,4},{6,7},{7,6},{8,9},{9,8},{10,11... | collective-permute-start | bytes 516104 | tf_op jit(solution)/shard_map/ppermute | solution.py:596
  23.6 5.1 %collective-permute-start.7 = (f32[2,136,256]{2,1,0:T(8,128)S(1)}, f32[2,136,256]{2,1,0:T(8,128)S(1)}, u32[]{:S(2)}, u32[]{:S(2)}) collective-permute-start(f32[2,136,256]{2,1,0:T(8,128)S(1)} %collective-permute-done.3.refs_4_), channel_id=1, source_target_pairs={{0,1},{1,0},{2,3},{3,2},{4,5},{5,4},{6,7},{7,6},{8,9},{9,8},{10,11... | collective-permute-start | bytes 835592 | tf_op jit(solution)/shard_map/ppermute | solution.py:596
  24.1 2.3 %collective-permute-start.9 = (f32[8,3,8,256]{3,2,1,0:T(8,128)S(1)}, f32[8,3,8,256]{3,2,1,0:T(8,128)S(1)}, u32[]{:S(2)}, u32[]{:S(2)}) collective-permute-start(f32[8,3,8,256]{3,2,1,0:T(8,128)S(1)} %collective-permute-done.1.refs_2_), channel_id=1, source_target_pairs={{0,1},{1,0},{2,3},{3,2},{4,5},{5,4},{6,7},{7,6},{8,9},{9,8},{10,11... | collective-permute-start | bytes 589832 | tf_op jit(solution)/shard_map/ppermute | solution.py:596
  24.2 2.2 %collective-permute-start.11 = (f32[8,3,8,256]{3,2,1,0:T(8,128)S(1)}, f32[8,3,8,256]{3,2,1,0:T(8,128)S(1)}, u32[]{:S(2)}, u32[]{:S(2)}) collective-permute-start(f32[8,3,8,256]{3,2,1,0:T(8,128)S(1)} %collective-permute-done.4.refs_6_), channel_id=1, source_target_pairs={{0,1},{1,0},{2,3},{3,2},{4,5},{5,4},{6,7},{7,6},{8,9},{9,8},{10,11... | collective-permute-start | bytes 589832 | tf_op jit(solution)/shard_map/ppermute | solution.py:596
  25.0 1.4 %collective-permute-start.12 = (f32[7,3,8,256]{3,2,1,0:T(8,128)S(1)}, f32[7,3,8,256]{3,2,1,0:T(8,128)S(1)}, u32[]{:S(2)}, u32[]{:S(2)}) collective-permute-start(f32[7,3,8,256]{3,2,1,0:T(8,128)S(1)} %collective-permute-done.5.refs_8_), channel_id=1, source_target_pairs={{0,1},{1,0},{2,3},{3,2},{4,5},{5,4},{6,7},{7,6},{8,9},{9,8},{10,11... | collective-permute-start | bytes 516104 | tf_op jit(solution)/shard_map/ppermute | solution.py:596
  33.2 13.6 %collective-permute-start.13 = (f32[24,8,256]{2,1,0:T(8,128)S(1)}, f32[24,8,256]{2,1,0:T(8,128)S(1)}, u32[]{:S(2)}, u32[]{:S(2)}) collective-permute-start(f32[24,8,256]{2,1,0:T(8,128)S(1)} %get-tuple-element.82), channel_id=1, source_target_pairs={{0,4},{4,0},{8,12},{12,8},{16,20},{20,16},{24,28},{28,24},{1,5},{5... | collective-permute-start | bytes 589832 | tf_op jit(solution)/shard_map/ppermute | solution.py:596
  34.8 12.1 %collective-permute-start.16 = (f32[6,8,256]{2,1,0:T(8,128)S(1)}, f32[6,8,256]{2,1,0:T(8,128)S(1)}, u32[]{:S(2)}, u32[]{:S(2)}) collective-permute-start(f32[6,8,256]{2,1,0:T(8,128)S(1)} %get-tuple-element.93), channel_id=1, source_target_pairs={{0,8},{4,12},{8,0},{12,4},{16,24},{20,28},{24,16},{28,20},{1,9},{5... | collective-permute-start | bytes 147464 | tf_op jit(solution)/shard_map/ppermute | solution.py:596
  35.2 11.6 %collective-permute-start.17 = (f32[6,8,256]{2,1,0:T(8,128)S(1)}, f32[6,8,256]{2,1,0:T(8,128)S(1)}, u32[]{:S(2)}, u32[]{:S(2)}) collective-permute-start(f32[6,8,256]{2,1,0:T(8,128)S(1)} %get-tuple-element.94), channel_id=1, source_target_pairs={{0,16},{4,20},{8,24},{12,28},{16,0},{20,4},{24,8},{28,12},{1,17},{... | collective-permute-start | bytes 147464 | tf_op jit(solution)/shard_map/ppermute | solution.py:596
  37.8 9.0 %collective-permute-start.18 = (f32[6,8,256]{2,1,0:T(8,128)S(1)}, f32[6,8,256]{2,1,0:T(8,128)S(1)}, u32[]{:S(2)}, u32[]{:S(2)}) collective-permute-start(f32[6,8,256]{2,1,0:T(8,128)S(1)} %get-tuple-element.95), channel_id=1, source_target_pairs={{0,24},{4,28},{8,16},{12,20},{16,8},{20,12},{24,0},{28,4},{1,25},{... | collective-permute-start | bytes 147464 | tf_op jit(solution)/shard_map/ppermute | solution.py:596
  39.1 3.7 %collective-permute-start.14 = (f32[2,8,256]{2,1,0:T(8,128)S(1)}, f32[2,8,256]{2,1,0:T(8,128)S(1)}, u32[]{:S(2)}, u32[]{:S(2)}) collective-permute-start(f32[2,8,256]{2,1,0:T(8,128)S(1)} %get-tuple-element.84), channel_id=1, source_target_pairs={{0,2},{1,3},{2,0},{3,1},{4,6},{5,7},{6,4},{7,5},{8,10},{9,11},{10,... | collective-permute-start | bytes 49160 | tf_op jit(solution)/shard_map/ppermute | solution.py:596
  42.9 3.9 %collective-permute-start.15 = (f32[2,8,256]{2,1,0:T(8,128)S(1)}, f32[2,8,256]{2,1,0:T(8,128)S(1)}, u32[]{:S(2)}, u32[]{:S(2)}) collective-permute-start(f32[2,8,256]{2,1,0:T(8,128)S(1)} %sum_over_z.2.refs_2_), channel_id=1, source_target_pairs={{0,4},{4,0},{8,12},{12,8},{16,20},{20,16},{24,28},{28,24},{1,5},{5... | collective-permute-start | bytes 49160 | tf_op jit(solution)/shard_map/ppermute | solution.py:596
  46.8 6.0 %collective-permute-start.19 = (f32[24,8,256]{2,1,0:T(8,128)S(1)}, f32[24,8,256]{2,1,0:T(8,128)S(1)}, u32[]{:S(2)}, u32[]{:S(2)}) collective-permute-start(f32[24,8,256]{2,1,0:T(8,128)S(1)} %get-tuple-element.97), channel_id=1, source_target_pairs={{0,4},{4,0},{8,12},{12,8},{16,20},{20,16},{24,28},{28,24},{1,5},{5... | collective-permute-start | bytes 589832 | tf_op jit(solution)/shard_map/ppermute | solution.py:596
  47.4 9.5 %collective-permute-start.21 = (f32[14,8,256]{2,1,0:T(8,128)S(1)}, f32[14,8,256]{2,1,0:T(8,128)S(1)}, u32[]{:S(2)}, u32[]{:S(2)}) collective-permute-start(f32[14,8,256]{2,1,0:T(8,128)S(1)} %get-tuple-element.90), channel_id=1, source_target_pairs={{0,16},{4,20},{8,24},{12,28},{16,0},{20,4},{24,8},{28,12},{1,17},{... | collective-permute-start | bytes 344072 | tf_op jit(solution)/shard_map/ppermute | solution.py:596
  49.2 7.7 %collective-permute-start.22 = (f32[14,8,256]{2,1,0:T(8,128)S(1)}, f32[14,8,256]{2,1,0:T(8,128)S(1)}, u32[]{:S(2)}, u32[]{:S(2)}) collective-permute-start(f32[14,8,256]{2,1,0:T(8,128)S(1)} %get-tuple-element.91), channel_id=1, source_target_pairs={{0,24},{4,28},{8,16},{12,20},{16,8},{20,12},{24,0},{28,4},{1,25},{... | collective-permute-start | bytes 344072 | tf_op jit(solution)/shard_map/ppermute | solution.py:596
  52.9 4.9 %collective-permute-start.20 = (f32[14,8,256]{2,1,0:T(8,128)S(1)}, f32[14,8,256]{2,1,0:T(8,128)S(1)}, u32[]{:S(2)}, u32[]{:S(2)}) collective-permute-start(f32[14,8,256]{2,1,0:T(8,128)S(1)} %get-tuple-element.99), channel_id=1, source_target_pairs={{0,8},{4,12},{8,0},{12,4},{16,24},{20,28},{24,16},{28,20},{1,9},{5... | collective-permute-start | bytes 344072 | tf_op jit(solution)/shard_map/ppermute | solution.py:596
  53.0 3.9 %collective-permute-start.23 = (f32[3,8,256]{2,1,0:T(8,128)S(1)}, f32[3,8,256]{2,1,0:T(8,128)S(1)}, u32[]{:S(2)}, u32[]{:S(2)}) collective-permute-start(f32[3,8,256]{2,1,0:T(8,128)S(1)} %get-tuple-element.101), channel_id=1, source_target_pairs={{0,4},{4,0},{8,12},{12,8},{16,20},{20,16},{24,28},{28,24},{1,5},{5... | collective-permute-start | bytes 73736 | tf_op jit(solution)/shard_map/ppermute | solution.py:596

commit v16 on v14

--- a/solution.py
+++ b/solution.py
@@ -241,12 +241,12 @@
     ready = refs[:4]
     raw_pieces = refs[4 : 4 + raw]
     orbit = refs[4 + raw]
-    outs = refs[5 + raw : 5 + raw + 2 * nx]
-    turned = refs[5 + raw + 2 * nx : 5 + raw + 2 * nx + nz]
-    own_out = refs[5 + raw + 2 * nx + nz]
+    outs = refs[5 + raw : 5 + raw + nx]
+    turned = refs[5 + raw + nx : 5 + raw + nx + nz]
+    own_out = refs[5 + raw + nx + nz]
     (acc, stream_a, stream_b, product_a, product_b, tropo_a, tropo_b, spread_tropo,
      dense_a, dense_b, raw_planes, rows_int, raw_track, track_sem) = refs[
-         6 + raw + 2 * nx + nz :]
+         6 + raw + nx + nz :]
     streams, denses = (stream_a, stream_b), (dense_a, dense_b)
     products, tropos = (product_a, product_b), (tropo_a, tropo_b)
     tracked, _, width = product_a.shape
@@ -369,14 +369,12 @@
 
     columns = sats * 8 // (nx * nz)
     own_out[...] = acc[pl.ds(first, own)]
-    half = nz // 2
+    size = outs[0].shape[0] // nz
+    last = window - size
     for dx in range(nx):
         for dz in range(nz):
             start = window_start(mine ^ (dz * nx + dx), columns, sats, window)
-            size = outs[0].shape[0] // half
-            last = window - size
-            at = (dz % half) * size
-            outs[2 * dx + (dz < half)][at : at + size] = acc[pl.ds(start, size)]
+            outs[dx][dz * size : (dz + 1) * size] = acc[pl.ds(start, size)]
             turned[dz][dx * last : (dx + 1) * last] = acc[pl.ds(start + size, last)]
 
 
@@ -387,8 +385,8 @@
     tracked = (rows - 8) // 4
     width = ready[2].shape[1]
     slabs = -(-(stations + more) // PACKED)
-    last = window // 5
-    outs = [jax.ShapeDtypeStruct((nz // 2 * (window - last), 8, width), jnp.float32)] * (2 * nx)
+    last = window * 4 // 15
+    outs = [jax.ShapeDtypeStruct((nz * (window - last), 8, width), jnp.float32)] * nx
     outs += [jax.ShapeDtypeStruct((nx * last, 8, width), jnp.float32)] * nz
     return pl.pallas_call(
         functools.partial(main_kernel, len(raw), own, nx, nz, window),
@@ -638,24 +636,17 @@
     *sums, own_rows = accumulate(
         ready, [pieces[d] for d in range(2, group)], every, own, nx, nz, window)
 
-    half = nz // 2
-    turned = sums[2 * nx :]
-    sums = sums[: 2 * nx]
-    size = sums[0].shape[0] // half
-    turned = [turned[0]] + [across(turned[dz], dz * nx) for dz in range(1, nz)]
+    turned = sums[nx:]
+    size = sums[0].shape[0] // nz
+    turned = [turned[0]] + [across(turned[dz], dz * nx) for dz in range(nz - 1, 0, -1)]
+    sums = [sums[0]] + [across(sums[dx], dx) for dx in range(1, nx)]
+    small = own_sums([pieces[d] for d in range(group)], own_rows, orbit)
+    smalls = [small] + [across(small, dx) for dx in range(1, nx)]
+    sums, smalls, turned = lax.optimization_barrier((sums, smalls, turned))
     lasts = sum_over_z(turned, nx)
     lasts = [lasts[0]] + [across(lasts[dx], dx) for dx in range(1, nx)]
-    far_sums = [sums[0]] + [across(sums[2 * dx], dx) for dx in range(1, nx)]
-    small = own_sums([pieces[d] for d in range(group)], own_rows, orbit)
-    smalls = [small] + [across(small, dx) for dx in range(1, nx)]
-    far_sums, smalls = lax.optimization_barrier((far_sums, smalls))
-    chunks = list(combine(far_sums, smalls, size))
-    near_out, _, _ = lax.optimization_barrier((sums[1::2], chunks, turned))
-    near_chunks = combine(
-        [near_out[0]] + [across(near_out[dx], dx) for dx in range(1, nx)], smalls, size)
-    final = [near_chunks[0]]
-    final += [across(near_chunks[n], n * nx) for n in range(1, half)]
-    final += [across(chunk, (half + n) * nx) for n, chunk in enumerate(chunks)]
+    chunks = combine(sums, smalls, size)
+    final = [chunks[0]] + [across(chunks[dz], dz * nx) for dz in range(nz - 1, 0, -1)]
     total_stations = stations * columns_axis * group
     factor = sats / (total_stations * tracked * epochs)
     cross_factor = sats / (total_stations * epochs) ** 0.5

time: 56.2 us -> 56.8 us (1.011)
  starting transfers between devices: 20.3 us -> 21.5 us
  waiting for transfers between devices: 21.7 us -> 21.1 us
    ppermute x22 -> x21, starting transfers between devices: 20.3 us -> 21.5 us  [shift(): return lax.ppermute(value, axis, [(i, i ^ step) for i in range(size)])]
    ppermute x22 -> x21, waiting for transfers between devices: 21.7 us -> 21.1 us  [shift(): return lax.ppermute(value, axis, [(i, i ^ step) for i in range(size)])]
  transfers between devices with their start and end apart: 22 -> 21, of which waited for: 11 -> 8; matrix products, arithmetic and copies ran while one was open for 0% -> 0% of each run, Pallas kernels for 10% -> 10%
where the time goes in v16:
time: 56.8 us; the launch traced here: 56.6 us
  starting transfers between devices  21.5 us (38%)
  waiting for transfers between devices  21.1 us (37%)
  Pallas kernels  11.2 us (20%)
  local copies, waits for them, and re-layouts  2.12 us (4%)
  between operations  0.75 us (1%)
    ppermute x21, starting transfers between devices, shift(): return lax.ppermute(value, axis, [(i, i ^ step) for i in range(size)])  21.5 us
    ppermute x21, waiting for transfers between devices, shift(): return lax.ppermute(value, axis, [(i, i ^ step) for i in range(size)])  21.1 us
    pallas_call x1, Pallas kernels, accumulate(): pl.pallas_call(functools.partial(main_kernel, len(raw), own, nx, nz, wind...  4.49 us
    unnamed x6, local copies, waits for them, and re-layouts  2.12 us
    pallas_call x1, Pallas kernels, own_rows_of(): pl.pallas_call(functools.partial(own_rows_kernel, groups, per, own, width...  2.07 us
    pallas_call x1, Pallas kernels, prepare(): pl.pallas_call(prepare_kernel, out_shape=jax.ShapeDtypeStruct((stations,...  1.99 us
    pallas_call x1, Pallas kernels, own_sums(): pl.pallas_call(functools.partial(blocks_kernel, groups, per), out_shape=j...  1.31 us
  transfers between devices with their start and end apart: 21, of which 8 were waited for; matrix products, arithmetic and copies ran while one was open for 0% of the time, Pallas kernels for 10%

profile of v16, /device:TPU:0, one launch (start us, length us, event | category | flops | bytes accessed | tf_op | source)
XLA Modules:
  0.0 56.6 jit_solution(2863379003448819386)
XLA Ops:
  0.6 0.0 copy-start.2
  0.6 1.1 %copy-done.2 = f32[30,3,8,256]{3,2,1,0:T(8,128)S(1)} copy-done((f32[30,3,8,256]{3,2,1,0:T(8,128)S(1)}, f32[30,3,8,256]{3,2,1,0:T(8,128)}, u32[]{:S(2)}) %copy-start.2) | copy-done | bytes 737304
  1.7 0.1 cut_parts.1
  1.8 3.0 %collective-permute-start.1 = (f32[8,3,8,256]{3,2,1,0:T(8,128)S(1)}, f32[8,3,8,256]{3,2,1,0:T(8,128)S(1)}, u32[]{:S(2)}, u32[]{:S(2)}) collective-permute-start(f32[8,3,8,256]{3,2,1,0:T(8,128)S(1)} %get-tuple-element.51), channel_id=1, source_target_pairs={{0,2},{1,3},{2,0},{3,1},{4,6},{5,7},{6,4},{7,5},{8,10},{9,11},{10,... | collective-permute-start | bytes 589832 | tf_op jit(solution)/shard_map/ppermute | solution.py:585
  4.9 2.0 %prepare.1.refs_0_ = f32[2,200,256]{2,1,0:T(8,128)} custom-call(f32[2,3,32,256]{3,2,1,0:T(8,128)} %refs_0_.1, f32[2,32,256]{2,1,0:T(8,128)} %refs_1_.1, f32[2,32,256]{2,1,0:T(8,128)} %refs_2_.1, s32[2,32,256]{2,1,0:T(8,128)} %refs_3_.1, s32[2,32]{1,0:T(2,128)} %refs_4_.1, s32[2,256]{1,0:T(2,128)} %refs_5_.1), custom_call_target="tpu_custom_call" | custom-call | tf_op jit(solution)/shard_map/prepare/pallas_call | solution.py:82
  6.9 0.1 collective-permute-start
  6.9 0.1 collective-permute-start.2
  7.0 0.4 collective-permute-start.7
  7.4 6.3 %collective-permute-done.2.refs_4_ = f32[7,3,8,256]{3,2,1,0:T(8,128)S(1)} collective-permute-done((f32[7,3,8,256]{3,2,1,0:T(8,128)S(1)}, f32[7,3,8,256]{3,2,1,0:T(8,128)S(1)}, u32[]{:S(2)}, u32[]{:S(2)}) %collective-permute-start.2) | collective-permute-done | bytes 172064 | tf_op jit(solution)/shard_map/ppermute | solution.py:585
  13.7 0.0 collective-permute-done.1.refs_2_
  13.7 1.5 %collective-permute-start.3 = (f32[2,200,256]{2,1,0:T(8,128)}, f32[2,200,256]{2,1,0:T(8,128)S(1)}, u32[]{:S(2)}, u32[]{:S(2)}) collective-permute-start(f32[2,200,256]{2,1,0:T(8,128)} %prepare.1.refs_0_), channel_id=1, source_target_pairs={{0,2},{1,3},{2,0},{3,1},{4,6},{5,7},{6,4},{7,5},{8,10},{9,11},{10,... | collective-permute-start | bytes 1228808 | tf_op jit(solution)/shard_map/ppermute | solution.py:585
  15.2 1.6 %collective-permute-start.4 = (f32[8,3,8,256]{3,2,1,0:T(8,128)S(1)}, f32[8,3,8,256]{3,2,1,0:T(8,128)S(1)}, u32[]{:S(2)}, u32[]{:S(2)}) collective-permute-start(f32[8,3,8,256]{3,2,1,0:T(8,128)S(1)} %collective-permute-done.1.refs_2_), channel_id=1, source_target_pairs={{0,8},{4,12},{8,0},{12,4},{16,24},{20,28},{24,16},{28,20},{1,9},{5... | collective-permute-start | bytes 589832 | tf_op jit(solution)/shard_map/ppermute | solution.py:585
  16.8 1.5 %collective-permute-start.5 = (f32[7,3,8,256]{3,2,1,0:T(8,128)S(1)}, f32[7,3,8,256]{3,2,1,0:T(8,128)S(1)}, u32[]{:S(2)}, u32[]{:S(2)}) collective-permute-start(f32[7,3,8,256]{3,2,1,0:T(8,128)S(1)} %collective-permute-done.2.refs_4_), channel_id=1, source_target_pairs={{0,4},{4,0},{8,12},{12,8},{16,20},{20,16},{24,28},{28,24},{1,5},{5... | collective-permute-start | bytes 516104 | tf_op jit(solution)/shard_map/ppermute | solution.py:585
  18.3 0.0 collective-permute-done.refs_1_
  18.3 0.0 copy-start
  18.3 1.0 %copy-done = f32[2,200,256]{2,1,0:T(8,128)S(1)} copy-done((f32[2,200,256]{2,1,0:T(8,128)S(1)}, f32[2,200,256]{2,1,0:T(8,128)}, u32[]{:S(2)}) %copy-start) | copy-done | bytes 409624
  19.3 2.1 %own_rows.1 = (f32[4,136,256]{2,1,0:T(8,128)S(1)}, s32[4,128]{1,0:T(4,128)S(1)}, bf16[4,256,256]{2,1,0:T(8,128)(2,1)S(1)}, bf16[4,256,256]{2,1,0:T(8,128)(2,1)S(1)}) custom-call(f32[2,200,256]{2,1,0:T(8,128)S(1)} %copy-done, f32[2,200,256]{2,1,0:T(8,128)S(1)} %collective-permute-done.refs_1_, f32[30,3,8,256]{3,2,1,0:T(8,128)S(1)} %get-tuple-element.46.refs_2_.refs_0_.refs_5_), custom_call_target="tpu_custom_call" | custom-call | flops 2000000000 | bytes 2000000 | tf_op jit(solution)/shard_map/own_rows/pallas_call | solution.py:196
  21.3 0.8 %collective-permute-done.5.refs_8_ = f32[7,3,8,256]{3,2,1,0:T(8,128)S(1)} collective-permute-done((f32[7,3,8,256]{3,2,1,0:T(8,128)S(1)}, f32[7,3,8,256]{3,2,1,0:T(8,128)S(1)}, u32[]{:S(2)}, u32[]{:S(2)}) %collective-permute-start.5) | collective-permute-done | bytes 172064 | tf_op jit(solution)/shard_map/ppermute | solution.py:585
  22.2 0.0 collective-permute-done.4.refs_6_
  22.2 2.8 %collective-permute-done.3.refs_4_.refs_2_ = f32[2,200,256]{2,1,0:T(8,128)S(1)} collective-permute-done((f32[2,200,256]{2,1,0:T(8,128)}, f32[2,200,256]{2,1,0:T(8,128)S(1)}, u32[]{:S(2)}, u32[]{:S(2)}) %collective-permute-start.3) | collective-permute-done | bytes 409632 | tf_op jit(solution)/shard_map/ppermute | solution.py:585
  25.0 0.0 collective-permute-start.6
  25.0 0.5 collective-permute-start.10
  25.5 0.0 collective-permute-start.8
  25.5 0.5 collective-permute-start.11
  26.0 0.0 collective-permute-done.7.refs_1_
  26.0 0.0 collective-permute-start.9
  26.0 1.5 %collective-permute-done.11.refs_9_ = f32[7,3,8,256]{3,2,1,0:T(8,128)S(1)} collective-permute-done((f32[7,3,8,256]{3,2,1,0:T(8,128)S(1)}, f32[7,3,8,256]{3,2,1,0:T(8,128)S(1)}, u32[]{:S(2)}, u32[]{:S(2)}) %collective-permute-start.11) | collective-permute-done | bytes 172064 | tf_op jit(solution)/shard_map/ppermute | solution.py:585
  27.5 0.2 collective-permute-done.9.refs_5_
  27.8 0.0 collective-permute-done.10.refs_7_
  27.8 0.0 collective-permute-done.8.refs_3_
  27.8 0.2 place.1.refs_6_
  28.0 0.0 copy-start.1
  28.0 0.0 collective-permute-done.6.refs_5_.refs_3_
  28.0 4.5 %accumulate.1 = (f32[44,8,256]{2,1,0:T(8,128)S(1)}, f32[44,8,256]{2,1,0:T(8,128)S(1)}, f32[8,8,256]{2,1,0:T(8,128)S(1)}, f32[8,8,256]{2,1,0:T(8,128)S(1)}, f32[8...) custom-call(f32[4,136,256]{2,1,0:T(8,128)S(1)} %get-tuple-element.56.refs_0_, ...), custom_call_target="tpu_custom_call" | custom-call | flops 8000000000 | bytes 8000000 | tf_op jit(solution)/shard_map/accumulate/pallas_call | solution.py:391
  32.5 1.5 %collective-permute-start.12 = (f32[44,8,256]{2,1,0:T(8,128)S(1)}, f32[44,8,256]{2,1,0:T(8,128)S(1)}, u32[]{:S(2)}, u32[]{:S(2)}) collective-permute-start(f32[44,8,256]{2,1,0:T(8,128)S(1)} %get-tuple-element.66), channel_id=1, source_target_pairs={{0,4},{4,0},{8,12},{12,8},{16,20},{20,16},{24,28},{28,24},{1,5},{5... | collective-permute-start | bytes 1081352 | tf_op jit(solution)/shard_map/ppermute | solution.py:585
  34.0 3.6 %collective-permute-start.14 = (f32[8,8,256]{2,1,0:T(8,128)S(1)}, f32[8,8,256]{2,1,0:T(8,128)S(1)}, u32[]{:S(2)}, u32[]{:S(2)}) collective-permute-start(f32[8,8,256]{2,1,0:T(8,128)S(1)} %get-tuple-element.69), channel_id=1, source_target_pairs={{0,24},{4,28},{8,16},{12,20},{16,8},{20,12},{24,0},{28,4},{1,25},{... | collective-permute-start | bytes 196616 | tf_op jit(solution)/shard_map/ppermute | solution.py:585
  37.6 0.0 collective-permute-start.15
  37.6 0.8 %collective-permute-start.16 = (f32[8,8,256]{2,1,0:T(8,128)S(1)}, f32[8,8,256]{2,1,0:T(8,128)S(1)}, u32[]{:S(2)}, u32[]{:S(2)}) collective-permute-start(f32[8,8,256]{2,1,0:T(8,128)S(1)} %get-tuple-element.71), channel_id=1, source_target_pairs={{0,8},{4,12},{8,0},{12,4},{16,24},{20,28},{24,16},{28,20},{1,9},{5... | collective-permute-start | bytes 196616 | tf_op jit(solution)/shard_map/ppermute | solution.py:585
  38.4 0.0 copy-done.1
  38.4 1.3 %own_sums.1.refs_2_ = f32[2,8,256]{2,1,0:T(8,128)S(1)} custom-call(f32[2,200,256]{2,1,0:T(8,128)S(1)} %copy-done.1, f32[2,200,256]{2,1,0:T(8,128)S(1)} %collective-permute-done.refs_1_, f32[2,200,256]{2,1,0:T(8,128)S(1)} %collective-permute-done.3.refs_4_.refs_2_, f32[2,200,256]{2,1,0:T(8,128)S(1)} %collective-permute-done.6.refs_5_.refs_3_, ...), custom_call_target="tpu_custom_call" | custom-call | flops 100000000 | bytes 100000 | tf_op jit(solution)/shard_map/own_sums/pallas_call | solution.py:475
  39.8 0.6 %collective-permute-start.13 = (f32[2,8,256]{2,1,0:T(8,128)S(1)}, f32[2,8,256]{2,1,0:T(8,128)S(1)}, u32[]{:S(2)}, u32[]{:S(2)}) collective-permute-start(f32[2,8,256]{2,1,0:T(8,128)S(1)} %own_sums.1.refs_2_), channel_id=1, source_target_pairs={{0,4},{4,0},{8,12},{12,8},{16,20},{20,16},{24,28},{28,24},{1,5},{5... | collective-permute-start | bytes 49160 | tf_op jit(solution)/shard_map/ppermute | solution.py:585
  40.4 3.2 %collective-permute-done.13.refs_3_ = f32[2,8,256]{2,1,0:T(8,128)S(1)} collective-permute-done((f32[2,8,256]{2,1,0:T(8,128)S(1)}, f32[2,8,256]{2,1,0:T(8,128)S(1)}, u32[]{:S(2)}, u32[]{:S(2)}) %collective-permute-start.13) | collective-permute-done | bytes 16416 | tf_op jit(solution)/shard_map/ppermute | solution.py:585
  43.6 0.0 collective-permute-done.14.refs_1_
  43.6 0.0 collective-permute-done.15.refs_2_
  43.6 0.0 collective-permute-done.16.refs_3_
  43.6 0.0 collective-permute-done.12.refs_1_
  43.6 3.6 %collective-permute-start.17 = (f32[13,8,256]{2,1,0:T(8,128)S(1)}, f32[13,8,256]{2,1,0:T(8,128)S(1)}, u32[]{:S(2)}, u32[]{:S(2)}) collective-permute-start(f32[13,8,256]{2,1,0:T(8,128)S(1)} %get-tuple-element.77), channel_id=1, source_target_pairs={{0,24},{4,28},{8,16},{12,20},{16,8},{20,12},{24,0},{28,4},{1,25},{... | collective-permute-start | bytes 319496 | tf_op jit(solution)/shard_map/ppermute | solution.py:585
  47.3 0.0 collective-permute-start.18
  47.3 0.8 %collective-permute-start.19 = (f32[13,8,256]{2,1,0:T(8,128)S(1)}, f32[13,8,256]{2,1,0:T(8,128)S(1)}, u32[]{:S(2)}, u32[]{:S(2)}) collective-permute-start(f32[13,8,256]{2,1,0:T(8,128)S(1)} %get-tuple-element.79), channel_id=1, source_target_pairs={{0,8},{4,12},{8,0},{12,4},{16,24},{20,28},{24,16},{28,20},{1,9},{5... | collective-permute-start | bytes 319496 | tf_op jit(solution)/shard_map/ppermute | solution.py:585
  48.1 1.3 %collective-permute-start.20 = (f32[4,8,256]{2,1,0:T(8,128)S(1)}, f32[4,8,256]{2,1,0:T(8,128)S(1)}, u32[]{:S(2)}, u32[]{:S(2)}) collective-permute-start(f32[4,8,256]{2,1,0:T(8,128)S(1)} %get-tuple-element.85), channel_id=1, source_target_pairs={{0,4},{4,0},{8,12},{12,8},{16,20},{20,16},{24,28},{28,24},{1,5},{5... | collective-permute-start | bytes 98312 | tf_op jit(solution)/shard_map/ppermute | solution.py:585
  49.5 2.6 %collective-permute-done.20.refs_5_ = f32[4,8,256]{2,1,0:T(8,128)S(1)} collective-permute-done((f32[4,8,256]{2,1,0:T(8,128)S(1)}, f32[4,8,256]{2,1,0:T(8,128)S(1)}, u32[]{:S(2)}, u32[]{:S(2)}) %collective-permute-start.20) | collective-permute-done | bytes 32800 | tf_op jit(solution)/shard_map/ppermute | solution.py:585
  52.1 0.0 collective-permute-done.17.refs_1_
  52.1 3.6 %collective-permute-done.18.refs_2_ = f32[13,8,256]{2,1,0:T(8,128)S(1)} collective-permute-done((f32[13,8,256]{2,1,0:T(8,128)S(1)}, f32[13,8,256]{2,1,0:T(8,128)S(1)}, u32[]{:S(2)}, u32[]{:S(2)}) %collective-permute-start.18) | collective-permute-done | bytes 106528 | tf_op jit(solution)/shard_map/ppermute | solution.py:585
  55.6 0.0 collective-permute-done.19.refs_3_
  55.6 1.0 %finish.1 = (f32[240,120]{1,0:T(8,128)}, f32[1,240]{1,0:T(1,128)}, f32[8,8,30]{2,1,0:T(8,128)}) custom-call(f32[13,8,256]{2,1,0:T(8,128)S(1)} %get-tuple-element.76.refs_0_, f32[13,8,256]{2,1,0:T(8,128)S(1)} %collective-permute-done.17.refs_1_, f32[13,8,256]{2,1,0:T(8,128)S(1)} %collective-permute-done.18.refs_2_, ...), custom_call_target="tpu_custom_call" | custom-call | tf_op jit(solution)/shard_map/finish/pallas_call | solution.py:569
  (2 shorter events, 0.1 us)
Async XLA Ops:
  0.6 1.1 %copy-start.2 = (f32[30,3,8,256]{3,2,1,0:T(8,128)S(1)}, f32[30,3,8,256]{3,2,1,0:T(8,128)}, u32[]{:S(2)}) copy-start(f32[30,3,8,256]{3,2,1,0:T(8,128)} %orbit.1) | copy-start | bytes 2211844
  1.8 11.9 %collective-permute-start.1 = (f32[8,3,8,256]{3,2,1,0:T(8,128)S(1)}, f32[8,3,8,256]{3,2,1,0:T(8,128)S(1)}, u32[]{:S(2)}, u32[]{:S(2)}) collective-permute-start(f32[8,3,8,256]{3,2,1,0:T(8,128)S(1)} %get-tuple-element.51), channel_id=1, source_target_pairs={{0,2},{1,3},{2,0},{3,1},{4,6},{5,7},{6,4},{7,5},{8,10},{9,11},{10,... | collective-permute-start | bytes 589832 | tf_op jit(solution)/shard_map/ppermute | solution.py:585
  6.9 11.4 %collective-permute-start = (f32[2,200,256]{2,1,0:T(8,128)}, f32[2,200,256]{2,1,0:T(8,128)S(1)}, u32[]{:S(2)}, u32[]{:S(2)}) collective-permute-start(f32[2,200,256]{2,1,0:T(8,128)} %prepare.1.refs_0_), channel_id=1, source_target_pairs={{0,1},{1,0},{2,3},{3,2},{4,5},{5,4},{6,7},{7,6},{8,9},{9,8},{10,11... | collective-permute-start | bytes 1228808 | tf_op jit(solution)/shard_map/ppermute | solution.py:585
  6.9 6.8 %collective-permute-start.2 = (f32[7,3,8,256]{3,2,1,0:T(8,128)S(1)}, f32[7,3,8,256]{3,2,1,0:T(8,128)S(1)}, u32[]{:S(2)}, u32[]{:S(2)}) collective-permute-start(f32[7,3,8,256]{3,2,1,0:T(8,128)S(1)} %get-tuple-element.52), channel_id=1, source_target_pairs={{0,2},{1,3},{2,0},{3,1},{4,6},{5,7},{6,4},{7,5},{8,10},{9,11},{10,... | collective-permute-start | bytes 516104 | tf_op jit(solution)/shard_map/ppermute | solution.py:585
  7.0 19.0 %collective-permute-start.7 = (f32[30,3,8,256]{3,2,1,0:T(8,128)S(1)}, f32[30,3,8,256]{3,2,1,0:T(8,128)S(1)}, u32[]{:S(2)}, u32[]{:S(2)}) collective-permute-start(f32[30,3,8,256]{3,2,1,0:T(8,128)S(1)} %get-tuple-element.46.refs_2_.refs_0_.refs_5_), channel_id=1, source_target_pairs={{0,1},{1,0},{2,3},{3,2},{4,5},{5,4},{6,7},{7,6},{8,9},{9,8},{10,11... | collective-permute-start | bytes 2211848 | tf_op jit(solution)/shard_map/ppermute | solution.py:585
  13.7 11.2 %collective-permute-start.3 = (f32[2,200,256]{2,1,0:T(8,128)}, f32[2,200,256]{2,1,0:T(8,128)S(1)}, u32[]{:S(2)}, u32[]{:S(2)}) collective-permute-start(f32[2,200,256]{2,1,0:T(8,128)} %prepare.1.refs_0_), channel_id=1, source_target_pairs={{0,2},{1,3},{2,0},{3,1},{4,6},{5,7},{6,4},{7,5},{8,10},{9,11},{10,... | collective-permute-start | bytes 1228808 | tf_op jit(solution)/shard_map/ppermute | solution.py:585
  15.2 7.0 %collective-permute-start.4 = (f32[8,3,8,256]{3,2,1,0:T(8,128)S(1)}, f32[8,3,8,256]{3,2,1,0:T(8,128)S(1)}, u32[]{:S(2)}, u32[]{:S(2)}) collective-permute-start(f32[8,3,8,256]{3,2,1,0:T(8,128)S(1)} %collective-permute-done.1.refs_2_), channel_id=1, source_target_pairs={{0,8},{4,12},{8,0},{12,4},{16,24},{20,28},{24,16},{28,20},{1,9},{5... | collective-permute-start | bytes 589832 | tf_op jit(solution)/shard_map/ppermute | solution.py:585
  16.8 5.4 %collective-permute-start.5 = (f32[7,3,8,256]{3,2,1,0:T(8,128)S(1)}, f32[7,3,8,256]{3,2,1,0:T(8,128)S(1)}, u32[]{:S(2)}, u32[]{:S(2)}) collective-permute-start(f32[7,3,8,256]{3,2,1,0:T(8,128)S(1)} %collective-permute-done.2.refs_4_), channel_id=1, source_target_pairs={{0,4},{4,0},{8,12},{12,8},{16,20},{20,16},{24,28},{28,24},{1,5},{5... | collective-permute-start | bytes 516104 | tf_op jit(solution)/shard_map/ppermute | solution.py:585
  18.3 1.0 %copy-start = (f32[2,200,256]{2,1,0:T(8,128)S(1)}, f32[2,200,256]{2,1,0:T(8,128)}, u32[]{:S(2)}) copy-start(f32[2,200,256]{2,1,0:T(8,128)} %prepare.1.refs_0_) | copy-start | bytes 1228804
  25.0 3.0 %collective-permute-start.6 = (f32[2,200,256]{2,1,0:T(8,128)S(1)}, f32[2,200,256]{2,1,0:T(8,128)S(1)}, u32[]{:S(2)}, u32[]{:S(2)}) collective-permute-start(f32[2,200,256]{2,1,0:T(8,128)S(1)} %collective-permute-done.3.refs_4_.refs_2_), channel_id=1, source_target_pairs={{0,1},{1,0},{2,3},{3,2},{4,5},{5,4},{6,7},{7,6},{8,9},{9,8},{10,11... | collective-permute-start | bytes 1228808 | tf_op jit(solution)/shard_map/ppermute | solution.py:585
  25.0 2.8 %collective-permute-start.10 = (f32[8,3,8,256]{3,2,1,0:T(8,128)S(1)}, f32[8,3,8,256]{3,2,1,0:T(8,128)S(1)}, u32[]{:S(2)}, u32[]{:S(2)}) collective-permute-start(f32[8,3,8,256]{3,2,1,0:T(8,128)S(1)} %collective-permute-done.4.refs_6_), channel_id=1, source_target_pairs={{0,1},{1,0},{2,3},{3,2},{4,5},{5,4},{6,7},{7,6},{8,9},{9,8},{10,11... | collective-permute-start | bytes 589832 | tf_op jit(solution)/shard_map/ppermute | solution.py:585
  25.5 2.3 %collective-permute-start.8 = (f32[8,3,8,256]{3,2,1,0:T(8,128)S(1)}, f32[8,3,8,256]{3,2,1,0:T(8,128)S(1)}, u32[]{:S(2)}, u32[]{:S(2)}) collective-permute-start(f32[8,3,8,256]{3,2,1,0:T(8,128)S(1)} %collective-permute-done.1.refs_2_), channel_id=1, source_target_pairs={{0,1},{1,0},{2,3},{3,2},{4,5},{5,4},{6,7},{7,6},{8,9},{9,8},{10,11... | collective-permute-start | bytes 589832 | tf_op jit(solution)/shard_map/ppermute | solution.py:585
  25.5 2.0 %collective-permute-start.11 = (f32[7,3,8,256]{3,2,1,0:T(8,128)S(1)}, f32[7,3,8,256]{3,2,1,0:T(8,128)S(1)}, u32[]{:S(2)}, u32[]{:S(2)}) collective-permute-start(f32[7,3,8,256]{3,2,1,0:T(8,128)S(1)} %collective-permute-done.5.refs_8_), channel_id=1, source_target_pairs={{0,1},{1,0},{2,3},{3,2},{4,5},{5,4},{6,7},{7,6},{8,9},{9,8},{10,11... | collective-permute-start | bytes 516104 | tf_op jit(solution)/shard_map/ppermute | solution.py:585
  26.0 1.8 %collective-permute-start.9 = (f32[7,3,8,256]{3,2,1,0:T(8,128)S(1)}, f32[7,3,8,256]{3,2,1,0:T(8,128)S(1)}, u32[]{:S(2)}, u32[]{:S(2)}) collective-permute-start(f32[7,3,8,256]{3,2,1,0:T(8,128)S(1)} %collective-permute-done.2.refs_4_), channel_id=1, source_target_pairs={{0,1},{1,0},{2,3},{3,2},{4,5},{5,4},{6,7},{7,6},{8,9},{9,8},{10,11... | collective-permute-start | bytes 516104 | tf_op jit(solution)/shard_map/ppermute | solution.py:585
  28.0 10.5 %copy-start.1 = (f32[2,200,256]{2,1,0:T(8,128)S(1)}, f32[2,200,256]{2,1,0:T(8,128)}, u32[]{:S(2)}) copy-start(f32[2,200,256]{2,1,0:T(8,128)} %prepare.1.refs_0_) | copy-start | bytes 1228804
  32.5 11.1 %collective-permute-start.12 = (f32[44,8,256]{2,1,0:T(8,128)S(1)}, f32[44,8,256]{2,1,0:T(8,128)S(1)}, u32[]{:S(2)}, u32[]{:S(2)}) collective-permute-start(f32[44,8,256]{2,1,0:T(8,128)S(1)} %get-tuple-element.66), channel_id=1, source_target_pairs={{0,4},{4,0},{8,12},{12,8},{16,20},{20,16},{24,28},{28,24},{1,5},{5... | collective-permute-start | bytes 1081352 | tf_op jit(solution)/shard_map/ppermute | solution.py:585
  34.0 9.5 %collective-permute-start.14 = (f32[8,8,256]{2,1,0:T(8,128)S(1)}, f32[8,8,256]{2,1,0:T(8,128)S(1)}, u32[]{:S(2)}, u32[]{:S(2)}) collective-permute-start(f32[8,8,256]{2,1,0:T(8,128)S(1)} %get-tuple-element.69), channel_id=1, source_target_pairs={{0,24},{4,28},{8,16},{12,20},{16,8},{20,12},{24,0},{28,4},{1,25},{... | collective-permute-start | bytes 196616 | tf_op jit(solution)/shard_map/ppermute | solution.py:585
  37.6 5.9 %collective-permute-start.15 = (f32[8,8,256]{2,1,0:T(8,128)S(1)}, f32[8,8,256]{2,1,0:T(8,128)S(1)}, u32[]{:S(2)}, u32[]{:S(2)}) collective-permute-start(f32[8,8,256]{2,1,0:T(8,128)S(1)} %get-tuple-element.70), channel_id=1, source_target_pairs={{0,16},{4,20},{8,24},{12,28},{16,0},{20,4},{24,8},{28,12},{1,17},{... | collective-permute-start | bytes 196616 | tf_op jit(solution)/shard_map/ppermute | solution.py:585
  37.6 5.9 %collective-permute-start.16 = (f32[8,8,256]{2,1,0:T(8,128)S(1)}, f32[8,8,256]{2,1,0:T(8,128)S(1)}, u32[]{:S(2)}, u32[]{:S(2)}) collective-permute-start(f32[8,8,256]{2,1,0:T(8,128)S(1)} %get-tuple-element.71), channel_id=1, source_target_pairs={{0,8},{4,12},{8,0},{12,4},{16,24},{20,28},{24,16},{28,20},{1,9},{5... | collective-permute-start | bytes 196616 | tf_op jit(solution)/shard_map/ppermute | solution.py:585
  39.8 3.8 %collective-permute-start.13 = (f32[2,8,256]{2,1,0:T(8,128)S(1)}, f32[2,8,256]{2,1,0:T(8,128)S(1)}, u32[]{:S(2)}, u32[]{:S(2)}) collective-permute-start(f32[2,8,256]{2,1,0:T(8,128)S(1)} %own_sums.1.refs_2_), channel_id=1, source_target_pairs={{0,4},{4,0},{8,12},{12,8},{16,20},{20,16},{24,28},{28,24},{1,5},{5... | collective-permute-start | bytes 49160 | tf_op jit(solution)/shard_map/ppermute | solution.py:585
  43.6 8.5 %collective-permute-start.17 = (f32[13,8,256]{2,1,0:T(8,128)S(1)}, f32[13,8,256]{2,1,0:T(8,128)S(1)}, u32[]{:S(2)}, u32[]{:S(2)}) collective-permute-start(f32[13,8,256]{2,1,0:T(8,128)S(1)} %get-tuple-element.77), channel_id=1, source_target_pairs={{0,24},{4,28},{8,16},{12,20},{16,8},{20,12},{24,0},{28,4},{1,25},{... | collective-permute-start | bytes 319496 | tf_op jit(solution)/shard_map/ppermute | solution.py:585
  47.3 8.4 %collective-permute-start.18 = (f32[13,8,256]{2,1,0:T(8,128)S(1)}, f32[13,8,256]{2,1,0:T(8,128)S(1)}, u32[]{:S(2)}, u32[]{:S(2)}) collective-permute-start(f32[13,8,256]{2,1,0:T(8,128)S(1)} %get-tuple-element.78), channel_id=1, source_target_pairs={{0,16},{4,20},{8,24},{12,28},{16,0},{20,4},{24,8},{28,12},{1,17},{... | collective-permute-start | bytes 319496 | tf_op jit(solution)/shard_map/ppermute | solution.py:585
  47.3 8.4 %collective-permute-start.19 = (f32[13,8,256]{2,1,0:T(8,128)S(1)}, f32[13,8,256]{2,1,0:T(8,128)S(1)}, u32[]{:S(2)}, u32[]{:S(2)}) collective-permute-start(f32[13,8,256]{2,1,0:T(8,128)S(1)} %get-tuple-element.79), channel_id=1, source_target_pairs={{0,8},{4,12},{8,0},{12,4},{16,24},{20,28},{24,16},{28,20},{1,9},{5... | collective-permute-start | bytes 319496 | tf_op jit(solution)/shard_map/ppermute | solution.py:585
  48.1 4.0 %collective-permute-start.20 = (f32[4,8,256]{2,1,0:T(8,128)S(1)}, f32[4,8,256]{2,1,0:T(8,128)S(1)}, u32[]{:S(2)}, u32[]{:S(2)}) collective-permute-start(f32[4,8,256]{2,1,0:T(8,128)S(1)} %get-tuple-element.85), channel_id=1, source_target_pairs={{0,4},{4,0},{8,12},{12,8},{16,20},{20,16},{24,28},{28,24},{1,5},{5... | collective-permute-start | bytes 98312 | tf_op jit(solution)/shard_map/ppermute | solution.py:585

commit v17 on v14

--- a/solution.py
+++ b/solution.py
@@ -535,6 +535,23 @@
     )(*pieces)
 
 
+def settle_kernel(value, out):
+    out[...] = value[...]
+
+
+def settle(value):
+    return pl.pallas_call(
+        settle_kernel,
+        out_shape=jax.ShapeDtypeStruct(value.shape, jnp.float32),
+        in_specs=[vmem()],
+        out_specs=vmem(),
+        compiler_params=pltpu.CompilerParams(vmem_limit_bytes=SMALL_LIMIT),
+        cost_estimate=pl.CostEstimate(
+            flops=8 * 10**9, bytes_accessed=8 * 10**6, transcendentals=0),
+        name="settle",
+    )(value)
+
+
 def finish_kernel(nz, window, own, columns, sats, factor, cross_factor, *refs):
     pieces, lasts = refs[:nz], refs[nz:-3]
     normal, right, blocks = refs[-3:]
@@ -623,8 +640,7 @@
     if len(parts) == 2:
         far = {d: [across(near[d][0], nx), across(near[d][1], 1)] for d in near}
     ready = own_rows_of([own_planes, other_planes], 4 * tracked + 8, orbit, width, 0)
-    ready, arrived, held_near, far = lax.optimization_barrier(
-        (tuple(ready), arrived, near, far))
+    ready, held_near, far = lax.optimization_barrier((tuple(ready), near, far))
     partials = [(0, 0, 0, orbit), (1, 0, 0, other_orbit)]
     for d in near:
         for turn, values in ((0, held_near[d]), (1, far.get(d, []))):
@@ -632,7 +648,9 @@
                 partials += [(d, turn, start, value), (d + 1, turn, start, core(value))]
     pieces = {0: own_planes, 1: other_planes}
     places = tuple(part[:3] for part in partials)
-    every = place([part[3] for part in partials], places, sats, own, nx)
+    arrived = {d: settle(value) for d, value in arrived.items()}
+    values, arrived = lax.optimization_barrier(([part[3] for part in partials], arrived))
+    every = place(values, places, sats, own, nx)
     for d, value in arrived.items():
         pieces[d], pieces[d + 1] = value, core(value)
     *sums, own_rows = accumulate(

time: 56.2 us -> 56.4 us (level)
  waiting for transfers between devices: 21.7 us -> 22.6 us
  starting transfers between devices: 20.3 us -> 19.6 us
    ppermute x22, waiting for transfers between devices: 21.7 us -> 22.6 us  [shift(): return lax.ppermute(value, axis, [(i, i ^ step) for i in range(size)])]
    ppermute x22, starting transfers between devices: 20.3 us -> 19.6 us  [shift(): return lax.ppermute(value, axis, [(i, i ^ step) for i in range(size)])]
  transfers between devices with their start and end apart: 22 -> 22, of which waited for: 11 -> 12; matrix products, arithmetic and copies ran while one was open for 0% -> 0% of each run, Pallas kernels for 10% -> 10%
where the time goes in v17:
time: 56.4 us; the launch traced here: 56.2 us
  waiting for transfers between devices  22.6 us (40%)
  starting transfers between devices  19.6 us (35%)
  Pallas kernels  11.2 us (20%)
  local copies, waits for them, and re-layouts  2.12 us (4%)
  between operations  0.75 us (1%)
    ppermute x22, waiting for transfers between devices, shift(): return lax.ppermute(value, axis, [(i, i ^ step) for i in range(size)])  22.6 us
    ppermute x22, starting transfers between devices, shift(): return lax.ppermute(value, axis, [(i, i ^ step) for i in range(size)])  19.6 us
    pallas_call x1, Pallas kernels, accumulate(): pl.pallas_call(functools.partial(main_kernel, len(raw), own, nx, nz, wind...  4.48 us
    unnamed x6, local copies, waits for them, and re-layouts  2.12 us
    pallas_call x1, Pallas kernels, own_rows_of(): pl.pallas_call(functools.partial(own_rows_kernel, groups, per, own, width...  2.07 us
    pallas_call x1, Pallas kernels, prepare(): pl.pallas_call(prepare_kernel, out_shape=jax.ShapeDtypeStruct((stations,...  1.98 us
    pallas_call x1, Pallas kernels, own_sums(): pl.pallas_call(functools.partial(blocks_kernel, groups, per), out_shape=j...  1.31 us
  transfers between devices with their start and end apart: 22, of which 12 were waited for; matrix products, arithmetic and copies ran while one was open for 0% of the time, Pallas kernels for 10%

profile of v17, /device:TPU:0, one launch (start us, length us, event | category | flops | bytes accessed | tf_op | source)
XLA Modules:
  0.0 56.2 jit_solution(6846022288056142425)
XLA Ops:
  0.6 0.0 copy-start.2
  0.6 1.1 %copy-done.2 = f32[30,3,8,256]{3,2,1,0:T(8,128)S(1)} copy-done((f32[30,3,8,256]{3,2,1,0:T(8,128)S(1)}, f32[30,3,8,256]{3,2,1,0:T(8,128)}, u32[]{:S(2)}) %copy-start.2) | copy-done | bytes 737304
  1.7 0.1 cut_parts.1
  1.8 3.0 %collective-permute-start.1 = (f32[8,3,8,256]{3,2,1,0:T(8,128)S(1)}, f32[8,3,8,256]{3,2,1,0:T(8,128)S(1)}, u32[]{:S(2)}, u32[]{:S(2)}) collective-permute-start(f32[8,3,8,256]{3,2,1,0:T(8,128)S(1)} %get-tuple-element.61), channel_id=1, source_target_pairs={{0,2},{1,3},{2,0},{3,1},{4,6},{5,7},{6,4},{7,5},{8,10},{9,11},{10,... | collective-permute-start | bytes 589832 | tf_op jit(solution)/shard_map/ppermute | solution.py:604
  4.9 2.0 %prepare.1.refs_0_ = f32[2,200,256]{2,1,0:T(8,128)} custom-call(f32[2,3,32,256]{3,2,1,0:T(8,128)} %refs_0_.1, f32[2,32,256]{2,1,0:T(8,128)} %refs_1_.1, f32[2,32,256]{2,1,0:T(8,128)} %refs_2_.1, s32[2,32,256]{2,1,0:T(8,128)} %refs_3_.1, s32[2,32]{1,0:T(2,128)} %refs_4_.1, s32[2,256]{1,0:T(2,128)} %refs_5_.1), custom_call_target="tpu_custom_call" | custom-call | tf_op jit(solution)/shard_map/prepare/pallas_call | solution.py:82
  6.8 0.1 collective-permute-start
  6.9 0.1 collective-permute-start.2
  7.0 6.7 %collective-permute-done.2.refs_4_ = f32[7,3,8,256]{3,2,1,0:T(8,128)S(1)} collective-permute-done((f32[7,3,8,256]{3,2,1,0:T(8,128)S(1)}, f32[7,3,8,256]{3,2,1,0:T(8,128)S(1)}, u32[]{:S(2)}, u32[]{:S(2)}) %collective-permute-start.2) | collective-permute-done | bytes 172064 | tf_op jit(solution)/shard_map/ppermute | solution.py:604
  13.7 0.0 collective-permute-done.1.refs_2_
  13.7 1.5 %collective-permute-start.10 = (f32[2,200,256]{2,1,0:T(8,128)}, f32[2,200,256]{2,1,0:T(8,128)S(1)}, u32[]{:S(2)}, u32[]{:S(2)}) collective-permute-start(f32[2,200,256]{2,1,0:T(8,128)} %prepare.1.refs_0_), channel_id=1, source_target_pairs={{0,2},{1,3},{2,0},{3,1},{4,6},{5,7},{6,4},{7,5},{8,10},{9,11},{10,... | collective-permute-start | bytes 1228808 | tf_op jit(solution)/shard_map/ppermute | solution.py:604
  15.2 1.6 %collective-permute-start.3 = (f32[8,3,8,256]{3,2,1,0:T(8,128)S(1)}, f32[8,3,8,256]{3,2,1,0:T(8,128)S(1)}, u32[]{:S(2)}, u32[]{:S(2)}) collective-permute-start(f32[8,3,8,256]{3,2,1,0:T(8,128)S(1)} %collective-permute-done.1.refs_2_), channel_id=1, source_target_pairs={{0,8},{4,12},{8,0},{12,4},{16,24},{20,28},{24,16},{28,20},{1,9},{5... | collective-permute-start | bytes 589832 | tf_op jit(solution)/shard_map/ppermute | solution.py:604
  16.8 0.0 collective-permute-start.5
  16.8 1.5 %collective-permute-start.4 = (f32[7,3,8,256]{3,2,1,0:T(8,128)S(1)}, f32[7,3,8,256]{3,2,1,0:T(8,128)S(1)}, u32[]{:S(2)}, u32[]{:S(2)}) collective-permute-start(f32[7,3,8,256]{3,2,1,0:T(8,128)S(1)} %collective-permute-done.2.refs_4_), channel_id=1, source_target_pairs={{0,4},{4,0},{8,12},{12,8},{16,20},{20,16},{24,28},{28,24},{1,5},{5... | collective-permute-start | bytes 516104 | tf_op jit(solution)/shard_map/ppermute | solution.py:604
  18.3 0.0 collective-permute-done.refs_1_
  18.3 0.0 copy-start
  18.3 1.0 %copy-done = f32[2,200,256]{2,1,0:T(8,128)S(1)} copy-done((f32[2,200,256]{2,1,0:T(8,128)S(1)}, f32[2,200,256]{2,1,0:T(8,128)}, u32[]{:S(2)}) %copy-start) | copy-done | bytes 409624
  19.3 2.1 %own_rows.1 = (f32[4,136,256]{2,1,0:T(8,128)S(1)}, s32[4,128]{1,0:T(4,128)S(1)}, bf16[4,256,256]{2,1,0:T(8,128)(2,1)S(1)}, bf16[4,256,256]{2,1,0:T(8,128)(2,1)S(1)}) custom-call(f32[2,200,256]{2,1,0:T(8,128)S(1)} %copy-done, f32[2,200,256]{2,1,0:T(8,128)S(1)} %collective-permute-done.refs_1_, f32[30,3,8,256]{3,2,1,0:T(8,128)S(1)} %get-tuple-element.75.refs_2_.refs_0_.refs_5_), custom_call_target="tpu_custom_call" | custom-call | flops 2000000000 | bytes 2000000 | tf_op jit(solution)/shard_map/own_rows/pallas_call | solution.py:196
  21.3 2.2 %collective-permute-done.4.refs_8_ = f32[7,3,8,256]{3,2,1,0:T(8,128)S(1)} collective-permute-done((f32[7,3,8,256]{3,2,1,0:T(8,128)S(1)}, f32[7,3,8,256]{3,2,1,0:T(8,128)S(1)}, u32[]{:S(2)}, u32[]{:S(2)}) %collective-permute-start.4) | collective-permute-done | bytes 172064 | tf_op jit(solution)/shard_map/ppermute | solution.py:604
  23.6 0.0 collective-permute-done.3.refs_6_
  23.6 0.0 collective-permute-start.6
  23.6 0.5 collective-permute-start.8
  24.1 0.0 collective-permute-start.7
  24.1 0.9 %collective-permute-done.10.value = f32[2,200,256]{2,1,0:T(8,128)S(1)} collective-permute-done((f32[2,200,256]{2,1,0:T(8,128)}, f32[2,200,256]{2,1,0:T(8,128)S(1)}, u32[]{:S(2)}, u32[]{:S(2)}) %collective-permute-start.10) | collective-permute-done | bytes 409632 | tf_op jit(solution)/shard_map/ppermute | solution.py:604
  25.0 0.0 collective-permute-start.9
  25.0 0.5 collective-permute-done.7.refs_5_
  25.5 0.8 %collective-permute-done.9.refs_9_ = f32[7,3,8,256]{3,2,1,0:T(8,128)S(1)} collective-permute-done((f32[7,3,8,256]{3,2,1,0:T(8,128)S(1)}, f32[7,3,8,256]{3,2,1,0:T(8,128)S(1)}, u32[]{:S(2)}, u32[]{:S(2)}) %collective-permute-start.9) | collective-permute-done | bytes 172064 | tf_op jit(solution)/shard_map/ppermute | solution.py:604
  26.4 0.0 collective-permute-done.6.refs_3_
  26.4 0.0 collective-permute-done.8.refs_7_
  26.4 0.0 collective-permute-done.5.refs_1_
  26.4 0.2 collective-permute-start.11
  26.6 0.2 place.1.refs_6_
  26.8 0.0 copy-start.1
  26.8 1.4 %collective-permute-done.11.refs_5_.refs_3_ = f32[2,200,256]{2,1,0:T(8,128)S(1)} collective-permute-done((f32[2,200,256]{2,1,0:T(8,128)S(1)}, f32[2,200,256]{2,1,0:T(8,128)S(1)}, u32[]{:S(2)}, u32[]{:S(2)}) %collective-permute-start.11) | collective-permute-done | bytes 409632 | tf_op jit(solution)/shard_map/ppermute | solution.py:604
  28.2 4.5 %accumulate.1 = (f32[24,8,256]{2,1,0:T(8,128)S(1)}, f32[24,8,256]{2,1,0:T(8,128)S(1)}, f32[24,8,256]{2,1,0:T(8,128)S(1)}, f32[24,8,256]{2,1,0:T(8,128)S(1)}, f32...) custom-call(f32[4,136,256]{2,1,0:T(8,128)S(1)} %get-tuple-element.65, ...), custom_call_target="tpu_custom_call" | custom-call | flops 8000000000 | bytes 8000000 | tf_op jit(solution)/shard_map/accumulate/pallas_call | solution.py:393
  32.7 1.5 %collective-permute-start.12 = (f32[24,8,256]{2,1,0:T(8,128)S(1)}, f32[24,8,256]{2,1,0:T(8,128)S(1)}, u32[]{:S(2)}, u32[]{:S(2)}) collective-permute-start(f32[24,8,256]{2,1,0:T(8,128)S(1)} %get-tuple-element.88), channel_id=1, source_target_pairs={{0,4},{4,0},{8,12},{12,8},{16,20},{20,16},{24,28},{28,24},{1,5},{5... | collective-permute-start | bytes 589832 | tf_op jit(solution)/shard_map/ppermute | solution.py:604
  34.2 1.6 %collective-permute-start.14 = (f32[6,8,256]{2,1,0:T(8,128)S(1)}, f32[6,8,256]{2,1,0:T(8,128)S(1)}, u32[]{:S(2)}, u32[]{:S(2)}) collective-permute-start(f32[6,8,256]{2,1,0:T(8,128)S(1)} %get-tuple-element.97), channel_id=1, source_target_pairs={{0,8},{4,12},{8,0},{12,4},{16,24},{20,28},{24,16},{28,20},{1,9},{5... | collective-permute-start | bytes 147464 | tf_op jit(solution)/shard_map/ppermute | solution.py:604
  35.8 2.6 %collective-permute-start.15 = (f32[6,8,256]{2,1,0:T(8,128)S(1)}, f32[6,8,256]{2,1,0:T(8,128)S(1)}, u32[]{:S(2)}, u32[]{:S(2)}) collective-permute-start(f32[6,8,256]{2,1,0:T(8,128)S(1)} %get-tuple-element.98), channel_id=1, source_target_pairs={{0,16},{4,20},{8,24},{12,28},{16,0},{20,4},{24,8},{28,12},{1,17},{... | collective-permute-start | bytes 147464 | tf_op jit(solution)/shard_map/ppermute | solution.py:604
  38.4 0.2 collective-permute-start.16
  38.6 0.0 copy-done.1
  38.6 1.3 %own_sums.1.refs_2_ = f32[2,8,256]{2,1,0:T(8,128)S(1)} custom-call(f32[2,200,256]{2,1,0:T(8,128)S(1)} %copy-done.1, f32[2,200,256]{2,1,0:T(8,128)S(1)} %collective-permute-done.refs_1_, f32[2,200,256]{2,1,0:T(8,128)S(1)} %settle.1.refs_4_.refs_2_, f32[2,200,256]{2,1,0:T(8,128)S(1)} %collective-permute-done.11.refs_5_.refs_3_, ...), custom_call_target="tpu_custom_call" | custom-call | flops 100000000 | bytes 100000 | tf_op jit(solution)/shard_map/own_sums/pallas_call | solution.py:477
  39.9 0.6 %collective-permute-start.13 = (f32[2,8,256]{2,1,0:T(8,128)S(1)}, f32[2,8,256]{2,1,0:T(8,128)S(1)}, u32[]{:S(2)}, u32[]{:S(2)}) collective-permute-start(f32[2,8,256]{2,1,0:T(8,128)S(1)} %own_sums.1.refs_2_), channel_id=1, source_target_pairs={{0,4},{4,0},{8,12},{12,8},{16,20},{20,16},{24,28},{28,24},{1,5},{5... | collective-permute-start | bytes 49160 | tf_op jit(solution)/shard_map/ppermute | solution.py:604
  40.5 3.2 %collective-permute-done.13.refs_3_ = f32[2,8,256]{2,1,0:T(8,128)S(1)} collective-permute-done((f32[2,8,256]{2,1,0:T(8,128)S(1)}, f32[2,8,256]{2,1,0:T(8,128)S(1)}, u32[]{:S(2)}, u32[]{:S(2)}) %collective-permute-start.13) | collective-permute-done | bytes 16416 | tf_op jit(solution)/shard_map/ppermute | solution.py:604
  43.7 0.0 collective-permute-done.12.refs_1_
  43.7 0.0 collective-permute-done.14.refs_1_
  43.8 0.0 collective-permute-done.15.refs_2_
  43.8 0.5 collective-permute-done.16.refs_3_
  44.3 0.5 collective-permute-start.17
  44.8 1.3 %collective-permute-start.19 = (f32[14,8,256]{2,1,0:T(8,128)S(1)}, f32[14,8,256]{2,1,0:T(8,128)S(1)}, u32[]{:S(2)}, u32[]{:S(2)}) collective-permute-start(f32[14,8,256]{2,1,0:T(8,128)S(1)} %get-tuple-element.94), channel_id=1, source_target_pairs={{0,16},{4,20},{8,24},{12,28},{16,0},{20,4},{24,8},{28,12},{1,17},{... | collective-permute-start | bytes 344072 | tf_op jit(solution)/shard_map/ppermute | solution.py:604
  46.1 1.9 %collective-permute-start.20 = (f32[14,8,256]{2,1,0:T(8,128)S(1)}, f32[14,8,256]{2,1,0:T(8,128)S(1)}, u32[]{:S(2)}, u32[]{:S(2)}) collective-permute-start(f32[14,8,256]{2,1,0:T(8,128)S(1)} %get-tuple-element.95), channel_id=1, source_target_pairs={{0,24},{4,28},{8,16},{12,20},{16,8},{20,12},{24,0},{28,4},{1,25},{... | collective-permute-start | bytes 344072 | tf_op jit(solution)/shard_map/ppermute | solution.py:604
  48.0 2.0 %collective-permute-done.17.refs_1_ = f32[24,8,256]{2,1,0:T(8,128)S(1)} collective-permute-done((f32[24,8,256]{2,1,0:T(8,128)S(1)}, f32[24,8,256]{2,1,0:T(8,128)S(1)}, u32[]{:S(2)}, u32[]{:S(2)}) %collective-permute-start.17) | collective-permute-done | bytes 196640 | tf_op jit(solution)/shard_map/ppermute | solution.py:604
  50.0 0.3 collective-permute-start.18
  50.3 0.6 %collective-permute-start.21 = (f32[3,8,256]{2,1,0:T(8,128)S(1)}, f32[3,8,256]{2,1,0:T(8,128)S(1)}, u32[]{:S(2)}, u32[]{:S(2)}) collective-permute-start(f32[3,8,256]{2,1,0:T(8,128)S(1)} %get-tuple-element.105), channel_id=1, source_target_pairs={{0,4},{4,0},{8,12},{12,8},{16,20},{20,16},{24,28},{28,24},{1,5},{5... | collective-permute-start | bytes 73736 | tf_op jit(solution)/shard_map/ppermute | solution.py:604
  50.9 3.3 %collective-permute-done.21.refs_5_ = f32[3,8,256]{2,1,0:T(8,128)S(1)} collective-permute-done((f32[3,8,256]{2,1,0:T(8,128)S(1)}, f32[3,8,256]{2,1,0:T(8,128)S(1)}, u32[]{:S(2)}, u32[]{:S(2)}) %collective-permute-start.21) | collective-permute-done | bytes 24608 | tf_op jit(solution)/shard_map/ppermute | solution.py:604
  54.2 0.1 collective-permute-done.19.refs_2_
  54.3 0.0 collective-permute-done.20.refs_3_
  54.3 0.9 %collective-permute-done.18.refs_1_ = f32[14,8,256]{2,1,0:T(8,128)S(1)} collective-permute-done((f32[14,8,256]{2,1,0:T(8,128)S(1)}, f32[14,8,256]{2,1,0:T(8,128)S(1)}, u32[]{:S(2)}, u32[]{:S(2)}) %collective-permute-start.18) | collective-permute-done | bytes 114720 | tf_op jit(solution)/shard_map/ppermute | solution.py:604
  55.2 1.0 %finish.1 = (f32[240,120]{1,0:T(8,128)}, f32[1,240]{1,0:T(1,128)}, f32[8,8,30]{2,1,0:T(8,128)}) custom-call(f32[14,8,256]{2,1,0:T(8,128)S(1)} %get-tuple-element.102.refs_0_, f32[14,8,256]{2,1,0:T(8,128)S(1)} %collective-permute-done.18.refs_1_, f32[14,8,256]{2,1,0:T(8,128)S(1)} %collective-permute-done.19.refs_2_, ...), custom_call_target="tpu_custom_call" | custom-call | tf_op jit(solution)/shard_map/finish/pallas_call | solution.py:588
  (4 shorter events, 0.1 us)
Async XLA Ops:
  0.6 1.1 %copy-start.2 = (f32[30,3,8,256]{3,2,1,0:T(8,128)S(1)}, f32[30,3,8,256]{3,2,1,0:T(8,128)}, u32[]{:S(2)}) copy-start(f32[30,3,8,256]{3,2,1,0:T(8,128)} %orbit.1) | copy-start | bytes 2211844
  1.8 11.9 %collective-permute-start.1 = (f32[8,3,8,256]{3,2,1,0:T(8,128)S(1)}, f32[8,3,8,256]{3,2,1,0:T(8,128)S(1)}, u32[]{:S(2)}, u32[]{:S(2)}) collective-permute-start(f32[8,3,8,256]{3,2,1,0:T(8,128)S(1)} %get-tuple-element.61), channel_id=1, source_target_pairs={{0,2},{1,3},{2,0},{3,1},{4,6},{5,7},{6,4},{7,5},{8,10},{9,11},{10,... | collective-permute-start | bytes 589832 | tf_op jit(solution)/shard_map/ppermute | solution.py:604
  6.8 11.4 %collective-permute-start = (f32[2,200,256]{2,1,0:T(8,128)}, f32[2,200,256]{2,1,0:T(8,128)S(1)}, u32[]{:S(2)}, u32[]{:S(2)}) collective-permute-start(f32[2,200,256]{2,1,0:T(8,128)} %prepare.1.refs_0_), channel_id=1, source_target_pairs={{0,1},{1,0},{2,3},{3,2},{4,5},{5,4},{6,7},{7,6},{8,9},{9,8},{10,11... | collective-permute-start | bytes 1228808 | tf_op jit(solution)/shard_map/ppermute | solution.py:604
  6.9 6.8 %collective-permute-start.2 = (f32[7,3,8,256]{3,2,1,0:T(8,128)S(1)}, f32[7,3,8,256]{3,2,1,0:T(8,128)S(1)}, u32[]{:S(2)}, u32[]{:S(2)}) collective-permute-start(f32[7,3,8,256]{3,2,1,0:T(8,128)S(1)} %get-tuple-element.62), channel_id=1, source_target_pairs={{0,2},{1,3},{2,0},{3,1},{4,6},{5,7},{6,4},{7,5},{8,10},{9,11},{10,... | collective-permute-start | bytes 516104 | tf_op jit(solution)/shard_map/ppermute | solution.py:604
  13.7 11.2 %collective-permute-start.10 = (f32[2,200,256]{2,1,0:T(8,128)}, f32[2,200,256]{2,1,0:T(8,128)S(1)}, u32[]{:S(2)}, u32[]{:S(2)}) collective-permute-start(f32[2,200,256]{2,1,0:T(8,128)} %prepare.1.refs_0_), channel_id=1, source_target_pairs={{0,2},{1,3},{2,0},{3,1},{4,6},{5,7},{6,4},{7,5},{8,10},{9,11},{10,... | collective-permute-start | bytes 1228808 | tf_op jit(solution)/shard_map/ppermute | solution.py:604
  15.2 8.4 %collective-permute-start.3 = (f32[8,3,8,256]{3,2,1,0:T(8,128)S(1)}, f32[8,3,8,256]{3,2,1,0:T(8,128)S(1)}, u32[]{:S(2)}, u32[]{:S(2)}) collective-permute-start(f32[8,3,8,256]{3,2,1,0:T(8,128)S(1)} %collective-permute-done.1.refs_2_), channel_id=1, source_target_pairs={{0,8},{4,12},{8,0},{12,4},{16,24},{20,28},{24,16},{28,20},{1,9},{5... | collective-permute-start | bytes 589832 | tf_op jit(solution)/shard_map/ppermute | solution.py:604
  16.8 9.6 %collective-permute-start.5 = (f32[30,3,8,256]{3,2,1,0:T(8,128)S(1)}, f32[30,3,8,256]{3,2,1,0:T(8,128)S(1)}, u32[]{:S(2)}, u32[]{:S(2)}) collective-permute-start(f32[30,3,8,256]{3,2,1,0:T(8,128)S(1)} %get-tuple-element.75.refs_2_.refs_0_.refs_5_), channel_id=1, source_target_pairs={{0,1},{1,0},{2,3},{3,2},{4,5},{5,4},{6,7},{7,6},{8,9},{9,8},{10,11... | collective-permute-start | bytes 2211848 | tf_op jit(solution)/shard_map/ppermute | solution.py:604
  16.8 6.8 %collective-permute-start.4 = (f32[7,3,8,256]{3,2,1,0:T(8,128)S(1)}, f32[7,3,8,256]{3,2,1,0:T(8,128)S(1)}, u32[]{:S(2)}, u32[]{:S(2)}) collective-permute-start(f32[7,3,8,256]{3,2,1,0:T(8,128)S(1)} %collective-permute-done.2.refs_4_), channel_id=1, source_target_pairs={{0,4},{4,0},{8,12},{12,8},{16,20},{20,16},{24,28},{28,24},{1,5},{5... | collective-permute-start | bytes 516104 | tf_op jit(solution)/shard_map/ppermute | solution.py:604
  18.3 1.0 %copy-start = (f32[2,200,256]{2,1,0:T(8,128)S(1)}, f32[2,200,256]{2,1,0:T(8,128)}, u32[]{:S(2)}) copy-start(f32[2,200,256]{2,1,0:T(8,128)} %prepare.1.refs_0_) | copy-start | bytes 1228804
  23.6 2.8 %collective-permute-start.6 = (f32[8,3,8,256]{3,2,1,0:T(8,128)S(1)}, f32[8,3,8,256]{3,2,1,0:T(8,128)S(1)}, u32[]{:S(2)}, u32[]{:S(2)}) collective-permute-start(f32[8,3,8,256]{3,2,1,0:T(8,128)S(1)} %collective-permute-done.1.refs_2_), channel_id=1, source_target_pairs={{0,1},{1,0},{2,3},{3,2},{4,5},{5,4},{6,7},{7,6},{8,9},{9,8},{10,11... | collective-permute-start | bytes 589832 | tf_op jit(solution)/shard_map/ppermute | solution.py:604
  23.6 2.8 %collective-permute-start.8 = (f32[8,3,8,256]{3,2,1,0:T(8,128)S(1)}, f32[8,3,8,256]{3,2,1,0:T(8,128)S(1)}, u32[]{:S(2)}, u32[]{:S(2)}) collective-permute-start(f32[8,3,8,256]{3,2,1,0:T(8,128)S(1)} %collective-permute-done.3.refs_6_), channel_id=1, source_target_pairs={{0,1},{1,0},{2,3},{3,2},{4,5},{5,4},{6,7},{7,6},{8,9},{9,8},{10,11... | collective-permute-start | bytes 589832 | tf_op jit(solution)/shard_map/ppermute | solution.py:604
  24.1 1.5 %collective-permute-start.7 = (f32[7,3,8,256]{3,2,1,0:T(8,128)S(1)}, f32[7,3,8,256]{3,2,1,0:T(8,128)S(1)}, u32[]{:S(2)}, u32[]{:S(2)}) collective-permute-start(f32[7,3,8,256]{3,2,1,0:T(8,128)S(1)} %collective-permute-done.2.refs_4_), channel_id=1, source_target_pairs={{0,1},{1,0},{2,3},{3,2},{4,5},{5,4},{6,7},{7,6},{8,9},{9,8},{10,11... | collective-permute-start | bytes 516104 | tf_op jit(solution)/shard_map/ppermute | solution.py:604
  25.0 1.4 %collective-permute-start.9 = (f32[7,3,8,256]{3,2,1,0:T(8,128)S(1)}, f32[7,3,8,256]{3,2,1,0:T(8,128)S(1)}, u32[]{:S(2)}, u32[]{:S(2)}) collective-permute-start(f32[7,3,8,256]{3,2,1,0:T(8,128)S(1)} %collective-permute-done.4.refs_8_), channel_id=1, source_target_pairs={{0,1},{1,0},{2,3},{3,2},{4,5},{5,4},{6,7},{7,6},{8,9},{9,8},{10,11... | collective-permute-start | bytes 516104 | tf_op jit(solution)/shard_map/ppermute | solution.py:604
  26.4 1.8 %collective-permute-start.11 = (f32[2,200,256]{2,1,0:T(8,128)S(1)}, f32[2,200,256]{2,1,0:T(8,128)S(1)}, u32[]{:S(2)}, u32[]{:S(2)}) collective-permute-start(f32[2,200,256]{2,1,0:T(8,128)S(1)} %settle.1.refs_4_.refs_2_), channel_id=1, source_target_pairs={{0,1},{1,0},{2,3},{3,2},{4,5},{5,4},{6,7},{7,6},{8,9},{9,8},{10,11... | collective-permute-start | bytes 1228808 | tf_op jit(solution)/shard_map/ppermute | solution.py:604
  26.8 11.8 %copy-start.1 = (f32[2,200,256]{2,1,0:T(8,128)S(1)}, f32[2,200,256]{2,1,0:T(8,128)}, u32[]{:S(2)}) copy-start(f32[2,200,256]{2,1,0:T(8,128)} %prepare.1.refs_0_) | copy-start | bytes 1228804
  32.7 11.0 %collective-permute-start.12 = (f32[24,8,256]{2,1,0:T(8,128)S(1)}, f32[24,8,256]{2,1,0:T(8,128)S(1)}, u32[]{:S(2)}, u32[]{:S(2)}) collective-permute-start(f32[24,8,256]{2,1,0:T(8,128)S(1)} %get-tuple-element.88), channel_id=1, source_target_pairs={{0,4},{4,0},{8,12},{12,8},{16,20},{20,16},{24,28},{28,24},{1,5},{5... | collective-permute-start | bytes 589832 | tf_op jit(solution)/shard_map/ppermute | solution.py:604
  34.2 9.5 %collective-permute-start.14 = (f32[6,8,256]{2,1,0:T(8,128)S(1)}, f32[6,8,256]{2,1,0:T(8,128)S(1)}, u32[]{:S(2)}, u32[]{:S(2)}) collective-permute-start(f32[6,8,256]{2,1,0:T(8,128)S(1)} %get-tuple-element.97), channel_id=1, source_target_pairs={{0,8},{4,12},{8,0},{12,4},{16,24},{20,28},{24,16},{28,20},{1,9},{5... | collective-permute-start | bytes 147464 | tf_op jit(solution)/shard_map/ppermute | solution.py:604
  35.8 8.0 %collective-permute-start.15 = (f32[6,8,256]{2,1,0:T(8,128)S(1)}, f32[6,8,256]{2,1,0:T(8,128)S(1)}, u32[]{:S(2)}, u32[]{:S(2)}) collective-permute-start(f32[6,8,256]{2,1,0:T(8,128)S(1)} %get-tuple-element.98), channel_id=1, source_target_pairs={{0,16},{4,20},{8,24},{12,28},{16,0},{20,4},{24,8},{28,12},{1,17},{... | collective-permute-start | bytes 147464 | tf_op jit(solution)/shard_map/ppermute | solution.py:604
  38.4 5.9 %collective-permute-start.16 = (f32[6,8,256]{2,1,0:T(8,128)S(1)}, f32[6,8,256]{2,1,0:T(8,128)S(1)}, u32[]{:S(2)}, u32[]{:S(2)}) collective-permute-start(f32[6,8,256]{2,1,0:T(8,128)S(1)} %get-tuple-element.99), channel_id=1, source_target_pairs={{0,24},{4,28},{8,16},{12,20},{16,8},{20,12},{24,0},{28,4},{1,25},{... | collective-permute-start | bytes 147464 | tf_op jit(solution)/shard_map/ppermute | solution.py:604
  39.9 3.8 %collective-permute-start.13 = (f32[2,8,256]{2,1,0:T(8,128)S(1)}, f32[2,8,256]{2,1,0:T(8,128)S(1)}, u32[]{:S(2)}, u32[]{:S(2)}) collective-permute-start(f32[2,8,256]{2,1,0:T(8,128)S(1)} %own_sums.1.refs_2_), channel_id=1, source_target_pairs={{0,4},{4,0},{8,12},{12,8},{16,20},{20,16},{24,28},{28,24},{1,5},{5... | collective-permute-start | bytes 49160 | tf_op jit(solution)/shard_map/ppermute | solution.py:604
  44.3 5.7 %collective-permute-start.17 = (f32[24,8,256]{2,1,0:T(8,128)S(1)}, f32[24,8,256]{2,1,0:T(8,128)S(1)}, u32[]{:S(2)}, u32[]{:S(2)}) collective-permute-start(f32[24,8,256]{2,1,0:T(8,128)S(1)} %get-tuple-element.101), channel_id=1, source_target_pairs={{0,4},{4,0},{8,12},{12,8},{16,20},{20,16},{24,28},{28,24},{1,5},{5... | collective-permute-start | bytes 589832 | tf_op jit(solution)/shard_map/ppermute | solution.py:604
  44.8 9.5 %collective-permute-start.19 = (f32[14,8,256]{2,1,0:T(8,128)S(1)}, f32[14,8,256]{2,1,0:T(8,128)S(1)}, u32[]{:S(2)}, u32[]{:S(2)}) collective-permute-start(f32[14,8,256]{2,1,0:T(8,128)S(1)} %get-tuple-element.94), channel_id=1, source_target_pairs={{0,16},{4,20},{8,24},{12,28},{16,0},{20,4},{24,8},{28,12},{1,17},{... | collective-permute-start | bytes 344072 | tf_op jit(solution)/shard_map/ppermute | solution.py:604
  46.1 8.2 %collective-permute-start.20 = (f32[14,8,256]{2,1,0:T(8,128)S(1)}, f32[14,8,256]{2,1,0:T(8,128)S(1)}, u32[]{:S(2)}, u32[]{:S(2)}) collective-permute-start(f32[14,8,256]{2,1,0:T(8,128)S(1)} %get-tuple-element.95), channel_id=1, source_target_pairs={{0,24},{4,28},{8,16},{12,20},{16,8},{20,12},{24,0},{28,4},{1,25},{... | collective-permute-start | bytes 344072 | tf_op jit(solution)/shard_map/ppermute | solution.py:604
  50.0 5.2 %collective-permute-start.18 = (f32[14,8,256]{2,1,0:T(8,128)S(1)}, f32[14,8,256]{2,1,0:T(8,128)S(1)}, u32[]{:S(2)}, u32[]{:S(2)}) collective-permute-start(f32[14,8,256]{2,1,0:T(8,128)S(1)} %get-tuple-element.103), channel_id=1, source_target_pairs={{0,8},{4,12},{8,0},{12,4},{16,24},{20,28},{24,16},{28,20},{1,9},{5... | collective-permute-start | bytes 344072 | tf_op jit(solution)/shard_map/ppermute | solution.py:604
  50.3 3.9 %collective-permute-start.21 = (f32[3,8,256]{2,1,0:T(8,128)S(1)}, f32[3,8,256]{2,1,0:T(8,128)S(1)}, u32[]{:S(2)}, u32[]{:S(2)}) collective-permute-start(f32[3,8,256]{2,1,0:T(8,128)S(1)} %get-tuple-element.105), channel_id=1, source_target_pairs={{0,4},{4,0},{8,12},{12,8},{16,20},{20,16},{24,28},{28,24},{1,5},{5... | collective-permute-start | bytes 73736 | tf_op jit(solution)/shard_map/ppermute | solution.py:604

commit v18 on v14

--- a/solution.py
+++ b/solution.py
@@ -486,31 +486,47 @@
     )(*planes, own_rows, orbit)
 
 
-def combine_kernel(pieces_count, smalls_count, window, *refs):
-    pieces, smalls = refs[:pieces_count], refs[pieces_count : pieces_count + smalls_count]
-    outs = refs[pieces_count + smalls_count :]
-    small = smalls[0][...]
-    for ref in smalls[1:]:
-        small = small + ref[...]
+def combine_kernel(pieces_count, *refs):
+    pieces, outs = refs[:pieces_count], refs[pieces_count:]
+    window = outs[0].shape[0]
     for n, out in enumerate(outs):
         part = pieces[0][n * window : (n + 1) * window]
         for piece in pieces[1:]:
             part = part + piece[n * window : (n + 1) * window]
-        out[:window] = part
-        out[window:] = small
-
-
-def combine(pieces, smalls, window):
+        out[...] = part
+
+
+def combine(pieces, window):
     count = pieces[0].shape[0] // window
-    width = pieces[0].shape[2]
-    return pl.pallas_call(
-        functools.partial(combine_kernel, len(pieces), len(smalls), window),
-        out_shape=[jax.ShapeDtypeStruct((window + 2, 8, width), jnp.float32)] * count,
-        in_specs=[vmem()] * (len(pieces) + len(smalls)),
+    return pl.pallas_call(
+        functools.partial(combine_kernel, len(pieces)),
+        out_shape=[jax.ShapeDtypeStruct((window,) + pieces[0].shape[1:], jnp.float32)] * count,
+        in_specs=[vmem()] * len(pieces),
         out_specs=[vmem()] * count,
         compiler_params=pltpu.CompilerParams(vmem_limit_bytes=SMALL_LIMIT),
         name="combine",
-    )(*pieces, *smalls)
+    )(*pieces)
+
+
+def attach_kernel(*refs):
+    count = len(refs) // 2
+    small = refs[count]
+    for piece, out in zip(refs[:count], refs[count + 1 :]):
+        rows = piece.shape[0]
+        out[:rows] = piece[...]
+        out[rows:] = small[...]
+
+
+def attach(pieces, small):
+    shape = (pieces[0].shape[0] + small.shape[0],) + small.shape[1:]
+    return pl.pallas_call(
+        attach_kernel,
+        out_shape=[jax.ShapeDtypeStruct(shape, jnp.float32)] * len(pieces),
+        in_specs=[vmem()] * (len(pieces) + 1),
+        out_specs=[vmem()] * len(pieces),
+        compiler_params=pltpu.CompilerParams(vmem_limit_bytes=SMALL_LIMIT),
+        name="attach",
+    )(*pieces, small)
 
 
 def sum_over_z_kernel(count, *refs):
@@ -518,16 +534,18 @@
     total = pieces[0][...]
     for piece in pieces[1:]:
         total = total + piece[...]
-    size = outs[0].shape[0]
+    size = outs[0].shape[0] - 2
     for dx, out in enumerate(outs):
-        out[...] = total[dx * size : (dx + 1) * size]
+        out[:size] = total[dx * size : (dx + 1) * size]
+        out[size:] = total[len(outs) * size :]
 
 
 def sum_over_z(pieces, nx):
     rows, _, width = pieces[0].shape
+    size = (rows - 2) // nx
     return pl.pallas_call(
         functools.partial(sum_over_z_kernel, len(pieces)),
-        out_shape=[jax.ShapeDtypeStruct((rows // nx, 8, width), jnp.float32)] * nx,
+        out_shape=[jax.ShapeDtypeStruct((size + 2, 8, width), jnp.float32)] * nx,
         in_specs=[vmem()] * len(pieces),
         out_specs=[vmem()] * nx,
         compiler_params=pltpu.CompilerParams(vmem_limit_bytes=SMALL_LIMIT),
@@ -545,16 +563,16 @@
     last = lasts[0][...]
     for piece in lasts[1:]:
         last = last + piece[...]
-    size = total.shape[0] - 2
+    size = last.shape[0] - 2
     first = lax.axis_index("sat") * own
     start = window_start(lax.axis_index("sta"), columns, sats, window)
-    part = jnp.concatenate([total[:size], last], 0).reshape(window * 8, width)
+    part = jnp.concatenate([total, last[:size]], 0).reshape(window * 8, width)
     row_owner = start + lax.broadcasted_iota(jnp.int32, part.shape, 0) // 8
     lane_owner = first + lax.broadcasted_iota(jnp.int32, part.shape, 1) // 8
     part = jnp.where(row_owner == lane_owner, 0.0, part * cross_factor)
     normal[...] = part.T[: own * 8, :]
-    right[...] = total[size + 1, :1, : own * 8] * factor
-    small = total[size]
+    right[...] = last[size + 1, :1, : own * 8] * factor
+    small = last[size]
     room = -(-own // 32) * 32
     lane = lax.broadcasted_iota(jnp.int32, (width, 8 * room), 0)
     slot = lax.broadcasted_iota(jnp.int32, (width, 8 * room), 1)
@@ -642,17 +660,16 @@
     turned = sums[2 * nx :]
     sums = sums[: 2 * nx]
     size = sums[0].shape[0] // half
+    far_sums = [sums[0]] + [across(sums[2 * dx], dx) for dx in range(1, nx)]
+    small = own_sums([pieces[d] for d in range(group)], own_rows, orbit)
+    turned = attach(turned, small)
     turned = [turned[0]] + [across(turned[dz], dz * nx) for dz in range(1, nz)]
     lasts = sum_over_z(turned, nx)
     lasts = [lasts[0]] + [across(lasts[dx], dx) for dx in range(1, nx)]
-    far_sums = [sums[0]] + [across(sums[2 * dx], dx) for dx in range(1, nx)]
-    small = own_sums([pieces[d] for d in range(group)], own_rows, orbit)
-    smalls = [small] + [across(small, dx) for dx in range(1, nx)]
-    far_sums, smalls = lax.optimization_barrier((far_sums, smalls))
-    chunks = list(combine(far_sums, smalls, size))
+    chunks = list(combine(far_sums, size))
     near_out, _, _ = lax.optimization_barrier((sums[1::2], chunks, turned))
     near_chunks = combine(
-        [near_out[0]] + [across(near_out[dx], dx) for dx in range(1, nx)], smalls, size)
+        [near_out[0]] + [across(near_out[dx], dx) for dx in range(1, nx)], size)
     final = [near_chunks[0]]
     final += [across(near_chunks[n], n * nx) for n in range(1, half)]
     final += [across(chunk, (half + n) * nx) for n, chunk in enumerate(chunks)]

time: 56.2 us -> 57.3 us (1.020)
  waiting for transfers between devices: 21.7 us -> 24.4 us
  starting transfers between devices: 20.3 us -> 18.6 us
    ppermute x22 -> x21, waiting for transfers between devices: 21.7 us -> 24.4 us  [shift(): return lax.ppermute(value, axis, [(i, i ^ step) for i in range(size)])]
    ppermute x22 -> x21, starting transfers between devices: 20.3 us -> 18.6 us  [shift(): return lax.ppermute(value, axis, [(i, i ^ step) for i in range(size)])]
  transfers between devices with their start and end apart: 22 -> 21, of which waited for: 11 -> 10; matrix products, arithmetic and copies ran while one was open for 0% -> 0% of each run, Pallas kernels for 10% -> 10%
where the time goes in v18:
time: 57.3 us; the launch traced here: 57.1 us
  waiting for transfers between devices  24.4 us (43%)
  starting transfers between devices  18.6 us (32%)
  Pallas kernels  11.2 us (20%)
  local copies, waits for them, and re-layouts  2.12 us (4%)
  between operations  0.75 us (1%)
    ppermute x21, waiting for transfers between devices, shift(): return lax.ppermute(value, axis, [(i, i ^ step) for i in range(size)])  24.4 us
    ppermute x21, starting transfers between devices, shift(): return lax.ppermute(value, axis, [(i, i ^ step) for i in range(size)])  18.6 us
    pallas_call x1, Pallas kernels, accumulate(): pl.pallas_call(functools.partial(main_kernel, len(raw), own, nx, nz, wind...  4.49 us
    unnamed x6, local copies, waits for them, and re-layouts  2.12 us
    pallas_call x1, Pallas kernels, own_rows_of(): pl.pallas_call(functools.partial(own_rows_kernel, groups, per, own, width...  2.06 us
    pallas_call x1, Pallas kernels, prepare(): pl.pallas_call(prepare_kernel, out_shape=jax.ShapeDtypeStruct((stations,...  1.98 us
    pallas_call x1, Pallas kernels, own_sums(): pl.pallas_call(functools.partial(blocks_kernel, groups, per), out_shape=j...  1.31 us
  transfers between devices with their start and end apart: 21, of which 10 were waited for; matrix products, arithmetic and copies ran while one was open for 0% of the time, Pallas kernels for 10%

profile of v18, /device:TPU:0, one launch (start us, length us, event | category | flops | bytes accessed | tf_op | source)
XLA Modules:
  0.0 57.1 jit_solution(3017854133281325937)
XLA Ops:
  0.6 0.0 copy-start.2
  0.6 1.1 %copy-done.2 = f32[30,3,8,256]{3,2,1,0:T(8,128)S(1)} copy-done((f32[30,3,8,256]{3,2,1,0:T(8,128)S(1)}, f32[30,3,8,256]{3,2,1,0:T(8,128)}, u32[]{:S(2)}) %copy-start.2) | copy-done | bytes 737304
  1.7 0.1 cut_parts.1
  1.8 3.0 %collective-permute-start.1 = (f32[8,3,8,256]{3,2,1,0:T(8,128)S(1)}, f32[8,3,8,256]{3,2,1,0:T(8,128)S(1)}, u32[]{:S(2)}, u32[]{:S(2)}) collective-permute-start(f32[8,3,8,256]{3,2,1,0:T(8,128)S(1)} %get-tuple-element.51), channel_id=1, source_target_pairs={{0,2},{1,3},{2,0},{3,1},{4,6},{5,7},{6,4},{7,5},{8,10},{9,11},{10,... | collective-permute-start | bytes 589832 | tf_op jit(solution)/shard_map/ppermute | solution.py:605
  4.9 2.0 %prepare.1.refs_0_ = f32[2,200,256]{2,1,0:T(8,128)} custom-call(f32[2,3,32,256]{3,2,1,0:T(8,128)} %refs_0_.1, f32[2,32,256]{2,1,0:T(8,128)} %refs_1_.1, f32[2,32,256]{2,1,0:T(8,128)} %refs_2_.1, s32[2,32,256]{2,1,0:T(8,128)} %refs_3_.1, s32[2,32]{1,0:T(2,128)} %refs_4_.1, s32[2,256]{1,0:T(2,128)} %refs_5_.1), custom_call_target="tpu_custom_call" | custom-call | tf_op jit(solution)/shard_map/prepare/pallas_call | solution.py:82
  6.8 0.1 collective-permute-start
  6.9 0.1 collective-permute-start.2
  7.0 0.4 collective-permute-start.7
  7.4 6.3 %collective-permute-done.2.refs_4_ = f32[7,3,8,256]{3,2,1,0:T(8,128)S(1)} collective-permute-done((f32[7,3,8,256]{3,2,1,0:T(8,128)S(1)}, f32[7,3,8,256]{3,2,1,0:T(8,128)S(1)}, u32[]{:S(2)}, u32[]{:S(2)}) %collective-permute-start.2) | collective-permute-done | bytes 172064 | tf_op jit(solution)/shard_map/ppermute | solution.py:605
  13.7 0.0 collective-permute-done.1.refs_2_
  13.7 1.5 %collective-permute-start.3 = (f32[2,200,256]{2,1,0:T(8,128)}, f32[2,200,256]{2,1,0:T(8,128)S(1)}, u32[]{:S(2)}, u32[]{:S(2)}) collective-permute-start(f32[2,200,256]{2,1,0:T(8,128)} %prepare.1.refs_0_), channel_id=1, source_target_pairs={{0,2},{1,3},{2,0},{3,1},{4,6},{5,7},{6,4},{7,5},{8,10},{9,11},{10,... | collective-permute-start | bytes 1228808 | tf_op jit(solution)/shard_map/ppermute | solution.py:605
  15.2 1.6 %collective-permute-start.4 = (f32[8,3,8,256]{3,2,1,0:T(8,128)S(1)}, f32[8,3,8,256]{3,2,1,0:T(8,128)S(1)}, u32[]{:S(2)}, u32[]{:S(2)}) collective-permute-start(f32[8,3,8,256]{3,2,1,0:T(8,128)S(1)} %collective-permute-done.1.refs_2_), channel_id=1, source_target_pairs={{0,8},{4,12},{8,0},{12,4},{16,24},{20,28},{24,16},{28,20},{1,9},{5... | collective-permute-start | bytes 589832 | tf_op jit(solution)/shard_map/ppermute | solution.py:605
  16.8 1.5 %collective-permute-start.5 = (f32[7,3,8,256]{3,2,1,0:T(8,128)S(1)}, f32[7,3,8,256]{3,2,1,0:T(8,128)S(1)}, u32[]{:S(2)}, u32[]{:S(2)}) collective-permute-start(f32[7,3,8,256]{3,2,1,0:T(8,128)S(1)} %collective-permute-done.2.refs_4_), channel_id=1, source_target_pairs={{0,4},{4,0},{8,12},{12,8},{16,20},{20,16},{24,28},{28,24},{1,5},{5... | collective-permute-start | bytes 516104 | tf_op jit(solution)/shard_map/ppermute | solution.py:605
  18.3 0.0 collective-permute-done.refs_1_
  18.3 0.0 copy-start
  18.3 1.0 %copy-done = f32[2,200,256]{2,1,0:T(8,128)S(1)} copy-done((f32[2,200,256]{2,1,0:T(8,128)S(1)}, f32[2,200,256]{2,1,0:T(8,128)}, u32[]{:S(2)}) %copy-start) | copy-done | bytes 409624
  19.3 2.1 %own_rows.1 = (f32[4,136,256]{2,1,0:T(8,128)S(1)}, s32[4,128]{1,0:T(4,128)S(1)}, bf16[4,256,256]{2,1,0:T(8,128)(2,1)S(1)}, bf16[4,256,256]{2,1,0:T(8,128)(2,1)S(1)}) custom-call(f32[2,200,256]{2,1,0:T(8,128)S(1)} %copy-done, f32[2,200,256]{2,1,0:T(8,128)S(1)} %collective-permute-done.refs_1_, f32[30,3,8,256]{3,2,1,0:T(8,128)S(1)} %get-tuple-element.46.refs_2_.refs_0_.refs_5_), custom_call_target="tpu_custom_call" | custom-call | flops 2000000000 | bytes 2000000 | tf_op jit(solution)/shard_map/own_rows/pallas_call | solution.py:196
  21.3 0.8 %collective-permute-done.5.refs_8_ = f32[7,3,8,256]{3,2,1,0:T(8,128)S(1)} collective-permute-done((f32[7,3,8,256]{3,2,1,0:T(8,128)S(1)}, f32[7,3,8,256]{3,2,1,0:T(8,128)S(1)}, u32[]{:S(2)}, u32[]{:S(2)}) %collective-permute-start.5) | collective-permute-done | bytes 172064 | tf_op jit(solution)/shard_map/ppermute | solution.py:605
  22.2 0.0 collective-permute-done.4.refs_6_
  22.2 2.8 %collective-permute-done.3.refs_4_.refs_2_ = f32[2,200,256]{2,1,0:T(8,128)S(1)} collective-permute-done((f32[2,200,256]{2,1,0:T(8,128)}, f32[2,200,256]{2,1,0:T(8,128)S(1)}, u32[]{:S(2)}, u32[]{:S(2)}) %collective-permute-start.3) | collective-permute-done | bytes 409632 | tf_op jit(solution)/shard_map/ppermute | solution.py:605
  25.0 0.0 collective-permute-start.6
  25.0 0.5 collective-permute-start.10
  25.5 0.0 collective-permute-start.8
  25.5 0.5 collective-permute-start.11
  26.0 0.0 collective-permute-done.7.refs_1_
  26.0 0.0 collective-permute-start.9
  26.0 1.5 %collective-permute-done.11.refs_9_ = f32[7,3,8,256]{3,2,1,0:T(8,128)S(1)} collective-permute-done((f32[7,3,8,256]{3,2,1,0:T(8,128)S(1)}, f32[7,3,8,256]{3,2,1,0:T(8,128)S(1)}, u32[]{:S(2)}, u32[]{:S(2)}) %collective-permute-start.11) | collective-permute-done | bytes 172064 | tf_op jit(solution)/shard_map/ppermute | solution.py:605
  27.5 0.2 collective-permute-done.9.refs_5_
  27.8 0.0 collective-permute-done.10.refs_7_
  27.8 0.0 collective-permute-done.8.refs_3_
  27.8 0.2 place.1.refs_6_
  28.0 0.0 copy-start.1
  28.0 0.0 collective-permute-done.6.refs_5_.refs_3_
  28.0 4.5 %accumulate.1 = (f32[24,8,256]{2,1,0:T(8,128)S(1)}, f32[24,8,256]{2,1,0:T(8,128)S(1)}, f32[24,8,256]{2,1,0:T(8,128)S(1)}, f32[24,8,256]{2,1,0:T(8,128)S(1)}, f32...) custom-call(f32[4,136,256]{2,1,0:T(8,128)S(1)} %get-tuple-element.56, ...), custom_call_target="tpu_custom_call" | custom-call | flops 8000000000 | bytes 8000000 | tf_op jit(solution)/shard_map/accumulate/pallas_call | solution.py:393
  32.5 1.6 %collective-permute-start.12 = (f32[24,8,256]{2,1,0:T(8,128)S(1)}, f32[24,8,256]{2,1,0:T(8,128)S(1)}, u32[]{:S(2)}, u32[]{:S(2)}) collective-permute-start(f32[24,8,256]{2,1,0:T(8,128)S(1)} %get-tuple-element.68), channel_id=1, source_target_pairs={{0,4},{4,0},{8,12},{12,8},{16,20},{20,16},{24,28},{28,24},{1,5},{5... | collective-permute-start | bytes 589832 | tf_op jit(solution)/shard_map/ppermute | solution.py:605
  34.0 0.0 copy-done.1
  34.0 1.3 %own_sums.1.refs_4_ = f32[2,8,256]{2,1,0:T(8,128)S(1)} custom-call(f32[2,200,256]{2,1,0:T(8,128)S(1)} %copy-done.1, f32[2,200,256]{2,1,0:T(8,128)S(1)} %collective-permute-done.refs_1_, f32[2,200,256]{2,1,0:T(8,128)S(1)} %collective-permute-done.3.refs_4_.refs_2_, f32[2,200,256]{2,1,0:T(8,128)S(1)} %collective-permute-done.6.refs_5_.refs_3_, ...), custom_call_target="tpu_custom_call" | custom-call | flops 100000000 | bytes 100000 | tf_op jit(solution)/shard_map/own_sums/pallas_call | solution.py:477
  35.4 1.6 %collective-permute-start.13 = (f32[8,8,256]{2,1,0:T(8,128)S(1)}, f32[8,8,256]{2,1,0:T(8,128)S(1)}, u32[]{:S(2)}, u32[]{:S(2)}) collective-permute-start(f32[8,8,256]{2,1,0:T(8,128)S(1)} %get-tuple-element.77), channel_id=1, source_target_pairs={{0,8},{4,12},{8,0},{12,4},{16,24},{20,28},{24,16},{28,20},{1,9},{5... | collective-permute-start | bytes 196616 | tf_op jit(solution)/shard_map/ppermute | solution.py:605
  37.0 2.6 %collective-permute-start.14 = (f32[8,8,256]{2,1,0:T(8,128)S(1)}, f32[8,8,256]{2,1,0:T(8,128)S(1)}, u32[]{:S(2)}, u32[]{:S(2)}) collective-permute-start(f32[8,8,256]{2,1,0:T(8,128)S(1)} %get-tuple-element.78), channel_id=1, source_target_pairs={{0,16},{4,20},{8,24},{12,28},{16,0},{20,4},{24,8},{28,12},{1,17},{... | collective-permute-start | bytes 196616 | tf_op jit(solution)/shard_map/ppermute | solution.py:605
  39.6 0.2 collective-permute-start.15
  39.8 0.0 collective-permute-done.12.refs_1_
  39.9 0.0 collective-permute-done.13.refs_1_
  39.9 4.4 %collective-permute-done.14.refs_2_ = f32[8,8,256]{2,1,0:T(8,128)S(1)} collective-permute-done((f32[8,8,256]{2,1,0:T(8,128)S(1)}, f32[8,8,256]{2,1,0:T(8,128)S(1)}, u32[]{:S(2)}, u32[]{:S(2)}) %collective-permute-start.14) | collective-permute-done | bytes 65568 | tf_op jit(solution)/shard_map/ppermute | solution.py:605
  44.3 1.4 %collective-permute-done.15.refs_3_ = f32[8,8,256]{2,1,0:T(8,128)S(1)} collective-permute-done((f32[8,8,256]{2,1,0:T(8,128)S(1)}, f32[8,8,256]{2,1,0:T(8,128)S(1)}, u32[]{:S(2)}, u32[]{:S(2)}) %collective-permute-start.15) | collective-permute-done | bytes 65568 | tf_op jit(solution)/shard_map/ppermute | solution.py:605
  45.7 0.5 collective-permute-start.16
  46.3 1.6 %collective-permute-start.18 = (f32[12,8,256]{2,1,0:T(8,128)S(1)}, f32[12,8,256]{2,1,0:T(8,128)S(1)}, u32[]{:S(2)}, u32[]{:S(2)}) collective-permute-start(f32[12,8,256]{2,1,0:T(8,128)S(1)} %get-tuple-element.69), channel_id=1, source_target_pairs={{0,16},{4,20},{8,24},{12,28},{16,0},{20,4},{24,8},{28,12},{1,17},{... | collective-permute-start | bytes 294920 | tf_op jit(solution)/shard_map/ppermute | solution.py:605
  47.8 0.7 %collective-permute-start.19 = (f32[12,8,256]{2,1,0:T(8,128)S(1)}, f32[12,8,256]{2,1,0:T(8,128)S(1)}, u32[]{:S(2)}, u32[]{:S(2)}) collective-permute-start(f32[12,8,256]{2,1,0:T(8,128)S(1)} %get-tuple-element.70), channel_id=1, source_target_pairs={{0,24},{4,28},{8,16},{12,20},{16,8},{20,12},{24,0},{28,4},{1,25},{... | collective-permute-start | bytes 294920 | tf_op jit(solution)/shard_map/ppermute | solution.py:605
  48.5 2.9 %collective-permute-done.16.refs_1_ = f32[24,8,256]{2,1,0:T(8,128)S(1)} collective-permute-done((f32[24,8,256]{2,1,0:T(8,128)S(1)}, f32[24,8,256]{2,1,0:T(8,128)S(1)}, u32[]{:S(2)}, u32[]{:S(2)}) %collective-permute-start.16) | collective-permute-done | bytes 196640 | tf_op jit(solution)/shard_map/ppermute | solution.py:605
  51.4 0.1 collective-permute-start.17
  51.6 0.6 collective-permute-start.20
  52.1 3.5 %collective-permute-done.20.refs_5_ = f32[5,8,256]{2,1,0:T(8,128)S(1)} collective-permute-done((f32[5,8,256]{2,1,0:T(8,128)S(1)}, f32[5,8,256]{2,1,0:T(8,128)S(1)}, u32[]{:S(2)}, u32[]{:S(2)}) %collective-permute-start.20) | collective-permute-done | bytes 40992 | tf_op jit(solution)/shard_map/ppermute | solution.py:605
  55.7 0.0 collective-permute-done.18.refs_2_
  55.7 0.0 collective-permute-done.19.refs_3_
  55.7 0.5 collective-permute-done.17.refs_1_
  56.1 1.0 %finish.1 = (f32[240,120]{1,0:T(8,128)}, f32[1,240]{1,0:T(1,128)}, f32[8,8,30]{2,1,0:T(8,128)}) custom-call(f32[12,8,256]{2,1,0:T(8,128)S(1)} %get-tuple-element.82.refs_0_, f32[12,8,256]{2,1,0:T(8,128)S(1)} %collective-permute-done.17.refs_1_, f32[12,8,256]{2,1,0:T(8,128)S(1)} %collective-permute-done.18.refs_2_, ...), custom_call_target="tpu_custom_call" | custom-call | tf_op jit(solution)/shard_map/finish/pallas_call | solution.py:589
  (4 shorter events, 0.1 us)
Async XLA Ops:
  0.6 1.1 %copy-start.2 = (f32[30,3,8,256]{3,2,1,0:T(8,128)S(1)}, f32[30,3,8,256]{3,2,1,0:T(8,128)}, u32[]{:S(2)}) copy-start(f32[30,3,8,256]{3,2,1,0:T(8,128)} %orbit.1) | copy-start | bytes 2211844
  1.8 11.9 %collective-permute-start.1 = (f32[8,3,8,256]{3,2,1,0:T(8,128)S(1)}, f32[8,3,8,256]{3,2,1,0:T(8,128)S(1)}, u32[]{:S(2)}, u32[]{:S(2)}) collective-permute-start(f32[8,3,8,256]{3,2,1,0:T(8,128)S(1)} %get-tuple-element.51), channel_id=1, source_target_pairs={{0,2},{1,3},{2,0},{3,1},{4,6},{5,7},{6,4},{7,5},{8,10},{9,11},{10,... | collective-permute-start | bytes 589832 | tf_op jit(solution)/shard_map/ppermute | solution.py:605
  6.8 11.4 %collective-permute-start = (f32[2,200,256]{2,1,0:T(8,128)}, f32[2,200,256]{2,1,0:T(8,128)S(1)}, u32[]{:S(2)}, u32[]{:S(2)}) collective-permute-start(f32[2,200,256]{2,1,0:T(8,128)} %prepare.1.refs_0_), channel_id=1, source_target_pairs={{0,1},{1,0},{2,3},{3,2},{4,5},{5,4},{6,7},{7,6},{8,9},{9,8},{10,11... | collective-permute-start | bytes 1228808 | tf_op jit(solution)/shard_map/ppermute | solution.py:605
  6.9 6.8 %collective-permute-start.2 = (f32[7,3,8,256]{3,2,1,0:T(8,128)S(1)}, f32[7,3,8,256]{3,2,1,0:T(8,128)S(1)}, u32[]{:S(2)}, u32[]{:S(2)}) collective-permute-start(f32[7,3,8,256]{3,2,1,0:T(8,128)S(1)} %get-tuple-element.52), channel_id=1, source_target_pairs={{0,2},{1,3},{2,0},{3,1},{4,6},{5,7},{6,4},{7,5},{8,10},{9,11},{10,... | collective-permute-start | bytes 516104 | tf_op jit(solution)/shard_map/ppermute | solution.py:605
  7.0 19.0 %collective-permute-start.7 = (f32[30,3,8,256]{3,2,1,0:T(8,128)S(1)}, f32[30,3,8,256]{3,2,1,0:T(8,128)S(1)}, u32[]{:S(2)}, u32[]{:S(2)}) collective-permute-start(f32[30,3,8,256]{3,2,1,0:T(8,128)S(1)} %get-tuple-element.46.refs_2_.refs_0_.refs_5_), channel_id=1, source_target_pairs={{0,1},{1,0},{2,3},{3,2},{4,5},{5,4},{6,7},{7,6},{8,9},{9,8},{10,11... | collective-permute-start | bytes 2211848 | tf_op jit(solution)/shard_map/ppermute | solution.py:605
  13.7 11.2 %collective-permute-start.3 = (f32[2,200,256]{2,1,0:T(8,128)}, f32[2,200,256]{2,1,0:T(8,128)S(1)}, u32[]{:S(2)}, u32[]{:S(2)}) collective-permute-start(f32[2,200,256]{2,1,0:T(8,128)} %prepare.1.refs_0_), channel_id=1, source_target_pairs={{0,2},{1,3},{2,0},{3,1},{4,6},{5,7},{6,4},{7,5},{8,10},{9,11},{10,... | collective-permute-start | bytes 1228808 | tf_op jit(solution)/shard_map/ppermute | solution.py:605
  15.2 7.0 %collective-permute-start.4 = (f32[8,3,8,256]{3,2,1,0:T(8,128)S(1)}, f32[8,3,8,256]{3,2,1,0:T(8,128)S(1)}, u32[]{:S(2)}, u32[]{:S(2)}) collective-permute-start(f32[8,3,8,256]{3,2,1,0:T(8,128)S(1)} %collective-permute-done.1.refs_2_), channel_id=1, source_target_pairs={{0,8},{4,12},{8,0},{12,4},{16,24},{20,28},{24,16},{28,20},{1,9},{5... | collective-permute-start | bytes 589832 | tf_op jit(solution)/shard_map/ppermute | solution.py:605
  16.8 5.4 %collective-permute-start.5 = (f32[7,3,8,256]{3,2,1,0:T(8,128)S(1)}, f32[7,3,8,256]{3,2,1,0:T(8,128)S(1)}, u32[]{:S(2)}, u32[]{:S(2)}) collective-permute-start(f32[7,3,8,256]{3,2,1,0:T(8,128)S(1)} %collective-permute-done.2.refs_4_), channel_id=1, source_target_pairs={{0,4},{4,0},{8,12},{12,8},{16,20},{20,16},{24,28},{28,24},{1,5},{5... | collective-permute-start | bytes 516104 | tf_op jit(solution)/shard_map/ppermute | solution.py:605
  18.3 1.0 %copy-start = (f32[2,200,256]{2,1,0:T(8,128)S(1)}, f32[2,200,256]{2,1,0:T(8,128)}, u32[]{:S(2)}) copy-start(f32[2,200,256]{2,1,0:T(8,128)} %prepare.1.refs_0_) | copy-start | bytes 1228804
  25.0 3.0 %collective-permute-start.6 = (f32[2,200,256]{2,1,0:T(8,128)S(1)}, f32[2,200,256]{2,1,0:T(8,128)S(1)}, u32[]{:S(2)}, u32[]{:S(2)}) collective-permute-start(f32[2,200,256]{2,1,0:T(8,128)S(1)} %collective-permute-done.3.refs_4_.refs_2_), channel_id=1, source_target_pairs={{0,1},{1,0},{2,3},{3,2},{4,5},{5,4},{6,7},{7,6},{8,9},{9,8},{10,11... | collective-permute-start | bytes 1228808 | tf_op jit(solution)/shard_map/ppermute | solution.py:605
  25.0 2.8 %collective-permute-start.10 = (f32[8,3,8,256]{3,2,1,0:T(8,128)S(1)}, f32[8,3,8,256]{3,2,1,0:T(8,128)S(1)}, u32[]{:S(2)}, u32[]{:S(2)}) collective-permute-start(f32[8,3,8,256]{3,2,1,0:T(8,128)S(1)} %collective-permute-done.4.refs_6_), channel_id=1, source_target_pairs={{0,1},{1,0},{2,3},{3,2},{4,5},{5,4},{6,7},{7,6},{8,9},{9,8},{10,11... | collective-permute-start | bytes 589832 | tf_op jit(solution)/shard_map/ppermute | solution.py:605
  25.5 2.3 %collective-permute-start.8 = (f32[8,3,8,256]{3,2,1,0:T(8,128)S(1)}, f32[8,3,8,256]{3,2,1,0:T(8,128)S(1)}, u32[]{:S(2)}, u32[]{:S(2)}) collective-permute-start(f32[8,3,8,256]{3,2,1,0:T(8,128)S(1)} %collective-permute-done.1.refs_2_), channel_id=1, source_target_pairs={{0,1},{1,0},{2,3},{3,2},{4,5},{5,4},{6,7},{7,6},{8,9},{9,8},{10,11... | collective-permute-start | bytes 589832 | tf_op jit(solution)/shard_map/ppermute | solution.py:605
  25.5 2.0 %collective-permute-start.11 = (f32[7,3,8,256]{3,2,1,0:T(8,128)S(1)}, f32[7,3,8,256]{3,2,1,0:T(8,128)S(1)}, u32[]{:S(2)}, u32[]{:S(2)}) collective-permute-start(f32[7,3,8,256]{3,2,1,0:T(8,128)S(1)} %collective-permute-done.5.refs_8_), channel_id=1, source_target_pairs={{0,1},{1,0},{2,3},{3,2},{4,5},{5,4},{6,7},{7,6},{8,9},{9,8},{10,11... | collective-permute-start | bytes 516104 | tf_op jit(solution)/shard_map/ppermute | solution.py:605
  26.0 1.8 %collective-permute-start.9 = (f32[7,3,8,256]{3,2,1,0:T(8,128)S(1)}, f32[7,3,8,256]{3,2,1,0:T(8,128)S(1)}, u32[]{:S(2)}, u32[]{:S(2)}) collective-permute-start(f32[7,3,8,256]{3,2,1,0:T(8,128)S(1)} %collective-permute-done.2.refs_4_), channel_id=1, source_target_pairs={{0,1},{1,0},{2,3},{3,2},{4,5},{5,4},{6,7},{7,6},{8,9},{9,8},{10,11... | collective-permute-start | bytes 516104 | tf_op jit(solution)/shard_map/ppermute | solution.py:605
  28.0 6.1 %copy-start.1 = (f32[2,200,256]{2,1,0:T(8,128)S(1)}, f32[2,200,256]{2,1,0:T(8,128)}, u32[]{:S(2)}) copy-start(f32[2,200,256]{2,1,0:T(8,128)} %prepare.1.refs_0_) | copy-start | bytes 1228804
  32.5 7.4 %collective-permute-start.12 = (f32[24,8,256]{2,1,0:T(8,128)S(1)}, f32[24,8,256]{2,1,0:T(8,128)S(1)}, u32[]{:S(2)}, u32[]{:S(2)}) collective-permute-start(f32[24,8,256]{2,1,0:T(8,128)S(1)} %get-tuple-element.68), channel_id=1, source_target_pairs={{0,4},{4,0},{8,12},{12,8},{16,20},{20,16},{24,28},{28,24},{1,5},{5... | collective-permute-start | bytes 589832 | tf_op jit(solution)/shard_map/ppermute | solution.py:605
  35.4 4.5 %collective-permute-start.13 = (f32[8,8,256]{2,1,0:T(8,128)S(1)}, f32[8,8,256]{2,1,0:T(8,128)S(1)}, u32[]{:S(2)}, u32[]{:S(2)}) collective-permute-start(f32[8,8,256]{2,1,0:T(8,128)S(1)} %get-tuple-element.77), channel_id=1, source_target_pairs={{0,8},{4,12},{8,0},{12,4},{16,24},{20,28},{24,16},{28,20},{1,9},{5... | collective-permute-start | bytes 196616 | tf_op jit(solution)/shard_map/ppermute | solution.py:605
  37.0 7.3 %collective-permute-start.14 = (f32[8,8,256]{2,1,0:T(8,128)S(1)}, f32[8,8,256]{2,1,0:T(8,128)S(1)}, u32[]{:S(2)}, u32[]{:S(2)}) collective-permute-start(f32[8,8,256]{2,1,0:T(8,128)S(1)} %get-tuple-element.78), channel_id=1, source_target_pairs={{0,16},{4,20},{8,24},{12,28},{16,0},{20,4},{24,8},{28,12},{1,17},{... | collective-permute-start | bytes 196616 | tf_op jit(solution)/shard_map/ppermute | solution.py:605
  39.6 6.1 %collective-permute-start.15 = (f32[8,8,256]{2,1,0:T(8,128)S(1)}, f32[8,8,256]{2,1,0:T(8,128)S(1)}, u32[]{:S(2)}, u32[]{:S(2)}) collective-permute-start(f32[8,8,256]{2,1,0:T(8,128)S(1)} %get-tuple-element.79), channel_id=1, source_target_pairs={{0,24},{4,28},{8,16},{12,20},{16,8},{20,12},{24,0},{28,4},{1,25},{... | collective-permute-start | bytes 196616 | tf_op jit(solution)/shard_map/ppermute | solution.py:605
  45.7 5.7 %collective-permute-start.16 = (f32[24,8,256]{2,1,0:T(8,128)S(1)}, f32[24,8,256]{2,1,0:T(8,128)S(1)}, u32[]{:S(2)}, u32[]{:S(2)}) collective-permute-start(f32[24,8,256]{2,1,0:T(8,128)S(1)} %get-tuple-element.81), channel_id=1, source_target_pairs={{0,4},{4,0},{8,12},{12,8},{16,20},{20,16},{24,28},{28,24},{1,5},{5... | collective-permute-start | bytes 589832 | tf_op jit(solution)/shard_map/ppermute | solution.py:605
  46.3 9.4 %collective-permute-start.18 = (f32[12,8,256]{2,1,0:T(8,128)S(1)}, f32[12,8,256]{2,1,0:T(8,128)S(1)}, u32[]{:S(2)}, u32[]{:S(2)}) collective-permute-start(f32[12,8,256]{2,1,0:T(8,128)S(1)} %get-tuple-element.69), channel_id=1, source_target_pairs={{0,16},{4,20},{8,24},{12,28},{16,0},{20,4},{24,8},{28,12},{1,17},{... | collective-permute-start | bytes 294920 | tf_op jit(solution)/shard_map/ppermute | solution.py:605
  47.8 7.8 %collective-permute-start.19 = (f32[12,8,256]{2,1,0:T(8,128)S(1)}, f32[12,8,256]{2,1,0:T(8,128)S(1)}, u32[]{:S(2)}, u32[]{:S(2)}) collective-permute-start(f32[12,8,256]{2,1,0:T(8,128)S(1)} %get-tuple-element.70), channel_id=1, source_target_pairs={{0,24},{4,28},{8,16},{12,20},{16,8},{20,12},{24,0},{28,4},{1,25},{... | collective-permute-start | bytes 294920 | tf_op jit(solution)/shard_map/ppermute | solution.py:605
  51.4 4.7 %collective-permute-start.17 = (f32[12,8,256]{2,1,0:T(8,128)S(1)}, f32[12,8,256]{2,1,0:T(8,128)S(1)}, u32[]{:S(2)}, u32[]{:S(2)}) collective-permute-start(f32[12,8,256]{2,1,0:T(8,128)S(1)} %get-tuple-element.83), channel_id=1, source_target_pairs={{0,8},{4,12},{8,0},{12,4},{16,24},{20,28},{24,16},{28,20},{1,9},{5... | collective-permute-start | bytes 294920 | tf_op jit(solution)/shard_map/ppermute | solution.py:605
  51.6 4.1 %collective-permute-start.20 = (f32[5,8,256]{2,1,0:T(8,128)S(1)}, f32[5,8,256]{2,1,0:T(8,128)S(1)}, u32[]{:S(2)}, u32[]{:S(2)}) collective-permute-start(f32[5,8,256]{2,1,0:T(8,128)S(1)} %get-tuple-element.85), channel_id=1, source_target_pairs={{0,4},{4,0},{8,12},{12,8},{16,20},{20,16},{24,28},{28,24},{1,5},{5... | collective-permute-start | bytes 122888 | tf_op jit(solution)/shard_map/ppermute | solution.py:605

commit v19 on v14

--- a/solution.py
+++ b/solution.py
@@ -387,7 +387,7 @@
     tracked = (rows - 8) // 4
     width = ready[2].shape[1]
     slabs = -(-(stations + more) // PACKED)
-    last = window // 5
+    last = window * 4 // 15
     outs = [jax.ShapeDtypeStruct((nz // 2 * (window - last), 8, width), jnp.float32)] * (2 * nx)
     outs += [jax.ShapeDtypeStruct((nx * last, 8, width), jnp.float32)] * nz
     return pl.pallas_call(

time: 56.2 us -> 56.5 us (level)
  waiting for transfers between devices: 21.7 us -> 22.3 us
    ppermute x22, waiting for transfers between devices: 21.7 us -> 22.3 us  [shift(): return lax.ppermute(value, axis, [(i, i ^ step) for i in range(size)])]
where the time goes in v19:
time: 56.5 us; the launch traced here: 56.2 us
  waiting for transfers between devices  22.3 us (39%)
  starting transfers between devices  19.9 us (35%)
  Pallas kernels  11.1 us (20%)
  local copies, waits for them, and re-layouts  2.12 us (4%)
  between operations  0.75 us (1%)
    ppermute x22, waiting for transfers between devices, shift(): return lax.ppermute(value, axis, [(i, i ^ step) for i in range(size)])  22.3 us
    ppermute x22, starting transfers between devices, shift(): return lax.ppermute(value, axis, [(i, i ^ step) for i in range(size)])  19.9 us
    pallas_call x1, Pallas kernels, accumulate(): pl.pallas_call(functools.partial(main_kernel, len(raw), own, nx, nz, wind...  4.48 us
    unnamed x6, local copies, waits for them, and re-layouts  2.12 us
    pallas_call x1, Pallas kernels, own_rows_of(): pl.pallas_call(functools.partial(own_rows_kernel, groups, per, own, width...  2.07 us
    pallas_call x1, Pallas kernels, prepare(): pl.pallas_call(prepare_kernel, out_shape=jax.ShapeDtypeStruct((stations,...  1.98 us
    pallas_call x1, Pallas kernels, own_sums(): pl.pallas_call(functools.partial(blocks_kernel, groups, per), out_shape=j...  1.31 us
  transfers between devices with their start and end apart: 22, of which 11 were waited for; matrix products, arithmetic and copies ran while one was open for 0% of the time, Pallas kernels for 10%

profile of v19, /device:TPU:0, one launch (start us, length us, event | category | flops | bytes accessed | tf_op | source)
XLA Modules:
  0.0 56.2 jit_solution(16495420724433978807)
XLA Ops:
  0.6 0.0 copy-start.2
  0.6 1.1 %copy-done.2 = f32[30,3,8,256]{3,2,1,0:T(8,128)S(1)} copy-done((f32[30,3,8,256]{3,2,1,0:T(8,128)S(1)}, f32[30,3,8,256]{3,2,1,0:T(8,128)}, u32[]{:S(2)}) %copy-start.2) | copy-done | bytes 737304
  1.7 0.1 cut_parts.1
  1.8 3.0 %collective-permute-start.1 = (f32[8,3,8,256]{3,2,1,0:T(8,128)S(1)}, f32[8,3,8,256]{3,2,1,0:T(8,128)S(1)}, u32[]{:S(2)}, u32[]{:S(2)}) collective-permute-start(f32[8,3,8,256]{3,2,1,0:T(8,128)S(1)} %get-tuple-element.51), channel_id=1, source_target_pairs={{0,2},{1,3},{2,0},{3,1},{4,6},{5,7},{6,4},{7,5},{8,10},{9,11},{10,... | collective-permute-start | bytes 589832 | tf_op jit(solution)/shard_map/ppermute | solution.py:587
  4.9 2.0 %prepare.1.refs_0_ = f32[2,200,256]{2,1,0:T(8,128)} custom-call(f32[2,3,32,256]{3,2,1,0:T(8,128)} %refs_0_.1, f32[2,32,256]{2,1,0:T(8,128)} %refs_1_.1, f32[2,32,256]{2,1,0:T(8,128)} %refs_2_.1, s32[2,32,256]{2,1,0:T(8,128)} %refs_3_.1, s32[2,32]{1,0:T(2,128)} %refs_4_.1, s32[2,256]{1,0:T(2,128)} %refs_5_.1), custom_call_target="tpu_custom_call" | custom-call | tf_op jit(solution)/shard_map/prepare/pallas_call | solution.py:82
  6.8 0.1 collective-permute-start
  6.9 0.1 collective-permute-start.2
  7.0 0.4 collective-permute-start.7
  7.4 6.3 %collective-permute-done.2.refs_4_ = f32[7,3,8,256]{3,2,1,0:T(8,128)S(1)} collective-permute-done((f32[7,3,8,256]{3,2,1,0:T(8,128)S(1)}, f32[7,3,8,256]{3,2,1,0:T(8,128)S(1)}, u32[]{:S(2)}, u32[]{:S(2)}) %collective-permute-start.2) | collective-permute-done | bytes 172064 | tf_op jit(solution)/shard_map/ppermute | solution.py:587
  13.7 0.0 collective-permute-done.1.refs_2_
  13.7 1.5 %collective-permute-start.3 = (f32[2,200,256]{2,1,0:T(8,128)}, f32[2,200,256]{2,1,0:T(8,128)S(1)}, u32[]{:S(2)}, u32[]{:S(2)}) collective-permute-start(f32[2,200,256]{2,1,0:T(8,128)} %prepare.1.refs_0_), channel_id=1, source_target_pairs={{0,2},{1,3},{2,0},{3,1},{4,6},{5,7},{6,4},{7,5},{8,10},{9,11},{10,... | collective-permute-start | bytes 1228808 | tf_op jit(solution)/shard_map/ppermute | solution.py:587
  15.2 1.6 %collective-permute-start.4 = (f32[8,3,8,256]{3,2,1,0:T(8,128)S(1)}, f32[8,3,8,256]{3,2,1,0:T(8,128)S(1)}, u32[]{:S(2)}, u32[]{:S(2)}) collective-permute-start(f32[8,3,8,256]{3,2,1,0:T(8,128)S(1)} %collective-permute-done.1.refs_2_), channel_id=1, source_target_pairs={{0,8},{4,12},{8,0},{12,4},{16,24},{20,28},{24,16},{28,20},{1,9},{5... | collective-permute-start | bytes 589832 | tf_op jit(solution)/shard_map/ppermute | solution.py:587
  16.8 1.5 %collective-permute-start.5 = (f32[7,3,8,256]{3,2,1,0:T(8,128)S(1)}, f32[7,3,8,256]{3,2,1,0:T(8,128)S(1)}, u32[]{:S(2)}, u32[]{:S(2)}) collective-permute-start(f32[7,3,8,256]{3,2,1,0:T(8,128)S(1)} %collective-permute-done.2.refs_4_), channel_id=1, source_target_pairs={{0,4},{4,0},{8,12},{12,8},{16,20},{20,16},{24,28},{28,24},{1,5},{5... | collective-permute-start | bytes 516104 | tf_op jit(solution)/shard_map/ppermute | solution.py:587
  18.3 0.0 collective-permute-done.refs_1_
  18.3 0.0 copy-start
  18.3 1.0 %copy-done = f32[2,200,256]{2,1,0:T(8,128)S(1)} copy-done((f32[2,200,256]{2,1,0:T(8,128)S(1)}, f32[2,200,256]{2,1,0:T(8,128)}, u32[]{:S(2)}) %copy-start) | copy-done | bytes 409624
  19.3 2.1 %own_rows.1 = (f32[4,136,256]{2,1,0:T(8,128)S(1)}, s32[4,128]{1,0:T(4,128)S(1)}, bf16[4,256,256]{2,1,0:T(8,128)(2,1)S(1)}, bf16[4,256,256]{2,1,0:T(8,128)(2,1)S(1)}) custom-call(f32[2,200,256]{2,1,0:T(8,128)S(1)} %copy-done, f32[2,200,256]{2,1,0:T(8,128)S(1)} %collective-permute-done.refs_1_, f32[30,3,8,256]{3,2,1,0:T(8,128)S(1)} %get-tuple-element.46.refs_2_.refs_0_.refs_5_), custom_call_target="tpu_custom_call" | custom-call | flops 2000000000 | bytes 2000000 | tf_op jit(solution)/shard_map/own_rows/pallas_call | solution.py:196
  21.3 0.8 %collective-permute-done.5.refs_8_ = f32[7,3,8,256]{3,2,1,0:T(8,128)S(1)} collective-permute-done((f32[7,3,8,256]{3,2,1,0:T(8,128)S(1)}, f32[7,3,8,256]{3,2,1,0:T(8,128)S(1)}, u32[]{:S(2)}, u32[]{:S(2)}) %collective-permute-start.5) | collective-permute-done | bytes 172064 | tf_op jit(solution)/shard_map/ppermute | solution.py:587
  22.2 0.0 collective-permute-done.4.refs_6_
  22.2 2.8 %collective-permute-done.3.refs_4_.refs_2_ = f32[2,200,256]{2,1,0:T(8,128)S(1)} collective-permute-done((f32[2,200,256]{2,1,0:T(8,128)}, f32[2,200,256]{2,1,0:T(8,128)S(1)}, u32[]{:S(2)}, u32[]{:S(2)}) %collective-permute-start.3) | collective-permute-done | bytes 409632 | tf_op jit(solution)/shard_map/ppermute | solution.py:587
  25.0 0.0 collective-permute-start.6
  25.0 0.5 collective-permute-start.10
  25.5 0.0 collective-permute-start.8
  25.5 0.5 collective-permute-start.11
  26.0 0.0 collective-permute-done.7.refs_1_
  26.0 0.0 collective-permute-start.9
  26.0 1.5 %collective-permute-done.11.refs_9_ = f32[7,3,8,256]{3,2,1,0:T(8,128)S(1)} collective-permute-done((f32[7,3,8,256]{3,2,1,0:T(8,128)S(1)}, f32[7,3,8,256]{3,2,1,0:T(8,128)S(1)}, u32[]{:S(2)}, u32[]{:S(2)}) %collective-permute-start.11) | collective-permute-done | bytes 172064 | tf_op jit(solution)/shard_map/ppermute | solution.py:587
  27.5 0.2 collective-permute-done.9.refs_5_
  27.8 0.0 collective-permute-done.10.refs_7_
  27.8 0.0 collective-permute-done.8.refs_3_
  27.8 0.2 place.1.refs_6_
  28.0 0.0 copy-start.1
  28.0 0.0 collective-permute-done.6.refs_5_.refs_3_
  28.0 4.5 %accumulate.1 = (f32[22,8,256]{2,1,0:T(8,128)S(1)}, f32[22,8,256]{2,1,0:T(8,128)S(1)}, f32[22,8,256]{2,1,0:T(8,128)S(1)}, f32[22,8,256]{2,1,0:T(8,128)S(1)}, f32...) custom-call(f32[4,136,256]{2,1,0:T(8,128)S(1)} %get-tuple-element.56, ...), custom_call_target="tpu_custom_call" | custom-call | flops 8000000000 | bytes 8000000 | tf_op jit(solution)/shard_map/accumulate/pallas_call | solution.py:393
  32.5 1.6 %collective-permute-start.12 = (f32[22,8,256]{2,1,0:T(8,128)S(1)}, f32[22,8,256]{2,1,0:T(8,128)S(1)}, u32[]{:S(2)}, u32[]{:S(2)}) collective-permute-start(f32[22,8,256]{2,1,0:T(8,128)S(1)} %get-tuple-element.68), channel_id=1, source_target_pairs={{0,4},{4,0},{8,12},{12,8},{16,20},{20,16},{24,28},{28,24},{1,5},{5... | collective-permute-start | bytes 540680 | tf_op jit(solution)/shard_map/ppermute | solution.py:587
  34.1 1.6 %collective-permute-start.14 = (f32[8,8,256]{2,1,0:T(8,128)S(1)}, f32[8,8,256]{2,1,0:T(8,128)S(1)}, u32[]{:S(2)}, u32[]{:S(2)}) collective-permute-start(f32[8,8,256]{2,1,0:T(8,128)S(1)} %get-tuple-element.77), channel_id=1, source_target_pairs={{0,8},{4,12},{8,0},{12,4},{16,24},{20,28},{24,16},{28,20},{1,9},{5... | collective-permute-start | bytes 196616 | tf_op jit(solution)/shard_map/ppermute | solution.py:587
  35.6 2.6 %collective-permute-start.15 = (f32[8,8,256]{2,1,0:T(8,128)S(1)}, f32[8,8,256]{2,1,0:T(8,128)S(1)}, u32[]{:S(2)}, u32[]{:S(2)}) collective-permute-start(f32[8,8,256]{2,1,0:T(8,128)S(1)} %get-tuple-element.78), channel_id=1, source_target_pairs={{0,16},{4,20},{8,24},{12,28},{16,0},{20,4},{24,8},{28,12},{1,17},{... | collective-permute-start | bytes 196616 | tf_op jit(solution)/shard_map/ppermute | solution.py:587
  38.2 0.2 collective-permute-start.16
  38.4 0.0 copy-done.1
  38.4 1.3 %own_sums.1.refs_2_ = f32[2,8,256]{2,1,0:T(8,128)S(1)} custom-call(f32[2,200,256]{2,1,0:T(8,128)S(1)} %copy-done.1, f32[2,200,256]{2,1,0:T(8,128)S(1)} %collective-permute-done.refs_1_, f32[2,200,256]{2,1,0:T(8,128)S(1)} %collective-permute-done.3.refs_4_.refs_2_, f32[2,200,256]{2,1,0:T(8,128)S(1)} %collective-permute-done.6.refs_5_.refs_3_, ...), custom_call_target="tpu_custom_call" | custom-call | flops 100000000 | bytes 100000 | tf_op jit(solution)/shard_map/own_sums/pallas_call | solution.py:477
  39.8 0.6 %collective-permute-start.13 = (f32[2,8,256]{2,1,0:T(8,128)S(1)}, f32[2,8,256]{2,1,0:T(8,128)S(1)}, u32[]{:S(2)}, u32[]{:S(2)}) collective-permute-start(f32[2,8,256]{2,1,0:T(8,128)S(1)} %own_sums.1.refs_2_), channel_id=1, source_target_pairs={{0,4},{4,0},{8,12},{12,8},{16,20},{20,16},{24,28},{28,24},{1,5},{5... | collective-permute-start | bytes 49160 | tf_op jit(solution)/shard_map/ppermute | solution.py:587
  40.3 3.2 %collective-permute-done.13.refs_3_ = f32[2,8,256]{2,1,0:T(8,128)S(1)} collective-permute-done((f32[2,8,256]{2,1,0:T(8,128)S(1)}, f32[2,8,256]{2,1,0:T(8,128)S(1)}, u32[]{:S(2)}, u32[]{:S(2)}) %collective-permute-start.13) | collective-permute-done | bytes 16416 | tf_op jit(solution)/shard_map/ppermute | solution.py:587
  43.6 0.0 collective-permute-done.12.refs_1_
  43.6 0.0 collective-permute-done.14.refs_1_
  43.6 0.0 collective-permute-done.15.refs_2_
  43.6 0.7 %collective-permute-done.16.refs_3_ = f32[8,8,256]{2,1,0:T(8,128)S(1)} collective-permute-done((f32[8,8,256]{2,1,0:T(8,128)S(1)}, f32[8,8,256]{2,1,0:T(8,128)S(1)}, u32[]{:S(2)}, u32[]{:S(2)}) %collective-permute-start.16) | collective-permute-done | bytes 65568 | tf_op jit(solution)/shard_map/ppermute | solution.py:587
  44.3 0.5 collective-permute-start.17
  44.8 1.6 %collective-permute-start.19 = (f32[13,8,256]{2,1,0:T(8,128)S(1)}, f32[13,8,256]{2,1,0:T(8,128)S(1)}, u32[]{:S(2)}, u32[]{:S(2)}) collective-permute-start(f32[13,8,256]{2,1,0:T(8,128)S(1)} %get-tuple-element.74), channel_id=1, source_target_pairs={{0,16},{4,20},{8,24},{12,28},{16,0},{20,4},{24,8},{28,12},{1,17},{... | collective-permute-start | bytes 319496 | tf_op jit(solution)/shard_map/ppermute | solution.py:587
  46.4 1.4 %collective-permute-start.20 = (f32[13,8,256]{2,1,0:T(8,128)S(1)}, f32[13,8,256]{2,1,0:T(8,128)S(1)}, u32[]{:S(2)}, u32[]{:S(2)}) collective-permute-start(f32[13,8,256]{2,1,0:T(8,128)S(1)} %get-tuple-element.75), channel_id=1, source_target_pairs={{0,24},{4,28},{8,16},{12,20},{16,8},{20,12},{24,0},{28,4},{1,25},{... | collective-permute-start | bytes 319496 | tf_op jit(solution)/shard_map/ppermute | solution.py:587
  47.8 2.0 %collective-permute-done.17.refs_1_ = f32[22,8,256]{2,1,0:T(8,128)S(1)} collective-permute-done((f32[22,8,256]{2,1,0:T(8,128)S(1)}, f32[22,8,256]{2,1,0:T(8,128)S(1)}, u32[]{:S(2)}, u32[]{:S(2)}) %collective-permute-start.17) | collective-permute-done | bytes 180256 | tf_op jit(solution)/shard_map/ppermute | solution.py:587
  49.8 0.1 collective-permute-start.18
  50.0 0.6 %collective-permute-start.21 = (f32[4,8,256]{2,1,0:T(8,128)S(1)}, f32[4,8,256]{2,1,0:T(8,128)S(1)}, u32[]{:S(2)}, u32[]{:S(2)}) collective-permute-start(f32[4,8,256]{2,1,0:T(8,128)S(1)} %get-tuple-element.85), channel_id=1, source_target_pairs={{0,4},{4,0},{8,12},{12,8},{16,20},{20,16},{24,28},{28,24},{1,5},{5... | collective-permute-start | bytes 98312 | tf_op jit(solution)/shard_map/ppermute | solution.py:587
  50.6 3.4 %collective-permute-done.21.refs_5_ = f32[4,8,256]{2,1,0:T(8,128)S(1)} collective-permute-done((f32[4,8,256]{2,1,0:T(8,128)S(1)}, f32[4,8,256]{2,1,0:T(8,128)S(1)}, u32[]{:S(2)}, u32[]{:S(2)}) %collective-permute-start.21) | collective-permute-done | bytes 32800 | tf_op jit(solution)/shard_map/ppermute | solution.py:587
  53.9 0.4 collective-permute-done.19.refs_2_
  54.3 0.0 collective-permute-done.20.refs_3_
  54.3 0.9 %collective-permute-done.18.refs_1_ = f32[13,8,256]{2,1,0:T(8,128)S(1)} collective-permute-done((f32[13,8,256]{2,1,0:T(8,128)S(1)}, f32[13,8,256]{2,1,0:T(8,128)S(1)}, u32[]{:S(2)}, u32[]{:S(2)}) %collective-permute-start.18) | collective-permute-done | bytes 106528 | tf_op jit(solution)/shard_map/ppermute | solution.py:587
  55.3 1.0 %finish.1 = (f32[240,120]{1,0:T(8,128)}, f32[1,240]{1,0:T(1,128)}, f32[8,8,30]{2,1,0:T(8,128)}) custom-call(f32[13,8,256]{2,1,0:T(8,128)S(1)} %get-tuple-element.82.refs_0_, f32[13,8,256]{2,1,0:T(8,128)S(1)} %collective-permute-done.18.refs_1_, f32[13,8,256]{2,1,0:T(8,128)S(1)} %collective-permute-done.19.refs_2_, ...), custom_call_target="tpu_custom_call" | custom-call | tf_op jit(solution)/shard_map/finish/pallas_call | solution.py:571
  (3 shorter events, 0.1 us)
Async XLA Ops:
  0.6 1.1 %copy-start.2 = (f32[30,3,8,256]{3,2,1,0:T(8,128)S(1)}, f32[30,3,8,256]{3,2,1,0:T(8,128)}, u32[]{:S(2)}) copy-start(f32[30,3,8,256]{3,2,1,0:T(8,128)} %orbit.1) | copy-start | bytes 2211844
  1.8 11.9 %collective-permute-start.1 = (f32[8,3,8,256]{3,2,1,0:T(8,128)S(1)}, f32[8,3,8,256]{3,2,1,0:T(8,128)S(1)}, u32[]{:S(2)}, u32[]{:S(2)}) collective-permute-start(f32[8,3,8,256]{3,2,1,0:T(8,128)S(1)} %get-tuple-element.51), channel_id=1, source_target_pairs={{0,2},{1,3},{2,0},{3,1},{4,6},{5,7},{6,4},{7,5},{8,10},{9,11},{10,... | collective-permute-start | bytes 589832 | tf_op jit(solution)/shard_map/ppermute | solution.py:587
  6.8 11.4 %collective-permute-start = (f32[2,200,256]{2,1,0:T(8,128)}, f32[2,200,256]{2,1,0:T(8,128)S(1)}, u32[]{:S(2)}, u32[]{:S(2)}) collective-permute-start(f32[2,200,256]{2,1,0:T(8,128)} %prepare.1.refs_0_), channel_id=1, source_target_pairs={{0,1},{1,0},{2,3},{3,2},{4,5},{5,4},{6,7},{7,6},{8,9},{9,8},{10,11... | collective-permute-start | bytes 1228808 | tf_op jit(solution)/shard_map/ppermute | solution.py:587
  6.9 6.8 %collective-permute-start.2 = (f32[7,3,8,256]{3,2,1,0:T(8,128)S(1)}, f32[7,3,8,256]{3,2,1,0:T(8,128)S(1)}, u32[]{:S(2)}, u32[]{:S(2)}) collective-permute-start(f32[7,3,8,256]{3,2,1,0:T(8,128)S(1)} %get-tuple-element.52), channel_id=1, source_target_pairs={{0,2},{1,3},{2,0},{3,1},{4,6},{5,7},{6,4},{7,5},{8,10},{9,11},{10,... | collective-permute-start | bytes 516104 | tf_op jit(solution)/shard_map/ppermute | solution.py:587
  7.0 19.0 %collective-permute-start.7 = (f32[30,3,8,256]{3,2,1,0:T(8,128)S(1)}, f32[30,3,8,256]{3,2,1,0:T(8,128)S(1)}, u32[]{:S(2)}, u32[]{:S(2)}) collective-permute-start(f32[30,3,8,256]{3,2,1,0:T(8,128)S(1)} %get-tuple-element.46.refs_2_.refs_0_.refs_5_), channel_id=1, source_target_pairs={{0,1},{1,0},{2,3},{3,2},{4,5},{5,4},{6,7},{7,6},{8,9},{9,8},{10,11... | collective-permute-start | bytes 2211848 | tf_op jit(solution)/shard_map/ppermute | solution.py:587
  13.7 11.2 %collective-permute-start.3 = (f32[2,200,256]{2,1,0:T(8,128)}, f32[2,200,256]{2,1,0:T(8,128)S(1)}, u32[]{:S(2)}, u32[]{:S(2)}) collective-permute-start(f32[2,200,256]{2,1,0:T(8,128)} %prepare.1.refs_0_), channel_id=1, source_target_pairs={{0,2},{1,3},{2,0},{3,1},{4,6},{5,7},{6,4},{7,5},{8,10},{9,11},{10,... | collective-permute-start | bytes 1228808 | tf_op jit(solution)/shard_map/ppermute | solution.py:587
  15.2 7.0 %collective-permute-start.4 = (f32[8,3,8,256]{3,2,1,0:T(8,128)S(1)}, f32[8,3,8,256]{3,2,1,0:T(8,128)S(1)}, u32[]{:S(2)}, u32[]{:S(2)}) collective-permute-start(f32[8,3,8,256]{3,2,1,0:T(8,128)S(1)} %collective-permute-done.1.refs_2_), channel_id=1, source_target_pairs={{0,8},{4,12},{8,0},{12,4},{16,24},{20,28},{24,16},{28,20},{1,9},{5... | collective-permute-start | bytes 589832 | tf_op jit(solution)/shard_map/ppermute | solution.py:587
  16.8 5.4 %collective-permute-start.5 = (f32[7,3,8,256]{3,2,1,0:T(8,128)S(1)}, f32[7,3,8,256]{3,2,1,0:T(8,128)S(1)}, u32[]{:S(2)}, u32[]{:S(2)}) collective-permute-start(f32[7,3,8,256]{3,2,1,0:T(8,128)S(1)} %collective-permute-done.2.refs_4_), channel_id=1, source_target_pairs={{0,4},{4,0},{8,12},{12,8},{16,20},{20,16},{24,28},{28,24},{1,5},{5... | collective-permute-start | bytes 516104 | tf_op jit(solution)/shard_map/ppermute | solution.py:587
  18.3 1.0 %copy-start = (f32[2,200,256]{2,1,0:T(8,128)S(1)}, f32[2,200,256]{2,1,0:T(8,128)}, u32[]{:S(2)}) copy-start(f32[2,200,256]{2,1,0:T(8,128)} %prepare.1.refs_0_) | copy-start | bytes 1228804
  25.0 3.0 %collective-permute-start.6 = (f32[2,200,256]{2,1,0:T(8,128)S(1)}, f32[2,200,256]{2,1,0:T(8,128)S(1)}, u32[]{:S(2)}, u32[]{:S(2)}) collective-permute-start(f32[2,200,256]{2,1,0:T(8,128)S(1)} %collective-permute-done.3.refs_4_.refs_2_), channel_id=1, source_target_pairs={{0,1},{1,0},{2,3},{3,2},{4,5},{5,4},{6,7},{7,6},{8,9},{9,8},{10,11... | collective-permute-start | bytes 1228808 | tf_op jit(solution)/shard_map/ppermute | solution.py:587
  25.0 2.8 %collective-permute-start.10 = (f32[8,3,8,256]{3,2,1,0:T(8,128)S(1)}, f32[8,3,8,256]{3,2,1,0:T(8,128)S(1)}, u32[]{:S(2)}, u32[]{:S(2)}) collective-permute-start(f32[8,3,8,256]{3,2,1,0:T(8,128)S(1)} %collective-permute-done.4.refs_6_), channel_id=1, source_target_pairs={{0,1},{1,0},{2,3},{3,2},{4,5},{5,4},{6,7},{7,6},{8,9},{9,8},{10,11... | collective-permute-start | bytes 589832 | tf_op jit(solution)/shard_map/ppermute | solution.py:587
  25.5 2.3 %collective-permute-start.8 = (f32[8,3,8,256]{3,2,1,0:T(8,128)S(1)}, f32[8,3,8,256]{3,2,1,0:T(8,128)S(1)}, u32[]{:S(2)}, u32[]{:S(2)}) collective-permute-start(f32[8,3,8,256]{3,2,1,0:T(8,128)S(1)} %collective-permute-done.1.refs_2_), channel_id=1, source_target_pairs={{0,1},{1,0},{2,3},{3,2},{4,5},{5,4},{6,7},{7,6},{8,9},{9,8},{10,11... | collective-permute-start | bytes 589832 | tf_op jit(solution)/shard_map/ppermute | solution.py:587
  25.5 2.0 %collective-permute-start.11 = (f32[7,3,8,256]{3,2,1,0:T(8,128)S(1)}, f32[7,3,8,256]{3,2,1,0:T(8,128)S(1)}, u32[]{:S(2)}, u32[]{:S(2)}) collective-permute-start(f32[7,3,8,256]{3,2,1,0:T(8,128)S(1)} %collective-permute-done.5.refs_8_), channel_id=1, source_target_pairs={{0,1},{1,0},{2,3},{3,2},{4,5},{5,4},{6,7},{7,6},{8,9},{9,8},{10,11... | collective-permute-start | bytes 516104 | tf_op jit(solution)/shard_map/ppermute | solution.py:587
  26.0 1.8 %collective-permute-start.9 = (f32[7,3,8,256]{3,2,1,0:T(8,128)S(1)}, f32[7,3,8,256]{3,2,1,0:T(8,128)S(1)}, u32[]{:S(2)}, u32[]{:S(2)}) collective-permute-start(f32[7,3,8,256]{3,2,1,0:T(8,128)S(1)} %collective-permute-done.2.refs_4_), channel_id=1, source_target_pairs={{0,1},{1,0},{2,3},{3,2},{4,5},{5,4},{6,7},{7,6},{8,9},{9,8},{10,11... | collective-permute-start | bytes 516104 | tf_op jit(solution)/shard_map/ppermute | solution.py:587
  28.0 10.5 %copy-start.1 = (f32[2,200,256]{2,1,0:T(8,128)S(1)}, f32[2,200,256]{2,1,0:T(8,128)}, u32[]{:S(2)}) copy-start(f32[2,200,256]{2,1,0:T(8,128)} %prepare.1.refs_0_) | copy-start | bytes 1228804
  32.5 11.1 %collective-permute-start.12 = (f32[22,8,256]{2,1,0:T(8,128)S(1)}, f32[22,8,256]{2,1,0:T(8,128)S(1)}, u32[]{:S(2)}, u32[]{:S(2)}) collective-permute-start(f32[22,8,256]{2,1,0:T(8,128)S(1)} %get-tuple-element.68), channel_id=1, source_target_pairs={{0,4},{4,0},{8,12},{12,8},{16,20},{20,16},{24,28},{28,24},{1,5},{5... | collective-permute-start | bytes 540680 | tf_op jit(solution)/shard_map/ppermute | solution.py:587
  34.1 9.5 %collective-permute-start.14 = (f32[8,8,256]{2,1,0:T(8,128)S(1)}, f32[8,8,256]{2,1,0:T(8,128)S(1)}, u32[]{:S(2)}, u32[]{:S(2)}) collective-permute-start(f32[8,8,256]{2,1,0:T(8,128)S(1)} %get-tuple-element.77), channel_id=1, source_target_pairs={{0,8},{4,12},{8,0},{12,4},{16,24},{20,28},{24,16},{28,20},{1,9},{5... | collective-permute-start | bytes 196616 | tf_op jit(solution)/shard_map/ppermute | solution.py:587
  35.6 8.0 %collective-permute-start.15 = (f32[8,8,256]{2,1,0:T(8,128)S(1)}, f32[8,8,256]{2,1,0:T(8,128)S(1)}, u32[]{:S(2)}, u32[]{:S(2)}) collective-permute-start(f32[8,8,256]{2,1,0:T(8,128)S(1)} %get-tuple-element.78), channel_id=1, source_target_pairs={{0,16},{4,20},{8,24},{12,28},{16,0},{20,4},{24,8},{28,12},{1,17},{... | collective-permute-start | bytes 196616 | tf_op jit(solution)/shard_map/ppermute | solution.py:587
  38.2 6.1 %collective-permute-start.16 = (f32[8,8,256]{2,1,0:T(8,128)S(1)}, f32[8,8,256]{2,1,0:T(8,128)S(1)}, u32[]{:S(2)}, u32[]{:S(2)}) collective-permute-start(f32[8,8,256]{2,1,0:T(8,128)S(1)} %get-tuple-element.79), channel_id=1, source_target_pairs={{0,24},{4,28},{8,16},{12,20},{16,8},{20,12},{24,0},{28,4},{1,25},{... | collective-permute-start | bytes 196616 | tf_op jit(solution)/shard_map/ppermute | solution.py:587
  39.8 3.8 %collective-permute-start.13 = (f32[2,8,256]{2,1,0:T(8,128)S(1)}, f32[2,8,256]{2,1,0:T(8,128)S(1)}, u32[]{:S(2)}, u32[]{:S(2)}) collective-permute-start(f32[2,8,256]{2,1,0:T(8,128)S(1)} %own_sums.1.refs_2_), channel_id=1, source_target_pairs={{0,4},{4,0},{8,12},{12,8},{16,20},{20,16},{24,28},{28,24},{1,5},{5... | collective-permute-start | bytes 49160 | tf_op jit(solution)/shard_map/ppermute | solution.py:587
  44.3 5.5 %collective-permute-start.17 = (f32[22,8,256]{2,1,0:T(8,128)S(1)}, f32[22,8,256]{2,1,0:T(8,128)S(1)}, u32[]{:S(2)}, u32[]{:S(2)}) collective-permute-start(f32[22,8,256]{2,1,0:T(8,128)S(1)} %get-tuple-element.81), channel_id=1, source_target_pairs={{0,4},{4,0},{8,12},{12,8},{16,20},{20,16},{24,28},{28,24},{1,5},{5... | collective-permute-start | bytes 540680 | tf_op jit(solution)/shard_map/ppermute | solution.py:587
  44.8 9.5 %collective-permute-start.19 = (f32[13,8,256]{2,1,0:T(8,128)S(1)}, f32[13,8,256]{2,1,0:T(8,128)S(1)}, u32[]{:S(2)}, u32[]{:S(2)}) collective-permute-start(f32[13,8,256]{2,1,0:T(8,128)S(1)} %get-tuple-element.74), channel_id=1, source_target_pairs={{0,16},{4,20},{8,24},{12,28},{16,0},{20,4},{24,8},{28,12},{1,17},{... | collective-permute-start | bytes 319496 | tf_op jit(solution)/shard_map/ppermute | solution.py:587
  46.4 7.9 %collective-permute-start.20 = (f32[13,8,256]{2,1,0:T(8,128)S(1)}, f32[13,8,256]{2,1,0:T(8,128)S(1)}, u32[]{:S(2)}, u32[]{:S(2)}) collective-permute-start(f32[13,8,256]{2,1,0:T(8,128)S(1)} %get-tuple-element.75), channel_id=1, source_target_pairs={{0,24},{4,28},{8,16},{12,20},{16,8},{20,12},{24,0},{28,4},{1,25},{... | collective-permute-start | bytes 319496 | tf_op jit(solution)/shard_map/ppermute | solution.py:587
  49.8 5.4 %collective-permute-start.18 = (f32[13,8,256]{2,1,0:T(8,128)S(1)}, f32[13,8,256]{2,1,0:T(8,128)S(1)}, u32[]{:S(2)}, u32[]{:S(2)}) collective-permute-start(f32[13,8,256]{2,1,0:T(8,128)S(1)} %get-tuple-element.83), channel_id=1, source_target_pairs={{0,8},{4,12},{8,0},{12,4},{16,24},{20,28},{24,16},{28,20},{1,9},{5... | collective-permute-start | bytes 319496 | tf_op jit(solution)/shard_map/ppermute | solution.py:587
  50.0 4.0 %collective-permute-start.21 = (f32[4,8,256]{2,1,0:T(8,128)S(1)}, f32[4,8,256]{2,1,0:T(8,128)S(1)}, u32[]{:S(2)}, u32[]{:S(2)}) collective-permute-start(f32[4,8,256]{2,1,0:T(8,128)S(1)} %get-tuple-element.85), channel_id=1, source_target_pairs={{0,4},{4,0},{8,12},{12,8},{16,20},{20,16},{24,28},{28,24},{1,5},{5... | collective-permute-start | bytes 98312 | tf_op jit(solution)/shard_map/ppermute | solution.py:587
